TPU v7x, 32 devices: a whole 2x2x4 slice. The times are simulated.
32 devices in a mesh: groups: 2 (over y), head: 4 (over z), hist: 4 (over x, core).
Axes of the slice: x: 2, y: 2, z: 4, core: 2. Of those that a mesh axis runs over, the one named last changes fastest.
Arguments:
- tokens: bfloat16 [1024, 8192], P('groups', 'hist'), parts along dimension 0, may hold values from -6 to 6
- w_qkvu: bfloat16 [8192, 4, 8192], P('hist', None, 'head'), may hold values from -0.0625 to 0.0625
- k_cache: bfloat16 [4096, 8192], P(('groups', 'hist'), 'head'), parts along dimension 0, may hold values from -6 to 6
- v_cache: bfloat16 [4096, 8192], P(('groups', 'hist'), 'head'), parts along dimension 0
- w_out: bfloat16 [8192, 8192], P('head', 'hist'), may hold values from -0.0625 to 0.0625
- vis_start: int32 [1024], P('groups'), parts along dimension 0, may hold values from 0 to 511, as said below
- vis_end: int32 [1024], P('groups'), parts along dimension 0, may hold values from 1025 to 2048
Outputs:
- layer_out: bfloat16 [1024, 8192], P(('groups', 'head'), 'hist'), parts along dimension 0
There are 2 independent parts, one for each index of `groups`. A program takes and returns all parts, laid end to end along the dimension named above; an argument that names none is the same for every part. Nothing has to cross between parts.
Inputs may be any that keep to these rules, and one draw needn't show every extreme that they name: vis_start and vis_end together leave every candidate 2048 // 4 + 2 or more visible history events.
All inputs are finite; a program needn't handle non-finite values.
Results may differ from a plain program's by a relative error of at most 0.02.
Values may be sent and summed in bfloat16 or wider, within the bound.
No kernel may reach another device: no remote copies, remote signals or barrier semaphores. Data moves between devices by JAX's collectives and lax.ppermute only.
A program may use at most 192 MiB of HBM per device.

v0:
```python
import jax
import jax.numpy as jnp
from jax import lax
from jax.sharding import PartitionSpec as P

DH = 128


epsilon = 1e-05


def history_terms(query_heads, key_block, value_block, vis_lo, vis_hi):
    head_total = query_heads.shape[1]
    head_size = query_heads.shape[2]
    block_len = key_block.shape[0]
    key_heads = key_block.reshape(block_len, head_total, head_size)
    value_heads = value_block.reshape(block_len, head_total, head_size)
    scores = jnp.einsum(
        "rhe,lhe->rhl", query_heads, key_heads, preferred_element_type=jnp.float32
    ) * head_size ** (-0.5)
    positions = lax.iota(jnp.int32, block_len)
    visible = (positions[None, :] >= vis_lo[:, None]) & (positions[None, :] < vis_hi[:, None])
    weights = jnp.where(visible[:, None, :], jax.nn.silu(scores), 0.0).astype(jnp.bfloat16)
    summed_values = jnp.einsum(
        "rhl,lhe->rhe", weights, value_heads, preferred_element_type=jnp.float32
    )
    return summed_values.reshape(query_heads.shape[0], head_total * head_size)


def local(tokens, w_qkvu, k_cache, v_cache, w_out, vis_start, vis_end):
    cand_total = tokens.shape[0]
    hist_count = lax.axis_size("hist")
    head_count = lax.axis_size("head")
    own_count = cand_total // hist_count
    own_first = lax.axis_index("hist") * own_count
    local_width = w_qkvu.shape[2]
    local_heads = local_width // DH
    full_width = local_width * head_count
    flat_weight = w_qkvu.reshape(w_qkvu.shape[0], 4 * local_width)
    start_own = lax.dynamic_slice_in_dim(vis_start, own_first, own_count)
    end_own = lax.dynamic_slice_in_dim(vis_end, own_first, own_count)
    summed = lax.psum_scatter(
        jnp.dot(tokens, flat_weight, preferred_element_type=jnp.float32).astype(jnp.bfloat16),
        "hist",
        scatter_dimension=0,
        tiled=True,
    ).astype(jnp.float32)
    own_part = jax.nn.silu(summed).astype(jnp.bfloat16).reshape(own_count, 4, local_width)
    own_query = own_part[:, 0]
    own_key = own_part[:, 1]
    own_value = own_part[:, 2]
    own_gate = own_part[:, 3]
    query_heads = own_query.reshape(own_count, local_heads, DH)
    history = history_terms(
        query_heads,
        lax.all_gather(k_cache, "hist", axis=0, tiled=True),
        lax.all_gather(v_cache, "hist", axis=0, tiled=True),
        start_own,
        end_own,
    )
    counts = (end_own - start_own).astype(jnp.float32)
    own_product = own_query.astype(jnp.float32) * own_key.astype(jnp.float32)
    own_score = jnp.sum(own_product.reshape(own_count, local_heads, DH), axis=2) * DH ** (-0.5)
    own_term = jax.nn.silu(own_score)[:, :, None] * own_value.astype(jnp.float32).reshape(
        own_count, local_heads, DH
    )
    attended = history / jnp.sqrt(counts)[:, None] + own_term.reshape(own_count, local_width)
    row_sum = lax.psum(jnp.sum(attended, axis=1), "head")
    centered = attended - (row_sum / full_width)[:, None]
    spread = lax.psum(jnp.sum(centered * centered, axis=1), "head")
    normed = centered * lax.rsqrt(spread / full_width + epsilon)[:, None]
    gated_rows = (normed * own_gate.astype(jnp.float32)).astype(jnp.bfloat16)
    gathered = lax.all_gather(gated_rows, "hist", axis=0, tiled=True)
    out_count = cand_total // head_count
    out_first = lax.axis_index("head") * out_count
    whole_out = jnp.dot(gathered, w_out, preferred_element_type=jnp.float32)
    total_out = lax.psum(whole_out.astype(jnp.bfloat16), "head").astype(jnp.float32)
    summed_out = lax.dynamic_slice_in_dim(total_out, out_first, out_count, 0)
    residual = lax.dynamic_slice_in_dim(tokens, out_first, out_count, 0).astype(jnp.float32)
    return (residual + summed_out).astype(jnp.bfloat16)


def solution(mesh):
    in_specs = (
        P("groups", "hist"),
        P("hist", None, "head"),
        P(("groups", "hist"), "head"),
        P(("groups", "hist"), "head"),
        P("head", "hist"),
        P("groups"),
        P("groups"),
    )
    out_specs = P(("groups", "head"), "hist")
    return jax.shard_map(local, mesh=mesh, in_specs=in_specs, out_specs=out_specs, check_vma=False)
```

profile of v0, /device:TPU:0, one launch (start us, length us, event | category | flops | bytes accessed | tf_op | source)
XLA Modules:
  0.0 368.2 jit_solution(18409414456210205719)
XLA Ops:
  6.5 0.0 all-gather.6.cloned.1.call-start
  6.5 0.7 all-gather.6.cloned.1.call-update
  7.3 0.0 reduce-scatter.2.cloned.1.call-start
  7.3 0.0 copy-start.2
  7.3 30.2 %copy.29 = bf16[256,8,4,2048]{3,1,2,0:T(8,128)(2,1)} copy(bf16[256,8,4,2048]{3,2,1,0:T(4,128)(2,1)} %bitcast.58) | data formatting | bytes 67108864
  37.5 0.0 copy-done.2
  37.5 25.5 %convolution_convert_fusion = bf16[512,8192]{1,0:T(8,128)(2,1)} fusion(bf16[512,2048]{1,0:T(8,128)(2,1)S(1)} %copy-done.2, bf16[2048,8192]{1,0:T(8,128)(2,1)} %bitcast.59), kind=kOutput, calls=%fused_computation.7 | convolution fusion | flops 17184063488 | bytes 44040192 | tf_op jit(solution)/shard_map/dot_general | solution.py:43
  63.0 0.0 copy-start.1
  63.0 0.0 reduce-scatter.2.cloned.1.call-update
  63.0 0.0 all-gather.4.cloned.1.call-start
  63.1 1.6 copy-done.1
  64.7 2.5 copy.14
  67.2 0.0 all-gather.4.cloned.1.call-update
  67.3 0.2 all-gather.8.cloned.1.call-start
  67.5 0.8 convert_sqrt_fusion
  68.3 0.5 fusion.19
  68.8 1.2 all-gather.6.cloned.1.call-done
  69.9 12.5 %copy.17 = bf16[2048,2048]{0,1:T(8,128)(2,1)} copy(bf16[2048,2048]{1,0:T(8,128)(2,1)} %all-gather.6.cloned.1.call-done) | data formatting | bytes 16777216 | tf_op jit(solution)/shard_map/all_gather | solution.py:57
  82.4 61.9 %reduce-scatter.2.cloned.1.call-done = bf16[128,8192]{1,0:T(8,128)(2,1)} async-done(((bf16[512,8192]{1,0:T(8,128)(2,1)}), bf16[128,8192]{1,0:T(8,128)(2,1)}) %reduce-scatter.2.cloned.1.call-update) | async-done | bytes 2097168 | tf_op jit(solution)/shard_map/reduce_scatter | solution.py:42
  144.3 4.0 %fusion.12 = bf16[128,8192]{1,0:T(8,128)(2,1)} fusion(bf16[128,8192]{1,0:T(8,128)(2,1)} %reduce-scatter.2.cloned.1.call-done), kind=kLoop, calls=%fused_computation.15 | loop fusion | flops 6291456 | bytes 4194304 | tf_op jit(solution)/shard_map/convert_element_type | solution.py:48
  148.3 3.3 reshape.92
  151.7 4.4 %fusion.24 = (bf16[128,1,2048]{2,1,0:T(2,128)(2,1)S(1)}, bf16[128,1,2048]{2,1,0:T(2,128)(2,1)}, f32[128,1,2048]{2,1,0:T(1,128)}, bf16[128,1,2048]{2,1,0:T(2,128)(2,1)}) fusion(bf16[128,4,2048]{2,1,0:T(4,128)(2,1)S(1)} %reshape.92), kind=kLoop, calls=%fused_computation.42 | loop fusion | flops 262144 | bytes 4718592 | tf_op jit(solution)/shard_map/slice | solution.py:51
  156.0 2.5 copy.27
  158.5 2.4 copy.26
  161.0 0.0 copy-start
  161.0 0.2 fusion.14
  161.2 0.6 copy-done
  161.8 0.1 mul.90
  161.9 1.3 copy.21
  163.2 0.4 copy_convert_fusion
  163.6 0.3 copy.22
  163.9 40.4 %all-gather.4.cloned.1.call-done = bf16[2048,2048]{0,1:T(8,128)(2,1)} async-done(((bf16[512,2048]{0,1:T(8,128)(2,1)}), bf16[2048,2048]{0,1:T(8,128)(2,1)}) %all-gather.4.cloned.1.call-update) | async-done | bytes 8388624 | tf_op jit(solution)/shard_map/all_gather | solution.py:56
  204.3 11.9 %fusion.23 = (f32[128]{0:T(128)S(1)}, f32[16,128,128]{1,2,0:T(8,128)S(1)}) fusion(f32[128,16,128]{0,2,1:T(8,128)S(1)} %bitcast.61, f32[128,16]{0,1:T(8,128)S(1)} %divide_multiply_fusion, f32[128]{0:T(128)S(1)} %get-tuple-element.5, bf16[2048,16,128]{0,2,1:T(8,128)(2,1)} %bitcast.60, pred[128,2048]{1,0:T(8,128)(4,1)S(1)} %fusion.19, ...), kind=kOutput, calls=%fused_computation.41 | convolution fusion | flops 2177892352 | bytes 19670016 | tf_op jit(solution)/shard_map/rhl,lhe->rhe/dot_general | solution.py:24
  216.2 1.3 copy.18
  217.5 11.7 %psum.21 = f32[128]{0:T(128)S(1)} all-reduce(f32[128]{0:T(128)S(1)} %get-tuple-element.12), channel_id=1, replica_groups=mesh['groups'=2,'head'=4,'hist'=4] {'head'}, use_global_device_ids=true, to_apply=%region_3.4 | all-reduce | flops 128 | bytes 1024 | tf_op jit(solution)/shard_map/psum | solution.py:68
  229.2 0.3 multiply_reduce_fusion
  229.5 8.4 %psum.22 = f32[128]{0:T(128)S(1)} all-reduce(f32[128]{0:T(128)S(1)} %multiply_reduce_fusion), channel_id=1, replica_groups=mesh['groups'=2,'head'=4,'hist'=4] {'head'}, use_global_device_ids=true, to_apply=%region_5.6 | all-reduce | flops 128 | bytes 1024 | tf_op jit(solution)/shard_map/psum | solution.py:70
  237.9 3.7 %fusion.13 = bf16[128,2048]{1,0:T(8,128)(2,1)} fusion(f32[128,1,2048]{2,1,0:T(1,128)} %get-tuple-element.10, f32[128,2048]{1,0:T(8,128)} %copy.21, f32[128,2048]{1,0:T(8,128)} %copy.18, f32[128]{0:T(128)S(1)} %add_rsqrt_fusion, f32[128]{0:T(128)S(1)} %broadcast_multiply_fusion, f32[128]{0:T(128)S(1)} %get-tuple-element.5, ...), kind=kLoop, calls=%fused_computation.19 | loop fusion | flops 2097152 | bytes 4195840 | tf_op jit(solution)/shard_map/convert_element_type | solution.py:72
  241.6 0.0 all-gather.8.cloned.1.call-update
  241.6 0.3 all-reduce.2.cloned.1.call-start
  241.9 21.1 %all-gather.8.cloned.1.call-done = bf16[512,2048]{1,0:T(8,128)(2,1)} async-done(((bf16[128,2048]{1,0:T(8,128)(2,1)}), bf16[512,2048]{1,0:T(8,128)(2,1)}) %all-gather.8.cloned.1.call-update) | async-done | bytes 2097168 | tf_op jit(solution)/shard_map/all_gather | solution.py:73
  263.0 9.9 %convolution_convert_fusion.1 = bf16[512,2048]{1,0:T(8,128)(2,1)} fusion(bf16[512,2048]{1,0:T(8,128)(2,1)} %all-gather.8.cloned.1.call-done, bf16[2048,2048]{1,0:T(8,128)(2,1)} %param.11), kind=kOutput, calls=%fused_computation.16 | convolution fusion | flops 4296015872 | bytes 12582912 | tf_op jit(solution)/shard_map/dot_general | solution.py:76
  272.9 0.0 all-reduce.2.cloned.1.call-update
  272.9 86.7 %all-reduce.2.cloned.1.call-done = bf16[512,2048]{1,0:T(8,128)(2,1)} async-done(((bf16[512,2048]{1,0:T(8,128)(2,1)}), bf16[512,2048]{1,0:T(8,128)(2,1)}) %all-reduce.2.cloned.1.call-update) | async-done | bytes 2097168 | tf_op jit(solution)/shard_map/psum | solution.py:77
  359.6 2.1 add_convert_fusion
  (3 shorter events, 0.0 us)
Async XLA Ops:
  6.5 63.4 %all-gather.6.cloned.1.call-start = ((), (), s32[]{:S(2)}) async-start(), calls=%async_computation.3 | async-start | bytes 10485760 | tf_op jit(solution)/shard_map/all_gather | solution.py:57
  7.3 137.0 %reduce-scatter.2.cloned.1.call-start = ((), (), s32[]{:S(2)}) async-start(), calls=%async_computation.1 | async-start | bytes 10485760 | tf_op jit(solution)/shard_map/reduce_scatter | solution.py:42
  7.3 30.2 %copy-start.2 = (bf16[512,2048]{1,0:T(8,128)(2,1)S(1)}, bf16[512,2048]{1,0:T(8,128)(2,1)}, u32[]{:S(2)}) copy-start(bf16[512,2048]{1,0:T(8,128)(2,1)} %param.7) | copy-start | bytes 6291460
  63.0 1.7 copy-start.1
  63.0 141.2 %all-gather.4.cloned.1.call-start = ((), (), s32[]{:S(2)}) async-start(), calls=%async_computation.2 | async-start | bytes 10485760 | tf_op jit(solution)/shard_map/all_gather | solution.py:56
  67.3 195.8 %all-gather.8.cloned.1.call-start = ((), (), s32[]{:S(2)}) async-start(), calls=%async_computation.4 | async-start | bytes 2621440 | tf_op jit(solution)/shard_map/all_gather | solution.py:73
  161.0 0.8 copy-start
  241.6 118.0 %all-reduce.2.cloned.1.call-start = ((), (), s32[]{:S(2)}) async-start(), calls=%async_computation.5 | async-start | bytes 4194304 | tf_op jit(solution)/shard_map/psum | solution.py:77
Sparse Core Ops, SparseCore 0:
  8.9 60.9 all-gather.5
  72.5 71.7 reduce-scatter.1
  145.9 58.2 all-gather.3
  241.7 21.2 all-gather.7
  273.0 86.4 all-reduce.1
where the time goes:
time: 369 us; the launch traced here: 368 us
  waiting for transfers between devices  212 us (57%)
  local copies, waits for them, and re-layouts  58.8 us (16%)
  matrix products  47.3 us (13%)
  blocking collectives  20 us (5%)
  other arithmetic  16.3 us (4%)
  between operations  13.2 us (4%)
    psum x1, waiting for transfers between devices, local(): lax.psum(whole_out.astype(jnp.bfloat16), 'head').astype(jnp.float32)  86.7 us
    reduce_scatter x1, waiting for transfers between devices, local(): lax.psum_scatter(jnp.dot(tokens, flat_weight, preferred_element_type=jnp....  61.9 us
    all_gather x1, waiting for transfers between devices, local(): lax.all_gather(k_cache, 'hist', axis=0, tiled=True)  40.4 us
    unnamed x10, local copies, waits for them, and re-layouts  39.9 us
    dot_general x1, matrix products, local(): jnp.dot(tokens, flat_weight, preferred_element_type=jnp.float32)  25.5 us
    all_gather x1, waiting for transfers between devices, local(): gathered = lax.all_gather(gated_rows, 'hist', axis=0, tiled=True)  21.1 us
    all_gather x1, local copies, waits for them, and re-layouts, local(): lax.all_gather(v_cache, 'hist', axis=0, tiled=True)  12.5 us
    dot_general x1, matrix products, history_terms(): jnp.einsum('rhl,lhe->rhe', weights, value_heads, preferred_element_type=j...  11.9 us
  transfers between devices with their start and end apart: 5, of which 5 were waited for; matrix products, arithmetic and copies ran while one was open for 25% of the time, Pallas kernels for 0%

commit v1 on v0

v1 whole, which is shorter than its diff:
```python
import functools

import jax
import jax.numpy as jnp
from jax import lax
from jax.experimental import pallas as pl
from jax.experimental.pallas import tpu as pltpu
from jax.sharding import PartitionSpec as P

DH = 128
EPSILON = 1e-05
VMEM_LIMIT = 48 * 1024 * 1024

bf16 = jnp.bfloat16
f32 = jnp.float32


def silu(v):
    return 0.5 * v * (1.0 + jnp.tanh(0.5 * v))


def params():
    return pltpu.CompilerParams(vmem_limit_bytes=VMEM_LIMIT)


def project_kernel(t_ref, w_ref, o_ref, wide_ref, rhs_ref):
    depth = w_ref.shape[0]
    wide_ref[...] = w_ref.reshape(depth * 4, DH)[...].astype(f32)
    for i in range(4):
        rhs_ref[:, i * DH:(i + 1) * DH] = wide_ref[pl.ds(i, depth, stride=4), :].astype(bf16)
    res = jnp.dot(t_ref[...], rhs_ref[...], preferred_element_type=f32).astype(bf16)
    owners, _, each, _ = o_ref.shape
    for p in range(owners):
        for i in range(4):
            o_ref[p, i] = res[p * each:(p + 1) * each, i * DH:(i + 1) * DH]


def project(tokens, w, row_chunk, rows, head_first, heads, owners):
    depth = w.shape[0]
    each = rows // owners
    return pl.pallas_call(
        project_kernel,
        grid=(heads,),
        in_specs=[
            pl.BlockSpec((rows, depth), lambda j: (row_chunk, 0)),
            pl.BlockSpec((depth, 4, DH), lambda j: (0, 0, head_first + j)),
        ],
        out_specs=pl.BlockSpec((owners, 4, each, DH), lambda j: (0, 0, 0, j)),
        out_shape=jax.ShapeDtypeStruct((owners, 4, each, heads * DH), bf16),
        scratch_shapes=[pltpu.VMEM((depth * 4, DH), f32), pltpu.VMEM((depth, 4 * DH), bf16)],
        compiler_params=params(),
        cost_estimate=pl.CostEstimate(
            flops=2 * rows * depth * 4 * heads * DH,
            bytes_accessed=depth * 8 * heads * DH + rows * depth * 2,
            transcendentals=0,
        ),
        name="project",
    )(tokens, w)


def attend_kernel(q_ref, k_ref, v_ref, lo_ref, hi_ref, o_ref):
    rows, events = q_ref.shape[0], k_ref.shape[0]
    scores = lax.dot_general(
        q_ref[...], k_ref[...], (((1,), (1,)), ((), ())), preferred_element_type=f32
    ) * DH ** (-0.5)
    at = lax.broadcasted_iota(jnp.int32, (rows, events), 1)
    seen = (at >= lo_ref[...]) & (at < hi_ref[...])
    weights = jnp.where(seen, silu(scores), 0.0).astype(bf16)
    o_ref[...] = jnp.dot(weights, v_ref[...], preferred_element_type=f32).astype(bf16)


def attend(query, k_cache, v_cache, lo, hi, head_first, heads):
    rows, events = query.shape[0], k_cache.shape[0]
    cache = pl.BlockSpec((events, DH), lambda j: (0, head_first + j))
    edge = pl.BlockSpec((rows, 1), lambda j: (0, 0))
    return pl.pallas_call(
        attend_kernel,
        grid=(heads,),
        in_specs=[pl.BlockSpec((rows, DH), lambda j: (0, j)), cache, cache, edge, edge],
        out_specs=pl.BlockSpec((rows, DH), lambda j: (0, j)),
        out_shape=jax.ShapeDtypeStruct((rows, heads * DH), bf16),
        compiler_params=params(),
        cost_estimate=pl.CostEstimate(
            flops=4 * rows * events * heads * DH,
            bytes_accessed=4 * (rows + events) * heads * DH,
            transcendentals=rows * events * heads,
        ),
        name="attend",
    )(query, k_cache, v_cache, lo, hi)


def finish_kernel(chunks, *refs):
    root_ref = refs[0]
    keeps, gots, parts = (refs[1 + k * chunks:1 + (k + 1) * chunks] for k in range(3))
    att_ref, stat_ref = refs[1 + 3 * chunks:]
    rows = root_ref.shape[0]
    root = root_ref[...]
    total = jnp.zeros((rows, 1), f32)
    column = 0
    for keep, got, part in zip(keeps, gots, parts):
        for h in range(keep.shape[1] // DH):
            at = slice(h * DH, (h + 1) * DH)
            summed = keep[:, at].astype(f32) + got[:, at].astype(f32)
            q, k, v = (part[i, :, at].astype(f32) for i in range(3))
            own = silu(jnp.sum(q * k, axis=1, keepdims=True) * DH ** (-0.5))
            value = summed * root + own * v
            att_ref[:, column:column + DH] = value
            total += jnp.sum(value, axis=1, keepdims=True)
            column += DH
    mean = total / column
    spread = jnp.zeros((rows, DH), f32)
    for first in range(0, column, DH):
        away = att_ref[:, first:first + DH] - mean
        spread += away * away
    square = jnp.sum(spread, axis=1, keepdims=True)
    lane = lax.broadcasted_iota(jnp.int32, (rows, DH), 1)
    stat_ref[...] = jnp.where(lane < DH // 2, mean, square)


def finish(root, keeps, gots, parts):
    rows = root.shape[0]
    width = sum(k.shape[1] for k in keeps)
    return pl.pallas_call(
        functools.partial(finish_kernel, len(keeps)),
        out_shape=(
            jax.ShapeDtypeStruct((rows, width), f32),
            jax.ShapeDtypeStruct((rows, DH), f32),
        ),
        compiler_params=params(),
        cost_estimate=pl.CostEstimate(
            flops=20 * rows * width, bytes_accessed=16 * rows * width, transcendentals=0
        ),
        name="finish",
    )(root, *keeps, *gots, *parts)


def gate_kernel(chunks, others, *refs):
    att_ref, stats = refs[0], refs[1:2 + others]
    parts = refs[2 + others:2 + others + chunks]
    out_ref = refs[-1]
    width = att_ref.shape[1]
    means = [s[:, :1] for s in stats]
    mean = sum(means) / len(means)
    square = sum(s[:, DH // 2:DH // 2 + 1] for s in stats)
    square += width * sum((m - mean) * (m - mean) for m in means)
    scale = lax.rsqrt(square / (width * len(means)) + EPSILON)
    column = 0
    for part in parts:
        span = part.shape[2]
        normed = (att_ref[:, column:column + span] - mean) * scale
        out_ref[:, column:column + span] = (normed * part[3].astype(f32)).astype(bf16)
        column += span


def gate_rows(att, stats, parts):
    rows, width = att.shape
    return pl.pallas_call(
        functools.partial(gate_kernel, len(parts), len(stats) - 1),
        out_shape=jax.ShapeDtypeStruct((rows, width), bf16),
        compiler_params=params(),
        cost_estimate=pl.CostEstimate(
            flops=4 * rows * width, bytes_accessed=8 * rows * width, transcendentals=0
        ),
        name="gate",
    )(att, *stats, *parts)


def halving(count):
    return count & (count - 1) == 0


def swap(x, axis, bit):
    count = lax.axis_size(axis)
    return lax.ppermute(x, axis, [(i, i ^ (1 << bit)) for i in range(count)])


def position(axis):
    count, index = lax.axis_size(axis), lax.axis_index(axis)
    if not halving(count):
        return index
    bits = count.bit_length() - 1
    return sum(((index >> b) & 1) << (bits - 1 - b) for b in range(bits))


def scatter(x, axis):
    count, index = lax.axis_size(axis), lax.axis_index(axis)
    if count == 1:
        return x[0], jnp.zeros_like(x[0])
    if not halving(count):
        mine = lax.psum_scatter(x, axis, scatter_dimension=0, tiled=True)[0]
        return mine, jnp.zeros_like(mine)
    bits = count.bit_length() - 1
    for b in range(bits):
        mine, half = (index >> b) & 1, x.shape[0] // 2
        send = lax.dynamic_slice_in_dim(x, (1 - mine) * half, half).astype(bf16)
        keep = lax.dynamic_slice_in_dim(x, mine * half, half)
        got = swap(send, axis, b)
        if b == bits - 1:
            return keep[0], got[0]
        x = keep.astype(f32) + got.astype(f32)


def gather(x, axis):
    count, index = lax.axis_size(axis), lax.axis_index(axis)
    x = x[None]
    if not halving(count):
        return lax.all_gather(x, axis, axis=0, tiled=True)
    for b in reversed(range(count.bit_length() - 1)):
        mine = (index >> b) & 1
        got = swap(x, axis, b)
        x = jnp.where(mine == 0, jnp.concatenate([x, got]), jnp.concatenate([got, x]))
    return x


def all_stats(stat, axis):
    count = lax.axis_size(axis)
    if count > 8:
        every = lax.all_gather(stat, axis)
        return [every[i] for i in range(count)]
    return [stat] + [
        lax.ppermute(stat, axis, [(i, (i + k) % count) for i in range(count)])
        for k in range(1, count)
    ]


def line_scatter(x, axis):
    count, index = lax.axis_size(axis), lax.axis_index(axis)
    if count > 8:
        return lax.psum_scatter(x, axis, scatter_dimension=0, tiled=True)[0].astype(f32)

    def block(at):
        return lax.dynamic_index_in_dim(x, jnp.clip(at, 0, count - 1), 0, False)

    from_left = from_right = None
    for far in range(count - 1, 0, -1):
        right, left = block(index + far), block(index - far)
        if from_left is not None:
            right = (right.astype(f32) + from_left.astype(f32)).astype(bf16)
            left = (left.astype(f32) + from_right.astype(f32)).astype(bf16)
        from_left = lax.ppermute(right, axis, [(i, i + 1) for i in range(count - far)])
        from_right = lax.ppermute(left, axis, [(i, i - 1) for i in range(far, count)])
    total = block(index).astype(f32)
    if from_left is not None:
        total = total + from_left.astype(f32) + from_right.astype(f32)
    return total


def local(tokens, w_qkvu, k_cache, v_cache, w_out, vis_start, vis_end):
    cand, depth = tokens.shape
    owners, zs = lax.axis_size("hist"), lax.axis_size("head")
    width = w_qkvu.shape[2]
    heads = width // DH
    events = k_cache.shape[0]
    place = position("hist")

    row_chunks = 2 if cand % (2 * owners * zs * 16) == 0 else 1
    head_chunks = 2 if heads % 2 == 0 else 1
    rows = cand // row_chunks
    each = rows // owners
    piece = each // zs
    per = heads // head_chunks

    def arrange(x):
        tail = x.shape[1:]
        x = x.reshape((zs, row_chunks, owners, piece) + tail)
        x = jnp.moveaxis(x, (1, 2), (0, 1))
        return x.reshape((cand,) + tail)

    ordered = arrange(tokens)
    first_event = lax.axis_index("hist") * events
    start, end = arrange(vis_start), arrange(vis_end)
    low, high = (start - first_event)[:, None], (end - first_event)[:, None]
    root = lax.rsqrt((end - start).astype(f32))[:, None]

    partials = {
        (r, c): project(ordered, w_qkvu, r, rows, c * per, per, owners)
        for r in range(row_chunks)
        for c in range(head_chunks)
    }
    outs = []
    for r in range(row_chunks):
        span = slice(r * rows, (r + 1) * rows)
        parts, keeps, gots = [], [], []
        for c in range(head_chunks):
            keep, got = scatter(partials[r, c], "hist")
            part = silu(keep.astype(f32) + got.astype(f32)).astype(bf16)
            query = gather(part[0], "hist").reshape(rows, per * DH)
            term = attend(query, k_cache, v_cache, low[span], high[span], c * per, per)
            keep, got = scatter(term.reshape(owners, each, per * DH), "hist")
            parts.append(part)
            keeps.append(keep)
            gots.append(got)
        own_root = lax.dynamic_slice_in_dim(root[span], place * each, each)
        att, stat = finish(own_root, keeps, gots, parts)
        gated = gate_rows(att, all_stats(stat, "head"), parts)
        every = gather(gated, "hist").reshape(rows, width)
        sums = jnp.dot(every, w_out, preferred_element_type=f32).astype(bf16)
        sums = sums.reshape(owners, zs, piece, -1).swapaxes(0, 1)
        outs.append(line_scatter(sums.reshape(zs, each * owners // zs, -1), "head"))
    block = cand // zs
    residual = lax.dynamic_slice_in_dim(tokens, lax.axis_index("head") * block, block)
    return (residual.astype(f32) + jnp.concatenate(outs)).astype(bf16)


def solution(mesh):
    in_specs = (
        P("groups", "hist"),
        P("hist", None, "head"),
        P(("groups", "hist"), "head"),
        P(("groups", "hist"), "head"),
        P("head", "hist"),
        P("groups"),
        P("groups"),
    )
    out_specs = P(("groups", "head"), "hist")
    return jax.shard_map(local, mesh=mesh, in_specs=in_specs, out_specs=out_specs, check_vma=False)
```

time: 369 us -> 250 us (0.68)
  waiting for transfers between devices: 212 us -> 77.4 us
  Pallas kernels: 0 us -> 76.8 us
  starting transfers between devices: 0.57 us -> 62.6 us
  local copies, waits for them, and re-layouts: 58.8 us -> 11.3 us
  matrix products: 47.3 us -> 8.28 us
  blocking collectives: 20 us -> 0 us
  between operations: 13.2 us -> 0.93 us
  other arithmetic: 16.3 us -> 11.6 us
    psum x1 -> x0, waiting for transfers between devices: 86.7 us -> none  [local(): lax.psum(whole_out.astype(jnp.bfloat16), 'head').astype(jnp.float32)]
    ppermute x0 -> x46, waiting for transfers between devices: none -> 77.4 us  [the longest x28 56.1 us: swap(): return lax.ppermute(x, axis, [(i, i ^ 1 << bit) for i in range(count)])]
    pallas_call x0 -> x12, Pallas kernels: none -> 76.8 us  [the longest x4 55.6 us: project(): pl.pallas_call(project_kernel, grid=(heads,), in_specs=[pl.BlockSpec((row...]
    all_gather x3 -> x0, waiting for transfers between devices: 62.7 us -> none  [the longest x1 40.4 us: local(): lax.all_gather(k_cache, 'hist', axis=0, tiled=True)]
    ppermute x0 -> x46, starting transfers between devices: none -> 62.6 us  [the longest x28 24.3 us: swap(): return lax.ppermute(x, axis, [(i, i ^ 1 << bit) for i in range(count)])]
    reduce_scatter x1 -> x0, waiting for transfers between devices: 61.9 us -> none  [local(): lax.psum_scatter(jnp.dot(tokens, flat_weight, preferred_element_type=jnp....]
    dot_general x3 -> x2, matrix products: 47.3 us -> 8.28 us  [local(): sums = jnp.dot(every, w_out, preferred_element_type=f32).astype(bf16)]
    unnamed x10 -> x28, local copies, waits for them, and re-layouts: 39.9 us -> 2.9 us
  transfers between devices with their start and end apart: 5 -> 46, of which waited for: 5 -> 22; matrix products, arithmetic and copies ran while one was open for 25% -> 9% of each run, Pallas kernels for 0% -> 25%
where the time goes in v1:
time: 250 us; the launch traced here: 249 us
  waiting for transfers between devices  77.4 us (31%)
  Pallas kernels  76.8 us (31%)
  starting transfers between devices  62.6 us (25%)
  other arithmetic  11.6 us (5%)
  local copies, waits for them, and re-layouts  11.3 us (5%)
  matrix products  8.28 us (3%)
    ppermute x28, waiting for transfers between devices, swap(): return lax.ppermute(x, axis, [(i, i ^ 1 << bit) for i in range(count)])  56.1 us
    pallas_call x4, Pallas kernels, project(): pl.pallas_call(project_kernel, grid=(heads,), in_specs=[pl.BlockSpec((row...  55.6 us
    ppermute x28, starting transfers between devices, swap(): return lax.ppermute(x, axis, [(i, i ^ 1 << bit) for i in range(count)])  24.3 us
    ppermute x6, starting transfers between devices, line_scatter(): lax.ppermute(right, axis, [(i, i + 1) for i in range(count - far)])  23.3 us
    pallas_call x4, Pallas kernels, attend(): pl.pallas_call(attend_kernel, grid=(heads,), in_specs=[pl.BlockSpec((rows...  19 us
    ppermute x6, waiting for transfers between devices, line_scatter(): lax.ppermute(left, axis, [(i, i - 1) for i in range(far, count)])  12.1 us
    ppermute x6, starting transfers between devices, all_stats(): lax.ppermute(stat, axis, [(i, (i + k) % count) for i in range(count)])  9.65 us
    dot_general x2, matrix products, local(): sums = jnp.dot(every, w_out, preferred_element_type=f32).astype(bf16)  8.28 us
  transfers between devices with their start and end apart: 46, of which 22 were waited for; matrix products, arithmetic and copies ran while one was open for 9% of the time, Pallas kernels for 25%

profile of v1, /device:TPU:0, one launch (start us, length us, event | category | flops | bytes accessed | tf_op | source)
XLA Modules:
  0.0 248.9 jit_solution(12066381288568370292)
XLA Ops:
  0.0 1.7 copy.31
  1.7 13.9 %project.5 = bf16[4,4,64,1024]{3,2,1,0:T(8,128)(2,1)S(1)} custom-call(bf16[512,2048]{1,0:T(8,128)(2,1)S(1)} %bitcast.121, bf16[2048,4,2048]{2,1,0:T(4,128)(2,1)} %w_ref.7), custom_call_target="tpu_custom_call" | custom-call | flops 4294967296 | bytes 17825792 | tf_op jit(solution)/shard_map/project/pallas_call | solution.py:41
  17.8 13.9 %project.4 = bf16[4,4,64,1024]{3,2,1,0:T(8,128)(2,1)S(1)} custom-call(bf16[512,2048]{1,0:T(8,128)(2,1)S(1)} %bitcast.122, bf16[2048,4,2048]{2,1,0:T(4,128)(2,1)} %w_ref.7), custom_call_target="tpu_custom_call" | custom-call | flops 4294967296 | bytes 17825792 | tf_op jit(solution)/shard_map/project/pallas_call | solution.py:41
  33.4 13.9 %project.7 = bf16[4,4,64,1024]{3,2,1,0:T(8,128)(2,1)S(1)} custom-call(bf16[512,2048]{1,0:T(8,128)(2,1)S(1)} %bitcast.123, bf16[2048,4,2048]{2,1,0:T(4,128)(2,1)} %w_ref.7), custom_call_target="tpu_custom_call" | custom-call | flops 4294967296 | bytes 17825792 | tf_op jit(solution)/shard_map/project/pallas_call | solution.py:41
  49.4 13.9 %project.6 = bf16[4,4,64,1024]{3,2,1,0:T(8,128)(2,1)S(1)} custom-call(bf16[512,2048]{1,0:T(8,128)(2,1)S(1)} %bitcast.124, bf16[2048,4,2048]{2,1,0:T(4,128)(2,1)} %w_ref.7), custom_call_target="tpu_custom_call" | custom-call | flops 4294967296 | bytes 17825792 | tf_op jit(solution)/shard_map/project/pallas_call | solution.py:41
  67.2 1.8 convert_add_fusion.2
  69.0 3.0 %collective-permute-start.6 = (bf16[1,4,64,1024]{3,2,1,0:T(8,128)(2,1)S(1)}, bf16[1,4,64,1024]{3,2,1,0:T(8,128)(2,1)S(1)}, u32[]{:S(2)}, u32[]{:S(2)}) collective-permute-start(bf16[1,4,64,1024]{3,2,1,0:T(8,128)(2,1)S(1)} %dynamic-slice_convert_fusion.2), channel_id=1, source_target_pairs={{0,2},{1,3},{2,0},{3,1},{4,6},{5,7},{6,4},{7,5},{8,10},{9,11},{10,... | collective-permute-start | bytes 1572872 | tf_op jit(solution)/shard_map/ppermute | solution.py:174
  72.0 1.6 convert_add_fusion.3
  74.0 1.8 convert_add_fusion
  75.8 1.8 collective-permute-start.29
  77.7 1.6 convert_add_fusion.1
  79.7 5.0 %collective-permute-done.6 = bf16[1,4,64,1024]{3,2,1,0:T(8,128)(2,1)S(1)} collective-permute-done((bf16[1,4,64,1024]{3,2,1,0:T(8,128)(2,1)S(1)}, bf16[1,4,64,1024]{3,2,1,0:T(8,128)(2,1)S(1)}, u32[]{:S(2)}, u32[]{:S(2)}) %collective-permute-start.6) | collective-permute-done | bytes 524320 | tf_op jit(solution)/shard_map/ppermute | solution.py:174
  85.0 2.1 collective-permute-start.7
  87.2 8.8 %collective-permute-done.1 = bf16[1,4,64,1024]{3,2,1,0:T(8,128)(2,1)S(1)} collective-permute-done((bf16[1,4,64,1024]{3,2,1,0:T(8,128)(2,1)S(1)}, bf16[1,4,64,1024]{3,2,1,0:T(8,128)(2,1)S(1)}, u32[]{:S(2)}, u32[]{:S(2)}) %collective-permute-start.1) | collective-permute-done | bytes 524320 | tf_op jit(solution)/shard_map/ppermute | solution.py:174
  96.3 2.1 collective-permute-start.2
  98.4 8.8 %collective-permute-done.29 = bf16[1,4,64,1024]{3,2,1,0:T(8,128)(2,1)S(1)} collective-permute-done((bf16[1,4,64,1024]{3,2,1,0:T(8,128)(2,1)S(1)}, bf16[1,4,64,1024]{3,2,1,0:T(8,128)(2,1)S(1)}, u32[]{:S(2)}, u32[]{:S(2)}) %collective-permute-start.29) | collective-permute-done | bytes 524320 | tf_op jit(solution)/shard_map/ppermute | solution.py:174
  107.5 2.1 collective-permute-start.30
  109.6 8.8 %collective-permute-done.24 = bf16[1,4,64,1024]{3,2,1,0:T(8,128)(2,1)S(1)} collective-permute-done((bf16[1,4,64,1024]{3,2,1,0:T(8,128)(2,1)S(1)}, bf16[1,4,64,1024]{3,2,1,0:T(8,128)(2,1)S(1)}, u32[]{:S(2)}, u32[]{:S(2)}) %collective-permute-start.24) | collective-permute-done | bytes 524320 | tf_op jit(solution)/shard_map/ppermute | solution.py:174
  118.7 2.1 collective-permute-start.25
  121.4 2.7 %collective-permute-done.2 = bf16[1,64,1024]{2,1,0:T(8,128)(2,1)S(1)} collective-permute-done((bf16[1,64,1024]{2,1,0:T(8,128)(2,1)S(1)}, bf16[1,64,1024]{2,1,0:T(8,128)(2,1)S(1)}, u32[]{:S(2)}, u32[]{:S(2)}) %collective-permute-start.2) | collective-permute-done | bytes 131104 | tf_op jit(solution)/shard_map/ppermute | solution.py:174
  124.2 2.7 %collective-permute-done.30 = bf16[1,64,1024]{2,1,0:T(8,128)(2,1)S(1)} collective-permute-done((bf16[1,64,1024]{2,1,0:T(8,128)(2,1)S(1)}, bf16[1,64,1024]{2,1,0:T(8,128)(2,1)S(1)}, u32[]{:S(2)}, u32[]{:S(2)}) %collective-permute-start.30) | collective-permute-done | bytes 131104 | tf_op jit(solution)/shard_map/ppermute | solution.py:174
  127.0 2.1 collective-permute-done.25
  129.3 4.7 %attend.5 = bf16[256,1024]{1,0:T(8,128)(2,1)S(1)} custom-call(bf16[256,1024]{1,0:T(8,128)(2,1)S(1)} %bitcast.135, bf16[512,2048]{1,0:T(8,128)(2,1)S(1)} %copy-done, bf16[512,2048]{1,0:T(8,128)(2,1)S(1)} %copy-done.1, s32[256,1]{1,0:T(8,128)S(1)} %slice.74.lo_ref, s32[256,1]{1,0:T(8,128)S(1)} %slice.75.hi_ref), custom_call_target="tpu_custom_call" | custom-call | flops 536870912 | bytes 3145728 | tf_op jit(solution)/shard_map/attend/pallas_call | solution.py:76
  134.7 4.7 %attend.4 = bf16[256,1024]{1,0:T(8,128)(2,1)S(1)} custom-call(bf16[256,1024]{1,0:T(8,128)(2,1)S(1)} %bitcast.133, bf16[512,2048]{1,0:T(8,128)(2,1)S(1)} %copy-done, bf16[512,2048]{1,0:T(8,128)(2,1)S(1)} %copy-done.1, s32[256,1]{1,0:T(8,128)S(1)} %slice.74.lo_ref, s32[256,1]{1,0:T(8,128)S(1)} %slice.75.hi_ref), custom_call_target="tpu_custom_call" | custom-call | flops 536870912 | bytes 3145728 | tf_op jit(solution)/shard_map/attend/pallas_call | solution.py:76
  139.6 4.7 %attend.7 = bf16[256,1024]{1,0:T(8,128)(2,1)S(1)} custom-call(bf16[256,1024]{1,0:T(8,128)(2,1)S(1)} %bitcast.136, bf16[512,2048]{1,0:T(8,128)(2,1)S(1)} %copy-done, bf16[512,2048]{1,0:T(8,128)(2,1)S(1)} %copy-done.1, s32[256,1]{1,0:T(8,128)S(1)} %slice.76.lo_ref, s32[256,1]{1,0:T(8,128)S(1)} %slice.77.hi_ref), custom_call_target="tpu_custom_call" | custom-call | flops 536870912 | bytes 3145728 | tf_op jit(solution)/shard_map/attend/pallas_call | solution.py:76
  145.0 4.9 %attend.6 = bf16[256,1024]{1,0:T(8,128)(2,1)S(1)} custom-call(bf16[256,1024]{1,0:T(8,128)(2,1)S(1)} %bitcast.134, bf16[512,2048]{1,0:T(8,128)(2,1)S(1)} %copy-done, bf16[512,2048]{1,0:T(8,128)(2,1)S(1)} %copy-done.1, s32[256,1]{1,0:T(8,128)S(1)} %slice.76.lo_ref, s32[256,1]{1,0:T(8,128)S(1)} %slice.77.hi_ref), custom_call_target="tpu_custom_call" | custom-call | flops 536870912 | bytes 3145728 | tf_op jit(solution)/shard_map/attend/pallas_call | solution.py:76
  150.1 1.8 collective-permute-start.11
  152.5 1.8 collective-permute-start.34
  154.3 2.1 collective-permute-done.11
  156.5 2.8 %collective-permute-done.10 = bf16[1,64,1024]{2,1,0:T(8,128)(2,1)S(1)} collective-permute-done((bf16[1,64,1024]{2,1,0:T(8,128)(2,1)S(1)}, bf16[1,64,1024]{2,1,0:T(8,128)(2,1)S(1)}, u32[]{:S(2)}, u32[]{:S(2)}) %collective-permute-start.10) | collective-permute-done | bytes 131104 | tf_op jit(solution)/shard_map/ppermute | solution.py:174
  160.2 1.9 collective-permute-start.12
  162.0 2.6 %collective-permute-start.13 = (f32[64,128]{1,0:T(8,128)S(1)}, f32[64,128]{1,0:T(8,128)S(1)}, u32[]{:S(2)}, u32[]{:S(2)}) collective-permute-start(f32[64,128]{1,0:T(8,128)S(1)} %get-tuple-element.10.refs_1_), channel_id=1, source_target_pairs={{0,8},{4,12},{8,0},{12,4},{1,9},{5,13},{9,1},{13,5},{2,10},{6,14},... | collective-permute-start | bytes 98312 | tf_op jit(solution)/shard_map/ppermute | solution.py:221
  166.9 1.6 collective-permute-done.14.refs_4_
  171.0 6.8 %collective-permute-done.33 = bf16[1,64,1024]{2,1,0:T(8,128)(2,1)S(1)} collective-permute-done((bf16[1,64,1024]{2,1,0:T(8,128)(2,1)S(1)}, bf16[1,64,1024]{2,1,0:T(8,128)(2,1)S(1)}, u32[]{:S(2)}, u32[]{:S(2)}) %collective-permute-start.33) | collective-permute-done | bytes 131104 | tf_op jit(solution)/shard_map/ppermute | solution.py:174
  179.3 2.7 %collective-permute-start.36 = (f32[64,128]{1,0:T(8,128)S(1)}, f32[64,128]{1,0:T(8,128)S(1)}, u32[]{:S(2)}, u32[]{:S(2)}) collective-permute-start(f32[64,128]{1,0:T(8,128)S(1)} %get-tuple-element.12.refs_1_), channel_id=1, source_target_pairs={{0,8},{4,12},{8,0},{12,4},{1,9},{5,13},{9,1},{13,5},{2,10},{6,14},... | collective-permute-start | bytes 98312 | tf_op jit(solution)/shard_map/ppermute | solution.py:221
  182.8 1.7 collective-permute-done.35.refs_2_
  186.2 1.6 collective-permute-start.38
  187.8 4.9 %collective-permute-done.38 = bf16[1,64,2048]{2,1,0:T(8,128)(2,1)S(1)} collective-permute-done((bf16[1,64,2048]{2,1,0:T(8,128)(2,1)S(1)}, bf16[1,64,2048]{2,1,0:T(8,128)(2,1)S(1)}, u32[]{:S(2)}, u32[]{:S(2)}) %collective-permute-start.38) | collective-permute-done | bytes 262176 | tf_op jit(solution)/shard_map/ppermute | solution.py:174
  193.0 5.9 %convolution_convert_fusion.1 = bf16[256,2048]{1,0:T(8,128)(2,1)S(1)} fusion(bf16[256,2048]{1,0:T(8,128)(2,1)S(1)} %bitcast.157, bf16[2048,2048]{1,0:T(8,128)(2,1)} %param.11), kind=kOutput, calls=%fused_computation.1 | convolution fusion | flops 2148007936 | bytes 10485760 | tf_op jit(solution)/shard_map/dot_general | solution.py:297
  199.1 3.0 %collective-permute-start.17 = (bf16[64,2048]{1,0:T(8,128)(2,1)S(1)}, bf16[64,2048]{1,0:T(8,128)(2,1)S(1)}, u32[]{:S(2)}, u32[]{:S(2)}) collective-permute-start(bf16[64,2048]{1,0:T(8,128)(2,1)S(1)} %get-tuple-element.15), channel_id=1, source_target_pairs={{0,4},{1,5},{2,6},{3,7},{16,20},{17,21},{18,22},{19,23}} | collective-permute-start | bytes 786440 | tf_op jit(solution)/shard_map/ppermute | solution.py:240
  203.0 2.4 convolution_convert_fusion
  208.8 4.4 %collective-permute-start.18 = (bf16[64,2048]{1,0:T(8,128)(2,1)S(1)}, bf16[64,2048]{1,0:T(8,128)(2,1)S(1)}, u32[]{:S(2)}, u32[]{:S(2)}) collective-permute-start(bf16[64,2048]{1,0:T(8,128)(2,1)S(1)} %fusion.16), channel_id=1, source_target_pairs={{0,4},{4,8},{1,5},{5,9},{2,6},{6,10},{3,7},{7,11},{16,20},{20,24},... | collective-permute-start | bytes 786440 | tf_op jit(solution)/shard_map/ppermute | solution.py:240
  214.4 4.4 %collective-permute-start.41 = (bf16[64,2048]{1,0:T(8,128)(2,1)S(1)}, bf16[64,2048]{1,0:T(8,128)(2,1)S(1)}, u32[]{:S(2)}, u32[]{:S(2)}) collective-permute-start(bf16[64,2048]{1,0:T(8,128)(2,1)S(1)} %fusion.11), channel_id=1, source_target_pairs={{0,4},{4,8},{1,5},{5,9},{2,6},{6,10},{3,7},{7,11},{16,20},{20,24},... | collective-permute-start | bytes 786440 | tf_op jit(solution)/shard_map/ppermute | solution.py:240
  220.8 5.0 %collective-permute-start.19 = (bf16[64,2048]{1,0:T(8,128)(2,1)S(1)}, bf16[64,2048]{1,0:T(8,128)(2,1)S(1)}, u32[]{:S(2)}, u32[]{:S(2)}) collective-permute-start(bf16[64,2048]{1,0:T(8,128)(2,1)S(1)} %get-tuple-element.13), channel_id=1, source_target_pairs={{0,4},{4,8},{8,12},{1,5},{5,9},{9,13},{2,6},{6,10},{10,14},{3,7},{... | collective-permute-start | bytes 786440 | tf_op jit(solution)/shard_map/ppermute | solution.py:240
  226.6 5.2 %collective-permute-start.42 = (bf16[64,2048]{1,0:T(8,128)(2,1)S(1)}, bf16[64,2048]{1,0:T(8,128)(2,1)S(1)}, u32[]{:S(2)}, u32[]{:S(2)}) collective-permute-start(bf16[64,2048]{1,0:T(8,128)(2,1)S(1)} %get-tuple-element.17), channel_id=1, source_target_pairs={{0,4},{4,8},{8,12},{1,5},{5,9},{9,13},{2,6},{6,10},{10,14},{3,7},{... | collective-permute-start | bytes 786440 | tf_op jit(solution)/shard_map/ppermute | solution.py:240
  234.6 9.1 %collective-permute-done.22 = bf16[64,2048]{1,0:T(8,128)(2,1)S(1)} collective-permute-done((bf16[64,2048]{1,0:T(8,128)(2,1)S(1)}, bf16[64,2048]{1,0:T(8,128)(2,1)S(1)}, u32[]{:S(2)}, u32[]{:S(2)}) %collective-permute-start.22) | collective-permute-done | bytes 262176 | tf_op jit(solution)/shard_map/ppermute | solution.py:241
  243.8 3.1 %collective-permute-done.45 = bf16[64,2048]{1,0:T(8,128)(2,1)S(1)} collective-permute-done((bf16[64,2048]{1,0:T(8,128)(2,1)S(1)}, bf16[64,2048]{1,0:T(8,128)(2,1)S(1)}, u32[]{:S(2)}, u32[]{:S(2)}) %collective-permute-start.45) | collective-permute-done | bytes 262176 | tf_op jit(solution)/shard_map/ppermute | solution.py:241
  246.9 2.0 fusion
  (173 shorter events, 35.9 us)
Async XLA Ops:
  17.3 49.8 %collective-permute-start.5 = (bf16[2,4,64,1024]{3,2,1,0:T(8,128)(2,1)}, bf16[2,4,64,1024]{3,2,1,0:T(8,128)(2,1)}, u32[]{:S(2)}, u32[]{:S(2)}) collective-permute-start(bf16[2,4,64,1024]{3,2,1,0:T(8,128)(2,1)} %constant_dynamic-slice_fusion.5), channel_id=1, source_target_pairs={{0,1},{1,0},{2,3},{3,2},{4,5},{5,4},{6,7},{7,6},{8,9},{9,8},{10,11... | collective-permute-start | bytes 3145736 | tf_op jit(solution)/shard_map/ppermute | solution.py:174
  33.3 38.7 %collective-permute-start = (bf16[2,4,64,1024]{3,2,1,0:T(8,128)(2,1)}, bf16[2,4,64,1024]{3,2,1,0:T(8,128)(2,1)}, u32[]{:S(2)}, u32[]{:S(2)}) collective-permute-start(bf16[2,4,64,1024]{3,2,1,0:T(8,128)(2,1)} %constant_dynamic-slice_fusion.7), channel_id=1, source_target_pairs={{0,1},{1,0},{2,3},{3,2},{4,5},{5,4},{6,7},{7,6},{8,9},{9,8},{10,11... | collective-permute-start | bytes 3145736 | tf_op jit(solution)/shard_map/ppermute | solution.py:174
  49.0 25.0 %collective-permute-start.28 = (bf16[2,4,64,1024]{3,2,1,0:T(8,128)(2,1)}, bf16[2,4,64,1024]{3,2,1,0:T(8,128)(2,1)}, u32[]{:S(2)}, u32[]{:S(2)}) collective-permute-start(bf16[2,4,64,1024]{3,2,1,0:T(8,128)(2,1)} %constant_dynamic-slice_fusion.1), channel_id=1, source_target_pairs={{0,1},{1,0},{2,3},{3,2},{4,5},{5,4},{6,7},{7,6},{8,9},{9,8},{10,11... | collective-permute-start | bytes 3145736 | tf_op jit(solution)/shard_map/ppermute | solution.py:174
  65.7 11.9 %collective-permute-start.23 = (bf16[2,4,64,1024]{3,2,1,0:T(8,128)(2,1)}, bf16[2,4,64,1024]{3,2,1,0:T(8,128)(2,1)}, u32[]{:S(2)}, u32[]{:S(2)}) collective-permute-start(bf16[2,4,64,1024]{3,2,1,0:T(8,128)(2,1)} %constant_dynamic-slice_fusion.3), channel_id=1, source_target_pairs={{0,1},{1,0},{2,3},{3,2},{4,5},{5,4},{6,7},{7,6},{8,9},{9,8},{10,11... | collective-permute-start | bytes 3145736 | tf_op jit(solution)/shard_map/ppermute | solution.py:174
  69.0 15.7 %collective-permute-start.6 = (bf16[1,4,64,1024]{3,2,1,0:T(8,128)(2,1)S(1)}, bf16[1,4,64,1024]{3,2,1,0:T(8,128)(2,1)S(1)}, u32[]{:S(2)}, u32[]{:S(2)}) collective-permute-start(bf16[1,4,64,1024]{3,2,1,0:T(8,128)(2,1)S(1)} %dynamic-slice_convert_fusion.2), channel_id=1, source_target_pairs={{0,2},{1,3},{2,0},{3,1},{4,6},{5,7},{6,4},{7,5},{8,10},{9,11},{10,... | collective-permute-start | bytes 1572872 | tf_op jit(solution)/shard_map/ppermute | solution.py:174
  73.8 22.2 %collective-permute-start.1 = (bf16[1,4,64,1024]{3,2,1,0:T(8,128)(2,1)S(1)}, bf16[1,4,64,1024]{3,2,1,0:T(8,128)(2,1)S(1)}, u32[]{:S(2)}, u32[]{:S(2)}) collective-permute-start(bf16[1,4,64,1024]{3,2,1,0:T(8,128)(2,1)S(1)} %dynamic-slice_convert_fusion.3), channel_id=1, source_target_pairs={{0,2},{1,3},{2,0},{3,1},{4,6},{5,7},{6,4},{7,5},{8,10},{9,11},{10,... | collective-permute-start | bytes 1572872 | tf_op jit(solution)/shard_map/ppermute | solution.py:174
  75.8 31.4 %collective-permute-start.29 = (bf16[1,4,64,1024]{3,2,1,0:T(8,128)(2,1)S(1)}, bf16[1,4,64,1024]{3,2,1,0:T(8,128)(2,1)S(1)}, u32[]{:S(2)}, u32[]{:S(2)}) collective-permute-start(bf16[1,4,64,1024]{3,2,1,0:T(8,128)(2,1)S(1)} %dynamic-slice_convert_fusion), channel_id=1, source_target_pairs={{0,2},{1,3},{2,0},{3,1},{4,6},{5,7},{6,4},{7,5},{8,10},{9,11},{10,... | collective-permute-start | bytes 1572872 | tf_op jit(solution)/shard_map/ppermute | solution.py:174
  79.4 39.1 %collective-permute-start.24 = (bf16[1,4,64,1024]{3,2,1,0:T(8,128)(2,1)S(1)}, bf16[1,4,64,1024]{3,2,1,0:T(8,128)(2,1)S(1)}, u32[]{:S(2)}, u32[]{:S(2)}) collective-permute-start(bf16[1,4,64,1024]{3,2,1,0:T(8,128)(2,1)S(1)} %dynamic-slice_convert_fusion.1), channel_id=1, source_target_pairs={{0,2},{1,3},{2,0},{3,1},{4,6},{5,7},{6,4},{7,5},{8,10},{9,11},{10,... | collective-permute-start | bytes 1572872 | tf_op jit(solution)/shard_map/ppermute | solution.py:174
  85.0 36.2 %collective-permute-start.7 = (bf16[1,64,1024]{2,1,0:T(8,128)(2,1)S(1)}, bf16[1,64,1024]{2,1,0:T(8,128)(2,1)S(1)}, u32[]{:S(2)}, u32[]{:S(2)}) collective-permute-start(bf16[1,64,1024]{2,1,0:T(8,128)(2,1)S(1)} %slice.82), channel_id=1, source_target_pairs={{0,2},{1,3},{2,0},{3,1},{4,6},{5,7},{6,4},{7,5},{8,10},{9,11},{10,... | collective-permute-start | bytes 393224 | tf_op jit(solution)/shard_map/ppermute | solution.py:174
  96.3 27.8 %collective-permute-start.2 = (bf16[1,64,1024]{2,1,0:T(8,128)(2,1)S(1)}, bf16[1,64,1024]{2,1,0:T(8,128)(2,1)S(1)}, u32[]{:S(2)}, u32[]{:S(2)}) collective-permute-start(bf16[1,64,1024]{2,1,0:T(8,128)(2,1)S(1)} %slice.79), channel_id=1, source_target_pairs={{0,2},{1,3},{2,0},{3,1},{4,6},{5,7},{6,4},{7,5},{8,10},{9,11},{10,... | collective-permute-start | bytes 393224 | tf_op jit(solution)/shard_map/ppermute | solution.py:174
  107.5 19.4 %collective-permute-start.30 = (bf16[1,64,1024]{2,1,0:T(8,128)(2,1)S(1)}, bf16[1,64,1024]{2,1,0:T(8,128)(2,1)S(1)}, u32[]{:S(2)}, u32[]{:S(2)}) collective-permute-start(bf16[1,64,1024]{2,1,0:T(8,128)(2,1)S(1)} %slice.87), channel_id=1, source_target_pairs={{0,2},{1,3},{2,0},{3,1},{4,6},{5,7},{6,4},{7,5},{8,10},{9,11},{10,... | collective-permute-start | bytes 393224 | tf_op jit(solution)/shard_map/ppermute | solution.py:174
  118.5 10.8 %copy-start.1 = (bf16[512,2048]{1,0:T(8,128)(2,1)S(1)}, bf16[512,2048]{1,0:T(8,128)(2,1)}, u32[]{:S(2)}) copy-start(bf16[512,2048]{1,0:T(8,128)(2,1)} %v_ref.7) | copy-start | bytes 6291460
  118.7 10.6 %copy-start = (bf16[512,2048]{1,0:T(8,128)(2,1)S(1)}, bf16[512,2048]{1,0:T(8,128)(2,1)}, u32[]{:S(2)}) copy-start(bf16[512,2048]{1,0:T(8,128)(2,1)} %k_ref.7) | copy-start | bytes 6291460
  118.7 10.3 %collective-permute-start.25 = (bf16[1,64,1024]{2,1,0:T(8,128)(2,1)S(1)}, bf16[1,64,1024]{2,1,0:T(8,128)(2,1)S(1)}, u32[]{:S(2)}, u32[]{:S(2)}) collective-permute-start(bf16[1,64,1024]{2,1,0:T(8,128)(2,1)S(1)} %slice.84), channel_id=1, source_target_pairs={{0,2},{1,3},{2,0},{3,1},{4,6},{5,7},{6,4},{7,5},{8,10},{9,11},{10,... | collective-permute-start | bytes 393224 | tf_op jit(solution)/shard_map/ppermute | solution.py:174
  121.3 7.9 %collective-permute-start.8 = (bf16[2,64,1024]{2,1,0:T(8,128)(2,1)S(1)}, bf16[2,64,1024]{2,1,0:T(8,128)(2,1)S(1)}, u32[]{:S(2)}, u32[]{:S(2)}) collective-permute-start(bf16[2,64,1024]{2,1,0:T(8,128)(2,1)S(1)} %maximum_select_fusion.9), channel_id=1, source_target_pairs={{0,1},{1,0},{2,3},{3,2},{4,5},{5,4},{6,7},{7,6},{8,9},{9,8},{10,11... | collective-permute-start | bytes 786440 | tf_op jit(solution)/shard_map/ppermute | solution.py:174
  124.1 10.5 %collective-permute-start.3 = (bf16[2,64,1024]{2,1,0:T(8,128)(2,1)S(1)}, bf16[2,64,1024]{2,1,0:T(8,128)(2,1)S(1)}, u32[]{:S(2)}, u32[]{:S(2)}) collective-permute-start(bf16[2,64,1024]{2,1,0:T(8,128)(2,1)S(1)} %maximum_select_fusion.8), channel_id=1, source_target_pairs={{0,1},{1,0},{2,3},{3,2},{4,5},{5,4},{6,7},{7,6},{8,9},{9,8},{10,11... | collective-permute-start | bytes 786440 | tf_op jit(solution)/shard_map/ppermute | solution.py:174
  126.9 12.6 %collective-permute-start.31 = (bf16[2,64,1024]{2,1,0:T(8,128)(2,1)S(1)}, bf16[2,64,1024]{2,1,0:T(8,128)(2,1)S(1)}, u32[]{:S(2)}, u32[]{:S(2)}) collective-permute-start(bf16[2,64,1024]{2,1,0:T(8,128)(2,1)S(1)} %maximum_select_fusion.11), channel_id=1, source_target_pairs={{0,1},{1,0},{2,3},{3,2},{4,5},{5,4},{6,7},{7,6},{8,9},{9,8},{10,11... | collective-permute-start | bytes 786440 | tf_op jit(solution)/shard_map/ppermute | solution.py:174
  129.1 15.8 %collective-permute-start.26 = (bf16[2,64,1024]{2,1,0:T(8,128)(2,1)S(1)}, bf16[2,64,1024]{2,1,0:T(8,128)(2,1)S(1)}, u32[]{:S(2)}, u32[]{:S(2)}) collective-permute-start(bf16[2,64,1024]{2,1,0:T(8,128)(2,1)S(1)} %maximum_select_fusion.10), channel_id=1, source_target_pairs={{0,1},{1,0},{2,3},{3,2},{4,5},{5,4},{6,7},{7,6},{8,9},{9,8},{10,11... | collective-permute-start | bytes 786440 | tf_op jit(solution)/shard_map/ppermute | solution.py:174
  134.1 16.0 %collective-permute-start.9 = (bf16[2,64,1024]{2,1,0:T(8,128)(2,1)S(1)}, bf16[2,64,1024]{2,1,0:T(8,128)(2,1)S(1)}, u32[]{:S(2)}, u32[]{:S(2)}) collective-permute-start(bf16[2,64,1024]{2,1,0:T(8,128)(2,1)S(1)} %constant_dynamic-slice_fusion.4), channel_id=1, source_target_pairs={{0,1},{1,0},{2,3},{3,2},{4,5},{5,4},{6,7},{7,6},{8,9},{9,8},{10,11... | collective-permute-start | bytes 786440 | tf_op jit(solution)/shard_map/ppermute | solution.py:174
  139.4 12.5 %collective-permute-start.4 = (bf16[2,64,1024]{2,1,0:T(8,128)(2,1)S(1)}, bf16[2,64,1024]{2,1,0:T(8,128)(2,1)S(1)}, u32[]{:S(2)}, u32[]{:S(2)}) collective-permute-start(bf16[2,64,1024]{2,1,0:T(8,128)(2,1)S(1)} %constant_dynamic-slice_fusion.6), channel_id=1, source_target_pairs={{0,1},{1,0},{2,3},{3,2},{4,5},{5,4},{6,7},{7,6},{8,9},{9,8},{10,11... | collective-permute-start | bytes 786440 | tf_op jit(solution)/shard_map/ppermute | solution.py:174
  144.4 8.0 %collective-permute-start.32 = (bf16[2,64,1024]{2,1,0:T(8,128)(2,1)S(1)}, bf16[2,64,1024]{2,1,0:T(8,128)(2,1)S(1)}, u32[]{:S(2)}, u32[]{:S(2)}) collective-permute-start(bf16[2,64,1024]{2,1,0:T(8,128)(2,1)S(1)} %constant_dynamic-slice_fusion), channel_id=1, source_target_pairs={{0,1},{1,0},{2,3},{3,2},{4,5},{5,4},{6,7},{7,6},{8,9},{9,8},{10,11... | collective-permute-start | bytes 786440 | tf_op jit(solution)/shard_map/ppermute | solution.py:174
  149.9 16.1 %collective-permute-start.27 = (bf16[2,64,1024]{2,1,0:T(8,128)(2,1)S(1)}, bf16[2,64,1024]{2,1,0:T(8,128)(2,1)S(1)}, u32[]{:S(2)}, u32[]{:S(2)}) collective-permute-start(bf16[2,64,1024]{2,1,0:T(8,128)(2,1)S(1)} %constant_dynamic-slice_fusion.2), channel_id=1, source_target_pairs={{0,1},{1,0},{2,3},{3,2},{4,5},{5,4},{6,7},{7,6},{8,9},{9,8},{10,11... | collective-permute-start | bytes 786440 | tf_op jit(solution)/shard_map/ppermute | solution.py:174
  150.1 6.4 %collective-permute-start.11 = (bf16[1,64,1024]{2,1,0:T(8,128)(2,1)S(1)}, bf16[1,64,1024]{2,1,0:T(8,128)(2,1)S(1)}, u32[]{:S(2)}, u32[]{:S(2)}) collective-permute-start(bf16[1,64,1024]{2,1,0:T(8,128)(2,1)S(1)} %dynamic-slice_convert_fusion.6), channel_id=1, source_target_pairs={{0,2},{1,3},{2,0},{3,1},{4,6},{5,7},{6,4},{7,5},{8,10},{9,11},{10,... | collective-permute-start | bytes 393224 | tf_op jit(solution)/shard_map/ppermute | solution.py:174
  152.0 7.3 %collective-permute-start.10 = (bf16[1,64,1024]{2,1,0:T(8,128)(2,1)S(1)}, bf16[1,64,1024]{2,1,0:T(8,128)(2,1)S(1)}, u32[]{:S(2)}, u32[]{:S(2)}) collective-permute-start(bf16[1,64,1024]{2,1,0:T(8,128)(2,1)S(1)} %dynamic-slice_convert_fusion.7), channel_id=1, source_target_pairs={{0,2},{1,3},{2,0},{3,1},{4,6},{5,7},{6,4},{7,5},{8,10},{9,11},{10,... | collective-permute-start | bytes 393224 | tf_op jit(solution)/shard_map/ppermute | solution.py:174
  152.5 18.5 %collective-permute-start.34 = (bf16[1,64,1024]{2,1,0:T(8,128)(2,1)S(1)}, bf16[1,64,1024]{2,1,0:T(8,128)(2,1)S(1)}, u32[]{:S(2)}, u32[]{:S(2)}) collective-permute-start(bf16[1,64,1024]{2,1,0:T(8,128)(2,1)S(1)} %dynamic-slice_convert_fusion.4), channel_id=1, source_target_pairs={{0,2},{1,3},{2,0},{3,1},{4,6},{5,7},{6,4},{7,5},{8,10},{9,11},{10,... | collective-permute-start | bytes 393224 | tf_op jit(solution)/shard_map/ppermute | solution.py:174
  160.2 6.2 %collective-permute-start.12 = (f32[64,128]{1,0:T(8,128)S(1)}, f32[64,128]{1,0:T(8,128)S(1)}, u32[]{:S(2)}, u32[]{:S(2)}) collective-permute-start(f32[64,128]{1,0:T(8,128)S(1)} %get-tuple-element.10.refs_1_), channel_id=1, source_target_pairs={{0,4},{4,8},{8,12},{12,0},{1,5},{5,9},{9,13},{13,1},{2,6},{6,10},{... | collective-permute-start | bytes 98312 | tf_op jit(solution)/shard_map/ppermute | solution.py:221
  162.0 4.9 %collective-permute-start.13 = (f32[64,128]{1,0:T(8,128)S(1)}, f32[64,128]{1,0:T(8,128)S(1)}, u32[]{:S(2)}, u32[]{:S(2)}) collective-permute-start(f32[64,128]{1,0:T(8,128)S(1)} %get-tuple-element.10.refs_1_), channel_id=1, source_target_pairs={{0,8},{4,12},{8,0},{12,4},{1,9},{5,13},{9,1},{13,5},{2,10},{6,14},... | collective-permute-start | bytes 98312 | tf_op jit(solution)/shard_map/ppermute | solution.py:221
  164.6 3.9 %collective-permute-start.14 = (f32[64,128]{1,0:T(8,128)S(1)}, f32[64,128]{1,0:T(8,128)S(1)}, u32[]{:S(2)}, u32[]{:S(2)}) collective-permute-start(f32[64,128]{1,0:T(8,128)S(1)} %get-tuple-element.10.refs_1_), channel_id=1, source_target_pairs={{0,12},{4,0},{8,4},{12,8},{1,13},{5,1},{9,5},{13,9},{2,14},{6,2},{... | collective-permute-start | bytes 98312 | tf_op jit(solution)/shard_map/ppermute | solution.py:221
  168.8 13.8 %collective-permute-start.15 = (bf16[1,64,2048]{2,1,0:T(8,128)(2,1)S(1)}, bf16[1,64,2048]{2,1,0:T(8,128)(2,1)S(1)}, u32[]{:S(2)}, u32[]{:S(2)}) collective-permute-start(bf16[1,64,2048]{2,1,0:T(8,128)(2,1)S(1)} %bitcast.139), channel_id=1, source_target_pairs={{0,2},{1,3},{2,0},{3,1},{4,6},{5,7},{6,4},{7,5},{8,10},{9,11},{10,... | collective-permute-start | bytes 786440 | tf_op jit(solution)/shard_map/ppermute | solution.py:174
  170.4 7.5 %collective-permute-start.33 = (bf16[1,64,1024]{2,1,0:T(8,128)(2,1)S(1)}, bf16[1,64,1024]{2,1,0:T(8,128)(2,1)S(1)}, u32[]{:S(2)}, u32[]{:S(2)}) collective-permute-start(bf16[1,64,1024]{2,1,0:T(8,128)(2,1)S(1)} %dynamic-slice_convert_fusion.5), channel_id=1, source_target_pairs={{0,2},{1,3},{2,0},{3,1},{4,6},{5,7},{6,4},{7,5},{8,10},{9,11},{10,... | collective-permute-start | bytes 393224 | tf_op jit(solution)/shard_map/ppermute | solution.py:174
  178.8 5.7 %collective-permute-start.35 = (f32[64,128]{1,0:T(8,128)S(1)}, f32[64,128]{1,0:T(8,128)S(1)}, u32[]{:S(2)}, u32[]{:S(2)}) collective-permute-start(f32[64,128]{1,0:T(8,128)S(1)} %get-tuple-element.12.refs_1_), channel_id=1, source_target_pairs={{0,4},{4,8},{8,12},{12,0},{1,5},{5,9},{9,13},{13,1},{2,6},{6,10},{... | collective-permute-start | bytes 98312 | tf_op jit(solution)/shard_map/ppermute | solution.py:221
  179.3 5.2 %collective-permute-start.36 = (f32[64,128]{1,0:T(8,128)S(1)}, f32[64,128]{1,0:T(8,128)S(1)}, u32[]{:S(2)}, u32[]{:S(2)}) collective-permute-start(f32[64,128]{1,0:T(8,128)S(1)} %get-tuple-element.12.refs_1_), channel_id=1, source_target_pairs={{0,8},{4,12},{8,0},{12,4},{1,9},{5,13},{9,1},{13,5},{2,10},{6,14},... | collective-permute-start | bytes 98312 | tf_op jit(solution)/shard_map/ppermute | solution.py:221
  182.1 3.9 %collective-permute-start.37 = (f32[64,128]{1,0:T(8,128)S(1)}, f32[64,128]{1,0:T(8,128)S(1)}, u32[]{:S(2)}, u32[]{:S(2)}) collective-permute-start(f32[64,128]{1,0:T(8,128)S(1)} %get-tuple-element.12.refs_1_), channel_id=1, source_target_pairs={{0,12},{4,0},{8,4},{12,8},{1,13},{5,1},{9,5},{13,9},{2,14},{6,2},{... | collective-permute-start | bytes 98312 | tf_op jit(solution)/shard_map/ppermute | solution.py:221
  182.7 10.1 %collective-permute-start.16 = (bf16[2,64,2048]{2,1,0:T(8,128)(2,1)S(1)}, bf16[2,64,2048]{2,1,0:T(8,128)(2,1)S(1)}, u32[]{:S(2)}, u32[]{:S(2)}) collective-permute-start(bf16[2,64,2048]{2,1,0:T(8,128)(2,1)S(1)} %maximum_select_fusion.4), channel_id=1, source_target_pairs={{0,1},{1,0},{2,3},{3,2},{4,5},{5,4},{6,7},{7,6},{8,9},{9,8},{10,11... | collective-permute-start | bytes 1572872 | tf_op jit(solution)/shard_map/ppermute | solution.py:174
  186.2 6.4 %collective-permute-start.38 = (bf16[1,64,2048]{2,1,0:T(8,128)(2,1)S(1)}, bf16[1,64,2048]{2,1,0:T(8,128)(2,1)S(1)}, u32[]{:S(2)}, u32[]{:S(2)}) collective-permute-start(bf16[1,64,2048]{2,1,0:T(8,128)(2,1)S(1)} %bitcast.137), channel_id=1, source_target_pairs={{0,2},{1,3},{2,0},{3,1},{4,6},{5,7},{6,4},{7,5},{8,10},{9,11},{10,... | collective-permute-start | bytes 786440 | tf_op jit(solution)/shard_map/ppermute | solution.py:174
  192.7 10.1 %collective-permute-start.39 = (bf16[2,64,2048]{2,1,0:T(8,128)(2,1)S(1)}, bf16[2,64,2048]{2,1,0:T(8,128)(2,1)S(1)}, u32[]{:S(2)}, u32[]{:S(2)}) collective-permute-start(bf16[2,64,2048]{2,1,0:T(8,128)(2,1)S(1)} %maximum_select_fusion.7), channel_id=1, source_target_pairs={{0,1},{1,0},{2,3},{3,2},{4,5},{5,4},{6,7},{7,6},{8,9},{9,8},{10,11... | collective-permute-start | bytes 1572872 | tf_op jit(solution)/shard_map/ppermute | solution.py:174
  199.1 9.6 %collective-permute-start.17 = (bf16[64,2048]{1,0:T(8,128)(2,1)S(1)}, bf16[64,2048]{1,0:T(8,128)(2,1)S(1)}, u32[]{:S(2)}, u32[]{:S(2)}) collective-permute-start(bf16[64,2048]{1,0:T(8,128)(2,1)S(1)} %get-tuple-element.15), channel_id=1, source_target_pairs={{0,4},{1,5},{2,6},{3,7},{16,20},{17,21},{18,22},{19,23}} | collective-permute-start | bytes 786440 | tf_op jit(solution)/shard_map/ppermute | solution.py:240
  202.1 16.7 %collective-permute-start.20 = (bf16[64,2048]{1,0:T(8,128)(2,1)S(1)}, bf16[64,2048]{1,0:T(8,128)(2,1)S(1)}, u32[]{:S(2)}, u32[]{:S(2)}) collective-permute-start(bf16[64,2048]{1,0:T(8,128)(2,1)S(1)} %get-tuple-element.16), channel_id=1, source_target_pairs={{12,8},{13,9},{14,10},{15,11},{28,24},{29,25},{30,26},{31,27}} | collective-permute-start | bytes 786440 | tf_op jit(solution)/shard_map/ppermute | solution.py:241
  205.6 8.8 %collective-permute-start.40 = (bf16[64,2048]{1,0:T(8,128)(2,1)S(1)}, bf16[64,2048]{1,0:T(8,128)(2,1)S(1)}, u32[]{:S(2)}, u32[]{:S(2)}) collective-permute-start(bf16[64,2048]{1,0:T(8,128)(2,1)S(1)} %get-tuple-element.19), channel_id=1, source_target_pairs={{0,4},{1,5},{2,6},{3,7},{16,20},{17,21},{18,22},{19,23}} | collective-permute-start | bytes 786440 | tf_op jit(solution)/shard_map/ppermute | solution.py:240
  206.9 18.9 %collective-permute-start.43 = (bf16[64,2048]{1,0:T(8,128)(2,1)S(1)}, bf16[64,2048]{1,0:T(8,128)(2,1)S(1)}, u32[]{:S(2)}, u32[]{:S(2)}) collective-permute-start(bf16[64,2048]{1,0:T(8,128)(2,1)S(1)} %get-tuple-element.20), channel_id=1, source_target_pairs={{12,8},{13,9},{14,10},{15,11},{28,24},{29,25},{30,26},{31,27}} | collective-permute-start | bytes 786440 | tf_op jit(solution)/shard_map/ppermute | solution.py:241
  208.8 11.2 %collective-permute-start.18 = (bf16[64,2048]{1,0:T(8,128)(2,1)S(1)}, bf16[64,2048]{1,0:T(8,128)(2,1)S(1)}, u32[]{:S(2)}, u32[]{:S(2)}) collective-permute-start(bf16[64,2048]{1,0:T(8,128)(2,1)S(1)} %fusion.16), channel_id=1, source_target_pairs={{0,4},{4,8},{1,5},{5,9},{2,6},{6,10},{3,7},{7,11},{16,20},{20,24},... | collective-permute-start | bytes 786440 | tf_op jit(solution)/shard_map/ppermute | solution.py:240
  214.4 11.4 %collective-permute-start.41 = (bf16[64,2048]{1,0:T(8,128)(2,1)S(1)}, bf16[64,2048]{1,0:T(8,128)(2,1)S(1)}, u32[]{:S(2)}, u32[]{:S(2)}) collective-permute-start(bf16[64,2048]{1,0:T(8,128)(2,1)S(1)} %fusion.11), channel_id=1, source_target_pairs={{0,4},{4,8},{1,5},{5,9},{2,6},{6,10},{3,7},{7,11},{16,20},{20,24},... | collective-permute-start | bytes 786440 | tf_op jit(solution)/shard_map/ppermute | solution.py:240
  220.1 11.7 %collective-permute-start.21 = (bf16[64,2048]{1,0:T(8,128)(2,1)S(1)}, bf16[64,2048]{1,0:T(8,128)(2,1)S(1)}, u32[]{:S(2)}, u32[]{:S(2)}) collective-permute-start(bf16[64,2048]{1,0:T(8,128)(2,1)S(1)} %get-tuple-element.14), channel_id=1, source_target_pairs={{8,4},{12,8},{9,5},{13,9},{10,6},{14,10},{11,7},{15,11},{24,20},{2... | collective-permute-start | bytes 786440 | tf_op jit(solution)/shard_map/ppermute | solution.py:241
  220.8 13.8 %collective-permute-start.19 = (bf16[64,2048]{1,0:T(8,128)(2,1)S(1)}, bf16[64,2048]{1,0:T(8,128)(2,1)S(1)}, u32[]{:S(2)}, u32[]{:S(2)}) collective-permute-start(bf16[64,2048]{1,0:T(8,128)(2,1)S(1)} %get-tuple-element.13), channel_id=1, source_target_pairs={{0,4},{4,8},{8,12},{1,5},{5,9},{9,13},{2,6},{6,10},{10,14},{3,7},{... | collective-permute-start | bytes 786440 | tf_op jit(solution)/shard_map/ppermute | solution.py:240
  226.0 7.2 %collective-permute-start.44 = (bf16[64,2048]{1,0:T(8,128)(2,1)S(1)}, bf16[64,2048]{1,0:T(8,128)(2,1)S(1)}, u32[]{:S(2)}, u32[]{:S(2)}) collective-permute-start(bf16[64,2048]{1,0:T(8,128)(2,1)S(1)} %get-tuple-element.18), channel_id=1, source_target_pairs={{8,4},{12,8},{9,5},{13,9},{10,6},{14,10},{11,7},{15,11},{24,20},{2... | collective-permute-start | bytes 786440 | tf_op jit(solution)/shard_map/ppermute | solution.py:241
  226.6 17.1 %collective-permute-start.42 = (bf16[64,2048]{1,0:T(8,128)(2,1)S(1)}, bf16[64,2048]{1,0:T(8,128)(2,1)S(1)}, u32[]{:S(2)}, u32[]{:S(2)}) collective-permute-start(bf16[64,2048]{1,0:T(8,128)(2,1)S(1)} %get-tuple-element.17), channel_id=1, source_target_pairs={{0,4},{4,8},{8,12},{1,5},{5,9},{9,13},{2,6},{6,10},{10,14},{3,7},{... | collective-permute-start | bytes 786440 | tf_op jit(solution)/shard_map/ppermute | solution.py:240
  231.9 11.8 %collective-permute-start.22 = (bf16[64,2048]{1,0:T(8,128)(2,1)S(1)}, bf16[64,2048]{1,0:T(8,128)(2,1)S(1)}, u32[]{:S(2)}, u32[]{:S(2)}) collective-permute-start(bf16[64,2048]{1,0:T(8,128)(2,1)S(1)} %fusion.15), channel_id=1, source_target_pairs={{4,0},{8,4},{12,8},{5,1},{9,5},{13,9},{6,2},{10,6},{14,10},{7,3},{... | collective-permute-start | bytes 786440 | tf_op jit(solution)/shard_map/ppermute | solution.py:241
  233.3 13.5 %collective-permute-start.45 = (bf16[64,2048]{1,0:T(8,128)(2,1)S(1)}, bf16[64,2048]{1,0:T(8,128)(2,1)S(1)}, u32[]{:S(2)}, u32[]{:S(2)}) collective-permute-start(bf16[64,2048]{1,0:T(8,128)(2,1)S(1)} %fusion.10), channel_id=1, source_target_pairs={{4,0},{8,4},{12,8},{5,1},{9,5},{13,9},{6,2},{10,6},{14,10},{7,3},{... | collective-permute-start | bytes 786440 | tf_op jit(solution)/shard_map/ppermute | solution.py:241
  (12 other events, 44.8 us)

commit v2 on v0

v2 whole, which is shorter than its diff:
```python
import functools

import jax
import jax.numpy as jnp
import numpy as np
from jax import lax
from jax.experimental import pallas as pl
from jax.experimental.pallas import tpu as pltpu
from jax.sharding import PartitionSpec as P

DH = 128
EPSILON = 1e-05
VMEM_LIMIT = 48 * 1024 * 1024

bf16 = jnp.bfloat16
f32 = jnp.float32


def silu(v):
    u = 0.5 * v
    return u + u * jnp.tanh(u)


def params():
    return pltpu.CompilerParams(vmem_limit_bytes=VMEM_LIMIT)


def cost(flops, moved, transcendentals=0):
    return pl.CostEstimate(flops=flops, bytes_accessed=moved, transcendentals=transcendentals)


def project_kernel(t_ref, w_ref, *refs):
    keep_ref, send_ref, wide_ref, rhs_ref = refs[-4:]
    depth = w_ref.shape[0]
    wide_ref[...] = w_ref.reshape(depth * 4, DH)[...].astype(f32)
    for i in range(4):
        rhs_ref[:, i * DH:(i + 1) * DH] = wide_ref[pl.ds(i, depth, stride=4), :].astype(bf16)
    res = jnp.dot(t_ref[...], rhs_ref[...], preferred_element_type=f32).astype(bf16)
    half, _, each, _ = keep_ref.shape
    for p in range(2 * half):
        into = keep_ref if p < half else send_ref
        for i in range(4):
            into[p % half, i] = res[p * each:(p + 1) * each, i * DH:(i + 1) * DH]


def project(tokens, w, head_first, heads, owners, after):
    rows, depth = tokens.shape
    half, each = owners // 2, rows // owners
    shape = jax.ShapeDtypeStruct((half, 4, each, heads * DH), bf16)
    spec = pl.BlockSpec((half, 4, each, DH), lambda j: (0, 0, 0, j))
    return pl.pallas_call(
        project_kernel,
        grid=(heads,),
        in_specs=[
            pl.BlockSpec((rows, depth), lambda j: (0, 0)),
            pl.BlockSpec((depth, 4, DH), lambda j: (0, 0, head_first + j)),
        ] + [pl.BlockSpec(memory_space=pl.ANY)] * len(after),
        out_specs=(spec, spec),
        out_shape=(shape, shape),
        scratch_shapes=[pltpu.VMEM((depth * 4, DH), f32), pltpu.VMEM((depth, 4 * DH), bf16)],
        compiler_params=params(),
        cost_estimate=cost(
            2 * rows * depth * 4 * heads * DH, depth * 8 * heads * DH + rows * depth * 2
        ),
        name="project",
    )(tokens, w, *after)


def activate_kernel(count, *refs):
    total = sum(r[0].astype(f32) for r in refs[:count])
    q_ref, rest_ref = refs[count:]
    part = silu(total).astype(bf16)
    q_ref[...] = part[0]
    rest_ref[...] = part[1:]


def activate(terms):
    _, _, each, width = terms[0].shape
    return pl.pallas_call(
        functools.partial(activate_kernel, len(terms)),
        grid=(1,),
        in_specs=[pl.BlockSpec((1, 4, each, width), lambda j: (0, 0, 0, 0)) for t in terms],
        out_specs=(
            pl.BlockSpec((each, width), lambda j: (0, 0)),
            pl.BlockSpec((3, each, width), lambda j: (0, 0, 0)),
        ),
        out_shape=(
            jax.ShapeDtypeStruct((each, width), bf16),
            jax.ShapeDtypeStruct((3, each, width), bf16),
        ),
        compiler_params=params(),
        cost_estimate=cost(40 * each * width, 32 * each * width),
        name="activate",
    )(*terms)


def attend_kernel(owners, *refs):
    queries = refs[:owners]
    k_ref, v_ref, lo_ref, hi_ref, keep_ref, send_ref, mask_ref = refs[owners:]
    rows, events = mask_ref.shape
    half, each, _ = keep_ref.shape

    @pl.when(pl.program_id(0) == 0)
    def _():
        at = lax.broadcasted_iota(jnp.int32, (rows, events), 1)
        seen = (at >= lo_ref[...]) & (at < hi_ref[...])
        mask_ref[...] = jnp.where(seen, 1.0, 0.0).astype(bf16)

    query = jnp.concatenate([q[...] for q in queries])
    u = lax.dot_general(
        query, k_ref[...], (((1,), (1,)), ((), ())), preferred_element_type=f32
    ) * (0.5 * DH ** (-0.5))
    weights = (u + u * jnp.tanh(u)).astype(bf16) * mask_ref[...]
    term = jnp.dot(weights, v_ref[...], preferred_element_type=f32).astype(bf16)
    for p in range(owners):
        into = keep_ref if p < half else send_ref
        into[p % half] = term[p * each:(p + 1) * each]


def attend(queries, k_cache, v_cache, lo, hi, head_first, heads):
    owners, (each, width) = len(queries), queries[0].shape
    rows, events, half = owners * each, k_cache.shape[0], owners // 2
    cache = pl.BlockSpec((events, DH), lambda j: (0, head_first + j))
    edge = pl.BlockSpec((rows, 1), lambda j: (0, 0))
    shape = jax.ShapeDtypeStruct((half, each, width), bf16)
    spec = pl.BlockSpec((half, each, DH), lambda j: (0, 0, j))
    return pl.pallas_call(
        functools.partial(attend_kernel, owners),
        grid=(heads,),
        in_specs=[pl.BlockSpec((each, DH), lambda j: (0, j))] * owners + [cache, cache, edge, edge],
        out_specs=(spec, spec),
        out_shape=(shape, shape),
        scratch_shapes=[pltpu.VMEM((rows, events), bf16)],
        compiler_params=params(),
        cost_estimate=cost(
            4 * rows * events * width, 4 * (rows + events) * width, rows * events * heads
        ),
        name="attend",
    )(*queries, k_cache, v_cache, lo, hi)


def finish_kernel(chunks, terms, *refs):
    root_ref, att_ref, stat_ref = refs[0], refs[-2], refs[-1]
    rows = root_ref.shape[0]
    root = root_ref[...]
    total = jnp.zeros((rows, 1), f32)
    column = 0
    for c in range(chunks):
        own = refs[1 + c * (terms + 2):1 + (c + 1) * (terms + 2)]
        sums, q_ref, rest_ref = own[:terms], own[terms], own[terms + 1]
        for h in range(q_ref.shape[1] // DH):
            at = slice(h * DH, (h + 1) * DH)
            summed = sum(s[0, :, at].astype(f32) for s in sums)
            product = q_ref[:, at].astype(f32) * rest_ref[0, :, at].astype(f32)
            weight = silu(jnp.sum(product, axis=1, keepdims=True) * DH ** (-0.5))
            value = summed * root + weight * rest_ref[1, :, at].astype(f32)
            att_ref[:, column:column + DH] = value
            total += jnp.sum(value, axis=1, keepdims=True)
            column += DH
    mean = total / column
    spread = jnp.zeros((rows, DH), f32)
    for first in range(0, column, DH):
        away = att_ref[:, first:first + DH] - mean
        spread += away * away
    square = jnp.sum(spread, axis=1, keepdims=True)
    lane = lax.broadcasted_iota(jnp.int32, (rows, DH), 1)
    stat_ref[...] = jnp.where(lane < DH // 2, mean, square)


def finish(root, chunks):
    rows = root.shape[0]
    width = sum(q.shape[1] for _, q, _ in chunks)
    flat, specs = [root], [pl.BlockSpec((rows, 1), lambda j: (0, 0))]
    for sums, q, rest in chunks:
        span = q.shape[1]
        flat += [*sums, q, rest]
        specs += [pl.BlockSpec((1, rows, span), lambda j: (0, 0, 0))] * len(sums)
        specs += [pl.BlockSpec((rows, span), lambda j: (0, 0))]
        specs += [pl.BlockSpec((2, rows, span), lambda j: (0, 0, 0))]
    return pl.pallas_call(
        functools.partial(finish_kernel, len(chunks), len(chunks[0][0])),
        grid=(1,),
        in_specs=specs,
        out_specs=(
            pl.BlockSpec((rows, width), lambda j: (0, 0)),
            pl.BlockSpec((rows, DH), lambda j: (0, 0)),
        ),
        out_shape=(
            jax.ShapeDtypeStruct((rows, width), f32),
            jax.ShapeDtypeStruct((rows, DH), f32),
        ),
        compiler_params=params(),
        cost_estimate=cost(20 * rows * width, 16 * rows * width),
        name="finish",
    )(*flat)


def gate_kernel(count, chunks, order_ref, *refs):
    att_ref, stats, parts, out_ref = refs[0], refs[1:1 + count], refs[1 + count:-1], refs[-1]
    zs, piece, width = att_ref.shape

    def column(first):
        return [s[..., first:first + 1] for s in stats]

    means, squares = column(0), column(DH // 2)
    mean = sum(means) / count
    square = sum(squares) + width * sum((m - mean) * (m - mean) for m in means)
    scale = lax.rsqrt(square / (width * count) + EPSILON)
    first = 0
    for part in parts:
        span = part.shape[-1]
        at = slice(first, first + span)
        normed = (att_ref[..., at] - mean) * scale
        out_ref[0, ..., at] = (normed * part[0].astype(f32)).astype(bf16)
        first += span


def gate_rows(order, att, stats, rests, zs):
    rows, width = att.shape
    piece = rows // zs

    def split(x):
        return x.reshape(x.shape[:-2] + (zs, piece, x.shape[-1]))

    def spec(x):
        return pl.BlockSpec((1,) + x.shape[1:], lambda j, order: (order[j],) + (0,) * (x.ndim - 1))

    att, stats, rests = split(att), [split(s) for s in stats], [split(r) for r in rests]
    return pl.pallas_call(
        functools.partial(gate_kernel, len(stats), len(rests)),
        grid_spec=pltpu.PrefetchScalarGridSpec(
            num_scalar_prefetch=1,
            grid=(zs,),
            in_specs=[spec(att)] + [spec(s) for s in stats] + [
                pl.BlockSpec((1, 1, piece, r.shape[-1]), lambda j, order: (2, order[j], 0, 0))
                for r in rests
            ],
            out_specs=pl.BlockSpec((1, 1, piece, width), lambda j, order: (j, 0, 0, 0)),
        ),
        out_shape=jax.ShapeDtypeStruct((zs, 1, piece, width), bf16),
        compiler_params=params(),
        cost_estimate=cost(4 * rows * width, 8 * rows * width),
        name="gate",
    )(order, att, *stats, *rests).reshape(zs, piece, width)


def close_kernel(at_ref, t_ref, *refs):
    total = t_ref[...].astype(f32)
    for r in refs[:-1]:
        total = total + r[...].astype(f32)
    refs[-1][...] = total.astype(bf16)


def close(place, first, tokens, terms):
    owners, piece, width = terms[0].shape
    term = pl.BlockSpec((1, piece, width), lambda j, at: (j ^ at[0], 0, 0))
    tokens = tokens.reshape(-1, piece, width)
    return pl.pallas_call(
        close_kernel,
        grid_spec=pltpu.PrefetchScalarGridSpec(
            num_scalar_prefetch=1,
            grid=(owners,),
            in_specs=[pl.BlockSpec((1, piece, width), lambda j, at: (at[1] + j, 0, 0))]
            + [term] * len(terms),
            out_specs=pl.BlockSpec((1, piece, width), lambda j, at: (j, 0, 0)),
        ),
        out_shape=jax.ShapeDtypeStruct((owners, piece, width), bf16),
        compiler_params=params(),
        cost_estimate=cost(4 * owners * piece * width, 10 * owners * piece * width),
        name="close",
    )(jnp.stack([place, first]).astype(jnp.int32), tokens, *terms)


def bits_of(axis):
    count = lax.axis_size(axis)
    assert count & (count - 1) == 0
    return count.bit_length() - 1


def place_of(axis):
    index, bits = lax.axis_index(axis), bits_of(axis)
    return sum((((index >> b) & 1) << (bits - 1 - b) for b in range(bits)), jnp.int32(0))


def swap(x, axis, bit):
    return lax.ppermute(
        x, axis, [(i, i ^ (1 << bit)) for i in range(lax.axis_size(axis))]
    )


def scatter(keep, send, axis):
    terms = [keep, swap(send, axis, 0)]
    for b in range(1, bits_of(axis)):
        half = terms[-1].shape[0] // 2
        total = sum(t[half:2 * half].astype(f32) for t in terms)
        send = total.astype(bf16)
        terms.append(swap(send, axis, b))
    return terms, send


def gather(x, axis):
    blocks = [x]
    for b in reversed(range(bits_of(axis))):
        blocks = blocks + [swap(block, axis, b) for block in blocks]
    return blocks


def all_stats(stat, axis):
    count = lax.axis_size(axis)
    if count > 8:
        every = lax.all_gather(stat, axis)
        return [every[i] for i in range(count)]
    return [stat] + [
        lax.ppermute(stat, axis, [(i, (i + k) % count) for i in range(count)])
        for k in range(1, count)
    ]


def far_first(count):
    return np.array(
        [sorted(range(count), key=lambda c: (-abs(c - i), c)) for i in range(count)], np.int32
    )


def line_scatter(blocks, axis):
    count, index = lax.axis_size(axis), lax.axis_index(axis)
    order = far_first(count)

    def pick(step):
        where = {}
        for i in range(count):
            if 0 <= i + step < count:
                where.setdefault(int(np.argmax(order[i] == i + step)), []).append(i)
        slots = sorted(where)
        out = blocks[slots[0]]
        for s in slots[1:]:
            here = functools.reduce(jnp.logical_or, [index == i for i in where[s]])
            out = jnp.where(here, blocks[s], out)
        return out

    from_left = from_right = None
    for far in range(count - 1, 0, -1):
        right, left = pick(far), pick(-far)
        if from_left is not None:
            right = (right.astype(f32) + from_left.astype(f32)).astype(bf16)
            left = (left.astype(f32) + from_right.astype(f32)).astype(bf16)
        from_left = lax.ppermute(right, axis, [(i, i + 1) for i in range(count - far)])
        from_right = lax.ppermute(left, axis, [(i, i - 1) for i in range(far, count)])
    return [blocks[-1]] + [x for x in (from_left, from_right) if x is not None]


def head_chunks(heads):
    if heads % 8:
        return [1] * heads
    unit = heads // 8
    return [unit, 2 * unit, 2 * unit, 2 * unit, unit]


def local(tokens, w_qkvu, k_cache, v_cache, w_out, vis_start, vis_end):
    cand, depth = tokens.shape
    owners, zs = lax.axis_size("hist"), lax.axis_size("head")
    index, place = lax.axis_index("head"), place_of("hist")
    width = w_qkvu.shape[2]
    events = k_cache.shape[0]
    each = cand // owners
    piece = each // zs

    def arrange(x):
        x = x.reshape((zs, owners, piece) + x.shape[1:])
        blocks = [lax.dynamic_index_in_dim(x, p ^ place, 1, False) for p in range(owners)]
        return jnp.stack(blocks).reshape((cand,) + x.shape[3:])

    ordered = arrange(tokens)
    first_event = lax.axis_index("hist") * events
    edges = arrange(jnp.stack([vis_start, vis_end], axis=1))
    start, end = edges[:, :1], edges[:, 1:]
    low, high = start - first_event, end - first_event
    root = lax.rsqrt((end - start)[:each].astype(f32))

    sizes = head_chunks(width // DH)
    firsts = [sum(sizes[:c]) for c in range(len(sizes))]
    summed, sent = [], []
    for c, (first, heads) in enumerate(zip(firsts, sizes)):
        after = [sent[c - 2]] if c >= 2 else []
        keep, send = project(ordered, w_qkvu, first, heads, owners, after)
        terms, last = scatter(keep, send, "hist")
        summed.append(terms)
        sent.append(last)
    chunks = []
    for terms, first, heads in zip(summed, firsts, sizes):
        query, rest = activate(terms)
        keep, send = attend(gather(query, "hist"), k_cache, v_cache, low, high, first, heads)
        sums, _ = scatter(keep, send, "hist")
        chunks.append((sums, query, rest))
    att, stat = finish(root, chunks)
    order = lax.dynamic_index_in_dim(jnp.asarray(far_first(zs)), index, 0, False)
    stats = all_stats(stat, "head")
    gated = gate_rows(order, att, stats, [rest for _, _, rest in chunks], zs)
    pieces = 2 if zs % 2 == 0 and (zs // 2 * piece) % 16 == 0 else 1
    per = zs // pieces
    blocks = []
    for g in range(pieces):
        part = gated[g * per:(g + 1) * per].reshape(per * piece, width)
        rows = jnp.concatenate(gather(part, "hist"))
        sums = jnp.dot(rows, w_out, preferred_element_type=f32).astype(bf16)
        sums = sums.reshape(owners, per, piece, -1)
        blocks += [sums[:, s] for s in range(per)]
    if zs > 8:
        stacked = jnp.stack(blocks)
        back = jnp.argsort(order)
        whole = jnp.take(stacked, back, axis=0)
        terms = [lax.psum_scatter(whole, "head", scatter_dimension=0, tiled=True)[0]]
    else:
        terms = line_scatter(blocks, "head")
    return close(place, index * owners, tokens, terms).reshape(cand // zs, -1)


def solution(mesh):
    in_specs = (
        P("groups", "hist"),
        P("hist", None, "head"),
        P(("groups", "hist"), "head"),
        P(("groups", "hist"), "head"),
        P("head", "hist"),
        P("groups"),
        P("groups"),
    )
    out_specs = P(("groups", "head"), "hist")
    return jax.shard_map(local, mesh=mesh, in_specs=in_specs, out_specs=out_specs, check_vma=False)
```

time: 369 us -> 217 us (0.59)
  waiting for transfers between devices: 212 us -> 66.2 us
  Pallas kernels: 0 us -> 61.4 us
  starting transfers between devices: 0.57 us -> 51.3 us
  local copies, waits for them, and re-layouts: 58.8 us -> 14.3 us
  matrix products: 47.3 us -> 11.5 us
  blocking collectives: 20 us -> 0 us
  between operations: 13.2 us -> 0.61 us
  other arithmetic: 16.3 us -> 11 us
    psum x1 -> x0, waiting for transfers between devices: 86.7 us -> none  [local(): lax.psum(whole_out.astype(jnp.bfloat16), 'head').astype(jnp.float32)]
    ppermute x0 -> x50, waiting for transfers between devices: none -> 66.2 us  [the longest x41 41.4 us: swap(): lax.ppermute(x, axis, [(i, i ^ 1 << bit) for i in range(lax.axis_size(axi...]
    all_gather x3 -> x0, waiting for transfers between devices: 62.7 us -> none  [the longest x1 40.4 us: local(): lax.all_gather(k_cache, 'hist', axis=0, tiled=True)]
    reduce_scatter x1 -> x0, waiting for transfers between devices: 61.9 us -> none  [local(): lax.psum_scatter(jnp.dot(tokens, flat_weight, preferred_element_type=jnp....]
    pallas_call x0 -> x18, Pallas kernels: none -> 61.4 us  [the longest x5 37.4 us: project(): pl.pallas_call(project_kernel, grid=(heads,), in_specs=[pl.BlockSpec((row...]
    ppermute x0 -> x50, starting transfers between devices: none -> 51.3 us  [the longest x41 25.4 us: swap(): lax.ppermute(x, axis, [(i, i ^ 1 << bit) for i in range(lax.axis_size(axi...]
    dot_general x3 -> x2, matrix products: 47.3 us -> 11.5 us  [local(): sums = jnp.dot(rows, w_out, preferred_element_type=f32).astype(bf16)]
    unnamed x10 -> x75, local copies, waits for them, and re-layouts: 39.9 us -> 9.98 us
  transfers between devices with their start and end apart: 5 -> 50, of which waited for: 5 -> 14; matrix products, arithmetic and copies ran while one was open for 25% -> 8% of each run, Pallas kernels for 0% -> 23%
where the time goes in v2:
time: 217 us; the launch traced here: 216 us
  waiting for transfers between devices  66.2 us (31%)
  Pallas kernels  61.4 us (28%)
  starting transfers between devices  51.3 us (24%)
  local copies, waits for them, and re-layouts  14.3 us (7%)
  matrix products  11.5 us (5%)
  other arithmetic  11 us (5%)
    ppermute x41, waiting for transfers between devices, swap(): lax.ppermute(x, axis, [(i, i ^ 1 << bit) for i in range(lax.axis_size(axi...  41.4 us
    pallas_call x5, Pallas kernels, project(): pl.pallas_call(project_kernel, grid=(heads,), in_specs=[pl.BlockSpec((row...  37.4 us
    ppermute x41, starting transfers between devices, swap(): lax.ppermute(x, axis, [(i, i ^ 1 << bit) for i in range(lax.axis_size(axi...  25.4 us
    ppermute x3, waiting for transfers between devices, line_scatter(): lax.ppermute(right, axis, [(i, i + 1) for i in range(count - far)])  22.3 us
    ppermute x3, starting transfers between devices, line_scatter(): lax.ppermute(right, axis, [(i, i + 1) for i in range(count - far)])  17.2 us
    pallas_call x5, Pallas kernels, attend(): pl.pallas_call(functools.partial(attend_kernel, owners), grid=(heads,), i...  12.9 us
    dot_general x2, matrix products, local(): sums = jnp.dot(rows, w_out, preferred_element_type=f32).astype(bf16)  11.5 us
    unnamed x75, local copies, waits for them, and re-layouts  9.98 us
  transfers between devices with their start and end apart: 50, of which 14 were waited for; matrix products, arithmetic and copies ran while one was open for 8% of the time, Pallas kernels for 23%

profile of v2, /device:TPU:0, one launch (start us, length us, event | category | flops | bytes accessed | tf_op | source)
XLA Modules:
  0.0 216.3 jit_solution(12310709868342915873)
XLA Ops:
  0.0 1.7 dynamic-slice_bitcast_fusion.3
  1.9 5.0 %project.5 = (bf16[2,4,128,256]{3,2,1,0:T(8,128)(2,1)S(1)}, bf16[2,4,128,256]{3,2,1,0:T(8,128)(2,1)S(1)}) custom-call(bf16[512,2048]{1,0:T(8,128)(2,1)S(1)} %bitcast.67, bf16[2048,4,2048]{2,1,0:T(4,128)(2,1)} %w_ref.9), custom_call_target="tpu_custom_call" | custom-call | flops 2147483648 | bytes 6291456 | tf_op jit(solution)/shard_map/project/pallas_call | solution.py:51
  7.5 8.4 %project.6 = (bf16[2,4,128,512]{3,2,1,0:T(8,128)(2,1)S(1)}, bf16[2,4,128,512]{3,2,1,0:T(8,128)(2,1)S(1)}) custom-call(bf16[512,2048]{1,0:T(8,128)(2,1)S(1)} %bitcast.68, bf16[2048,4,2048]{2,1,0:T(4,128)(2,1)} %w_ref.9), custom_call_target="tpu_custom_call" | custom-call | flops 4294967296 | bytes 10485760 | tf_op jit(solution)/shard_map/project/pallas_call | solution.py:51
  17.1 9.0 %project.7 = (bf16[2,4,128,512]{3,2,1,0:T(8,128)(2,1)S(1)}, bf16[2,4,128,512]{3,2,1,0:T(8,128)(2,1)}) custom-call(bf16[512,2048]{1,0:T(8,128)(2,1)S(1)} %bitcast.69, bf16[2048,4,2048]{2,1,0:T(4,128)(2,1)} %w_ref.9, bf16[1,4,128,256]{3,2,1,0:T(8,128)(2,1)S(1)} %add_convert_fusion.8.refs_0_), custom_call_target="tpu_custom_call" | custom-call | flops 4294967296 | bytes 10485760 | tf_op jit(solution)/shard_map/project/pallas_call | solution.py:51
  27.5 9.4 %project.8 = (bf16[2,4,128,512]{3,2,1,0:T(8,128)(2,1)S(1)}, bf16[2,4,128,512]{3,2,1,0:T(8,128)(2,1)}) custom-call(bf16[512,2048]{1,0:T(8,128)(2,1)S(1)} %bitcast.70, bf16[2048,4,2048]{2,1,0:T(4,128)(2,1)} %w_ref.9, bf16[1,4,128,512]{3,2,1,0:T(8,128)(2,1)S(1)} %add_convert_fusion.6.refs_0_), custom_call_target="tpu_custom_call" | custom-call | flops 4294967296 | bytes 10485760 | tf_op jit(solution)/shard_map/project/pallas_call | solution.py:51
  37.3 2.8 %collective-permute-start.1 = (bf16[1,4,128,256]{3,2,1,0:T(8,128)(2,1)S(1)}, bf16[1,4,128,256]{3,2,1,0:T(8,128)(2,1)S(1)}, u32[]{:S(2)}, u32[]{:S(2)}) collective-permute-start(bf16[1,4,128,256]{3,2,1,0:T(8,128)(2,1)S(1)} %add_convert_fusion.8.refs_0_), channel_id=1, source_target_pairs={{0,2},{1,3},{2,0},{3,1},{4,6},{5,7},{6,4},{7,5},{8,10},{9,11},{10,... | collective-permute-start | bytes 786440 | tf_op jit(solution)/shard_map/ppermute | solution.py:286
  40.1 2.2 %add_convert_fusion.5.refs_0_ = bf16[1,4,128,512]{3,2,1,0:T(8,128)(2,1)} fusion(bf16[2,4,128,512]{3,2,1,0:T(8,128)(2,1)} %collective-permute-done.14.refs_1_, bf16[2,4,128,512]{3,2,1,0:T(8,128)(2,1)} %copy-done.3), kind=kLoop, calls=%fused_computation.22 | loop fusion | flops 1048576 | bytes 1572864 | tf_op jit(solution)/shard_map/convert_element_type | solution.py:296
  42.3 5.7 %project.9 = (bf16[2,4,128,256]{3,2,1,0:T(8,128)(2,1)S(1)}, bf16[2,4,128,256]{3,2,1,0:T(8,128)(2,1)}) custom-call(bf16[512,2048]{1,0:T(8,128)(2,1)S(1)} %bitcast.71, bf16[2048,4,2048]{2,1,0:T(4,128)(2,1)} %w_ref.9, bf16[1,4,128,512]{3,2,1,0:T(8,128)(2,1)} %add_convert_fusion.5.refs_0_), custom_call_target="tpu_custom_call" | custom-call | flops 2147483648 | bytes 6291456 | tf_op jit(solution)/shard_map/project/pallas_call | solution.py:51
  49.1 2.0 collective-permute-start.2
  52.1 7.7 %collective-permute-done.2.refs_1_ = bf16[128,256]{1,0:T(8,128)(2,1)S(1)} collective-permute-done((bf16[128,256]{1,0:T(8,128)(2,1)S(1)}, bf16[128,256]{1,0:T(8,128)(2,1)S(1)}, u32[]{:S(2)}, u32[]{:S(2)}) %collective-permute-start.2) | collective-permute-done | bytes 65568 | tf_op jit(solution)/shard_map/ppermute | solution.py:286
  61.5 1.4 activate.6
  63.0 2.1 collective-permute-start.9
  66.7 7.2 %collective-permute-done.9.refs_1_ = bf16[128,512]{1,0:T(8,128)(2,1)S(1)} collective-permute-done((bf16[128,512]{1,0:T(8,128)(2,1)S(1)}, bf16[128,512]{1,0:T(8,128)(2,1)S(1)}, u32[]{:S(2)}, u32[]{:S(2)}) %collective-permute-start.9) | collective-permute-done | bytes 131104 | tf_op jit(solution)/shard_map/ppermute | solution.py:286
  73.8 2.1 collective-permute-start.29
  76.1 1.7 activate.7
  78.4 1.7 attend.5
  80.5 3.1 %attend.6 = (bf16[2,128,512]{2,1,0:T(8,128)(2,1)S(1)}, bf16[2,128,512]{2,1,0:T(8,128)(2,1)S(1)}) custom-call(bf16[128,512]{1,0:T(8,128)(2,1)S(1)} %get-tuple-element.45.refs_0_.refs_9_, bf16[128,512]{1,0:T(8,128)(2,1)S(1)} %collective-permute-done.9.refs_1_, bf16[128,512]{1,0:T(8,128)(2,1)S(1)} %collective-permute-done.10.refs_2_, ...), custom_call_target="tpu_custom_call" | custom-call | flops 536870912 | bytes 2097152 | tf_op jit(solution)/shard_map/attend/pallas_call | solution.py:127
  84.0 9.2 %collective-permute-done.16.refs_1_ = bf16[128,512]{1,0:T(8,128)(2,1)S(1)} collective-permute-done((bf16[128,512]{1,0:T(8,128)(2,1)S(1)}, bf16[128,512]{1,0:T(8,128)(2,1)S(1)}, u32[]{:S(2)}, u32[]{:S(2)}) %collective-permute-start.16) | collective-permute-done | bytes 131104 | tf_op jit(solution)/shard_map/ppermute | solution.py:286
  93.8 1.8 collective-permute-start.30
  95.6 1.4 activate.8
  98.1 3.2 %attend.7 = (bf16[2,128,512]{2,1,0:T(8,128)(2,1)S(1)}, bf16[2,128,512]{2,1,0:T(8,128)(2,1)S(1)}) custom-call(bf16[128,512]{1,0:T(8,128)(2,1)S(1)} %get-tuple-element.51.refs_0_.refs_14_, bf16[128,512]{1,0:T(8,128)(2,1)S(1)} %collective-permute-done.16.refs_1_, bf16[128,512]{1,0:T(8,128)(2,1)S(1)} %collective-permute-done.17.refs_2_, ...), custom_call_target="tpu_custom_call" | custom-call | flops 536870912 | bytes 2097152 | tf_op jit(solution)/shard_map/attend/pallas_call | solution.py:127
  103.1 1.7 collective-permute-start.6
  105.1 1.7 attend.9
  107.0 3.2 %attend.8 = (bf16[2,128,512]{2,1,0:T(8,128)(2,1)S(1)}, bf16[2,128,512]{2,1,0:T(8,128)(2,1)S(1)}) custom-call(bf16[128,512]{1,0:T(8,128)(2,1)S(1)} %get-tuple-element.57.refs_0_.refs_19_, bf16[128,512]{1,0:T(8,128)(2,1)S(1)} %collective-permute-done.23.refs_1_, bf16[128,512]{1,0:T(8,128)(2,1)S(1)} %collective-permute-done.24.refs_2_, ...), custom_call_target="tpu_custom_call" | custom-call | flops 536870912 | bytes 2097152 | tf_op jit(solution)/shard_map/attend/pallas_call | solution.py:127
  111.4 1.7 collective-permute-start.20
  114.8 1.7 collective-permute-start.27
  117.2 2.0 collective-permute-done.34.refs_23_
  119.2 2.2 %collective-permute-done.27.refs_18_ = bf16[1,128,512]{2,1,0:T(8,128)(2,1)} collective-permute-done((bf16[1,128,512]{2,1,0:T(8,128)(2,1)}, bf16[1,128,512]{2,1,0:T(8,128)(2,1)}, u32[]{:S(2)}, u32[]{:S(2)}) %collective-permute-start.27) | collective-permute-done | bytes 131104 | tf_op jit(solution)/shard_map/ppermute | solution.py:286
  126.7 2.7 %finish.1 = (f32[128,2048]{1,0:T(8,128)S(1)}, f32[128,128]{1,0:T(8,128)S(1)}) custom-call(f32[128,1]{1,0:T(8,128)S(1)} %copy-done.32, bf16[2,128,256]{2,1,0:T(8,128)(2,1)S(1)} %copy-done.25, bf16[2,128,256]{2,1,0:T(8,128)(2,1)S(1)} %copy-done.27, bf16[1,128,256]{2,1,0:T(8,128)(2,1)} %collective-permute-done.6.refs_3_, ...), custom_call_target="tpu_custom_call" | custom-call | flops 5242880 | bytes 4194304 | tf_op jit(solution)/shard_map/finish/pallas_call | solution.py:180
  129.5 1.9 collective-permute-start.35
  131.3 2.6 %collective-permute-start.36 = (f32[128,128]{1,0:T(8,128)S(1)}, f32[128,128]{1,0:T(8,128)S(1)}, u32[]{:S(2)}, u32[]{:S(2)}) collective-permute-start(f32[128,128]{1,0:T(8,128)S(1)} %get-tuple-element.68), channel_id=1, source_target_pairs={{0,8},{4,12},{8,0},{12,4},{1,9},{5,13},{9,1},{13,5},{2,10},{6,14},... | collective-permute-start | bytes 196616 | tf_op jit(solution)/shard_map/ppermute | solution.py:314
  136.4 2.0 collective-permute-done.36
  138.5 1.4 gate.1
  140.0 1.6 collective-permute-start.41
  141.6 4.9 %collective-permute-done.41 = bf16[64,2048]{1,0:T(8,128)(2,1)S(1)} collective-permute-done((bf16[64,2048]{1,0:T(8,128)(2,1)S(1)}, bf16[64,2048]{1,0:T(8,128)(2,1)S(1)}, u32[]{:S(2)}, u32[]{:S(2)}) %collective-permute-start.41) | collective-permute-done | bytes 262176 | tf_op jit(solution)/shard_map/ppermute | solution.py:286
  146.5 1.5 collective-permute-done.43
  148.0 5.7 %convolution_convert_fusion = bf16[256,2048]{1,0:T(8,128)(2,1)S(1)} fusion(bf16[2048,2048]{1,0:T(8,128)(2,1)} %param.12, bf16[64,2048]{1,0:T(8,128)(2,1)S(1)} %collective-permute-done.43, bf16[64,2048]{1,0:T(8,128)(2,1)S(1)} %collective-permute-done.42, bf16[64,2048]{1,0:T(8,128)(2,1)S(1)} %collective-permute-done.41, bf16[64,2048]{1,0:T(8,128)(2,1)S(1)} %bitcast.96), kind=kOutput, calls=%fused_computation | convolution fusion | flops 2152202240 | bytes 10485760 | tf_op jit(solution)/shard_map/dot_general | solution.py:405
  155.3 1.7 collective-permute-start.38
  157.0 6.7 %collective-permute-done.38 = bf16[64,2048]{1,0:T(8,128)(2,1)S(1)} collective-permute-done((bf16[64,2048]{1,0:T(8,128)(2,1)S(1)}, bf16[64,2048]{1,0:T(8,128)(2,1)S(1)}, u32[]{:S(2)}, u32[]{:S(2)}) %collective-permute-start.38) | collective-permute-done | bytes 262176 | tf_op jit(solution)/shard_map/ppermute | solution.py:286
  163.7 3.8 %collective-permute-start.44 = (bf16[4,32,2048]{2,1,0:T(8,128)(2,1)}, bf16[4,32,2048]{2,1,0:T(8,128)(2,1)S(1)}, u32[]{:S(2)}, u32[]{:S(2)}) collective-permute-start(bf16[4,32,2048]{2,1,0:T(8,128)(2,1)} %slice_bitcast_fusion), channel_id=1, source_target_pairs={{0,4},{1,5},{2,6},{3,7},{16,20},{17,21},{18,22},{19,23}} | collective-permute-start | bytes 1572872 | tf_op jit(solution)/shard_map/ppermute | solution.py:347
  168.7 5.8 %convolution_convert_fusion.1 = bf16[256,2048]{1,0:T(8,128)(2,1)S(1)} fusion(bf16[2048,2048]{1,0:T(8,128)(2,1)} %param.12, bf16[64,2048]{1,0:T(8,128)(2,1)S(1)} %collective-permute-done.40, bf16[64,2048]{1,0:T(8,128)(2,1)S(1)} %collective-permute-done.39, bf16[64,2048]{1,0:T(8,128)(2,1)} %copy-done.36, bf16[64,2048]{1,0:T(8,128)(2,1)S(1)} %bitcast.93), kind=kOutput, calls=%fused_computation.1 | convolution fusion | flops 2152202240 | bytes 10485760 | tf_op jit(solution)/shard_map/dot_general | solution.py:405
  174.5 5.1 %collective-permute-done.44 = bf16[4,32,2048]{2,1,0:T(8,128)(2,1)S(1)} collective-permute-done((bf16[4,32,2048]{2,1,0:T(8,128)(2,1)}, bf16[4,32,2048]{2,1,0:T(8,128)(2,1)S(1)}, u32[]{:S(2)}, u32[]{:S(2)}) %collective-permute-start.44) | collective-permute-done | bytes 524320 | tf_op jit(solution)/shard_map/ppermute | solution.py:347
  179.6 1.4 add_convert_fusion
  181.1 9.0 %collective-permute-start.45 = (bf16[4,32,2048]{2,1,0:T(8,128)(2,1)}, bf16[4,32,2048]{2,1,0:T(8,128)(2,1)}, u32[]{:S(2)}, u32[]{:S(2)}) collective-permute-start(bf16[4,32,2048]{2,1,0:T(8,128)(2,1)} %get-tuple-element.74), channel_id=1, source_target_pairs={{0,4},{4,8},{1,5},{5,9},{2,6},{6,10},{3,7},{7,11},{16,20},{20,24},... | collective-permute-start | bytes 1572872 | tf_op jit(solution)/shard_map/ppermute | solution.py:347
  191.3 8.2 %collective-permute-done.45 = bf16[4,32,2048]{2,1,0:T(8,128)(2,1)} collective-permute-done((bf16[4,32,2048]{2,1,0:T(8,128)(2,1)}, bf16[4,32,2048]{2,1,0:T(8,128)(2,1)}, u32[]{:S(2)}, u32[]{:S(2)}) %collective-permute-start.45) | collective-permute-done | bytes 524320 | tf_op jit(solution)/shard_map/ppermute | solution.py:347
  200.7 4.4 %collective-permute-start.46 = (bf16[4,32,2048]{2,1,0:T(8,128)(2,1)S(1)}, bf16[4,32,2048]{2,1,0:T(8,128)(2,1)S(1)}, u32[]{:S(2)}, u32[]{:S(2)}) collective-permute-start(bf16[4,32,2048]{2,1,0:T(8,128)(2,1)S(1)} %add_convert_fusion.2), channel_id=1, source_target_pairs={{0,4},{4,8},{8,12},{1,5},{5,9},{9,13},{2,6},{6,10},{10,14},{3,7},{... | collective-permute-start | bytes 1572872 | tf_op jit(solution)/shard_map/ppermute | solution.py:347
  205.3 8.9 %collective-permute-done.46.refs_1_ = bf16[4,32,2048]{2,1,0:T(8,128)(2,1)S(1)} collective-permute-done((bf16[4,32,2048]{2,1,0:T(8,128)(2,1)S(1)}, bf16[4,32,2048]{2,1,0:T(8,128)(2,1)S(1)}, u32[]{:S(2)}, u32[]{:S(2)}) %collective-permute-start.46) | collective-permute-done | bytes 524320 | tf_op jit(solution)/shard_map/ppermute | solution.py:347
  214.2 2.1 close.1
  (175 shorter events, 31.3 us)
Async XLA Ops:
  7.0 9.1 %collective-permute-start = (bf16[2,4,128,256]{3,2,1,0:T(8,128)(2,1)S(1)}, bf16[2,4,128,256]{3,2,1,0:T(8,128)(2,1)S(1)}, u32[]{:S(2)}, u32[]{:S(2)}) collective-permute-start(bf16[2,4,128,256]{3,2,1,0:T(8,128)(2,1)S(1)} %get-tuple-element.38), channel_id=1, source_target_pairs={{0,1},{1,0},{2,3},{3,2},{4,5},{5,4},{6,7},{7,6},{8,9},{9,8},{10,11... | collective-permute-start | bytes 1572872 | tf_op jit(solution)/shard_map/ppermute | solution.py:286
  15.9 11.4 %collective-permute-start.7 = (bf16[2,4,128,512]{3,2,1,0:T(8,128)(2,1)S(1)}, bf16[2,4,128,512]{3,2,1,0:T(8,128)(2,1)S(1)}, u32[]{:S(2)}, u32[]{:S(2)}) collective-permute-start(bf16[2,4,128,512]{3,2,1,0:T(8,128)(2,1)S(1)} %get-tuple-element.44), channel_id=1, source_target_pairs={{0,1},{1,0},{2,3},{3,2},{4,5},{5,4},{6,7},{7,6},{8,9},{9,8},{10,11... | collective-permute-start | bytes 3145736 | tf_op jit(solution)/shard_map/ppermute | solution.py:286
  27.1 13.1 %collective-permute-start.14 = (bf16[2,4,128,512]{3,2,1,0:T(8,128)(2,1)}, bf16[2,4,128,512]{3,2,1,0:T(8,128)(2,1)}, u32[]{:S(2)}, u32[]{:S(2)}) collective-permute-start(bf16[2,4,128,512]{3,2,1,0:T(8,128)(2,1)} %get-tuple-element.50), channel_id=1, source_target_pairs={{0,1},{1,0},{2,3},{3,2},{4,5},{5,4},{6,7},{7,6},{8,9},{9,8},{10,11... | collective-permute-start | bytes 3145736 | tf_op jit(solution)/shard_map/ppermute | solution.py:286
  36.9 26.1 %collective-permute-start.21 = (bf16[2,4,128,512]{3,2,1,0:T(8,128)(2,1)}, bf16[2,4,128,512]{3,2,1,0:T(8,128)(2,1)}, u32[]{:S(2)}, u32[]{:S(2)}) collective-permute-start(bf16[2,4,128,512]{3,2,1,0:T(8,128)(2,1)} %get-tuple-element.56), channel_id=1, source_target_pairs={{0,1},{1,0},{2,3},{3,2},{4,5},{5,4},{6,7},{7,6},{8,9},{9,8},{10,11... | collective-permute-start | bytes 3145736 | tf_op jit(solution)/shard_map/ppermute | solution.py:286
  37.3 11.6 %collective-permute-start.1 = (bf16[1,4,128,256]{3,2,1,0:T(8,128)(2,1)S(1)}, bf16[1,4,128,256]{3,2,1,0:T(8,128)(2,1)S(1)}, u32[]{:S(2)}, u32[]{:S(2)}) collective-permute-start(bf16[1,4,128,256]{3,2,1,0:T(8,128)(2,1)S(1)} %add_convert_fusion.8.refs_0_), channel_id=1, source_target_pairs={{0,2},{1,3},{2,0},{3,1},{4,6},{5,7},{6,4},{7,5},{8,10},{9,11},{10,... | collective-permute-start | bytes 786440 | tf_op jit(solution)/shard_map/ppermute | solution.py:286
  40.1 19.7 %collective-permute-start.8 = (bf16[1,4,128,512]{3,2,1,0:T(8,128)(2,1)}, bf16[1,4,128,512]{3,2,1,0:T(8,128)(2,1)}, u32[]{:S(2)}, u32[]{:S(2)}) collective-permute-start(bf16[1,4,128,512]{3,2,1,0:T(8,128)(2,1)} %copy-done.9), channel_id=1, source_target_pairs={{0,2},{1,3},{2,0},{3,1},{4,6},{5,7},{6,4},{7,5},{8,10},{9,11},{10,... | collective-permute-start | bytes 1572872 | tf_op jit(solution)/shard_map/ppermute | solution.py:286
  48.8 17.5 %collective-permute-start.28 = (bf16[2,4,128,256]{3,2,1,0:T(8,128)(2,1)}, bf16[2,4,128,256]{3,2,1,0:T(8,128)(2,1)S(1)}, u32[]{:S(2)}, u32[]{:S(2)}) collective-permute-start(bf16[2,4,128,256]{3,2,1,0:T(8,128)(2,1)} %get-tuple-element.62), channel_id=1, source_target_pairs={{0,1},{1,0},{2,3},{3,2},{4,5},{5,4},{6,7},{7,6},{8,9},{9,8},{10,11... | collective-permute-start | bytes 1572872 | tf_op jit(solution)/shard_map/ppermute | solution.py:286
  49.1 10.7 %collective-permute-start.2 = (bf16[128,256]{1,0:T(8,128)(2,1)S(1)}, bf16[128,256]{1,0:T(8,128)(2,1)S(1)}, u32[]{:S(2)}, u32[]{:S(2)}) collective-permute-start(bf16[128,256]{1,0:T(8,128)(2,1)S(1)} %get-tuple-element.39.refs_0_.refs_4_), channel_id=1, source_target_pairs={{0,2},{1,3},{2,0},{3,1},{4,6},{5,7},{6,4},{7,5},{8,10},{9,11},{10,... | collective-permute-start | bytes 196616 | tf_op jit(solution)/shard_map/ppermute | solution.py:286
  51.1 22.7 %collective-permute-start.15 = (bf16[1,4,128,512]{3,2,1,0:T(8,128)(2,1)}, bf16[1,4,128,512]{3,2,1,0:T(8,128)(2,1)}, u32[]{:S(2)}, u32[]{:S(2)}) collective-permute-start(bf16[1,4,128,512]{3,2,1,0:T(8,128)(2,1)} %add_convert_fusion.5.refs_0_), channel_id=1, source_target_pairs={{0,2},{1,3},{2,0},{3,1},{4,6},{5,7},{6,4},{7,5},{8,10},{9,11},{10,... | collective-permute-start | bytes 1572872 | tf_op jit(solution)/shard_map/ppermute | solution.py:286
  59.8 6.8 %collective-permute-start.3 = (bf16[128,256]{1,0:T(8,128)(2,1)S(1)}, bf16[128,256]{1,0:T(8,128)(2,1)S(1)}, u32[]{:S(2)}, u32[]{:S(2)}) collective-permute-start(bf16[128,256]{1,0:T(8,128)(2,1)S(1)} %get-tuple-element.39.refs_0_.refs_4_), channel_id=1, source_target_pairs={{0,1},{1,0},{2,3},{3,2},{4,5},{5,4},{6,7},{7,6},{8,9},{9,8},{10,11... | collective-permute-start | bytes 196616 | tf_op jit(solution)/shard_map/ppermute | solution.py:286
  59.8 18.0 %collective-permute-start.4 = (bf16[128,256]{1,0:T(8,128)(2,1)S(1)}, bf16[128,256]{1,0:T(8,128)(2,1)S(1)}, u32[]{:S(2)}, u32[]{:S(2)}) collective-permute-start(bf16[128,256]{1,0:T(8,128)(2,1)S(1)} %collective-permute-done.2.refs_1_), channel_id=1, source_target_pairs={{0,1},{1,0},{2,3},{3,2},{4,5},{5,4},{6,7},{7,6},{8,9},{9,8},{10,11... | collective-permute-start | bytes 196616 | tf_op jit(solution)/shard_map/ppermute | solution.py:286
  63.0 10.8 %collective-permute-start.9 = (bf16[128,512]{1,0:T(8,128)(2,1)S(1)}, bf16[128,512]{1,0:T(8,128)(2,1)S(1)}, u32[]{:S(2)}, u32[]{:S(2)}) collective-permute-start(bf16[128,512]{1,0:T(8,128)(2,1)S(1)} %get-tuple-element.45.refs_0_.refs_9_), channel_id=1, source_target_pairs={{0,2},{1,3},{2,0},{3,1},{4,6},{5,7},{6,4},{7,5},{8,10},{9,11},{10,... | collective-permute-start | bytes 393224 | tf_op jit(solution)/shard_map/ppermute | solution.py:286
  66.3 27.5 %collective-permute-start.22 = (bf16[1,4,128,512]{3,2,1,0:T(8,128)(2,1)S(1)}, bf16[1,4,128,512]{3,2,1,0:T(8,128)(2,1)S(1)}, u32[]{:S(2)}, u32[]{:S(2)}) collective-permute-start(bf16[1,4,128,512]{3,2,1,0:T(8,128)(2,1)S(1)} %add_convert_fusion.4), channel_id=1, source_target_pairs={{0,2},{1,3},{2,0},{3,1},{4,6},{5,7},{6,4},{7,5},{8,10},{9,11},{10,... | collective-permute-start | bytes 1572872 | tf_op jit(solution)/shard_map/ppermute | solution.py:286
  66.6 13.6 %collective-permute-start.10 = (bf16[128,512]{1,0:T(8,128)(2,1)S(1)}, bf16[128,512]{1,0:T(8,128)(2,1)S(1)}, u32[]{:S(2)}, u32[]{:S(2)}) collective-permute-start(bf16[128,512]{1,0:T(8,128)(2,1)S(1)} %get-tuple-element.45.refs_0_.refs_9_), channel_id=1, source_target_pairs={{0,1},{1,0},{2,3},{3,2},{4,5},{5,4},{6,7},{7,6},{8,9},{9,8},{10,11... | collective-permute-start | bytes 393224 | tf_op jit(solution)/shard_map/ppermute | solution.py:286
  73.8 6.7 %collective-permute-start.11 = (bf16[128,512]{1,0:T(8,128)(2,1)S(1)}, bf16[128,512]{1,0:T(8,128)(2,1)S(1)}, u32[]{:S(2)}, u32[]{:S(2)}) collective-permute-start(bf16[128,512]{1,0:T(8,128)(2,1)S(1)} %collective-permute-done.9.refs_1_), channel_id=1, source_target_pairs={{0,1},{1,0},{2,3},{3,2},{4,5},{5,4},{6,7},{7,6},{8,9},{9,8},{10,11... | collective-permute-start | bytes 393224 | tf_op jit(solution)/shard_map/ppermute | solution.py:286
  73.8 19.3 %collective-permute-start.29 = (bf16[1,4,128,256]{3,2,1,0:T(8,128)(2,1)S(1)}, bf16[1,4,128,256]{3,2,1,0:T(8,128)(2,1)S(1)}, u32[]{:S(2)}, u32[]{:S(2)}) collective-permute-start(bf16[1,4,128,256]{3,2,1,0:T(8,128)(2,1)S(1)} %add_convert_fusion.7), channel_id=1, source_target_pairs={{0,2},{1,3},{2,0},{3,1},{4,6},{5,7},{6,4},{7,5},{8,10},{9,11},{10,... | collective-permute-start | bytes 786440 | tf_op jit(solution)/shard_map/ppermute | solution.py:286
  77.8 15.4 %collective-permute-start.16 = (bf16[128,512]{1,0:T(8,128)(2,1)S(1)}, bf16[128,512]{1,0:T(8,128)(2,1)S(1)}, u32[]{:S(2)}, u32[]{:S(2)}) collective-permute-start(bf16[128,512]{1,0:T(8,128)(2,1)S(1)} %get-tuple-element.51.refs_0_.refs_14_), channel_id=1, source_target_pairs={{0,2},{1,3},{2,0},{3,1},{4,6},{5,7},{6,4},{7,5},{8,10},{9,11},{10,... | collective-permute-start | bytes 393224 | tf_op jit(solution)/shard_map/ppermute | solution.py:286
  80.2 16.8 %collective-permute-start.5 = (bf16[2,128,256]{2,1,0:T(8,128)(2,1)S(1)}, bf16[2,128,256]{2,1,0:T(8,128)(2,1)S(1)}, u32[]{:S(2)}, u32[]{:S(2)}) collective-permute-start(bf16[2,128,256]{2,1,0:T(8,128)(2,1)S(1)} %get-tuple-element.41), channel_id=1, source_target_pairs={{0,1},{1,0},{2,3},{3,2},{4,5},{5,4},{6,7},{7,6},{8,9},{9,8},{10,11... | collective-permute-start | bytes 393224 | tf_op jit(solution)/shard_map/ppermute | solution.py:286
  83.6 18.2 %collective-permute-start.12 = (bf16[2,128,512]{2,1,0:T(8,128)(2,1)S(1)}, bf16[2,128,512]{2,1,0:T(8,128)(2,1)S(1)}, u32[]{:S(2)}, u32[]{:S(2)}) collective-permute-start(bf16[2,128,512]{2,1,0:T(8,128)(2,1)S(1)} %get-tuple-element.47), channel_id=1, source_target_pairs={{0,1},{1,0},{2,3},{3,2},{4,5},{5,4},{6,7},{7,6},{8,9},{9,8},{10,11... | collective-permute-start | bytes 786440 | tf_op jit(solution)/shard_map/ppermute | solution.py:286
  93.1 4.9 %collective-permute-start.17 = (bf16[128,512]{1,0:T(8,128)(2,1)S(1)}, bf16[128,512]{1,0:T(8,128)(2,1)S(1)}, u32[]{:S(2)}, u32[]{:S(2)}) collective-permute-start(bf16[128,512]{1,0:T(8,128)(2,1)S(1)} %get-tuple-element.51.refs_0_.refs_14_), channel_id=1, source_target_pairs={{0,1},{1,0},{2,3},{3,2},{4,5},{5,4},{6,7},{7,6},{8,9},{9,8},{10,11... | collective-permute-start | bytes 393224 | tf_op jit(solution)/shard_map/ppermute | solution.py:286
  93.1 4.9 %collective-permute-start.18 = (bf16[128,512]{1,0:T(8,128)(2,1)S(1)}, bf16[128,512]{1,0:T(8,128)(2,1)S(1)}, u32[]{:S(2)}, u32[]{:S(2)}) collective-permute-start(bf16[128,512]{1,0:T(8,128)(2,1)S(1)} %collective-permute-done.16.refs_1_), channel_id=1, source_target_pairs={{0,1},{1,0},{2,3},{3,2},{4,5},{5,4},{6,7},{7,6},{8,9},{9,8},{10,11... | collective-permute-start | bytes 393224 | tf_op jit(solution)/shard_map/ppermute | solution.py:286
  93.8 7.9 %collective-permute-start.30 = (bf16[128,256]{1,0:T(8,128)(2,1)S(1)}, bf16[128,256]{1,0:T(8,128)(2,1)S(1)}, u32[]{:S(2)}, u32[]{:S(2)}) collective-permute-start(bf16[128,256]{1,0:T(8,128)(2,1)S(1)} %get-tuple-element.63.refs_0_.refs_24_), channel_id=1, source_target_pairs={{0,2},{1,3},{2,0},{3,1},{4,6},{5,7},{6,4},{7,5},{8,10},{9,11},{10,... | collective-permute-start | bytes 196616 | tf_op jit(solution)/shard_map/ppermute | solution.py:286
  97.0 5.3 %collective-permute-start.23 = (bf16[128,512]{1,0:T(8,128)(2,1)S(1)}, bf16[128,512]{1,0:T(8,128)(2,1)S(1)}, u32[]{:S(2)}, u32[]{:S(2)}) collective-permute-start(bf16[128,512]{1,0:T(8,128)(2,1)S(1)} %get-tuple-element.57.refs_0_.refs_19_), channel_id=1, source_target_pairs={{0,2},{1,3},{2,0},{3,1},{4,6},{5,7},{6,4},{7,5},{8,10},{9,11},{10,... | collective-permute-start | bytes 393224 | tf_op jit(solution)/shard_map/ppermute | solution.py:286
  98.0 5.0 %collective-permute-start.31 = (bf16[128,256]{1,0:T(8,128)(2,1)S(1)}, bf16[128,256]{1,0:T(8,128)(2,1)S(1)}, u32[]{:S(2)}, u32[]{:S(2)}) collective-permute-start(bf16[128,256]{1,0:T(8,128)(2,1)S(1)} %get-tuple-element.63.refs_0_.refs_24_), channel_id=1, source_target_pairs={{0,1},{1,0},{2,3},{3,2},{4,5},{5,4},{6,7},{7,6},{8,9},{9,8},{10,11... | collective-permute-start | bytes 196616 | tf_op jit(solution)/shard_map/ppermute | solution.py:286
  101.2 9.5 %collective-permute-start.19 = (bf16[2,128,512]{2,1,0:T(8,128)(2,1)S(1)}, bf16[2,128,512]{2,1,0:T(8,128)(2,1)S(1)}, u32[]{:S(2)}, u32[]{:S(2)}) collective-permute-start(bf16[2,128,512]{2,1,0:T(8,128)(2,1)S(1)} %get-tuple-element.53), channel_id=1, source_target_pairs={{0,1},{1,0},{2,3},{3,2},{4,5},{5,4},{6,7},{7,6},{8,9},{9,8},{10,11... | collective-permute-start | bytes 786440 | tf_op jit(solution)/shard_map/ppermute | solution.py:286
  101.9 5.0 %collective-permute-start.24 = (bf16[128,512]{1,0:T(8,128)(2,1)S(1)}, bf16[128,512]{1,0:T(8,128)(2,1)S(1)}, u32[]{:S(2)}, u32[]{:S(2)}) collective-permute-start(bf16[128,512]{1,0:T(8,128)(2,1)S(1)} %get-tuple-element.57.refs_0_.refs_19_), channel_id=1, source_target_pairs={{0,1},{1,0},{2,3},{3,2},{4,5},{5,4},{6,7},{7,6},{8,9},{9,8},{10,11... | collective-permute-start | bytes 393224 | tf_op jit(solution)/shard_map/ppermute | solution.py:286
  102.3 4.7 %collective-permute-start.25 = (bf16[128,512]{1,0:T(8,128)(2,1)S(1)}, bf16[128,512]{1,0:T(8,128)(2,1)S(1)}, u32[]{:S(2)}, u32[]{:S(2)}) collective-permute-start(bf16[128,512]{1,0:T(8,128)(2,1)S(1)} %collective-permute-done.23.refs_1_), channel_id=1, source_target_pairs={{0,1},{1,0},{2,3},{3,2},{4,5},{5,4},{6,7},{7,6},{8,9},{9,8},{10,11... | collective-permute-start | bytes 393224 | tf_op jit(solution)/shard_map/ppermute | solution.py:286
  103.1 14.1 %collective-permute-start.6 = (bf16[1,128,256]{2,1,0:T(8,128)(2,1)}, bf16[1,128,256]{2,1,0:T(8,128)(2,1)}, u32[]{:S(2)}, u32[]{:S(2)}) collective-permute-start(bf16[1,128,256]{2,1,0:T(8,128)(2,1)} %add_convert_fusion.13), channel_id=1, source_target_pairs={{0,2},{1,3},{2,0},{3,1},{4,6},{5,7},{6,4},{7,5},{8,10},{9,11},{10,... | collective-permute-start | bytes 196616 | tf_op jit(solution)/shard_map/ppermute | solution.py:286
  104.8 12.4 %collective-permute-start.13 = (bf16[1,128,512]{2,1,0:T(8,128)(2,1)}, bf16[1,128,512]{2,1,0:T(8,128)(2,1)}, u32[]{:S(2)}, u32[]{:S(2)}) collective-permute-start(bf16[1,128,512]{2,1,0:T(8,128)(2,1)} %add_convert_fusion.11), channel_id=1, source_target_pairs={{0,2},{1,3},{2,0},{3,1},{4,6},{5,7},{6,4},{7,5},{8,10},{9,11},{10,... | collective-permute-start | bytes 393224 | tf_op jit(solution)/shard_map/ppermute | solution.py:286
  106.9 6.2 %collective-permute-start.33 = (bf16[2,128,256]{2,1,0:T(8,128)(2,1)S(1)}, bf16[2,128,256]{2,1,0:T(8,128)(2,1)S(1)}, u32[]{:S(2)}, u32[]{:S(2)}) collective-permute-start(bf16[2,128,256]{2,1,0:T(8,128)(2,1)S(1)} %get-tuple-element.65), channel_id=1, source_target_pairs={{0,1},{1,0},{2,3},{3,2},{4,5},{5,4},{6,7},{7,6},{8,9},{9,8},{10,11... | collective-permute-start | bytes 393224 | tf_op jit(solution)/shard_map/ppermute | solution.py:286
  110.2 3.9 %collective-permute-start.26 = (bf16[2,128,512]{2,1,0:T(8,128)(2,1)S(1)}, bf16[2,128,512]{2,1,0:T(8,128)(2,1)S(1)}, u32[]{:S(2)}, u32[]{:S(2)}) collective-permute-start(bf16[2,128,512]{2,1,0:T(8,128)(2,1)S(1)} %get-tuple-element.59), channel_id=1, source_target_pairs={{0,1},{1,0},{2,3},{3,2},{4,5},{5,4},{6,7},{7,6},{8,9},{9,8},{10,11... | collective-permute-start | bytes 786440 | tf_op jit(solution)/shard_map/ppermute | solution.py:286
  111.4 7.8 %collective-permute-start.20 = (bf16[1,128,512]{2,1,0:T(8,128)(2,1)}, bf16[1,128,512]{2,1,0:T(8,128)(2,1)}, u32[]{:S(2)}, u32[]{:S(2)}) collective-permute-start(bf16[1,128,512]{2,1,0:T(8,128)(2,1)} %add_convert_fusion.10), channel_id=1, source_target_pairs={{0,2},{1,3},{2,0},{3,1},{4,6},{5,7},{6,4},{7,5},{8,10},{9,11},{10,... | collective-permute-start | bytes 393224 | tf_op jit(solution)/shard_map/ppermute | solution.py:286
  113.8 5.3 %collective-permute-start.34 = (bf16[1,128,256]{2,1,0:T(8,128)(2,1)}, bf16[1,128,256]{2,1,0:T(8,128)(2,1)}, u32[]{:S(2)}, u32[]{:S(2)}) collective-permute-start(bf16[1,128,256]{2,1,0:T(8,128)(2,1)} %add_convert_fusion.12), channel_id=1, source_target_pairs={{0,2},{1,3},{2,0},{3,1},{4,6},{5,7},{6,4},{7,5},{8,10},{9,11},{10,... | collective-permute-start | bytes 196616 | tf_op jit(solution)/shard_map/ppermute | solution.py:286
  114.8 6.6 %collective-permute-start.27 = (bf16[1,128,512]{2,1,0:T(8,128)(2,1)}, bf16[1,128,512]{2,1,0:T(8,128)(2,1)}, u32[]{:S(2)}, u32[]{:S(2)}) collective-permute-start(bf16[1,128,512]{2,1,0:T(8,128)(2,1)} %add_convert_fusion.9), channel_id=1, source_target_pairs={{0,2},{1,3},{2,0},{3,1},{4,6},{5,7},{6,4},{7,5},{8,10},{9,11},{10,... | collective-permute-start | bytes 393224 | tf_op jit(solution)/shard_map/ppermute | solution.py:286
  129.5 6.9 %collective-permute-start.35 = (f32[128,128]{1,0:T(8,128)S(1)}, f32[128,128]{1,0:T(8,128)S(1)}, u32[]{:S(2)}, u32[]{:S(2)}) collective-permute-start(f32[128,128]{1,0:T(8,128)S(1)} %get-tuple-element.68), channel_id=1, source_target_pairs={{0,4},{4,8},{8,12},{12,0},{1,5},{5,9},{9,13},{13,1},{2,6},{6,10},{... | collective-permute-start | bytes 196616 | tf_op jit(solution)/shard_map/ppermute | solution.py:314
  131.3 7.1 %collective-permute-start.36 = (f32[128,128]{1,0:T(8,128)S(1)}, f32[128,128]{1,0:T(8,128)S(1)}, u32[]{:S(2)}, u32[]{:S(2)}) collective-permute-start(f32[128,128]{1,0:T(8,128)S(1)} %get-tuple-element.68), channel_id=1, source_target_pairs={{0,8},{4,12},{8,0},{12,4},{1,9},{5,13},{9,1},{13,5},{2,10},{6,14},... | collective-permute-start | bytes 196616 | tf_op jit(solution)/shard_map/ppermute | solution.py:314
  133.9 4.6 %collective-permute-start.37 = (f32[128,128]{1,0:T(8,128)S(1)}, f32[128,128]{1,0:T(8,128)S(1)}, u32[]{:S(2)}, u32[]{:S(2)}) collective-permute-start(f32[128,128]{1,0:T(8,128)S(1)} %get-tuple-element.68), channel_id=1, source_target_pairs={{0,12},{4,0},{8,4},{12,8},{1,13},{5,1},{9,5},{13,9},{2,14},{6,2},{... | collective-permute-start | bytes 196616 | tf_op jit(solution)/shard_map/ppermute | solution.py:314
  140.0 6.5 %collective-permute-start.41 = (bf16[64,2048]{1,0:T(8,128)(2,1)S(1)}, bf16[64,2048]{1,0:T(8,128)(2,1)S(1)}, u32[]{:S(2)}, u32[]{:S(2)}) collective-permute-start(bf16[64,2048]{1,0:T(8,128)(2,1)S(1)} %bitcast.94), channel_id=1, source_target_pairs={{0,2},{1,3},{2,0},{3,1},{4,6},{5,7},{6,4},{7,5},{8,10},{9,11},{10,... | collective-permute-start | bytes 786440 | tf_op jit(solution)/shard_map/ppermute | solution.py:286
  141.6 4.9 %collective-permute-start.42 = (bf16[64,2048]{1,0:T(8,128)(2,1)S(1)}, bf16[64,2048]{1,0:T(8,128)(2,1)S(1)}, u32[]{:S(2)}, u32[]{:S(2)}) collective-permute-start(bf16[64,2048]{1,0:T(8,128)(2,1)S(1)} %bitcast.95), channel_id=1, source_target_pairs={{0,1},{1,0},{2,3},{3,2},{4,5},{5,4},{6,7},{7,6},{8,9},{9,8},{10,11... | collective-permute-start | bytes 786440 | tf_op jit(solution)/shard_map/ppermute | solution.py:286
  154.6 12.9 %collective-permute-start.47 = (bf16[4,32,2048]{2,1,0:T(8,128)(2,1)}, bf16[4,32,2048]{2,1,0:T(8,128)(2,1)S(1)}, u32[]{:S(2)}, u32[]{:S(2)}) collective-permute-start(bf16[4,32,2048]{2,1,0:T(8,128)(2,1)} %slice_bitcast_fusion), channel_id=1, source_target_pairs={{12,8},{13,9},{14,10},{15,11},{28,24},{29,25},{30,26},{31,27}} | collective-permute-start | bytes 1572872 | tf_op jit(solution)/shard_map/ppermute | solution.py:348
  155.3 8.4 %collective-permute-start.38 = (bf16[64,2048]{1,0:T(8,128)(2,1)S(1)}, bf16[64,2048]{1,0:T(8,128)(2,1)S(1)}, u32[]{:S(2)}, u32[]{:S(2)}) collective-permute-start(bf16[64,2048]{1,0:T(8,128)(2,1)S(1)} %bitcast.91), channel_id=1, source_target_pairs={{0,2},{1,3},{2,0},{3,1},{4,6},{5,7},{6,4},{7,5},{8,10},{9,11},{10,... | collective-permute-start | bytes 786440 | tf_op jit(solution)/shard_map/ppermute | solution.py:286
  157.0 11.7 %collective-permute-start.39 = (bf16[64,2048]{1,0:T(8,128)(2,1)S(1)}, bf16[64,2048]{1,0:T(8,128)(2,1)S(1)}, u32[]{:S(2)}, u32[]{:S(2)}) collective-permute-start(bf16[64,2048]{1,0:T(8,128)(2,1)S(1)} %bitcast.92), channel_id=1, source_target_pairs={{0,1},{1,0},{2,3},{3,2},{4,5},{5,4},{6,7},{7,6},{8,9},{9,8},{10,11... | collective-permute-start | bytes 786440 | tf_op jit(solution)/shard_map/ppermute | solution.py:286
  163.7 5.0 %collective-permute-start.40 = (bf16[64,2048]{1,0:T(8,128)(2,1)S(1)}, bf16[64,2048]{1,0:T(8,128)(2,1)S(1)}, u32[]{:S(2)}, u32[]{:S(2)}) collective-permute-start(bf16[64,2048]{1,0:T(8,128)(2,1)S(1)} %collective-permute-done.38), channel_id=1, source_target_pairs={{0,1},{1,0},{2,3},{3,2},{4,5},{5,4},{6,7},{7,6},{8,9},{9,8},{10,11... | collective-permute-start | bytes 786440 | tf_op jit(solution)/shard_map/ppermute | solution.py:286
  163.7 15.9 %collective-permute-start.44 = (bf16[4,32,2048]{2,1,0:T(8,128)(2,1)}, bf16[4,32,2048]{2,1,0:T(8,128)(2,1)S(1)}, u32[]{:S(2)}, u32[]{:S(2)}) collective-permute-start(bf16[4,32,2048]{2,1,0:T(8,128)(2,1)} %slice_bitcast_fusion), channel_id=1, source_target_pairs={{0,4},{1,5},{2,6},{3,7},{16,20},{17,21},{18,22},{19,23}} | collective-permute-start | bytes 1572872 | tf_op jit(solution)/shard_map/ppermute | solution.py:347
  167.8 11.9 %collective-permute-start.48 = (bf16[4,32,2048]{2,1,0:T(8,128)(2,1)S(1)}, bf16[4,32,2048]{2,1,0:T(8,128)(2,1)S(1)}, u32[]{:S(2)}, u32[]{:S(2)}) collective-permute-start(bf16[4,32,2048]{2,1,0:T(8,128)(2,1)S(1)} %add_convert_fusion.1), channel_id=1, source_target_pairs={{8,4},{12,8},{9,5},{13,9},{10,6},{14,10},{11,7},{15,11},{24,20},{2... | collective-permute-start | bytes 1572872 | tf_op jit(solution)/shard_map/ppermute | solution.py:348
  181.1 18.5 %collective-permute-start.45 = (bf16[4,32,2048]{2,1,0:T(8,128)(2,1)}, bf16[4,32,2048]{2,1,0:T(8,128)(2,1)}, u32[]{:S(2)}, u32[]{:S(2)}) collective-permute-start(bf16[4,32,2048]{2,1,0:T(8,128)(2,1)} %get-tuple-element.74), channel_id=1, source_target_pairs={{0,4},{4,8},{1,5},{5,9},{2,6},{6,10},{3,7},{7,11},{16,20},{20,24},... | collective-permute-start | bytes 1572872 | tf_op jit(solution)/shard_map/ppermute | solution.py:347
  190.0 15.2 %collective-permute-start.49 = (bf16[4,32,2048]{2,1,0:T(8,128)(2,1)}, bf16[4,32,2048]{2,1,0:T(8,128)(2,1)S(1)}, u32[]{:S(2)}, u32[]{:S(2)}) collective-permute-start(bf16[4,32,2048]{2,1,0:T(8,128)(2,1)} %get-tuple-element.73), channel_id=1, source_target_pairs={{4,0},{8,4},{12,8},{5,1},{9,5},{13,9},{6,2},{10,6},{14,10},{7,3},{... | collective-permute-start | bytes 1572872 | tf_op jit(solution)/shard_map/ppermute | solution.py:348
  200.7 13.5 %collective-permute-start.46 = (bf16[4,32,2048]{2,1,0:T(8,128)(2,1)S(1)}, bf16[4,32,2048]{2,1,0:T(8,128)(2,1)S(1)}, u32[]{:S(2)}, u32[]{:S(2)}) collective-permute-start(bf16[4,32,2048]{2,1,0:T(8,128)(2,1)S(1)} %add_convert_fusion.2), channel_id=1, source_target_pairs={{0,4},{4,8},{8,12},{1,5},{5,9},{9,13},{2,6},{6,10},{10,14},{3,7},{... | collective-permute-start | bytes 1572872 | tf_op jit(solution)/shard_map/ppermute | solution.py:347
  (39 other events, 297.4 us)

commit v3 on v0

v3 whole, which is shorter than its diff:
```python
import functools

import jax
import jax.numpy as jnp
from jax import lax
from jax.experimental import pallas as pl
from jax.experimental.pallas import tpu as pltpu
from jax.sharding import PartitionSpec as P

DH = 128
EPSILON = 1e-05
VMEM_LIMIT = 48 * 1024 * 1024

bf16 = jnp.bfloat16
f32 = jnp.float32


def silu(v):
    u = 0.5 * v
    return u + u * jnp.tanh(u)


def params():
    return pltpu.CompilerParams(vmem_limit_bytes=VMEM_LIMIT)


LIGHT = pl.CostEstimate(flops=1000, bytes_accessed=1000, transcendentals=0)


def project_kernel(parts, owners, at_ref, *refs):
    rows, w_ref = refs[:owners], refs[owners]
    keep_ref, send_ref, lhs_ref = refs[-3 - parts:-parts]
    wides = refs[-parts:]
    zs, chunks, _, piece, _ = rows[0].shape
    depth = w_ref.shape[0] // parts

    @pl.when(pl.program_id(0) == 0)
    def _():
        first = 0
        for r in range(chunks):
            for p in range(owners):
                for z in range(zs):
                    lhs_ref[first:first + piece, :] = rows[p][z, r, 0]
                    first += piece

    flat = w_ref.reshape(depth * parts * 4, DH)
    res = None
    for k, wide in enumerate(wides):
        wide[...] = flat[k * depth * 4:(k + 1) * depth * 4, :].astype(f32)
        rhs = jnp.concatenate(
            [wide[pl.ds(i, depth, stride=4), :].astype(bf16) for i in range(4)], axis=1
        )
        term = jnp.dot(lhs_ref[:, k * depth:(k + 1) * depth], rhs, preferred_element_type=f32)
        res = term if res is None else res + term
    res = res.astype(bf16)
    half, each = keep_ref.shape[1], keep_ref.shape[3]
    for r in range(chunks):
        for p in range(owners):
            into = keep_ref if p < half else send_ref
            first = (r * owners + p) * each
            for i in range(4):
                into[r, p % half, i] = res[first:first + each, i * DH:(i + 1) * DH]


def project(at, tokens, w, head_first, heads, after):
    zs, chunks, owners, piece, depth = tokens.shape
    half, each = owners // 2, zs * piece
    parts = 4 if depth % 512 == 0 else 1
    shape = jax.ShapeDtypeStruct((chunks, half, 4, each, heads * DH), bf16)
    spec = pl.BlockSpec((chunks, half, 4, each, DH), lambda j, at: (0, 0, 0, 0, j))
    return pl.pallas_call(
        functools.partial(project_kernel, parts, owners),
        grid_spec=pltpu.PrefetchScalarGridSpec(
            num_scalar_prefetch=1,
            grid=(heads,),
            in_specs=[
                pl.BlockSpec(
                    (zs, chunks, 1, piece, depth), lambda j, at, p=p: (0, 0, at[0] ^ p, 0, 0)
                )
                for p in range(owners)
            ]
            + [pl.BlockSpec((depth, 4, DH), lambda j, at: (0, 0, head_first + j))]
            + [pl.BlockSpec(memory_space=pl.ANY)] * len(after),
            out_specs=(spec, spec),
            scratch_shapes=[pltpu.VMEM((chunks * owners * each, depth), bf16)]
            + [pltpu.VMEM((depth // parts * 4, DH), f32) for _ in range(parts)],
        ),
        out_shape=(shape, shape),
        compiler_params=params(),
        cost_estimate=LIGHT,
        name="project",
    )(at, *[tokens] * owners, w, *after)


def tie_kernel(*refs):
    pass


def tie(x, *after):
    anywhere = pl.BlockSpec(memory_space=pl.ANY)
    return pl.pallas_call(
        tie_kernel,
        in_specs=[anywhere] * (1 + len(after)),
        out_specs=anywhere,
        out_shape=jax.ShapeDtypeStruct(x.shape, x.dtype),
        input_output_aliases={0: 0},
        cost_estimate=LIGHT,
        name="tie",
    )(x, *after)


def activate_kernel(counts, *refs):
    q_ref, rest_ref = refs[-2:]
    column, at = 0, 0
    for count in counts:
        terms = refs[at:at + count]
        span = terms[0].shape[-1]
        for i in range(4):
            part = silu(sum(t[0, 0, i].astype(f32) for t in terms)).astype(bf16)
            if i == 0:
                q_ref[:, column:column + span] = part
            else:
                rest_ref[i - 1, :, column:column + span] = part
        column += span
        at += count


def activate(r, chunks):
    flat, specs, width = [], [], 0
    for terms in chunks:
        _, _, _, each, span = terms[0][0].shape
        width += span
        for array, offset in terms:
            flat.append(array)
            specs.append(
                pl.BlockSpec((1, 1, 4, each, span), lambda j, at=r - offset: (at, 0, 0, 0, 0))
            )
    return pl.pallas_call(
        functools.partial(activate_kernel, [len(terms) for terms in chunks]),
        grid=(1,),
        in_specs=specs,
        out_specs=(
            pl.BlockSpec((each, width), lambda j: (0, 0)),
            pl.BlockSpec((3, each, width), lambda j: (0, 0, 0)),
        ),
        out_shape=(
            jax.ShapeDtypeStruct((each, width), bf16),
            jax.ShapeDtypeStruct((3, each, width), bf16),
        ),
        compiler_params=params(),
        cost_estimate=LIGHT,
        name="activate",
    )(*flat)


def attend_kernel(owners, at_ref, *refs):
    queries, edges = refs[:owners], refs[owners:2 * owners]
    k_ref, v_ref, keep_ref, send_ref, mask_ref = refs[2 * owners:]
    events = mask_ref.shape[1]
    half, each, _ = keep_ref.shape

    @pl.when(pl.program_id(0) == 0)
    def _():
        zs, _, _, piece, _ = edges[0].shape
        at = lax.broadcasted_iota(jnp.int32, (piece, events), 1)
        for p in range(owners):
            for z in range(zs):
                edge = edges[p][z, 0, 0]
                seen = (at >= edge[:, :1]) & (at < edge[:, 1:])
                first = p * each + z * piece
                mask_ref[first:first + piece, :] = jnp.where(seen, 1.0, 0.0).astype(bf16)

    query = jnp.concatenate([q[...] for q in queries])
    u = lax.dot_general(
        query, k_ref[...], (((1,), (1,)), ((), ())), preferred_element_type=f32
    ) * (0.5 * DH ** (-0.5))
    weights = (u + u * jnp.tanh(u)).astype(bf16) * mask_ref[...]
    term = jnp.dot(weights, v_ref[...], preferred_element_type=f32).astype(bf16)
    for p in range(owners):
        into = keep_ref if p < half else send_ref
        into[p % half] = term[p * each:(p + 1) * each]


def edge_spec(edges, r, p):
    zs, _, _, piece, ends = edges.shape
    return pl.BlockSpec((zs, 1, 1, piece, ends), lambda j, at: (0, r, at[0] ^ p, 0, 0))


def attend(at, r, queries, k_cache, v_cache, edges):
    owners, (each, width) = len(queries), queries[0].shape
    rows, events, half = owners * each, k_cache.shape[0], owners // 2
    cache = pl.BlockSpec((events, DH), lambda j, at: (0, j))
    shape = jax.ShapeDtypeStruct((half, each, width), bf16)
    spec = pl.BlockSpec((half, each, DH), lambda j, at: (0, 0, j))
    return pl.pallas_call(
        functools.partial(attend_kernel, owners),
        grid_spec=pltpu.PrefetchScalarGridSpec(
            num_scalar_prefetch=1,
            grid=(width // DH,),
            in_specs=[pl.BlockSpec((each, DH), lambda j, at: (0, j))] * owners
            + [edge_spec(edges, r, p) for p in range(owners)]
            + [cache, cache],
            out_specs=(spec, spec),
            scratch_shapes=[pltpu.VMEM((rows, events), bf16)],
        ),
        out_shape=(shape, shape),
        compiler_params=params(),
        cost_estimate=LIGHT,
        name="attend",
    )(at, *queries, *[edges] * owners, k_cache, v_cache)


def finish_kernel(terms, at_ref, edge_ref, q_ref, rest_ref, *refs):
    sums, (att_ref, stat_ref) = refs[:terms], refs[terms:]
    rows, width = att_ref.shape
    edge = jnp.concatenate([edge_ref[z, 0, 0] for z in range(edge_ref.shape[0])]).astype(f32)
    root = lax.rsqrt(edge[:, 1:] - edge[:, :1])
    total = jnp.zeros((rows, 1), f32)
    for first in range(0, width, DH):
        at = slice(first, first + DH)
        summed = sum(s[0, 0, :, at].astype(f32) for s in sums)
        product = q_ref[:, at].astype(f32) * rest_ref[0, :, at].astype(f32)
        weight = silu(jnp.sum(product, axis=1, keepdims=True) * DH ** (-0.5))
        value = summed * root + weight * rest_ref[1, :, at].astype(f32)
        att_ref[:, at] = value
        total += jnp.sum(value, axis=1, keepdims=True)
    mean = total / width
    spread = jnp.zeros((rows, DH), f32)
    for first in range(0, width, DH):
        away = att_ref[:, first:first + DH] - mean
        spread += away * away
    square = jnp.sum(spread, axis=1, keepdims=True)
    lane = lax.broadcasted_iota(jnp.int32, (rows, DH), 1)
    stat_ref[...] = jnp.where(lane < DH // 2, mean, square)


def finish(at, r, edges, query, rest, sums):
    rows, width = query.shape
    return pl.pallas_call(
        functools.partial(finish_kernel, len(sums)),
        grid_spec=pltpu.PrefetchScalarGridSpec(
            num_scalar_prefetch=1,
            grid=(1,),
            in_specs=[
                edge_spec(edges, r, 0),
                pl.BlockSpec((rows, width), lambda j, at: (0, 0)),
                pl.BlockSpec((2, rows, width), lambda j, at: (0, 0, 0)),
            ] + [pl.BlockSpec((1, 1, rows, width), lambda j, at: (0, 0, 0, 0))] * len(sums),
            out_specs=(
                pl.BlockSpec((rows, width), lambda j, at: (0, 0)),
                pl.BlockSpec((rows, DH), lambda j, at: (0, 0)),
            ),
        ),
        out_shape=(
            jax.ShapeDtypeStruct((rows, width), f32),
            jax.ShapeDtypeStruct((rows, DH), f32),
        ),
        compiler_params=params(),
        cost_estimate=LIGHT,
        name="finish",
    )(at, edges, query, rest, *sums)


def gate_kernel(count, att_ref, rest_ref, *refs):
    stats, out_ref = refs[:count], refs[-1]
    width = att_ref.shape[1]
    means = [s[:, :1] for s in stats]
    squares = [s[:, DH // 2:DH // 2 + 1] for s in stats]
    mean = sum(means) / count
    square = sum(squares) + width * sum((m - mean) * (m - mean) for m in means)
    scale = lax.rsqrt(square / (width * count) + EPSILON)
    for first in range(0, width, 4 * DH):
        at = slice(first, min(first + 4 * DH, width))
        normed = (att_ref[:, at] - mean) * scale
        out_ref[:, at] = (normed * rest_ref[0, :, at].astype(f32)).astype(bf16)


def gate_rows(att, stats, rest):
    rows, width = att.shape
    return pl.pallas_call(
        functools.partial(gate_kernel, len(stats)),
        grid=(1,),
        in_specs=[
            pl.BlockSpec((rows, width), lambda j: (0, 0)),
            pl.BlockSpec((1, rows, width), lambda j: (2, 0, 0)),
        ] + [pl.BlockSpec((rows, DH), lambda j: (0, 0))] * len(stats),
        out_specs=pl.BlockSpec((rows, width), lambda j: (0, 0)),
        out_shape=jax.ShapeDtypeStruct((rows, width), bf16),
        compiler_params=params(),
        cost_estimate=LIGHT,
        name="gate",
    )(att, rest, *stats)


def output_kernel(owners, zs, index_ref, *refs):
    rows, w_ref, outs, lhs_ref = refs[:owners], refs[owners], refs[owners + 1:-1], refs[-1]
    piece = rows[0].shape[1]

    @pl.when(pl.program_id(0) == 0)
    def _():
        for k in range(zs):
            at = lax.rem(index_ref[0] + k, zs)
            for p in range(owners):
                first = (k * owners + p) * piece
                lhs_ref[first:first + piece, :] = rows[p][at]

    sums = jnp.dot(lhs_ref[...], w_ref[...], preferred_element_type=f32).astype(bf16)
    for k in range(zs):
        for p in range(owners):
            first = (k * owners + p) * piece
            outs[k][p] = sums[first:first + piece]


def output(index, blocks, w_out, zs):
    owners, (each, width) = len(blocks), blocks[0].shape
    piece, columns = each // zs, w_out.shape[1]
    span = 512 if columns % 512 == 0 else columns
    row_spec = pl.BlockSpec((zs, piece, width), lambda j, at: (0, 0, 0))
    return pl.pallas_call(
        functools.partial(output_kernel, owners, zs),
        grid_spec=pltpu.PrefetchScalarGridSpec(
            num_scalar_prefetch=1,
            grid=(columns // span,),
            in_specs=[row_spec] * owners + [pl.BlockSpec((width, span), lambda j, at: (0, j))],
            out_specs=[pl.BlockSpec((owners, piece, span), lambda j, at: (0, 0, j))] * zs,
            scratch_shapes=[pltpu.VMEM((owners * each, width), bf16)],
        ),
        out_shape=[jax.ShapeDtypeStruct((owners, piece, columns), bf16)] * zs,
        compiler_params=params(),
        cost_estimate=LIGHT,
        name="output",
    )(index.reshape(1).astype(jnp.int32), *[b.reshape(zs, piece, width) for b in blocks], w_out)


def close_kernel(counts, at_ref, t_ref, *refs):
    out_ref, first = refs[-1], 0
    for r, count in enumerate(counts):
        terms = refs[first:first + count]
        first += count

        @pl.when(pl.program_id(0) == r)
        def _():
            total = t_ref[...].astype(f32)
            for term in terms:
                total = total + term[...].astype(f32)
            out_ref[...] = total.astype(bf16)


def close(place, first, tokens, chunks):
    owners, piece, width = chunks[0][0].shape
    specs = []
    for r, terms in enumerate(chunks):
        def at_block(i, j, at, r=r):
            return (jnp.where(i == r, j ^ at[0], jnp.where(i < r, at[0], (owners - 1) ^ at[0])), 0, 0)
        specs += [pl.BlockSpec((1, piece, width), at_block)] * len(terms)

    def own(i, j, at):
        return (at[1] + i * owners + j, 0, 0)

    return pl.pallas_call(
        functools.partial(close_kernel, [len(terms) for terms in chunks]),
        grid_spec=pltpu.PrefetchScalarGridSpec(
            num_scalar_prefetch=1,
            grid=(len(chunks), owners),
            in_specs=[pl.BlockSpec((1, piece, width), own)] + specs,
            out_specs=pl.BlockSpec((1, piece, width), lambda i, j, at: (i * owners + j, 0, 0)),
        ),
        out_shape=jax.ShapeDtypeStruct((len(chunks) * owners, piece, width), bf16),
        compiler_params=params(),
        cost_estimate=LIGHT,
        name="close",
    )(
        jnp.stack([place, first]).astype(jnp.int32),
        tokens.reshape(-1, piece, width),
        *[term for terms in chunks for term in terms],
    )


def bits_of(axis):
    count = lax.axis_size(axis)
    assert count & (count - 1) == 0
    return count.bit_length() - 1


def place_of(axis):
    index, bits = lax.axis_index(axis), bits_of(axis)
    return sum((((index >> b) & 1) << (bits - 1 - b) for b in range(bits)), jnp.int32(0))


def swap(x, axis, bit):
    return lax.ppermute(
        x, axis, [(i, i ^ (1 << bit)) for i in range(lax.axis_size(axis))]
    )


def scatter_rest(terms, first, count, axis):
    terms, sent = list(terms), None
    for b in range(1, bits_of(axis)):
        half = terms[-1][0].shape[1] // 2
        total = sum(
            t[first - offset:first - offset + count, half:2 * half].astype(f32)
            for t, offset in terms
        )
        sent = total.astype(bf16)
        terms.append((swap(sent, axis, b), first))
    return terms, sent


def gather(x, axis):
    blocks = [x]
    for b in reversed(range(bits_of(axis))):
        blocks = blocks + [swap(block, axis, b) for block in blocks]
    return blocks


def shifts(blocks, axis):
    count = lax.axis_size(axis)
    return [blocks[0]] + [
        lax.ppermute(blocks[k], axis, [(i, (i + k) % count) for i in range(count)])
        for k in range(1, count)
    ]


def all_stats(stat, axis):
    count = lax.axis_size(axis)
    if count > 8:
        every = lax.all_gather(stat, axis)
        return [every[i] for i in range(count)]
    return shifts([stat] * count, axis)


def head_chunks(heads):
    if heads % 8:
        return [1] * heads
    unit = heads // 8
    return [unit, 2 * unit, 2 * unit, 2 * unit, unit]


def local(tokens, w_qkvu, k_cache, v_cache, w_out, vis_start, vis_end):
    cand, depth = tokens.shape
    owners, zs = lax.axis_size("hist"), lax.axis_size("head")
    index, place = lax.axis_index("head"), place_of("hist")
    width = w_qkvu.shape[2]
    events = k_cache.shape[0]
    chunks = 2 if cand % (2 * owners * zs * 16) == 0 else 1
    piece = cand // (zs * chunks * owners)

    def arrange(x):
        x = x.reshape((zs, chunks, owners, piece) + x.shape[1:])
        if piece % 16 == 0:
            return x
        blocks = [lax.dynamic_index_in_dim(x, p ^ place, 2, False) for p in range(owners)]
        x = jnp.moveaxis(jnp.stack(blocks), 2, 0)
        return x.reshape((1, chunks, owners, zs * piece) + x.shape[4:])

    at = (place if piece % 16 == 0 else jnp.int32(0)).reshape(1)
    ordered = arrange(tokens)
    first_event = lax.axis_index("hist") * events
    edges = arrange(jnp.stack([vis_start - first_event, vis_end - first_event], axis=1))

    sizes = head_chunks(width // DH)
    summed, sent = [[] for _ in range(chunks)], []
    for c, heads in enumerate(sizes):
        after = sent[c - 2] if c >= 2 else []
        keep, send = project(at, ordered, w_qkvu, sum(sizes[:c]), heads, after)
        if c >= 2:
            send = tie(send, summed[0][c - 2][-1][0])
        terms = [(keep, 0), (swap(send, "hist", 0), 0)]
        groups = [(0, chunks)] if c + 1 < len(sizes) else [(r, 1) for r in range(chunks)]
        sent.append([])
        for first, count in groups:
            sums, last = scatter_rest(terms, first, count, "hist")
            for r in range(first, first + count):
                summed[r].append(sums)
            if last is not None:
                sent[-1].append(last)

    results = []
    for r in range(chunks):
        query, rest = activate(r, summed[r])
        keep, send = attend(at, r, gather(query, "hist"), k_cache, v_cache, edges)
        terms = [(keep[None], 0), (swap(send, "hist", 0)[None], 0)]
        sums, _ = scatter_rest(terms, 0, 1, "hist")
        att, stat = finish(at, r, edges, query, rest, [t for t, _ in sums])
        gated = gate_rows(att, all_stats(stat, "head"), rest)
        blocks = gather(gated, "hist")
        if piece % 16 == 0:
            results.append(shifts(output(index, blocks, w_out, zs), "head"))
        else:
            whole = jnp.dot(jnp.concatenate(blocks), w_out, preferred_element_type=f32)
            whole = whole.astype(bf16).reshape(owners, zs, piece, -1).swapaxes(0, 1)
            results.append(
                [lax.psum_scatter(whole, "head", scatter_dimension=0, tiled=True)[0]]
            )
    out = close(place, index * (chunks * owners), tokens, results)
    return out.reshape(cand // zs, -1)


def solution(mesh):
    in_specs = (
        P("groups", "hist"),
        P("hist", None, "head"),
        P(("groups", "hist"), "head"),
        P(("groups", "hist"), "head"),
        P("head", "hist"),
        P("groups"),
        P("groups"),
    )
    out_specs = P(("groups", "head"), "hist")
    return jax.shard_map(local, mesh=mesh, in_specs=in_specs, out_specs=out_specs, check_vma=False)
```

time: 369 us -> 231 us (0.63)
  waiting for transfers between devices: 212 us -> 82.2 us
  Pallas kernels: 0 us -> 84.8 us
  matrix products: 47.3 us -> 0 us
  local copies, waits for them, and re-layouts: 58.8 us -> 21.7 us
  starting transfers between devices: 0.57 us -> 32.4 us
  blocking collectives: 20 us -> 0 us
  between operations: 13.2 us -> 0.29 us
  other arithmetic: 16.3 us -> 6.28 us
    psum x1 -> x0, waiting for transfers between devices: 86.7 us -> none  [local(): lax.psum(whole_out.astype(jnp.bfloat16), 'head').astype(jnp.float32)]
    pallas_call x0 -> x19, Pallas kernels: none -> 84.8 us  [the longest x5 34.6 us: project(): pl.pallas_call(functools.partial(project_kernel, parts, owners), grid_spe...]
    ppermute x0 -> x39, waiting for transfers between devices: none -> 82.2 us  [the longest x27 45.5 us: swap(): lax.ppermute(x, axis, [(i, i ^ 1 << bit) for i in range(lax.axis_size(axi...]
    all_gather x3 -> x0, waiting for transfers between devices: 62.7 us -> none  [the longest x1 40.4 us: local(): lax.all_gather(k_cache, 'hist', axis=0, tiled=True)]
    reduce_scatter x1 -> x0, waiting for transfers between devices: 61.9 us -> none  [local(): lax.psum_scatter(jnp.dot(tokens, flat_weight, preferred_element_type=jnp....]
    dot_general x3 -> x0, matrix products: 47.3 us -> none  [the longest x1 25.5 us: local(): jnp.dot(tokens, flat_weight, preferred_element_type=jnp.float32)]
    ppermute x0 -> x39, starting transfers between devices: none -> 32.4 us  [the longest x12 16.8 us: shifts(): lax.ppermute(blocks[k], axis, [(i, (i + k) % count) for i in range(count)])]
    unnamed x10 -> x70, local copies, waits for them, and re-layouts: 39.9 us -> 19.8 us
  transfers between devices with their start and end apart: 5 -> 39, of which waited for: 5 -> 18; matrix products, arithmetic and copies ran while one was open for 25% -> 4% of each run, Pallas kernels for 0% -> 32%
where the time goes in v3:
time: 231 us; the launch traced here: 228 us
  Pallas kernels  84.8 us (37%)
  waiting for transfers between devices  82.2 us (36%)
  starting transfers between devices  32.4 us (14%)
  local copies, waits for them, and re-layouts  21.7 us (9%)
  other arithmetic  6.28 us (3%)
    ppermute x27, waiting for transfers between devices, swap(): lax.ppermute(x, axis, [(i, i ^ 1 << bit) for i in range(lax.axis_size(axi...  45.5 us
    ppermute x12, waiting for transfers between devices, shifts(): lax.ppermute(blocks[k], axis, [(i, (i + k) % count) for i in range(count)])  36.7 us
    pallas_call x5, Pallas kernels, project(): pl.pallas_call(functools.partial(project_kernel, parts, owners), grid_spe...  34.6 us
    pallas_call x2, Pallas kernels, attend(): pl.pallas_call(functools.partial(attend_kernel, owners), grid_spec=pltpu....  24.4 us
    unnamed x70, local copies, waits for them, and re-layouts  19.8 us
    ppermute x12, starting transfers between devices, shifts(): lax.ppermute(blocks[k], axis, [(i, (i + k) % count) for i in range(count)])  16.8 us
    ppermute x27, starting transfers between devices, swap(): lax.ppermute(x, axis, [(i, i ^ 1 << bit) for i in range(lax.axis_size(axi...  15.5 us
    pallas_call x2, Pallas kernels, output(): pl.pallas_call(functools.partial(output_kernel, owners, zs), grid_spec=pl...  12.7 us
  transfers between devices with their start and end apart: 39, of which 18 were waited for; matrix products, arithmetic and copies ran while one was open for 4% of the time, Pallas kernels for 32%

profile of v3, /device:TPU:0, one launch (start us, length us, event | category | flops | bytes accessed | tf_op | source)
XLA Modules:
  0.0 227.6 jit_solution(10441027499495324991)
XLA Ops:
  0.0 1.6 copy-done
  1.6 4.8 %project.5 = (bf16[2,2,4,64,256]{4,3,2,1,0:T(8,128)(2,1)S(1)}, bf16[2,2,4,64,256]{4,3,2,1,0:T(8,128)(2,1)S(1)}) custom-call(s32[1]{0:T(128)} %bitcast.at_ref, bf16[4,2,4,16,2048]{4,3,2,1,0:T(8,128)(2,1)S(1)} %bitcast.18, bf16[4,2,4,16,2048]{4,3,2,1,0:T(8,128)(2,1)S(1)} %bitcast.19, bf16[4,2,4,16,2048]{4,3,2,1,0:T(8,128)(2,1)S(1)} %bitcast.20, ...), custom_call_target="tpu_custom_call" | custom-call | flops 1000 | bytes 1000 | tf_op jit(solution)/shard_map/project/pallas_call | solution.py:71
  7.0 8.7 %project.6 = (bf16[2,2,4,64,512]{4,3,2,1,0:T(8,128)(2,1)S(1)}, bf16[2,2,4,64,512]{4,3,2,1,0:T(8,128)(2,1)}) custom-call(s32[1]{0:T(128)} %bitcast.at_ref, bf16[4,2,4,16,2048]{4,3,2,1,0:T(8,128)(2,1)S(1)} %bitcast.22, bf16[4,2,4,16,2048]{4,3,2,1,0:T(8,128)(2,1)S(1)} %bitcast.23, bf16[4,2,4,16,2048]{4,3,2,1,0:T(8,128)(2,1)S(1)} %bitcast.24, ...), custom_call_target="tpu_custom_call" | custom-call | flops 1000 | bytes 1000 | tf_op jit(solution)/shard_map/project/pallas_call | solution.py:71
  16.6 2.9 %collective-permute-start.1 = (bf16[2,1,4,64,256]{4,3,2,1,0:T(8,128)(2,1)S(1)}, bf16[2,1,4,64,256]{4,3,2,1,0:T(8,128)(2,1)S(1)}, u32[]{:S(2)}, u32[]{:S(2)}) collective-permute-start(bf16[2,1,4,64,256]{4,3,2,1,0:T(8,128)(2,1)S(1)} %add_convert_fusion.5.refs_5_), channel_id=1, source_target_pairs={{0,2},{1,3},{2,0},{3,1},{4,6},{5,7},{6,4},{7,5},{8,10},{9,11},{10,... | collective-permute-start | bytes 786440 | tf_op jit(solution)/shard_map/ppermute | solution.py:391
  19.5 8.0 %project.7 = (bf16[2,2,4,64,512]{4,3,2,1,0:T(8,128)(2,1)S(1)}, bf16[2,2,4,64,512]{4,3,2,1,0:T(8,128)(2,1)S(1)}) custom-call(s32[1]{0:T(128)} %bitcast.at_ref, bf16[4,2,4,16,2048]{4,3,2,1,0:T(8,128)(2,1)S(1)} %bitcast.26, bf16[4,2,4,16,2048]{4,3,2,1,0:T(8,128)(2,1)S(1)} %bitcast.27, bf16[4,2,4,16,2048]{4,3,2,1,0:T(8,128)(2,1)S(1)} %bitcast.28, ...), custom_call_target="tpu_custom_call" | custom-call | flops 1000 | bytes 1000 | tf_op jit(solution)/shard_map/project/pallas_call | solution.py:71
  30.2 1.2 add_convert_fusion.2.refs_5_
  31.6 8.0 %project.8 = (bf16[2,2,4,64,512]{4,3,2,1,0:T(8,128)(2,1)S(1)}, bf16[2,2,4,64,512]{4,3,2,1,0:T(8,128)(2,1)S(1)}) custom-call(s32[1]{0:T(128)} %bitcast.at_ref, bf16[4,2,4,16,2048]{4,3,2,1,0:T(8,128)(2,1)S(1)} %bitcast.30, bf16[4,2,4,16,2048]{4,3,2,1,0:T(8,128)(2,1)S(1)} %bitcast.31, bf16[4,2,4,16,2048]{4,3,2,1,0:T(8,128)(2,1)S(1)} %bitcast.32, ...), custom_call_target="tpu_custom_call" | custom-call | flops 1000 | bytes 1000 | tf_op jit(solution)/shard_map/project/pallas_call | solution.py:71
  40.6 1.1 copy-done.23
  41.7 4.2 %collective-permute-done.3.refs_1_.refs_5_ = bf16[2,1,4,64,512]{4,3,2,1,0:T(8,128)(2,1)} collective-permute-done((bf16[2,1,4,64,512]{4,3,2,1,0:T(8,128)(2,1)S(1)}, bf16[2,1,4,64,512]{4,3,2,1,0:T(8,128)(2,1)}, u32[]{:S(2)}, u32[]{:S(2)}) %collective-permute-start.3) | collective-permute-done | bytes 524320 | tf_op jit(solution)/shard_map/ppermute | solution.py:391
  45.9 1.3 add_convert_fusion.1.refs_5_
  47.6 5.0 %project.9 = (bf16[2,2,4,64,256]{4,3,2,1,0:T(8,128)(2,1)S(1)}, bf16[2,2,4,64,256]{4,3,2,1,0:T(8,128)(2,1)S(1)}) custom-call(s32[1]{0:T(128)} %bitcast.at_ref, bf16[4,2,4,16,2048]{4,3,2,1,0:T(8,128)(2,1)S(1)} %bitcast.34, bf16[4,2,4,16,2048]{4,3,2,1,0:T(8,128)(2,1)S(1)} %bitcast.35, bf16[4,2,4,16,2048]{4,3,2,1,0:T(8,128)(2,1)S(1)} %bitcast.36, ...), custom_call_target="tpu_custom_call" | custom-call | flops 1000 | bytes 1000 | tf_op jit(solution)/shard_map/project/pallas_call | solution.py:71
  54.3 7.5 %collective-permute-done.5.refs_1_.refs_8_ = bf16[2,1,4,64,512]{4,3,2,1,0:T(8,128)(2,1)} collective-permute-done((bf16[2,1,4,64,512]{4,3,2,1,0:T(8,128)(2,1)S(1)}, bf16[2,1,4,64,512]{4,3,2,1,0:T(8,128)(2,1)}, u32[]{:S(2)}, u32[]{:S(2)}) %collective-permute-start.5) | collective-permute-done | bytes 524320 | tf_op jit(solution)/shard_map/ppermute | solution.py:391
  61.9 1.4 add_convert_fusion
  64.0 1.9 add_convert_fusion.6
  65.8 1.5 collective-permute-start.9
  67.3 13.1 %collective-permute-done.9.refs_14_ = bf16[1,1,4,64,256]{4,3,2,1,0:T(8,128)(2,1)S(1)} collective-permute-done((bf16[1,1,4,64,256]{4,3,2,1,0:T(8,128)(2,1)S(1)}, bf16[1,1,4,64,256]{4,3,2,1,0:T(8,128)(2,1)S(1)}, u32[]{:S(2)}, u32[]{:S(2)}) %collective-permute-start.9) | collective-permute-done | bytes 131104 | tf_op jit(solution)/shard_map/ppermute | solution.py:391
  80.4 2.5 %activate.2 = (bf16[64,2048]{1,0:T(8,128)(2,1)}, bf16[3,64,2048]{2,1,0:T(8,128)(2,1)S(1)}) custom-call(bf16[2,2,4,64,256]{4,3,2,1,0:T(8,128)(2,1)S(1)} %copy-done.6, bf16[2,2,4,64,256]{4,3,2,1,0:T(8,128)(2,1)S(1)} %copy-done.9, bf16[2,1,4,64,256]{4,3,2,1,0:T(8,128)(2,1)S(1)} %copy-done.19, bf16[2,2,4,64,512]{4,3,2,1,0:T(8,128)(2,1)S(1)} %get-tuple-element.37.refs_3_, ...), custom_call_target="tpu_custom_call" | custom-call | flops 1000 | bytes 1000 | tf_op jit(solution)/shard_map/activate/pallas_call | solution.py:138
  84.1 1.7 collective-permute-start.24
  85.9 7.5 %collective-permute-done.10.refs_1_ = bf16[64,2048]{1,0:T(8,128)(2,1)} collective-permute-done((bf16[64,2048]{1,0:T(8,128)(2,1)}, bf16[64,2048]{1,0:T(8,128)(2,1)}, u32[]{:S(2)}, u32[]{:S(2)}) %collective-permute-start.10) | collective-permute-done | bytes 262176 | tf_op jit(solution)/shard_map/ppermute | solution.py:391
  95.2 1.0 copy-done.7
  96.2 1.0 copy-done.10
  97.3 1.0 copy-done.13
  99.4 1.0 copy-done.21
  100.4 2.2 activate.3
  103.2 12.2 %attend.2 = (bf16[2,64,2048]{2,1,0:T(8,128)(2,1)S(1)}, bf16[2,64,2048]{2,1,0:T(8,128)(2,1)S(1)}) custom-call(s32[1]{0:T(128)} %bitcast.at_ref, bf16[64,2048]{1,0:T(8,128)(2,1)} %get-tuple-element.45.refs_0_.q_ref, bf16[64,2048]{1,0:T(8,128)(2,1)} %collective-permute-done.10.refs_1_, bf16[64,2048]{1,0:T(8,128)(2,1)} %collective-permute-done.11.refs_2_, ...), custom_call_target="tpu_custom_call" | custom-call | flops 1000 | bytes 1000 | tf_op jit(solution)/shard_map/attend/pallas_call | solution.py:195
  116.2 1.5 collective-permute-done.26.refs_2_
  118.1 12.2 %attend.3 = (bf16[2,64,2048]{2,1,0:T(8,128)(2,1)S(1)}, bf16[2,64,2048]{2,1,0:T(8,128)(2,1)S(1)}) custom-call(s32[1]{0:T(128)} %bitcast.at_ref, bf16[64,2048]{1,0:T(8,128)(2,1)S(1)} %get-tuple-element.55.refs_0_.q_ref, bf16[64,2048]{1,0:T(8,128)(2,1)S(1)} %collective-permute-done.25.refs_1_, bf16[64,2048]{1,0:T(8,128)(2,1)S(1)} %collective-permute-done.26.refs_2_, ...), custom_call_target="tpu_custom_call" | custom-call | flops 1000 | bytes 1000 | tf_op jit(solution)/shard_map/attend/pallas_call | solution.py:195
  130.7 1.8 collective-permute-start.14
  132.5 1.6 collective-permute-start.29
  134.1 5.7 %collective-permute-done.14.refs_2_ = bf16[1,1,64,2048]{3,2,1,0:T(8,128)(2,1)S(1)} collective-permute-done((bf16[1,1,64,2048]{3,2,1,0:T(8,128)(2,1)S(1)}, bf16[1,1,64,2048]{3,2,1,0:T(8,128)(2,1)S(1)}, u32[]{:S(2)}, u32[]{:S(2)}) %collective-permute-start.14) | collective-permute-done | bytes 262176 | tf_op jit(solution)/shard_map/ppermute | solution.py:391
  139.9 1.7 finish.2
  141.6 3.9 %collective-permute-start.17 = (f32[64,128]{1,0:T(8,128)S(1)}, f32[64,128]{1,0:T(8,128)S(1)}, u32[]{:S(2)}, u32[]{:S(2)}) collective-permute-start(f32[64,128]{1,0:T(8,128)S(1)} %get-tuple-element.50.refs_0_), channel_id=1, source_target_pairs={{0,12},{4,0},{8,4},{12,8},{1,13},{5,1},{9,5},{13,9},{2,14},{6,2},{... | collective-permute-start | bytes 98312 | tf_op jit(solution)/shard_map/ppermute | solution.py:419
  147.1 3.2 %collective-permute-done.16.refs_2_ = f32[64,128]{1,0:T(8,128)S(1)} collective-permute-done((f32[64,128]{1,0:T(8,128)S(1)}, f32[64,128]{1,0:T(8,128)S(1)}, u32[]{:S(2)}, u32[]{:S(2)}) %collective-permute-start.16) | collective-permute-done | bytes 32800 | tf_op jit(solution)/shard_map/ppermute | solution.py:419
  151.4 1.5 collective-permute-start.18
  154.9 1.9 collective-permute-start.30
  157.7 1.5 collective-permute-done.31.refs_2_
  159.1 1.5 collective-permute-done.30.refs_1_
  162.0 5.3 %collective-permute-done.33 = bf16[64,2048]{1,0:T(8,128)(2,1)S(1)} collective-permute-done((bf16[64,2048]{1,0:T(8,128)(2,1)S(1)}, bf16[64,2048]{1,0:T(8,128)(2,1)S(1)}, u32[]{:S(2)}, u32[]{:S(2)}) %collective-permute-start.33) | collective-permute-done | bytes 262176 | tf_op jit(solution)/shard_map/ppermute | solution.py:391
  169.0 6.3 %output.2 = (bf16[4,16,2048]{2,1,0:T(8,128)(2,1)S(1)}, bf16[4,16,2048]{2,1,0:T(8,128)(2,1)S(1)}, bf16[4,16,2048]{2,1,0:T(8,128)(2,1)}, bf16[4,16,2048]{2,1,0:T(8,128)(2,1)}) custom-call(s32[1]{0:T(128)} %bitcast.3.index_ref, bf16[4,16,2048]{2,1,0:T(8,128)(2,1)S(1)} %bitcast.47, bf16[4,16,2048]{2,1,0:T(8,128)(2,1)S(1)} %bitcast.49, ...), custom_call_target="tpu_custom_call" | custom-call | flops 1000 | bytes 1000 | tf_op jit(solution)/shard_map/output/pallas_call | solution.py:319
  175.4 1.8 collective-permute-start.22
  177.2 1.9 collective-permute-start.23
  179.1 6.4 %output.3 = (bf16[4,16,2048]{2,1,0:T(8,128)(2,1)S(1)}, bf16[4,16,2048]{2,1,0:T(8,128)(2,1)}, bf16[4,16,2048]{2,1,0:T(8,128)(2,1)}, bf16[4,16,2048]{2,1,0:T(8,128)(2,1)}) custom-call(s32[1]{0:T(128)} %bitcast.3.index_ref, bf16[4,16,2048]{2,1,0:T(8,128)(2,1)S(1)} %bitcast.48, bf16[4,16,2048]{2,1,0:T(8,128)(2,1)S(1)} %bitcast.50, ...), custom_call_target="tpu_custom_call" | custom-call | flops 1000 | bytes 1000 | tf_op jit(solution)/shard_map/output/pallas_call | solution.py:319
  186.8 1.4 collective-permute-start.37
  188.2 2.9 %collective-permute-start.38 = (bf16[4,16,2048]{2,1,0:T(8,128)(2,1)}, bf16[4,16,2048]{2,1,0:T(8,128)(2,1)}, u32[]{:S(2)}, u32[]{:S(2)}) collective-permute-start(bf16[4,16,2048]{2,1,0:T(8,128)(2,1)} %get-tuple-element.64), channel_id=1, source_target_pairs={{0,12},{4,0},{8,4},{12,8},{1,13},{5,1},{9,5},{13,9},{2,14},{6,2},{... | collective-permute-start | bytes 786440 | tf_op jit(solution)/shard_map/ppermute | solution.py:419
  191.2 6.0 %collective-permute-done.22.refs_2_ = bf16[4,16,2048]{2,1,0:T(8,128)(2,1)S(1)} collective-permute-done((bf16[4,16,2048]{2,1,0:T(8,128)(2,1)}, bf16[4,16,2048]{2,1,0:T(8,128)(2,1)S(1)}, u32[]{:S(2)}, u32[]{:S(2)}) %collective-permute-start.22) | collective-permute-done | bytes 262176 | tf_op jit(solution)/shard_map/ppermute | solution.py:419
  197.3 6.0 %collective-permute-done.36.refs_5_ = bf16[4,16,2048]{2,1,0:T(8,128)(2,1)S(1)} collective-permute-done((bf16[4,16,2048]{2,1,0:T(8,128)(2,1)}, bf16[4,16,2048]{2,1,0:T(8,128)(2,1)S(1)}, u32[]{:S(2)}, u32[]{:S(2)}) %collective-permute-start.36) | collective-permute-done | bytes 262176 | tf_op jit(solution)/shard_map/ppermute | solution.py:419
  203.2 16.2 %collective-permute-done.37.refs_6_ = bf16[4,16,2048]{2,1,0:T(8,128)(2,1)S(1)} collective-permute-done((bf16[4,16,2048]{2,1,0:T(8,128)(2,1)}, bf16[4,16,2048]{2,1,0:T(8,128)(2,1)S(1)}, u32[]{:S(2)}, u32[]{:S(2)}) %collective-permute-start.37) | collective-permute-done | bytes 262176 | tf_op jit(solution)/shard_map/ppermute | solution.py:419
  222.1 5.5 %close.1 = bf16[8,16,2048]{2,1,0:T(8,128)(2,1)} custom-call(s32[2]{0:T(128)S(1)} %pad_add_fusion.1.at_ref, bf16[32,16,2048]{2,1,0:T(8,128)(2,1)S(1)} %bitcast.38, bf16[4,16,2048]{2,1,0:T(8,128)(2,1)S(1)} %get-tuple-element.51.refs_0_, bf16[4,16,2048]{2,1,0:T(8,128)(2,1)S(1)} %collective-permute-done.21.refs_1_, ...), custom_call_target="tpu_custom_call" | custom-call | flops 1000 | bytes 1000 | tf_op jit(solution)/shard_map/close/pallas_call | solution.py:360
  (131 shorter events, 26.9 us)
Async XLA Ops:
  6.4 9.3 %copy-start.5 = (bf16[2,2,4,64,256]{4,3,2,1,0:T(8,128)(2,1)}, bf16[2,2,4,64,256]{4,3,2,1,0:T(8,128)(2,1)S(1)}, u32[]{:S(2)}) copy-start(bf16[2,2,4,64,256]{4,3,2,1,0:T(8,128)(2,1)S(1)} %get-tuple-element.35.refs_0_) | copy-start | bytes 1572868
  6.5 9.3 %collective-permute-start = (bf16[2,2,4,64,256]{4,3,2,1,0:T(8,128)(2,1)S(1)}, bf16[2,2,4,64,256]{4,3,2,1,0:T(8,128)(2,1)S(1)}, u32[]{:S(2)}, u32[]{:S(2)}) collective-permute-start(bf16[2,2,4,64,256]{4,3,2,1,0:T(8,128)(2,1)S(1)} %get-tuple-element.36), channel_id=1, source_target_pairs={{0,1},{1,0},{2,3},{3,2},{4,5},{5,4},{6,7},{7,6},{8,9},{9,8},{10,11... | collective-permute-start | bytes 1572872 | tf_op jit(solution)/shard_map/ppermute | solution.py:391
  15.7 14.6 %collective-permute-start.2 = (bf16[2,2,4,64,512]{4,3,2,1,0:T(8,128)(2,1)}, bf16[2,2,4,64,512]{4,3,2,1,0:T(8,128)(2,1)}, u32[]{:S(2)}, u32[]{:S(2)}) collective-permute-start(bf16[2,2,4,64,512]{4,3,2,1,0:T(8,128)(2,1)} %get-tuple-element.38), channel_id=1, source_target_pairs={{0,1},{1,0},{2,3},{3,2},{4,5},{5,4},{6,7},{7,6},{8,9},{9,8},{10,11... | collective-permute-start | bytes 3145736 | tf_op jit(solution)/shard_map/ppermute | solution.py:391
  16.6 12.9 %collective-permute-start.1 = (bf16[2,1,4,64,256]{4,3,2,1,0:T(8,128)(2,1)S(1)}, bf16[2,1,4,64,256]{4,3,2,1,0:T(8,128)(2,1)S(1)}, u32[]{:S(2)}, u32[]{:S(2)}) collective-permute-start(bf16[2,1,4,64,256]{4,3,2,1,0:T(8,128)(2,1)S(1)} %add_convert_fusion.5.refs_5_), channel_id=1, source_target_pairs={{0,2},{1,3},{2,0},{3,1},{4,6},{5,7},{6,4},{7,5},{8,10},{9,11},{10,... | collective-permute-start | bytes 786440 | tf_op jit(solution)/shard_map/ppermute | solution.py:391
  30.2 15.7 %collective-permute-start.4 = (bf16[2,2,4,64,512]{4,3,2,1,0:T(8,128)(2,1)}, bf16[2,2,4,64,512]{4,3,2,1,0:T(8,128)(2,1)}, u32[]{:S(2)}, u32[]{:S(2)}) collective-permute-start(bf16[2,2,4,64,512]{4,3,2,1,0:T(8,128)(2,1)} %tie.3), channel_id=1, source_target_pairs={{0,1},{1,0},{2,3},{3,2},{4,5},{5,4},{6,7},{7,6},{8,9},{9,8},{10,11... | collective-permute-start | bytes 3145736 | tf_op jit(solution)/shard_map/ppermute | solution.py:391
  31.4 14.5 %collective-permute-start.3 = (bf16[2,1,4,64,512]{4,3,2,1,0:T(8,128)(2,1)S(1)}, bf16[2,1,4,64,512]{4,3,2,1,0:T(8,128)(2,1)}, u32[]{:S(2)}, u32[]{:S(2)}) collective-permute-start(bf16[2,1,4,64,512]{4,3,2,1,0:T(8,128)(2,1)S(1)} %add_convert_fusion.2.refs_5_), channel_id=1, source_target_pairs={{0,2},{1,3},{2,0},{3,1},{4,6},{5,7},{6,4},{7,5},{8,10},{9,11},{10,... | collective-permute-start | bytes 1572872 | tf_op jit(solution)/shard_map/ppermute | solution.py:391
  45.9 15.9 %collective-permute-start.6 = (bf16[2,2,4,64,512]{4,3,2,1,0:T(8,128)(2,1)}, bf16[2,2,4,64,512]{4,3,2,1,0:T(8,128)(2,1)}, u32[]{:S(2)}, u32[]{:S(2)}) collective-permute-start(bf16[2,2,4,64,512]{4,3,2,1,0:T(8,128)(2,1)} %tie.4), channel_id=1, source_target_pairs={{0,1},{1,0},{2,3},{3,2},{4,5},{5,4},{6,7},{7,6},{8,9},{9,8},{10,11... | collective-permute-start | bytes 3145736 | tf_op jit(solution)/shard_map/ppermute | solution.py:391
  47.3 14.5 %collective-permute-start.5 = (bf16[2,1,4,64,512]{4,3,2,1,0:T(8,128)(2,1)S(1)}, bf16[2,1,4,64,512]{4,3,2,1,0:T(8,128)(2,1)}, u32[]{:S(2)}, u32[]{:S(2)}) collective-permute-start(bf16[2,1,4,64,512]{4,3,2,1,0:T(8,128)(2,1)S(1)} %add_convert_fusion.1.refs_5_), channel_id=1, source_target_pairs={{0,2},{1,3},{2,0},{3,1},{4,6},{5,7},{6,4},{7,5},{8,10},{9,11},{10,... | collective-permute-start | bytes 1572872 | tf_op jit(solution)/shard_map/ppermute | solution.py:391
  54.3 26.1 %copy-start.19 = (bf16[2,1,4,64,256]{4,3,2,1,0:T(8,128)(2,1)S(1)}, bf16[2,1,4,64,256]{4,3,2,1,0:T(8,128)(2,1)}, u32[]{:S(2)}) copy-start(bf16[2,1,4,64,256]{4,3,2,1,0:T(8,128)(2,1)} %copy-done.18) | copy-start | bytes 786436
  61.8 18.6 %copy-start.6 = (bf16[2,2,4,64,256]{4,3,2,1,0:T(8,128)(2,1)S(1)}, bf16[2,2,4,64,256]{4,3,2,1,0:T(8,128)(2,1)}, u32[]{:S(2)}) copy-start(bf16[2,2,4,64,256]{4,3,2,1,0:T(8,128)(2,1)} %copy-done.5) | copy-start | bytes 1572868
  61.8 18.6 %copy-start.9 = (bf16[2,2,4,64,256]{4,3,2,1,0:T(8,128)(2,1)S(1)}, bf16[2,2,4,64,256]{4,3,2,1,0:T(8,128)(2,1)}, u32[]{:S(2)}) copy-start(bf16[2,2,4,64,256]{4,3,2,1,0:T(8,128)(2,1)} %copy-done.8) | copy-start | bytes 1572868
  61.8 18.7 %copy-start.12 = (bf16[2,2,4,64,256]{4,3,2,1,0:T(8,128)(2,1)S(1)}, bf16[2,2,4,64,256]{4,3,2,1,0:T(8,128)(2,1)}, u32[]{:S(2)}) copy-start(bf16[2,2,4,64,256]{4,3,2,1,0:T(8,128)(2,1)} %copy-done.11) | copy-start | bytes 1572868
  61.8 2.2 collective-permute-start.8
  63.3 17.1 %collective-permute-start.7 = (bf16[2,1,4,64,512]{4,3,2,1,0:T(8,128)(2,1)S(1)}, bf16[2,1,4,64,512]{4,3,2,1,0:T(8,128)(2,1)S(1)}, u32[]{:S(2)}, u32[]{:S(2)}) collective-permute-start(bf16[2,1,4,64,512]{4,3,2,1,0:T(8,128)(2,1)S(1)} %add_convert_fusion), channel_id=1, source_target_pairs={{0,2},{1,3},{2,0},{3,1},{4,6},{5,7},{6,4},{7,5},{8,10},{9,11},{10,... | collective-permute-start | bytes 1572872 | tf_op jit(solution)/shard_map/ppermute | solution.py:391
  63.9 19.0 %copy-start.14 = (bf16[2,2,4,64,256]{4,3,2,1,0:T(8,128)(2,1)}, bf16[2,2,4,64,256]{4,3,2,1,0:T(8,128)(2,1)S(1)}, u32[]{:S(2)}) copy-start(bf16[2,2,4,64,256]{4,3,2,1,0:T(8,128)(2,1)S(1)} %collective-permute-done.8.refs_13_) | copy-start | bytes 1572868
  65.8 27.5 %copy-start.33 = (s32[512]{0:T(512)S(1)}, s32[512]{0:T(512)}, u32[]{:S(2)}) copy-start(s32[512]{0:T(512)} %param.13) | copy-start | bytes 6148
  65.8 27.5 %copy-start.34 = (s32[512]{0:T(512)S(1)}, s32[512]{0:T(512)}, u32[]{:S(2)}) copy-start(s32[512]{0:T(512)} %param.12) | copy-start | bytes 6148
  65.8 14.6 %collective-permute-start.9 = (bf16[1,1,4,64,256]{4,3,2,1,0:T(8,128)(2,1)S(1)}, bf16[1,1,4,64,256]{4,3,2,1,0:T(8,128)(2,1)S(1)}, u32[]{:S(2)}, u32[]{:S(2)}) collective-permute-start(bf16[1,1,4,64,256]{4,3,2,1,0:T(8,128)(2,1)S(1)} %get-tuple-element.66), channel_id=1, source_target_pairs={{0,2},{1,3},{2,0},{3,1},{4,6},{5,7},{6,4},{7,5},{8,10},{9,11},{10,... | collective-permute-start | bytes 393224 | tf_op jit(solution)/shard_map/ppermute | solution.py:391
  83.9 9.5 %collective-permute-start.10 = (bf16[64,2048]{1,0:T(8,128)(2,1)}, bf16[64,2048]{1,0:T(8,128)(2,1)}, u32[]{:S(2)}, u32[]{:S(2)}) collective-permute-start(bf16[64,2048]{1,0:T(8,128)(2,1)} %get-tuple-element.45.refs_0_.q_ref), channel_id=1, source_target_pairs={{0,2},{1,3},{2,0},{3,1},{4,6},{5,7},{6,4},{7,5},{8,10},{9,11},{10,... | collective-permute-start | bytes 786440 | tf_op jit(solution)/shard_map/ppermute | solution.py:391
  84.1 11.1 %collective-permute-start.24 = (bf16[1,1,4,64,256]{4,3,2,1,0:T(8,128)(2,1)}, bf16[1,1,4,64,256]{4,3,2,1,0:T(8,128)(2,1)S(1)}, u32[]{:S(2)}, u32[]{:S(2)}) collective-permute-start(bf16[1,1,4,64,256]{4,3,2,1,0:T(8,128)(2,1)} %get-tuple-element.65), channel_id=1, source_target_pairs={{0,2},{1,3},{2,0},{3,1},{4,6},{5,7},{6,4},{7,5},{8,10},{9,11},{10,... | collective-permute-start | bytes 393224 | tf_op jit(solution)/shard_map/ppermute | solution.py:391
  85.9 17.3 %collective-permute-start.11 = (bf16[64,2048]{1,0:T(8,128)(2,1)}, bf16[64,2048]{1,0:T(8,128)(2,1)}, u32[]{:S(2)}, u32[]{:S(2)}) collective-permute-start(bf16[64,2048]{1,0:T(8,128)(2,1)} %get-tuple-element.45.refs_0_.q_ref), channel_id=1, source_target_pairs={{0,1},{1,0},{2,3},{3,2},{4,5},{5,4},{6,7},{7,6},{8,9},{9,8},{10,11... | collective-permute-start | bytes 786440 | tf_op jit(solution)/shard_map/ppermute | solution.py:391
  93.3 9.8 %collective-permute-start.12 = (bf16[64,2048]{1,0:T(8,128)(2,1)}, bf16[64,2048]{1,0:T(8,128)(2,1)}, u32[]{:S(2)}, u32[]{:S(2)}) collective-permute-start(bf16[64,2048]{1,0:T(8,128)(2,1)} %collective-permute-done.10.refs_1_), channel_id=1, source_target_pairs={{0,1},{1,0},{2,3},{3,2},{4,5},{5,4},{6,7},{7,6},{8,9},{9,8},{10,11... | collective-permute-start | bytes 786440 | tf_op jit(solution)/shard_map/ppermute | solution.py:391
  102.6 13.3 %collective-permute-start.25 = (bf16[64,2048]{1,0:T(8,128)(2,1)S(1)}, bf16[64,2048]{1,0:T(8,128)(2,1)S(1)}, u32[]{:S(2)}, u32[]{:S(2)}) collective-permute-start(bf16[64,2048]{1,0:T(8,128)(2,1)S(1)} %get-tuple-element.55.refs_0_.q_ref), channel_id=1, source_target_pairs={{0,2},{1,3},{2,0},{3,1},{4,6},{5,7},{6,4},{7,5},{8,10},{9,11},{10,... | collective-permute-start | bytes 786440 | tf_op jit(solution)/shard_map/ppermute | solution.py:391
  115.4 15.2 %collective-permute-start.13 = (bf16[2,64,2048]{2,1,0:T(8,128)(2,1)S(1)}, bf16[2,64,2048]{2,1,0:T(8,128)(2,1)S(1)}, u32[]{:S(2)}, u32[]{:S(2)}) collective-permute-start(bf16[2,64,2048]{2,1,0:T(8,128)(2,1)S(1)} %get-tuple-element.48), channel_id=1, source_target_pairs={{0,1},{1,0},{2,3},{3,2},{4,5},{5,4},{6,7},{7,6},{8,9},{9,8},{10,11... | collective-permute-start | bytes 1572872 | tf_op jit(solution)/shard_map/ppermute | solution.py:391
  115.7 2.0 collective-permute-start.26
  116.0 2.1 collective-permute-start.27
  130.3 9.6 %copy-start.17 = (bf16[3,64,2048]{2,1,0:T(8,128)(2,1)S(1)}, bf16[3,64,2048]{2,1,0:T(8,128)(2,1)}, u32[]{:S(2)}) copy-start(bf16[3,64,2048]{2,1,0:T(8,128)(2,1)} %copy-done.16) | copy-start | bytes 2359300
  130.3 2.2 collective-permute-start.28
  130.7 9.2 %collective-permute-start.14 = (bf16[1,1,64,2048]{3,2,1,0:T(8,128)(2,1)S(1)}, bf16[1,1,64,2048]{3,2,1,0:T(8,128)(2,1)S(1)}, u32[]{:S(2)}, u32[]{:S(2)}) collective-permute-start(bf16[1,1,64,2048]{3,2,1,0:T(8,128)(2,1)S(1)} %add_convert_fusion.4), channel_id=1, source_target_pairs={{0,2},{1,3},{2,0},{3,1},{4,6},{5,7},{6,4},{7,5},{8,10},{9,11},{10,... | collective-permute-start | bytes 786440 | tf_op jit(solution)/shard_map/ppermute | solution.py:391
  132.5 20.4 %collective-permute-start.29 = (bf16[1,1,64,2048]{3,2,1,0:T(8,128)(2,1)S(1)}, bf16[1,1,64,2048]{3,2,1,0:T(8,128)(2,1)S(1)}, u32[]{:S(2)}, u32[]{:S(2)}) collective-permute-start(bf16[1,1,64,2048]{3,2,1,0:T(8,128)(2,1)S(1)} %add_convert_fusion.3), channel_id=1, source_target_pairs={{0,2},{1,3},{2,0},{3,1},{4,6},{5,7},{6,4},{7,5},{8,10},{9,11},{10,... | collective-permute-start | bytes 786440 | tf_op jit(solution)/shard_map/ppermute | solution.py:391
  141.6 5.5 %collective-permute-start.17 = (f32[64,128]{1,0:T(8,128)S(1)}, f32[64,128]{1,0:T(8,128)S(1)}, u32[]{:S(2)}, u32[]{:S(2)}) collective-permute-start(f32[64,128]{1,0:T(8,128)S(1)} %get-tuple-element.50.refs_0_), channel_id=1, source_target_pairs={{0,12},{4,0},{8,4},{12,8},{1,13},{5,1},{9,5},{13,9},{2,14},{6,2},{... | collective-permute-start | bytes 98312 | tf_op jit(solution)/shard_map/ppermute | solution.py:419
  145.5 4.8 %collective-permute-start.16 = (f32[64,128]{1,0:T(8,128)S(1)}, f32[64,128]{1,0:T(8,128)S(1)}, u32[]{:S(2)}, u32[]{:S(2)}) collective-permute-start(f32[64,128]{1,0:T(8,128)S(1)} %get-tuple-element.50.refs_0_), channel_id=1, source_target_pairs={{0,8},{4,12},{8,0},{12,4},{1,9},{5,13},{9,1},{13,5},{2,10},{6,14},... | collective-permute-start | bytes 98312 | tf_op jit(solution)/shard_map/ppermute | solution.py:419
  145.5 5.7 %collective-permute-start.15 = (f32[64,128]{1,0:T(8,128)S(1)}, f32[64,128]{1,0:T(8,128)S(1)}, u32[]{:S(2)}, u32[]{:S(2)}) collective-permute-start(f32[64,128]{1,0:T(8,128)S(1)} %get-tuple-element.50.refs_0_), channel_id=1, source_target_pairs={{0,4},{4,8},{8,12},{12,0},{1,5},{5,9},{9,13},{13,1},{2,6},{6,10},{... | collective-permute-start | bytes 98312 | tf_op jit(solution)/shard_map/ppermute | solution.py:419
  151.4 10.1 %collective-permute-start.18 = (bf16[64,2048]{1,0:T(8,128)(2,1)S(1)}, bf16[64,2048]{1,0:T(8,128)(2,1)S(1)}, u32[]{:S(2)}, u32[]{:S(2)}) collective-permute-start(bf16[64,2048]{1,0:T(8,128)(2,1)S(1)} %gate.2), channel_id=1, source_target_pairs={{0,2},{1,3},{2,0},{3,1},{4,6},{5,7},{6,4},{7,5},{8,10},{9,11},{10,... | collective-permute-start | bytes 786440 | tf_op jit(solution)/shard_map/ppermute | solution.py:391
  153.7 3.9 %collective-permute-start.32 = (f32[64,128]{1,0:T(8,128)S(1)}, f32[64,128]{1,0:T(8,128)S(1)}, u32[]{:S(2)}, u32[]{:S(2)}) collective-permute-start(f32[64,128]{1,0:T(8,128)S(1)} %get-tuple-element.60.refs_0_), channel_id=1, source_target_pairs={{0,12},{4,0},{8,4},{12,8},{1,13},{5,1},{9,5},{13,9},{2,14},{6,2},{... | collective-permute-start | bytes 98312 | tf_op jit(solution)/shard_map/ppermute | solution.py:419
  154.3 4.8 %collective-permute-start.31 = (f32[64,128]{1,0:T(8,128)S(1)}, f32[64,128]{1,0:T(8,128)S(1)}, u32[]{:S(2)}, u32[]{:S(2)}) collective-permute-start(f32[64,128]{1,0:T(8,128)S(1)} %get-tuple-element.60.refs_0_), channel_id=1, source_target_pairs={{0,8},{4,12},{8,0},{12,4},{1,9},{5,13},{9,1},{13,5},{2,10},{6,14},... | collective-permute-start | bytes 98312 | tf_op jit(solution)/shard_map/ppermute | solution.py:419
  154.9 5.7 %collective-permute-start.30 = (f32[64,128]{1,0:T(8,128)S(1)}, f32[64,128]{1,0:T(8,128)S(1)}, u32[]{:S(2)}, u32[]{:S(2)}) collective-permute-start(f32[64,128]{1,0:T(8,128)S(1)} %get-tuple-element.60.refs_0_), channel_id=1, source_target_pairs={{0,4},{4,8},{8,12},{12,0},{1,5},{5,9},{9,13},{13,1},{2,6},{6,10},{... | collective-permute-start | bytes 98312 | tf_op jit(solution)/shard_map/ppermute | solution.py:419
  160.9 6.4 %collective-permute-start.33 = (bf16[64,2048]{1,0:T(8,128)(2,1)S(1)}, bf16[64,2048]{1,0:T(8,128)(2,1)S(1)}, u32[]{:S(2)}, u32[]{:S(2)}) collective-permute-start(bf16[64,2048]{1,0:T(8,128)(2,1)S(1)} %gate.3), channel_id=1, source_target_pairs={{0,2},{1,3},{2,0},{3,1},{4,6},{5,7},{6,4},{7,5},{8,10},{9,11},{10,... | collective-permute-start | bytes 786440 | tf_op jit(solution)/shard_map/ppermute | solution.py:391
  161.5 5.8 %collective-permute-start.19 = (bf16[64,2048]{1,0:T(8,128)(2,1)S(1)}, bf16[64,2048]{1,0:T(8,128)(2,1)S(1)}, u32[]{:S(2)}, u32[]{:S(2)}) collective-permute-start(bf16[64,2048]{1,0:T(8,128)(2,1)S(1)} %gate.2), channel_id=1, source_target_pairs={{0,1},{1,0},{2,3},{3,2},{4,5},{5,4},{6,7},{7,6},{8,9},{9,8},{10,11... | collective-permute-start | bytes 786440 | tf_op jit(solution)/shard_map/ppermute | solution.py:391
  161.5 6.5 %collective-permute-start.20 = (bf16[64,2048]{1,0:T(8,128)(2,1)S(1)}, bf16[64,2048]{1,0:T(8,128)(2,1)}, u32[]{:S(2)}, u32[]{:S(2)}) collective-permute-start(bf16[64,2048]{1,0:T(8,128)(2,1)S(1)} %collective-permute-done.18), channel_id=1, source_target_pairs={{0,1},{1,0},{2,3},{3,2},{4,5},{5,4},{6,7},{7,6},{8,9},{9,8},{10,11... | collective-permute-start | bytes 786440 | tf_op jit(solution)/shard_map/ppermute | solution.py:391
  162.0 17.1 %collective-permute-start.34 = (bf16[64,2048]{1,0:T(8,128)(2,1)S(1)}, bf16[64,2048]{1,0:T(8,128)(2,1)S(1)}, u32[]{:S(2)}, u32[]{:S(2)}) collective-permute-start(bf16[64,2048]{1,0:T(8,128)(2,1)S(1)} %gate.3), channel_id=1, source_target_pairs={{0,1},{1,0},{2,3},{3,2},{4,5},{5,4},{6,7},{7,6},{8,9},{9,8},{10,11... | collective-permute-start | bytes 786440 | tf_op jit(solution)/shard_map/ppermute | solution.py:391
  167.3 11.8 %collective-permute-start.35 = (bf16[64,2048]{1,0:T(8,128)(2,1)S(1)}, bf16[64,2048]{1,0:T(8,128)(2,1)S(1)}, u32[]{:S(2)}, u32[]{:S(2)}) collective-permute-start(bf16[64,2048]{1,0:T(8,128)(2,1)S(1)} %collective-permute-done.33), channel_id=1, source_target_pairs={{0,1},{1,0},{2,3},{3,2},{4,5},{5,4},{6,7},{7,6},{8,9},{9,8},{10,11... | collective-permute-start | bytes 786440 | tf_op jit(solution)/shard_map/ppermute | solution.py:391
  175.3 12.9 %collective-permute-start.21 = (bf16[4,16,2048]{2,1,0:T(8,128)(2,1)S(1)}, bf16[4,16,2048]{2,1,0:T(8,128)(2,1)S(1)}, u32[]{:S(2)}, u32[]{:S(2)}) collective-permute-start(bf16[4,16,2048]{2,1,0:T(8,128)(2,1)S(1)} %get-tuple-element.52), channel_id=1, source_target_pairs={{0,4},{4,8},{8,12},{12,0},{1,5},{5,9},{9,13},{13,1},{2,6},{6,10},{... | collective-permute-start | bytes 786440 | tf_op jit(solution)/shard_map/ppermute | solution.py:419
  175.4 21.8 %collective-permute-start.22 = (bf16[4,16,2048]{2,1,0:T(8,128)(2,1)}, bf16[4,16,2048]{2,1,0:T(8,128)(2,1)S(1)}, u32[]{:S(2)}, u32[]{:S(2)}) collective-permute-start(bf16[4,16,2048]{2,1,0:T(8,128)(2,1)} %get-tuple-element.53), channel_id=1, source_target_pairs={{0,8},{4,12},{8,0},{12,4},{1,9},{5,13},{9,1},{13,5},{2,10},{6,14},... | collective-permute-start | bytes 786440 | tf_op jit(solution)/shard_map/ppermute | solution.py:419
  177.2 20.0 %collective-permute-start.23 = (bf16[4,16,2048]{2,1,0:T(8,128)(2,1)}, bf16[4,16,2048]{2,1,0:T(8,128)(2,1)}, u32[]{:S(2)}, u32[]{:S(2)}) collective-permute-start(bf16[4,16,2048]{2,1,0:T(8,128)(2,1)} %get-tuple-element.54), channel_id=1, source_target_pairs={{0,12},{4,0},{8,4},{12,8},{1,13},{5,1},{9,5},{13,9},{2,14},{6,2},{... | collective-permute-start | bytes 786440 | tf_op jit(solution)/shard_map/ppermute | solution.py:419
  186.2 17.0 %collective-permute-start.36 = (bf16[4,16,2048]{2,1,0:T(8,128)(2,1)}, bf16[4,16,2048]{2,1,0:T(8,128)(2,1)S(1)}, u32[]{:S(2)}, u32[]{:S(2)}) collective-permute-start(bf16[4,16,2048]{2,1,0:T(8,128)(2,1)} %get-tuple-element.62), channel_id=1, source_target_pairs={{0,4},{4,8},{8,12},{12,0},{1,5},{5,9},{9,13},{13,1},{2,6},{6,10},{... | collective-permute-start | bytes 786440 | tf_op jit(solution)/shard_map/ppermute | solution.py:419
  186.8 32.7 %collective-permute-start.37 = (bf16[4,16,2048]{2,1,0:T(8,128)(2,1)}, bf16[4,16,2048]{2,1,0:T(8,128)(2,1)S(1)}, u32[]{:S(2)}, u32[]{:S(2)}) collective-permute-start(bf16[4,16,2048]{2,1,0:T(8,128)(2,1)} %get-tuple-element.63), channel_id=1, source_target_pairs={{0,8},{4,12},{8,0},{12,4},{1,9},{5,13},{9,1},{13,5},{2,10},{6,14},... | collective-permute-start | bytes 786440 | tf_op jit(solution)/shard_map/ppermute | solution.py:419
  188.2 32.0 %collective-permute-start.38 = (bf16[4,16,2048]{2,1,0:T(8,128)(2,1)}, bf16[4,16,2048]{2,1,0:T(8,128)(2,1)}, u32[]{:S(2)}, u32[]{:S(2)}) collective-permute-start(bf16[4,16,2048]{2,1,0:T(8,128)(2,1)} %get-tuple-element.64), channel_id=1, source_target_pairs={{0,12},{4,0},{8,4},{12,8},{1,13},{5,1},{9,5},{13,9},{2,14},{6,2},{... | collective-permute-start | bytes 786440 | tf_op jit(solution)/shard_map/ppermute | solution.py:419
  (26 other events, 32.5 us)

commit v4 on v3

--- a/solution.py
+++ b/solution.py
@@ -9,7 +9,7 @@
 
 DH = 128
 EPSILON = 1e-05
-VMEM_LIMIT = 48 * 1024 * 1024
+VMEM_LIMIT = 60 * 1024 * 1024
 
 bf16 = jnp.bfloat16
 f32 = jnp.float32
@@ -27,69 +27,98 @@
 LIGHT = pl.CostEstimate(flops=1000, bytes_accessed=1000, transcendentals=0)
 
 
-def project_kernel(parts, owners, at_ref, *refs):
-    rows, w_ref = refs[:owners], refs[owners]
-    keep_ref, send_ref, lhs_ref = refs[-3 - parts:-parts]
-    wides = refs[-parts:]
-    zs, chunks, _, piece, _ = rows[0].shape
+def shuffle(depth):
+    row = lax.broadcasted_iota(jnp.int32, (depth, depth), 0)
+    column = lax.broadcasted_iota(jnp.int32, (depth, depth), 1)
+    slot = column % 8
+    return jnp.where(row == column - slot + 2 * (slot % 4) + slot // 4, 1.0, 0.0).astype(bf16)
+
+
+def split_rows(x):
+    x = x.reshape(x.shape[0] // 32, 4, 8, DH)
+    slot = lax.broadcasted_iota(jnp.int32, (x.shape[0], 8, DH), 1) % 4
+    turned = [x[:, 0]] + [pltpu.roll(x[:, j], j, 1) for j in range(1, 4)]
+    outs = []
+    for i in range(4):
+        out = turned[0]
+        for j in range(1, 4):
+            out = jnp.where(slot == (i + j) % 4, turned[j], out)
+        outs.append(out if i == 0 else pltpu.roll(out, 8 - i, 1))
+    return [out.reshape(-1, DH).astype(bf16) for out in outs]
+
+
+def arrange_kernel(owners, at_ref, *refs):
+    rows, out_ref = refs[:owners], refs[owners]
+    zs, chunks, _, piece, depth = rows[0].shape
+    lhs = jnp.concatenate(
+        [rows[p][z, r, 0] for r in range(chunks) for p in range(owners) for z in range(zs)]
+    )
+    out_ref[...] = jnp.dot(lhs, shuffle(depth), preferred_element_type=f32).astype(bf16)
+
+
+def arrange_rows(at, tokens):
+    zs, chunks, owners, piece, depth = tokens.shape
+    rows, span = zs * chunks * owners * piece, 256
+    return pl.pallas_call(
+        functools.partial(arrange_kernel, owners),
+        grid_spec=pltpu.PrefetchScalarGridSpec(
+            num_scalar_prefetch=1,
+            grid=(depth // span,),
+            in_specs=[
+                pl.BlockSpec(
+                    (zs, chunks, 1, piece, span), lambda j, at, p=p: (0, 0, at[0] ^ p, 0, j)
+                )
+                for p in range(owners)
+            ],
+            out_specs=pl.BlockSpec((rows, span), lambda j, at: (0, j)),
+        ),
+        out_shape=jax.ShapeDtypeStruct((rows, depth), bf16),
+        compiler_params=params(),
+        cost_estimate=LIGHT,
+        name="arrange",
+    )(at, *[tokens] * owners)
+
+
+def project_kernel(parts, t_ref, w_ref, *refs):
+    keep_ref, send_ref = refs[-2:]
+    chunks, half, _, each, _ = keep_ref.shape
     depth = w_ref.shape[0] // parts
-
-    @pl.when(pl.program_id(0) == 0)
-    def _():
-        first = 0
-        for r in range(chunks):
-            for p in range(owners):
-                for z in range(zs):
-                    lhs_ref[first:first + piece, :] = rows[p][z, r, 0]
-                    first += piece
-
     flat = w_ref.reshape(depth * parts * 4, DH)
     res = None
-    for k, wide in enumerate(wides):
-        wide[...] = flat[k * depth * 4:(k + 1) * depth * 4, :].astype(f32)
+    for k in range(parts):
         rhs = jnp.concatenate(
-            [wide[pl.ds(i, depth, stride=4), :].astype(bf16) for i in range(4)], axis=1
+            split_rows(flat[k * depth * 4:(k + 1) * depth * 4, :].astype(f32)), axis=1
         )
-        term = jnp.dot(lhs_ref[:, k * depth:(k + 1) * depth], rhs, preferred_element_type=f32)
+        term = jnp.dot(t_ref[:, k * depth:(k + 1) * depth], rhs, preferred_element_type=f32)
         res = term if res is None else res + term
     res = res.astype(bf16)
-    half, each = keep_ref.shape[1], keep_ref.shape[3]
     for r in range(chunks):
-        for p in range(owners):
+        for p in range(2 * half):
             into = keep_ref if p < half else send_ref
-            first = (r * owners + p) * each
+            first = (r * 2 * half + p) * each
             for i in range(4):
                 into[r, p % half, i] = res[first:first + each, i * DH:(i + 1) * DH]
 
 
-def project(at, tokens, w, head_first, heads, after):
-    zs, chunks, owners, piece, depth = tokens.shape
-    half, each = owners // 2, zs * piece
+def project(tokens, w, head_first, heads, chunks, owners, after):
+    rows, depth = tokens.shape
+    half, each = owners // 2, rows // (chunks * owners)
     parts = 4 if depth % 512 == 0 else 1
     shape = jax.ShapeDtypeStruct((chunks, half, 4, each, heads * DH), bf16)
-    spec = pl.BlockSpec((chunks, half, 4, each, DH), lambda j, at: (0, 0, 0, 0, j))
-    return pl.pallas_call(
-        functools.partial(project_kernel, parts, owners),
-        grid_spec=pltpu.PrefetchScalarGridSpec(
-            num_scalar_prefetch=1,
-            grid=(heads,),
-            in_specs=[
-                pl.BlockSpec(
-                    (zs, chunks, 1, piece, depth), lambda j, at, p=p: (0, 0, at[0] ^ p, 0, 0)
-                )
-                for p in range(owners)
-            ]
-            + [pl.BlockSpec((depth, 4, DH), lambda j, at: (0, 0, head_first + j))]
-            + [pl.BlockSpec(memory_space=pl.ANY)] * len(after),
-            out_specs=(spec, spec),
-            scratch_shapes=[pltpu.VMEM((chunks * owners * each, depth), bf16)]
-            + [pltpu.VMEM((depth // parts * 4, DH), f32) for _ in range(parts)],
-        ),
+    spec = pl.BlockSpec((chunks, half, 4, each, DH), lambda j: (0, 0, 0, 0, j))
+    return pl.pallas_call(
+        functools.partial(project_kernel, parts),
+        grid=(heads,),
+        in_specs=[
+            pl.BlockSpec((rows, depth), lambda j: (0, 0)),
+            pl.BlockSpec((depth, 4, DH), lambda j: (0, 0, head_first + j)),
+        ] + [pl.BlockSpec(memory_space=pl.ANY)] * len(after),
+        out_specs=(spec, spec),
         out_shape=(shape, shape),
         compiler_params=params(),
         cost_estimate=LIGHT,
         name="project",
-    )(at, *[tokens] * owners, w, *after)
+    )(tokens, w, *after)
 
 
 def tie_kernel(*refs):
@@ -104,9 +133,35 @@
         out_specs=anywhere,
         out_shape=jax.ShapeDtypeStruct(x.shape, x.dtype),
         input_output_aliases={0: 0},
+        compiler_params=params(),
         cost_estimate=LIGHT,
         name="tie",
     )(x, *after)
+
+
+def fold_kernel(*refs):
+    refs[-1][...] = sum(r[...].astype(f32) for r in refs[:-1]).astype(bf16)
+
+
+def fold(terms, first, count):
+    half = terms[-1][0].shape[1] // 2
+    tail = terms[0][0].shape[2:]
+    steps = 2 if tail[-1] % 256 == 0 else 1
+    block = (count, half) + tail[:-1] + (tail[-1] // steps,)
+    middle = (0,) * (len(tail) - 1)
+    return pl.pallas_call(
+        fold_kernel,
+        grid=(steps,),
+        in_specs=[
+            pl.BlockSpec(block, lambda j, at=(first - offset) // count: (at, 1) + middle + (j,))
+            for _, offset in terms
+        ],
+        out_specs=pl.BlockSpec(block, lambda j: (0, 0) + middle + (j,)),
+        out_shape=jax.ShapeDtypeStruct((count, half) + tail, bf16),
+        compiler_params=params(),
+        cost_estimate=LIGHT,
+        name="fold",
+    )(*[t for t, _ in terms])
 
 
 def activate_kernel(counts, *refs):
@@ -170,15 +225,17 @@
                 first = p * each + z * piece
                 mask_ref[first:first + piece, :] = jnp.where(seen, 1.0, 0.0).astype(bf16)
 
-    query = jnp.concatenate([q[...] for q in queries])
-    u = lax.dot_general(
-        query, k_ref[...], (((1,), (1,)), ((), ())), preferred_element_type=f32
-    ) * (0.5 * DH ** (-0.5))
-    weights = (u + u * jnp.tanh(u)).astype(bf16) * mask_ref[...]
-    term = jnp.dot(weights, v_ref[...], preferred_element_type=f32).astype(bf16)
-    for p in range(owners):
-        into = keep_ref if p < half else send_ref
-        into[p % half] = term[p * each:(p + 1) * each]
+    for h in range(k_ref.shape[1] // DH):
+        at = slice(h * DH, (h + 1) * DH)
+        query = jnp.concatenate([q[:, at] for q in queries])
+        u = lax.dot_general(
+            query, k_ref[:, at], (((1,), (1,)), ((), ())), preferred_element_type=f32
+        ) * (0.5 * DH ** (-0.5))
+        weights = (u + u * jnp.tanh(u)).astype(bf16) * mask_ref[...]
+        term = jnp.dot(weights, v_ref[:, at], preferred_element_type=f32).astype(bf16)
+        for p in range(owners):
+            into = keep_ref if p < half else send_ref
+            into[p % half, :, at] = term[p * each:(p + 1) * each]
 
 
 def edge_spec(edges, r, p):
@@ -189,15 +246,16 @@
 def attend(at, r, queries, k_cache, v_cache, edges):
     owners, (each, width) = len(queries), queries[0].shape
     rows, events, half = owners * each, k_cache.shape[0], owners // 2
-    cache = pl.BlockSpec((events, DH), lambda j, at: (0, j))
+    span = 4 * DH if width % (4 * DH) == 0 else DH
+    cache = pl.BlockSpec((events, span), lambda j, at: (0, j))
     shape = jax.ShapeDtypeStruct((half, each, width), bf16)
-    spec = pl.BlockSpec((half, each, DH), lambda j, at: (0, 0, j))
+    spec = pl.BlockSpec((half, each, span), lambda j, at: (0, 0, j))
     return pl.pallas_call(
         functools.partial(attend_kernel, owners),
         grid_spec=pltpu.PrefetchScalarGridSpec(
             num_scalar_prefetch=1,
-            grid=(width // DH,),
-            in_specs=[pl.BlockSpec((each, DH), lambda j, at: (0, j))] * owners
+            grid=(width // span,),
+            in_specs=[pl.BlockSpec((each, span), lambda j, at: (0, j))] * owners
             + [edge_spec(edges, r, p) for p in range(owners)]
             + [cache, cache],
             out_specs=(spec, spec),
@@ -334,43 +392,36 @@
 
 def close_kernel(counts, at_ref, t_ref, *refs):
     out_ref, first = refs[-1], 0
+    owners = refs[0].shape[0]
     for r, count in enumerate(counts):
         terms = refs[first:first + count]
         first += count
-
-        @pl.when(pl.program_id(0) == r)
-        def _():
-            total = t_ref[...].astype(f32)
+        for p in range(owners):
+            total = t_ref[r * owners + p].astype(f32)
             for term in terms:
-                total = total + term[...].astype(f32)
-            out_ref[...] = total.astype(bf16)
-
-
-def close(place, first, tokens, chunks):
+                total = total + term[p ^ at_ref[0]].astype(f32)
+            out_ref[r * owners + p] = total.astype(bf16)
+
+
+def close(place, index, tokens, chunks):
     owners, piece, width = chunks[0][0].shape
-    specs = []
-    for r, terms in enumerate(chunks):
-        def at_block(i, j, at, r=r):
-            return (jnp.where(i == r, j ^ at[0], jnp.where(i < r, at[0], (owners - 1) ^ at[0])), 0, 0)
-        specs += [pl.BlockSpec((1, piece, width), at_block)] * len(terms)
-
-    def own(i, j, at):
-        return (at[1] + i * owners + j, 0, 0)
-
+    blocks, span = len(chunks) * owners, width // 2
+    term = pl.BlockSpec((owners, piece, span), lambda j, at: (0, 0, j))
     return pl.pallas_call(
         functools.partial(close_kernel, [len(terms) for terms in chunks]),
         grid_spec=pltpu.PrefetchScalarGridSpec(
             num_scalar_prefetch=1,
-            grid=(len(chunks), owners),
-            in_specs=[pl.BlockSpec((1, piece, width), own)] + specs,
-            out_specs=pl.BlockSpec((1, piece, width), lambda i, j, at: (i * owners + j, 0, 0)),
-        ),
-        out_shape=jax.ShapeDtypeStruct((len(chunks) * owners, piece, width), bf16),
+            grid=(2,),
+            in_specs=[pl.BlockSpec((blocks, piece, span), lambda j, at: (at[1], 0, j))]
+            + [term] * sum(len(terms) for terms in chunks),
+            out_specs=pl.BlockSpec((blocks, piece, span), lambda j, at: (0, 0, j)),
+        ),
+        out_shape=jax.ShapeDtypeStruct((blocks, piece, width), bf16),
         compiler_params=params(),
         cost_estimate=LIGHT,
         name="close",
     )(
-        jnp.stack([place, first]).astype(jnp.int32),
+        jnp.stack([place, index]).astype(jnp.int32),
         tokens.reshape(-1, piece, width),
         *[term for terms in chunks for term in terms],
     )
@@ -396,12 +447,7 @@
 def scatter_rest(terms, first, count, axis):
     terms, sent = list(terms), None
     for b in range(1, bits_of(axis)):
-        half = terms[-1][0].shape[1] // 2
-        total = sum(
-            t[first - offset:first - offset + count, half:2 * half].astype(f32)
-            for t, offset in terms
-        )
-        sent = total.astype(bf16)
+        sent = fold(terms, first, count)
         terms.append((swap(sent, axis, b), first))
     return terms, sent
 
@@ -454,17 +500,17 @@
         return x.reshape((1, chunks, owners, zs * piece) + x.shape[4:])
 
     at = (place if piece % 16 == 0 else jnp.int32(0)).reshape(1)
-    ordered = arrange(tokens)
+    ordered = arrange_rows(at, arrange(tokens))
     first_event = lax.axis_index("hist") * events
     edges = arrange(jnp.stack([vis_start - first_event, vis_end - first_event], axis=1))
 
     sizes = head_chunks(width // DH)
     summed, sent = [[] for _ in range(chunks)], []
     for c, heads in enumerate(sizes):
-        after = sent[c - 2] if c >= 2 else []
-        keep, send = project(at, ordered, w_qkvu, sum(sizes[:c]), heads, after)
+        after = sent[c - 2] if c >= 2 else [keep] if c else []
+        keep, send = project(ordered, w_qkvu, sum(sizes[:c]), heads, chunks, owners, after)
         if c >= 2:
-            send = tie(send, summed[0][c - 2][-1][0])
+            send = tie(send, summed[0][c - 2][-1][0], *sent[c - 1])
         terms = [(keep, 0), (swap(send, "hist", 0), 0)]
         groups = [(0, chunks)] if c + 1 < len(sizes) else [(r, 1) for r in range(chunks)]
         sent.append([])
@@ -492,7 +538,7 @@
             results.append(
                 [lax.psum_scatter(whole, "head", scatter_dimension=0, tiled=True)[0]]
             )
-    out = close(place, index * (chunks * owners), tokens, results)
+    out = close(place, index, tokens, results)
     return out.reshape(cand // zs, -1)
 
 

time: 231 us -> 243 us (1.052)
  Pallas kernels: 84.8 us -> 108 us
  other arithmetic: 6.28 us -> 1.42 us
  local copies, waits for them, and re-layouts: 21.7 us -> 18.5 us
  starting transfers between devices: 32.4 us -> 29.5 us
    pallas_call x5 -> x14, Pallas kernels: 34.6 us -> 60.4 us  [the longest x5 39.3 us: project(): pl.pallas_call(functools.partial(project_kernel, parts), grid=(heads,), i...]
    pallas_call x2, Pallas kernels: 24.4 us -> 14.5 us  [attend(): pl.pallas_call(functools.partial(attend_kernel, owners), grid_spec=pltpu....]
    convert_element_type x7 -> x0, other arithmetic: 6.06 us -> none  [scatter_rest(): sent = total.astype(bf16)]
    pallas_call x2, Pallas kernels: 0.46 us -> 4.16 us  [gate_rows(): pl.pallas_call(functools.partial(gate_kernel, len(stats)), grid=(1,), in_...]
    pallas_call x2, Pallas kernels: 2.45 us -> 5.48 us  [finish(): pl.pallas_call(functools.partial(finish_kernel, len(sums)), grid_spec=plt...]
    ppermute x27, starting transfers between devices: 15.5 us -> 12.9 us  [swap(): lax.ppermute(x, axis, [(i, i ^ 1 << bit) for i in range(lax.axis_size(axi...]
    unnamed x70 -> x92, local copies, waits for them, and re-layouts: 19.8 us -> 18.1 us
  transfers between devices with their start and end apart: 39 -> 39, of which waited for: 18 -> 19; matrix products, arithmetic and copies ran while one was open for 4% -> 1% of each run, Pallas kernels for 32% -> 33%
where the time goes in v4:
time: 243 us; the launch traced here: 239 us
  Pallas kernels  108 us (44%)
  waiting for transfers between devices  81.5 us (34%)
  starting transfers between devices  29.5 us (12%)
  local copies, waits for them, and re-layouts  18.5 us (8%)
    ppermute x27, waiting for transfers between devices, swap(): lax.ppermute(x, axis, [(i, i ^ 1 << bit) for i in range(lax.axis_size(axi...  45.1 us
    pallas_call x5, Pallas kernels, project(): pl.pallas_call(functools.partial(project_kernel, parts), grid=(heads,), i...  39.3 us
    ppermute x12, waiting for transfers between devices, shifts(): lax.ppermute(blocks[k], axis, [(i, (i + k) % count) for i in range(count)])  36.3 us
    unnamed x92, local copies, waits for them, and re-layouts  18.1 us
    ppermute x12, starting transfers between devices, shifts(): lax.ppermute(blocks[k], axis, [(i, (i + k) % count) for i in range(count)])  16.6 us
    pallas_call x8, Pallas kernels, fold(): pl.pallas_call(fold_kernel, grid=(steps,), in_specs=[pl.BlockSpec(block,...  14.5 us
    pallas_call x2, Pallas kernels, attend(): pl.pallas_call(functools.partial(attend_kernel, owners), grid_spec=pltpu....  14.5 us
    pallas_call x2, Pallas kernels, output(): pl.pallas_call(functools.partial(output_kernel, owners, zs), grid_spec=pl...  13.1 us
  transfers between devices with their start and end apart: 39, of which 19 were waited for; matrix products, arithmetic and copies ran while one was open for 1% of the time, Pallas kernels for 33%

profile of v4, /device:TPU:0, one launch (start us, length us, event | category | flops | bytes accessed | tf_op | source)
XLA Modules:
  0.0 238.9 jit_solution(17688926423316587632)
XLA Ops:
  0.0 6.5 %arrange.1.t_ref = bf16[512,2048]{1,0:T(8,128)(2,1)} custom-call(s32[1]{0:T(128)} %bitcast.at_ref, bf16[4,2,4,16,2048]{4,3,2,1,0:T(8,128)(2,1)} %bitcast.17, bf16[4,2,4,16,2048]{4,3,2,1,0:T(8,128)(2,1)} %bitcast.18, bf16[4,2,4,16,2048]{4,3,2,1,0:T(8,128)(2,1)} %bitcast.19, bf16[4,2,4,16,2048]{4,3,2,1,0:T(8,128)(2,1)} %bitcast.20), custom_call_target="tpu_custom_call" | custom-call | flops 1000 | bytes 1000 | tf_op jit(solution)/shard_map/arrange/pallas_call | solution.py:62
  6.5 5.9 %project.5 = (bf16[2,2,4,64,256]{4,3,2,1,0:T(8,128)(2,1)}, bf16[2,2,4,64,256]{4,3,2,1,0:T(8,128)(2,1)}) custom-call(bf16[512,2048]{1,0:T(8,128)(2,1)} %arrange.1.t_ref, bf16[2048,4,2048]{2,1,0:T(4,128)(2,1)} %w_ref.9), custom_call_target="tpu_custom_call" | custom-call | flops 1000 | bytes 1000 | tf_op jit(solution)/shard_map/project/pallas_call | solution.py:109
  12.4 9.3 %project.6 = (bf16[2,2,4,64,512]{4,3,2,1,0:T(8,128)(2,1)}, bf16[2,2,4,64,512]{4,3,2,1,0:T(8,128)(2,1)}) custom-call(bf16[512,2048]{1,0:T(8,128)(2,1)} %arrange.1.t_ref, bf16[2048,4,2048]{2,1,0:T(4,128)(2,1)} %w_ref.9, bf16[2,2,4,64,256]{4,3,2,1,0:T(8,128)(2,1)} %get-tuple-element.35.refs_0_), custom_call_target="tpu_custom_call" | custom-call | flops 1000 | bytes 1000 | tf_op jit(solution)/shard_map/project/pallas_call | solution.py:109
  22.2 3.0 %collective-permute-done.refs_1_ = bf16[2,2,4,64,256]{4,3,2,1,0:T(8,128)(2,1)S(1)} collective-permute-done((bf16[2,2,4,64,256]{4,3,2,1,0:T(8,128)(2,1)S(1)}, bf16[2,2,4,64,256]{4,3,2,1,0:T(8,128)(2,1)S(1)}, u32[]{:S(2)}, u32[]{:S(2)}) %collective-permute-start) | collective-permute-done | bytes 524320 | tf_op jit(solution)/shard_map/ppermute | solution.py:442
  26.0 1.8 fold.8.refs_0_
  27.8 2.9 %collective-permute-start.1 = (bf16[2,1,4,64,256]{4,3,2,1,0:T(8,128)(2,1)}, bf16[2,1,4,64,256]{4,3,2,1,0:T(8,128)(2,1)S(1)}, u32[]{:S(2)}, u32[]{:S(2)}) collective-permute-start(bf16[2,1,4,64,256]{4,3,2,1,0:T(8,128)(2,1)} %fold.8.refs_0_), channel_id=1, source_target_pairs={{0,2},{1,3},{2,0},{3,1},{4,6},{5,7},{6,4},{7,5},{8,10},{9,11},{10,... | collective-permute-start | bytes 786440 | tf_op jit(solution)/shard_map/ppermute | solution.py:442
  30.6 9.2 %project.7 = (bf16[2,2,4,64,512]{4,3,2,1,0:T(8,128)(2,1)}, bf16[2,2,4,64,512]{4,3,2,1,0:T(8,128)(2,1)}) custom-call(bf16[512,2048]{1,0:T(8,128)(2,1)} %arrange.1.t_ref, bf16[2048,4,2048]{2,1,0:T(4,128)(2,1)} %w_ref.9, bf16[2,1,4,64,256]{4,3,2,1,0:T(8,128)(2,1)} %fold.8.refs_0_), custom_call_target="tpu_custom_call" | custom-call | flops 1000 | bytes 1000 | tf_op jit(solution)/shard_map/project/pallas_call | solution.py:109
  40.8 2.0 fold.9.refs_2_.refs_0_
  43.9 9.2 %project.8 = (bf16[2,2,4,64,512]{4,3,2,1,0:T(8,128)(2,1)}, bf16[2,2,4,64,512]{4,3,2,1,0:T(8,128)(2,1)}) custom-call(bf16[512,2048]{1,0:T(8,128)(2,1)} %arrange.1.t_ref, bf16[2048,4,2048]{2,1,0:T(4,128)(2,1)} %w_ref.9, bf16[2,1,4,64,512]{4,3,2,1,0:T(8,128)(2,1)} %fold.9.refs_2_.refs_0_), custom_call_target="tpu_custom_call" | custom-call | flops 1000 | bytes 1000 | tf_op jit(solution)/shard_map/project/pallas_call | solution.py:109
  54.1 2.0 fold.10.refs_2_.refs_0_
  56.1 1.7 collective-permute-done.3.refs_1_.refs_5_
  59.4 5.9 %project.9 = (bf16[2,2,4,64,256]{4,3,2,1,0:T(8,128)(2,1)}, bf16[2,2,4,64,256]{4,3,2,1,0:T(8,128)(2,1)}) custom-call(bf16[512,2048]{1,0:T(8,128)(2,1)} %arrange.1.t_ref, bf16[2048,4,2048]{2,1,0:T(4,128)(2,1)} %w_ref.9, bf16[2,1,4,64,512]{4,3,2,1,0:T(8,128)(2,1)} %fold.10.refs_2_.refs_0_), custom_call_target="tpu_custom_call" | custom-call | flops 1000 | bytes 1000 | tf_op jit(solution)/shard_map/project/pallas_call | solution.py:109
  66.2 2.0 fold.11.refs_2_
  68.2 4.7 %collective-permute-done.5.refs_1_.refs_8_ = bf16[2,1,4,64,512]{4,3,2,1,0:T(8,128)(2,1)S(1)} collective-permute-done((bf16[2,1,4,64,512]{4,3,2,1,0:T(8,128)(2,1)S(1)}, bf16[2,1,4,64,512]{4,3,2,1,0:T(8,128)(2,1)S(1)}, u32[]{:S(2)}, u32[]{:S(2)}) %collective-permute-start.5) | collective-permute-done | bytes 524320 | tf_op jit(solution)/shard_map/ppermute | solution.py:442
  74.1 1.8 collective-permute-done.8.refs_1_.refs_13_
  76.7 1.6 fold.12
  78.6 9.9 %collective-permute-done.7.refs_11_ = bf16[2,1,4,64,512]{4,3,2,1,0:T(8,128)(2,1)S(1)} collective-permute-done((bf16[2,1,4,64,512]{4,3,2,1,0:T(8,128)(2,1)S(1)}, bf16[2,1,4,64,512]{4,3,2,1,0:T(8,128)(2,1)S(1)}, u32[]{:S(2)}, u32[]{:S(2)}) %collective-permute-start.7) | collective-permute-done | bytes 524320 | tf_op jit(solution)/shard_map/ppermute | solution.py:442
  88.5 2.4 %collective-permute-done.9.refs_14_ = bf16[1,1,4,64,256]{4,3,2,1,0:T(8,128)(2,1)S(1)} collective-permute-done((bf16[1,1,4,64,256]{4,3,2,1,0:T(8,128)(2,1)}, bf16[1,1,4,64,256]{4,3,2,1,0:T(8,128)(2,1)S(1)}, u32[]{:S(2)}, u32[]{:S(2)}) %collective-permute-start.9) | collective-permute-done | bytes 131104 | tf_op jit(solution)/shard_map/ppermute | solution.py:442
  91.6 3.4 %activate.2 = (bf16[64,2048]{1,0:T(8,128)(2,1)}, bf16[3,64,2048]{2,1,0:T(8,128)(2,1)}) custom-call(bf16[2,2,4,64,256]{4,3,2,1,0:T(8,128)(2,1)} %get-tuple-element.35.refs_0_, bf16[2,2,4,64,256]{4,3,2,1,0:T(8,128)(2,1)} %copy-done.6, bf16[2,1,4,64,256]{4,3,2,1,0:T(8,128)(2,1)} %copy-done.9, bf16[2,2,4,64,512]{4,3,2,1,0:T(8,128)(2,1)} %get-tuple-element.37.refs_0_.refs_3_, ...), custom_call_target="tpu_custom_call" | custom-call | flops 1000 | bytes 1000 | tf_op jit(solution)/shard_map/activate/pallas_call | solution.py:193
  95.3 1.6 fold.14
  96.9 1.7 collective-permute-start.24
  98.6 7.3 %collective-permute-done.24.refs_14_ = bf16[1,1,4,64,256]{4,3,2,1,0:T(8,128)(2,1)S(1)} collective-permute-done((bf16[1,1,4,64,256]{4,3,2,1,0:T(8,128)(2,1)}, bf16[1,1,4,64,256]{4,3,2,1,0:T(8,128)(2,1)S(1)}, u32[]{:S(2)}, u32[]{:S(2)}) %collective-permute-start.24) | collective-permute-done | bytes 131104 | tf_op jit(solution)/shard_map/ppermute | solution.py:442
  106.6 3.4 %activate.3 = (bf16[64,2048]{1,0:T(8,128)(2,1)}, bf16[3,64,2048]{2,1,0:T(8,128)(2,1)}) custom-call(bf16[2,2,4,64,256]{4,3,2,1,0:T(8,128)(2,1)} %get-tuple-element.35.refs_0_, bf16[2,2,4,64,256]{4,3,2,1,0:T(8,128)(2,1)} %copy-done.6, bf16[2,1,4,64,256]{4,3,2,1,0:T(8,128)(2,1)} %copy-done.9, bf16[2,2,4,64,512]{4,3,2,1,0:T(8,128)(2,1)} %get-tuple-element.37.refs_0_.refs_3_, ...), custom_call_target="tpu_custom_call" | custom-call | flops 1000 | bytes 1000 | tf_op jit(solution)/shard_map/activate/pallas_call | solution.py:193
  112.1 5.1 %collective-permute-done.25.refs_1_ = bf16[64,2048]{1,0:T(8,128)(2,1)S(1)} collective-permute-done((bf16[64,2048]{1,0:T(8,128)(2,1)}, bf16[64,2048]{1,0:T(8,128)(2,1)S(1)}, u32[]{:S(2)}, u32[]{:S(2)}) %collective-permute-start.25) | collective-permute-done | bytes 262176 | tf_op jit(solution)/shard_map/ppermute | solution.py:442
  118.7 7.3 %attend.2 = (bf16[2,64,2048]{2,1,0:T(8,128)(2,1)}, bf16[2,64,2048]{2,1,0:T(8,128)(2,1)}) custom-call(s32[1]{0:T(128)} %bitcast.at_ref, bf16[64,2048]{1,0:T(8,128)(2,1)} %get-tuple-element.45.refs_0_.q_ref, bf16[64,2048]{1,0:T(8,128)(2,1)} %copy-done.16, bf16[64,2048]{1,0:T(8,128)(2,1)} %copy-done.18, bf16[64,2048]{1,0:T(8,128)(2,1)} %copy-done.28, ...), custom_call_target="tpu_custom_call" | custom-call | flops 1000 | bytes 1000 | tf_op jit(solution)/shard_map/attend/pallas_call | solution.py:253
  127.9 7.2 %attend.3 = (bf16[2,64,2048]{2,1,0:T(8,128)(2,1)}, bf16[2,64,2048]{2,1,0:T(8,128)(2,1)}) custom-call(s32[1]{0:T(128)} %bitcast.at_ref, bf16[64,2048]{1,0:T(8,128)(2,1)} %get-tuple-element.55.refs_0_.q_ref, bf16[64,2048]{1,0:T(8,128)(2,1)} %copy-done.22, bf16[64,2048]{1,0:T(8,128)(2,1)} %copy-done.29, bf16[64,2048]{1,0:T(8,128)(2,1)} %copy-done.32, ...), custom_call_target="tpu_custom_call" | custom-call | flops 1000 | bytes 1000 | tf_op jit(solution)/shard_map/attend/pallas_call | solution.py:253
  136.0 1.8 fold.13
  138.9 1.8 fold.15
  140.7 1.7 collective-permute-start.29
  142.4 4.7 %collective-permute-done.14.refs_2_ = bf16[1,1,64,2048]{3,2,1,0:T(8,128)(2,1)S(1)} collective-permute-done((bf16[1,1,64,2048]{3,2,1,0:T(8,128)(2,1)}, bf16[1,1,64,2048]{3,2,1,0:T(8,128)(2,1)S(1)}, u32[]{:S(2)}, u32[]{:S(2)}) %collective-permute-start.14) | collective-permute-done | bytes 262176 | tf_op jit(solution)/shard_map/ppermute | solution.py:442
  147.8 2.7 %finish.2 = (f32[64,2048]{1,0:T(8,128)}, f32[64,128]{1,0:T(8,128)}) custom-call(s32[1]{0:T(128)} %bitcast.at_ref, s32[4,2,4,16,2]{4,3,2,1,0:T(8,128)} %pad_add_fusion.refs_4_.refs_5_.refs_6_.refs_7_.edge_ref, bf16[64,2048]{1,0:T(8,128)(2,1)} %get-tuple-element.45.refs_0_.q_ref, bf16[3,64,2048]{2,1,0:T(8,128)(2,1)} %get-tuple-element.46.rest_ref, ...), custom_call_target="tpu_custom_call" | custom-call | flops 1000 | bytes 1000 | tf_op jit(solution)/shard_map/finish/pallas_call | solution.py:297
  150.5 3.6 %collective-permute-start.17 = (f32[64,128]{1,0:T(8,128)}, f32[64,128]{1,0:T(8,128)S(1)}, u32[]{:S(2)}, u32[]{:S(2)}) collective-permute-start(f32[64,128]{1,0:T(8,128)} %get-tuple-element.50.refs_0_), channel_id=1, source_target_pairs={{0,12},{4,0},{8,4},{12,8},{1,13},{5,1},{9,5},{13,9},{2,14},{6,2},{... | collective-permute-start | bytes 98312 | tf_op jit(solution)/shard_map/ppermute | solution.py:465
  156.0 3.1 %collective-permute-done.16.refs_2_ = f32[64,128]{1,0:T(8,128)S(1)} collective-permute-done((f32[64,128]{1,0:T(8,128)}, f32[64,128]{1,0:T(8,128)S(1)}, u32[]{:S(2)}, u32[]{:S(2)}) %collective-permute-start.16) | collective-permute-done | bytes 32800 | tf_op jit(solution)/shard_map/ppermute | solution.py:465
  160.7 2.1 gate.2
  164.0 2.8 %finish.3 = (f32[64,2048]{1,0:T(8,128)}, f32[64,128]{1,0:T(8,128)}) custom-call(s32[1]{0:T(128)} %bitcast.at_ref, s32[4,2,4,16,2]{4,3,2,1,0:T(8,128)} %pad_add_fusion.refs_4_.refs_5_.refs_6_.refs_7_.edge_ref, bf16[64,2048]{1,0:T(8,128)(2,1)} %get-tuple-element.55.refs_0_.q_ref, bf16[3,64,2048]{2,1,0:T(8,128)(2,1)} %get-tuple-element.56.rest_ref, ...), custom_call_target="tpu_custom_call" | custom-call | flops 1000 | bytes 1000 | tf_op jit(solution)/shard_map/finish/pallas_call | solution.py:297
  167.9 2.0 collective-permute-start.30
  174.4 2.1 gate.3
  178.6 4.5 %collective-permute-done.33 = bf16[64,2048]{1,0:T(8,128)(2,1)S(1)} collective-permute-done((bf16[64,2048]{1,0:T(8,128)(2,1)}, bf16[64,2048]{1,0:T(8,128)(2,1)S(1)}, u32[]{:S(2)}, u32[]{:S(2)}) %collective-permute-start.33) | collective-permute-done | bytes 262176 | tf_op jit(solution)/shard_map/ppermute | solution.py:442
  183.9 6.6 %output.2 = (bf16[4,16,2048]{2,1,0:T(8,128)(2,1)}, bf16[4,16,2048]{2,1,0:T(8,128)(2,1)}, bf16[4,16,2048]{2,1,0:T(8,128)(2,1)}, bf16[4,16,2048]{2,1,0:T(8,128)(2,1)}) custom-call(s32[1]{0:T(128)} %bitcast.1.index_ref, bf16[4,16,2048]{2,1,0:T(8,128)(2,1)} %bitcast.30, bf16[4,16,2048]{2,1,0:T(8,128)(2,1)} %bitcast.32, bf16[4,16,2048]{2,1,0:T(8,128)(2,1)} %bitcast.36, ...), custom_call_target="tpu_custom_call" | custom-call | flops 1000 | bytes 1000 | tf_op jit(solution)/shard_map/output/pallas_call | solution.py:377
  190.8 1.8 collective-permute-start.22
  192.6 1.8 collective-permute-start.23
  195.2 6.6 %output.3 = (bf16[4,16,2048]{2,1,0:T(8,128)(2,1)}, bf16[4,16,2048]{2,1,0:T(8,128)(2,1)}, bf16[4,16,2048]{2,1,0:T(8,128)(2,1)}, bf16[4,16,2048]{2,1,0:T(8,128)(2,1)}) custom-call(s32[1]{0:T(128)} %bitcast.1.index_ref, bf16[4,16,2048]{2,1,0:T(8,128)(2,1)} %bitcast.31, bf16[4,16,2048]{2,1,0:T(8,128)(2,1)} %bitcast.33, bf16[4,16,2048]{2,1,0:T(8,128)(2,1)} %bitcast.34, ...), custom_call_target="tpu_custom_call" | custom-call | flops 1000 | bytes 1000 | tf_op jit(solution)/shard_map/output/pallas_call | solution.py:377
  202.3 1.5 collective-permute-start.37
  203.8 2.9 %collective-permute-start.38 = (bf16[4,16,2048]{2,1,0:T(8,128)(2,1)}, bf16[4,16,2048]{2,1,0:T(8,128)(2,1)S(1)}, u32[]{:S(2)}, u32[]{:S(2)}) collective-permute-start(bf16[4,16,2048]{2,1,0:T(8,128)(2,1)} %get-tuple-element.64), channel_id=1, source_target_pairs={{0,12},{4,0},{8,4},{12,8},{1,13},{5,1},{9,5},{13,9},{2,14},{6,2},{... | collective-permute-start | bytes 786440 | tf_op jit(solution)/shard_map/ppermute | solution.py:465
  207.3 5.3 %collective-permute-done.22.refs_2_ = bf16[4,16,2048]{2,1,0:T(8,128)(2,1)S(1)} collective-permute-done((bf16[4,16,2048]{2,1,0:T(8,128)(2,1)}, bf16[4,16,2048]{2,1,0:T(8,128)(2,1)S(1)}, u32[]{:S(2)}, u32[]{:S(2)}) %collective-permute-start.22) | collective-permute-done | bytes 262176 | tf_op jit(solution)/shard_map/ppermute | solution.py:465
  212.6 6.1 %collective-permute-done.36.refs_5_ = bf16[4,16,2048]{2,1,0:T(8,128)(2,1)S(1)} collective-permute-done((bf16[4,16,2048]{2,1,0:T(8,128)(2,1)}, bf16[4,16,2048]{2,1,0:T(8,128)(2,1)S(1)}, u32[]{:S(2)}, u32[]{:S(2)}) %collective-permute-start.36) | collective-permute-done | bytes 262176 | tf_op jit(solution)/shard_map/ppermute | solution.py:465
  218.7 16.1 %collective-permute-done.37.refs_6_ = bf16[4,16,2048]{2,1,0:T(8,128)(2,1)S(1)} collective-permute-done((bf16[4,16,2048]{2,1,0:T(8,128)(2,1)}, bf16[4,16,2048]{2,1,0:T(8,128)(2,1)S(1)}, u32[]{:S(2)}, u32[]{:S(2)}) %collective-permute-start.37) | collective-permute-done | bytes 262176 | tf_op jit(solution)/shard_map/ppermute | solution.py:465
  235.6 3.3 %close.1 = bf16[8,16,2048]{2,1,0:T(8,128)(2,1)} custom-call(s32[2]{0:T(128)} %pad_add_fusion.1.at_ref, bf16[32,16,2048]{2,1,0:T(8,128)(2,1)} %bitcast.21, bf16[4,16,2048]{2,1,0:T(8,128)(2,1)} %get-tuple-element.51.refs_0_, bf16[4,16,2048]{2,1,0:T(8,128)(2,1)} %copy-done.19, bf16[4,16,2048]{2,1,0:T(8,128)(2,1)} %copy-done.20, ...), custom_call_target="tpu_custom_call" | custom-call | flops 1000 | bytes 1000 | tf_op jit(solution)/shard_map/close/pallas_call | solution.py:410
  (155 shorter events, 35.3 us)
Async XLA Ops:
  12.4 9.7 %copy-start.45 = (bf16[2,2,4,64,256]{4,3,2,1,0:T(8,128)(2,1)S(1)}, bf16[2,2,4,64,256]{4,3,2,1,0:T(8,128)(2,1)}, u32[]{:S(2)}) copy-start(bf16[2,2,4,64,256]{4,3,2,1,0:T(8,128)(2,1)} %get-tuple-element.36) | copy-start | bytes 1572868
  21.7 18.1 %collective-permute-start.2 = (bf16[2,2,4,64,512]{4,3,2,1,0:T(8,128)(2,1)}, bf16[2,2,4,64,512]{4,3,2,1,0:T(8,128)(2,1)S(1)}, u32[]{:S(2)}, u32[]{:S(2)}) collective-permute-start(bf16[2,2,4,64,512]{4,3,2,1,0:T(8,128)(2,1)} %get-tuple-element.38), channel_id=1, source_target_pairs={{0,1},{1,0},{2,3},{3,2},{4,5},{5,4},{6,7},{7,6},{8,9},{9,8},{10,11... | collective-permute-start | bytes 3145736 | tf_op jit(solution)/shard_map/ppermute | solution.py:442
  22.1 3.0 %collective-permute-start = (bf16[2,2,4,64,256]{4,3,2,1,0:T(8,128)(2,1)S(1)}, bf16[2,2,4,64,256]{4,3,2,1,0:T(8,128)(2,1)S(1)}, u32[]{:S(2)}, u32[]{:S(2)}) collective-permute-start(bf16[2,2,4,64,256]{4,3,2,1,0:T(8,128)(2,1)S(1)} %copy-done.45), channel_id=1, source_target_pairs={{0,1},{1,0},{2,3},{3,2},{4,5},{5,4},{6,7},{7,6},{8,9},{9,8},{10,11... | collective-permute-start | bytes 1572872 | tf_op jit(solution)/shard_map/ppermute | solution.py:442
  27.8 15.0 %collective-permute-start.1 = (bf16[2,1,4,64,256]{4,3,2,1,0:T(8,128)(2,1)}, bf16[2,1,4,64,256]{4,3,2,1,0:T(8,128)(2,1)S(1)}, u32[]{:S(2)}, u32[]{:S(2)}) collective-permute-start(bf16[2,1,4,64,256]{4,3,2,1,0:T(8,128)(2,1)} %fold.8.refs_0_), channel_id=1, source_target_pairs={{0,2},{1,3},{2,0},{3,1},{4,6},{5,7},{6,4},{7,5},{8,10},{9,11},{10,... | collective-permute-start | bytes 786440 | tf_op jit(solution)/shard_map/ppermute | solution.py:442
  43.5 9.6 %collective-permute-start.4 = (bf16[2,2,4,64,512]{4,3,2,1,0:T(8,128)(2,1)}, bf16[2,2,4,64,512]{4,3,2,1,0:T(8,128)(2,1)S(1)}, u32[]{:S(2)}, u32[]{:S(2)}) collective-permute-start(bf16[2,2,4,64,512]{4,3,2,1,0:T(8,128)(2,1)} %tie.3), channel_id=1, source_target_pairs={{0,1},{1,0},{2,3},{3,2},{4,5},{5,4},{6,7},{7,6},{8,9},{9,8},{10,11... | collective-permute-start | bytes 3145736 | tf_op jit(solution)/shard_map/ppermute | solution.py:442
  43.9 13.9 %collective-permute-start.3 = (bf16[2,1,4,64,512]{4,3,2,1,0:T(8,128)(2,1)S(1)}, bf16[2,1,4,64,512]{4,3,2,1,0:T(8,128)(2,1)S(1)}, u32[]{:S(2)}, u32[]{:S(2)}) collective-permute-start(bf16[2,1,4,64,512]{4,3,2,1,0:T(8,128)(2,1)S(1)} %copy-done.5), channel_id=1, source_target_pairs={{0,2},{1,3},{2,0},{3,1},{4,6},{5,7},{6,4},{7,5},{8,10},{9,11},{10,... | collective-permute-start | bytes 1572872 | tf_op jit(solution)/shard_map/ppermute | solution.py:442
  58.6 6.6 %collective-permute-start.6 = (bf16[2,2,4,64,512]{4,3,2,1,0:T(8,128)(2,1)}, bf16[2,2,4,64,512]{4,3,2,1,0:T(8,128)(2,1)S(1)}, u32[]{:S(2)}, u32[]{:S(2)}) collective-permute-start(bf16[2,2,4,64,512]{4,3,2,1,0:T(8,128)(2,1)} %tie.4), channel_id=1, source_target_pairs={{0,1},{1,0},{2,3},{3,2},{4,5},{5,4},{6,7},{7,6},{8,9},{9,8},{10,11... | collective-permute-start | bytes 3145736 | tf_op jit(solution)/shard_map/ppermute | solution.py:442
  58.6 14.3 %collective-permute-start.5 = (bf16[2,1,4,64,512]{4,3,2,1,0:T(8,128)(2,1)S(1)}, bf16[2,1,4,64,512]{4,3,2,1,0:T(8,128)(2,1)S(1)}, u32[]{:S(2)}, u32[]{:S(2)}) collective-permute-start(bf16[2,1,4,64,512]{4,3,2,1,0:T(8,128)(2,1)S(1)} %copy-done.4), channel_id=1, source_target_pairs={{0,2},{1,3},{2,0},{3,1},{4,6},{5,7},{6,4},{7,5},{8,10},{9,11},{10,... | collective-permute-start | bytes 1572872 | tf_op jit(solution)/shard_map/ppermute | solution.py:442
  73.8 2.1 collective-permute-start.8
  73.8 14.7 %collective-permute-start.7 = (bf16[2,1,4,64,512]{4,3,2,1,0:T(8,128)(2,1)S(1)}, bf16[2,1,4,64,512]{4,3,2,1,0:T(8,128)(2,1)S(1)}, u32[]{:S(2)}, u32[]{:S(2)}) collective-permute-start(bf16[2,1,4,64,512]{4,3,2,1,0:T(8,128)(2,1)S(1)} %copy-done.11), channel_id=1, source_target_pairs={{0,2},{1,3},{2,0},{3,1},{4,6},{5,7},{6,4},{7,5},{8,10},{9,11},{10,... | collective-permute-start | bytes 1572872 | tf_op jit(solution)/shard_map/ppermute | solution.py:442
  78.3 12.6 %collective-permute-start.9 = (bf16[1,1,4,64,256]{4,3,2,1,0:T(8,128)(2,1)}, bf16[1,1,4,64,256]{4,3,2,1,0:T(8,128)(2,1)S(1)}, u32[]{:S(2)}, u32[]{:S(2)}) collective-permute-start(bf16[1,1,4,64,256]{4,3,2,1,0:T(8,128)(2,1)} %fold.12), channel_id=1, source_target_pairs={{0,2},{1,3},{2,0},{3,1},{4,6},{5,7},{6,4},{7,5},{8,10},{9,11},{10,... | collective-permute-start | bytes 393224 | tf_op jit(solution)/shard_map/ppermute | solution.py:442
  95.0 15.4 %collective-permute-start.10 = (bf16[64,2048]{1,0:T(8,128)(2,1)}, bf16[64,2048]{1,0:T(8,128)(2,1)S(1)}, u32[]{:S(2)}, u32[]{:S(2)}) collective-permute-start(bf16[64,2048]{1,0:T(8,128)(2,1)} %get-tuple-element.45.refs_0_.q_ref), channel_id=1, source_target_pairs={{0,2},{1,3},{2,0},{3,1},{4,6},{5,7},{6,4},{7,5},{8,10},{9,11},{10,... | collective-permute-start | bytes 786440 | tf_op jit(solution)/shard_map/ppermute | solution.py:442
  96.9 9.0 %collective-permute-start.24 = (bf16[1,1,4,64,256]{4,3,2,1,0:T(8,128)(2,1)}, bf16[1,1,4,64,256]{4,3,2,1,0:T(8,128)(2,1)S(1)}, u32[]{:S(2)}, u32[]{:S(2)}) collective-permute-start(bf16[1,1,4,64,256]{4,3,2,1,0:T(8,128)(2,1)} %fold.14), channel_id=1, source_target_pairs={{0,2},{1,3},{2,0},{3,1},{4,6},{5,7},{6,4},{7,5},{8,10},{9,11},{10,... | collective-permute-start | bytes 393224 | tf_op jit(solution)/shard_map/ppermute | solution.py:442
  98.6 11.8 %copy-start.43 = (s32[512]{0:T(512)S(1)}, s32[512]{0:T(512)}, u32[]{:S(2)}) copy-start(s32[512]{0:T(512)} %param.13) | copy-start | bytes 6148
  98.6 11.8 %copy-start.44 = (s32[512]{0:T(512)S(1)}, s32[512]{0:T(512)}, u32[]{:S(2)}) copy-start(s32[512]{0:T(512)} %param.12) | copy-start | bytes 6148
  98.6 18.7 %collective-permute-start.11 = (bf16[64,2048]{1,0:T(8,128)(2,1)}, bf16[64,2048]{1,0:T(8,128)(2,1)S(1)}, u32[]{:S(2)}, u32[]{:S(2)}) collective-permute-start(bf16[64,2048]{1,0:T(8,128)(2,1)} %get-tuple-element.45.refs_0_.q_ref), channel_id=1, source_target_pairs={{0,1},{1,0},{2,3},{3,2},{4,5},{5,4},{6,7},{7,6},{8,9},{9,8},{10,11... | collective-permute-start | bytes 786440 | tf_op jit(solution)/shard_map/ppermute | solution.py:442
  110.0 7.3 %collective-permute-start.25 = (bf16[64,2048]{1,0:T(8,128)(2,1)}, bf16[64,2048]{1,0:T(8,128)(2,1)S(1)}, u32[]{:S(2)}, u32[]{:S(2)}) collective-permute-start(bf16[64,2048]{1,0:T(8,128)(2,1)} %get-tuple-element.55.refs_0_.q_ref), channel_id=1, source_target_pairs={{0,2},{1,3},{2,0},{3,1},{4,6},{5,7},{6,4},{7,5},{8,10},{9,11},{10,... | collective-permute-start | bytes 786440 | tf_op jit(solution)/shard_map/ppermute | solution.py:442
  110.3 6.9 %collective-permute-start.12 = (bf16[64,2048]{1,0:T(8,128)(2,1)S(1)}, bf16[64,2048]{1,0:T(8,128)(2,1)S(1)}, u32[]{:S(2)}, u32[]{:S(2)}) collective-permute-start(bf16[64,2048]{1,0:T(8,128)(2,1)S(1)} %collective-permute-done.10.refs_1_), channel_id=1, source_target_pairs={{0,1},{1,0},{2,3},{3,2},{4,5},{5,4},{6,7},{7,6},{8,9},{9,8},{10,11... | collective-permute-start | bytes 786440 | tf_op jit(solution)/shard_map/ppermute | solution.py:442
  111.6 14.9 %collective-permute-start.26 = (bf16[64,2048]{1,0:T(8,128)(2,1)}, bf16[64,2048]{1,0:T(8,128)(2,1)S(1)}, u32[]{:S(2)}, u32[]{:S(2)}) collective-permute-start(bf16[64,2048]{1,0:T(8,128)(2,1)} %get-tuple-element.55.refs_0_.q_ref), channel_id=1, source_target_pairs={{0,1},{1,0},{2,3},{3,2},{4,5},{5,4},{6,7},{7,6},{8,9},{9,8},{10,11... | collective-permute-start | bytes 786440 | tf_op jit(solution)/shard_map/ppermute | solution.py:442
  117.2 9.3 %copy-start.22 = (bf16[64,2048]{1,0:T(8,128)(2,1)}, bf16[64,2048]{1,0:T(8,128)(2,1)S(1)}, u32[]{:S(2)}) copy-start(bf16[64,2048]{1,0:T(8,128)(2,1)S(1)} %collective-permute-done.25.refs_1_) | copy-start | bytes 786436
  117.3 9.3 %collective-permute-start.27 = (bf16[64,2048]{1,0:T(8,128)(2,1)S(1)}, bf16[64,2048]{1,0:T(8,128)(2,1)S(1)}, u32[]{:S(2)}, u32[]{:S(2)}) collective-permute-start(bf16[64,2048]{1,0:T(8,128)(2,1)S(1)} %collective-permute-done.25.refs_1_), channel_id=1, source_target_pairs={{0,1},{1,0},{2,3},{3,2},{4,5},{5,4},{6,7},{7,6},{8,9},{9,8},{10,11... | collective-permute-start | bytes 786440 | tf_op jit(solution)/shard_map/ppermute | solution.py:442
  126.0 9.2 %collective-permute-start.13 = (bf16[2,64,2048]{2,1,0:T(8,128)(2,1)}, bf16[2,64,2048]{2,1,0:T(8,128)(2,1)S(1)}, u32[]{:S(2)}, u32[]{:S(2)}) collective-permute-start(bf16[2,64,2048]{2,1,0:T(8,128)(2,1)} %get-tuple-element.48), channel_id=1, source_target_pairs={{0,1},{1,0},{2,3},{3,2},{4,5},{5,4},{6,7},{7,6},{8,9},{9,8},{10,11... | collective-permute-start | bytes 1572872 | tf_op jit(solution)/shard_map/ppermute | solution.py:442
  135.1 3.1 %collective-permute-start.28 = (bf16[2,64,2048]{2,1,0:T(8,128)(2,1)}, bf16[2,64,2048]{2,1,0:T(8,128)(2,1)S(1)}, u32[]{:S(2)}, u32[]{:S(2)}) collective-permute-start(bf16[2,64,2048]{2,1,0:T(8,128)(2,1)} %get-tuple-element.58), channel_id=1, source_target_pairs={{0,1},{1,0},{2,3},{3,2},{4,5},{5,4},{6,7},{7,6},{8,9},{9,8},{10,11... | collective-permute-start | bytes 1572872 | tf_op jit(solution)/shard_map/ppermute | solution.py:442
  137.8 9.3 %collective-permute-start.14 = (bf16[1,1,64,2048]{3,2,1,0:T(8,128)(2,1)}, bf16[1,1,64,2048]{3,2,1,0:T(8,128)(2,1)S(1)}, u32[]{:S(2)}, u32[]{:S(2)}) collective-permute-start(bf16[1,1,64,2048]{3,2,1,0:T(8,128)(2,1)} %fold.13), channel_id=1, source_target_pairs={{0,2},{1,3},{2,0},{3,1},{4,6},{5,7},{6,4},{7,5},{8,10},{9,11},{10,... | collective-permute-start | bytes 786440 | tf_op jit(solution)/shard_map/ppermute | solution.py:442
  140.7 22.6 %collective-permute-start.29 = (bf16[1,1,64,2048]{3,2,1,0:T(8,128)(2,1)}, bf16[1,1,64,2048]{3,2,1,0:T(8,128)(2,1)S(1)}, u32[]{:S(2)}, u32[]{:S(2)}) collective-permute-start(bf16[1,1,64,2048]{3,2,1,0:T(8,128)(2,1)} %fold.15), channel_id=1, source_target_pairs={{0,2},{1,3},{2,0},{3,1},{4,6},{5,7},{6,4},{7,5},{8,10},{9,11},{10,... | collective-permute-start | bytes 786440 | tf_op jit(solution)/shard_map/ppermute | solution.py:442
  150.5 5.5 %collective-permute-start.17 = (f32[64,128]{1,0:T(8,128)}, f32[64,128]{1,0:T(8,128)S(1)}, u32[]{:S(2)}, u32[]{:S(2)}) collective-permute-start(f32[64,128]{1,0:T(8,128)} %get-tuple-element.50.refs_0_), channel_id=1, source_target_pairs={{0,12},{4,0},{8,4},{12,8},{1,13},{5,1},{9,5},{13,9},{2,14},{6,2},{... | collective-permute-start | bytes 98312 | tf_op jit(solution)/shard_map/ppermute | solution.py:465
  154.1 5.0 %collective-permute-start.16 = (f32[64,128]{1,0:T(8,128)}, f32[64,128]{1,0:T(8,128)S(1)}, u32[]{:S(2)}, u32[]{:S(2)}) collective-permute-start(f32[64,128]{1,0:T(8,128)} %get-tuple-element.50.refs_0_), channel_id=1, source_target_pairs={{0,8},{4,12},{8,0},{12,4},{1,9},{5,13},{9,1},{13,5},{2,10},{6,14},... | collective-permute-start | bytes 98312 | tf_op jit(solution)/shard_map/ppermute | solution.py:465
  154.1 5.9 %collective-permute-start.15 = (f32[64,128]{1,0:T(8,128)}, f32[64,128]{1,0:T(8,128)S(1)}, u32[]{:S(2)}, u32[]{:S(2)}) collective-permute-start(f32[64,128]{1,0:T(8,128)} %get-tuple-element.50.refs_0_), channel_id=1, source_target_pairs={{0,4},{4,8},{8,12},{12,0},{1,5},{5,9},{9,13},{13,1},{2,6},{6,10},{... | collective-permute-start | bytes 98312 | tf_op jit(solution)/shard_map/ppermute | solution.py:465
  162.7 15.2 %collective-permute-start.18 = (bf16[64,2048]{1,0:T(8,128)(2,1)}, bf16[64,2048]{1,0:T(8,128)(2,1)S(1)}, u32[]{:S(2)}, u32[]{:S(2)}) collective-permute-start(bf16[64,2048]{1,0:T(8,128)(2,1)} %gate.2), channel_id=1, source_target_pairs={{0,2},{1,3},{2,0},{3,1},{4,6},{5,7},{6,4},{7,5},{8,10},{9,11},{10,... | collective-permute-start | bytes 786440 | tf_op jit(solution)/shard_map/ppermute | solution.py:442
  164.0 14.0 %copy-start.14 = (bf16[64,2048]{1,0:T(8,128)(2,1)S(1)}, bf16[64,2048]{1,0:T(8,128)(2,1)}, u32[]{:S(2)}) copy-start(bf16[64,2048]{1,0:T(8,128)(2,1)} %gate.2) | copy-start | bytes 786436
  166.8 4.3 %collective-permute-start.32 = (f32[64,128]{1,0:T(8,128)}, f32[64,128]{1,0:T(8,128)S(1)}, u32[]{:S(2)}, u32[]{:S(2)}) collective-permute-start(f32[64,128]{1,0:T(8,128)} %get-tuple-element.60.refs_0_), channel_id=1, source_target_pairs={{0,12},{4,0},{8,4},{12,8},{1,13},{5,1},{9,5},{13,9},{2,14},{6,2},{... | collective-permute-start | bytes 98312 | tf_op jit(solution)/shard_map/ppermute | solution.py:465
  167.3 5.0 %collective-permute-start.31 = (f32[64,128]{1,0:T(8,128)}, f32[64,128]{1,0:T(8,128)S(1)}, u32[]{:S(2)}, u32[]{:S(2)}) collective-permute-start(f32[64,128]{1,0:T(8,128)} %get-tuple-element.60.refs_0_), channel_id=1, source_target_pairs={{0,8},{4,12},{8,0},{12,4},{1,9},{5,13},{9,1},{13,5},{2,10},{6,14},... | collective-permute-start | bytes 98312 | tf_op jit(solution)/shard_map/ppermute | solution.py:465
  167.9 5.9 %collective-permute-start.30 = (f32[64,128]{1,0:T(8,128)}, f32[64,128]{1,0:T(8,128)S(1)}, u32[]{:S(2)}, u32[]{:S(2)}) collective-permute-start(f32[64,128]{1,0:T(8,128)} %get-tuple-element.60.refs_0_), channel_id=1, source_target_pairs={{0,4},{4,8},{8,12},{12,0},{1,5},{5,9},{9,13},{13,1},{2,6},{6,10},{... | collective-permute-start | bytes 98312 | tf_op jit(solution)/shard_map/ppermute | solution.py:465
  176.5 6.6 %collective-permute-start.33 = (bf16[64,2048]{1,0:T(8,128)(2,1)}, bf16[64,2048]{1,0:T(8,128)(2,1)S(1)}, u32[]{:S(2)}, u32[]{:S(2)}) collective-permute-start(bf16[64,2048]{1,0:T(8,128)(2,1)} %gate.3), channel_id=1, source_target_pairs={{0,2},{1,3},{2,0},{3,1},{4,6},{5,7},{6,4},{7,5},{8,10},{9,11},{10,... | collective-permute-start | bytes 786440 | tf_op jit(solution)/shard_map/ppermute | solution.py:442
  178.0 5.1 %collective-permute-start.19 = (bf16[64,2048]{1,0:T(8,128)(2,1)S(1)}, bf16[64,2048]{1,0:T(8,128)(2,1)S(1)}, u32[]{:S(2)}, u32[]{:S(2)}) collective-permute-start(bf16[64,2048]{1,0:T(8,128)(2,1)S(1)} %copy-done.14), channel_id=1, source_target_pairs={{0,1},{1,0},{2,3},{3,2},{4,5},{5,4},{6,7},{7,6},{8,9},{9,8},{10,11... | collective-permute-start | bytes 786440 | tf_op jit(solution)/shard_map/ppermute | solution.py:442
  178.0 5.1 %collective-permute-start.20 = (bf16[64,2048]{1,0:T(8,128)(2,1)S(1)}, bf16[64,2048]{1,0:T(8,128)(2,1)S(1)}, u32[]{:S(2)}, u32[]{:S(2)}) collective-permute-start(bf16[64,2048]{1,0:T(8,128)(2,1)S(1)} %collective-permute-done.18), channel_id=1, source_target_pairs={{0,1},{1,0},{2,3},{3,2},{4,5},{5,4},{6,7},{7,6},{8,9},{9,8},{10,11... | collective-permute-start | bytes 786440 | tf_op jit(solution)/shard_map/ppermute | solution.py:442
  178.5 15.9 %collective-permute-start.34 = (bf16[64,2048]{1,0:T(8,128)(2,1)}, bf16[64,2048]{1,0:T(8,128)(2,1)S(1)}, u32[]{:S(2)}, u32[]{:S(2)}) collective-permute-start(bf16[64,2048]{1,0:T(8,128)(2,1)} %gate.3), channel_id=1, source_target_pairs={{0,1},{1,0},{2,3},{3,2},{4,5},{5,4},{6,7},{7,6},{8,9},{9,8},{10,11... | collective-permute-start | bytes 786440 | tf_op jit(solution)/shard_map/ppermute | solution.py:442
  183.1 11.3 %collective-permute-start.35 = (bf16[64,2048]{1,0:T(8,128)(2,1)S(1)}, bf16[64,2048]{1,0:T(8,128)(2,1)S(1)}, u32[]{:S(2)}, u32[]{:S(2)}) collective-permute-start(bf16[64,2048]{1,0:T(8,128)(2,1)S(1)} %collective-permute-done.33), channel_id=1, source_target_pairs={{0,1},{1,0},{2,3},{3,2},{4,5},{5,4},{6,7},{7,6},{8,9},{9,8},{10,11... | collective-permute-start | bytes 786440 | tf_op jit(solution)/shard_map/ppermute | solution.py:442
  190.5 13.3 %collective-permute-start.21 = (bf16[4,16,2048]{2,1,0:T(8,128)(2,1)}, bf16[4,16,2048]{2,1,0:T(8,128)(2,1)S(1)}, u32[]{:S(2)}, u32[]{:S(2)}) collective-permute-start(bf16[4,16,2048]{2,1,0:T(8,128)(2,1)} %get-tuple-element.52), channel_id=1, source_target_pairs={{0,4},{4,8},{8,12},{12,0},{1,5},{5,9},{9,13},{13,1},{2,6},{6,10},{... | collective-permute-start | bytes 786440 | tf_op jit(solution)/shard_map/ppermute | solution.py:465
  190.8 21.8 %collective-permute-start.22 = (bf16[4,16,2048]{2,1,0:T(8,128)(2,1)}, bf16[4,16,2048]{2,1,0:T(8,128)(2,1)S(1)}, u32[]{:S(2)}, u32[]{:S(2)}) collective-permute-start(bf16[4,16,2048]{2,1,0:T(8,128)(2,1)} %get-tuple-element.53), channel_id=1, source_target_pairs={{0,8},{4,12},{8,0},{12,4},{1,9},{5,13},{9,1},{13,5},{2,10},{6,14},... | collective-permute-start | bytes 786440 | tf_op jit(solution)/shard_map/ppermute | solution.py:465
  192.6 20.0 %collective-permute-start.23 = (bf16[4,16,2048]{2,1,0:T(8,128)(2,1)}, bf16[4,16,2048]{2,1,0:T(8,128)(2,1)S(1)}, u32[]{:S(2)}, u32[]{:S(2)}) collective-permute-start(bf16[4,16,2048]{2,1,0:T(8,128)(2,1)} %get-tuple-element.54), channel_id=1, source_target_pairs={{0,12},{4,0},{8,4},{12,8},{1,13},{5,1},{9,5},{13,9},{2,14},{6,2},{... | collective-permute-start | bytes 786440 | tf_op jit(solution)/shard_map/ppermute | solution.py:465
  201.7 17.0 %collective-permute-start.36 = (bf16[4,16,2048]{2,1,0:T(8,128)(2,1)}, bf16[4,16,2048]{2,1,0:T(8,128)(2,1)S(1)}, u32[]{:S(2)}, u32[]{:S(2)}) collective-permute-start(bf16[4,16,2048]{2,1,0:T(8,128)(2,1)} %get-tuple-element.62), channel_id=1, source_target_pairs={{0,4},{4,8},{8,12},{12,0},{1,5},{5,9},{9,13},{13,1},{2,6},{6,10},{... | collective-permute-start | bytes 786440 | tf_op jit(solution)/shard_map/ppermute | solution.py:465
  202.3 32.5 %collective-permute-start.37 = (bf16[4,16,2048]{2,1,0:T(8,128)(2,1)}, bf16[4,16,2048]{2,1,0:T(8,128)(2,1)S(1)}, u32[]{:S(2)}, u32[]{:S(2)}) collective-permute-start(bf16[4,16,2048]{2,1,0:T(8,128)(2,1)} %get-tuple-element.63), channel_id=1, source_target_pairs={{0,8},{4,12},{8,0},{12,4},{1,9},{5,13},{9,1},{13,5},{2,10},{6,14},... | collective-permute-start | bytes 786440 | tf_op jit(solution)/shard_map/ppermute | solution.py:465
  203.8 31.0 %copy-start.19 = (bf16[4,16,2048]{2,1,0:T(8,128)(2,1)}, bf16[4,16,2048]{2,1,0:T(8,128)(2,1)S(1)}, u32[]{:S(2)}) copy-start(bf16[4,16,2048]{2,1,0:T(8,128)(2,1)S(1)} %collective-permute-done.21.refs_1_) | copy-start | bytes 786436
  203.8 31.0 %collective-permute-start.38 = (bf16[4,16,2048]{2,1,0:T(8,128)(2,1)}, bf16[4,16,2048]{2,1,0:T(8,128)(2,1)S(1)}, u32[]{:S(2)}, u32[]{:S(2)}) collective-permute-start(bf16[4,16,2048]{2,1,0:T(8,128)(2,1)} %get-tuple-element.64), channel_id=1, source_target_pairs={{0,12},{4,0},{8,4},{12,8},{1,13},{5,1},{9,5},{13,9},{2,14},{6,2},{... | collective-permute-start | bytes 786440 | tf_op jit(solution)/shard_map/ppermute | solution.py:465
  212.6 22.3 %copy-start.20 = (bf16[4,16,2048]{2,1,0:T(8,128)(2,1)}, bf16[4,16,2048]{2,1,0:T(8,128)(2,1)S(1)}, u32[]{:S(2)}) copy-start(bf16[4,16,2048]{2,1,0:T(8,128)(2,1)S(1)} %collective-permute-done.22.refs_2_) | copy-start | bytes 786436
  212.6 22.3 %copy-start.21 = (bf16[4,16,2048]{2,1,0:T(8,128)(2,1)}, bf16[4,16,2048]{2,1,0:T(8,128)(2,1)S(1)}, u32[]{:S(2)}) copy-start(bf16[4,16,2048]{2,1,0:T(8,128)(2,1)S(1)} %collective-permute-done.23.refs_3_) | copy-start | bytes 786436
  218.7 16.1 %copy-start.24 = (bf16[4,16,2048]{2,1,0:T(8,128)(2,1)}, bf16[4,16,2048]{2,1,0:T(8,128)(2,1)S(1)}, u32[]{:S(2)}) copy-start(bf16[4,16,2048]{2,1,0:T(8,128)(2,1)S(1)} %collective-permute-done.36.refs_5_) | copy-start | bytes 786436
  (37 other events, 60.0 us)

commit v5 on v3

v5 whole, which is shorter than its diff:
```python
import functools

import jax
import jax.numpy as jnp
from jax import lax
from jax.experimental import pallas as pl
from jax.experimental.pallas import tpu as pltpu
from jax.sharding import PartitionSpec as P

DH = 128
EPSILON = 1e-05
VMEM_LIMIT = 28 * 1024 * 1024

bf16 = jnp.bfloat16
f32 = jnp.float32


def silu(v):
    u = 0.5 * v
    return u + u * jnp.tanh(u)


def params():
    return pltpu.CompilerParams(vmem_limit_bytes=VMEM_LIMIT)


LIGHT = pl.CostEstimate(flops=1000, bytes_accessed=1000, transcendentals=0)


def anywhere(arrays):
    return [pl.BlockSpec(memory_space=pl.ANY)] * len(arrays)


def project_kernel(parts, owners, after, at_ref, *refs):
    rows, weights = refs[:owners], refs[owners:owners + parts]
    keep_ref, send_ref, lhs_ref = refs[owners + parts + after:][:3]
    wides = refs[-parts:]
    zs, chunks, _, piece, _ = rows[0].shape
    depth = weights[0].shape[0]

    @pl.when(pl.program_id(0) == 0)
    def _():
        first = 0
        for p in range(owners):
            for r in range(chunks):
                for z in range(zs):
                    lhs_ref[first:first + piece, :] = rows[p][z, r, 0]
                    first += piece

    res = None
    for k, wide in enumerate(wides):
        wide[...] = weights[k].reshape(depth * 4, DH)[...].astype(f32)
        rhs = jnp.concatenate(
            [wide[pl.ds(i, depth, stride=4), :].astype(bf16) for i in range(4)], axis=1
        )
        term = jnp.dot(lhs_ref[:, k * depth:(k + 1) * depth], rhs, preferred_element_type=f32)
        res = term if res is None else res + term
    res = res.astype(bf16)
    half, _, each, _ = keep_ref.shape
    for p in range(owners):
        into = keep_ref if p < half else send_ref
        for i in range(4):
            into[p % half, i] = res[p * each:(p + 1) * each, i * DH:(i + 1) * DH]


def project(at, tokens, w, head_first, heads, after):
    zs, chunks, owners, piece, depth = tokens.shape
    half, each = owners // 2, zs * chunks * piece
    parts = 4 if depth % 512 == 0 else 1
    shape = jax.ShapeDtypeStruct((half, 4, each, heads * DH), bf16)
    spec = pl.BlockSpec((half, 4, each, DH), lambda j, at: (0, 0, 0, j))
    return pl.pallas_call(
        functools.partial(project_kernel, parts, owners, len(after)),
        grid_spec=pltpu.PrefetchScalarGridSpec(
            num_scalar_prefetch=1,
            grid=(heads,),
            in_specs=[
                pl.BlockSpec(
                    (zs, chunks, 1, piece, depth), lambda j, at, p=p: (0, 0, at[0] ^ p, 0, 0)
                )
                for p in range(owners)
            ]
            + [
                pl.BlockSpec((depth // parts, 4, DH), lambda j, at, k=k: (k, 0, head_first + j))
                for k in range(parts)
            ]
            + anywhere(after),
            out_specs=(spec, spec),
            scratch_shapes=[pltpu.VMEM((owners * each, depth), bf16)]
            + [pltpu.VMEM((depth // parts * 4, DH), f32) for _ in range(parts)],
        ),
        out_shape=(shape, shape),
        compiler_params=params(),
        cost_estimate=LIGHT,
        name="project",
    )(at, *[tokens] * owners, *[w] * parts, *after)


def tie_kernel(*refs):
    pass


def tie(x, after):
    if not after:
        return x
    return pl.pallas_call(
        tie_kernel,
        in_specs=anywhere([x, *after]),
        out_specs=pl.BlockSpec(memory_space=pl.ANY),
        out_shape=jax.ShapeDtypeStruct(x.shape, x.dtype),
        input_output_aliases={0: 0},
        compiler_params=params(),
        cost_estimate=LIGHT,
        name="tie",
    )(x, *after)


def fold_kernel(*refs):
    refs[-1][...] = sum(r[...].astype(f32) for r in refs[:-1]).astype(bf16)


def fold(terms):
    half, tail = terms[-1].shape[0] // 2, terms[0].shape[1:]
    steps = 2 if tail[-1] % 256 == 0 else 1
    block = (half,) + tail[:-1] + (tail[-1] // steps,)
    middle = (0,) * (len(tail) - 1)
    return pl.pallas_call(
        fold_kernel,
        grid=(steps,),
        in_specs=[pl.BlockSpec(block, lambda j: (1,) + middle + (j,))] * len(terms),
        out_specs=pl.BlockSpec(block, lambda j: (0,) + middle + (j,)),
        out_shape=jax.ShapeDtypeStruct((half,) + tail, bf16),
        compiler_params=params(),
        cost_estimate=LIGHT,
        name="fold",
    )(*terms)


def activate_kernel(count, *refs):
    q_ref, rest_ref = refs[-2:]
    for i in range(4):
        part = silu(sum(t[0, i].astype(f32) for t in refs[:count])).astype(bf16)
        if i == 0:
            q_ref[...] = part
        else:
            rest_ref[i - 1] = part


def activate(terms, after):
    _, _, each, width = terms[0].shape
    return pl.pallas_call(
        functools.partial(activate_kernel, len(terms)),
        grid=(1,),
        in_specs=[pl.BlockSpec((1, 4, each, width), lambda j: (0, 0, 0, 0))] * len(terms)
        + anywhere(after),
        out_specs=(
            pl.BlockSpec((each, width), lambda j: (0, 0)),
            pl.BlockSpec((3, each, width), lambda j: (0, 0, 0)),
        ),
        out_shape=(
            jax.ShapeDtypeStruct((each, width), bf16),
            jax.ShapeDtypeStruct((3, each, width), bf16),
        ),
        compiler_params=params(),
        cost_estimate=LIGHT,
        name="activate",
    )(*terms, *after)


def attend_kernel(owners, at_ref, *refs):
    queries, edges = refs[:owners], refs[owners:2 * owners]
    k_ref, v_ref, keep_ref, send_ref, mask_ref = refs[2 * owners:]
    events = mask_ref.shape[1]
    half, each, _ = keep_ref.shape

    @pl.when(pl.program_id(0) == 0)
    def _():
        zs, chunks, _, piece, _ = edges[0].shape
        at = lax.broadcasted_iota(jnp.int32, (piece, events), 1)
        first = 0
        for p in range(owners):
            for r in range(chunks):
                for z in range(zs):
                    edge = edges[p][z, r, 0]
                    seen = (at >= edge[:, :1]) & (at < edge[:, 1:])
                    mask_ref[first:first + piece, :] = jnp.where(seen, 1.0, 0.0).astype(bf16)
                    first += piece

    for h in range(k_ref.shape[1] // DH):
        at = slice(h * DH, (h + 1) * DH)
        query = jnp.concatenate([q[:, at] for q in queries])
        u = lax.dot_general(
            query, k_ref[:, at], (((1,), (1,)), ((), ())), preferred_element_type=f32
        ) * (0.5 * DH ** (-0.5))
        weights = (u + u * jnp.tanh(u)).astype(bf16) * mask_ref[...]
        term = jnp.dot(weights, v_ref[:, at], preferred_element_type=f32).astype(bf16)
        for p in range(owners):
            into = keep_ref if p < half else send_ref
            into[p % half, :, at] = term[p * each:(p + 1) * each]


def edge_spec(edges, p):
    zs, chunks, _, piece, ends = edges.shape
    return pl.BlockSpec((zs, chunks, 1, piece, ends), lambda j, at: (0, 0, at[0] ^ p, 0, 0))


def attend(at, queries, k_cache, v_cache, edges, head_first):
    owners, (each, width) = len(queries), queries[0].shape
    rows, events, half = owners * each, k_cache.shape[0], owners // 2
    first = head_first * DH
    span = 2 * DH if width % (2 * DH) == 0 and first % (2 * DH) == 0 else DH
    cache = pl.BlockSpec((events, span), lambda j, at: (0, first // span + j))
    shape = jax.ShapeDtypeStruct((half, each, width), bf16)
    spec = pl.BlockSpec((half, each, span), lambda j, at: (0, 0, j))
    return pl.pallas_call(
        functools.partial(attend_kernel, owners),
        grid_spec=pltpu.PrefetchScalarGridSpec(
            num_scalar_prefetch=1,
            grid=(width // span,),
            in_specs=[pl.BlockSpec((each, span), lambda j, at: (0, j))] * owners
            + [edge_spec(edges, p) for p in range(owners)]
            + [cache, cache],
            out_specs=(spec, spec),
            scratch_shapes=[pltpu.VMEM((rows, events), bf16)],
        ),
        out_shape=(shape, shape),
        compiler_params=params(),
        cost_estimate=LIGHT,
        name="attend",
    )(at, *queries, *[edges] * owners, k_cache, v_cache)


def merge(means, squares, widths):
    width = sum(widths)
    mean = sum(m * (w / width) for m, w in zip(means, widths))
    square = sum(squares) + sum(w * (m - mean) * (m - mean) for m, w in zip(means, widths))
    return mean, square


def stat_columns(stats):
    return [s[:, :1] for s in stats], [s[:, DH // 2:DH // 2 + 1] for s in stats]


def finish_kernel(terms, widths, at_ref, edge_ref, q_ref, rest_ref, *refs):
    sums, others, (att_ref, stat_ref) = refs[:terms], refs[terms:-2], refs[-2:]
    rows, width = att_ref.shape
    zs, chunks = edge_ref.shape[:2]
    edge = jnp.concatenate(
        [edge_ref[z, r, 0] for r in range(chunks) for z in range(zs)]
    ).astype(f32)
    root = lax.rsqrt(edge[:, 1:] - edge[:, :1])
    total = jnp.zeros((rows, 1), f32)
    for first in range(0, width, DH):
        at = slice(first, first + DH)
        summed = sum(s[0, :, at].astype(f32) for s in sums)
        product = q_ref[:, at].astype(f32) * rest_ref[0, :, at].astype(f32)
        weight = silu(jnp.sum(product, axis=1, keepdims=True) * DH ** (-0.5))
        value = summed * root + weight * rest_ref[1, :, at].astype(f32)
        att_ref[:, at] = value
        total += jnp.sum(value, axis=1, keepdims=True)
    mean = total / width
    spread = jnp.zeros((rows, DH), f32)
    for first in range(0, width, DH):
        away = att_ref[:, first:first + DH] - mean
        spread += away * away
    square = jnp.sum(spread, axis=1, keepdims=True)
    if others:
        means, squares = stat_columns(others)
        mean, square = merge([mean] + means, [square] + squares, [width] + widths)
    lane = lax.broadcasted_iota(jnp.int32, (rows, DH), 1)
    stat_ref[...] = jnp.where(lane < DH // 2, mean, square)


def finish(at, edges, query, rest, sums, others, widths):
    rows, width = query.shape
    return pl.pallas_call(
        functools.partial(finish_kernel, len(sums), widths),
        grid_spec=pltpu.PrefetchScalarGridSpec(
            num_scalar_prefetch=1,
            grid=(1,),
            in_specs=[
                edge_spec(edges, 0),
                pl.BlockSpec((rows, width), lambda j, at: (0, 0)),
                pl.BlockSpec((2, rows, width), lambda j, at: (0, 0, 0)),
            ]
            + [pl.BlockSpec((1, rows, width), lambda j, at: (0, 0, 0))] * len(sums)
            + [pl.BlockSpec((rows, DH), lambda j, at: (0, 0))] * len(others),
            out_specs=(
                pl.BlockSpec((rows, width), lambda j, at: (0, 0)),
                pl.BlockSpec((rows, DH), lambda j, at: (0, 0)),
            ),
        ),
        out_shape=(
            jax.ShapeDtypeStruct((rows, width), f32),
            jax.ShapeDtypeStruct((rows, DH), f32),
        ),
        compiler_params=params(),
        cost_estimate=LIGHT,
        name="finish",
    )(at, edges, query, rest, *sums, *others)


def gate_kernel(count, parts, *refs):
    stats, atts, rests, outs = (
        refs[:count], refs[count:count + parts],
        refs[count + parts:count + 2 * parts], refs[count + 2 * parts:],
    )
    width = sum(a.shape[1] for a in atts)
    means, squares = stat_columns(stats)
    mean, square = merge(means, squares, [width] * count)
    scale = lax.rsqrt(square / (width * count) + EPSILON)
    rows, column = outs[0].shape[0], 0
    for att, rest in zip(atts, rests):
        span = att.shape[1]
        normed = (att[...] - mean) * scale
        gated = (normed * rest[0].astype(f32)).astype(bf16)
        for r, out in enumerate(outs):
            out[:, column:column + span] = gated[r * rows:(r + 1) * rows]
        column += span


def gate_rows(stats, atts, rests, chunks):
    rows, width = atts[0].shape[0], sum(a.shape[1] for a in atts)
    return pl.pallas_call(
        functools.partial(gate_kernel, len(stats), len(atts)),
        grid=(1,),
        in_specs=[pl.BlockSpec((rows, DH), lambda j: (0, 0))] * len(stats)
        + [pl.BlockSpec((rows, a.shape[1]), lambda j: (0, 0)) for a in atts]
        + [pl.BlockSpec((1, rows, r.shape[2]), lambda j: (2, 0, 0)) for r in rests],
        out_specs=[pl.BlockSpec((rows // chunks, width), lambda j: (0, 0))] * chunks,
        out_shape=[jax.ShapeDtypeStruct((rows // chunks, width), bf16)] * chunks,
        compiler_params=params(),
        cost_estimate=LIGHT,
        name="gate",
    )(*stats, *atts, *rests)


def output_kernel(owners, slots, index_ref, *refs):
    rows, w_ref, (keep_ref, send_ref, lhs_ref) = refs[:owners], refs[owners], refs[-3:]
    piece, half = rows[0].shape[1], len(slots) // 2

    @pl.when(pl.program_id(0) == 0)
    def _():
        first = 0
        for slot in slots:
            for p in range(owners):
                lhs_ref[first:first + piece, :] = rows[p][index_ref[0] ^ slot]
                first += piece

    sums = jnp.dot(lhs_ref[...], w_ref[...], preferred_element_type=f32).astype(bf16)
    for k in range(len(slots)):
        into = keep_ref if k < half else send_ref
        for p in range(owners):
            first = (k * owners + p) * piece
            into[k % half, p] = sums[first:first + piece]


def output(index, blocks, w_out, slots, after):
    owners, (each, width) = len(blocks), blocks[0].shape
    zs = len(slots)
    piece, columns = each // zs, w_out.shape[1]
    span = 512 if columns % 512 == 0 else columns
    row_spec = pl.BlockSpec((zs, piece, width), lambda j, at: (0, 0, 0))
    spec = pl.BlockSpec((zs // 2, owners, piece, span), lambda j, at: (0, 0, 0, j))
    shape = jax.ShapeDtypeStruct((zs // 2, owners, piece, columns), bf16)
    return pl.pallas_call(
        functools.partial(output_kernel, owners, slots),
        grid_spec=pltpu.PrefetchScalarGridSpec(
            num_scalar_prefetch=1,
            grid=(columns // span,),
            in_specs=[row_spec] * owners
            + [pl.BlockSpec((width, span), lambda j, at: (0, j))]
            + anywhere(after),
            out_specs=(spec, spec),
            scratch_shapes=[pltpu.VMEM((owners * each, width), bf16)],
        ),
        out_shape=(shape, shape),
        compiler_params=params(),
        cost_estimate=LIGHT,
        name="output",
    )(
        index.reshape(1).astype(jnp.int32),
        *[b.reshape(zs, piece, width) for b in blocks], w_out, *after,
    )


def close_kernel(counts, at_ref, t_ref, *refs):
    out_ref, first = refs[-1], 0
    owners = refs[0].shape[1]
    for r, count in enumerate(counts):
        terms = refs[first:first + count]
        first += count
        for p in range(owners):
            total = t_ref[r * owners + p].astype(f32)
            for term in terms:
                total = total + term[0, p ^ at_ref[0]].astype(f32)
            out_ref[r * owners + p] = total.astype(bf16)


def close(place, index, tokens, chunks):
    _, owners, piece, width = chunks[0][0].shape
    blocks, span = len(chunks) * owners, width // 2
    term = pl.BlockSpec((1, owners, piece, span), lambda j, at: (0, 0, 0, j))
    return pl.pallas_call(
        functools.partial(close_kernel, [len(terms) for terms in chunks]),
        grid_spec=pltpu.PrefetchScalarGridSpec(
            num_scalar_prefetch=1,
            grid=(2,),
            in_specs=[pl.BlockSpec((blocks, piece, span), lambda j, at: (at[1], 0, j))]
            + [term] * sum(len(terms) for terms in chunks),
            out_specs=pl.BlockSpec((blocks, piece, span), lambda j, at: (0, 0, j)),
        ),
        out_shape=jax.ShapeDtypeStruct((blocks, piece, width), bf16),
        compiler_params=params(),
        cost_estimate=LIGHT,
        name="close",
    )(
        jnp.stack([place, index]).astype(jnp.int32),
        tokens.reshape(-1, piece, width),
        *[term for terms in chunks for term in terms],
    )


def bits_of(axis):
    count = lax.axis_size(axis)
    assert count & (count - 1) == 0
    return count.bit_length() - 1


def reverse(index, bits):
    return sum((((index >> b) & 1) << (bits - 1 - b) for b in range(bits)), 0 * index)


def swap(x, axis, bit):
    return lax.ppermute(
        x, axis, [(i, i ^ (1 << bit)) for i in range(lax.axis_size(axis))]
    )


def scatter(keep, send, axis):
    terms, sent = [keep, swap(send, axis, 0)], send
    for b in range(1, bits_of(axis)):
        sent = fold(terms)
        terms.append(swap(sent, axis, b))
    return terms, sent


def gather(x, axis):
    blocks = [x]
    for b in reversed(range(bits_of(axis))):
        blocks = blocks + [swap(block, axis, b) for block in blocks]
    return blocks


def all_stats(stat, axis):
    count = lax.axis_size(axis)
    if count > 8:
        every = lax.all_gather(stat, axis)
        return [every[i] for i in range(count)]
    return [stat] + [
        lax.ppermute(stat, axis, [(i, (i + k) % count) for i in range(count)])
        for k in range(1, count)
    ]


def head_chunks(heads):
    if heads % 8:
        return [1] * heads
    unit = heads // 8
    return [unit, 2 * unit, 2 * unit, 2 * unit, unit]


def local(tokens, w_qkvu, k_cache, v_cache, w_out, vis_start, vis_end):
    cand, depth = tokens.shape
    owners, zs = lax.axis_size("hist"), lax.axis_size("head")
    index = lax.axis_index("head")
    place = reverse(lax.axis_index("hist"), bits_of("hist"))
    width = w_qkvu.shape[2]
    events = k_cache.shape[0]
    chunks = 2 if cand % (2 * owners * zs * 16) == 0 else 1
    piece = cand // (zs * chunks * owners)

    def arrange(x):
        x = x.reshape((zs, chunks, owners, piece) + x.shape[1:])
        if piece % 16 == 0:
            return x
        blocks = [lax.dynamic_index_in_dim(x, p ^ place, 2, False) for p in range(owners)]
        x = jnp.stack(blocks).swapaxes(1, 2)
        return x.reshape((1, 1, owners, zs * chunks * piece) + x.shape[4:])

    at = (place if piece % 16 == 0 else jnp.int32(0)).reshape(1)
    ordered = arrange(tokens)
    first_event = lax.axis_index("hist") * events
    edges = arrange(jnp.stack([vis_start - first_event, vis_end - first_event], axis=1))

    sizes = head_chunks(width // DH)
    firsts = [sum(sizes[:c]) for c in range(len(sizes))]
    last = len(sizes) - 1
    keeps, sent, parts, terms_of, atts, stats = [], [], [], [], [], []

    def front(c):
        after = keeps[-1:]
        if c >= 2:
            after = after + [sent[c - 2]]
        keep, send = project(at, ordered, w_qkvu, firsts[c], sizes[c], after)
        keeps.append(keep)
        before = [terms_of[c - 1][1]] if c >= 1 else []
        if c >= 2:
            before = before + [terms_of[c - 2][-1]]
        send = tie(send, before)
        terms, out = scatter(keep, send, "hist")
        sent.append(out)
        terms_of.append(terms)

    waits = []

    def middle(c):
        query, rest = activate(terms_of[c], waits[-1:] + (atts[c - 2:c - 1] if c >= 2 else []))
        parts.append((query, rest))
        keep, send = attend(at, gather(query, "hist"), k_cache, v_cache, edges, firsts[c])
        waits.append(keep)
        sums, _ = scatter(keep, send, "hist")
        others = stats if c == last else []
        widths = [s * DH for s in sizes[:c]] if c == last else []
        att, stat = finish(at, edges, query, rest, sums, list(others), widths)
        atts.append(att)
        stats.append(stat)

    for c in range(len(sizes)):
        front(c)
        if c >= 2:
            middle(c - 2)
    for c in range(max(0, len(sizes) - 2), len(sizes)):
        middle(c)

    gated = gate_rows(all_stats(stats[-1], "head"), atts, [rest for _, rest in parts], chunks)
    results, after = [], []
    for rows in gated:
        blocks = gather(rows, "hist")
        if piece % 16 == 0 and zs & (zs - 1) == 0:
            slots = [reverse(k, bits_of("head")) for k in range(zs)]
            keep, send = output(index, blocks, w_out, slots, [])
            send = tie(send, after)
            terms, _ = scatter(keep, send, "head")
            after = [terms[1]]
            results.append(terms)
        else:
            whole = jnp.dot(jnp.concatenate(blocks), w_out, preferred_element_type=f32)
            whole = whole.astype(bf16).reshape(owners, zs, piece, -1).swapaxes(0, 1)
            results.append([lax.psum_scatter(whole, "head", scatter_dimension=0, tiled=True)])
    out = close(place, index, tokens, results)
    return out.reshape(cand // zs, -1)


def solution(mesh):
    in_specs = (
        P("groups", "hist"),
        P("hist", None, "head"),
        P(("groups", "hist"), "head"),
        P(("groups", "hist"), "head"),
        P("head", "hist"),
        P("groups"),
        P("groups"),
    )
    out_specs = P(("groups", "head"), "hist")
    return jax.shard_map(local, mesh=mesh, in_specs=in_specs, out_specs=out_specs, check_vma=False)
```

time: 231 us -> 204 us (0.88); the launches traced: 228 us -> 203 us
  Pallas kernels: 84.8 us -> 62.1 us
  waiting for transfers between devices: 82.2 us -> 90.4 us
  other arithmetic: 6.28 us -> 1.22 us
  starting transfers between devices: 32.4 us -> 27.8 us
    ppermute x27 -> x45, waiting for transfers between devices: 45.5 us -> 85.2 us  [swap(): lax.ppermute(x, axis, [(i, i ^ 1 << bit) for i in range(lax.axis_size(axi...]
    ppermute x12 -> x3, waiting for transfers between devices: 36.7 us -> 5.19 us  [all_stats(): lax.ppermute(stat, axis, [(i, (i + k) % count) for i in range(count)])]
    pallas_call x2 -> x5, Pallas kernels: 24.4 us -> 8.91 us  [attend(): pl.pallas_call(functools.partial(attend_kernel, owners), grid_spec=pltpu....]
    ppermute x12 -> x3, starting transfers between devices: 16.8 us -> 4.66 us  [all_stats(): lax.ppermute(stat, axis, [(i, (i + k) % count) for i in range(count)])]
    ppermute x27 -> x45, starting transfers between devices: 15.5 us -> 23.1 us  [swap(): lax.ppermute(x, axis, [(i, i ^ 1 << bit) for i in range(lax.axis_size(axi...]
    convert_element_type x7 -> x0, other arithmetic: 6.06 us -> none  [scatter_rest(): sent = total.astype(bf16)]
    pallas_call x1, Pallas kernels: 5.5 us -> 1.76 us  [close(): pl.pallas_call(functools.partial(close_kernel, [len(terms) for terms in c...]
    pallas_call x16 -> x35, Pallas kernels: 54.9 us -> 51.5 us  [the longest x5 34.5 us: project(): pl.pallas_call(functools.partial(project_kernel, parts, owners, len(after...]
  transfers between devices with their start and end apart: 39 -> 48, of which waited for: 18 -> 23; matrix products, arithmetic and copies ran while one was open for 4% -> 1% of each run, Pallas kernels for 32% -> 27%
where the time goes in v5:
time: 204 us; the launch traced here: 203 us
  waiting for transfers between devices  90.4 us (44%)
  Pallas kernels  62.1 us (30%)
  starting transfers between devices  27.8 us (14%)
  local copies, waits for them, and re-layouts  20.9 us (10%)
    ppermute x45, waiting for transfers between devices, swap(): lax.ppermute(x, axis, [(i, i ^ 1 << bit) for i in range(lax.axis_size(axi...  85.2 us
    pallas_call x5, Pallas kernels, project(): pl.pallas_call(functools.partial(project_kernel, parts, owners, len(after...  34.5 us
    ppermute x45, starting transfers between devices, swap(): lax.ppermute(x, axis, [(i, i ^ 1 << bit) for i in range(lax.axis_size(axi...  23.1 us
    unnamed x56, local copies, waits for them, and re-layouts  19.8 us
    pallas_call x5, Pallas kernels, attend(): pl.pallas_call(functools.partial(attend_kernel, owners), grid_spec=pltpu....  8.91 us
    pallas_call x2, Pallas kernels, output(): pl.pallas_call(functools.partial(output_kernel, owners, slots), grid_spec...  7.33 us
    ppermute x3, waiting for transfers between devices, all_stats(): lax.ppermute(stat, axis, [(i, (i + k) % count) for i in range(count)])  5.19 us
    ppermute x3, starting transfers between devices, all_stats(): lax.ppermute(stat, axis, [(i, (i + k) % count) for i in range(count)])  4.66 us
  transfers between devices with their start and end apart: 48, of which 23 were waited for; matrix products, arithmetic and copies ran while one was open for 1% of the time, Pallas kernels for 27%

profile of v5, /device:TPU:0, one launch (start us, length us, event | category | flops | bytes accessed | tf_op | source)
XLA Modules:
  0.0 203.0 jit_solution(3923982496304627198)
XLA Ops:
  0.0 1.6 copy-done
  1.6 4.8 %project.5 = (bf16[2,4,128,256]{3,2,1,0:T(8,128)(2,1)S(1)}, bf16[2,4,128,256]{3,2,1,0:T(8,128)(2,1)S(1)}) custom-call(s32[1]{0:T(128)} %bitcast.at_ref, bf16[4,2,4,16,2048]{4,3,2,1,0:T(8,128)(2,1)S(1)} %bitcast.13, bf16[4,2,4,16,2048]{4,3,2,1,0:T(8,128)(2,1)S(1)} %bitcast.14, bf16[4,2,4,16,2048]{4,3,2,1,0:T(8,128)(2,1)S(1)} %bitcast.15, ...), custom_call_target="tpu_custom_call" | custom-call | flops 1000 | bytes 1000 | tf_op jit(solution)/shard_map/project/pallas_call | solution.py:72
  7.0 8.0 %project.6 = (bf16[2,4,128,512]{3,2,1,0:T(8,128)(2,1)S(1)}, bf16[2,4,128,512]{3,2,1,0:T(8,128)(2,1)S(1)}) custom-call(s32[1]{0:T(128)} %bitcast.at_ref, bf16[4,2,4,16,2048]{4,3,2,1,0:T(8,128)(2,1)S(1)} %bitcast.17, bf16[4,2,4,16,2048]{4,3,2,1,0:T(8,128)(2,1)S(1)} %bitcast.18, bf16[4,2,4,16,2048]{4,3,2,1,0:T(8,128)(2,1)S(1)} %bitcast.19, ...), custom_call_target="tpu_custom_call" | custom-call | flops 1000 | bytes 1000 | tf_op jit(solution)/shard_map/project/pallas_call | solution.py:72
  15.5 2.9 %collective-permute-start.2 = (bf16[1,4,128,256]{3,2,1,0:T(8,128)(2,1)S(1)}, bf16[1,4,128,256]{3,2,1,0:T(8,128)(2,1)S(1)}, u32[]{:S(2)}, u32[]{:S(2)}) collective-permute-start(bf16[1,4,128,256]{3,2,1,0:T(8,128)(2,1)S(1)} %fold.12.refs_9_), channel_id=1, source_target_pairs={{0,2},{1,3},{2,0},{3,1},{4,6},{5,7},{6,4},{7,5},{8,10},{9,11},{10,... | collective-permute-start | bytes 786440 | tf_op jit(solution)/shard_map/ppermute | solution.py:435
  18.4 8.0 %project.7 = (bf16[2,4,128,512]{3,2,1,0:T(8,128)(2,1)S(1)}, bf16[2,4,128,512]{3,2,1,0:T(8,128)(2,1)S(1)}) custom-call(s32[1]{0:T(128)} %bitcast.at_ref, bf16[4,2,4,16,2048]{4,3,2,1,0:T(8,128)(2,1)S(1)} %bitcast.21, bf16[4,2,4,16,2048]{4,3,2,1,0:T(8,128)(2,1)S(1)} %bitcast.22, bf16[4,2,4,16,2048]{4,3,2,1,0:T(8,128)(2,1)S(1)} %bitcast.23, ...), custom_call_target="tpu_custom_call" | custom-call | flops 1000 | bytes 1000 | tf_op jit(solution)/shard_map/project/pallas_call | solution.py:72
  27.6 1.4 collective-permute-start.4
  29.0 8.7 %project.8 = (bf16[2,4,128,512]{3,2,1,0:T(8,128)(2,1)S(1)}, bf16[2,4,128,512]{3,2,1,0:T(8,128)(2,1)}) custom-call(s32[1]{0:T(128)} %bitcast.at_ref, bf16[4,2,4,16,2048]{4,3,2,1,0:T(8,128)(2,1)S(1)} %bitcast.25, bf16[4,2,4,16,2048]{4,3,2,1,0:T(8,128)(2,1)S(1)} %bitcast.26, bf16[4,2,4,16,2048]{4,3,2,1,0:T(8,128)(2,1)S(1)} %bitcast.27, ...), custom_call_target="tpu_custom_call" | custom-call | flops 1000 | bytes 1000 | tf_op jit(solution)/shard_map/project/pallas_call | solution.py:72
  37.6 3.7 %collective-permute-done.4.refs_2_ = bf16[1,4,128,512]{3,2,1,0:T(8,128)(2,1)S(1)} collective-permute-done((bf16[1,4,128,512]{3,2,1,0:T(8,128)(2,1)S(1)}, bf16[1,4,128,512]{3,2,1,0:T(8,128)(2,1)S(1)}, u32[]{:S(2)}, u32[]{:S(2)}) %collective-permute-start.4) | collective-permute-done | bytes 524320 | tf_op jit(solution)/shard_map/ppermute | solution.py:435
  43.2 1.0 copy-done.19
  46.2 1.7 collective-permute-start.10
  47.9 1.2 copy-done.9
  49.1 1.2 copy-done.14
  53.2 1.1 pad_add_fusion.refs_4_.refs_5_.refs_6_.refs_7_.edge_ref
  54.4 1.6 copy-done.2
  56.0 1.6 copy-done.4
  59.5 1.8 collective-permute-start.13
  61.8 6.6 %collective-permute-done.13.refs_1_ = bf16[128,512]{1,0:T(8,128)(2,1)S(1)} collective-permute-done((bf16[128,512]{1,0:T(8,128)(2,1)S(1)}, bf16[128,512]{1,0:T(8,128)(2,1)S(1)}, u32[]{:S(2)}, u32[]{:S(2)}) %collective-permute-start.13) | collective-permute-done | bytes 131104 | tf_op jit(solution)/shard_map/ppermute | solution.py:435
  68.4 1.2 fold.16
  69.9 5.0 %project.9 = (bf16[2,4,128,256]{3,2,1,0:T(8,128)(2,1)S(1)}, bf16[2,4,128,256]{3,2,1,0:T(8,128)(2,1)S(1)}) custom-call(s32[1]{0:T(128)} %bitcast.at_ref, bf16[4,2,4,16,2048]{4,3,2,1,0:T(8,128)(2,1)S(1)} %bitcast.29, bf16[4,2,4,16,2048]{4,3,2,1,0:T(8,128)(2,1)S(1)} %bitcast.30, bf16[4,2,4,16,2048]{4,3,2,1,0:T(8,128)(2,1)S(1)} %bitcast.31, ...), custom_call_target="tpu_custom_call" | custom-call | flops 1000 | bytes 1000 | tf_op jit(solution)/shard_map/project/pallas_call | solution.py:72
  75.6 1.6 collective-permute-start.17
  77.2 2.3 %attend.6 = (bf16[2,128,512]{2,1,0:T(8,128)(2,1)S(1)}, bf16[2,128,512]{2,1,0:T(8,128)(2,1)S(1)}) custom-call(s32[1]{0:T(128)} %bitcast.at_ref, bf16[128,512]{1,0:T(8,128)(2,1)S(1)} %get-tuple-element.63.refs_0_.q_ref, bf16[128,512]{1,0:T(8,128)(2,1)S(1)} %collective-permute-done.13.refs_1_, bf16[128,512]{1,0:T(8,128)(2,1)S(1)} %collective-permute-done.14.refs_2_, ...), custom_call_target="tpu_custom_call" | custom-call | flops 1000 | bytes 1000 | tf_op jit(solution)/shard_map/attend/pallas_call | solution.py:215
  79.6 5.7 %collective-permute-done.17.refs_2_ = bf16[1,128,256]{2,1,0:T(8,128)(2,1)S(1)} collective-permute-done((bf16[1,128,256]{2,1,0:T(8,128)(2,1)S(1)}, bf16[1,128,256]{2,1,0:T(8,128)(2,1)S(1)}, u32[]{:S(2)}, u32[]{:S(2)}) %collective-permute-start.17) | collective-permute-done | bytes 65568 | tf_op jit(solution)/shard_map/ppermute | solution.py:435
  85.7 1.4 activate.7
  87.4 4.8 %collective-permute-done.18.refs_1_ = bf16[128,512]{1,0:T(8,128)(2,1)S(1)} collective-permute-done((bf16[128,512]{1,0:T(8,128)(2,1)S(1)}, bf16[128,512]{1,0:T(8,128)(2,1)S(1)}, u32[]{:S(2)}, u32[]{:S(2)}) %collective-permute-start.18) | collective-permute-done | bytes 131104 | tf_op jit(solution)/shard_map/ppermute | solution.py:435
  93.6 2.3 %attend.7 = (bf16[2,128,512]{2,1,0:T(8,128)(2,1)S(1)}, bf16[2,128,512]{2,1,0:T(8,128)(2,1)S(1)}) custom-call(s32[1]{0:T(128)} %bitcast.at_ref, bf16[128,512]{1,0:T(8,128)(2,1)S(1)} %get-tuple-element.68.refs_0_.q_ref, bf16[128,512]{1,0:T(8,128)(2,1)S(1)} %collective-permute-done.18.refs_1_, bf16[128,512]{1,0:T(8,128)(2,1)S(1)} %collective-permute-done.19.refs_2_, ...), custom_call_target="tpu_custom_call" | custom-call | flops 1000 | bytes 1000 | tf_op jit(solution)/shard_map/attend/pallas_call | solution.py:215
  96.1 2.2 %collective-permute-done.22.refs_2_ = bf16[1,128,512]{2,1,0:T(8,128)(2,1)S(1)} collective-permute-done((bf16[1,128,512]{2,1,0:T(8,128)(2,1)S(1)}, bf16[1,128,512]{2,1,0:T(8,128)(2,1)S(1)}, u32[]{:S(2)}, u32[]{:S(2)}) %collective-permute-start.22) | collective-permute-done | bytes 131104 | tf_op jit(solution)/shard_map/ppermute | solution.py:435
  98.8 1.4 activate.8
  100.8 1.8 collective-permute-start.8
  102.6 4.0 %collective-permute-done.23.refs_1_ = bf16[128,512]{1,0:T(8,128)(2,1)S(1)} collective-permute-done((bf16[128,512]{1,0:T(8,128)(2,1)S(1)}, bf16[128,512]{1,0:T(8,128)(2,1)S(1)}, u32[]{:S(2)}, u32[]{:S(2)}) %collective-permute-start.23) | collective-permute-done | bytes 131104 | tf_op jit(solution)/shard_map/ppermute | solution.py:435
  108.0 2.3 %attend.8 = (bf16[2,128,512]{2,1,0:T(8,128)(2,1)S(1)}, bf16[2,128,512]{2,1,0:T(8,128)(2,1)S(1)}) custom-call(s32[1]{0:T(128)} %bitcast.at_ref, bf16[128,512]{1,0:T(8,128)(2,1)S(1)} %get-tuple-element.73.refs_0_.q_ref, bf16[128,512]{1,0:T(8,128)(2,1)S(1)} %collective-permute-done.23.refs_1_, bf16[128,512]{1,0:T(8,128)(2,1)S(1)} %collective-permute-done.24.refs_2_, ...), custom_call_target="tpu_custom_call" | custom-call | flops 1000 | bytes 1000 | tf_op jit(solution)/shard_map/attend/pallas_call | solution.py:215
  110.5 3.3 %collective-permute-done.27.refs_2_ = bf16[1,128,512]{2,1,0:T(8,128)(2,1)S(1)} collective-permute-done((bf16[1,128,512]{2,1,0:T(8,128)(2,1)S(1)}, bf16[1,128,512]{2,1,0:T(8,128)(2,1)S(1)}, u32[]{:S(2)}, u32[]{:S(2)}) %collective-permute-start.27) | collective-permute-done | bytes 131104 | tf_op jit(solution)/shard_map/ppermute | solution.py:435
  114.8 4.0 %collective-permute-done.28.refs_1_ = bf16[128,256]{1,0:T(8,128)(2,1)S(1)} collective-permute-done((bf16[128,256]{1,0:T(8,128)(2,1)S(1)}, bf16[128,256]{1,0:T(8,128)(2,1)S(1)}, u32[]{:S(2)}, u32[]{:S(2)}) %collective-permute-start.28) | collective-permute-done | bytes 65568 | tf_op jit(solution)/shard_map/ppermute | solution.py:435
  118.8 1.2 collective-permute-done.30.refs_3_
  122.6 1.1 collective-permute-start.32
  123.7 4.1 %collective-permute-done.34.refs_2_ = bf16[1,128,512]{2,1,0:T(8,128)(2,1)S(1)} collective-permute-done((bf16[1,128,512]{2,1,0:T(8,128)(2,1)S(1)}, bf16[1,128,512]{2,1,0:T(8,128)(2,1)S(1)}, u32[]{:S(2)}, u32[]{:S(2)}) %collective-permute-start.34) | collective-permute-done | bytes 131104 | tf_op jit(solution)/shard_map/ppermute | solution.py:435
  129.1 3.6 %collective-permute-start.37 = (f32[128,128]{1,0:T(8,128)S(1)}, f32[128,128]{1,0:T(8,128)S(1)}, u32[]{:S(2)}, u32[]{:S(2)}) collective-permute-start(f32[128,128]{1,0:T(8,128)S(1)} %get-tuple-element.88.refs_0_), channel_id=1, source_target_pairs={{0,12},{4,0},{8,4},{12,8},{1,13},{5,1},{9,5},{13,9},{2,14},{6,2},{... | collective-permute-start | bytes 196616 | tf_op jit(solution)/shard_map/ppermute | solution.py:461
  133.8 1.4 collective-permute-done.37.refs_3_
  135.2 3.7 %collective-permute-done.36.refs_2_ = f32[128,128]{1,0:T(8,128)S(1)} collective-permute-done((f32[128,128]{1,0:T(8,128)S(1)}, f32[128,128]{1,0:T(8,128)S(1)}, u32[]{:S(2)}, u32[]{:S(2)}) %collective-permute-start.36) | collective-permute-done | bytes 65568 | tf_op jit(solution)/shard_map/ppermute | solution.py:461
  139.9 6.6 %collective-permute-done.38 = bf16[64,2048]{1,0:T(8,128)(2,1)S(1)} collective-permute-done((bf16[64,2048]{1,0:T(8,128)(2,1)S(1)}, bf16[64,2048]{1,0:T(8,128)(2,1)S(1)}, u32[]{:S(2)}, u32[]{:S(2)}) %collective-permute-start.38) | collective-permute-done | bytes 262176 | tf_op jit(solution)/shard_map/ppermute | solution.py:435
  148.1 3.4 %copy-done.6 = bf16[2048,2048]{1,0:T(8,128)(2,1)S(1)} copy-done((bf16[2048,2048]{1,0:T(8,128)(2,1)S(1)}, bf16[2048,2048]{1,0:T(8,128)(2,1)}, u32[]{:S(2)}) %copy-start.6) | copy-done | bytes 8388632
  151.4 3.7 %output.2 = (bf16[2,4,16,2048]{3,2,1,0:T(8,128)(2,1)S(1)}, bf16[2,4,16,2048]{3,2,1,0:T(8,128)(2,1)S(1)}) custom-call(s32[1]{0:T(128)} %bitcast.1.index_ref, bf16[4,16,2048]{2,1,0:T(8,128)(2,1)S(1)} %bitcast.35, bf16[4,16,2048]{2,1,0:T(8,128)(2,1)S(1)} %bitcast.37, bf16[4,16,2048]{2,1,0:T(8,128)(2,1)S(1)} %bitcast.38, bf16[4,16,2048]{2,1,0:T(8,128)(2,1)S(1)} %bitcast.39, ...), custom_call_target="tpu_custom_call" | custom-call | flops 1000 | bytes 1000 | tf_op jit(solution)/shard_map/output/pallas_call | solution.py:366
  157.4 3.4 %copy-done.7 = bf16[2048,2048]{1,0:T(8,128)(2,1)S(1)} copy-done((bf16[2048,2048]{1,0:T(8,128)(2,1)S(1)}, bf16[2048,2048]{1,0:T(8,128)(2,1)}, u32[]{:S(2)}) %copy-start.7) | copy-done | bytes 8388632
  160.8 3.7 %output.3 = (bf16[2,4,16,2048]{3,2,1,0:T(8,128)(2,1)S(1)}, bf16[2,4,16,2048]{3,2,1,0:T(8,128)(2,1)S(1)}) custom-call(s32[1]{0:T(128)} %bitcast.1.index_ref, bf16[4,16,2048]{2,1,0:T(8,128)(2,1)S(1)} %bitcast.34, bf16[4,16,2048]{2,1,0:T(8,128)(2,1)S(1)} %bitcast.36, bf16[4,16,2048]{2,1,0:T(8,128)(2,1)S(1)} %bitcast.40, bf16[4,16,2048]{2,1,0:T(8,128)(2,1)S(1)} %bitcast.41, ...), custom_call_target="tpu_custom_call" | custom-call | flops 1000 | bytes 1000 | tf_op jit(solution)/shard_map/output/pallas_call | solution.py:366
  164.5 4.7 %collective-permute-done.41.refs_1_ = bf16[2,4,16,2048]{3,2,1,0:T(8,128)(2,1)S(1)} collective-permute-done((bf16[2,4,16,2048]{3,2,1,0:T(8,128)(2,1)S(1)}, bf16[2,4,16,2048]{3,2,1,0:T(8,128)(2,1)S(1)}, u32[]{:S(2)}, u32[]{:S(2)}) %collective-permute-start.41) | collective-permute-done | bytes 524320 | tf_op jit(solution)/shard_map/ppermute | solution.py:435
  169.6 2.3 %collective-permute-start.42 = (bf16[1,4,16,2048]{3,2,1,0:T(8,128)(2,1)S(1)}, bf16[1,4,16,2048]{3,2,1,0:T(8,128)(2,1)S(1)}, u32[]{:S(2)}, u32[]{:S(2)}) collective-permute-start(bf16[1,4,16,2048]{3,2,1,0:T(8,128)(2,1)S(1)} %fold.22), channel_id=1, source_target_pairs={{0,8},{4,12},{8,0},{12,4},{1,9},{5,13},{9,1},{13,5},{2,10},{6,14},... | collective-permute-start | bytes 786440 | tf_op jit(solution)/shard_map/ppermute | solution.py:435
  171.9 16.0 %collective-permute-done.46.refs_1_.refs_4_ = bf16[2,4,16,2048]{3,2,1,0:T(8,128)(2,1)S(1)} collective-permute-done((bf16[2,4,16,2048]{3,2,1,0:T(8,128)(2,1)S(1)}, bf16[2,4,16,2048]{3,2,1,0:T(8,128)(2,1)S(1)}, u32[]{:S(2)}, u32[]{:S(2)}) %collective-permute-start.46) | collective-permute-done | bytes 524320 | tf_op jit(solution)/shard_map/ppermute | solution.py:435
  188.6 12.7 %collective-permute-done.47.refs_5_ = bf16[1,4,16,2048]{3,2,1,0:T(8,128)(2,1)S(1)} collective-permute-done((bf16[1,4,16,2048]{3,2,1,0:T(8,128)(2,1)S(1)}, bf16[1,4,16,2048]{3,2,1,0:T(8,128)(2,1)S(1)}, u32[]{:S(2)}, u32[]{:S(2)}) %collective-permute-start.47) | collective-permute-done | bytes 262176 | tf_op jit(solution)/shard_map/ppermute | solution.py:435
  201.2 1.8 close.1
  (150 shorter events, 28.6 us)
Async XLA Ops:
  6.5 8.6 %collective-permute-start = (bf16[2,4,128,256]{3,2,1,0:T(8,128)(2,1)S(1)}, bf16[2,4,128,256]{3,2,1,0:T(8,128)(2,1)S(1)}, u32[]{:S(2)}, u32[]{:S(2)}) collective-permute-start(bf16[2,4,128,256]{3,2,1,0:T(8,128)(2,1)S(1)} %get-tuple-element.53), channel_id=1, source_target_pairs={{0,1},{1,0},{2,3},{3,2},{4,5},{5,4},{6,7},{7,6},{8,9},{9,8},{10,11... | collective-permute-start | bytes 1572872 | tf_op jit(solution)/shard_map/ppermute | solution.py:435
  15.0 11.4 %collective-permute-start.1 = (bf16[2,4,128,512]{3,2,1,0:T(8,128)(2,1)S(1)}, bf16[2,4,128,512]{3,2,1,0:T(8,128)(2,1)S(1)}, u32[]{:S(2)}, u32[]{:S(2)}) collective-permute-start(bf16[2,4,128,512]{3,2,1,0:T(8,128)(2,1)S(1)} %tie.5), channel_id=1, source_target_pairs={{0,1},{1,0},{2,3},{3,2},{4,5},{5,4},{6,7},{7,6},{8,9},{9,8},{10,11... | collective-permute-start | bytes 3145736 | tf_op jit(solution)/shard_map/ppermute | solution.py:435
  15.5 11.0 %collective-permute-start.2 = (bf16[1,4,128,256]{3,2,1,0:T(8,128)(2,1)S(1)}, bf16[1,4,128,256]{3,2,1,0:T(8,128)(2,1)S(1)}, u32[]{:S(2)}, u32[]{:S(2)}) collective-permute-start(bf16[1,4,128,256]{3,2,1,0:T(8,128)(2,1)S(1)} %fold.12.refs_9_), channel_id=1, source_target_pairs={{0,2},{1,3},{2,0},{3,1},{4,6},{5,7},{6,4},{7,5},{8,10},{9,11},{10,... | collective-permute-start | bytes 786440 | tf_op jit(solution)/shard_map/ppermute | solution.py:435
  26.5 14.9 %collective-permute-start.3 = (bf16[2,4,128,512]{3,2,1,0:T(8,128)(2,1)S(1)}, bf16[2,4,128,512]{3,2,1,0:T(8,128)(2,1)S(1)}, u32[]{:S(2)}, u32[]{:S(2)}) collective-permute-start(bf16[2,4,128,512]{3,2,1,0:T(8,128)(2,1)S(1)} %tie.6), channel_id=1, source_target_pairs={{0,1},{1,0},{2,3},{3,2},{4,5},{5,4},{6,7},{7,6},{8,9},{9,8},{10,11... | collective-permute-start | bytes 3145736 | tf_op jit(solution)/shard_map/ppermute | solution.py:435
  27.6 13.8 %collective-permute-start.4 = (bf16[1,4,128,512]{3,2,1,0:T(8,128)(2,1)S(1)}, bf16[1,4,128,512]{3,2,1,0:T(8,128)(2,1)S(1)}, u32[]{:S(2)}, u32[]{:S(2)}) collective-permute-start(bf16[1,4,128,512]{3,2,1,0:T(8,128)(2,1)S(1)} %fold.13.refs_9_), channel_id=1, source_target_pairs={{0,2},{1,3},{2,0},{3,1},{4,6},{5,7},{6,4},{7,5},{8,10},{9,11},{10,... | collective-permute-start | bytes 1572872 | tf_op jit(solution)/shard_map/ppermute | solution.py:435
  43.2 25.2 %collective-permute-start.5 = (bf16[2,4,128,512]{3,2,1,0:T(8,128)(2,1)}, bf16[2,4,128,512]{3,2,1,0:T(8,128)(2,1)}, u32[]{:S(2)}, u32[]{:S(2)}) collective-permute-start(bf16[2,4,128,512]{3,2,1,0:T(8,128)(2,1)} %tie.7), channel_id=1, source_target_pairs={{0,1},{1,0},{2,3},{3,2},{4,5},{5,4},{6,7},{7,6},{8,9},{9,8},{10,11... | collective-permute-start | bytes 3145736 | tf_op jit(solution)/shard_map/ppermute | solution.py:435
  46.2 6.6 %collective-permute-start.10 = (bf16[128,256]{1,0:T(8,128)(2,1)S(1)}, bf16[128,256]{1,0:T(8,128)(2,1)S(1)}, u32[]{:S(2)}, u32[]{:S(2)}) collective-permute-start(bf16[128,256]{1,0:T(8,128)(2,1)S(1)} %get-tuple-element.61.refs_0_.q_ref), channel_id=1, source_target_pairs={{0,2},{1,3},{2,0},{3,1},{4,6},{5,7},{6,4},{7,5},{8,10},{9,11},{10,... | collective-permute-start | bytes 196616 | tf_op jit(solution)/shard_map/ppermute | solution.py:435
  51.3 23.6 %collective-permute-start.6 = (bf16[1,4,128,512]{3,2,1,0:T(8,128)(2,1)}, bf16[1,4,128,512]{3,2,1,0:T(8,128)(2,1)}, u32[]{:S(2)}, u32[]{:S(2)}) collective-permute-start(bf16[1,4,128,512]{3,2,1,0:T(8,128)(2,1)} %fold.14.refs_9_), channel_id=1, source_target_pairs={{0,2},{1,3},{2,0},{3,1},{4,6},{5,7},{6,4},{7,5},{8,10},{9,11},{10,... | collective-permute-start | bytes 1572872 | tf_op jit(solution)/shard_map/ppermute | solution.py:435
  52.7 1.7 collective-permute-start.11
  52.7 1.7 collective-permute-start.12
  59.5 8.9 %collective-permute-start.13 = (bf16[128,512]{1,0:T(8,128)(2,1)S(1)}, bf16[128,512]{1,0:T(8,128)(2,1)S(1)}, u32[]{:S(2)}, u32[]{:S(2)}) collective-permute-start(bf16[128,512]{1,0:T(8,128)(2,1)S(1)} %get-tuple-element.63.refs_0_.q_ref), channel_id=1, source_target_pairs={{0,2},{1,3},{2,0},{3,1},{4,6},{5,7},{6,4},{7,5},{8,10},{9,11},{10,... | collective-permute-start | bytes 393224 | tf_op jit(solution)/shard_map/ppermute | solution.py:435
  61.3 14.1 %collective-permute-start.16 = (bf16[2,128,256]{2,1,0:T(8,128)(2,1)S(1)}, bf16[2,128,256]{2,1,0:T(8,128)(2,1)S(1)}, u32[]{:S(2)}, u32[]{:S(2)}) collective-permute-start(bf16[2,128,256]{2,1,0:T(8,128)(2,1)S(1)} %get-tuple-element.66), channel_id=1, source_target_pairs={{0,1},{1,0},{2,3},{3,2},{4,5},{5,4},{6,7},{7,6},{8,9},{9,8},{10,11... | collective-permute-start | bytes 393224 | tf_op jit(solution)/shard_map/ppermute | solution.py:435
  61.3 15.9 %collective-permute-start.14 = (bf16[128,512]{1,0:T(8,128)(2,1)S(1)}, bf16[128,512]{1,0:T(8,128)(2,1)S(1)}, u32[]{:S(2)}, u32[]{:S(2)}) collective-permute-start(bf16[128,512]{1,0:T(8,128)(2,1)S(1)} %get-tuple-element.63.refs_0_.q_ref), channel_id=1, source_target_pairs={{0,1},{1,0},{2,3},{3,2},{4,5},{5,4},{6,7},{7,6},{8,9},{9,8},{10,11... | collective-permute-start | bytes 393224 | tf_op jit(solution)/shard_map/ppermute | solution.py:435
  68.4 8.8 %collective-permute-start.15 = (bf16[128,512]{1,0:T(8,128)(2,1)S(1)}, bf16[128,512]{1,0:T(8,128)(2,1)S(1)}, u32[]{:S(2)}, u32[]{:S(2)}) collective-permute-start(bf16[128,512]{1,0:T(8,128)(2,1)S(1)} %collective-permute-done.13.refs_1_), channel_id=1, source_target_pairs={{0,1},{1,0},{2,3},{3,2},{4,5},{5,4},{6,7},{7,6},{8,9},{9,8},{10,11... | collective-permute-start | bytes 393224 | tf_op jit(solution)/shard_map/ppermute | solution.py:435
  69.5 29.3 %collective-permute-start.9 = (bf16[1,4,128,512]{3,2,1,0:T(8,128)(2,1)S(1)}, bf16[1,4,128,512]{3,2,1,0:T(8,128)(2,1)S(1)}, u32[]{:S(2)}, u32[]{:S(2)}) collective-permute-start(bf16[1,4,128,512]{3,2,1,0:T(8,128)(2,1)S(1)} %fold.16), channel_id=1, source_target_pairs={{0,2},{1,3},{2,0},{3,1},{4,6},{5,7},{6,4},{7,5},{8,10},{9,11},{10,... | collective-permute-start | bytes 1572872 | tf_op jit(solution)/shard_map/ppermute | solution.py:435
  74.9 25.6 %collective-permute-start.7 = (bf16[2,4,128,256]{3,2,1,0:T(8,128)(2,1)S(1)}, bf16[2,4,128,256]{3,2,1,0:T(8,128)(2,1)S(1)}, u32[]{:S(2)}, u32[]{:S(2)}) collective-permute-start(bf16[2,4,128,256]{3,2,1,0:T(8,128)(2,1)S(1)} %tie.8), channel_id=1, source_target_pairs={{0,1},{1,0},{2,3},{3,2},{4,5},{5,4},{6,7},{7,6},{8,9},{9,8},{10,11... | collective-permute-start | bytes 1572872 | tf_op jit(solution)/shard_map/ppermute | solution.py:435
  75.6 9.8 %collective-permute-start.17 = (bf16[1,128,256]{2,1,0:T(8,128)(2,1)S(1)}, bf16[1,128,256]{2,1,0:T(8,128)(2,1)S(1)}, u32[]{:S(2)}, u32[]{:S(2)}) collective-permute-start(bf16[1,128,256]{2,1,0:T(8,128)(2,1)S(1)} %fold.17), channel_id=1, source_target_pairs={{0,2},{1,3},{2,0},{3,1},{4,6},{5,7},{6,4},{7,5},{8,10},{9,11},{10,... | collective-permute-start | bytes 196616 | tf_op jit(solution)/shard_map/ppermute | solution.py:435
  79.5 12.7 %collective-permute-start.21 = (bf16[2,128,512]{2,1,0:T(8,128)(2,1)S(1)}, bf16[2,128,512]{2,1,0:T(8,128)(2,1)S(1)}, u32[]{:S(2)}, u32[]{:S(2)}) collective-permute-start(bf16[2,128,512]{2,1,0:T(8,128)(2,1)S(1)} %get-tuple-element.71), channel_id=1, source_target_pairs={{0,1},{1,0},{2,3},{3,2},{4,5},{5,4},{6,7},{7,6},{8,9},{9,8},{10,11... | collective-permute-start | bytes 786440 | tf_op jit(solution)/shard_map/ppermute | solution.py:435
  87.1 5.2 %collective-permute-start.18 = (bf16[128,512]{1,0:T(8,128)(2,1)S(1)}, bf16[128,512]{1,0:T(8,128)(2,1)S(1)}, u32[]{:S(2)}, u32[]{:S(2)}) collective-permute-start(bf16[128,512]{1,0:T(8,128)(2,1)S(1)} %get-tuple-element.68.refs_0_.q_ref), channel_id=1, source_target_pairs={{0,2},{1,3},{2,0},{3,1},{4,6},{5,7},{6,4},{7,5},{8,10},{9,11},{10,... | collective-permute-start | bytes 393224 | tf_op jit(solution)/shard_map/ppermute | solution.py:435
  87.4 5.3 %collective-permute-start.19 = (bf16[128,512]{1,0:T(8,128)(2,1)S(1)}, bf16[128,512]{1,0:T(8,128)(2,1)S(1)}, u32[]{:S(2)}, u32[]{:S(2)}) collective-permute-start(bf16[128,512]{1,0:T(8,128)(2,1)S(1)} %get-tuple-element.68.refs_0_.q_ref), channel_id=1, source_target_pairs={{0,1},{1,0},{2,3},{3,2},{4,5},{5,4},{6,7},{7,6},{8,9},{9,8},{10,11... | collective-permute-start | bytes 393224 | tf_op jit(solution)/shard_map/ppermute | solution.py:435
  92.3 1.3 collective-permute-start.20
  92.4 6.0 %collective-permute-start.22 = (bf16[1,128,512]{2,1,0:T(8,128)(2,1)S(1)}, bf16[1,128,512]{2,1,0:T(8,128)(2,1)S(1)}, u32[]{:S(2)}, u32[]{:S(2)}) collective-permute-start(bf16[1,128,512]{2,1,0:T(8,128)(2,1)S(1)} %fold.18), channel_id=1, source_target_pairs={{0,2},{1,3},{2,0},{3,1},{4,6},{5,7},{6,4},{7,5},{8,10},{9,11},{10,... | collective-permute-start | bytes 393224 | tf_op jit(solution)/shard_map/ppermute | solution.py:435
  95.9 10.7 %collective-permute-start.26 = (bf16[2,128,512]{2,1,0:T(8,128)(2,1)S(1)}, bf16[2,128,512]{2,1,0:T(8,128)(2,1)S(1)}, u32[]{:S(2)}, u32[]{:S(2)}) collective-permute-start(bf16[2,128,512]{2,1,0:T(8,128)(2,1)S(1)} %get-tuple-element.76), channel_id=1, source_target_pairs={{0,1},{1,0},{2,3},{3,2},{4,5},{5,4},{6,7},{7,6},{8,9},{9,8},{10,11... | collective-permute-start | bytes 786440 | tf_op jit(solution)/shard_map/ppermute | solution.py:435
  100.2 6.5 %collective-permute-start.23 = (bf16[128,512]{1,0:T(8,128)(2,1)S(1)}, bf16[128,512]{1,0:T(8,128)(2,1)S(1)}, u32[]{:S(2)}, u32[]{:S(2)}) collective-permute-start(bf16[128,512]{1,0:T(8,128)(2,1)S(1)} %get-tuple-element.73.refs_0_.q_ref), channel_id=1, source_target_pairs={{0,2},{1,3},{2,0},{3,1},{4,6},{5,7},{6,4},{7,5},{8,10},{9,11},{10,... | collective-permute-start | bytes 393224 | tf_op jit(solution)/shard_map/ppermute | solution.py:435
  100.8 13.4 %collective-permute-start.8 = (bf16[1,4,128,256]{3,2,1,0:T(8,128)(2,1)S(1)}, bf16[1,4,128,256]{3,2,1,0:T(8,128)(2,1)S(1)}, u32[]{:S(2)}, u32[]{:S(2)}) collective-permute-start(bf16[1,4,128,256]{3,2,1,0:T(8,128)(2,1)S(1)} %fold.15), channel_id=1, source_target_pairs={{0,2},{1,3},{2,0},{3,1},{4,6},{5,7},{6,4},{7,5},{8,10},{9,11},{10,... | collective-permute-start | bytes 786440 | tf_op jit(solution)/shard_map/ppermute | solution.py:435
  102.6 4.4 %collective-permute-start.24 = (bf16[128,512]{1,0:T(8,128)(2,1)S(1)}, bf16[128,512]{1,0:T(8,128)(2,1)S(1)}, u32[]{:S(2)}, u32[]{:S(2)}) collective-permute-start(bf16[128,512]{1,0:T(8,128)(2,1)S(1)} %get-tuple-element.73.refs_0_.q_ref), channel_id=1, source_target_pairs={{0,1},{1,0},{2,3},{3,2},{4,5},{5,4},{6,7},{7,6},{8,9},{9,8},{10,11... | collective-permute-start | bytes 393224 | tf_op jit(solution)/shard_map/ppermute | solution.py:435
  106.7 1.3 collective-permute-start.25
  106.8 7.0 %collective-permute-start.27 = (bf16[1,128,512]{2,1,0:T(8,128)(2,1)S(1)}, bf16[1,128,512]{2,1,0:T(8,128)(2,1)S(1)}, u32[]{:S(2)}, u32[]{:S(2)}) collective-permute-start(bf16[1,128,512]{2,1,0:T(8,128)(2,1)S(1)} %fold.19), channel_id=1, source_target_pairs={{0,2},{1,3},{2,0},{3,1},{4,6},{5,7},{6,4},{7,5},{8,10},{9,11},{10,... | collective-permute-start | bytes 393224 | tf_op jit(solution)/shard_map/ppermute | solution.py:435
  110.3 10.9 %collective-permute-start.33 = (bf16[2,128,512]{2,1,0:T(8,128)(2,1)S(1)}, bf16[2,128,512]{2,1,0:T(8,128)(2,1)S(1)}, u32[]{:S(2)}, u32[]{:S(2)}) collective-permute-start(bf16[2,128,512]{2,1,0:T(8,128)(2,1)S(1)} %get-tuple-element.86), channel_id=1, source_target_pairs={{0,1},{1,0},{2,3},{3,2},{4,5},{5,4},{6,7},{7,6},{8,9},{9,8},{10,11... | collective-permute-start | bytes 786440 | tf_op jit(solution)/shard_map/ppermute | solution.py:435
  114.4 4.3 %collective-permute-start.28 = (bf16[128,256]{1,0:T(8,128)(2,1)S(1)}, bf16[128,256]{1,0:T(8,128)(2,1)S(1)}, u32[]{:S(2)}, u32[]{:S(2)}) collective-permute-start(bf16[128,256]{1,0:T(8,128)(2,1)S(1)} %get-tuple-element.78.refs_0_.q_ref), channel_id=1, source_target_pairs={{0,2},{1,3},{2,0},{3,1},{4,6},{5,7},{6,4},{7,5},{8,10},{9,11},{10,... | collective-permute-start | bytes 196616 | tf_op jit(solution)/shard_map/ppermute | solution.py:435
  114.8 4.0 %collective-permute-start.29 = (bf16[128,256]{1,0:T(8,128)(2,1)S(1)}, bf16[128,256]{1,0:T(8,128)(2,1)S(1)}, u32[]{:S(2)}, u32[]{:S(2)}) collective-permute-start(bf16[128,256]{1,0:T(8,128)(2,1)S(1)} %get-tuple-element.78.refs_0_.q_ref), channel_id=1, source_target_pairs={{0,1},{1,0},{2,3},{3,2},{4,5},{5,4},{6,7},{7,6},{8,9},{9,8},{10,11... | collective-permute-start | bytes 196616 | tf_op jit(solution)/shard_map/ppermute | solution.py:435
  118.8 1.3 collective-permute-start.30
  121.0 1.4 collective-permute-start.31
  121.4 6.4 %collective-permute-start.34 = (bf16[1,128,512]{2,1,0:T(8,128)(2,1)S(1)}, bf16[1,128,512]{2,1,0:T(8,128)(2,1)S(1)}, u32[]{:S(2)}, u32[]{:S(2)}) collective-permute-start(bf16[1,128,512]{2,1,0:T(8,128)(2,1)S(1)} %fold.21), channel_id=1, source_target_pairs={{0,2},{1,3},{2,0},{3,1},{4,6},{5,7},{6,4},{7,5},{8,10},{9,11},{10,... | collective-permute-start | bytes 393224 | tf_op jit(solution)/shard_map/ppermute | solution.py:435
  122.6 6.0 %collective-permute-start.32 = (bf16[1,128,256]{2,1,0:T(8,128)(2,1)S(1)}, bf16[1,128,256]{2,1,0:T(8,128)(2,1)S(1)}, u32[]{:S(2)}, u32[]{:S(2)}) collective-permute-start(bf16[1,128,256]{2,1,0:T(8,128)(2,1)S(1)} %fold.20), channel_id=1, source_target_pairs={{0,2},{1,3},{2,0},{3,1},{4,6},{5,7},{6,4},{7,5},{8,10},{9,11},{10,... | collective-permute-start | bytes 196616 | tf_op jit(solution)/shard_map/ppermute | solution.py:435
  129.1 6.1 %collective-permute-start.37 = (f32[128,128]{1,0:T(8,128)S(1)}, f32[128,128]{1,0:T(8,128)S(1)}, u32[]{:S(2)}, u32[]{:S(2)}) collective-permute-start(f32[128,128]{1,0:T(8,128)S(1)} %get-tuple-element.88.refs_0_), channel_id=1, source_target_pairs={{0,12},{4,0},{8,4},{12,8},{1,13},{5,1},{9,5},{13,9},{2,14},{6,2},{... | collective-permute-start | bytes 196616 | tf_op jit(solution)/shard_map/ppermute | solution.py:461
  132.7 6.2 %collective-permute-start.36 = (f32[128,128]{1,0:T(8,128)S(1)}, f32[128,128]{1,0:T(8,128)S(1)}, u32[]{:S(2)}, u32[]{:S(2)}) collective-permute-start(f32[128,128]{1,0:T(8,128)S(1)} %get-tuple-element.88.refs_0_), channel_id=1, source_target_pairs={{0,8},{4,12},{8,0},{12,4},{1,9},{5,13},{9,1},{13,5},{2,10},{6,14},... | collective-permute-start | bytes 196616 | tf_op jit(solution)/shard_map/ppermute | solution.py:461
  132.7 6.2 %collective-permute-start.35 = (f32[128,128]{1,0:T(8,128)S(1)}, f32[128,128]{1,0:T(8,128)S(1)}, u32[]{:S(2)}, u32[]{:S(2)}) collective-permute-start(f32[128,128]{1,0:T(8,128)S(1)} %get-tuple-element.88.refs_0_), channel_id=1, source_target_pairs={{0,4},{4,8},{8,12},{12,0},{1,5},{5,9},{9,13},{13,1},{2,6},{6,10},{... | collective-permute-start | bytes 196616 | tf_op jit(solution)/shard_map/ppermute | solution.py:461
  139.3 7.3 %collective-permute-start.38 = (bf16[64,2048]{1,0:T(8,128)(2,1)S(1)}, bf16[64,2048]{1,0:T(8,128)(2,1)S(1)}, u32[]{:S(2)}, u32[]{:S(2)}) collective-permute-start(bf16[64,2048]{1,0:T(8,128)(2,1)S(1)} %get-tuple-element.91), channel_id=1, source_target_pairs={{0,2},{1,3},{2,0},{3,1},{4,6},{5,7},{6,4},{7,5},{8,10},{9,11},{10,... | collective-permute-start | bytes 786440 | tf_op jit(solution)/shard_map/ppermute | solution.py:435
  139.9 7.2 %collective-permute-start.39 = (bf16[64,2048]{1,0:T(8,128)(2,1)S(1)}, bf16[64,2048]{1,0:T(8,128)(2,1)S(1)}, u32[]{:S(2)}, u32[]{:S(2)}) collective-permute-start(bf16[64,2048]{1,0:T(8,128)(2,1)S(1)} %get-tuple-element.91), channel_id=1, source_target_pairs={{0,1},{1,0},{2,3},{3,2},{4,5},{5,4},{6,7},{7,6},{8,9},{9,8},{10,11... | collective-permute-start | bytes 786440 | tf_op jit(solution)/shard_map/ppermute | solution.py:435
  146.5 1.5 collective-permute-start.40
  146.5 9.0 %collective-permute-start.43 = (bf16[64,2048]{1,0:T(8,128)(2,1)S(1)}, bf16[64,2048]{1,0:T(8,128)(2,1)S(1)}, u32[]{:S(2)}, u32[]{:S(2)}) collective-permute-start(bf16[64,2048]{1,0:T(8,128)(2,1)S(1)} %get-tuple-element.94), channel_id=1, source_target_pairs={{0,2},{1,3},{2,0},{3,1},{4,6},{5,7},{6,4},{7,5},{8,10},{9,11},{10,... | collective-permute-start | bytes 786440 | tf_op jit(solution)/shard_map/ppermute | solution.py:435
  155.1 14.0 %collective-permute-start.41 = (bf16[2,4,16,2048]{3,2,1,0:T(8,128)(2,1)S(1)}, bf16[2,4,16,2048]{3,2,1,0:T(8,128)(2,1)S(1)}, u32[]{:S(2)}, u32[]{:S(2)}) collective-permute-start(bf16[2,4,16,2048]{3,2,1,0:T(8,128)(2,1)S(1)} %get-tuple-element.93), channel_id=1, source_target_pairs={{0,4},{4,0},{8,12},{12,8},{1,5},{5,1},{9,13},{13,9},{2,6},{6,2},{1... | collective-permute-start | bytes 1572872 | tf_op jit(solution)/shard_map/ppermute | solution.py:435
  155.5 1.5 collective-permute-start.44
  155.5 1.9 collective-permute-start.45
  169.2 18.8 %collective-permute-start.46 = (bf16[2,4,16,2048]{3,2,1,0:T(8,128)(2,1)S(1)}, bf16[2,4,16,2048]{3,2,1,0:T(8,128)(2,1)S(1)}, u32[]{:S(2)}, u32[]{:S(2)}) collective-permute-start(bf16[2,4,16,2048]{3,2,1,0:T(8,128)(2,1)S(1)} %tie.9), channel_id=1, source_target_pairs={{0,4},{4,0},{8,12},{12,8},{1,5},{5,1},{9,13},{13,9},{2,6},{6,2},{1... | collective-permute-start | bytes 1572872 | tf_op jit(solution)/shard_map/ppermute | solution.py:435
  169.6 18.9 %collective-permute-start.42 = (bf16[1,4,16,2048]{3,2,1,0:T(8,128)(2,1)S(1)}, bf16[1,4,16,2048]{3,2,1,0:T(8,128)(2,1)S(1)}, u32[]{:S(2)}, u32[]{:S(2)}) collective-permute-start(bf16[1,4,16,2048]{3,2,1,0:T(8,128)(2,1)S(1)} %fold.22), channel_id=1, source_target_pairs={{0,8},{4,12},{8,0},{12,4},{1,9},{5,13},{9,1},{13,5},{2,10},{6,14},... | collective-permute-start | bytes 786440 | tf_op jit(solution)/shard_map/ppermute | solution.py:435
  188.1 13.2 %collective-permute-start.47 = (bf16[1,4,16,2048]{3,2,1,0:T(8,128)(2,1)S(1)}, bf16[1,4,16,2048]{3,2,1,0:T(8,128)(2,1)S(1)}, u32[]{:S(2)}, u32[]{:S(2)}) collective-permute-start(bf16[1,4,16,2048]{3,2,1,0:T(8,128)(2,1)S(1)} %fold.23), channel_id=1, source_target_pairs={{0,8},{4,12},{8,0},{12,4},{1,9},{5,13},{9,1},{13,5},{2,10},{6,14},... | collective-permute-start | bytes 786440 | tf_op jit(solution)/shard_map/ppermute | solution.py:435
  (28 other events, 125.7 us)

commit v6 on v5

--- a/solution.py
+++ b/solution.py
@@ -25,6 +25,10 @@
 
 
 LIGHT = pl.CostEstimate(flops=1000, bytes_accessed=1000, transcendentals=0)
+
+
+def far(x):
+    return pltpu.with_memory_space_constraint(x, pltpu.HBM)
 
 
 def anywhere(arrays):
@@ -93,7 +97,7 @@
         compiler_params=params(),
         cost_estimate=LIGHT,
         name="project",
-    )(at, *[tokens] * owners, *[w] * parts, *after)
+    )(at, *[far(tokens)] * owners, *[far(w)] * parts, *after)
 
 
 def tie_kernel(*refs):
@@ -169,7 +173,8 @@
 
 def attend_kernel(owners, at_ref, *refs):
     queries, edges = refs[:owners], refs[owners:2 * owners]
-    k_ref, v_ref, keep_ref, send_ref, mask_ref = refs[2 * owners:]
+    k_ref, v_ref = refs[2 * owners:2 * owners + 2]
+    keep_ref, send_ref, mask_ref = refs[-3:]
     events = mask_ref.shape[1]
     half, each, _ = keep_ref.shape
 
@@ -204,7 +209,7 @@
     return pl.BlockSpec((zs, chunks, 1, piece, ends), lambda j, at: (0, 0, at[0] ^ p, 0, 0))
 
 
-def attend(at, queries, k_cache, v_cache, edges, head_first):
+def attend(at, queries, k_cache, v_cache, edges, head_first, after):
     owners, (each, width) = len(queries), queries[0].shape
     rows, events, half = owners * each, k_cache.shape[0], owners // 2
     first = head_first * DH
@@ -219,7 +224,8 @@
             grid=(width // span,),
             in_specs=[pl.BlockSpec((each, span), lambda j, at: (0, j))] * owners
             + [edge_spec(edges, p) for p in range(owners)]
-            + [cache, cache],
+            + [cache, cache]
+            + anywhere(after),
             out_specs=(spec, spec),
             scratch_shapes=[pltpu.VMEM((rows, events), bf16)],
         ),
@@ -227,7 +233,7 @@
         compiler_params=params(),
         cost_estimate=LIGHT,
         name="attend",
-    )(at, *queries, *[edges] * owners, k_cache, v_cache)
+    )(at, *queries, *[edges] * owners, far(k_cache), far(v_cache), *after)
 
 
 def merge(means, squares, widths):
@@ -238,7 +244,9 @@
 
 
 def stat_columns(stats):
-    return [s[:, :1] for s in stats], [s[:, DH // 2:DH // 2 + 1] for s in stats]
+    stats = [s[...] for s in stats]
+    stats = [s if s.shape[0] > 8 else jnp.concatenate([s] * (DH // 8)).T for s in stats]
+    return [s[:, :1] for s in stats], [s[:, 4:5] for s in stats]
 
 
 def finish_kernel(terms, widths, at_ref, edge_ref, q_ref, rest_ref, *refs):
@@ -268,11 +276,13 @@
         means, squares = stat_columns(others)
         mean, square = merge([mean] + means, [square] + squares, [width] + widths)
     lane = lax.broadcasted_iota(jnp.int32, (rows, DH), 1)
-    stat_ref[...] = jnp.where(lane < DH // 2, mean, square)
+    stat = jnp.where(lane < 4, mean, square)
+    stat_ref[...] = stat if stat_ref.shape == stat.shape else stat.T[:8]
 
 
 def finish(at, edges, query, rest, sums, others, widths):
     rows, width = query.shape
+    stat = (8, rows) if others and rows == DH else (rows, DH)
     return pl.pallas_call(
         functools.partial(finish_kernel, len(sums), widths),
         grid_spec=pltpu.PrefetchScalarGridSpec(
@@ -287,12 +297,12 @@
             + [pl.BlockSpec((rows, DH), lambda j, at: (0, 0))] * len(others),
             out_specs=(
                 pl.BlockSpec((rows, width), lambda j, at: (0, 0)),
-                pl.BlockSpec((rows, DH), lambda j, at: (0, 0)),
+                pl.BlockSpec(stat, lambda j, at: (0, 0)),
             ),
         ),
         out_shape=(
             jax.ShapeDtypeStruct((rows, width), f32),
-            jax.ShapeDtypeStruct((rows, DH), f32),
+            jax.ShapeDtypeStruct(stat, f32),
         ),
         compiler_params=params(),
         cost_estimate=LIGHT,
@@ -324,7 +334,7 @@
     return pl.pallas_call(
         functools.partial(gate_kernel, len(stats), len(atts)),
         grid=(1,),
-        in_specs=[pl.BlockSpec((rows, DH), lambda j: (0, 0))] * len(stats)
+        in_specs=[pl.BlockSpec(s.shape, lambda j: (0, 0)) for s in stats]
         + [pl.BlockSpec((rows, a.shape[1]), lambda j: (0, 0)) for a in atts]
         + [pl.BlockSpec((1, rows, r.shape[2]), lambda j: (2, 0, 0)) for r in rests],
         out_specs=[pl.BlockSpec((rows // chunks, width), lambda j: (0, 0))] * chunks,
@@ -355,10 +365,10 @@
             into[k % half, p] = sums[first:first + piece]
 
 
-def output(index, blocks, w_out, slots, after):
+def output(index, blocks, w_out, slots, column, columns, after):
     owners, (each, width) = len(blocks), blocks[0].shape
     zs = len(slots)
-    piece, columns = each // zs, w_out.shape[1]
+    piece = each // zs
     span = 512 if columns % 512 == 0 else columns
     row_spec = pl.BlockSpec((zs, piece, width), lambda j, at: (0, 0, 0))
     spec = pl.BlockSpec((zs // 2, owners, piece, span), lambda j, at: (0, 0, 0, j))
@@ -369,7 +379,7 @@
             num_scalar_prefetch=1,
             grid=(columns // span,),
             in_specs=[row_spec] * owners
-            + [pl.BlockSpec((width, span), lambda j, at: (0, j))]
+            + [pl.BlockSpec((width, span), lambda j, at: (0, column // span + j))]
             + anywhere(after),
             out_specs=(spec, spec),
             scratch_shapes=[pltpu.VMEM((owners * each, width), bf16)],
@@ -380,35 +390,39 @@
         name="output",
     )(
         index.reshape(1).astype(jnp.int32),
-        *[b.reshape(zs, piece, width) for b in blocks], w_out, *after,
+        *[b.reshape(zs, piece, width) for b in blocks], far(w_out), *after,
     )
 
 
 def close_kernel(counts, at_ref, t_ref, *refs):
     out_ref, first = refs[-1], 0
     owners = refs[0].shape[1]
-    for r, count in enumerate(counts):
-        terms = refs[first:first + count]
-        first += count
-        for p in range(owners):
-            total = t_ref[r * owners + p].astype(f32)
-            for term in terms:
-                total = total + term[0, p ^ at_ref[0]].astype(f32)
-            out_ref[r * owners + p] = total.astype(bf16)
+    for r, row in enumerate(counts):
+        column = 0
+        for count in row:
+            terms = refs[first:first + count]
+            first += count
+            span = terms[0].shape[-1]
+            for p in range(owners):
+                total = t_ref[r * owners + p, :, column:column + span].astype(f32)
+                for term in terms:
+                    total = total + term[0, p ^ at_ref[0]].astype(f32)
+                out_ref[r * owners + p, :, column:column + span] = total.astype(bf16)
+            column += span
 
 
 def close(place, index, tokens, chunks):
-    _, owners, piece, width = chunks[0][0].shape
-    blocks, span = len(chunks) * owners, width // 2
-    term = pl.BlockSpec((1, owners, piece, span), lambda j, at: (0, 0, 0, j))
-    return pl.pallas_call(
-        functools.partial(close_kernel, [len(terms) for terms in chunks]),
+    _, owners, piece, _ = chunks[0][0][0].shape
+    blocks, width = len(chunks) * owners, sum(terms[0].shape[-1] for terms in chunks[0])
+    flat = [term for row in chunks for terms in row for term in terms]
+    return pl.pallas_call(
+        functools.partial(close_kernel, [[len(terms) for terms in row] for row in chunks]),
         grid_spec=pltpu.PrefetchScalarGridSpec(
             num_scalar_prefetch=1,
-            grid=(2,),
-            in_specs=[pl.BlockSpec((blocks, piece, span), lambda j, at: (at[1], 0, j))]
-            + [term] * sum(len(terms) for terms in chunks),
-            out_specs=pl.BlockSpec((blocks, piece, span), lambda j, at: (0, 0, j)),
+            grid=(1,),
+            in_specs=[pl.BlockSpec((blocks, piece, width), lambda j, at: (at[1], 0, 0))]
+            + [pl.BlockSpec((1,) + t.shape[1:], lambda j, at: (0, 0, 0, 0)) for t in flat],
+            out_specs=pl.BlockSpec((blocks, piece, width), lambda j, at: (0, 0, 0)),
         ),
         out_shape=jax.ShapeDtypeStruct((blocks, piece, width), bf16),
         compiler_params=params(),
@@ -416,8 +430,8 @@
         name="close",
     )(
         jnp.stack([place, index]).astype(jnp.int32),
-        tokens.reshape(-1, piece, width),
-        *[term for terms in chunks for term in terms],
+        far(tokens.reshape(-1, piece, width)),
+        *flat,
     )
 
 
@@ -467,7 +481,7 @@
     if heads % 8:
         return [1] * heads
     unit = heads // 8
-    return [unit, 2 * unit, 2 * unit, 2 * unit, unit]
+    return [unit, 2 * unit, 2 * unit, 3 * unit]
 
 
 def local(tokens, w_qkvu, k_cache, v_cache, w_out, vis_start, vis_end):
@@ -502,22 +516,31 @@
         after = keeps[-1:]
         if c >= 2:
             after = after + [sent[c - 2]]
+        if c >= 3:
+            after = after + [parts[c - 3][0]]
         keep, send = project(at, ordered, w_qkvu, firsts[c], sizes[c], after)
         keeps.append(keep)
         before = [terms_of[c - 1][1]] if c >= 1 else []
         if c >= 2:
             before = before + [terms_of[c - 2][-1]]
+        if c >= 3:
+            before = before + queries[c - 3][1:2]
         send = tie(send, before)
         terms, out = scatter(keep, send, "hist")
         sent.append(out)
         terms_of.append(terms)
 
-    waits = []
+    waits, queries = [], []
+
+    def middle_first(c):
+        after = waits[-1:] + (atts[:-1] if c == last else [])
+        parts.append(activate(terms_of[c], after))
+        queries.append(gather(parts[c][0], "hist"))
 
     def middle(c):
-        query, rest = activate(terms_of[c], waits[-1:] + (atts[c - 2:c - 1] if c >= 2 else []))
-        parts.append((query, rest))
-        keep, send = attend(at, gather(query, "hist"), k_cache, v_cache, edges, firsts[c])
+        query, rest = parts[c]
+        after = atts[-1:] if c == last else []
+        keep, send = attend(at, queries[c], k_cache, v_cache, edges, firsts[c], after)
         waits.append(keep)
         sums, _ = scatter(keep, send, "hist")
         others = stats if c == last else []
@@ -528,26 +551,37 @@
 
     for c in range(len(sizes)):
         front(c)
-        if c >= 2:
-            middle(c - 2)
-    for c in range(max(0, len(sizes) - 2), len(sizes)):
+        if c == 2:
+            middle_first(0)
+    for c in range(len(sizes)):
+        if c == len(parts):
+            middle_first(c)
         middle(c)
 
     gated = gate_rows(all_stats(stats[-1], "head"), atts, [rest for _, rest in parts], chunks)
-    results, after = [], []
+    columns = w_out.shape[1]
+    straight = piece % 16 == 0 and zs & (zs - 1) == 0
+    groups = 2 if straight and columns % 1024 == 0 else 1
+    results, sends, first_steps, ends = [], [], [], []
     for rows in gated:
         blocks = gather(rows, "hist")
-        if piece % 16 == 0 and zs & (zs - 1) == 0:
-            slots = [reverse(k, bits_of("head")) for k in range(zs)]
-            keep, send = output(index, blocks, w_out, slots, [])
-            send = tie(send, after)
-            terms, _ = scatter(keep, send, "head")
-            after = [terms[1]]
-            results.append(terms)
-        else:
-            whole = jnp.dot(jnp.concatenate(blocks), w_out, preferred_element_type=f32)
-            whole = whole.astype(bf16).reshape(owners, zs, piece, -1).swapaxes(0, 1)
-            results.append([lax.psum_scatter(whole, "head", scatter_dimension=0, tiled=True)])
+        results.append([])
+        for g in range(groups):
+            if straight:
+                slots = [reverse(k, bits_of("head")) for k in range(zs)]
+                span = columns // groups
+                keep, send = output(index, blocks, w_out, slots, g * span, span, sends[-1:])
+                before = first_steps[-2:-1] + ends[-3:-2]
+                send = tie(send, before)
+                sends.append(send)
+                terms, _ = scatter(keep, send, "head")
+                first_steps.append(terms[1])
+                ends.append(terms[-1])
+            else:
+                whole = jnp.dot(jnp.concatenate(blocks), w_out, preferred_element_type=f32)
+                whole = whole.astype(bf16).reshape(owners, zs, piece, -1).swapaxes(0, 1)
+                terms = [lax.psum_scatter(whole, "head", scatter_dimension=0, tiled=True)]
+            results[-1].append(terms)
     out = close(place, index, tokens, results)
     return out.reshape(cand // zs, -1)
 

time: 204 us -> 200 us (0.980)
  local copies, waits for them, and re-layouts: 20.9 us -> 5.4 us
  Pallas kernels: 62.1 us -> 74.1 us
    unnamed x56 -> x20, local copies, waits for them, and re-layouts: 19.8 us -> 3.55 us
    pallas_call x2 -> x4, Pallas kernels: 7.33 us -> 12.5 us  [output(): pl.pallas_call(functools.partial(output_kernel, owners, slots), grid_spec...]
    pallas_call x5 -> x4, Pallas kernels: 8.91 us -> 12.6 us  [attend(): pl.pallas_call(functools.partial(attend_kernel, owners), grid_spec=pltpu....]
    ppermute x3, waiting for transfers between devices: 5.19 us -> 2.26 us  [all_stats(): lax.ppermute(stat, axis, [(i, (i + k) % count) for i in range(count)])]
    ppermute x45 -> x42, waiting for transfers between devices: 85.2 us -> 86.7 us  [swap(): lax.ppermute(x, axis, [(i, i ^ 1 << bit) for i in range(lax.axis_size(axi...]
    pallas_call x5 -> x4, Pallas kernels: 34.5 us -> 35.5 us  [project(): pl.pallas_call(functools.partial(project_kernel, parts, owners, len(after...]
    ppermute x45 -> x42, starting transfers between devices: 23.1 us -> 23.3 us  [swap(): lax.ppermute(x, axis, [(i, i ^ 1 << bit) for i in range(lax.axis_size(axi...]
  transfers between devices with their start and end apart: 48 -> 45, of which waited for: 23 -> 20; matrix products, arithmetic and copies ran while one was open for 1% -> 2% of each run, Pallas kernels for 27% -> 30%
where the time goes in v6:
time: 200 us; the launch traced here: 199 us
  waiting for transfers between devices  89 us (44%)
  Pallas kernels  74.1 us (37%)
  starting transfers between devices  28.9 us (14%)
  local copies, waits for them, and re-layouts  5.4 us (3%)
    ppermute x42, waiting for transfers between devices, swap(): lax.ppermute(x, axis, [(i, i ^ 1 << bit) for i in range(lax.axis_size(axi...  86.7 us
    pallas_call x4, Pallas kernels, project(): pl.pallas_call(functools.partial(project_kernel, parts, owners, len(after...  35.5 us
    ppermute x42, starting transfers between devices, swap(): lax.ppermute(x, axis, [(i, i ^ 1 << bit) for i in range(lax.axis_size(axi...  23.3 us
    pallas_call x4, Pallas kernels, attend(): pl.pallas_call(functools.partial(attend_kernel, owners), grid_spec=pltpu....  12.6 us
    pallas_call x4, Pallas kernels, output(): pl.pallas_call(functools.partial(output_kernel, owners, slots), grid_spec...  12.5 us
    ppermute x3, starting transfers between devices, all_stats(): lax.ppermute(stat, axis, [(i, (i + k) % count) for i in range(count)])  5.54 us
    pallas_call x12, Pallas kernels, fold(): pl.pallas_call(fold_kernel, grid=(steps,), in_specs=[pl.BlockSpec(block,...  4.55 us
  transfers between devices with their start and end apart: 45, of which 20 were waited for; matrix products, arithmetic and copies ran while one was open for 2% of the time, Pallas kernels for 30%

profile of v6, /device:TPU:0, one launch (start us, length us, event | category | flops | bytes accessed | tf_op | source)
XLA Modules:
  0.0 199.1 jit_solution(12072992598518241893)
XLA Ops:
  0.0 5.5 %project.4 = (bf16[2,4,128,256]{3,2,1,0:T(8,128)(2,1)S(1)}, bf16[2,4,128,256]{3,2,1,0:T(8,128)(2,1)S(1)}) custom-call(s32[1]{0:T(128)} %bitcast.at_ref, bf16[4,2,4,16,2048]{4,3,2,1,0:T(8,128)(2,1)} %bitcast.29, bf16[4,2,4,16,2048]{4,3,2,1,0:T(8,128)(2,1)} %bitcast.30, bf16[4,2,4,16,2048]{4,3,2,1,0:T(8,128)(2,1)} %bitcast.31, ...), custom_call_target="tpu_custom_call" | custom-call | flops 1000 | bytes 1000 | tf_op jit(solution)/shard_map/project/pallas_call | solution.py:76
  6.1 8.7 %project.5 = (bf16[2,4,128,512]{3,2,1,0:T(8,128)(2,1)S(1)}, bf16[2,4,128,512]{3,2,1,0:T(8,128)(2,1)S(1)}) custom-call(s32[1]{0:T(128)} %bitcast.at_ref, bf16[4,2,4,16,2048]{4,3,2,1,0:T(8,128)(2,1)} %bitcast.33, bf16[4,2,4,16,2048]{4,3,2,1,0:T(8,128)(2,1)} %bitcast.34, bf16[4,2,4,16,2048]{4,3,2,1,0:T(8,128)(2,1)} %bitcast.35, ...), custom_call_target="tpu_custom_call" | custom-call | flops 1000 | bytes 1000 | tf_op jit(solution)/shard_map/project/pallas_call | solution.py:76
  15.2 3.0 %collective-permute-start.2 = (bf16[1,4,128,256]{3,2,1,0:T(8,128)(2,1)S(1)}, bf16[1,4,128,256]{3,2,1,0:T(8,128)(2,1)S(1)}, u32[]{:S(2)}, u32[]{:S(2)}) collective-permute-start(bf16[1,4,128,256]{3,2,1,0:T(8,128)(2,1)S(1)} %fold.12.refs_9_), channel_id=1, source_target_pairs={{0,2},{1,3},{2,0},{3,1},{4,6},{5,7},{6,4},{7,5},{8,10},{9,11},{10,... | collective-permute-start | bytes 786440 | tf_op jit(solution)/shard_map/ppermute | solution.py:449
  18.2 8.7 %project.6 = (bf16[2,4,128,512]{3,2,1,0:T(8,128)(2,1)S(1)}, bf16[2,4,128,512]{3,2,1,0:T(8,128)(2,1)S(1)}) custom-call(s32[1]{0:T(128)} %bitcast.at_ref, bf16[4,2,4,16,2048]{4,3,2,1,0:T(8,128)(2,1)} %bitcast.37, bf16[4,2,4,16,2048]{4,3,2,1,0:T(8,128)(2,1)} %bitcast.38, bf16[4,2,4,16,2048]{4,3,2,1,0:T(8,128)(2,1)} %bitcast.39, ...), custom_call_target="tpu_custom_call" | custom-call | flops 1000 | bytes 1000 | tf_op jit(solution)/shard_map/project/pallas_call | solution.py:76
  27.7 2.0 collective-permute-start.5
  29.7 12.5 %project.7 = (bf16[2,4,128,768]{3,2,1,0:T(8,128)(2,1)S(1)}, bf16[2,4,128,768]{3,2,1,0:T(8,128)(2,1)}) custom-call(s32[1]{0:T(128)} %bitcast.at_ref, bf16[4,2,4,16,2048]{4,3,2,1,0:T(8,128)(2,1)} %bitcast.41, bf16[4,2,4,16,2048]{4,3,2,1,0:T(8,128)(2,1)} %bitcast.42, bf16[4,2,4,16,2048]{4,3,2,1,0:T(8,128)(2,1)} %bitcast.43, ...), custom_call_target="tpu_custom_call" | custom-call | flops 1000 | bytes 1000 | tf_op jit(solution)/shard_map/project/pallas_call | solution.py:76
  42.2 1.2 copy-done.3
  44.5 1.2 copy-done.1
  45.8 0.9 fold.15
  47.0 1.3 collective-permute-done.6.refs_1_
  48.3 2.1 %fold.14 = bf16[1,4,128,768]{3,2,1,0:T(8,128)(2,1)} custom-call(bf16[2,4,128,768]{3,2,1,0:T(8,128)(2,1)S(1)} %copy-done.4, bf16[2,4,128,768]{3,2,1,0:T(8,128)(2,1)} %collective-permute-done.6.refs_1_), custom_call_target="tpu_custom_call" | custom-call | flops 1000 | bytes 1000 | tf_op jit(solution)/shard_map/fold/pallas_call | solution.py:131
  53.2 1.2 pad_add_fusion.refs_4_.refs_5_.refs_6_.refs_7_.edge_ref
  54.4 2.1 %attend.4 = (bf16[2,128,256]{2,1,0:T(8,128)(2,1)S(1)}, bf16[2,128,256]{2,1,0:T(8,128)(2,1)S(1)}) custom-call(s32[1]{0:T(128)} %bitcast.at_ref, bf16[128,256]{1,0:T(8,128)(2,1)S(1)} %get-tuple-element.52.refs_10_.refs_0_.q_ref, bf16[128,256]{1,0:T(8,128)(2,1)S(1)} %collective-permute-done.5.refs_3_.refs_1_, ...), custom_call_target="tpu_custom_call" | custom-call | flops 1000 | bytes 1000 | tf_op jit(solution)/shard_map/attend/pallas_call | solution.py:220
  56.8 1.6 collective-permute-start.11
  58.5 22.5 %collective-permute-done.11.refs_1_ = bf16[128,512]{1,0:T(8,128)(2,1)S(1)} collective-permute-done((bf16[128,512]{1,0:T(8,128)(2,1)S(1)}, bf16[128,512]{1,0:T(8,128)(2,1)S(1)}, u32[]{:S(2)}, u32[]{:S(2)}) %collective-permute-start.11) | collective-permute-done | bytes 131104 | tf_op jit(solution)/shard_map/ppermute | solution.py:449
  80.9 1.3 collective-permute-done.13.refs_3_
  82.3 3.1 %attend.5 = (bf16[2,128,512]{2,1,0:T(8,128)(2,1)S(1)}, bf16[2,128,512]{2,1,0:T(8,128)(2,1)S(1)}) custom-call(s32[1]{0:T(128)} %bitcast.at_ref, bf16[128,512]{1,0:T(8,128)(2,1)S(1)} %get-tuple-element.57.refs_0_.q_ref, bf16[128,512]{1,0:T(8,128)(2,1)S(1)} %collective-permute-done.11.refs_1_, bf16[128,512]{1,0:T(8,128)(2,1)S(1)} %collective-permute-done.12.refs_2_, ...), custom_call_target="tpu_custom_call" | custom-call | flops 1000 | bytes 1000 | tf_op jit(solution)/shard_map/attend/pallas_call | solution.py:220
  85.6 1.4 activate.6
  87.6 1.7 collective-permute-start.20
  89.5 3.9 %collective-permute-done.14.refs_1_ = bf16[128,512]{1,0:T(8,128)(2,1)S(1)} collective-permute-done((bf16[128,512]{1,0:T(8,128)(2,1)S(1)}, bf16[128,512]{1,0:T(8,128)(2,1)S(1)}, u32[]{:S(2)}, u32[]{:S(2)}) %collective-permute-start.14) | collective-permute-done | bytes 131104 | tf_op jit(solution)/shard_map/ppermute | solution.py:449
  93.8 4.2 %collective-permute-done.18.refs_2_ = bf16[1,128,256]{2,1,0:T(8,128)(2,1)S(1)} collective-permute-done((bf16[1,128,256]{2,1,0:T(8,128)(2,1)S(1)}, bf16[1,128,256]{2,1,0:T(8,128)(2,1)S(1)}, u32[]{:S(2)}, u32[]{:S(2)}) %collective-permute-start.18) | collective-permute-done | bytes 65568 | tf_op jit(solution)/shard_map/ppermute | solution.py:449
  98.9 3.3 %attend.6 = (bf16[2,128,512]{2,1,0:T(8,128)(2,1)S(1)}, bf16[2,128,512]{2,1,0:T(8,128)(2,1)S(1)}) custom-call(s32[1]{0:T(128)} %bitcast.at_ref, bf16[128,512]{1,0:T(8,128)(2,1)S(1)} %get-tuple-element.59.refs_0_.q_ref, bf16[128,512]{1,0:T(8,128)(2,1)S(1)} %collective-permute-done.14.refs_1_, bf16[128,512]{1,0:T(8,128)(2,1)S(1)} %collective-permute-done.15.refs_2_, ...), custom_call_target="tpu_custom_call" | custom-call | flops 1000 | bytes 1000 | tf_op jit(solution)/shard_map/attend/pallas_call | solution.py:220
  102.3 1.9 activate.7
  104.7 6.7 %collective-permute-done.21.refs_1_ = bf16[128,768]{1,0:T(8,128)(2,1)S(1)} collective-permute-done((bf16[128,768]{1,0:T(8,128)(2,1)S(1)}, bf16[128,768]{1,0:T(8,128)(2,1)S(1)}, u32[]{:S(2)}, u32[]{:S(2)}) %collective-permute-start.21) | collective-permute-done | bytes 196640 | tf_op jit(solution)/shard_map/ppermute | solution.py:449
  112.0 5.6 %collective-permute-done.25.refs_2_ = bf16[1,128,512]{2,1,0:T(8,128)(2,1)S(1)} collective-permute-done((bf16[1,128,512]{2,1,0:T(8,128)(2,1)S(1)}, bf16[1,128,512]{2,1,0:T(8,128)(2,1)S(1)}, u32[]{:S(2)}, u32[]{:S(2)}) %collective-permute-start.25) | collective-permute-done | bytes 131104 | tf_op jit(solution)/shard_map/ppermute | solution.py:449
  118.0 4.2 %attend.7 = (bf16[2,128,768]{2,1,0:T(8,128)(2,1)S(1)}, bf16[2,128,768]{2,1,0:T(8,128)(2,1)S(1)}) custom-call(s32[1]{0:T(128)} %bitcast.at_ref, bf16[128,768]{1,0:T(8,128)(2,1)S(1)} %get-tuple-element.67.refs_0_.q_ref, bf16[128,768]{1,0:T(8,128)(2,1)S(1)} %collective-permute-done.21.refs_1_, bf16[128,768]{1,0:T(8,128)(2,1)S(1)} %collective-permute-done.22.refs_2_, ...), custom_call_target="tpu_custom_call" | custom-call | flops 1000 | bytes 1000 | tf_op jit(solution)/shard_map/attend/pallas_call | solution.py:220
  122.3 1.7 collective-permute-done.26.refs_1_
  124.6 6.6 %collective-permute-done.27.refs_2_ = bf16[1,128,768]{2,1,0:T(8,128)(2,1)S(1)} collective-permute-done((bf16[1,128,768]{2,1,0:T(8,128)(2,1)S(1)}, bf16[1,128,768]{2,1,0:T(8,128)(2,1)S(1)}, u32[]{:S(2)}, u32[]{:S(2)}) %collective-permute-start.27) | collective-permute-done | bytes 196640 | tf_op jit(solution)/shard_map/ppermute | solution.py:449
  132.1 1.6 collective-permute-start.28
  133.7 2.6 %collective-permute-start.29 = (f32[8,128]{1,0:T(8,128)S(1)}, f32[8,128]{1,0:T(8,128)S(1)}, u32[]{:S(2)}, u32[]{:S(2)}) collective-permute-start(f32[8,128]{1,0:T(8,128)S(1)} %get-tuple-element.77.refs_0_), channel_id=1, source_target_pairs={{0,8},{4,12},{8,0},{12,4},{1,9},{5,13},{9,1},{13,5},{2,10},{6,14},... | collective-permute-start | bytes 12296 | tf_op jit(solution)/shard_map/ppermute | solution.py:475
  136.3 1.3 collective-permute-start.30
  138.2 1.7 collective-permute-done.30.refs_3_
  140.9 5.8 %collective-permute-done.31 = bf16[64,2048]{1,0:T(8,128)(2,1)S(1)} collective-permute-done((bf16[64,2048]{1,0:T(8,128)(2,1)S(1)}, bf16[64,2048]{1,0:T(8,128)(2,1)S(1)}, u32[]{:S(2)}, u32[]{:S(2)}) %collective-permute-start.31) | collective-permute-done | bytes 262176 | tf_op jit(solution)/shard_map/ppermute | solution.py:449
  147.3 1.0 collective-permute-done.33
  148.3 3.1 %output.4 = (bf16[2,4,16,1024]{3,2,1,0:T(8,128)(2,1)S(1)}, bf16[2,4,16,1024]{3,2,1,0:T(8,128)(2,1)S(1)}) custom-call(s32[1]{0:T(128)} %bitcast.1.index_ref, bf16[4,16,2048]{2,1,0:T(8,128)(2,1)S(1)} %bitcast.15, bf16[4,16,2048]{2,1,0:T(8,128)(2,1)S(1)} %bitcast.19, bf16[4,16,2048]{2,1,0:T(8,128)(2,1)S(1)} %bitcast.21, bf16[4,16,2048]{2,1,0:T(8,128)(2,1)S(1)} %bitcast.25, ...), custom_call_target="tpu_custom_call" | custom-call | flops 1000 | bytes 1000 | tf_op jit(solution)/shard_map/output/pallas_call | solution.py:376
  151.7 3.8 %collective-permute-done.38 = bf16[64,2048]{1,0:T(8,128)(2,1)S(1)} collective-permute-done((bf16[64,2048]{1,0:T(8,128)(2,1)S(1)}, bf16[64,2048]{1,0:T(8,128)(2,1)S(1)}, u32[]{:S(2)}, u32[]{:S(2)}) %collective-permute-start.38) | collective-permute-done | bytes 262176 | tf_op jit(solution)/shard_map/ppermute | solution.py:449
  155.5 3.1 %output.5 = (bf16[2,4,16,1024]{3,2,1,0:T(8,128)(2,1)S(1)}, bf16[2,4,16,1024]{3,2,1,0:T(8,128)(2,1)S(1)}) custom-call(s32[1]{0:T(128)} %bitcast.1.index_ref, bf16[4,16,2048]{2,1,0:T(8,128)(2,1)S(1)} %bitcast.16, bf16[4,16,2048]{2,1,0:T(8,128)(2,1)S(1)} %bitcast.20, bf16[4,16,2048]{2,1,0:T(8,128)(2,1)S(1)} %bitcast.22, bf16[4,16,2048]{2,1,0:T(8,128)(2,1)S(1)} %bitcast.26, ...), custom_call_target="tpu_custom_call" | custom-call | flops 1000 | bytes 1000 | tf_op jit(solution)/shard_map/output/pallas_call | solution.py:376
  160.0 2.6 %collective-permute-start.35 = (bf16[1,4,16,1024]{3,2,1,0:T(8,128)(2,1)S(1)}, bf16[1,4,16,1024]{3,2,1,0:T(8,128)(2,1)S(1)}, u32[]{:S(2)}, u32[]{:S(2)}) collective-permute-start(bf16[1,4,16,1024]{3,2,1,0:T(8,128)(2,1)S(1)} %fold.20), channel_id=1, source_target_pairs={{0,8},{4,12},{8,0},{12,4},{1,9},{5,13},{9,1},{13,5},{2,10},{6,14},... | collective-permute-start | bytes 393224 | tf_op jit(solution)/shard_map/ppermute | solution.py:449
  162.6 3.1 %output.6 = (bf16[2,4,16,1024]{3,2,1,0:T(8,128)(2,1)S(1)}, bf16[2,4,16,1024]{3,2,1,0:T(8,128)(2,1)S(1)}) custom-call(s32[1]{0:T(128)} %bitcast.1.index_ref, bf16[4,16,2048]{2,1,0:T(8,128)(2,1)S(1)} %bitcast.13, bf16[4,16,2048]{2,1,0:T(8,128)(2,1)S(1)} %bitcast.17, bf16[4,16,2048]{2,1,0:T(8,128)(2,1)S(1)} %bitcast.23, bf16[4,16,2048]{2,1,0:T(8,128)(2,1)S(1)} %bitcast.27, ...), custom_call_target="tpu_custom_call" | custom-call | flops 1000 | bytes 1000 | tf_op jit(solution)/shard_map/output/pallas_call | solution.py:376
  165.7 3.2 %output.7 = (bf16[2,4,16,1024]{3,2,1,0:T(8,128)(2,1)S(1)}, bf16[2,4,16,1024]{3,2,1,0:T(8,128)(2,1)S(1)}) custom-call(s32[1]{0:T(128)} %bitcast.1.index_ref, bf16[4,16,2048]{2,1,0:T(8,128)(2,1)S(1)} %bitcast.14, bf16[4,16,2048]{2,1,0:T(8,128)(2,1)S(1)} %bitcast.18, bf16[4,16,2048]{2,1,0:T(8,128)(2,1)S(1)} %bitcast.24, bf16[4,16,2048]{2,1,0:T(8,128)(2,1)S(1)} %bitcast.28, ...), custom_call_target="tpu_custom_call" | custom-call | flops 1000 | bytes 1000 | tf_op jit(solution)/shard_map/output/pallas_call | solution.py:376
  168.9 1.2 collective-permute-start.41
  170.2 2.1 %collective-permute-start.43 = (bf16[2,4,16,1024]{3,2,1,0:T(8,128)(2,1)S(1)}, bf16[2,4,16,1024]{3,2,1,0:T(8,128)(2,1)S(1)}, u32[]{:S(2)}, u32[]{:S(2)}) collective-permute-start(bf16[2,4,16,1024]{3,2,1,0:T(8,128)(2,1)S(1)} %tie.9), channel_id=1, source_target_pairs={{0,4},{4,0},{8,12},{12,8},{1,5},{5,1},{9,13},{13,9},{2,6},{6,2},{1... | collective-permute-start | bytes 786440 | tf_op jit(solution)/shard_map/ppermute | solution.py:449
  172.5 2.0 %collective-permute-start.37 = (bf16[1,4,16,1024]{3,2,1,0:T(8,128)(2,1)S(1)}, bf16[1,4,16,1024]{3,2,1,0:T(8,128)(2,1)S(1)}, u32[]{:S(2)}, u32[]{:S(2)}) collective-permute-start(bf16[1,4,16,1024]{3,2,1,0:T(8,128)(2,1)S(1)} %fold.21), channel_id=1, source_target_pairs={{0,8},{4,12},{8,0},{12,4},{1,9},{5,13},{9,1},{13,5},{2,10},{6,14},... | collective-permute-start | bytes 393224 | tf_op jit(solution)/shard_map/ppermute | solution.py:449
  174.5 6.5 %collective-permute-done.41.refs_1_.refs_7_ = bf16[2,4,16,1024]{3,2,1,0:T(8,128)(2,1)S(1)} collective-permute-done((bf16[2,4,16,1024]{3,2,1,0:T(8,128)(2,1)S(1)}, bf16[2,4,16,1024]{3,2,1,0:T(8,128)(2,1)S(1)}, u32[]{:S(2)}, u32[]{:S(2)}) %collective-permute-start.41) | collective-permute-done | bytes 262176 | tf_op jit(solution)/shard_map/ppermute | solution.py:449
  181.2 4.9 %collective-permute-done.43.refs_1_.refs_10_ = bf16[2,4,16,1024]{3,2,1,0:T(8,128)(2,1)S(1)} collective-permute-done((bf16[2,4,16,1024]{3,2,1,0:T(8,128)(2,1)S(1)}, bf16[2,4,16,1024]{3,2,1,0:T(8,128)(2,1)S(1)}, u32[]{:S(2)}, u32[]{:S(2)}) %collective-permute-start.43) | collective-permute-done | bytes 262176 | tf_op jit(solution)/shard_map/ppermute | solution.py:449
  186.6 7.6 %collective-permute-done.42.refs_8_ = bf16[1,4,16,1024]{3,2,1,0:T(8,128)(2,1)S(1)} collective-permute-done((bf16[1,4,16,1024]{3,2,1,0:T(8,128)(2,1)S(1)}, bf16[1,4,16,1024]{3,2,1,0:T(8,128)(2,1)S(1)}, u32[]{:S(2)}, u32[]{:S(2)}) %collective-permute-start.42) | collective-permute-done | bytes 131104 | tf_op jit(solution)/shard_map/ppermute | solution.py:449
  194.2 2.2 %collective-permute-done.44.refs_11_ = bf16[1,4,16,1024]{3,2,1,0:T(8,128)(2,1)S(1)} collective-permute-done((bf16[1,4,16,1024]{3,2,1,0:T(8,128)(2,1)S(1)}, bf16[1,4,16,1024]{3,2,1,0:T(8,128)(2,1)S(1)}, u32[]{:S(2)}, u32[]{:S(2)}) %collective-permute-start.44) | collective-permute-done | bytes 131104 | tf_op jit(solution)/shard_map/ppermute | solution.py:449
  196.4 2.6 %close.1 = bf16[8,16,2048]{2,1,0:T(8,128)(2,1)} custom-call(s32[2]{0:T(128)S(1)} %pad_add_fusion.1.at_ref, bf16[32,16,2048]{2,1,0:T(8,128)(2,1)} %bitcast.45, bf16[2,4,16,1024]{3,2,1,0:T(8,128)(2,1)S(1)} %get-tuple-element.80.refs_0_, bf16[2,4,16,1024]{3,2,1,0:T(8,128)(2,1)S(1)} %collective-permute-done.34.refs_1_, ...), custom_call_target="tpu_custom_call" | custom-call | flops 1000 | bytes 1000 | tf_op jit(solution)/shard_map/close/pallas_call | solution.py:418
  (106 shorter events, 16.3 us)
Async XLA Ops:
  5.5 9.3 %collective-permute-start = (bf16[2,4,128,256]{3,2,1,0:T(8,128)(2,1)S(1)}, bf16[2,4,128,256]{3,2,1,0:T(8,128)(2,1)S(1)}, u32[]{:S(2)}, u32[]{:S(2)}) collective-permute-start(bf16[2,4,128,256]{3,2,1,0:T(8,128)(2,1)S(1)} %get-tuple-element.49), channel_id=1, source_target_pairs={{0,1},{1,0},{2,3},{3,2},{4,5},{5,4},{6,7},{7,6},{8,9},{9,8},{10,11... | collective-permute-start | bytes 1572872 | tf_op jit(solution)/shard_map/ppermute | solution.py:449
  14.8 12.1 %collective-permute-start.1 = (bf16[2,4,128,512]{3,2,1,0:T(8,128)(2,1)S(1)}, bf16[2,4,128,512]{3,2,1,0:T(8,128)(2,1)S(1)}, u32[]{:S(2)}, u32[]{:S(2)}) collective-permute-start(bf16[2,4,128,512]{3,2,1,0:T(8,128)(2,1)S(1)} %tie.5), channel_id=1, source_target_pairs={{0,1},{1,0},{2,3},{3,2},{4,5},{5,4},{6,7},{7,6},{8,9},{9,8},{10,11... | collective-permute-start | bytes 3145736 | tf_op jit(solution)/shard_map/ppermute | solution.py:449
  15.2 11.7 %collective-permute-start.2 = (bf16[1,4,128,256]{3,2,1,0:T(8,128)(2,1)S(1)}, bf16[1,4,128,256]{3,2,1,0:T(8,128)(2,1)S(1)}, u32[]{:S(2)}, u32[]{:S(2)}) collective-permute-start(bf16[1,4,128,256]{3,2,1,0:T(8,128)(2,1)S(1)} %fold.12.refs_9_), channel_id=1, source_target_pairs={{0,2},{1,3},{2,0},{3,1},{4,6},{5,7},{6,4},{7,5},{8,10},{9,11},{10,... | collective-permute-start | bytes 786440 | tf_op jit(solution)/shard_map/ppermute | solution.py:449
  27.0 16.4 %collective-permute-start.3 = (bf16[2,4,128,512]{3,2,1,0:T(8,128)(2,1)S(1)}, bf16[2,4,128,512]{3,2,1,0:T(8,128)(2,1)S(1)}, u32[]{:S(2)}, u32[]{:S(2)}) collective-permute-start(bf16[2,4,128,512]{3,2,1,0:T(8,128)(2,1)S(1)} %tie.6), channel_id=1, source_target_pairs={{0,1},{1,0},{2,3},{3,2},{4,5},{5,4},{6,7},{7,6},{8,9},{9,8},{10,11... | collective-permute-start | bytes 3145736 | tf_op jit(solution)/shard_map/ppermute | solution.py:449
  27.4 16.0 %collective-permute-start.4 = (bf16[1,4,128,512]{3,2,1,0:T(8,128)(2,1)S(1)}, bf16[1,4,128,512]{3,2,1,0:T(8,128)(2,1)S(1)}, u32[]{:S(2)}, u32[]{:S(2)}) collective-permute-start(bf16[1,4,128,512]{3,2,1,0:T(8,128)(2,1)S(1)} %fold.13.refs_9_), channel_id=1, source_target_pairs={{0,2},{1,3},{2,0},{3,1},{4,6},{5,7},{6,4},{7,5},{8,10},{9,11},{10,... | collective-permute-start | bytes 1572872 | tf_op jit(solution)/shard_map/ppermute | solution.py:449
  27.7 15.7 %collective-permute-start.5 = (bf16[128,256]{1,0:T(8,128)(2,1)S(1)}, bf16[128,256]{1,0:T(8,128)(2,1)S(1)}, u32[]{:S(2)}, u32[]{:S(2)}) collective-permute-start(bf16[128,256]{1,0:T(8,128)(2,1)S(1)} %get-tuple-element.52.refs_10_.refs_0_.q_ref), channel_id=1, source_target_pairs={{0,2},{1,3},{2,0},{3,1},{4,6},{5,7},{6,4},{7,5},{8,10},{9,11},{10,... | collective-permute-start | bytes 196616 | tf_op jit(solution)/shard_map/ppermute | solution.py:449
  44.5 3.8 %collective-permute-start.6 = (bf16[2,4,128,768]{3,2,1,0:T(8,128)(2,1)}, bf16[2,4,128,768]{3,2,1,0:T(8,128)(2,1)}, u32[]{:S(2)}, u32[]{:S(2)}) collective-permute-start(bf16[2,4,128,768]{3,2,1,0:T(8,128)(2,1)} %tie.7), channel_id=1, source_target_pairs={{0,1},{1,0},{2,3},{3,2},{4,5},{5,4},{6,7},{7,6},{8,9},{9,8},{10,11... | collective-permute-start | bytes 4718600 | tf_op jit(solution)/shard_map/ppermute | solution.py:449
  46.7 4.1 %copy-start.8 = (s32[512]{0:T(512)S(1)}, s32[512]{0:T(512)}, u32[]{:S(2)}) copy-start(s32[512]{0:T(512)} %param.13) | copy-start | bytes 6148
  46.7 4.1 %copy-start.9 = (s32[512]{0:T(512)S(1)}, s32[512]{0:T(512)}, u32[]{:S(2)}) copy-start(s32[512]{0:T(512)} %param.12) | copy-start | bytes 6148
  46.7 38.9 %collective-permute-start.8 = (bf16[1,4,128,512]{3,2,1,0:T(8,128)(2,1)}, bf16[1,4,128,512]{3,2,1,0:T(8,128)(2,1)}, u32[]{:S(2)}, u32[]{:S(2)}) collective-permute-start(bf16[1,4,128,512]{3,2,1,0:T(8,128)(2,1)} %fold.15), channel_id=1, source_target_pairs={{0,2},{1,3},{2,0},{3,1},{4,6},{5,7},{6,4},{7,5},{8,10},{9,11},{10,... | collective-permute-start | bytes 1572872 | tf_op jit(solution)/shard_map/ppermute | solution.py:449
  50.4 51.9 %collective-permute-start.7 = (bf16[1,4,128,768]{3,2,1,0:T(8,128)(2,1)}, bf16[1,4,128,768]{3,2,1,0:T(8,128)(2,1)}, u32[]{:S(2)}, u32[]{:S(2)}) collective-permute-start(bf16[1,4,128,768]{3,2,1,0:T(8,128)(2,1)} %fold.14), channel_id=1, source_target_pairs={{0,2},{1,3},{2,0},{3,1},{4,6},{5,7},{6,4},{7,5},{8,10},{9,11},{10,... | collective-permute-start | bytes 2359304 | tf_op jit(solution)/shard_map/ppermute | solution.py:449
  52.7 1.7 collective-permute-start.9
  52.7 1.7 collective-permute-start.10
  56.8 28.8 %copy-start.2 = (bf16[2,4,128,512]{3,2,1,0:T(8,128)(2,1)S(1)}, bf16[2,4,128,512]{3,2,1,0:T(8,128)(2,1)}, u32[]{:S(2)}) copy-start(bf16[2,4,128,512]{3,2,1,0:T(8,128)(2,1)} %copy-done) | copy-start | bytes 3145732
  56.8 24.1 %collective-permute-start.11 = (bf16[128,512]{1,0:T(8,128)(2,1)S(1)}, bf16[128,512]{1,0:T(8,128)(2,1)S(1)}, u32[]{:S(2)}, u32[]{:S(2)}) collective-permute-start(bf16[128,512]{1,0:T(8,128)(2,1)S(1)} %get-tuple-element.57.refs_0_.q_ref), channel_id=1, source_target_pairs={{0,2},{1,3},{2,0},{3,1},{4,6},{5,7},{6,4},{7,5},{8,10},{9,11},{10,... | collective-permute-start | bytes 393224 | tf_op jit(solution)/shard_map/ppermute | solution.py:449
  58.4 22.5 %collective-permute-start.12 = (bf16[128,512]{1,0:T(8,128)(2,1)S(1)}, bf16[128,512]{1,0:T(8,128)(2,1)S(1)}, u32[]{:S(2)}, u32[]{:S(2)}) collective-permute-start(bf16[128,512]{1,0:T(8,128)(2,1)S(1)} %get-tuple-element.57.refs_0_.q_ref), channel_id=1, source_target_pairs={{0,1},{1,0},{2,3},{3,2},{4,5},{5,4},{6,7},{7,6},{8,9},{9,8},{10,11... | collective-permute-start | bytes 393224 | tf_op jit(solution)/shard_map/ppermute | solution.py:449
  80.9 1.3 collective-permute-start.13
  85.4 2.1 %collective-permute-start.19 = (bf16[2,128,512]{2,1,0:T(8,128)(2,1)S(1)}, bf16[2,128,512]{2,1,0:T(8,128)(2,1)S(1)}, u32[]{:S(2)}, u32[]{:S(2)}) collective-permute-start(bf16[2,128,512]{2,1,0:T(8,128)(2,1)S(1)} %get-tuple-element.65), channel_id=1, source_target_pairs={{0,1},{1,0},{2,3},{3,2},{4,5},{5,4},{6,7},{7,6},{8,9},{9,8},{10,11... | collective-permute-start | bytes 786440 | tf_op jit(solution)/shard_map/ppermute | solution.py:449
  87.0 6.4 %collective-permute-start.14 = (bf16[128,512]{1,0:T(8,128)(2,1)S(1)}, bf16[128,512]{1,0:T(8,128)(2,1)S(1)}, u32[]{:S(2)}, u32[]{:S(2)}) collective-permute-start(bf16[128,512]{1,0:T(8,128)(2,1)S(1)} %get-tuple-element.59.refs_0_.q_ref), channel_id=1, source_target_pairs={{0,2},{1,3},{2,0},{3,1},{4,6},{5,7},{6,4},{7,5},{8,10},{9,11},{10,... | collective-permute-start | bytes 393224 | tf_op jit(solution)/shard_map/ppermute | solution.py:449
  87.3 6.0 %collective-permute-start.17 = (bf16[2,128,256]{2,1,0:T(8,128)(2,1)S(1)}, bf16[2,128,256]{2,1,0:T(8,128)(2,1)S(1)}, u32[]{:S(2)}, u32[]{:S(2)}) collective-permute-start(bf16[2,128,256]{2,1,0:T(8,128)(2,1)S(1)} %get-tuple-element.62), channel_id=1, source_target_pairs={{0,1},{1,0},{2,3},{3,2},{4,5},{5,4},{6,7},{7,6},{8,9},{9,8},{10,11... | collective-permute-start | bytes 393224 | tf_op jit(solution)/shard_map/ppermute | solution.py:449
  87.6 10.8 %collective-permute-start.20 = (bf16[1,128,512]{2,1,0:T(8,128)(2,1)S(1)}, bf16[1,128,512]{2,1,0:T(8,128)(2,1)S(1)}, u32[]{:S(2)}, u32[]{:S(2)}) collective-permute-start(bf16[1,128,512]{2,1,0:T(8,128)(2,1)S(1)} %fold.17), channel_id=1, source_target_pairs={{0,2},{1,3},{2,0},{3,1},{4,6},{5,7},{6,4},{7,5},{8,10},{9,11},{10,... | collective-permute-start | bytes 393224 | tf_op jit(solution)/shard_map/ppermute | solution.py:449
  89.3 9.5 %collective-permute-start.15 = (bf16[128,512]{1,0:T(8,128)(2,1)S(1)}, bf16[128,512]{1,0:T(8,128)(2,1)S(1)}, u32[]{:S(2)}, u32[]{:S(2)}) collective-permute-start(bf16[128,512]{1,0:T(8,128)(2,1)S(1)} %get-tuple-element.59.refs_0_.q_ref), channel_id=1, source_target_pairs={{0,1},{1,0},{2,3},{3,2},{4,5},{5,4},{6,7},{7,6},{8,9},{9,8},{10,11... | collective-permute-start | bytes 393224 | tf_op jit(solution)/shard_map/ppermute | solution.py:449
  93.4 5.5 %collective-permute-start.16 = (bf16[128,512]{1,0:T(8,128)(2,1)S(1)}, bf16[128,512]{1,0:T(8,128)(2,1)S(1)}, u32[]{:S(2)}, u32[]{:S(2)}) collective-permute-start(bf16[128,512]{1,0:T(8,128)(2,1)S(1)} %collective-permute-done.14.refs_1_), channel_id=1, source_target_pairs={{0,1},{1,0},{2,3},{3,2},{4,5},{5,4},{6,7},{7,6},{8,9},{9,8},{10,11... | collective-permute-start | bytes 393224 | tf_op jit(solution)/shard_map/ppermute | solution.py:449
  93.5 4.6 %collective-permute-start.18 = (bf16[1,128,256]{2,1,0:T(8,128)(2,1)S(1)}, bf16[1,128,256]{2,1,0:T(8,128)(2,1)S(1)}, u32[]{:S(2)}, u32[]{:S(2)}) collective-permute-start(bf16[1,128,256]{2,1,0:T(8,128)(2,1)S(1)} %fold.16), channel_id=1, source_target_pairs={{0,2},{1,3},{2,0},{3,1},{4,6},{5,7},{6,4},{7,5},{8,10},{9,11},{10,... | collective-permute-start | bytes 196616 | tf_op jit(solution)/shard_map/ppermute | solution.py:449
  102.2 9.3 %collective-permute-start.24 = (bf16[2,128,512]{2,1,0:T(8,128)(2,1)S(1)}, bf16[2,128,512]{2,1,0:T(8,128)(2,1)S(1)}, u32[]{:S(2)}, u32[]{:S(2)}) collective-permute-start(bf16[2,128,512]{2,1,0:T(8,128)(2,1)S(1)} %get-tuple-element.70), channel_id=1, source_target_pairs={{0,1},{1,0},{2,3},{3,2},{4,5},{5,4},{6,7},{7,6},{8,9},{9,8},{10,11... | collective-permute-start | bytes 786440 | tf_op jit(solution)/shard_map/ppermute | solution.py:449
  104.1 7.4 %collective-permute-start.21 = (bf16[128,768]{1,0:T(8,128)(2,1)S(1)}, bf16[128,768]{1,0:T(8,128)(2,1)S(1)}, u32[]{:S(2)}, u32[]{:S(2)}) collective-permute-start(bf16[128,768]{1,0:T(8,128)(2,1)S(1)} %get-tuple-element.67.refs_0_.q_ref), channel_id=1, source_target_pairs={{0,2},{1,3},{2,0},{3,1},{4,6},{5,7},{6,4},{7,5},{8,10},{9,11},{10,... | collective-permute-start | bytes 589832 | tf_op jit(solution)/shard_map/ppermute | solution.py:449
  104.5 13.5 %collective-permute-start.22 = (bf16[128,768]{1,0:T(8,128)(2,1)S(1)}, bf16[128,768]{1,0:T(8,128)(2,1)S(1)}, u32[]{:S(2)}, u32[]{:S(2)}) collective-permute-start(bf16[128,768]{1,0:T(8,128)(2,1)S(1)} %get-tuple-element.67.refs_0_.q_ref), channel_id=1, source_target_pairs={{0,1},{1,0},{2,3},{3,2},{4,5},{5,4},{6,7},{7,6},{8,9},{9,8},{10,11... | collective-permute-start | bytes 589832 | tf_op jit(solution)/shard_map/ppermute | solution.py:449
  111.5 6.6 %collective-permute-start.23 = (bf16[128,768]{1,0:T(8,128)(2,1)S(1)}, bf16[128,768]{1,0:T(8,128)(2,1)S(1)}, u32[]{:S(2)}, u32[]{:S(2)}) collective-permute-start(bf16[128,768]{1,0:T(8,128)(2,1)S(1)} %collective-permute-done.21.refs_1_), channel_id=1, source_target_pairs={{0,1},{1,0},{2,3},{3,2},{4,5},{5,4},{6,7},{7,6},{8,9},{9,8},{10,11... | collective-permute-start | bytes 589832 | tf_op jit(solution)/shard_map/ppermute | solution.py:449
  111.6 6.0 %collective-permute-start.25 = (bf16[1,128,512]{2,1,0:T(8,128)(2,1)S(1)}, bf16[1,128,512]{2,1,0:T(8,128)(2,1)S(1)}, u32[]{:S(2)}, u32[]{:S(2)}) collective-permute-start(bf16[1,128,512]{2,1,0:T(8,128)(2,1)S(1)} %fold.18), channel_id=1, source_target_pairs={{0,2},{1,3},{2,0},{3,1},{4,6},{5,7},{6,4},{7,5},{8,10},{9,11},{10,... | collective-permute-start | bytes 393224 | tf_op jit(solution)/shard_map/ppermute | solution.py:449
  122.3 1.8 collective-permute-start.26
  124.2 7.0 %collective-permute-start.27 = (bf16[1,128,768]{2,1,0:T(8,128)(2,1)S(1)}, bf16[1,128,768]{2,1,0:T(8,128)(2,1)S(1)}, u32[]{:S(2)}, u32[]{:S(2)}) collective-permute-start(bf16[1,128,768]{2,1,0:T(8,128)(2,1)S(1)} %fold.19), channel_id=1, source_target_pairs={{0,2},{1,3},{2,0},{3,1},{4,6},{5,7},{6,4},{7,5},{8,10},{9,11},{10,... | collective-permute-start | bytes 589832 | tf_op jit(solution)/shard_map/ppermute | solution.py:449
  132.1 5.5 %collective-permute-start.28 = (f32[8,128]{1,0:T(8,128)S(1)}, f32[8,128]{1,0:T(8,128)S(1)}, u32[]{:S(2)}, u32[]{:S(2)}) collective-permute-start(f32[8,128]{1,0:T(8,128)S(1)} %get-tuple-element.77.refs_0_), channel_id=1, source_target_pairs={{0,4},{4,8},{8,12},{12,0},{1,5},{5,9},{9,13},{13,1},{2,6},{6,10},{... | collective-permute-start | bytes 12296 | tf_op jit(solution)/shard_map/ppermute | solution.py:475
  133.7 4.5 %collective-permute-start.29 = (f32[8,128]{1,0:T(8,128)S(1)}, f32[8,128]{1,0:T(8,128)S(1)}, u32[]{:S(2)}, u32[]{:S(2)}) collective-permute-start(f32[8,128]{1,0:T(8,128)S(1)} %get-tuple-element.77.refs_0_), channel_id=1, source_target_pairs={{0,8},{4,12},{8,0},{12,4},{1,9},{5,13},{9,1},{13,5},{2,10},{6,14},... | collective-permute-start | bytes 12296 | tf_op jit(solution)/shard_map/ppermute | solution.py:475
  136.3 3.6 %collective-permute-start.30 = (f32[8,128]{1,0:T(8,128)S(1)}, f32[8,128]{1,0:T(8,128)S(1)}, u32[]{:S(2)}, u32[]{:S(2)}) collective-permute-start(f32[8,128]{1,0:T(8,128)S(1)} %get-tuple-element.77.refs_0_), channel_id=1, source_target_pairs={{0,12},{4,0},{8,4},{12,8},{1,13},{5,1},{9,5},{13,9},{2,14},{6,2},{... | collective-permute-start | bytes 12296 | tf_op jit(solution)/shard_map/ppermute | solution.py:475
  140.3 6.4 %collective-permute-start.31 = (bf16[64,2048]{1,0:T(8,128)(2,1)S(1)}, bf16[64,2048]{1,0:T(8,128)(2,1)S(1)}, u32[]{:S(2)}, u32[]{:S(2)}) collective-permute-start(bf16[64,2048]{1,0:T(8,128)(2,1)S(1)} %get-tuple-element.79), channel_id=1, source_target_pairs={{0,2},{1,3},{2,0},{3,1},{4,6},{5,7},{6,4},{7,5},{8,10},{9,11},{10,... | collective-permute-start | bytes 786440 | tf_op jit(solution)/shard_map/ppermute | solution.py:449
  140.9 6.4 %collective-permute-start.32 = (bf16[64,2048]{1,0:T(8,128)(2,1)S(1)}, bf16[64,2048]{1,0:T(8,128)(2,1)S(1)}, u32[]{:S(2)}, u32[]{:S(2)}) collective-permute-start(bf16[64,2048]{1,0:T(8,128)(2,1)S(1)} %get-tuple-element.79), channel_id=1, source_target_pairs={{0,1},{1,0},{2,3},{3,2},{4,5},{5,4},{6,7},{7,6},{8,9},{9,8},{10,11... | collective-permute-start | bytes 786440 | tf_op jit(solution)/shard_map/ppermute | solution.py:449
  146.7 1.5 collective-permute-start.33
  146.7 8.7 %collective-permute-start.38 = (bf16[64,2048]{1,0:T(8,128)(2,1)S(1)}, bf16[64,2048]{1,0:T(8,128)(2,1)S(1)}, u32[]{:S(2)}, u32[]{:S(2)}) collective-permute-start(bf16[64,2048]{1,0:T(8,128)(2,1)S(1)} %get-tuple-element.84), channel_id=1, source_target_pairs={{0,2},{1,3},{2,0},{3,1},{4,6},{5,7},{6,4},{7,5},{8,10},{9,11},{10,... | collective-permute-start | bytes 786440 | tf_op jit(solution)/shard_map/ppermute | solution.py:449
  151.4 8.4 %collective-permute-start.34 = (bf16[2,4,16,1024]{3,2,1,0:T(8,128)(2,1)S(1)}, bf16[2,4,16,1024]{3,2,1,0:T(8,128)(2,1)S(1)}, u32[]{:S(2)}, u32[]{:S(2)}) collective-permute-start(bf16[2,4,16,1024]{3,2,1,0:T(8,128)(2,1)S(1)} %get-tuple-element.81.refs_5_), channel_id=1, source_target_pairs={{0,4},{4,0},{8,12},{12,8},{1,5},{5,1},{9,13},{13,9},{2,6},{6,2},{1... | collective-permute-start | bytes 786440 | tf_op jit(solution)/shard_map/ppermute | solution.py:449
  151.7 10.9 %collective-permute-start.39 = (bf16[64,2048]{1,0:T(8,128)(2,1)S(1)}, bf16[64,2048]{1,0:T(8,128)(2,1)S(1)}, u32[]{:S(2)}, u32[]{:S(2)}) collective-permute-start(bf16[64,2048]{1,0:T(8,128)(2,1)S(1)} %get-tuple-element.84), channel_id=1, source_target_pairs={{0,1},{1,0},{2,3},{3,2},{4,5},{5,4},{6,7},{7,6},{8,9},{9,8},{10,11... | collective-permute-start | bytes 786440 | tf_op jit(solution)/shard_map/ppermute | solution.py:449
  155.5 7.1 %collective-permute-start.40 = (bf16[64,2048]{1,0:T(8,128)(2,1)S(1)}, bf16[64,2048]{1,0:T(8,128)(2,1)S(1)}, u32[]{:S(2)}, u32[]{:S(2)}) collective-permute-start(bf16[64,2048]{1,0:T(8,128)(2,1)S(1)} %collective-permute-done.38), channel_id=1, source_target_pairs={{0,1},{1,0},{2,3},{3,2},{4,5},{5,4},{6,7},{7,6},{8,9},{9,8},{10,11... | collective-permute-start | bytes 786440 | tf_op jit(solution)/shard_map/ppermute | solution.py:449
  158.6 11.6 %collective-permute-start.36 = (bf16[2,4,16,1024]{3,2,1,0:T(8,128)(2,1)S(1)}, bf16[2,4,16,1024]{3,2,1,0:T(8,128)(2,1)S(1)}, u32[]{:S(2)}, u32[]{:S(2)}) collective-permute-start(bf16[2,4,16,1024]{3,2,1,0:T(8,128)(2,1)S(1)} %get-tuple-element.83.refs_5_), channel_id=1, source_target_pairs={{0,4},{4,0},{8,12},{12,8},{1,5},{5,1},{9,13},{13,9},{2,6},{6,2},{1... | collective-permute-start | bytes 786440 | tf_op jit(solution)/shard_map/ppermute | solution.py:449
  160.0 10.3 %collective-permute-start.35 = (bf16[1,4,16,1024]{3,2,1,0:T(8,128)(2,1)S(1)}, bf16[1,4,16,1024]{3,2,1,0:T(8,128)(2,1)S(1)}, u32[]{:S(2)}, u32[]{:S(2)}) collective-permute-start(bf16[1,4,16,1024]{3,2,1,0:T(8,128)(2,1)S(1)} %fold.20), channel_id=1, source_target_pairs={{0,8},{4,12},{8,0},{12,4},{1,9},{5,13},{9,1},{13,5},{2,10},{6,14},... | collective-permute-start | bytes 393224 | tf_op jit(solution)/shard_map/ppermute | solution.py:449
  168.9 12.1 %collective-permute-start.41 = (bf16[2,4,16,1024]{3,2,1,0:T(8,128)(2,1)S(1)}, bf16[2,4,16,1024]{3,2,1,0:T(8,128)(2,1)S(1)}, u32[]{:S(2)}, u32[]{:S(2)}) collective-permute-start(bf16[2,4,16,1024]{3,2,1,0:T(8,128)(2,1)S(1)} %tie.8.refs_5_), channel_id=1, source_target_pairs={{0,4},{4,0},{8,12},{12,8},{1,5},{5,1},{9,13},{13,9},{2,6},{6,2},{1... | collective-permute-start | bytes 786440 | tf_op jit(solution)/shard_map/ppermute | solution.py:449
  170.2 15.9 %collective-permute-start.43 = (bf16[2,4,16,1024]{3,2,1,0:T(8,128)(2,1)S(1)}, bf16[2,4,16,1024]{3,2,1,0:T(8,128)(2,1)S(1)}, u32[]{:S(2)}, u32[]{:S(2)}) collective-permute-start(bf16[2,4,16,1024]{3,2,1,0:T(8,128)(2,1)S(1)} %tie.9), channel_id=1, source_target_pairs={{0,4},{4,0},{8,12},{12,8},{1,5},{5,1},{9,13},{13,9},{2,6},{6,2},{1... | collective-permute-start | bytes 786440 | tf_op jit(solution)/shard_map/ppermute | solution.py:449
  172.5 14.2 %collective-permute-start.37 = (bf16[1,4,16,1024]{3,2,1,0:T(8,128)(2,1)S(1)}, bf16[1,4,16,1024]{3,2,1,0:T(8,128)(2,1)S(1)}, u32[]{:S(2)}, u32[]{:S(2)}) collective-permute-start(bf16[1,4,16,1024]{3,2,1,0:T(8,128)(2,1)S(1)} %fold.21), channel_id=1, source_target_pairs={{0,8},{4,12},{8,0},{12,4},{1,9},{5,13},{9,1},{13,5},{2,10},{6,14},... | collective-permute-start | bytes 393224 | tf_op jit(solution)/shard_map/ppermute | solution.py:449
  181.1 13.2 %collective-permute-start.42 = (bf16[1,4,16,1024]{3,2,1,0:T(8,128)(2,1)S(1)}, bf16[1,4,16,1024]{3,2,1,0:T(8,128)(2,1)S(1)}, u32[]{:S(2)}, u32[]{:S(2)}) collective-permute-start(bf16[1,4,16,1024]{3,2,1,0:T(8,128)(2,1)S(1)} %fold.22), channel_id=1, source_target_pairs={{0,8},{4,12},{8,0},{12,4},{1,9},{5,13},{9,1},{13,5},{2,10},{6,14},... | collective-permute-start | bytes 393224 | tf_op jit(solution)/shard_map/ppermute | solution.py:449
  186.2 10.2 %collective-permute-start.44 = (bf16[1,4,16,1024]{3,2,1,0:T(8,128)(2,1)S(1)}, bf16[1,4,16,1024]{3,2,1,0:T(8,128)(2,1)S(1)}, u32[]{:S(2)}, u32[]{:S(2)}) collective-permute-start(bf16[1,4,16,1024]{3,2,1,0:T(8,128)(2,1)S(1)} %fold.23), channel_id=1, source_target_pairs={{0,8},{4,12},{8,0},{12,4},{1,9},{5,13},{9,1},{13,5},{2,10},{6,14},... | collective-permute-start | bytes 393224 | tf_op jit(solution)/shard_map/ppermute | solution.py:449
  (7 other events, 12.3 us)

commit v7 on v6

--- a/solution.py
+++ b/solution.py
@@ -119,25 +119,26 @@
     )(x, *after)
 
 
-def fold_kernel(*refs):
-    refs[-1][...] = sum(r[...].astype(f32) for r in refs[:-1]).astype(bf16)
-
-
-def fold(terms):
+def fold_kernel(count, *refs):
+    refs[-1][...] = sum(r[...].astype(f32) for r in refs[:count]).astype(bf16)
+
+
+def fold(terms, after=()):
     half, tail = terms[-1].shape[0] // 2, terms[0].shape[1:]
     steps = 2 if tail[-1] % 256 == 0 else 1
     block = (half,) + tail[:-1] + (tail[-1] // steps,)
     middle = (0,) * (len(tail) - 1)
     return pl.pallas_call(
-        fold_kernel,
+        functools.partial(fold_kernel, len(terms)),
         grid=(steps,),
-        in_specs=[pl.BlockSpec(block, lambda j: (1,) + middle + (j,))] * len(terms),
+        in_specs=[pl.BlockSpec(block, lambda j: (1,) + middle + (j,))] * len(terms)
+        + anywhere(after),
         out_specs=pl.BlockSpec(block, lambda j: (0,) + middle + (j,)),
         out_shape=jax.ShapeDtypeStruct((half,) + tail, bf16),
         compiler_params=params(),
         cost_estimate=LIGHT,
         name="fold",
-    )(*terms)
+    )(*terms, *after)
 
 
 def activate_kernel(count, *refs):
@@ -250,7 +251,8 @@
 
 
 def finish_kernel(terms, widths, at_ref, edge_ref, q_ref, rest_ref, *refs):
-    sums, others, (att_ref, stat_ref) = refs[:terms], refs[terms:-2], refs[-2:]
+    sums, others = refs[:terms], refs[terms:terms + len(widths)]
+    att_ref, stat_ref = refs[-2:]
     rows, width = att_ref.shape
     zs, chunks = edge_ref.shape[:2]
     edge = jnp.concatenate(
@@ -280,7 +282,7 @@
     stat_ref[...] = stat if stat_ref.shape == stat.shape else stat.T[:8]
 
 
-def finish(at, edges, query, rest, sums, others, widths):
+def finish(at, edges, query, rest, sums, others, widths, after):
     rows, width = query.shape
     stat = (8, rows) if others and rows == DH else (rows, DH)
     return pl.pallas_call(
@@ -294,7 +296,8 @@
                 pl.BlockSpec((2, rows, width), lambda j, at: (0, 0, 0)),
             ]
             + [pl.BlockSpec((1, rows, width), lambda j, at: (0, 0, 0))] * len(sums)
-            + [pl.BlockSpec((rows, DH), lambda j, at: (0, 0))] * len(others),
+            + [pl.BlockSpec((rows, DH), lambda j, at: (0, 0))] * len(others)
+            + anywhere(after),
             out_specs=(
                 pl.BlockSpec((rows, width), lambda j, at: (0, 0)),
                 pl.BlockSpec(stat, lambda j, at: (0, 0)),
@@ -307,7 +310,7 @@
         compiler_params=params(),
         cost_estimate=LIGHT,
         name="finish",
-    )(at, edges, query, rest, *sums, *others)
+    )(at, edges, query, rest, *sums, *others, *after)
 
 
 def gate_kernel(count, parts, *refs):
@@ -451,10 +454,10 @@
     )
 
 
-def scatter(keep, send, axis):
-    terms, sent = [keep, swap(send, axis, 0)], send
+def scatter(keep, got, axis, after=()):
+    terms, sent = [keep, got], got
     for b in range(1, bits_of(axis)):
-        sent = fold(terms)
+        sent = fold(terms, after)
         terms.append(swap(sent, axis, b))
     return terms, sent
 
@@ -481,7 +484,13 @@
     if heads % 8:
         return [1] * heads
     unit = heads // 8
-    return [unit, 2 * unit, 2 * unit, 3 * unit]
+    return [unit, 2 * unit, 2 * unit, 2 * unit, unit]
+
+
+ORDER = [
+    "P0", "P1", "F0", "P2", "F1", "A0", "P3", "F2", "P4", "A1", "F3", "T0", "A2", "F4", "T1",
+    "A3", "G0", "G1", "T2", "A4", "E0", "E1", "T3", "G2", "T4", "G3", "E2", "G4", "E3", "E4",
+]
 
 
 def local(tokens, w_qkvu, k_cache, v_cache, w_out, vis_start, vis_end):
@@ -510,55 +519,42 @@
     sizes = head_chunks(width // DH)
     firsts = [sum(sizes[:c]) for c in range(len(sizes))]
     last = len(sizes) - 1
-    keeps, sent, parts, terms_of, atts, stats = [], [], [], [], [], []
-
-    def front(c):
-        after = keeps[-1:]
-        if c >= 2:
-            after = after + [sent[c - 2]]
-        if c >= 3:
-            after = after + [parts[c - 3][0]]
-        keep, send = project(at, ordered, w_qkvu, firsts[c], sizes[c], after)
-        keeps.append(keep)
-        before = [terms_of[c - 1][1]] if c >= 1 else []
-        if c >= 2:
-            before = before + [terms_of[c - 2][-1]]
-        if c >= 3:
-            before = before + queries[c - 3][1:2]
-        send = tie(send, before)
-        terms, out = scatter(keep, send, "hist")
-        sent.append(out)
-        terms_of.append(terms)
-
-    waits, queries = [], []
-
-    def middle_first(c):
-        after = waits[-1:] + (atts[:-1] if c == last else [])
-        parts.append(activate(terms_of[c], after))
-        queries.append(gather(parts[c][0], "hist"))
-
-    def middle(c):
-        query, rest = parts[c]
-        after = atts[-1:] if c == last else []
-        keep, send = attend(at, queries[c], k_cache, v_cache, edges, firsts[c], after)
-        waits.append(keep)
-        sums, _ = scatter(keep, send, "hist")
-        others = stats if c == last else []
-        widths = [s * DH for s in sizes[:c]] if c == last else []
-        att, stat = finish(at, edges, query, rest, sums, list(others), widths)
-        atts.append(att)
-        stats.append(stat)
-
-    for c in range(len(sizes)):
-        front(c)
-        if c == 2:
-            middle_first(0)
-    for c in range(len(sizes)):
-        if c == len(parts):
-            middle_first(c)
-        middle(c)
-
-    gated = gate_rows(all_stats(stats[-1], "head"), atts, [rest for _, rest in parts], chunks)
+    order = ORDER
+    if last != 4:
+        order = [step + str(c) for step in "PFATGE" for c in range(last + 1)]
+    chain, terms, sums, halves, queries, parts, atts, stats = [], {}, {}, {}, {}, {}, {}, {}
+    for step, c in [(name[0], int(name[1:])) for name in order]:
+        after = chain[-1:]
+        if step == "P":
+            keep, send = project(at, ordered, w_qkvu, firsts[c], sizes[c], after)
+            before = [terms[c - 1][1]] if c >= 1 else []
+            before += [terms[c - 2][-1]] if c - 2 in terms and len(terms[c - 2]) > 2 else []
+            before += [queries[0][1]] if c == last and 0 in queries else []
+            terms[c] = [keep, swap(tie(send, before), "hist", 0)]
+            chain.append(keep)
+        elif step == "F":
+            terms[c], sent = scatter(*terms[c], "hist", after)
+            chain.append(sent)
+        elif step == "A":
+            parts[c] = activate(terms[c], after)
+            queries[c] = gather(parts[c][0], "hist")
+            chain.append(parts[c][0])
+        elif step == "T":
+            keep, send = attend(at, queries[c], k_cache, v_cache, edges, firsts[c], after)
+            halves[c] = keep, swap(send, "hist", 0)
+            chain.append(keep)
+        elif step == "G":
+            sums[c], sent = scatter(*halves[c], "hist", after)
+            chain.append(sent)
+        else:
+            others = [stats[k] for k in range(last)] if c == last else []
+            widths = [size * DH for size in sizes[:last]] if c == last else []
+            atts[c], stats[c] = finish(at, edges, *parts[c], sums[c], others, widths, after)
+            chain.append(atts[c])
+
+    atts = [atts[c] for c in range(last + 1)]
+    rests = [parts[c][1] for c in range(last + 1)]
+    gated = gate_rows(all_stats(stats[last], "head"), atts, rests, chunks)
     columns = w_out.shape[1]
     straight = piece % 16 == 0 and zs & (zs - 1) == 0
     groups = 2 if straight and columns % 1024 == 0 else 1
@@ -574,7 +570,7 @@
                 before = first_steps[-2:-1] + ends[-3:-2]
                 send = tie(send, before)
                 sends.append(send)
-                terms, _ = scatter(keep, send, "head")
+                terms, _ = scatter(keep, swap(send, "head", 0), "head")
                 first_steps.append(terms[1])
                 ends.append(terms[-1])
             else:

time: 200 us -> 188 us (0.940)
  waiting for transfers between devices: 89 us -> 65.8 us
  starting transfers between devices: 28.9 us -> 37.1 us
  Pallas kernels: 74.1 us -> 78.2 us
    ppermute x42 -> x49, waiting for transfers between devices: 86.7 us -> 63.5 us  [swap(): lax.ppermute(x, axis, [(i, i ^ 1 << bit) for i in range(lax.axis_size(axi...]
    ppermute x42 -> x49, starting transfers between devices: 23.3 us -> 31.5 us  [swap(): lax.ppermute(x, axis, [(i, i ^ 1 << bit) for i in range(lax.axis_size(axi...]
    pallas_call x4 -> x5, Pallas kernels: 35.5 us -> 37.9 us  [project(): pl.pallas_call(functools.partial(project_kernel, parts, owners, len(after...]
    pallas_call x4 -> x5, Pallas kernels: 12.6 us -> 13.7 us  [attend(): pl.pallas_call(functools.partial(attend_kernel, owners), grid_spec=pltpu....]
    pallas_call x12 -> x14, Pallas kernels: 4.55 us -> 3.96 us  [fold(): pl.pallas_call(functools.partial(fold_kernel, len(terms)), grid=(steps,),...]
  transfers between devices with their start and end apart: 45 -> 52, of which waited for: 20 -> 20; matrix products, arithmetic and copies ran while one was open for 2% -> 2% of each run, Pallas kernels for 30% -> 37%
where the time goes in v7:
time: 188 us; the launch traced here: 187 us
  Pallas kernels  78.2 us (42%)
  waiting for transfers between devices  65.8 us (35%)
  starting transfers between devices  37.1 us (20%)
  local copies, waits for them, and re-layouts  4.28 us (2%)
    ppermute x49, waiting for transfers between devices, swap(): lax.ppermute(x, axis, [(i, i ^ 1 << bit) for i in range(lax.axis_size(axi...  63.5 us
    pallas_call x5, Pallas kernels, project(): pl.pallas_call(functools.partial(project_kernel, parts, owners, len(after...  37.9 us
    ppermute x49, starting transfers between devices, swap(): lax.ppermute(x, axis, [(i, i ^ 1 << bit) for i in range(lax.axis_size(axi...  31.5 us
    pallas_call x5, Pallas kernels, attend(): pl.pallas_call(functools.partial(attend_kernel, owners), grid_spec=pltpu....  13.7 us
    pallas_call x4, Pallas kernels, output(): pl.pallas_call(functools.partial(output_kernel, owners, slots), grid_spec...  12.5 us
    ppermute x3, starting transfers between devices, all_stats(): lax.ppermute(stat, axis, [(i, (i + k) % count) for i in range(count)])  5.54 us
    pallas_call x14, Pallas kernels, fold(): pl.pallas_call(functools.partial(fold_kernel, len(terms)), grid=(steps,),...  3.96 us
    pallas_call x5, Pallas kernels, activate(): pl.pallas_call(functools.partial(activate_kernel, len(terms)), grid=(1,),...  3.94 us
  transfers between devices with their start and end apart: 52, of which 20 were waited for; matrix products, arithmetic and copies ran while one was open for 2% of the time, Pallas kernels for 37%

profile of v7, /device:TPU:0, one launch (start us, length us, event | category | flops | bytes accessed | tf_op | source)
XLA Modules:
  0.0 187.2 jit_solution(3507401981567104849)
XLA Ops:
  0.0 5.5 %project.5 = (bf16[2,4,128,256]{3,2,1,0:T(8,128)(2,1)S(1)}, bf16[2,4,128,256]{3,2,1,0:T(8,128)(2,1)S(1)}) custom-call(s32[1]{0:T(128)} %bitcast.at_ref, bf16[4,2,4,16,2048]{4,3,2,1,0:T(8,128)(2,1)} %bitcast.29, bf16[4,2,4,16,2048]{4,3,2,1,0:T(8,128)(2,1)} %bitcast.30, bf16[4,2,4,16,2048]{4,3,2,1,0:T(8,128)(2,1)} %bitcast.31, ...), custom_call_target="tpu_custom_call" | custom-call | flops 1000 | bytes 1000 | tf_op jit(solution)/shard_map/project/pallas_call | solution.py:76
  6.1 8.7 %project.6 = (bf16[2,4,128,512]{3,2,1,0:T(8,128)(2,1)S(1)}, bf16[2,4,128,512]{3,2,1,0:T(8,128)(2,1)S(1)}) custom-call(s32[1]{0:T(128)} %bitcast.at_ref, bf16[4,2,4,16,2048]{4,3,2,1,0:T(8,128)(2,1)} %bitcast.33, bf16[4,2,4,16,2048]{4,3,2,1,0:T(8,128)(2,1)} %bitcast.34, bf16[4,2,4,16,2048]{4,3,2,1,0:T(8,128)(2,1)} %bitcast.35, ...), custom_call_target="tpu_custom_call" | custom-call | flops 1000 | bytes 1000 | tf_op jit(solution)/shard_map/project/pallas_call | solution.py:76
  15.2 3.0 %collective-permute-start.2 = (bf16[1,4,128,256]{3,2,1,0:T(8,128)(2,1)S(1)}, bf16[1,4,128,256]{3,2,1,0:T(8,128)(2,1)S(1)}, u32[]{:S(2)}, u32[]{:S(2)}) collective-permute-start(bf16[1,4,128,256]{3,2,1,0:T(8,128)(2,1)S(1)} %fold.14.refs_8_), channel_id=1, source_target_pairs={{0,2},{1,3},{2,0},{3,1},{4,6},{5,7},{6,4},{7,5},{8,10},{9,11},{10,... | collective-permute-start | bytes 786440 | tf_op jit(solution)/shard_map/ppermute | solution.py:452
  18.2 8.7 %project.7 = (bf16[2,4,128,512]{3,2,1,0:T(8,128)(2,1)S(1)}, bf16[2,4,128,512]{3,2,1,0:T(8,128)(2,1)S(1)}) custom-call(s32[1]{0:T(128)} %bitcast.at_ref, bf16[4,2,4,16,2048]{4,3,2,1,0:T(8,128)(2,1)} %bitcast.37, bf16[4,2,4,16,2048]{4,3,2,1,0:T(8,128)(2,1)} %bitcast.38, bf16[4,2,4,16,2048]{4,3,2,1,0:T(8,128)(2,1)} %bitcast.39, ...), custom_call_target="tpu_custom_call" | custom-call | flops 1000 | bytes 1000 | tf_op jit(solution)/shard_map/project/pallas_call | solution.py:76
  27.7 8.8 %project.8 = (bf16[2,4,128,512]{3,2,1,0:T(8,128)(2,1)S(1)}, bf16[2,4,128,512]{3,2,1,0:T(8,128)(2,1)S(1)}) custom-call(s32[1]{0:T(128)} %bitcast.at_ref, bf16[4,2,4,16,2048]{4,3,2,1,0:T(8,128)(2,1)} %bitcast.41, bf16[4,2,4,16,2048]{4,3,2,1,0:T(8,128)(2,1)} %bitcast.42, bf16[4,2,4,16,2048]{4,3,2,1,0:T(8,128)(2,1)} %bitcast.43, ...), custom_call_target="tpu_custom_call" | custom-call | flops 1000 | bytes 1000 | tf_op jit(solution)/shard_map/project/pallas_call | solution.py:76
  36.6 5.2 %collective-permute-done.4.refs_2_ = bf16[1,4,128,512]{3,2,1,0:T(8,128)(2,1)S(1)} collective-permute-done((bf16[1,4,128,512]{3,2,1,0:T(8,128)(2,1)S(1)}, bf16[1,4,128,512]{3,2,1,0:T(8,128)(2,1)S(1)}, u32[]{:S(2)}, u32[]{:S(2)}) %collective-permute-start.4) | collective-permute-done | bytes 524320 | tf_op jit(solution)/shard_map/ppermute | solution.py:452
  42.4 1.7 collective-permute-start.7
  44.1 6.1 %project.9 = (bf16[2,4,128,256]{3,2,1,0:T(8,128)(2,1)S(1)}, bf16[2,4,128,256]{3,2,1,0:T(8,128)(2,1)}) custom-call(s32[1]{0:T(128)} %bitcast.at_ref, bf16[4,2,4,16,2048]{4,3,2,1,0:T(8,128)(2,1)} %bitcast.45, bf16[4,2,4,16,2048]{4,3,2,1,0:T(8,128)(2,1)} %bitcast.46, bf16[4,2,4,16,2048]{4,3,2,1,0:T(8,128)(2,1)} %bitcast.47, ...), custom_call_target="tpu_custom_call" | custom-call | flops 1000 | bytes 1000 | tf_op jit(solution)/shard_map/project/pallas_call | solution.py:76
  50.3 7.6 %collective-permute-done.7.refs_3_.refs_1_ = bf16[128,256]{1,0:T(8,128)(2,1)S(1)} collective-permute-done((bf16[128,256]{1,0:T(8,128)(2,1)S(1)}, bf16[128,256]{1,0:T(8,128)(2,1)S(1)}, u32[]{:S(2)}, u32[]{:S(2)}) %collective-permute-start.7) | collective-permute-done | bytes 65568 | tf_op jit(solution)/shard_map/ppermute | solution.py:452
  60.3 1.7 collective-permute-start.20
  62.5 3.1 %collective-permute-done.15.refs_1_ = bf16[128,512]{1,0:T(8,128)(2,1)} collective-permute-done((bf16[128,512]{1,0:T(8,128)(2,1)}, bf16[128,512]{1,0:T(8,128)(2,1)}, u32[]{:S(2)}, u32[]{:S(2)}) %collective-permute-start.15) | collective-permute-done | bytes 131104 | tf_op jit(solution)/shard_map/ppermute | solution.py:452
  68.0 1.2 pad_add_fusion.refs_4_.refs_5_.refs_6_.refs_7_.edge_ref
  70.9 2.0 %attend.5 = (bf16[2,128,256]{2,1,0:T(8,128)(2,1)S(1)}, bf16[2,128,256]{2,1,0:T(8,128)(2,1)S(1)}) custom-call(s32[1]{0:T(128)} %bitcast.at_ref, bf16[128,256]{1,0:T(8,128)(2,1)S(1)} %copy-done.9, bf16[128,256]{1,0:T(8,128)(2,1)S(1)} %copy-done.12, bf16[128,256]{1,0:T(8,128)(2,1)} %collective-permute-done.9.refs_2_, ...), custom_call_target="tpu_custom_call" | custom-call | flops 1000 | bytes 1000 | tf_op jit(solution)/shard_map/attend/pallas_call | solution.py:221
  75.1 3.3 %attend.6 = (bf16[2,128,512]{2,1,0:T(8,128)(2,1)S(1)}, bf16[2,128,512]{2,1,0:T(8,128)(2,1)S(1)}) custom-call(s32[1]{0:T(128)} %bitcast.at_ref, bf16[128,512]{1,0:T(8,128)(2,1)} %get-tuple-element.66.refs_2_.refs_0_.q_ref, bf16[128,512]{1,0:T(8,128)(2,1)} %collective-permute-done.15.refs_1_, bf16[128,512]{1,0:T(8,128)(2,1)} %collective-permute-done.16.refs_2_, ...), custom_call_target="tpu_custom_call" | custom-call | flops 1000 | bytes 1000 | tf_op jit(solution)/shard_map/attend/pallas_call | solution.py:221
  79.0 2.0 %collective-permute-start.11 = (bf16[1,4,128,256]{3,2,1,0:T(8,128)(2,1)S(1)}, bf16[1,4,128,256]{3,2,1,0:T(8,128)(2,1)S(1)}, u32[]{:S(2)}, u32[]{:S(2)}) collective-permute-start(bf16[1,4,128,256]{3,2,1,0:T(8,128)(2,1)S(1)} %fold.18.refs_10_), channel_id=1, source_target_pairs={{0,2},{1,3},{2,0},{3,1},{4,6},{5,7},{6,4},{7,5},{8,10},{9,11},{10,... | collective-permute-start | bytes 786440 | tf_op jit(solution)/shard_map/ppermute | solution.py:452
  81.1 1.4 activate.8
  82.6 2.8 %collective-permute-done.12.refs_1_ = bf16[128,512]{1,0:T(8,128)(2,1)S(1)} collective-permute-done((bf16[128,512]{1,0:T(8,128)(2,1)S(1)}, bf16[128,512]{1,0:T(8,128)(2,1)S(1)}, u32[]{:S(2)}, u32[]{:S(2)}) %collective-permute-start.12) | collective-permute-done | bytes 131104 | tf_op jit(solution)/shard_map/ppermute | solution.py:452
  86.3 7.5 %collective-permute-done.25.refs_1_ = bf16[128,512]{1,0:T(8,128)(2,1)S(1)} collective-permute-done((bf16[128,512]{1,0:T(8,128)(2,1)S(1)}, bf16[128,512]{1,0:T(8,128)(2,1)S(1)}, u32[]{:S(2)}, u32[]{:S(2)}) %collective-permute-start.25) | collective-permute-done | bytes 131104 | tf_op jit(solution)/shard_map/ppermute | solution.py:452
  93.8 3.2 %attend.7 = (bf16[2,128,512]{2,1,0:T(8,128)(2,1)S(1)}, bf16[2,128,512]{2,1,0:T(8,128)(2,1)S(1)}) custom-call(s32[1]{0:T(128)} %bitcast.at_ref, bf16[128,512]{1,0:T(8,128)(2,1)S(1)} %get-tuple-element.68.refs_2_.refs_0_.q_ref, bf16[128,512]{1,0:T(8,128)(2,1)S(1)} %collective-permute-done.12.refs_1_, bf16[128,512]{1,0:T(8,128)(2,1)S(1)} %collective-permute-done.13.refs_2_, ...), custom_call_target="tpu_custom_call" | custom-call | flops 1000 | bytes 1000 | tf_op jit(solution)/shard_map/attend/pallas_call | solution.py:221
  99.0 1.3 finish.6
  100.4 3.2 %attend.8 = (bf16[2,128,512]{2,1,0:T(8,128)(2,1)S(1)}, bf16[2,128,512]{2,1,0:T(8,128)(2,1)S(1)}) custom-call(s32[1]{0:T(128)} %bitcast.at_ref, bf16[128,512]{1,0:T(8,128)(2,1)S(1)} %get-tuple-element.72.refs_2_.refs_0_.q_ref, bf16[128,512]{1,0:T(8,128)(2,1)S(1)} %collective-permute-done.25.refs_1_, bf16[128,512]{1,0:T(8,128)(2,1)S(1)} %collective-permute-done.26.refs_2_, ...), custom_call_target="tpu_custom_call" | custom-call | flops 1000 | bytes 1000 | tf_op jit(solution)/shard_map/attend/pallas_call | solution.py:221
  103.7 2.0 %collective-permute-start.21 = (bf16[128,256]{1,0:T(8,128)(2,1)S(1)}, bf16[128,256]{1,0:T(8,128)(2,1)S(1)}, u32[]{:S(2)}, u32[]{:S(2)}) collective-permute-start(bf16[128,256]{1,0:T(8,128)(2,1)S(1)} %get-tuple-element.74.refs_3_.refs_0_.q_ref), channel_id=1, source_target_pairs={{0,2},{1,3},{2,0},{3,1},{4,6},{5,7},{6,4},{7,5},{8,10},{9,11},{10,... | collective-permute-start | bytes 196616 | tf_op jit(solution)/shard_map/ppermute | solution.py:452
  105.6 2.5 %collective-permute-done.21.refs_1_ = bf16[128,256]{1,0:T(8,128)(2,1)S(1)} collective-permute-done((bf16[128,256]{1,0:T(8,128)(2,1)S(1)}, bf16[128,256]{1,0:T(8,128)(2,1)S(1)}, u32[]{:S(2)}, u32[]{:S(2)}) %collective-permute-start.21) | collective-permute-done | bytes 65568 | tf_op jit(solution)/shard_map/ppermute | solution.py:452
  108.3 1.8 collective-permute-start.31
  110.1 2.0 %attend.9 = (bf16[2,128,256]{2,1,0:T(8,128)(2,1)S(1)}, bf16[2,128,256]{2,1,0:T(8,128)(2,1)S(1)}) custom-call(s32[1]{0:T(128)} %bitcast.at_ref, bf16[128,256]{1,0:T(8,128)(2,1)S(1)} %get-tuple-element.74.refs_3_.refs_0_.q_ref, bf16[128,256]{1,0:T(8,128)(2,1)S(1)} %collective-permute-done.21.refs_1_, bf16[128,256]{1,0:T(8,128)(2,1)S(1)} %collective-permute-done.22.refs_2_, ...), custom_call_target="tpu_custom_call" | custom-call | flops 1000 | bytes 1000 | tf_op jit(solution)/shard_map/attend/pallas_call | solution.py:221
  114.8 1.8 collective-permute-start.33
  116.7 2.3 %collective-permute-done.34.refs_2_ = bf16[1,128,512]{2,1,0:T(8,128)(2,1)S(1)} collective-permute-done((bf16[1,128,512]{2,1,0:T(8,128)(2,1)S(1)}, bf16[1,128,512]{2,1,0:T(8,128)(2,1)S(1)}, u32[]{:S(2)}, u32[]{:S(2)}) %collective-permute-start.34) | collective-permute-done | bytes 131104 | tf_op jit(solution)/shard_map/ppermute | solution.py:452
  120.2 1.7 collective-permute-start.35
  121.9 2.5 %collective-permute-start.36 = (f32[8,128]{1,0:T(8,128)S(1)}, f32[8,128]{1,0:T(8,128)S(1)}, u32[]{:S(2)}, u32[]{:S(2)}) collective-permute-start(f32[8,128]{1,0:T(8,128)S(1)} %get-tuple-element.93.refs_0_), channel_id=1, source_target_pairs={{0,8},{4,12},{8,0},{12,4},{1,9},{5,13},{9,1},{13,5},{2,10},{6,14},... | collective-permute-start | bytes 12296 | tf_op jit(solution)/shard_map/ppermute | solution.py:478
  124.4 1.3 collective-permute-start.37
  126.4 1.6 collective-permute-done.37.refs_3_
  128.4 1.3 collective-permute-start.38
  129.7 5.2 %collective-permute-done.38 = bf16[64,2048]{1,0:T(8,128)(2,1)S(1)} collective-permute-done((bf16[64,2048]{1,0:T(8,128)(2,1)S(1)}, bf16[64,2048]{1,0:T(8,128)(2,1)S(1)}, u32[]{:S(2)}, u32[]{:S(2)}) %collective-permute-start.38) | collective-permute-done | bytes 262176 | tf_op jit(solution)/shard_map/ppermute | solution.py:452
  134.9 1.2 collective-permute-start.45
  136.4 3.1 %output.4 = (bf16[2,4,16,1024]{3,2,1,0:T(8,128)(2,1)S(1)}, bf16[2,4,16,1024]{3,2,1,0:T(8,128)(2,1)S(1)}) custom-call(s32[1]{0:T(128)} %bitcast.1.index_ref, bf16[4,16,2048]{2,1,0:T(8,128)(2,1)S(1)} %bitcast.15, bf16[4,16,2048]{2,1,0:T(8,128)(2,1)S(1)} %bitcast.19, bf16[4,16,2048]{2,1,0:T(8,128)(2,1)S(1)} %bitcast.21, bf16[4,16,2048]{2,1,0:T(8,128)(2,1)S(1)} %bitcast.25, ...), custom_call_target="tpu_custom_call" | custom-call | flops 1000 | bytes 1000 | tf_op jit(solution)/shard_map/output/pallas_call | solution.py:379
  139.8 3.8 %collective-permute-done.45 = bf16[64,2048]{1,0:T(8,128)(2,1)S(1)} collective-permute-done((bf16[64,2048]{1,0:T(8,128)(2,1)S(1)}, bf16[64,2048]{1,0:T(8,128)(2,1)S(1)}, u32[]{:S(2)}, u32[]{:S(2)}) %collective-permute-start.45) | collective-permute-done | bytes 262176 | tf_op jit(solution)/shard_map/ppermute | solution.py:452
  143.6 3.1 %output.5 = (bf16[2,4,16,1024]{3,2,1,0:T(8,128)(2,1)S(1)}, bf16[2,4,16,1024]{3,2,1,0:T(8,128)(2,1)S(1)}) custom-call(s32[1]{0:T(128)} %bitcast.1.index_ref, bf16[4,16,2048]{2,1,0:T(8,128)(2,1)S(1)} %bitcast.16, bf16[4,16,2048]{2,1,0:T(8,128)(2,1)S(1)} %bitcast.20, bf16[4,16,2048]{2,1,0:T(8,128)(2,1)S(1)} %bitcast.22, bf16[4,16,2048]{2,1,0:T(8,128)(2,1)S(1)} %bitcast.26, ...), custom_call_target="tpu_custom_call" | custom-call | flops 1000 | bytes 1000 | tf_op jit(solution)/shard_map/output/pallas_call | solution.py:379
  148.1 2.6 %collective-permute-start.42 = (bf16[1,4,16,1024]{3,2,1,0:T(8,128)(2,1)S(1)}, bf16[1,4,16,1024]{3,2,1,0:T(8,128)(2,1)S(1)}, u32[]{:S(2)}, u32[]{:S(2)}) collective-permute-start(bf16[1,4,16,1024]{3,2,1,0:T(8,128)(2,1)S(1)} %fold.24), channel_id=1, source_target_pairs={{0,8},{4,12},{8,0},{12,4},{1,9},{5,13},{9,1},{13,5},{2,10},{6,14},... | collective-permute-start | bytes 393224 | tf_op jit(solution)/shard_map/ppermute | solution.py:452
  150.7 3.1 %output.6 = (bf16[2,4,16,1024]{3,2,1,0:T(8,128)(2,1)S(1)}, bf16[2,4,16,1024]{3,2,1,0:T(8,128)(2,1)S(1)}) custom-call(s32[1]{0:T(128)} %bitcast.1.index_ref, bf16[4,16,2048]{2,1,0:T(8,128)(2,1)S(1)} %bitcast.13, bf16[4,16,2048]{2,1,0:T(8,128)(2,1)S(1)} %bitcast.17, bf16[4,16,2048]{2,1,0:T(8,128)(2,1)S(1)} %bitcast.23, bf16[4,16,2048]{2,1,0:T(8,128)(2,1)S(1)} %bitcast.27, ...), custom_call_target="tpu_custom_call" | custom-call | flops 1000 | bytes 1000 | tf_op jit(solution)/shard_map/output/pallas_call | solution.py:379
  153.9 3.2 %output.7 = (bf16[2,4,16,1024]{3,2,1,0:T(8,128)(2,1)S(1)}, bf16[2,4,16,1024]{3,2,1,0:T(8,128)(2,1)S(1)}) custom-call(s32[1]{0:T(128)} %bitcast.1.index_ref, bf16[4,16,2048]{2,1,0:T(8,128)(2,1)S(1)} %bitcast.14, bf16[4,16,2048]{2,1,0:T(8,128)(2,1)S(1)} %bitcast.18, bf16[4,16,2048]{2,1,0:T(8,128)(2,1)S(1)} %bitcast.24, bf16[4,16,2048]{2,1,0:T(8,128)(2,1)S(1)} %bitcast.28, ...), custom_call_target="tpu_custom_call" | custom-call | flops 1000 | bytes 1000 | tf_op jit(solution)/shard_map/output/pallas_call | solution.py:379
  157.0 1.2 collective-permute-start.48
  158.4 2.1 %collective-permute-start.50 = (bf16[2,4,16,1024]{3,2,1,0:T(8,128)(2,1)S(1)}, bf16[2,4,16,1024]{3,2,1,0:T(8,128)(2,1)S(1)}, u32[]{:S(2)}, u32[]{:S(2)}) collective-permute-start(bf16[2,4,16,1024]{3,2,1,0:T(8,128)(2,1)S(1)} %tie.11), channel_id=1, source_target_pairs={{0,4},{4,0},{8,12},{12,8},{1,5},{5,1},{9,13},{13,9},{2,6},{6,2},{1... | collective-permute-start | bytes 786440 | tf_op jit(solution)/shard_map/ppermute | solution.py:452
  160.6 2.0 %collective-permute-start.44 = (bf16[1,4,16,1024]{3,2,1,0:T(8,128)(2,1)S(1)}, bf16[1,4,16,1024]{3,2,1,0:T(8,128)(2,1)S(1)}, u32[]{:S(2)}, u32[]{:S(2)}) collective-permute-start(bf16[1,4,16,1024]{3,2,1,0:T(8,128)(2,1)S(1)} %fold.25), channel_id=1, source_target_pairs={{0,8},{4,12},{8,0},{12,4},{1,9},{5,13},{9,1},{13,5},{2,10},{6,14},... | collective-permute-start | bytes 393224 | tf_op jit(solution)/shard_map/ppermute | solution.py:452
  162.6 6.5 %collective-permute-done.48.refs_1_.refs_7_ = bf16[2,4,16,1024]{3,2,1,0:T(8,128)(2,1)S(1)} collective-permute-done((bf16[2,4,16,1024]{3,2,1,0:T(8,128)(2,1)S(1)}, bf16[2,4,16,1024]{3,2,1,0:T(8,128)(2,1)S(1)}, u32[]{:S(2)}, u32[]{:S(2)}) %collective-permute-start.48) | collective-permute-done | bytes 262176 | tf_op jit(solution)/shard_map/ppermute | solution.py:452
  169.3 4.9 %collective-permute-done.50.refs_1_.refs_10_ = bf16[2,4,16,1024]{3,2,1,0:T(8,128)(2,1)S(1)} collective-permute-done((bf16[2,4,16,1024]{3,2,1,0:T(8,128)(2,1)S(1)}, bf16[2,4,16,1024]{3,2,1,0:T(8,128)(2,1)S(1)}, u32[]{:S(2)}, u32[]{:S(2)}) %collective-permute-start.50) | collective-permute-done | bytes 262176 | tf_op jit(solution)/shard_map/ppermute | solution.py:452
  174.8 7.6 %collective-permute-done.49.refs_8_ = bf16[1,4,16,1024]{3,2,1,0:T(8,128)(2,1)S(1)} collective-permute-done((bf16[1,4,16,1024]{3,2,1,0:T(8,128)(2,1)S(1)}, bf16[1,4,16,1024]{3,2,1,0:T(8,128)(2,1)S(1)}, u32[]{:S(2)}, u32[]{:S(2)}) %collective-permute-start.49) | collective-permute-done | bytes 131104 | tf_op jit(solution)/shard_map/ppermute | solution.py:452
  182.4 2.2 %collective-permute-done.51.refs_11_ = bf16[1,4,16,1024]{3,2,1,0:T(8,128)(2,1)S(1)} collective-permute-done((bf16[1,4,16,1024]{3,2,1,0:T(8,128)(2,1)S(1)}, bf16[1,4,16,1024]{3,2,1,0:T(8,128)(2,1)S(1)}, u32[]{:S(2)}, u32[]{:S(2)}) %collective-permute-start.51) | collective-permute-done | bytes 131104 | tf_op jit(solution)/shard_map/ppermute | solution.py:452
  184.6 2.6 %close.1 = bf16[8,16,2048]{2,1,0:T(8,128)(2,1)} custom-call(s32[2]{0:T(128)S(1)} %pad_add_fusion.1.at_ref, bf16[32,16,2048]{2,1,0:T(8,128)(2,1)} %bitcast.49, bf16[2,4,16,1024]{3,2,1,0:T(8,128)(2,1)S(1)} %get-tuple-element.96.refs_0_, bf16[2,4,16,1024]{3,2,1,0:T(8,128)(2,1)S(1)} %collective-permute-done.41.refs_1_, ...), custom_call_target="tpu_custom_call" | custom-call | flops 1000 | bytes 1000 | tf_op jit(solution)/shard_map/close/pallas_call | solution.py:421
  (137 shorter events, 23.0 us)
Async XLA Ops:
  5.5 9.3 %collective-permute-start = (bf16[2,4,128,256]{3,2,1,0:T(8,128)(2,1)S(1)}, bf16[2,4,128,256]{3,2,1,0:T(8,128)(2,1)S(1)}, u32[]{:S(2)}, u32[]{:S(2)}) collective-permute-start(bf16[2,4,128,256]{3,2,1,0:T(8,128)(2,1)S(1)} %get-tuple-element.56), channel_id=1, source_target_pairs={{0,1},{1,0},{2,3},{3,2},{4,5},{5,4},{6,7},{7,6},{8,9},{9,8},{10,11... | collective-permute-start | bytes 1572872 | tf_op jit(solution)/shard_map/ppermute | solution.py:452
  14.8 12.1 %collective-permute-start.1 = (bf16[2,4,128,512]{3,2,1,0:T(8,128)(2,1)S(1)}, bf16[2,4,128,512]{3,2,1,0:T(8,128)(2,1)S(1)}, u32[]{:S(2)}, u32[]{:S(2)}) collective-permute-start(bf16[2,4,128,512]{3,2,1,0:T(8,128)(2,1)S(1)} %tie.6), channel_id=1, source_target_pairs={{0,1},{1,0},{2,3},{3,2},{4,5},{5,4},{6,7},{7,6},{8,9},{9,8},{10,11... | collective-permute-start | bytes 3145736 | tf_op jit(solution)/shard_map/ppermute | solution.py:452
  15.2 11.7 %collective-permute-start.2 = (bf16[1,4,128,256]{3,2,1,0:T(8,128)(2,1)S(1)}, bf16[1,4,128,256]{3,2,1,0:T(8,128)(2,1)S(1)}, u32[]{:S(2)}, u32[]{:S(2)}) collective-permute-start(bf16[1,4,128,256]{3,2,1,0:T(8,128)(2,1)S(1)} %fold.14.refs_8_), channel_id=1, source_target_pairs={{0,2},{1,3},{2,0},{3,1},{4,6},{5,7},{6,4},{7,5},{8,10},{9,11},{10,... | collective-permute-start | bytes 786440 | tf_op jit(solution)/shard_map/ppermute | solution.py:452
  27.0 14.8 %collective-permute-start.3 = (bf16[2,4,128,512]{3,2,1,0:T(8,128)(2,1)S(1)}, bf16[2,4,128,512]{3,2,1,0:T(8,128)(2,1)S(1)}, u32[]{:S(2)}, u32[]{:S(2)}) collective-permute-start(bf16[2,4,128,512]{3,2,1,0:T(8,128)(2,1)S(1)} %tie.7), channel_id=1, source_target_pairs={{0,1},{1,0},{2,3},{3,2},{4,5},{5,4},{6,7},{7,6},{8,9},{9,8},{10,11... | collective-permute-start | bytes 3145736 | tf_op jit(solution)/shard_map/ppermute | solution.py:452
  27.4 14.4 %collective-permute-start.4 = (bf16[1,4,128,512]{3,2,1,0:T(8,128)(2,1)S(1)}, bf16[1,4,128,512]{3,2,1,0:T(8,128)(2,1)S(1)}, u32[]{:S(2)}, u32[]{:S(2)}) collective-permute-start(bf16[1,4,128,512]{3,2,1,0:T(8,128)(2,1)S(1)} %fold.15.refs_3_), channel_id=1, source_target_pairs={{0,2},{1,3},{2,0},{3,1},{4,6},{5,7},{6,4},{7,5},{8,10},{9,11},{10,... | collective-permute-start | bytes 1572872 | tf_op jit(solution)/shard_map/ppermute | solution.py:452
  41.7 16.1 %collective-permute-start.5 = (bf16[2,4,128,512]{3,2,1,0:T(8,128)(2,1)S(1)}, bf16[2,4,128,512]{3,2,1,0:T(8,128)(2,1)S(1)}, u32[]{:S(2)}, u32[]{:S(2)}) collective-permute-start(bf16[2,4,128,512]{3,2,1,0:T(8,128)(2,1)S(1)} %tie.8), channel_id=1, source_target_pairs={{0,1},{1,0},{2,3},{3,2},{4,5},{5,4},{6,7},{7,6},{8,9},{9,8},{10,11... | collective-permute-start | bytes 3145736 | tf_op jit(solution)/shard_map/ppermute | solution.py:452
  42.0 15.8 %collective-permute-start.6 = (bf16[1,4,128,512]{3,2,1,0:T(8,128)(2,1)S(1)}, bf16[1,4,128,512]{3,2,1,0:T(8,128)(2,1)S(1)}, u32[]{:S(2)}, u32[]{:S(2)}) collective-permute-start(bf16[1,4,128,512]{3,2,1,0:T(8,128)(2,1)S(1)} %fold.16.refs_8_), channel_id=1, source_target_pairs={{0,2},{1,3},{2,0},{3,1},{4,6},{5,7},{6,4},{7,5},{8,10},{9,11},{10,... | collective-permute-start | bytes 1572872 | tf_op jit(solution)/shard_map/ppermute | solution.py:452
  42.4 15.4 %collective-permute-start.7 = (bf16[128,256]{1,0:T(8,128)(2,1)S(1)}, bf16[128,256]{1,0:T(8,128)(2,1)S(1)}, u32[]{:S(2)}, u32[]{:S(2)}) collective-permute-start(bf16[128,256]{1,0:T(8,128)(2,1)S(1)} %get-tuple-element.61.refs_8_.refs_0_.q_ref), channel_id=1, source_target_pairs={{0,2},{1,3},{2,0},{3,1},{4,6},{5,7},{6,4},{7,5},{8,10},{9,11},{10,... | collective-permute-start | bytes 196616 | tf_op jit(solution)/shard_map/ppermute | solution.py:452
  57.9 15.4 %collective-permute-start.8 = (bf16[2,4,128,256]{3,2,1,0:T(8,128)(2,1)}, bf16[2,4,128,256]{3,2,1,0:T(8,128)(2,1)}, u32[]{:S(2)}, u32[]{:S(2)}) collective-permute-start(bf16[2,4,128,256]{3,2,1,0:T(8,128)(2,1)} %tie.9), channel_id=1, source_target_pairs={{0,1},{1,0},{2,3},{3,2},{4,5},{5,4},{6,7},{7,6},{8,9},{9,8},{10,11... | collective-permute-start | bytes 1572872 | tf_op jit(solution)/shard_map/ppermute | solution.py:452
  58.9 6.7 %collective-permute-start.15 = (bf16[128,512]{1,0:T(8,128)(2,1)}, bf16[128,512]{1,0:T(8,128)(2,1)}, u32[]{:S(2)}, u32[]{:S(2)}) collective-permute-start(bf16[128,512]{1,0:T(8,128)(2,1)} %get-tuple-element.66.refs_2_.refs_0_.q_ref), channel_id=1, source_target_pairs={{0,2},{1,3},{2,0},{3,1},{4,6},{5,7},{6,4},{7,5},{8,10},{9,11},{10,... | collective-permute-start | bytes 393224 | tf_op jit(solution)/shard_map/ppermute | solution.py:452
  60.3 20.8 %collective-permute-start.20 = (bf16[1,4,128,512]{3,2,1,0:T(8,128)(2,1)}, bf16[1,4,128,512]{3,2,1,0:T(8,128)(2,1)}, u32[]{:S(2)}, u32[]{:S(2)}) collective-permute-start(bf16[1,4,128,512]{3,2,1,0:T(8,128)(2,1)} %fold.17.refs_10_), channel_id=1, source_target_pairs={{0,2},{1,3},{2,0},{3,1},{4,6},{5,7},{6,4},{7,5},{8,10},{9,11},{10,... | collective-permute-start | bytes 1572872 | tf_op jit(solution)/shard_map/ppermute | solution.py:452
  62.0 5.5 %collective-permute-start.9 = (bf16[128,256]{1,0:T(8,128)(2,1)}, bf16[128,256]{1,0:T(8,128)(2,1)}, u32[]{:S(2)}, u32[]{:S(2)}) collective-permute-start(bf16[128,256]{1,0:T(8,128)(2,1)} %copy-done.8), channel_id=1, source_target_pairs={{0,1},{1,0},{2,3},{3,2},{4,5},{5,4},{6,7},{7,6},{8,9},{9,8},{10,11... | collective-permute-start | bytes 196616 | tf_op jit(solution)/shard_map/ppermute | solution.py:452
  62.0 13.1 %collective-permute-start.16 = (bf16[128,512]{1,0:T(8,128)(2,1)}, bf16[128,512]{1,0:T(8,128)(2,1)}, u32[]{:S(2)}, u32[]{:S(2)}) collective-permute-start(bf16[128,512]{1,0:T(8,128)(2,1)} %get-tuple-element.66.refs_2_.refs_0_.q_ref), channel_id=1, source_target_pairs={{0,1},{1,0},{2,3},{3,2},{4,5},{5,4},{6,7},{7,6},{8,9},{9,8},{10,11... | collective-permute-start | bytes 393224 | tf_op jit(solution)/shard_map/ppermute | solution.py:452
  65.6 9.5 %collective-permute-start.17 = (bf16[128,512]{1,0:T(8,128)(2,1)}, bf16[128,512]{1,0:T(8,128)(2,1)}, u32[]{:S(2)}, u32[]{:S(2)}) collective-permute-start(bf16[128,512]{1,0:T(8,128)(2,1)} %collective-permute-done.15.refs_1_), channel_id=1, source_target_pairs={{0,1},{1,0},{2,3},{3,2},{4,5},{5,4},{6,7},{7,6},{8,9},{9,8},{10,11... | collective-permute-start | bytes 393224 | tf_op jit(solution)/shard_map/ppermute | solution.py:452
  78.5 7.0 %collective-permute-start.18 = (bf16[2,128,512]{2,1,0:T(8,128)(2,1)S(1)}, bf16[2,128,512]{2,1,0:T(8,128)(2,1)S(1)}, u32[]{:S(2)}, u32[]{:S(2)}) collective-permute-start(bf16[2,128,512]{2,1,0:T(8,128)(2,1)S(1)} %get-tuple-element.70), channel_id=1, source_target_pairs={{0,1},{1,0},{2,3},{3,2},{4,5},{5,4},{6,7},{7,6},{8,9},{9,8},{10,11... | collective-permute-start | bytes 786440 | tf_op jit(solution)/shard_map/ppermute | solution.py:452
  78.7 3.7 %collective-permute-start.19 = (bf16[2,128,256]{2,1,0:T(8,128)(2,1)S(1)}, bf16[2,128,256]{2,1,0:T(8,128)(2,1)S(1)}, u32[]{:S(2)}, u32[]{:S(2)}) collective-permute-start(bf16[2,128,256]{2,1,0:T(8,128)(2,1)S(1)} %get-tuple-element.71), channel_id=1, source_target_pairs={{0,1},{1,0},{2,3},{3,2},{4,5},{5,4},{6,7},{7,6},{8,9},{9,8},{10,11... | collective-permute-start | bytes 393224 | tf_op jit(solution)/shard_map/ppermute | solution.py:452
  79.0 6.3 %collective-permute-start.12 = (bf16[128,512]{1,0:T(8,128)(2,1)S(1)}, bf16[128,512]{1,0:T(8,128)(2,1)S(1)}, u32[]{:S(2)}, u32[]{:S(2)}) collective-permute-start(bf16[128,512]{1,0:T(8,128)(2,1)S(1)} %get-tuple-element.68.refs_2_.refs_0_.q_ref), channel_id=1, source_target_pairs={{0,2},{1,3},{2,0},{3,1},{4,6},{5,7},{6,4},{7,5},{8,10},{9,11},{10,... | collective-permute-start | bytes 393224 | tf_op jit(solution)/shard_map/ppermute | solution.py:452
  79.0 17.9 %collective-permute-start.11 = (bf16[1,4,128,256]{3,2,1,0:T(8,128)(2,1)S(1)}, bf16[1,4,128,256]{3,2,1,0:T(8,128)(2,1)S(1)}, u32[]{:S(2)}, u32[]{:S(2)}) collective-permute-start(bf16[1,4,128,256]{3,2,1,0:T(8,128)(2,1)S(1)} %fold.18.refs_10_), channel_id=1, source_target_pairs={{0,2},{1,3},{2,0},{3,1},{4,6},{5,7},{6,4},{7,5},{8,10},{9,11},{10,... | collective-permute-start | bytes 786440 | tf_op jit(solution)/shard_map/ppermute | solution.py:452
  81.1 4.7 %collective-permute-start.13 = (bf16[128,512]{1,0:T(8,128)(2,1)S(1)}, bf16[128,512]{1,0:T(8,128)(2,1)S(1)}, u32[]{:S(2)}, u32[]{:S(2)}) collective-permute-start(bf16[128,512]{1,0:T(8,128)(2,1)S(1)} %get-tuple-element.68.refs_2_.refs_0_.q_ref), channel_id=1, source_target_pairs={{0,1},{1,0},{2,3},{3,2},{4,5},{5,4},{6,7},{7,6},{8,9},{9,8},{10,11... | collective-permute-start | bytes 393224 | tf_op jit(solution)/shard_map/ppermute | solution.py:452
  82.5 11.3 %collective-permute-start.25 = (bf16[128,512]{1,0:T(8,128)(2,1)S(1)}, bf16[128,512]{1,0:T(8,128)(2,1)S(1)}, u32[]{:S(2)}, u32[]{:S(2)}) collective-permute-start(bf16[128,512]{1,0:T(8,128)(2,1)S(1)} %get-tuple-element.72.refs_2_.refs_0_.q_ref), channel_id=1, source_target_pairs={{0,2},{1,3},{2,0},{3,1},{4,6},{5,7},{6,4},{7,5},{8,10},{9,11},{10,... | collective-permute-start | bytes 393224 | tf_op jit(solution)/shard_map/ppermute | solution.py:452
  85.4 8.4 %collective-permute-start.14 = (bf16[128,512]{1,0:T(8,128)(2,1)S(1)}, bf16[128,512]{1,0:T(8,128)(2,1)S(1)}, u32[]{:S(2)}, u32[]{:S(2)}) collective-permute-start(bf16[128,512]{1,0:T(8,128)(2,1)S(1)} %collective-permute-done.12.refs_1_), channel_id=1, source_target_pairs={{0,1},{1,0},{2,3},{3,2},{4,5},{5,4},{6,7},{7,6},{8,9},{9,8},{10,11... | collective-permute-start | bytes 393224 | tf_op jit(solution)/shard_map/ppermute | solution.py:452
  85.7 13.4 %collective-permute-start.28 = (bf16[1,128,512]{2,1,0:T(8,128)(2,1)S(1)}, bf16[1,128,512]{2,1,0:T(8,128)(2,1)S(1)}, u32[]{:S(2)}, u32[]{:S(2)}) collective-permute-start(bf16[1,128,512]{2,1,0:T(8,128)(2,1)S(1)} %fold.20.refs_10_), channel_id=1, source_target_pairs={{0,2},{1,3},{2,0},{3,1},{4,6},{5,7},{6,4},{7,5},{8,10},{9,11},{10,... | collective-permute-start | bytes 393224 | tf_op jit(solution)/shard_map/ppermute | solution.py:452
  85.8 14.6 %collective-permute-start.26 = (bf16[128,512]{1,0:T(8,128)(2,1)S(1)}, bf16[128,512]{1,0:T(8,128)(2,1)S(1)}, u32[]{:S(2)}, u32[]{:S(2)}) collective-permute-start(bf16[128,512]{1,0:T(8,128)(2,1)S(1)} %get-tuple-element.72.refs_2_.refs_0_.q_ref), channel_id=1, source_target_pairs={{0,1},{1,0},{2,3},{3,2},{4,5},{5,4},{6,7},{7,6},{8,9},{9,8},{10,11... | collective-permute-start | bytes 393224 | tf_op jit(solution)/shard_map/ppermute | solution.py:452
  93.8 6.6 %collective-permute-start.27 = (bf16[128,512]{1,0:T(8,128)(2,1)S(1)}, bf16[128,512]{1,0:T(8,128)(2,1)S(1)}, u32[]{:S(2)}, u32[]{:S(2)}) collective-permute-start(bf16[128,512]{1,0:T(8,128)(2,1)S(1)} %collective-permute-done.25.refs_1_), channel_id=1, source_target_pairs={{0,1},{1,0},{2,3},{3,2},{4,5},{5,4},{6,7},{7,6},{8,9},{9,8},{10,11... | collective-permute-start | bytes 393224 | tf_op jit(solution)/shard_map/ppermute | solution.py:452
  93.8 4.9 %collective-permute-start.29 = (bf16[1,128,256]{2,1,0:T(8,128)(2,1)S(1)}, bf16[1,128,256]{2,1,0:T(8,128)(2,1)S(1)}, u32[]{:S(2)}, u32[]{:S(2)}) collective-permute-start(bf16[1,128,256]{2,1,0:T(8,128)(2,1)S(1)} %fold.19.refs_2_), channel_id=1, source_target_pairs={{0,2},{1,3},{2,0},{3,1},{4,6},{5,7},{6,4},{7,5},{8,10},{9,11},{10,... | collective-permute-start | bytes 196616 | tf_op jit(solution)/shard_map/ppermute | solution.py:452
  97.0 11.2 %collective-permute-start.24 = (bf16[2,128,512]{2,1,0:T(8,128)(2,1)S(1)}, bf16[2,128,512]{2,1,0:T(8,128)(2,1)S(1)}, u32[]{:S(2)}, u32[]{:S(2)}) collective-permute-start(bf16[2,128,512]{2,1,0:T(8,128)(2,1)S(1)} %get-tuple-element.76), channel_id=1, source_target_pairs={{0,1},{1,0},{2,3},{3,2},{4,5},{5,4},{6,7},{7,6},{8,9},{9,8},{10,11... | collective-permute-start | bytes 786440 | tf_op jit(solution)/shard_map/ppermute | solution.py:452
  103.6 8.8 %collective-permute-start.32 = (bf16[2,128,512]{2,1,0:T(8,128)(2,1)S(1)}, bf16[2,128,512]{2,1,0:T(8,128)(2,1)S(1)}, u32[]{:S(2)}, u32[]{:S(2)}) collective-permute-start(bf16[2,128,512]{2,1,0:T(8,128)(2,1)S(1)} %get-tuple-element.85), channel_id=1, source_target_pairs={{0,1},{1,0},{2,3},{3,2},{4,5},{5,4},{6,7},{7,6},{8,9},{9,8},{10,11... | collective-permute-start | bytes 786440 | tf_op jit(solution)/shard_map/ppermute | solution.py:452
  103.7 4.5 %collective-permute-start.21 = (bf16[128,256]{1,0:T(8,128)(2,1)S(1)}, bf16[128,256]{1,0:T(8,128)(2,1)S(1)}, u32[]{:S(2)}, u32[]{:S(2)}) collective-permute-start(bf16[128,256]{1,0:T(8,128)(2,1)S(1)} %get-tuple-element.74.refs_3_.refs_0_.q_ref), channel_id=1, source_target_pairs={{0,2},{1,3},{2,0},{3,1},{4,6},{5,7},{6,4},{7,5},{8,10},{9,11},{10,... | collective-permute-start | bytes 196616 | tf_op jit(solution)/shard_map/ppermute | solution.py:452
  105.6 4.5 %collective-permute-start.22 = (bf16[128,256]{1,0:T(8,128)(2,1)S(1)}, bf16[128,256]{1,0:T(8,128)(2,1)S(1)}, u32[]{:S(2)}, u32[]{:S(2)}) collective-permute-start(bf16[128,256]{1,0:T(8,128)(2,1)S(1)} %get-tuple-element.74.refs_3_.refs_0_.q_ref), channel_id=1, source_target_pairs={{0,1},{1,0},{2,3},{3,2},{4,5},{5,4},{6,7},{7,6},{8,9},{9,8},{10,11... | collective-permute-start | bytes 196616 | tf_op jit(solution)/shard_map/ppermute | solution.py:452
  108.3 6.0 %collective-permute-start.31 = (bf16[1,128,512]{2,1,0:T(8,128)(2,1)S(1)}, bf16[1,128,512]{2,1,0:T(8,128)(2,1)S(1)}, u32[]{:S(2)}, u32[]{:S(2)}) collective-permute-start(bf16[1,128,512]{2,1,0:T(8,128)(2,1)S(1)} %fold.21.refs_10_), channel_id=1, source_target_pairs={{0,2},{1,3},{2,0},{3,1},{4,6},{5,7},{6,4},{7,5},{8,10},{9,11},{10,... | collective-permute-start | bytes 393224 | tf_op jit(solution)/shard_map/ppermute | solution.py:452
  112.6 6.4 %collective-permute-start.34 = (bf16[1,128,512]{2,1,0:T(8,128)(2,1)S(1)}, bf16[1,128,512]{2,1,0:T(8,128)(2,1)S(1)}, u32[]{:S(2)}, u32[]{:S(2)}) collective-permute-start(bf16[1,128,512]{2,1,0:T(8,128)(2,1)S(1)} %fold.22.refs_3_), channel_id=1, source_target_pairs={{0,2},{1,3},{2,0},{3,1},{4,6},{5,7},{6,4},{7,5},{8,10},{9,11},{10,... | collective-permute-start | bytes 393224 | tf_op jit(solution)/shard_map/ppermute | solution.py:452
  114.8 4.9 %collective-permute-start.33 = (bf16[1,128,256]{2,1,0:T(8,128)(2,1)S(1)}, bf16[1,128,256]{2,1,0:T(8,128)(2,1)S(1)}, u32[]{:S(2)}, u32[]{:S(2)}) collective-permute-start(bf16[1,128,256]{2,1,0:T(8,128)(2,1)S(1)} %fold.23.refs_3_), channel_id=1, source_target_pairs={{0,2},{1,3},{2,0},{3,1},{4,6},{5,7},{6,4},{7,5},{8,10},{9,11},{10,... | collective-permute-start | bytes 196616 | tf_op jit(solution)/shard_map/ppermute | solution.py:452
  120.2 5.5 %collective-permute-start.35 = (f32[8,128]{1,0:T(8,128)S(1)}, f32[8,128]{1,0:T(8,128)S(1)}, u32[]{:S(2)}, u32[]{:S(2)}) collective-permute-start(f32[8,128]{1,0:T(8,128)S(1)} %get-tuple-element.93.refs_0_), channel_id=1, source_target_pairs={{0,4},{4,8},{8,12},{12,0},{1,5},{5,9},{9,13},{13,1},{2,6},{6,10},{... | collective-permute-start | bytes 12296 | tf_op jit(solution)/shard_map/ppermute | solution.py:478
  121.9 4.5 %collective-permute-start.36 = (f32[8,128]{1,0:T(8,128)S(1)}, f32[8,128]{1,0:T(8,128)S(1)}, u32[]{:S(2)}, u32[]{:S(2)}) collective-permute-start(f32[8,128]{1,0:T(8,128)S(1)} %get-tuple-element.93.refs_0_), channel_id=1, source_target_pairs={{0,8},{4,12},{8,0},{12,4},{1,9},{5,13},{9,1},{13,5},{2,10},{6,14},... | collective-permute-start | bytes 12296 | tf_op jit(solution)/shard_map/ppermute | solution.py:478
  124.4 3.6 %collective-permute-start.37 = (f32[8,128]{1,0:T(8,128)S(1)}, f32[8,128]{1,0:T(8,128)S(1)}, u32[]{:S(2)}, u32[]{:S(2)}) collective-permute-start(f32[8,128]{1,0:T(8,128)S(1)} %get-tuple-element.93.refs_0_), channel_id=1, source_target_pairs={{0,12},{4,0},{8,4},{12,8},{1,13},{5,1},{9,5},{13,9},{2,14},{6,2},{... | collective-permute-start | bytes 12296 | tf_op jit(solution)/shard_map/ppermute | solution.py:478
  128.4 6.4 %collective-permute-start.38 = (bf16[64,2048]{1,0:T(8,128)(2,1)S(1)}, bf16[64,2048]{1,0:T(8,128)(2,1)S(1)}, u32[]{:S(2)}, u32[]{:S(2)}) collective-permute-start(bf16[64,2048]{1,0:T(8,128)(2,1)S(1)} %get-tuple-element.95), channel_id=1, source_target_pairs={{0,2},{1,3},{2,0},{3,1},{4,6},{5,7},{6,4},{7,5},{8,10},{9,11},{10,... | collective-permute-start | bytes 786440 | tf_op jit(solution)/shard_map/ppermute | solution.py:452
  129.7 6.4 %collective-permute-start.39 = (bf16[64,2048]{1,0:T(8,128)(2,1)S(1)}, bf16[64,2048]{1,0:T(8,128)(2,1)S(1)}, u32[]{:S(2)}, u32[]{:S(2)}) collective-permute-start(bf16[64,2048]{1,0:T(8,128)(2,1)S(1)} %get-tuple-element.95), channel_id=1, source_target_pairs={{0,1},{1,0},{2,3},{3,2},{4,5},{5,4},{6,7},{7,6},{8,9},{9,8},{10,11... | collective-permute-start | bytes 786440 | tf_op jit(solution)/shard_map/ppermute | solution.py:452
  134.9 8.7 %collective-permute-start.45 = (bf16[64,2048]{1,0:T(8,128)(2,1)S(1)}, bf16[64,2048]{1,0:T(8,128)(2,1)S(1)}, u32[]{:S(2)}, u32[]{:S(2)}) collective-permute-start(bf16[64,2048]{1,0:T(8,128)(2,1)S(1)} %get-tuple-element.100), channel_id=1, source_target_pairs={{0,2},{1,3},{2,0},{3,1},{4,6},{5,7},{6,4},{7,5},{8,10},{9,11},{10,... | collective-permute-start | bytes 786440 | tf_op jit(solution)/shard_map/ppermute | solution.py:452
  139.6 8.4 %collective-permute-start.41 = (bf16[2,4,16,1024]{3,2,1,0:T(8,128)(2,1)S(1)}, bf16[2,4,16,1024]{3,2,1,0:T(8,128)(2,1)S(1)}, u32[]{:S(2)}, u32[]{:S(2)}) collective-permute-start(bf16[2,4,16,1024]{3,2,1,0:T(8,128)(2,1)S(1)} %get-tuple-element.97.refs_5_), channel_id=1, source_target_pairs={{0,4},{4,0},{8,12},{12,8},{1,5},{5,1},{9,13},{13,9},{2,6},{6,2},{1... | collective-permute-start | bytes 786440 | tf_op jit(solution)/shard_map/ppermute | solution.py:452
  139.8 10.9 %collective-permute-start.46 = (bf16[64,2048]{1,0:T(8,128)(2,1)S(1)}, bf16[64,2048]{1,0:T(8,128)(2,1)S(1)}, u32[]{:S(2)}, u32[]{:S(2)}) collective-permute-start(bf16[64,2048]{1,0:T(8,128)(2,1)S(1)} %get-tuple-element.100), channel_id=1, source_target_pairs={{0,1},{1,0},{2,3},{3,2},{4,5},{5,4},{6,7},{7,6},{8,9},{9,8},{10,11... | collective-permute-start | bytes 786440 | tf_op jit(solution)/shard_map/ppermute | solution.py:452
  143.6 7.1 %collective-permute-start.47 = (bf16[64,2048]{1,0:T(8,128)(2,1)S(1)}, bf16[64,2048]{1,0:T(8,128)(2,1)S(1)}, u32[]{:S(2)}, u32[]{:S(2)}) collective-permute-start(bf16[64,2048]{1,0:T(8,128)(2,1)S(1)} %collective-permute-done.45), channel_id=1, source_target_pairs={{0,1},{1,0},{2,3},{3,2},{4,5},{5,4},{6,7},{7,6},{8,9},{9,8},{10,11... | collective-permute-start | bytes 786440 | tf_op jit(solution)/shard_map/ppermute | solution.py:452
  146.8 11.6 %collective-permute-start.43 = (bf16[2,4,16,1024]{3,2,1,0:T(8,128)(2,1)S(1)}, bf16[2,4,16,1024]{3,2,1,0:T(8,128)(2,1)S(1)}, u32[]{:S(2)}, u32[]{:S(2)}) collective-permute-start(bf16[2,4,16,1024]{3,2,1,0:T(8,128)(2,1)S(1)} %get-tuple-element.99.refs_5_), channel_id=1, source_target_pairs={{0,4},{4,0},{8,12},{12,8},{1,5},{5,1},{9,13},{13,9},{2,6},{6,2},{1... | collective-permute-start | bytes 786440 | tf_op jit(solution)/shard_map/ppermute | solution.py:452
  148.1 10.2 %collective-permute-start.42 = (bf16[1,4,16,1024]{3,2,1,0:T(8,128)(2,1)S(1)}, bf16[1,4,16,1024]{3,2,1,0:T(8,128)(2,1)S(1)}, u32[]{:S(2)}, u32[]{:S(2)}) collective-permute-start(bf16[1,4,16,1024]{3,2,1,0:T(8,128)(2,1)S(1)} %fold.24), channel_id=1, source_target_pairs={{0,8},{4,12},{8,0},{12,4},{1,9},{5,13},{9,1},{13,5},{2,10},{6,14},... | collective-permute-start | bytes 393224 | tf_op jit(solution)/shard_map/ppermute | solution.py:452
  157.0 12.1 %collective-permute-start.48 = (bf16[2,4,16,1024]{3,2,1,0:T(8,128)(2,1)S(1)}, bf16[2,4,16,1024]{3,2,1,0:T(8,128)(2,1)S(1)}, u32[]{:S(2)}, u32[]{:S(2)}) collective-permute-start(bf16[2,4,16,1024]{3,2,1,0:T(8,128)(2,1)S(1)} %tie.10.refs_5_), channel_id=1, source_target_pairs={{0,4},{4,0},{8,12},{12,8},{1,5},{5,1},{9,13},{13,9},{2,6},{6,2},{1... | collective-permute-start | bytes 786440 | tf_op jit(solution)/shard_map/ppermute | solution.py:452
  158.4 15.9 %collective-permute-start.50 = (bf16[2,4,16,1024]{3,2,1,0:T(8,128)(2,1)S(1)}, bf16[2,4,16,1024]{3,2,1,0:T(8,128)(2,1)S(1)}, u32[]{:S(2)}, u32[]{:S(2)}) collective-permute-start(bf16[2,4,16,1024]{3,2,1,0:T(8,128)(2,1)S(1)} %tie.11), channel_id=1, source_target_pairs={{0,4},{4,0},{8,12},{12,8},{1,5},{5,1},{9,13},{13,9},{2,6},{6,2},{1... | collective-permute-start | bytes 786440 | tf_op jit(solution)/shard_map/ppermute | solution.py:452
  160.6 14.2 %collective-permute-start.44 = (bf16[1,4,16,1024]{3,2,1,0:T(8,128)(2,1)S(1)}, bf16[1,4,16,1024]{3,2,1,0:T(8,128)(2,1)S(1)}, u32[]{:S(2)}, u32[]{:S(2)}) collective-permute-start(bf16[1,4,16,1024]{3,2,1,0:T(8,128)(2,1)S(1)} %fold.25), channel_id=1, source_target_pairs={{0,8},{4,12},{8,0},{12,4},{1,9},{5,13},{9,1},{13,5},{2,10},{6,14},... | collective-permute-start | bytes 393224 | tf_op jit(solution)/shard_map/ppermute | solution.py:452
  169.2 13.2 %collective-permute-start.49 = (bf16[1,4,16,1024]{3,2,1,0:T(8,128)(2,1)S(1)}, bf16[1,4,16,1024]{3,2,1,0:T(8,128)(2,1)S(1)}, u32[]{:S(2)}, u32[]{:S(2)}) collective-permute-start(bf16[1,4,16,1024]{3,2,1,0:T(8,128)(2,1)S(1)} %fold.26), channel_id=1, source_target_pairs={{0,8},{4,12},{8,0},{12,4},{1,9},{5,13},{9,1},{13,5},{2,10},{6,14},... | collective-permute-start | bytes 393224 | tf_op jit(solution)/shard_map/ppermute | solution.py:452
  174.4 10.2 %collective-permute-start.51 = (bf16[1,4,16,1024]{3,2,1,0:T(8,128)(2,1)S(1)}, bf16[1,4,16,1024]{3,2,1,0:T(8,128)(2,1)S(1)}, u32[]{:S(2)}, u32[]{:S(2)}) collective-permute-start(bf16[1,4,16,1024]{3,2,1,0:T(8,128)(2,1)S(1)} %fold.27), channel_id=1, source_target_pairs={{0,8},{4,12},{8,0},{12,4},{1,9},{5,13},{9,1},{13,5},{2,10},{6,14},... | collective-permute-start | bytes 393224 | tf_op jit(solution)/shard_map/ppermute | solution.py:452
  (19 other events, 95.6 us)

commit v8 on v7

--- a/solution.py
+++ b/solution.py
@@ -37,7 +37,7 @@
 
 def project_kernel(parts, owners, after, at_ref, *refs):
     rows, weights = refs[:owners], refs[owners:owners + parts]
-    keep_ref, send_ref, lhs_ref = refs[owners + parts + after:][:3]
+    outs, lhs_ref = refs[owners + parts + after:-parts - 1], refs[-parts - 1]
     wides = refs[-parts:]
     zs, chunks, _, piece, _ = rows[0].shape
     depth = weights[0].shape[0]
@@ -60,19 +60,19 @@
         term = jnp.dot(lhs_ref[:, k * depth:(k + 1) * depth], rhs, preferred_element_type=f32)
         res = term if res is None else res + term
     res = res.astype(bf16)
-    half, _, each, _ = keep_ref.shape
-    for p in range(owners):
-        into = keep_ref if p < half else send_ref
-        for i in range(4):
-            into[p % half, i] = res[p * each:(p + 1) * each, i * DH:(i + 1) * DH]
+    each, first = outs[0].shape[2], 0
+    for out in outs:
+        for p in range(out.shape[0]):
+            for i in range(4):
+                out[p, i] = res[first:first + each, i * DH:(i + 1) * DH]
+            first += each
 
 
 def project(at, tokens, w, head_first, heads, after):
     zs, chunks, owners, piece, depth = tokens.shape
     half, each = owners // 2, zs * chunks * piece
     parts = 4 if depth % 512 == 0 else 1
-    shape = jax.ShapeDtypeStruct((half, 4, each, heads * DH), bf16)
-    spec = pl.BlockSpec((half, 4, each, DH), lambda j, at: (0, 0, 0, j))
+    counts = [half] + ([half // 2] * 2 if half > 1 else [half])
     return pl.pallas_call(
         functools.partial(project_kernel, parts, owners, len(after)),
         grid_spec=pltpu.PrefetchScalarGridSpec(
@@ -89,11 +89,13 @@
                 for k in range(parts)
             ]
             + anywhere(after),
-            out_specs=(spec, spec),
+            out_specs=[
+                pl.BlockSpec((n, 4, each, DH), lambda j, at: (0, 0, 0, j)) for n in counts
+            ],
             scratch_shapes=[pltpu.VMEM((owners * each, depth), bf16)]
             + [pltpu.VMEM((depth // parts * 4, DH), f32) for _ in range(parts)],
         ),
-        out_shape=(shape, shape),
+        out_shape=[jax.ShapeDtypeStruct((n, 4, each, heads * DH), bf16) for n in counts],
         compiler_params=params(),
         cost_estimate=LIGHT,
         name="project",
@@ -124,14 +126,16 @@
 
 
 def fold(terms, after=()):
-    half, tail = terms[-1].shape[0] // 2, terms[0].shape[1:]
+    half = terms[0].shape[0] // 2 if len(terms) == 2 else terms[-1].shape[0] // 2
+    tail = terms[0].shape[1:]
     steps = 2 if tail[-1] % 256 == 0 else 1
     block = (half,) + tail[:-1] + (tail[-1] // steps,)
     middle = (0,) * (len(tail) - 1)
+    firsts = [0 if t.shape[0] == half else 1 for t in terms]
     return pl.pallas_call(
         functools.partial(fold_kernel, len(terms)),
         grid=(steps,),
-        in_specs=[pl.BlockSpec(block, lambda j: (1,) + middle + (j,))] * len(terms)
+        in_specs=[pl.BlockSpec(block, lambda j, f=f: (f,) + middle + (j,)) for f in firsts]
         + anywhere(after),
         out_specs=pl.BlockSpec(block, lambda j: (0,) + middle + (j,)),
         out_shape=jax.ShapeDtypeStruct((half,) + tail, bf16),
@@ -141,22 +145,29 @@
     )(*terms, *after)
 
 
-def activate_kernel(count, *refs):
+def activate_kernel(counts, *refs):
     q_ref, rest_ref = refs[-2:]
-    for i in range(4):
-        part = silu(sum(t[0, i].astype(f32) for t in refs[:count])).astype(bf16)
-        if i == 0:
-            q_ref[...] = part
-        else:
-            rest_ref[i - 1] = part
-
-
-def activate(terms, after):
-    _, _, each, width = terms[0].shape
-    return pl.pallas_call(
-        functools.partial(activate_kernel, len(terms)),
+    first, column = 0, 0
+    for count in counts:
+        terms = refs[first:first + count]
+        span = terms[0].shape[-1]
+        for i in range(4):
+            part = silu(sum(t[0, i].astype(f32) for t in terms)).astype(bf16)
+            if i == 0:
+                q_ref[:, column:column + span] = part
+            else:
+                rest_ref[i - 1, :, column:column + span] = part
+        first += count
+        column += span
+
+
+def activate(chunks, after):
+    each, width = chunks[0][0].shape[2], sum(terms[0].shape[3] for terms in chunks)
+    flat = [term for terms in chunks for term in terms]
+    return pl.pallas_call(
+        functools.partial(activate_kernel, [len(terms) for terms in chunks]),
         grid=(1,),
-        in_specs=[pl.BlockSpec((1, 4, each, width), lambda j: (0, 0, 0, 0))] * len(terms)
+        in_specs=[pl.BlockSpec((1,) + t.shape[1:], lambda j: (0, 0, 0, 0)) for t in flat]
         + anywhere(after),
         out_specs=(
             pl.BlockSpec((each, width), lambda j: (0, 0)),
@@ -169,7 +180,33 @@
         compiler_params=params(),
         cost_estimate=LIGHT,
         name="activate",
-    )(*terms, *after)
+    )(*flat, *after)
+
+
+def edge_kernel(base_ref, start_ref, end_ref, out_ref):
+    row = lax.broadcasted_iota(jnp.int32, (DH, DH), 0)
+    for b in range(start_ref.shape[0]):
+        start, end = start_ref[b:b + 1, :], end_ref[b:b + 1, :]
+        both = jnp.where(row == 0, start, end) - base_ref[0]
+        out_ref[b * DH:(b + 1) * DH, :] = both.astype(f32).T[:, :2].astype(jnp.int32)
+
+
+def edge_columns(base, start, end):
+    count = start.shape[0]
+    lines = pl.BlockSpec((count // DH, DH), lambda j, base: (0, 0))
+    return pl.pallas_call(
+        edge_kernel,
+        grid_spec=pltpu.PrefetchScalarGridSpec(
+            num_scalar_prefetch=1,
+            grid=(1,),
+            in_specs=[lines, lines],
+            out_specs=pl.BlockSpec((count, 2), lambda j, base: (0, 0)),
+        ),
+        out_shape=jax.ShapeDtypeStruct((count, 2), jnp.int32),
+        compiler_params=params(),
+        cost_estimate=LIGHT,
+        name="edges",
+    )(base.reshape(1), start.reshape(-1, DH), end.reshape(-1, DH))
 
 
 def attend_kernel(owners, at_ref, *refs):
@@ -214,7 +251,7 @@
     owners, (each, width) = len(queries), queries[0].shape
     rows, events, half = owners * each, k_cache.shape[0], owners // 2
     first = head_first * DH
-    span = 2 * DH if width % (2 * DH) == 0 and first % (2 * DH) == 0 else DH
+    span = max(h for h in range(DH, 4 * DH, DH) if width % h == 0 and first % h == 0)
     cache = pl.BlockSpec((events, span), lambda j, at: (0, first // span + j))
     shape = jax.ShapeDtypeStruct((half, each, width), bf16)
     spec = pl.BlockSpec((half, each, span), lambda j, at: (0, 0, j))
@@ -372,7 +409,7 @@
     owners, (each, width) = len(blocks), blocks[0].shape
     zs = len(slots)
     piece = each // zs
-    span = 512 if columns % 512 == 0 else columns
+    span = max(c for c in (512, 256, columns) if columns % c == 0 and column % c == 0)
     row_spec = pl.BlockSpec((zs, piece, width), lambda j, at: (0, 0, 0))
     spec = pl.BlockSpec((zs // 2, owners, piece, span), lambda j, at: (0, 0, 0, j))
     shape = jax.ShapeDtypeStruct((zs // 2, owners, piece, columns), bf16)
@@ -454,18 +491,20 @@
     )
 
 
-def scatter(keep, got, axis, after=()):
-    terms, sent = [keep, got], got
+def scatter(keep, gots, axis, after=()):
+    terms, sent = [keep, gots[0]], gots[-1]
     for b in range(1, bits_of(axis)):
-        sent = fold(terms, after)
+        sent = fold([keep, gots[-1]] if b == 1 else terms, after)
         terms.append(swap(sent, axis, b))
     return terms, sent
 
 
-def gather(x, axis):
+def gather(x, axis, after=()):
     blocks = [x]
     for b in reversed(range(bits_of(axis))):
         blocks = blocks + [swap(block, axis, b) for block in blocks]
+        if len(blocks) == 2:
+            blocks[1] = tie(blocks[1], after)
     return blocks
 
 
@@ -487,9 +526,10 @@
     return [unit, 2 * unit, 2 * unit, 2 * unit, unit]
 
 
+GROUPS = [[0, 1], [2], [3], [4]]
 ORDER = [
-    "P0", "P1", "F0", "P2", "F1", "A0", "P3", "F2", "P4", "A1", "F3", "T0", "A2", "F4", "T1",
-    "A3", "G0", "G1", "T2", "A4", "E0", "E1", "T3", "G2", "T4", "G3", "E2", "G4", "E3", "E4",
+    "P0", "P1", "F0", "P2", "F1", "P3", "F2", "A0", "F3", "P4", "A1", "F4", "T0", "G0", "A2",
+    "T1", "A3", "G1", "E0", "T2", "G2", "T3", "E1", "G3", "E2", "E3",
 ]
 
 
@@ -514,41 +554,45 @@
     at = (place if piece % 16 == 0 else jnp.int32(0)).reshape(1)
     ordered = arrange(tokens)
     first_event = lax.axis_index("hist") * events
-    edges = arrange(jnp.stack([vis_start - first_event, vis_end - first_event], axis=1))
+    edges = arrange(edge_columns(first_event, vis_start, vis_end))
 
     sizes = head_chunks(width // DH)
     firsts = [sum(sizes[:c]) for c in range(len(sizes))]
-    last = len(sizes) - 1
-    order = ORDER
-    if last != 4:
-        order = [step + str(c) for step in "PFATGE" for c in range(last + 1)]
-    chain, terms, sums, halves, queries, parts, atts, stats = [], {}, {}, {}, {}, {}, {}, {}
+    groups, order = GROUPS, ORDER
+    if len(sizes) != 5:
+        groups = [[c] for c in range(len(sizes))]
+        order = [step + str(c) for step in "PFATGE" for c in range(len(sizes))]
+    last = len(groups) - 1
+    heads = [sum(sizes[c] for c in group) for group in groups]
+    chain, keeps, firsts_got, terms, sums = [], {}, {}, {}, {}
+    halves, queries, parts, atts, stats = {}, {}, {}, {}, {}
     for step, c in [(name[0], int(name[1:])) for name in order]:
         after = chain[-1:]
         if step == "P":
-            keep, send = project(at, ordered, w_qkvu, firsts[c], sizes[c], after)
-            before = [terms[c - 1][1]] if c >= 1 else []
-            before += [terms[c - 2][-1]] if c - 2 in terms and len(terms[c - 2]) > 2 else []
-            before += [queries[0][1]] if c == last and 0 in queries else []
-            terms[c] = [keep, swap(tie(send, before), "hist", 0)]
+            keep, *sends = project(at, ordered, w_qkvu, firsts[c], sizes[c], after)
+            before = firsts_got[c - 1] if c >= 1 else []
+            before = before + [terms[0][-1]] if c == 2 and 0 in terms else before
+            firsts_got[c] = [swap(tie(send, before), "hist", 0) for send in reversed(sends)][::-1]
+            keeps[c] = keep
             chain.append(keep)
         elif step == "F":
-            terms[c], sent = scatter(*terms[c], "hist", after)
+            terms[c], sent = scatter(keeps[c], firsts_got[c], "hist", after)
             chain.append(sent)
         elif step == "A":
-            parts[c] = activate(terms[c], after)
+            parts[c] = activate([terms[k] for k in groups[c]], after)
             queries[c] = gather(parts[c][0], "hist")
             chain.append(parts[c][0])
         elif step == "T":
-            keep, send = attend(at, queries[c], k_cache, v_cache, edges, firsts[c], after)
-            halves[c] = keep, swap(send, "hist", 0)
+            first = firsts[groups[c][0]]
+            keep, send = attend(at, queries[c], k_cache, v_cache, edges, first, after)
+            halves[c] = keep, [swap(send, "hist", 0)]
             chain.append(keep)
         elif step == "G":
             sums[c], sent = scatter(*halves[c], "hist", after)
             chain.append(sent)
         else:
             others = [stats[k] for k in range(last)] if c == last else []
-            widths = [size * DH for size in sizes[:last]] if c == last else []
+            widths = [size * DH for size in heads[:last]] if c == last else []
             atts[c], stats[c] = finish(at, edges, *parts[c], sums[c], others, widths, after)
             chain.append(atts[c])
 
@@ -557,26 +601,30 @@
     gated = gate_rows(all_stats(stats[last], "head"), atts, rests, chunks)
     columns = w_out.shape[1]
     straight = piece % 16 == 0 and zs & (zs - 1) == 0
-    groups = 2 if straight and columns % 1024 == 0 else 1
     results, sends, first_steps, ends = [], [], [], []
-    for rows in gated:
-        blocks = gather(rows, "hist")
+    for r, rows in enumerate(gated):
         results.append([])
-        for g in range(groups):
-            if straight:
-                slots = [reverse(k, bits_of("head")) for k in range(zs)]
-                span = columns // groups
-                keep, send = output(index, blocks, w_out, slots, g * span, span, sends[-1:])
-                before = first_steps[-2:-1] + ends[-3:-2]
-                send = tie(send, before)
-                sends.append(send)
-                terms, _ = scatter(keep, swap(send, "head", 0), "head")
-                first_steps.append(terms[1])
-                ends.append(terms[-1])
-            else:
-                whole = jnp.dot(jnp.concatenate(blocks), w_out, preferred_element_type=f32)
-                whole = whole.astype(bf16).reshape(owners, zs, piece, -1).swapaxes(0, 1)
-                terms = [lax.psum_scatter(whole, "head", scatter_dimension=0, tiled=True)]
+        if not straight:
+            blocks = gather(rows, "hist")
+            whole = jnp.dot(jnp.concatenate(blocks), w_out, preferred_element_type=f32)
+            whole = whole.astype(bf16).reshape(owners, zs, piece, -1).swapaxes(0, 1)
+            whole = lax.psum_scatter(whole, "head", scatter_dimension=0, tiled=True)
+            results[-1].append([whole])
+            continue
+        blocks = gather(rows, "hist", sends[-1:] + first_steps[:1])
+        slots = [reverse(k, bits_of("head")) for k in range(zs)]
+        unit = columns // 8
+        spans = [columns]
+        if unit % (2 * DH) == 0:
+            spans = [4 * unit, 4 * unit] if r == 0 else [5 * unit, 3 * unit]
+        for g, span in enumerate(spans):
+            first = sum(spans[:g])
+            keep, send = output(index, blocks, w_out, slots, first, span, sends[-1:])
+            send = tie(send, first_steps[-2:-1] + ends[-3:-2])
+            sends.append(send)
+            terms, _ = scatter(keep, [swap(send, "head", 0)], "head")
+            first_steps.append(terms[1])
+            ends.append(terms[-1])
             results[-1].append(terms)
     out = close(place, index, tokens, results)
     return out.reshape(cand // zs, -1)

time: 188 us -> 184 us (0.979)
  waiting for transfers between devices: 65.8 us -> 70.1 us
  starting transfers between devices: 37.1 us -> 33 us
  local copies, waits for them, and re-layouts: 4.28 us -> 2.4 us
    ppermute x49, starting transfers between devices: 31.5 us -> 28.3 us  [swap(): lax.ppermute(x, axis, [(i, i ^ 1 << bit) for i in range(lax.axis_size(axi...]
    ppermute x49, waiting for transfers between devices: 63.5 us -> 65.7 us  [swap(): lax.ppermute(x, axis, [(i, i ^ 1 << bit) for i in range(lax.axis_size(axi...]
    ppermute x3, waiting for transfers between devices: 2.26 us -> 4.39 us  [all_stats(): lax.ppermute(stat, axis, [(i, (i + k) % count) for i in range(count)])]
    pallas_call x5 -> x4, Pallas kernels: 13.7 us -> 12.4 us  [attend(): pl.pallas_call(functools.partial(attend_kernel, owners), grid_spec=pltpu....]
    pallas_call x14 -> x13, Pallas kernels: 3.96 us -> 4.57 us  [fold(): pl.pallas_call(functools.partial(fold_kernel, len(terms)), grid=(steps,),...]
  transfers between devices with their start and end apart: 52 -> 52, of which waited for: 20 -> 21; matrix products, arithmetic and copies ran while one was open for 2% -> 0% of each run, Pallas kernels for 37% -> 36%
where the time goes in v8:
time: 184 us
  Pallas kernels  77.7 us (42%)
  waiting for transfers between devices  70.1 us (38%)
  starting transfers between devices  33 us (18%)
  local copies, waits for them, and re-layouts  2.4 us (1%)
    ppermute x49, waiting for transfers between devices, swap(): lax.ppermute(x, axis, [(i, i ^ 1 << bit) for i in range(lax.axis_size(axi...  65.7 us
    pallas_call x5, Pallas kernels, project(): pl.pallas_call(functools.partial(project_kernel, parts, owners, len(after...  37.9 us
    ppermute x49, starting transfers between devices, swap(): lax.ppermute(x, axis, [(i, i ^ 1 << bit) for i in range(lax.axis_size(axi...  28.3 us
    pallas_call x4, Pallas kernels, output(): pl.pallas_call(functools.partial(output_kernel, owners, slots), grid_spec...  14.3 us
    pallas_call x4, Pallas kernels, attend(): pl.pallas_call(functools.partial(attend_kernel, owners), grid_spec=pltpu....  12.4 us
    ppermute x3, starting transfers between devices, all_stats(): lax.ppermute(stat, axis, [(i, (i + k) % count) for i in range(count)])  4.64 us
    pallas_call x13, Pallas kernels, fold(): pl.pallas_call(functools.partial(fold_kernel, len(terms)), grid=(steps,),...  4.57 us
    ppermute x3, waiting for transfers between devices, all_stats(): lax.ppermute(stat, axis, [(i, (i + k) % count) for i in range(count)])  4.39 us
  transfers between devices with their start and end apart: 52, of which 21 were waited for; matrix products, arithmetic and copies ran while one was open for 0% of the time, Pallas kernels for 36%

profile of v8, /device:TPU:0, one launch (start us, length us, event | category | flops | bytes accessed | tf_op | source)
XLA Modules:
  0.0 183.8 jit_solution(4011173406164314534)
XLA Ops:
  0.0 5.5 %project.5 = (bf16[2,4,128,256]{3,2,1,0:T(8,128)(2,1)S(1)}, bf16[1,4,128,256]{3,2,1,0:T(8,128)(2,1)S(1)}, bf16[1,4,128,256]{3,2,1,0:T(8,128)(2,1)S(1)}) custom-call(s32[1]{0:T(128)} %bitcast.at_ref, bf16[4,2,4,16,2048]{4,3,2,1,0:T(8,128)(2,1)} %bitcast.55, bf16[4,2,4,16,2048]{4,3,2,1,0:T(8,128)(2,1)} %bitcast.56, bf16[4,2,4,16,2048]{4,3,2,1,0:T(8,128)(2,1)} %bitcast.57, ...), custom_call_target="tpu_custom_call" | custom-call | flops 1000 | bytes 1000 | tf_op jit(solution)/shard_map/project/pallas_call | solution.py:76
  6.1 8.7 %project.6 = (bf16[2,4,128,512]{3,2,1,0:T(8,128)(2,1)S(1)}, bf16[1,4,128,512]{3,2,1,0:T(8,128)(2,1)S(1)}, bf16[1,4,128,512]{3,2,1,0:T(8,128)(2,1)S(1)}) custom-call(s32[1]{0:T(128)} %bitcast.at_ref, bf16[4,2,4,16,2048]{4,3,2,1,0:T(8,128)(2,1)} %bitcast.59, bf16[4,2,4,16,2048]{4,3,2,1,0:T(8,128)(2,1)} %bitcast.60, bf16[4,2,4,16,2048]{4,3,2,1,0:T(8,128)(2,1)} %bitcast.61, ...), custom_call_target="tpu_custom_call" | custom-call | flops 1000 | bytes 1000 | tf_op jit(solution)/shard_map/project/pallas_call | solution.py:76
  15.8 3.0 %collective-permute-start.4 = (bf16[1,4,128,256]{3,2,1,0:T(8,128)(2,1)S(1)}, bf16[1,4,128,256]{3,2,1,0:T(8,128)(2,1)S(1)}, u32[]{:S(2)}, u32[]{:S(2)}) collective-permute-start(bf16[1,4,128,256]{3,2,1,0:T(8,128)(2,1)S(1)} %fold.13.refs_8_), channel_id=1, source_target_pairs={{0,2},{1,3},{2,0},{3,1},{4,6},{5,7},{6,4},{7,5},{8,10},{9,11},{10,... | collective-permute-start | bytes 786440 | tf_op jit(solution)/shard_map/ppermute | solution.py:489
  18.7 8.7 %project.7 = (bf16[2,4,128,512]{3,2,1,0:T(8,128)(2,1)S(1)}, bf16[1,4,128,512]{3,2,1,0:T(8,128)(2,1)S(1)}, bf16[1,4,128,512]{3,2,1,0:T(8,128)(2,1)S(1)}) custom-call(s32[1]{0:T(128)} %bitcast.at_ref, bf16[4,2,4,16,2048]{4,3,2,1,0:T(8,128)(2,1)} %bitcast.63, bf16[4,2,4,16,2048]{4,3,2,1,0:T(8,128)(2,1)} %bitcast.64, bf16[4,2,4,16,2048]{4,3,2,1,0:T(8,128)(2,1)} %bitcast.65, ...), custom_call_target="tpu_custom_call" | custom-call | flops 1000 | bytes 1000 | tf_op jit(solution)/shard_map/project/pallas_call | solution.py:76
  28.5 8.8 %project.8 = (bf16[2,4,128,512]{3,2,1,0:T(8,128)(2,1)S(1)}, bf16[1,4,128,512]{3,2,1,0:T(8,128)(2,1)S(1)}, bf16[1,4,128,512]{3,2,1,0:T(8,128)(2,1)S(1)}) custom-call(s32[1]{0:T(128)} %bitcast.at_ref, bf16[4,2,4,16,2048]{4,3,2,1,0:T(8,128)(2,1)} %bitcast.67, bf16[4,2,4,16,2048]{4,3,2,1,0:T(8,128)(2,1)} %bitcast.68, bf16[4,2,4,16,2048]{4,3,2,1,0:T(8,128)(2,1)} %bitcast.69, ...), custom_call_target="tpu_custom_call" | custom-call | flops 1000 | bytes 1000 | tf_op jit(solution)/shard_map/project/pallas_call | solution.py:76
  38.2 0.9 fold.15.refs_6_
  39.1 1.9 %collective-permute-start.12 = (bf16[1,4,128,512]{3,2,1,0:T(8,128)(2,1)}, bf16[1,4,128,512]{3,2,1,0:T(8,128)(2,1)}, u32[]{:S(2)}, u32[]{:S(2)}) collective-permute-start(bf16[1,4,128,512]{3,2,1,0:T(8,128)(2,1)} %fold.15.refs_6_), channel_id=1, source_target_pairs={{0,2},{1,3},{2,0},{3,1},{4,6},{5,7},{6,4},{7,5},{8,10},{9,11},{10,... | collective-permute-start | bytes 1572872 | tf_op jit(solution)/shard_map/ppermute | solution.py:489
  41.0 1.4 collective-permute-done.8.refs_5_
  43.2 1.0 fold.16.refs_8_
  44.2 6.2 %project.9 = (bf16[2,4,128,256]{3,2,1,0:T(8,128)(2,1)S(1)}, bf16[1,4,128,256]{3,2,1,0:T(8,128)(2,1)S(1)}, bf16[1,4,128,256]{3,2,1,0:T(8,128)(2,1)}) custom-call(s32[1]{0:T(128)} %bitcast.at_ref, bf16[4,2,4,16,2048]{4,3,2,1,0:T(8,128)(2,1)} %bitcast.71, bf16[4,2,4,16,2048]{4,3,2,1,0:T(8,128)(2,1)} %bitcast.72, bf16[4,2,4,16,2048]{4,3,2,1,0:T(8,128)(2,1)} %bitcast.73, ...), custom_call_target="tpu_custom_call" | custom-call | flops 1000 | bytes 1000 | tf_op jit(solution)/shard_map/project/pallas_call | solution.py:76
  51.6 6.4 %collective-permute-done.18.refs_1_ = bf16[128,768]{1,0:T(8,128)(2,1)S(1)} collective-permute-done((bf16[128,768]{1,0:T(8,128)(2,1)S(1)}, bf16[128,768]{1,0:T(8,128)(2,1)S(1)}, u32[]{:S(2)}, u32[]{:S(2)}) %collective-permute-start.18) | collective-permute-done | bytes 196640 | tf_op jit(solution)/shard_map/ppermute | solution.py:489
  58.0 1.7 collective-permute-start.17
  59.9 1.0 copy-done.3
  61.0 1.4 activate.5
  62.3 1.1 fold.17.refs_10_
  63.5 4.1 %attend.4 = (bf16[2,128,768]{2,1,0:T(8,128)(2,1)S(1)}, bf16[2,128,768]{2,1,0:T(8,128)(2,1)S(1)}) custom-call(s32[1]{0:T(128)} %bitcast.at_ref, bf16[128,768]{1,0:T(8,128)(2,1)S(1)} %get-tuple-element.65.refs_2_.refs_0_.q_ref, bf16[128,768]{1,0:T(8,128)(2,1)S(1)} %collective-permute-done.18.refs_1_, bf16[128,768]{1,0:T(8,128)(2,1)} %collective-permute-done.19.refs_2_, ...), custom_call_target="tpu_custom_call" | custom-call | flops 1000 | bytes 1000 | tf_op jit(solution)/shard_map/attend/pallas_call | solution.py:258
  68.1 7.2 %collective-permute-done.14.refs_1_ = bf16[128,512]{1,0:T(8,128)(2,1)S(1)} collective-permute-done((bf16[128,512]{1,0:T(8,128)(2,1)S(1)}, bf16[128,512]{1,0:T(8,128)(2,1)S(1)}, u32[]{:S(2)}, u32[]{:S(2)}) %collective-permute-start.14) | collective-permute-done | bytes 131104 | tf_op jit(solution)/shard_map/ppermute | solution.py:489
  75.9 1.7 collective-permute-start.13
  77.8 1.4 activate.6
  79.2 3.2 %attend.5 = (bf16[2,128,512]{2,1,0:T(8,128)(2,1)S(1)}, bf16[2,128,512]{2,1,0:T(8,128)(2,1)S(1)}) custom-call(s32[1]{0:T(128)} %bitcast.at_ref, bf16[128,512]{1,0:T(8,128)(2,1)S(1)} %get-tuple-element.70.refs_2_.refs_0_.q_ref, bf16[128,512]{1,0:T(8,128)(2,1)S(1)} %collective-permute-done.14.refs_1_, bf16[128,512]{1,0:T(8,128)(2,1)S(1)} %collective-permute-done.15.refs_2_, ...), custom_call_target="tpu_custom_call" | custom-call | flops 1000 | bytes 1000 | tf_op jit(solution)/shard_map/attend/pallas_call | solution.py:258
  82.8 1.7 collective-permute-start.28
  84.6 4.3 %collective-permute-done.25.refs_1_ = bf16[128,512]{1,0:T(8,128)(2,1)S(1)} collective-permute-done((bf16[128,512]{1,0:T(8,128)(2,1)S(1)}, bf16[128,512]{1,0:T(8,128)(2,1)S(1)}, u32[]{:S(2)}, u32[]{:S(2)}) %collective-permute-start.25) | collective-permute-done | bytes 131104 | tf_op jit(solution)/shard_map/ppermute | solution.py:489
  89.2 3.4 %collective-permute-done.28.refs_2_ = bf16[1,128,768]{2,1,0:T(8,128)(2,1)S(1)} collective-permute-done((bf16[1,128,768]{2,1,0:T(8,128)(2,1)S(1)}, bf16[1,128,768]{2,1,0:T(8,128)(2,1)S(1)}, u32[]{:S(2)}, u32[]{:S(2)}) %collective-permute-start.28) | collective-permute-done | bytes 196640 | tf_op jit(solution)/shard_map/ppermute | solution.py:489
  93.2 3.2 %attend.6 = (bf16[2,128,512]{2,1,0:T(8,128)(2,1)S(1)}, bf16[2,128,512]{2,1,0:T(8,128)(2,1)S(1)}) custom-call(s32[1]{0:T(128)} %bitcast.at_ref, bf16[128,512]{1,0:T(8,128)(2,1)S(1)} %get-tuple-element.73.refs_10_.refs_0_.q_ref, bf16[128,512]{1,0:T(8,128)(2,1)S(1)} %collective-permute-done.25.refs_1_, bf16[128,512]{1,0:T(8,128)(2,1)S(1)} %collective-permute-done.26.refs_2_, ...), custom_call_target="tpu_custom_call" | custom-call | flops 1000 | bytes 1000 | tf_op jit(solution)/shard_map/attend/pallas_call | solution.py:258
  97.0 3.9 %collective-permute-done.22.refs_1_ = bf16[128,256]{1,0:T(8,128)(2,1)S(1)} collective-permute-done((bf16[128,256]{1,0:T(8,128)(2,1)S(1)}, bf16[128,256]{1,0:T(8,128)(2,1)S(1)}, u32[]{:S(2)}, u32[]{:S(2)}) %collective-permute-start.22) | collective-permute-done | bytes 65568 | tf_op jit(solution)/shard_map/ppermute | solution.py:489
  102.2 2.0 %attend.7 = (bf16[2,128,256]{2,1,0:T(8,128)(2,1)S(1)}, bf16[2,128,256]{2,1,0:T(8,128)(2,1)S(1)}) custom-call(s32[1]{0:T(128)} %bitcast.at_ref, bf16[128,256]{1,0:T(8,128)(2,1)S(1)} %get-tuple-element.75.refs_2_.refs_0_.q_ref, bf16[128,256]{1,0:T(8,128)(2,1)S(1)} %collective-permute-done.22.refs_1_, bf16[128,256]{1,0:T(8,128)(2,1)S(1)} %collective-permute-done.23.refs_2_, ...), custom_call_target="tpu_custom_call" | custom-call | flops 1000 | bytes 1000 | tf_op jit(solution)/shard_map/attend/pallas_call | solution.py:258
  104.4 1.0 collective-permute-start.34
  105.4 1.4 collective-permute-done.32.refs_2_
  107.8 2.7 %collective-permute-done.34.refs_2_ = bf16[1,128,512]{2,1,0:T(8,128)(2,1)S(1)} collective-permute-done((bf16[1,128,512]{2,1,0:T(8,128)(2,1)S(1)}, bf16[1,128,512]{2,1,0:T(8,128)(2,1)S(1)}, u32[]{:S(2)}, u32[]{:S(2)}) %collective-permute-start.34) | collective-permute-done | bytes 131104 | tf_op jit(solution)/shard_map/ppermute | solution.py:489
  112.2 3.6 %collective-permute-start.37 = (f32[8,128]{1,0:T(8,128)S(1)}, f32[8,128]{1,0:T(8,128)S(1)}, u32[]{:S(2)}, u32[]{:S(2)}) collective-permute-start(f32[8,128]{1,0:T(8,128)S(1)} %get-tuple-element.91.refs_0_), channel_id=1, source_target_pairs={{0,12},{4,0},{8,4},{12,8},{1,13},{5,1},{9,5},{13,9},{2,14},{6,2},{... | collective-permute-start | bytes 12296 | tf_op jit(solution)/shard_map/ppermute | solution.py:517
  115.9 1.0 collective-permute-start.35
  117.2 3.2 %collective-permute-done.36.refs_2_ = f32[8,128]{1,0:T(8,128)S(1)} collective-permute-done((f32[8,128]{1,0:T(8,128)S(1)}, f32[8,128]{1,0:T(8,128)S(1)}, u32[]{:S(2)}, u32[]{:S(2)}) %collective-permute-start.36) | collective-permute-done | bytes 4128 | tf_op jit(solution)/shard_map/ppermute | solution.py:517
  120.4 0.9 collective-permute-done.35.refs_1_
  122.5 5.6 %collective-permute-done.38 = bf16[64,2048]{1,0:T(8,128)(2,1)S(1)} collective-permute-done((bf16[64,2048]{1,0:T(8,128)(2,1)S(1)}, bf16[64,2048]{1,0:T(8,128)(2,1)S(1)}, u32[]{:S(2)}, u32[]{:S(2)}) %collective-permute-start.38) | collective-permute-done | bytes 262176 | tf_op jit(solution)/shard_map/ppermute | solution.py:489
  129.7 3.4 %output.4 = (bf16[2,4,16,1024]{3,2,1,0:T(8,128)(2,1)S(1)}, bf16[2,4,16,1024]{3,2,1,0:T(8,128)(2,1)S(1)}) custom-call(s32[1]{0:T(128)} %bitcast.1.index_ref, bf16[4,16,2048]{2,1,0:T(8,128)(2,1)S(1)} %bitcast.41, bf16[4,16,2048]{2,1,0:T(8,128)(2,1)S(1)} %bitcast.45, bf16[4,16,2048]{2,1,0:T(8,128)(2,1)S(1)} %bitcast.47, bf16[4,16,2048]{2,1,0:T(8,128)(2,1)S(1)} %bitcast.49, ...), custom_call_target="tpu_custom_call" | custom-call | flops 1000 | bytes 1000 | tf_op jit(solution)/shard_map/output/pallas_call | solution.py:416
  133.4 3.4 %output.5 = (bf16[2,4,16,1024]{3,2,1,0:T(8,128)(2,1)S(1)}, bf16[2,4,16,1024]{3,2,1,0:T(8,128)(2,1)S(1)}) custom-call(s32[1]{0:T(128)} %bitcast.1.index_ref, bf16[4,16,2048]{2,1,0:T(8,128)(2,1)S(1)} %bitcast.42, bf16[4,16,2048]{2,1,0:T(8,128)(2,1)S(1)} %bitcast.46, bf16[4,16,2048]{2,1,0:T(8,128)(2,1)S(1)} %bitcast.48, bf16[4,16,2048]{2,1,0:T(8,128)(2,1)S(1)} %bitcast.50, ...), custom_call_target="tpu_custom_call" | custom-call | flops 1000 | bytes 1000 | tf_op jit(solution)/shard_map/output/pallas_call | solution.py:416
  136.9 4.7 %collective-permute-done.41.refs_1_.refs_2_ = bf16[2,4,16,1024]{3,2,1,0:T(8,128)(2,1)S(1)} collective-permute-done((bf16[2,4,16,1024]{3,2,1,0:T(8,128)(2,1)S(1)}, bf16[2,4,16,1024]{3,2,1,0:T(8,128)(2,1)S(1)}, u32[]{:S(2)}, u32[]{:S(2)}) %collective-permute-start.41) | collective-permute-done | bytes 262176 | tf_op jit(solution)/shard_map/ppermute | solution.py:489
  141.8 1.2 collective-permute-done.47
  143.1 4.0 %output.6 = (bf16[2,4,16,1280]{3,2,1,0:T(8,128)(2,1)S(1)}, bf16[2,4,16,1280]{3,2,1,0:T(8,128)(2,1)S(1)}) custom-call(s32[1]{0:T(128)} %bitcast.1.index_ref, bf16[4,16,2048]{2,1,0:T(8,128)(2,1)S(1)} %bitcast.39, bf16[4,16,2048]{2,1,0:T(8,128)(2,1)S(1)} %bitcast.37, bf16[4,16,2048]{2,1,0:T(8,128)(2,1)S(1)} %bitcast.43, bf16[4,16,2048]{2,1,0:T(8,128)(2,1)S(1)} %bitcast.51, ...), custom_call_target="tpu_custom_call" | custom-call | flops 1000 | bytes 1000 | tf_op jit(solution)/shard_map/output/pallas_call | solution.py:416
  147.8 1.2 collective-permute-start.42
  149.0 3.4 %output.7 = (bf16[2,4,16,768]{3,2,1,0:T(8,128)(2,1)S(1)}, bf16[2,4,16,768]{3,2,1,0:T(8,128)(2,1)S(1)}) custom-call(s32[1]{0:T(128)} %bitcast.1.index_ref, bf16[4,16,2048]{2,1,0:T(8,128)(2,1)S(1)} %bitcast.40, bf16[4,16,2048]{2,1,0:T(8,128)(2,1)S(1)} %bitcast.38, bf16[4,16,2048]{2,1,0:T(8,128)(2,1)S(1)} %bitcast.44, bf16[4,16,2048]{2,1,0:T(8,128)(2,1)S(1)} %bitcast.52, ...), custom_call_target="tpu_custom_call" | custom-call | flops 1000 | bytes 1000 | tf_op jit(solution)/shard_map/output/pallas_call | solution.py:416
  152.4 5.4 %collective-permute-done.42.refs_2_ = bf16[1,4,16,1024]{3,2,1,0:T(8,128)(2,1)S(1)} collective-permute-done((bf16[1,4,16,1024]{3,2,1,0:T(8,128)(2,1)S(1)}, bf16[1,4,16,1024]{3,2,1,0:T(8,128)(2,1)S(1)}, u32[]{:S(2)}, u32[]{:S(2)}) %collective-permute-start.42) | collective-permute-done | bytes 131104 | tf_op jit(solution)/shard_map/ppermute | solution.py:489
  157.9 3.3 %collective-permute-start.50 = (bf16[2,4,16,768]{3,2,1,0:T(8,128)(2,1)S(1)}, bf16[2,4,16,768]{3,2,1,0:T(8,128)(2,1)S(1)}, u32[]{:S(2)}, u32[]{:S(2)}) collective-permute-start(bf16[2,4,16,768]{3,2,1,0:T(8,128)(2,1)S(1)} %tie.21), channel_id=1, source_target_pairs={{0,4},{4,0},{8,12},{12,8},{1,5},{5,1},{9,13},{13,9},{2,6},{6,2},{1... | collective-permute-start | bytes 589832 | tf_op jit(solution)/shard_map/ppermute | solution.py:489
  161.6 2.9 %collective-permute-start.44 = (bf16[1,4,16,1024]{3,2,1,0:T(8,128)(2,1)S(1)}, bf16[1,4,16,1024]{3,2,1,0:T(8,128)(2,1)S(1)}, u32[]{:S(2)}, u32[]{:S(2)}) collective-permute-start(bf16[1,4,16,1024]{3,2,1,0:T(8,128)(2,1)S(1)} %fold.23), channel_id=1, source_target_pairs={{0,8},{4,12},{8,0},{12,4},{1,9},{5,13},{9,1},{13,5},{2,10},{6,14},... | collective-permute-start | bytes 393224 | tf_op jit(solution)/shard_map/ppermute | solution.py:489
  164.5 4.0 %collective-permute-done.50.refs_1_.refs_10_ = bf16[2,4,16,768]{3,2,1,0:T(8,128)(2,1)S(1)} collective-permute-done((bf16[2,4,16,768]{3,2,1,0:T(8,128)(2,1)S(1)}, bf16[2,4,16,768]{3,2,1,0:T(8,128)(2,1)S(1)}, u32[]{:S(2)}, u32[]{:S(2)}) %collective-permute-start.50) | collective-permute-done | bytes 196640 | tf_op jit(solution)/shard_map/ppermute | solution.py:489
  169.5 10.6 %collective-permute-done.44.refs_5_ = bf16[1,4,16,1024]{3,2,1,0:T(8,128)(2,1)S(1)} collective-permute-done((bf16[1,4,16,1024]{3,2,1,0:T(8,128)(2,1)S(1)}, bf16[1,4,16,1024]{3,2,1,0:T(8,128)(2,1)S(1)}, u32[]{:S(2)}, u32[]{:S(2)}) %collective-permute-start.44) | collective-permute-done | bytes 131104 | tf_op jit(solution)/shard_map/ppermute | solution.py:489
  180.1 1.1 collective-permute-done.51.refs_11_
  181.2 2.6 %close.1 = bf16[8,16,2048]{2,1,0:T(8,128)(2,1)} custom-call(s32[2]{0:T(128)S(1)} %pad_add_fusion.at_ref, bf16[32,16,2048]{2,1,0:T(8,128)(2,1)} %bitcast.75, bf16[2,4,16,1024]{3,2,1,0:T(8,128)(2,1)S(1)} %get-tuple-element.94.refs_0_, bf16[2,4,16,1024]{3,2,1,0:T(8,128)(2,1)S(1)} %collective-permute-done.41.refs_1_.refs_2_, ...), custom_call_target="tpu_custom_call" | custom-call | flops 1000 | bytes 1000 | tf_op jit(solution)/shard_map/close/pallas_call | solution.py:458
  (125 shorter events, 18.7 us)
Async XLA Ops:
  5.5 9.4 %collective-permute-start = (bf16[1,4,128,256]{3,2,1,0:T(8,128)(2,1)S(1)}, bf16[1,4,128,256]{3,2,1,0:T(8,128)(2,1)S(1)}, u32[]{:S(2)}, u32[]{:S(2)}) collective-permute-start(bf16[1,4,128,256]{3,2,1,0:T(8,128)(2,1)S(1)} %get-tuple-element.57), channel_id=1, source_target_pairs={{0,1},{1,0},{2,3},{3,2},{4,5},{5,4},{6,7},{7,6},{8,9},{9,8},{10,11... | collective-permute-start | bytes 786440 | tf_op jit(solution)/shard_map/ppermute | solution.py:489
  6.1 8.8 %collective-permute-start.1 = (bf16[1,4,128,256]{3,2,1,0:T(8,128)(2,1)S(1)}, bf16[1,4,128,256]{3,2,1,0:T(8,128)(2,1)S(1)}, u32[]{:S(2)}, u32[]{:S(2)}) collective-permute-start(bf16[1,4,128,256]{3,2,1,0:T(8,128)(2,1)S(1)} %get-tuple-element.58), channel_id=1, source_target_pairs={{0,1},{1,0},{2,3},{3,2},{4,5},{5,4},{6,7},{7,6},{8,9},{9,8},{10,11... | collective-permute-start | bytes 786440 | tf_op jit(solution)/shard_map/ppermute | solution.py:489
  14.9 12.6 %collective-permute-start.3 = (bf16[1,4,128,512]{3,2,1,0:T(8,128)(2,1)S(1)}, bf16[1,4,128,512]{3,2,1,0:T(8,128)(2,1)S(1)}, u32[]{:S(2)}, u32[]{:S(2)}) collective-permute-start(bf16[1,4,128,512]{3,2,1,0:T(8,128)(2,1)S(1)} %tie.12), channel_id=1, source_target_pairs={{0,1},{1,0},{2,3},{3,2},{4,5},{5,4},{6,7},{7,6},{8,9},{9,8},{10,11... | collective-permute-start | bytes 1572872 | tf_op jit(solution)/shard_map/ppermute | solution.py:489
  15.4 12.1 %collective-permute-start.2 = (bf16[1,4,128,512]{3,2,1,0:T(8,128)(2,1)S(1)}, bf16[1,4,128,512]{3,2,1,0:T(8,128)(2,1)S(1)}, u32[]{:S(2)}, u32[]{:S(2)}) collective-permute-start(bf16[1,4,128,512]{3,2,1,0:T(8,128)(2,1)S(1)} %tie.11), channel_id=1, source_target_pairs={{0,1},{1,0},{2,3},{3,2},{4,5},{5,4},{6,7},{7,6},{8,9},{9,8},{10,11... | collective-permute-start | bytes 1572872 | tf_op jit(solution)/shard_map/ppermute | solution.py:489
  15.8 11.7 %collective-permute-start.4 = (bf16[1,4,128,256]{3,2,1,0:T(8,128)(2,1)S(1)}, bf16[1,4,128,256]{3,2,1,0:T(8,128)(2,1)S(1)}, u32[]{:S(2)}, u32[]{:S(2)}) collective-permute-start(bf16[1,4,128,256]{3,2,1,0:T(8,128)(2,1)S(1)} %fold.13.refs_8_), channel_id=1, source_target_pairs={{0,2},{1,3},{2,0},{3,1},{4,6},{5,7},{6,4},{7,5},{8,10},{9,11},{10,... | collective-permute-start | bytes 786440 | tf_op jit(solution)/shard_map/ppermute | solution.py:489
  27.5 9.8 %collective-permute-start.6 = (bf16[1,4,128,512]{3,2,1,0:T(8,128)(2,1)S(1)}, bf16[1,4,128,512]{3,2,1,0:T(8,128)(2,1)S(1)}, u32[]{:S(2)}, u32[]{:S(2)}) collective-permute-start(bf16[1,4,128,512]{3,2,1,0:T(8,128)(2,1)S(1)} %tie.14), channel_id=1, source_target_pairs={{0,1},{1,0},{2,3},{3,2},{4,5},{5,4},{6,7},{7,6},{8,9},{9,8},{10,11... | collective-permute-start | bytes 1572872 | tf_op jit(solution)/shard_map/ppermute | solution.py:489
  27.6 9.7 %collective-permute-start.5 = (bf16[1,4,128,512]{3,2,1,0:T(8,128)(2,1)S(1)}, bf16[1,4,128,512]{3,2,1,0:T(8,128)(2,1)S(1)}, u32[]{:S(2)}, u32[]{:S(2)}) collective-permute-start(bf16[1,4,128,512]{3,2,1,0:T(8,128)(2,1)S(1)} %tie.13), channel_id=1, source_target_pairs={{0,1},{1,0},{2,3},{3,2},{4,5},{5,4},{6,7},{7,6},{8,9},{9,8},{10,11... | collective-permute-start | bytes 1572872 | tf_op jit(solution)/shard_map/ppermute | solution.py:489
  28.4 14.0 %collective-permute-start.8 = (bf16[1,4,128,512]{3,2,1,0:T(8,128)(2,1)S(1)}, bf16[1,4,128,512]{3,2,1,0:T(8,128)(2,1)S(1)}, u32[]{:S(2)}, u32[]{:S(2)}) collective-permute-start(bf16[1,4,128,512]{3,2,1,0:T(8,128)(2,1)S(1)} %fold.14.refs_8_), channel_id=1, source_target_pairs={{0,2},{1,3},{2,0},{3,1},{4,6},{5,7},{6,4},{7,5},{8,10},{9,11},{10,... | collective-permute-start | bytes 1572872 | tf_op jit(solution)/shard_map/ppermute | solution.py:489
  37.3 5.9 %collective-permute-start.7 = (bf16[1,4,128,512]{3,2,1,0:T(8,128)(2,1)S(1)}, bf16[1,4,128,512]{3,2,1,0:T(8,128)(2,1)S(1)}, u32[]{:S(2)}, u32[]{:S(2)}) collective-permute-start(bf16[1,4,128,512]{3,2,1,0:T(8,128)(2,1)S(1)} %tie.15), channel_id=1, source_target_pairs={{0,1},{1,0},{2,3},{3,2},{4,5},{5,4},{6,7},{7,6},{8,9},{9,8},{10,11... | collective-permute-start | bytes 1572872 | tf_op jit(solution)/shard_map/ppermute | solution.py:489
  38.1 13.0 %collective-permute-start.9 = (bf16[1,4,128,512]{3,2,1,0:T(8,128)(2,1)S(1)}, bf16[1,4,128,512]{3,2,1,0:T(8,128)(2,1)S(1)}, u32[]{:S(2)}, u32[]{:S(2)}) collective-permute-start(bf16[1,4,128,512]{3,2,1,0:T(8,128)(2,1)S(1)} %tie.16), channel_id=1, source_target_pairs={{0,1},{1,0},{2,3},{3,2},{4,5},{5,4},{6,7},{7,6},{8,9},{9,8},{10,11... | collective-permute-start | bytes 1572872 | tf_op jit(solution)/shard_map/ppermute | solution.py:489
  39.1 20.8 %collective-permute-start.12 = (bf16[1,4,128,512]{3,2,1,0:T(8,128)(2,1)}, bf16[1,4,128,512]{3,2,1,0:T(8,128)(2,1)}, u32[]{:S(2)}, u32[]{:S(2)}) collective-permute-start(bf16[1,4,128,512]{3,2,1,0:T(8,128)(2,1)} %fold.15.refs_6_), channel_id=1, source_target_pairs={{0,2},{1,3},{2,0},{3,1},{4,6},{5,7},{6,4},{7,5},{8,10},{9,11},{10,... | collective-permute-start | bytes 1572872 | tf_op jit(solution)/shard_map/ppermute | solution.py:489
  42.9 15.1 %collective-permute-start.18 = (bf16[128,768]{1,0:T(8,128)(2,1)S(1)}, bf16[128,768]{1,0:T(8,128)(2,1)S(1)}, u32[]{:S(2)}, u32[]{:S(2)}) collective-permute-start(bf16[128,768]{1,0:T(8,128)(2,1)S(1)} %get-tuple-element.65.refs_2_.refs_0_.q_ref), channel_id=1, source_target_pairs={{0,2},{1,3},{2,0},{3,1},{4,6},{5,7},{6,4},{7,5},{8,10},{9,11},{10,... | collective-permute-start | bytes 589832 | tf_op jit(solution)/shard_map/ppermute | solution.py:489
  51.1 11.2 %collective-permute-start.11 = (bf16[1,4,128,256]{3,2,1,0:T(8,128)(2,1)}, bf16[1,4,128,256]{3,2,1,0:T(8,128)(2,1)}, u32[]{:S(2)}, u32[]{:S(2)}) collective-permute-start(bf16[1,4,128,256]{3,2,1,0:T(8,128)(2,1)} %tie.18), channel_id=1, source_target_pairs={{0,1},{1,0},{2,3},{3,2},{4,5},{5,4},{6,7},{7,6},{8,9},{9,8},{10,11... | collective-permute-start | bytes 786440 | tf_op jit(solution)/shard_map/ppermute | solution.py:489
  51.1 12.3 %collective-permute-start.19 = (bf16[128,768]{1,0:T(8,128)(2,1)S(1)}, bf16[128,768]{1,0:T(8,128)(2,1)}, u32[]{:S(2)}, u32[]{:S(2)}) collective-permute-start(bf16[128,768]{1,0:T(8,128)(2,1)S(1)} %get-tuple-element.65.refs_2_.refs_0_.q_ref), channel_id=1, source_target_pairs={{0,1},{1,0},{2,3},{3,2},{4,5},{5,4},{6,7},{7,6},{8,9},{9,8},{10,11... | collective-permute-start | bytes 589832 | tf_op jit(solution)/shard_map/ppermute | solution.py:489
  58.0 5.4 %collective-permute-start.20 = (bf16[128,768]{1,0:T(8,128)(2,1)S(1)}, bf16[128,768]{1,0:T(8,128)(2,1)}, u32[]{:S(2)}, u32[]{:S(2)}) collective-permute-start(bf16[128,768]{1,0:T(8,128)(2,1)S(1)} %collective-permute-done.18.refs_1_), channel_id=1, source_target_pairs={{0,1},{1,0},{2,3},{3,2},{4,5},{5,4},{6,7},{7,6},{8,9},{9,8},{10,11... | collective-permute-start | bytes 589832 | tf_op jit(solution)/shard_map/ppermute | solution.py:489
  58.0 19.8 %collective-permute-start.17 = (bf16[1,4,128,512]{3,2,1,0:T(8,128)(2,1)}, bf16[1,4,128,512]{3,2,1,0:T(8,128)(2,1)}, u32[]{:S(2)}, u32[]{:S(2)}) collective-permute-start(bf16[1,4,128,512]{3,2,1,0:T(8,128)(2,1)} %fold.16.refs_8_), channel_id=1, source_target_pairs={{0,2},{1,3},{2,0},{3,1},{4,6},{5,7},{6,4},{7,5},{8,10},{9,11},{10,... | collective-permute-start | bytes 1572872 | tf_op jit(solution)/shard_map/ppermute | solution.py:489
  67.5 8.3 %collective-permute-start.21 = (bf16[2,128,768]{2,1,0:T(8,128)(2,1)S(1)}, bf16[2,128,768]{2,1,0:T(8,128)(2,1)S(1)}, u32[]{:S(2)}, u32[]{:S(2)}) collective-permute-start(bf16[2,128,768]{2,1,0:T(8,128)(2,1)S(1)} %get-tuple-element.72), channel_id=1, source_target_pairs={{0,1},{1,0},{2,3},{3,2},{4,5},{5,4},{6,7},{7,6},{8,9},{9,8},{10,11... | collective-permute-start | bytes 1179656 | tf_op jit(solution)/shard_map/ppermute | solution.py:489
  67.8 7.5 %collective-permute-start.14 = (bf16[128,512]{1,0:T(8,128)(2,1)S(1)}, bf16[128,512]{1,0:T(8,128)(2,1)S(1)}, u32[]{:S(2)}, u32[]{:S(2)}) collective-permute-start(bf16[128,512]{1,0:T(8,128)(2,1)S(1)} %get-tuple-element.70.refs_2_.refs_0_.q_ref), channel_id=1, source_target_pairs={{0,2},{1,3},{2,0},{3,1},{4,6},{5,7},{6,4},{7,5},{8,10},{9,11},{10,... | collective-permute-start | bytes 393224 | tf_op jit(solution)/shard_map/ppermute | solution.py:489
  68.1 11.1 %collective-permute-start.15 = (bf16[128,512]{1,0:T(8,128)(2,1)S(1)}, bf16[128,512]{1,0:T(8,128)(2,1)S(1)}, u32[]{:S(2)}, u32[]{:S(2)}) collective-permute-start(bf16[128,512]{1,0:T(8,128)(2,1)S(1)} %get-tuple-element.70.refs_2_.refs_0_.q_ref), channel_id=1, source_target_pairs={{0,1},{1,0},{2,3},{3,2},{4,5},{5,4},{6,7},{7,6},{8,9},{9,8},{10,11... | collective-permute-start | bytes 393224 | tf_op jit(solution)/shard_map/ppermute | solution.py:489
  75.4 3.8 %collective-permute-start.16 = (bf16[128,512]{1,0:T(8,128)(2,1)S(1)}, bf16[128,512]{1,0:T(8,128)(2,1)S(1)}, u32[]{:S(2)}, u32[]{:S(2)}) collective-permute-start(bf16[128,512]{1,0:T(8,128)(2,1)S(1)} %collective-permute-done.14.refs_1_), channel_id=1, source_target_pairs={{0,1},{1,0},{2,3},{3,2},{4,5},{5,4},{6,7},{7,6},{8,9},{9,8},{10,11... | collective-permute-start | bytes 393224 | tf_op jit(solution)/shard_map/ppermute | solution.py:489
  75.4 9.2 %collective-permute-start.10 = (bf16[1,4,128,256]{3,2,1,0:T(8,128)(2,1)S(1)}, bf16[1,4,128,256]{3,2,1,0:T(8,128)(2,1)S(1)}, u32[]{:S(2)}, u32[]{:S(2)}) collective-permute-start(bf16[1,4,128,256]{3,2,1,0:T(8,128)(2,1)S(1)} %tie.17), channel_id=1, source_target_pairs={{0,1},{1,0},{2,3},{3,2},{4,5},{5,4},{6,7},{7,6},{8,9},{9,8},{10,11... | collective-permute-start | bytes 786440 | tf_op jit(solution)/shard_map/ppermute | solution.py:489
  75.9 12.9 %collective-permute-start.13 = (bf16[1,4,128,256]{3,2,1,0:T(8,128)(2,1)S(1)}, bf16[1,4,128,256]{3,2,1,0:T(8,128)(2,1)S(1)}, u32[]{:S(2)}, u32[]{:S(2)}) collective-permute-start(bf16[1,4,128,256]{3,2,1,0:T(8,128)(2,1)S(1)} %fold.17.refs_10_), channel_id=1, source_target_pairs={{0,2},{1,3},{2,0},{3,1},{4,6},{5,7},{6,4},{7,5},{8,10},{9,11},{10,... | collective-permute-start | bytes 786440 | tf_op jit(solution)/shard_map/ppermute | solution.py:489
  82.4 6.6 %collective-permute-start.29 = (bf16[2,128,512]{2,1,0:T(8,128)(2,1)S(1)}, bf16[2,128,512]{2,1,0:T(8,128)(2,1)S(1)}, u32[]{:S(2)}, u32[]{:S(2)}) collective-permute-start(bf16[2,128,512]{2,1,0:T(8,128)(2,1)S(1)} %get-tuple-element.78), channel_id=1, source_target_pairs={{0,1},{1,0},{2,3},{3,2},{4,5},{5,4},{6,7},{7,6},{8,9},{9,8},{10,11... | collective-permute-start | bytes 786440 | tf_op jit(solution)/shard_map/ppermute | solution.py:489
  82.5 6.4 %collective-permute-start.25 = (bf16[128,512]{1,0:T(8,128)(2,1)S(1)}, bf16[128,512]{1,0:T(8,128)(2,1)S(1)}, u32[]{:S(2)}, u32[]{:S(2)}) collective-permute-start(bf16[128,512]{1,0:T(8,128)(2,1)S(1)} %get-tuple-element.73.refs_10_.refs_0_.q_ref), channel_id=1, source_target_pairs={{0,2},{1,3},{2,0},{3,1},{4,6},{5,7},{6,4},{7,5},{8,10},{9,11},{10,... | collective-permute-start | bytes 393224 | tf_op jit(solution)/shard_map/ppermute | solution.py:489
  82.8 9.8 %collective-permute-start.28 = (bf16[1,128,768]{2,1,0:T(8,128)(2,1)S(1)}, bf16[1,128,768]{2,1,0:T(8,128)(2,1)S(1)}, u32[]{:S(2)}, u32[]{:S(2)}) collective-permute-start(bf16[1,128,768]{2,1,0:T(8,128)(2,1)S(1)} %fold.18.refs_3_), channel_id=1, source_target_pairs={{0,2},{1,3},{2,0},{3,1},{4,6},{5,7},{6,4},{7,5},{8,10},{9,11},{10,... | collective-permute-start | bytes 589832 | tf_op jit(solution)/shard_map/ppermute | solution.py:489
  84.6 8.6 %collective-permute-start.26 = (bf16[128,512]{1,0:T(8,128)(2,1)S(1)}, bf16[128,512]{1,0:T(8,128)(2,1)S(1)}, u32[]{:S(2)}, u32[]{:S(2)}) collective-permute-start(bf16[128,512]{1,0:T(8,128)(2,1)S(1)} %get-tuple-element.73.refs_10_.refs_0_.q_ref), channel_id=1, source_target_pairs={{0,1},{1,0},{2,3},{3,2},{4,5},{5,4},{6,7},{7,6},{8,9},{9,8},{10,11... | collective-permute-start | bytes 393224 | tf_op jit(solution)/shard_map/ppermute | solution.py:489
  88.8 4.3 %collective-permute-start.27 = (bf16[128,512]{1,0:T(8,128)(2,1)S(1)}, bf16[128,512]{1,0:T(8,128)(2,1)S(1)}, u32[]{:S(2)}, u32[]{:S(2)}) collective-permute-start(bf16[128,512]{1,0:T(8,128)(2,1)S(1)} %collective-permute-done.25.refs_1_), channel_id=1, source_target_pairs={{0,1},{1,0},{2,3},{3,2},{4,5},{5,4},{6,7},{7,6},{8,9},{9,8},{10,11... | collective-permute-start | bytes 393224 | tf_op jit(solution)/shard_map/ppermute | solution.py:489
  96.3 5.0 %collective-permute-start.30 = (bf16[2,128,512]{2,1,0:T(8,128)(2,1)S(1)}, bf16[2,128,512]{2,1,0:T(8,128)(2,1)S(1)}, u32[]{:S(2)}, u32[]{:S(2)}) collective-permute-start(bf16[2,128,512]{2,1,0:T(8,128)(2,1)S(1)} %get-tuple-element.81), channel_id=1, source_target_pairs={{0,1},{1,0},{2,3},{3,2},{4,5},{5,4},{6,7},{7,6},{8,9},{9,8},{10,11... | collective-permute-start | bytes 786440 | tf_op jit(solution)/shard_map/ppermute | solution.py:489
  96.4 4.5 %collective-permute-start.22 = (bf16[128,256]{1,0:T(8,128)(2,1)S(1)}, bf16[128,256]{1,0:T(8,128)(2,1)S(1)}, u32[]{:S(2)}, u32[]{:S(2)}) collective-permute-start(bf16[128,256]{1,0:T(8,128)(2,1)S(1)} %get-tuple-element.75.refs_2_.refs_0_.q_ref), channel_id=1, source_target_pairs={{0,2},{1,3},{2,0},{3,1},{4,6},{5,7},{6,4},{7,5},{8,10},{9,11},{10,... | collective-permute-start | bytes 196616 | tf_op jit(solution)/shard_map/ppermute | solution.py:489
  96.8 4.6 %collective-permute-start.23 = (bf16[128,256]{1,0:T(8,128)(2,1)S(1)}, bf16[128,256]{1,0:T(8,128)(2,1)S(1)}, u32[]{:S(2)}, u32[]{:S(2)}) collective-permute-start(bf16[128,256]{1,0:T(8,128)(2,1)S(1)} %get-tuple-element.75.refs_2_.refs_0_.q_ref), channel_id=1, source_target_pairs={{0,1},{1,0},{2,3},{3,2},{4,5},{5,4},{6,7},{7,6},{8,9},{9,8},{10,11... | collective-permute-start | bytes 196616 | tf_op jit(solution)/shard_map/ppermute | solution.py:489
  100.9 5.9 %collective-permute-start.32 = (bf16[1,128,512]{2,1,0:T(8,128)(2,1)S(1)}, bf16[1,128,512]{2,1,0:T(8,128)(2,1)S(1)}, u32[]{:S(2)}, u32[]{:S(2)}) collective-permute-start(bf16[1,128,512]{2,1,0:T(8,128)(2,1)S(1)} %fold.19.refs_3_), channel_id=1, source_target_pairs={{0,2},{1,3},{2,0},{3,1},{4,6},{5,7},{6,4},{7,5},{8,10},{9,11},{10,... | collective-permute-start | bytes 393224 | tf_op jit(solution)/shard_map/ppermute | solution.py:489
  104.4 6.1 %collective-permute-start.34 = (bf16[1,128,512]{2,1,0:T(8,128)(2,1)S(1)}, bf16[1,128,512]{2,1,0:T(8,128)(2,1)S(1)}, u32[]{:S(2)}, u32[]{:S(2)}) collective-permute-start(bf16[1,128,512]{2,1,0:T(8,128)(2,1)S(1)} %fold.20.refs_10_), channel_id=1, source_target_pairs={{0,2},{1,3},{2,0},{3,1},{4,6},{5,7},{6,4},{7,5},{8,10},{9,11},{10,... | collective-permute-start | bytes 393224 | tf_op jit(solution)/shard_map/ppermute | solution.py:489
  107.4 4.3 %collective-permute-start.33 = (bf16[1,128,256]{2,1,0:T(8,128)(2,1)S(1)}, bf16[1,128,256]{2,1,0:T(8,128)(2,1)S(1)}, u32[]{:S(2)}, u32[]{:S(2)}) collective-permute-start(bf16[1,128,256]{2,1,0:T(8,128)(2,1)S(1)} %fold.21.refs_3_), channel_id=1, source_target_pairs={{0,2},{1,3},{2,0},{3,1},{4,6},{5,7},{6,4},{7,5},{8,10},{9,11},{10,... | collective-permute-start | bytes 196616 | tf_op jit(solution)/shard_map/ppermute | solution.py:489
  112.2 5.0 %collective-permute-start.37 = (f32[8,128]{1,0:T(8,128)S(1)}, f32[8,128]{1,0:T(8,128)S(1)}, u32[]{:S(2)}, u32[]{:S(2)}) collective-permute-start(f32[8,128]{1,0:T(8,128)S(1)} %get-tuple-element.91.refs_0_), channel_id=1, source_target_pairs={{0,12},{4,0},{8,4},{12,8},{1,13},{5,1},{9,5},{13,9},{2,14},{6,2},{... | collective-permute-start | bytes 12296 | tf_op jit(solution)/shard_map/ppermute | solution.py:517
  115.9 4.5 %collective-permute-start.36 = (f32[8,128]{1,0:T(8,128)S(1)}, f32[8,128]{1,0:T(8,128)S(1)}, u32[]{:S(2)}, u32[]{:S(2)}) collective-permute-start(f32[8,128]{1,0:T(8,128)S(1)} %get-tuple-element.91.refs_0_), channel_id=1, source_target_pairs={{0,8},{4,12},{8,0},{12,4},{1,9},{5,13},{9,1},{13,5},{2,10},{6,14},... | collective-permute-start | bytes 12296 | tf_op jit(solution)/shard_map/ppermute | solution.py:517
  115.9 5.4 %collective-permute-start.35 = (f32[8,128]{1,0:T(8,128)S(1)}, f32[8,128]{1,0:T(8,128)S(1)}, u32[]{:S(2)}, u32[]{:S(2)}) collective-permute-start(f32[8,128]{1,0:T(8,128)S(1)} %get-tuple-element.91.refs_0_), channel_id=1, source_target_pairs={{0,4},{4,8},{8,12},{12,0},{1,5},{5,9},{9,13},{13,1},{2,6},{6,10},{... | collective-permute-start | bytes 12296 | tf_op jit(solution)/shard_map/ppermute | solution.py:517
  121.7 6.4 %collective-permute-start.38 = (bf16[64,2048]{1,0:T(8,128)(2,1)S(1)}, bf16[64,2048]{1,0:T(8,128)(2,1)S(1)}, u32[]{:S(2)}, u32[]{:S(2)}) collective-permute-start(bf16[64,2048]{1,0:T(8,128)(2,1)S(1)} %get-tuple-element.93), channel_id=1, source_target_pairs={{0,2},{1,3},{2,0},{3,1},{4,6},{5,7},{6,4},{7,5},{8,10},{9,11},{10,... | collective-permute-start | bytes 786440 | tf_op jit(solution)/shard_map/ppermute | solution.py:489
  122.5 6.4 %collective-permute-start.39 = (bf16[64,2048]{1,0:T(8,128)(2,1)S(1)}, bf16[64,2048]{1,0:T(8,128)(2,1)S(1)}, u32[]{:S(2)}, u32[]{:S(2)}) collective-permute-start(bf16[64,2048]{1,0:T(8,128)(2,1)S(1)} %get-tuple-element.93), channel_id=1, source_target_pairs={{0,1},{1,0},{2,3},{3,2},{4,5},{5,4},{6,7},{7,6},{8,9},{9,8},{10,11... | collective-permute-start | bytes 786440 | tf_op jit(solution)/shard_map/ppermute | solution.py:489
  128.1 8.7 %collective-permute-start.45 = (bf16[64,2048]{1,0:T(8,128)(2,1)S(1)}, bf16[64,2048]{1,0:T(8,128)(2,1)S(1)}, u32[]{:S(2)}, u32[]{:S(2)}) collective-permute-start(bf16[64,2048]{1,0:T(8,128)(2,1)S(1)} %get-tuple-element.98), channel_id=1, source_target_pairs={{0,2},{1,3},{2,0},{3,1},{4,6},{5,7},{6,4},{7,5},{8,10},{9,11},{10,... | collective-permute-start | bytes 786440 | tf_op jit(solution)/shard_map/ppermute | solution.py:489
  133.1 8.4 %collective-permute-start.41 = (bf16[2,4,16,1024]{3,2,1,0:T(8,128)(2,1)S(1)}, bf16[2,4,16,1024]{3,2,1,0:T(8,128)(2,1)S(1)}, u32[]{:S(2)}, u32[]{:S(2)}) collective-permute-start(bf16[2,4,16,1024]{3,2,1,0:T(8,128)(2,1)S(1)} %get-tuple-element.95.refs_5_), channel_id=1, source_target_pairs={{0,4},{4,0},{8,12},{12,8},{1,5},{5,1},{9,13},{13,9},{2,6},{6,2},{1... | collective-permute-start | bytes 786440 | tf_op jit(solution)/shard_map/ppermute | solution.py:489
  133.2 8.6 %collective-permute-start.46 = (bf16[64,2048]{1,0:T(8,128)(2,1)S(1)}, bf16[64,2048]{1,0:T(8,128)(2,1)S(1)}, u32[]{:S(2)}, u32[]{:S(2)}) collective-permute-start(bf16[64,2048]{1,0:T(8,128)(2,1)S(1)} %get-tuple-element.98), channel_id=1, source_target_pairs={{0,1},{1,0},{2,3},{3,2},{4,5},{5,4},{6,7},{7,6},{8,9},{9,8},{10,11... | collective-permute-start | bytes 786440 | tf_op jit(solution)/shard_map/ppermute | solution.py:489
  141.5 10.9 %collective-permute-start.43 = (bf16[2,4,16,1024]{3,2,1,0:T(8,128)(2,1)S(1)}, bf16[2,4,16,1024]{3,2,1,0:T(8,128)(2,1)S(1)}, u32[]{:S(2)}, u32[]{:S(2)}) collective-permute-start(bf16[2,4,16,1024]{3,2,1,0:T(8,128)(2,1)S(1)} %get-tuple-element.97.refs_1_.refs_5_), channel_id=1, source_target_pairs={{0,4},{4,0},{8,12},{12,8},{1,5},{5,1},{9,13},{13,9},{2,6},{6,2},{1... | collective-permute-start | bytes 786440 | tf_op jit(solution)/shard_map/ppermute | solution.py:489
  147.1 14.1 %collective-permute-start.48 = (bf16[2,4,16,1280]{3,2,1,0:T(8,128)(2,1)S(1)}, bf16[2,4,16,1280]{3,2,1,0:T(8,128)(2,1)S(1)}, u32[]{:S(2)}, u32[]{:S(2)}) collective-permute-start(bf16[2,4,16,1280]{3,2,1,0:T(8,128)(2,1)S(1)} %tie.20.refs_5_), channel_id=1, source_target_pairs={{0,4},{4,0},{8,12},{12,8},{1,5},{5,1},{9,13},{13,9},{2,6},{6,2},{1... | collective-permute-start | bytes 983048 | tf_op jit(solution)/shard_map/ppermute | solution.py:489
  147.8 10.1 %collective-permute-start.42 = (bf16[1,4,16,1024]{3,2,1,0:T(8,128)(2,1)S(1)}, bf16[1,4,16,1024]{3,2,1,0:T(8,128)(2,1)S(1)}, u32[]{:S(2)}, u32[]{:S(2)}) collective-permute-start(bf16[1,4,16,1024]{3,2,1,0:T(8,128)(2,1)S(1)} %fold.22), channel_id=1, source_target_pairs={{0,8},{4,12},{8,0},{12,4},{1,9},{5,13},{9,1},{13,5},{2,10},{6,14},... | collective-permute-start | bytes 393224 | tf_op jit(solution)/shard_map/ppermute | solution.py:489
  157.9 10.7 %collective-permute-start.50 = (bf16[2,4,16,768]{3,2,1,0:T(8,128)(2,1)S(1)}, bf16[2,4,16,768]{3,2,1,0:T(8,128)(2,1)S(1)}, u32[]{:S(2)}, u32[]{:S(2)}) collective-permute-start(bf16[2,4,16,768]{3,2,1,0:T(8,128)(2,1)S(1)} %tie.21), channel_id=1, source_target_pairs={{0,4},{4,0},{8,12},{12,8},{1,5},{5,1},{9,13},{13,9},{2,6},{6,2},{1... | collective-permute-start | bytes 589832 | tf_op jit(solution)/shard_map/ppermute | solution.py:489
  161.4 19.8 %collective-permute-start.49 = (bf16[1,4,16,1280]{3,2,1,0:T(8,128)(2,1)S(1)}, bf16[1,4,16,1280]{3,2,1,0:T(8,128)(2,1)S(1)}, u32[]{:S(2)}, u32[]{:S(2)}) collective-permute-start(bf16[1,4,16,1280]{3,2,1,0:T(8,128)(2,1)S(1)} %fold.24), channel_id=1, source_target_pairs={{0,8},{4,12},{8,0},{12,4},{1,9},{5,13},{9,1},{13,5},{2,10},{6,14},... | collective-permute-start | bytes 491528 | tf_op jit(solution)/shard_map/ppermute | solution.py:489
  161.6 18.5 %collective-permute-start.44 = (bf16[1,4,16,1024]{3,2,1,0:T(8,128)(2,1)S(1)}, bf16[1,4,16,1024]{3,2,1,0:T(8,128)(2,1)S(1)}, u32[]{:S(2)}, u32[]{:S(2)}) collective-permute-start(bf16[1,4,16,1024]{3,2,1,0:T(8,128)(2,1)S(1)} %fold.23), channel_id=1, source_target_pairs={{0,8},{4,12},{8,0},{12,4},{1,9},{5,13},{9,1},{13,5},{2,10},{6,14},... | collective-permute-start | bytes 393224 | tf_op jit(solution)/shard_map/ppermute | solution.py:489
  168.7 12.5 %collective-permute-start.51 = (bf16[1,4,16,768]{3,2,1,0:T(8,128)(2,1)S(1)}, bf16[1,4,16,768]{3,2,1,0:T(8,128)(2,1)S(1)}, u32[]{:S(2)}, u32[]{:S(2)}) collective-permute-start(bf16[1,4,16,768]{3,2,1,0:T(8,128)(2,1)S(1)} %fold.25), channel_id=1, source_target_pairs={{0,8},{4,12},{8,0},{12,4},{1,9},{5,13},{9,1},{13,5},{2,10},{6,14},... | collective-permute-start | bytes 294920 | tf_op jit(solution)/shard_map/ppermute | solution.py:489
  (14 other events, 90.5 us)

commit v9 on v8

--- a/solution.py
+++ b/solution.py
@@ -68,11 +68,15 @@
             first += each
 
 
+def parts_of(owners):
+    half = owners // 2
+    return [half, half // 2, half // 2] if half > 1 else [half, half]
+
+
 def project(at, tokens, w, head_first, heads, after):
     zs, chunks, owners, piece, depth = tokens.shape
-    half, each = owners // 2, zs * chunks * piece
+    each, counts = zs * chunks * piece, parts_of(owners)
     parts = 4 if depth % 512 == 0 else 1
-    counts = [half] + ([half // 2] * 2 if half > 1 else [half])
     return pl.pallas_call(
         functools.partial(project_kernel, parts, owners, len(after)),
         grid_spec=pltpu.PrefetchScalarGridSpec(
@@ -209,12 +213,12 @@
     )(base.reshape(1), start.reshape(-1, DH), end.reshape(-1, DH))
 
 
-def attend_kernel(owners, at_ref, *refs):
+def attend_kernel(owners, sends, at_ref, *refs):
     queries, edges = refs[:owners], refs[owners:2 * owners]
     k_ref, v_ref = refs[2 * owners:2 * owners + 2]
-    keep_ref, send_ref, mask_ref = refs[-3:]
+    outs, mask_ref = refs[-1 - sends:-1], refs[-1]
     events = mask_ref.shape[1]
-    half, each, _ = keep_ref.shape
+    each = outs[0].shape[1]
 
     @pl.when(pl.program_id(0) == 0)
     def _():
@@ -237,9 +241,11 @@
         ) * (0.5 * DH ** (-0.5))
         weights = (u + u * jnp.tanh(u)).astype(bf16) * mask_ref[...]
         term = jnp.dot(weights, v_ref[:, at], preferred_element_type=f32).astype(bf16)
-        for p in range(owners):
-            into = keep_ref if p < half else send_ref
-            into[p % half, :, at] = term[p * each:(p + 1) * each]
+        first = 0
+        for out in outs:
+            for p in range(out.shape[0]):
+                out[p, :, at] = term[first:first + each]
+                first += each
 
 
 def edge_spec(edges, p):
@@ -249,14 +255,12 @@
 
 def attend(at, queries, k_cache, v_cache, edges, head_first, after):
     owners, (each, width) = len(queries), queries[0].shape
-    rows, events, half = owners * each, k_cache.shape[0], owners // 2
+    rows, events, counts = owners * each, k_cache.shape[0], parts_of(owners)
     first = head_first * DH
     span = max(h for h in range(DH, 4 * DH, DH) if width % h == 0 and first % h == 0)
     cache = pl.BlockSpec((events, span), lambda j, at: (0, first // span + j))
-    shape = jax.ShapeDtypeStruct((half, each, width), bf16)
-    spec = pl.BlockSpec((half, each, span), lambda j, at: (0, 0, j))
-    return pl.pallas_call(
-        functools.partial(attend_kernel, owners),
+    return pl.pallas_call(
+        functools.partial(attend_kernel, owners, len(counts)),
         grid_spec=pltpu.PrefetchScalarGridSpec(
             num_scalar_prefetch=1,
             grid=(width // span,),
@@ -264,10 +268,10 @@
             + [edge_spec(edges, p) for p in range(owners)]
             + [cache, cache]
             + anywhere(after),
-            out_specs=(spec, spec),
+            out_specs=[pl.BlockSpec((n, each, span), lambda j, at: (0, 0, j)) for n in counts],
             scratch_shapes=[pltpu.VMEM((rows, events), bf16)],
         ),
-        out_shape=(shape, shape),
+        out_shape=[jax.ShapeDtypeStruct((n, each, width), bf16) for n in counts],
         compiler_params=params(),
         cost_estimate=LIGHT,
         name="attend",
@@ -385,53 +389,50 @@
     )(*stats, *atts, *rests)
 
 
-def output_kernel(owners, slots, index_ref, *refs):
-    rows, w_ref, (keep_ref, send_ref, lhs_ref) = refs[:owners], refs[owners], refs[-3:]
-    piece, half = rows[0].shape[1], len(slots) // 2
+def output_kernel(owners, after, order_ref, *refs):
+    rows, w_ref, outs, lhs_ref = refs[:owners], refs[owners], refs[owners + 1 + after:-1], refs[-1]
+    piece = rows[0].shape[1]
 
     @pl.when(pl.program_id(0) == 0)
     def _():
         first = 0
-        for slot in slots:
+        for k in range(rows[0].shape[0]):
             for p in range(owners):
-                lhs_ref[first:first + piece, :] = rows[p][index_ref[0] ^ slot]
+                lhs_ref[first:first + piece, :] = rows[p][order_ref[k]]
                 first += piece
 
     sums = jnp.dot(lhs_ref[...], w_ref[...], preferred_element_type=f32).astype(bf16)
-    for k in range(len(slots)):
-        into = keep_ref if k < half else send_ref
-        for p in range(owners):
-            first = (k * owners + p) * piece
-            into[k % half, p] = sums[first:first + piece]
-
-
-def output(index, blocks, w_out, slots, column, columns, after):
-    owners, (each, width) = len(blocks), blocks[0].shape
-    zs = len(slots)
+    first = 0
+    for out in outs:
+        for k in range(out.shape[0]):
+            for p in range(owners):
+                out[k, p] = sums[first:first + piece]
+                first += piece
+
+
+def output(order, counts, blocks, w_out, column, columns, after):
+    owners, (each, width), zs = len(blocks), blocks[0].shape, sum(counts)
     piece = each // zs
     span = max(c for c in (512, 256, columns) if columns % c == 0 and column % c == 0)
     row_spec = pl.BlockSpec((zs, piece, width), lambda j, at: (0, 0, 0))
-    spec = pl.BlockSpec((zs // 2, owners, piece, span), lambda j, at: (0, 0, 0, j))
-    shape = jax.ShapeDtypeStruct((zs // 2, owners, piece, columns), bf16)
-    return pl.pallas_call(
-        functools.partial(output_kernel, owners, slots),
+    return pl.pallas_call(
+        functools.partial(output_kernel, owners, len(after)),
         grid_spec=pltpu.PrefetchScalarGridSpec(
             num_scalar_prefetch=1,
             grid=(columns // span,),
             in_specs=[row_spec] * owners
             + [pl.BlockSpec((width, span), lambda j, at: (0, column // span + j))]
             + anywhere(after),
-            out_specs=(spec, spec),
+            out_specs=[
+                pl.BlockSpec((n, owners, piece, span), lambda j, at: (0, 0, 0, j)) for n in counts
+            ],
             scratch_shapes=[pltpu.VMEM((owners * each, width), bf16)],
         ),
-        out_shape=(shape, shape),
+        out_shape=[jax.ShapeDtypeStruct((n, owners, piece, columns), bf16) for n in counts],
         compiler_params=params(),
         cost_estimate=LIGHT,
         name="output",
-    )(
-        index.reshape(1).astype(jnp.int32),
-        *[b.reshape(zs, piece, width) for b in blocks], far(w_out), *after,
-    )
+    )(order, *[b.reshape(zs, piece, width) for b in blocks], far(w_out), *after)
 
 
 def close_kernel(counts, at_ref, t_ref, *refs):
@@ -508,15 +509,17 @@
     return blocks
 
 
+def shift(x, axis, k):
+    count = lax.axis_size(axis)
+    return lax.ppermute(x, axis, [(i, (i + k) % count) for i in range(count)])
+
+
 def all_stats(stat, axis):
     count = lax.axis_size(axis)
     if count > 8:
         every = lax.all_gather(stat, axis)
         return [every[i] for i in range(count)]
-    return [stat] + [
-        lax.ppermute(stat, axis, [(i, (i + k) % count) for i in range(count)])
-        for k in range(1, count)
-    ]
+    return [stat] + [shift(stat, axis, k) for k in range(1, count)]
 
 
 def head_chunks(heads):
@@ -584,8 +587,8 @@
             chain.append(parts[c][0])
         elif step == "T":
             first = firsts[groups[c][0]]
-            keep, send = attend(at, queries[c], k_cache, v_cache, edges, first, after)
-            halves[c] = keep, [swap(send, "hist", 0)]
+            keep, *sends = attend(at, queries[c], k_cache, v_cache, edges, first, after)
+            halves[c] = keep, [swap(send, "hist", 0) for send in sends]
             chain.append(keep)
         elif step == "G":
             sums[c], sent = scatter(*halves[c], "hist", after)
@@ -601,7 +604,10 @@
     gated = gate_rows(all_stats(stats[last], "head"), atts, rests, chunks)
     columns = w_out.shape[1]
     straight = piece % 16 == 0 and zs & (zs - 1) == 0
-    results, sends, first_steps, ends = [], [], [], []
+    steps = jnp.arange(zs, dtype=jnp.int32)
+    shifted = (index + steps) % zs
+    halved = index ^ reverse(steps, bits_of("head")) if straight else shifted
+    results, last_sent, before = [], [], {}
     for r, rows in enumerate(gated):
         results.append([])
         if not straight:
@@ -611,20 +617,27 @@
             whole = lax.psum_scatter(whole, "head", scatter_dimension=0, tiled=True)
             results[-1].append([whole])
             continue
-        blocks = gather(rows, "hist", sends[-1:] + first_steps[:1])
-        slots = [reverse(k, bits_of("head")) for k in range(zs)]
-        unit = columns // 8
-        spans = [columns]
-        if unit % (2 * DH) == 0:
-            spans = [4 * unit, 4 * unit] if r == 0 else [5 * unit, 3 * unit]
+        blocks = gather(rows, "hist", before.get(r, []))
+        spans = [columns // 2] * 2 if columns % 1024 == 0 else [columns]
         for g, span in enumerate(spans):
-            first = sum(spans[:g])
-            keep, send = output(index, blocks, w_out, slots, first, span, sends[-1:])
-            send = tie(send, first_steps[-2:-1] + ends[-3:-2])
-            sends.append(send)
-            terms, _ = scatter(keep, [swap(send, "head", 0)], "head")
-            first_steps.append(terms[1])
-            ends.append(terms[-1])
+            direct = len(spans) == 1 or g == r
+            order = shifted if direct else halved
+            counts = [1] * zs if direct else [zs // 2] * 2
+            own, *others = output(order, counts, blocks, w_out, g * span, span, last_sent)
+            others = [tie(x, before.get((r, g), [])) for x in others]
+            last_sent = others[-1:]
+            if direct:
+                arrived = [shift(x, "head", k + 1) for k, x in enumerate(others)]
+                terms = [own] + arrived
+                if r == 0:
+                    before[1] = arrived[zs // 2 - 1:zs // 2]
+                    before[1, 0] = arrived
+            else:
+                arrived = swap(others[0], "head", 0)
+                terms, _ = scatter(own, [arrived], "head")
+                if r == 0:
+                    before[1, 0] = before.get((1, 0), []) + [arrived]
+                    before[1, 1] = [terms[-1]]
             results[-1].append(terms)
     out = close(place, index, tokens, results)
     return out.reshape(cand // zs, -1)

time: 184 us -> 186 us (1.011)
  starting transfers between devices: 33 us -> 42 us
  waiting for transfers between devices: 70.1 us -> 61.1 us
    ppermute x49, waiting for transfers between devices: 65.7 us -> 31.7 us  [swap(): lax.ppermute(x, axis, [(i, i ^ 1 << bit) for i in range(lax.axis_size(axi...]
    ppermute x3 -> x9, waiting for transfers between devices: 4.39 us -> 29.4 us  [shift(): return lax.ppermute(x, axis, [(i, (i + k) % count) for i in range(count)])]
    ppermute x3 -> x9, starting transfers between devices: 4.64 us -> 15.1 us  [shift(): return lax.ppermute(x, axis, [(i, (i + k) % count) for i in range(count)])]
    pallas_call x13 -> x11, Pallas kernels: 4.57 us -> 4.29 us  [fold(): pl.pallas_call(functools.partial(fold_kernel, len(terms)), grid=(steps,),...]
  transfers between devices with their start and end apart: 52 -> 58, of which waited for: 21 -> 21; matrix products, arithmetic and copies ran while one was open for 0% -> 0% of each run, Pallas kernels for 36% -> 36%
where the time goes in v9:
time: 186 us; the launch traced here: 185 us
  Pallas kernels  79.1 us (43%)
  waiting for transfers between devices  61.1 us (33%)
  starting transfers between devices  42 us (23%)
  local copies, waits for them, and re-layouts  2.39 us (1%)
    pallas_call x5, Pallas kernels, project(): pl.pallas_call(functools.partial(project_kernel, parts, owners, len(after...  37.9 us
    ppermute x49, waiting for transfers between devices, swap(): lax.ppermute(x, axis, [(i, i ^ 1 << bit) for i in range(lax.axis_size(axi...  31.7 us
    ppermute x9, waiting for transfers between devices, shift(): return lax.ppermute(x, axis, [(i, (i + k) % count) for i in range(count)])  29.4 us
    ppermute x49, starting transfers between devices, swap(): lax.ppermute(x, axis, [(i, i ^ 1 << bit) for i in range(lax.axis_size(axi...  26.8 us
    pallas_call x4, Pallas kernels, output(): pl.pallas_call(functools.partial(output_kernel, owners, len(after)), grid...  15.9 us
    ppermute x9, starting transfers between devices, shift(): return lax.ppermute(x, axis, [(i, (i + k) % count) for i in range(count)])  15.1 us
    pallas_call x4, Pallas kernels, attend(): pl.pallas_call(functools.partial(attend_kernel, owners, len(counts)), gri...  12.4 us
    pallas_call x11, Pallas kernels, fold(): pl.pallas_call(functools.partial(fold_kernel, len(terms)), grid=(steps,),...  4.29 us
  transfers between devices with their start and end apart: 58, of which 21 were waited for; matrix products, arithmetic and copies ran while one was open for 0% of the time, Pallas kernels for 36%

profile of v9, /device:TPU:0, one launch (start us, length us, event | category | flops | bytes accessed | tf_op | source)
XLA Modules:
  0.0 185.1 jit_solution(5854438881420390932)
XLA Ops:
  0.0 5.5 %project.5 = (bf16[2,4,128,256]{3,2,1,0:T(8,128)(2,1)S(1)}, bf16[1,4,128,256]{3,2,1,0:T(8,128)(2,1)S(1)}, bf16[1,4,128,256]{3,2,1,0:T(8,128)(2,1)S(1)}) custom-call(s32[1]{0:T(128)} %bitcast.at_ref, bf16[4,2,4,16,2048]{4,3,2,1,0:T(8,128)(2,1)} %bitcast.55, bf16[4,2,4,16,2048]{4,3,2,1,0:T(8,128)(2,1)} %bitcast.56, bf16[4,2,4,16,2048]{4,3,2,1,0:T(8,128)(2,1)} %bitcast.57, ...), custom_call_target="tpu_custom_call" | custom-call | flops 1000 | bytes 1000 | tf_op jit(solution)/shard_map/project/pallas_call | solution.py:80
  6.1 8.7 %project.6 = (bf16[2,4,128,512]{3,2,1,0:T(8,128)(2,1)S(1)}, bf16[1,4,128,512]{3,2,1,0:T(8,128)(2,1)S(1)}, bf16[1,4,128,512]{3,2,1,0:T(8,128)(2,1)S(1)}) custom-call(s32[1]{0:T(128)} %bitcast.at_ref, bf16[4,2,4,16,2048]{4,3,2,1,0:T(8,128)(2,1)} %bitcast.59, bf16[4,2,4,16,2048]{4,3,2,1,0:T(8,128)(2,1)} %bitcast.60, bf16[4,2,4,16,2048]{4,3,2,1,0:T(8,128)(2,1)} %bitcast.61, ...), custom_call_target="tpu_custom_call" | custom-call | flops 1000 | bytes 1000 | tf_op jit(solution)/shard_map/project/pallas_call | solution.py:80
  15.8 3.0 %collective-permute-start.4 = (bf16[1,4,128,256]{3,2,1,0:T(8,128)(2,1)S(1)}, bf16[1,4,128,256]{3,2,1,0:T(8,128)(2,1)S(1)}, u32[]{:S(2)}, u32[]{:S(2)}) collective-permute-start(bf16[1,4,128,256]{3,2,1,0:T(8,128)(2,1)S(1)} %fold.11.refs_8_), channel_id=1, source_target_pairs={{0,2},{1,3},{2,0},{3,1},{4,6},{5,7},{6,4},{7,5},{8,10},{9,11},{10,... | collective-permute-start | bytes 786440 | tf_op jit(solution)/shard_map/ppermute | solution.py:490
  18.7 8.7 %project.7 = (bf16[2,4,128,512]{3,2,1,0:T(8,128)(2,1)S(1)}, bf16[1,4,128,512]{3,2,1,0:T(8,128)(2,1)S(1)}, bf16[1,4,128,512]{3,2,1,0:T(8,128)(2,1)S(1)}) custom-call(s32[1]{0:T(128)} %bitcast.at_ref, bf16[4,2,4,16,2048]{4,3,2,1,0:T(8,128)(2,1)} %bitcast.63, bf16[4,2,4,16,2048]{4,3,2,1,0:T(8,128)(2,1)} %bitcast.64, bf16[4,2,4,16,2048]{4,3,2,1,0:T(8,128)(2,1)} %bitcast.65, ...), custom_call_target="tpu_custom_call" | custom-call | flops 1000 | bytes 1000 | tf_op jit(solution)/shard_map/project/pallas_call | solution.py:80
  28.5 8.8 %project.8 = (bf16[2,4,128,512]{3,2,1,0:T(8,128)(2,1)S(1)}, bf16[1,4,128,512]{3,2,1,0:T(8,128)(2,1)S(1)}, bf16[1,4,128,512]{3,2,1,0:T(8,128)(2,1)S(1)}) custom-call(s32[1]{0:T(128)} %bitcast.at_ref, bf16[4,2,4,16,2048]{4,3,2,1,0:T(8,128)(2,1)} %bitcast.67, bf16[4,2,4,16,2048]{4,3,2,1,0:T(8,128)(2,1)} %bitcast.68, bf16[4,2,4,16,2048]{4,3,2,1,0:T(8,128)(2,1)} %bitcast.69, ...), custom_call_target="tpu_custom_call" | custom-call | flops 1000 | bytes 1000 | tf_op jit(solution)/shard_map/project/pallas_call | solution.py:80
  39.1 1.9 %collective-permute-start.12 = (bf16[1,4,128,512]{3,2,1,0:T(8,128)(2,1)}, bf16[1,4,128,512]{3,2,1,0:T(8,128)(2,1)}, u32[]{:S(2)}, u32[]{:S(2)}) collective-permute-start(bf16[1,4,128,512]{3,2,1,0:T(8,128)(2,1)} %fold.13.refs_6_), channel_id=1, source_target_pairs={{0,2},{1,3},{2,0},{3,1},{4,6},{5,7},{6,4},{7,5},{8,10},{9,11},{10,... | collective-permute-start | bytes 1572872 | tf_op jit(solution)/shard_map/ppermute | solution.py:490
  41.0 1.4 collective-permute-done.8.refs_5_
  44.2 6.2 %project.9 = (bf16[2,4,128,256]{3,2,1,0:T(8,128)(2,1)S(1)}, bf16[1,4,128,256]{3,2,1,0:T(8,128)(2,1)S(1)}, bf16[1,4,128,256]{3,2,1,0:T(8,128)(2,1)}) custom-call(s32[1]{0:T(128)} %bitcast.at_ref, bf16[4,2,4,16,2048]{4,3,2,1,0:T(8,128)(2,1)} %bitcast.71, bf16[4,2,4,16,2048]{4,3,2,1,0:T(8,128)(2,1)} %bitcast.72, bf16[4,2,4,16,2048]{4,3,2,1,0:T(8,128)(2,1)} %bitcast.73, ...), custom_call_target="tpu_custom_call" | custom-call | flops 1000 | bytes 1000 | tf_op jit(solution)/shard_map/project/pallas_call | solution.py:80
  51.1 1.8 collective-permute-start.17
  53.1 5.3 %collective-permute-done.18.refs_1_ = bf16[128,768]{1,0:T(8,128)(2,1)S(1)} collective-permute-done((bf16[128,768]{1,0:T(8,128)(2,1)S(1)}, bf16[128,768]{1,0:T(8,128)(2,1)S(1)}, u32[]{:S(2)}, u32[]{:S(2)}) %collective-permute-start.18) | collective-permute-done | bytes 196640 | tf_op jit(solution)/shard_map/ppermute | solution.py:490
  58.5 1.0 copy-done.3
  59.6 1.4 activate.5
  60.9 1.1 fold.15.refs_10_
  62.1 4.1 %attend.4 = (bf16[2,128,768]{2,1,0:T(8,128)(2,1)S(1)}, bf16[1,128,768]{2,1,0:T(8,128)(2,1)S(1)}, bf16[1,128,768]{2,1,0:T(8,128)(2,1)S(1)}) custom-call(s32[1]{0:T(128)} %bitcast.at_ref, bf16[128,768]{1,0:T(8,128)(2,1)S(1)} %get-tuple-element.73.refs_2_.refs_0_.q_ref, bf16[128,768]{1,0:T(8,128)(2,1)S(1)} %collective-permute-done.18.refs_1_, ...), custom_call_target="tpu_custom_call" | custom-call | flops 1000 | bytes 1000 | tf_op jit(solution)/shard_map/attend/pallas_call | solution.py:262
  66.7 1.8 collective-permute-start.14
  68.8 4.0 %collective-permute-done.14.refs_1_ = bf16[128,512]{1,0:T(8,128)(2,1)S(1)} collective-permute-done((bf16[128,512]{1,0:T(8,128)(2,1)S(1)}, bf16[128,512]{1,0:T(8,128)(2,1)S(1)}, u32[]{:S(2)}, u32[]{:S(2)}) %collective-permute-start.14) | collective-permute-done | bytes 131104 | tf_op jit(solution)/shard_map/ppermute | solution.py:490
  73.5 1.4 activate.6
  74.9 2.1 %collective-permute-start.25 = (bf16[128,512]{1,0:T(8,128)(2,1)S(1)}, bf16[128,512]{1,0:T(8,128)(2,1)S(1)}, u32[]{:S(2)}, u32[]{:S(2)}) collective-permute-start(bf16[128,512]{1,0:T(8,128)(2,1)S(1)} %get-tuple-element.81.refs_10_.refs_0_.q_ref), channel_id=1, source_target_pairs={{0,2},{1,3},{2,0},{3,1},{4,6},{5,7},{6,4},{7,5},{8,10},{9,11},{10,... | collective-permute-start | bytes 393224 | tf_op jit(solution)/shard_map/ppermute | solution.py:490
  77.2 3.1 %attend.5 = (bf16[2,128,512]{2,1,0:T(8,128)(2,1)S(1)}, bf16[1,128,512]{2,1,0:T(8,128)(2,1)S(1)}, bf16[1,128,512]{2,1,0:T(8,128)(2,1)S(1)}) custom-call(s32[1]{0:T(128)} %bitcast.at_ref, bf16[128,512]{1,0:T(8,128)(2,1)S(1)} %get-tuple-element.78.refs_2_.refs_0_.q_ref, bf16[128,512]{1,0:T(8,128)(2,1)S(1)} %collective-permute-done.14.refs_1_, ...), custom_call_target="tpu_custom_call" | custom-call | flops 1000 | bytes 1000 | tf_op jit(solution)/shard_map/attend/pallas_call | solution.py:262
  81.9 3.0 %collective-permute-done.29.refs_2_ = bf16[1,128,768]{2,1,0:T(8,128)(2,1)S(1)} collective-permute-done((bf16[1,128,768]{2,1,0:T(8,128)(2,1)S(1)}, bf16[1,128,768]{2,1,0:T(8,128)(2,1)S(1)}, u32[]{:S(2)}, u32[]{:S(2)}) %collective-permute-start.29) | collective-permute-done | bytes 196640 | tf_op jit(solution)/shard_map/ppermute | solution.py:490
  85.5 3.2 %attend.6 = (bf16[2,128,512]{2,1,0:T(8,128)(2,1)S(1)}, bf16[1,128,512]{2,1,0:T(8,128)(2,1)S(1)}, bf16[1,128,512]{2,1,0:T(8,128)(2,1)S(1)}) custom-call(s32[1]{0:T(128)} %bitcast.at_ref, bf16[128,512]{1,0:T(8,128)(2,1)S(1)} %get-tuple-element.81.refs_10_.refs_0_.q_ref, bf16[128,512]{1,0:T(8,128)(2,1)S(1)} %collective-permute-done.25.refs_1_, ...), custom_call_target="tpu_custom_call" | custom-call | flops 1000 | bytes 1000 | tf_op jit(solution)/shard_map/attend/pallas_call | solution.py:262
  88.7 1.8 collective-permute-start.22
  91.3 1.9 %collective-permute-done.22.refs_1_ = bf16[128,256]{1,0:T(8,128)(2,1)S(1)} collective-permute-done((bf16[128,256]{1,0:T(8,128)(2,1)S(1)}, bf16[128,256]{1,0:T(8,128)(2,1)S(1)}, u32[]{:S(2)}, u32[]{:S(2)}) %collective-permute-start.22) | collective-permute-done | bytes 65568 | tf_op jit(solution)/shard_map/ppermute | solution.py:490
  93.9 2.3 %collective-permute-start.38 = (bf16[1,128,512]{2,1,0:T(8,128)(2,1)S(1)}, bf16[1,128,512]{2,1,0:T(8,128)(2,1)S(1)}, u32[]{:S(2)}, u32[]{:S(2)}) collective-permute-start(bf16[1,128,512]{2,1,0:T(8,128)(2,1)S(1)} %fold.18.refs_10_), channel_id=1, source_target_pairs={{0,2},{1,3},{2,0},{3,1},{4,6},{5,7},{6,4},{7,5},{8,10},{9,11},{10,... | collective-permute-start | bytes 393224 | tf_op jit(solution)/shard_map/ppermute | solution.py:490
  96.1 2.0 %attend.7 = (bf16[2,128,256]{2,1,0:T(8,128)(2,1)S(1)}, bf16[1,128,256]{2,1,0:T(8,128)(2,1)S(1)}, bf16[1,128,256]{2,1,0:T(8,128)(2,1)S(1)}) custom-call(s32[1]{0:T(128)} %bitcast.at_ref, bf16[128,256]{1,0:T(8,128)(2,1)S(1)} %get-tuple-element.83.refs_2_.refs_0_.q_ref, bf16[128,256]{1,0:T(8,128)(2,1)S(1)} %collective-permute-done.22.refs_1_, ...), custom_call_target="tpu_custom_call" | custom-call | flops 1000 | bytes 1000 | tf_op jit(solution)/shard_map/attend/pallas_call | solution.py:262
  100.7 3.3 %collective-permute-done.36.refs_2_ = bf16[1,128,256]{2,1,0:T(8,128)(2,1)S(1)} collective-permute-done((bf16[1,128,256]{2,1,0:T(8,128)(2,1)S(1)}, bf16[1,128,256]{2,1,0:T(8,128)(2,1)S(1)}, u32[]{:S(2)}, u32[]{:S(2)}) %collective-permute-start.36) | collective-permute-done | bytes 65568 | tf_op jit(solution)/shard_map/ppermute | solution.py:490
  104.4 3.6 %collective-permute-start.41 = (f32[8,128]{1,0:T(8,128)S(1)}, f32[8,128]{1,0:T(8,128)S(1)}, u32[]{:S(2)}, u32[]{:S(2)}) collective-permute-start(f32[8,128]{1,0:T(8,128)S(1)} %get-tuple-element.103.refs_0_), channel_id=1, source_target_pairs={{0,12},{4,0},{8,4},{12,8},{1,13},{5,1},{9,5},{13,9},{2,14},{6,2},{... | collective-permute-start | bytes 12296 | tf_op jit(solution)/shard_map/ppermute | solution.py:514
  108.1 1.0 collective-permute-start.39
  109.4 3.2 %collective-permute-done.40.refs_2_ = f32[8,128]{1,0:T(8,128)S(1)} collective-permute-done((f32[8,128]{1,0:T(8,128)S(1)}, f32[8,128]{1,0:T(8,128)S(1)}, u32[]{:S(2)}, u32[]{:S(2)}) %collective-permute-start.40) | collective-permute-done | bytes 4128 | tf_op jit(solution)/shard_map/ppermute | solution.py:514
  114.5 5.8 %collective-permute-done.42 = bf16[64,2048]{1,0:T(8,128)(2,1)S(1)} collective-permute-done((bf16[64,2048]{1,0:T(8,128)(2,1)S(1)}, bf16[64,2048]{1,0:T(8,128)(2,1)S(1)}, u32[]{:S(2)}, u32[]{:S(2)}) %collective-permute-start.42) | collective-permute-done | bytes 262176 | tf_op jit(solution)/shard_map/ppermute | solution.py:490
  121.9 4.0 %output.4 = (bf16[1,4,16,1024]{3,2,1,0:T(8,128)(2,1)S(1)}, bf16[1,4,16,1024]{3,2,1,0:T(8,128)(2,1)S(1)}, bf16[1,4,16,1024]{3,2,1,0:T(8,128)(2,1)S(1)}, bf16[1,4,16,1024]{3,2,1,0:T(8,128)(2,1)S(1)}) custom-call(s32[4]{0:T(128)S(1)} %and_select_fusion.order_ref, bf16[4,16,2048]{2,1,0:T(8,128)(2,1)S(1)} %bitcast.41, bf16[4,16,2048]{2,1,0:T(8,128)(2,1)S(1)} %bitcast.47, ...), custom_call_target="tpu_custom_call" | custom-call | flops 1000 | bytes 1000 | tf_op jit(solution)/shard_map/output/pallas_call | solution.py:418
  125.8 1.2 collective-permute-start.46
  127.0 2.0 %collective-permute-done.50.refs_0_ = bf16[64,2048]{1,0:T(8,128)(2,1)S(1)} collective-permute-done((bf16[64,2048]{1,0:T(8,128)(2,1)S(1)}, bf16[64,2048]{1,0:T(8,128)(2,1)S(1)}, u32[]{:S(2)}, u32[]{:S(2)}) %collective-permute-start.50) | collective-permute-done | bytes 262176 | tf_op jit(solution)/shard_map/ppermute | solution.py:490
  129.1 4.9 %collective-permute-done.46.refs_1_.refs_2_ = bf16[1,4,16,1024]{3,2,1,0:T(8,128)(2,1)S(1)} collective-permute-done((bf16[1,4,16,1024]{3,2,1,0:T(8,128)(2,1)S(1)}, bf16[1,4,16,1024]{3,2,1,0:T(8,128)(2,1)S(1)}, u32[]{:S(2)}, u32[]{:S(2)}) %collective-permute-start.46) | collective-permute-done | bytes 131104 | tf_op jit(solution)/shard_map/ppermute | solution.py:514
  134.0 4.0 %output.5 = (bf16[2,4,16,1024]{3,2,1,0:T(8,128)(2,1)S(1)}, bf16[2,4,16,1024]{3,2,1,0:T(8,128)(2,1)S(1)}) custom-call(s32[4]{0:T(128)S(1)} %fusion.3.order_ref, bf16[4,16,2048]{2,1,0:T(8,128)(2,1)S(1)} %bitcast.42, bf16[4,16,2048]{2,1,0:T(8,128)(2,1)S(1)} %bitcast.48, bf16[4,16,2048]{2,1,0:T(8,128)(2,1)S(1)} %bitcast.50, bf16[4,16,2048]{2,1,0:T(8,128)(2,1)S(1)} %bitcast.52, ...), custom_call_target="tpu_custom_call" | custom-call | flops 1000 | bytes 1000 | tf_op jit(solution)/shard_map/output/pallas_call | solution.py:418
  138.1 2.0 %collective-permute-start.45 = (bf16[1,4,16,1024]{3,2,1,0:T(8,128)(2,1)S(1)}, bf16[1,4,16,1024]{3,2,1,0:T(8,128)(2,1)S(1)}, u32[]{:S(2)}, u32[]{:S(2)}) collective-permute-start(bf16[1,4,16,1024]{3,2,1,0:T(8,128)(2,1)S(1)} %get-tuple-element.107), channel_id=1, source_target_pairs={{0,4},{4,8},{8,12},{12,0},{1,5},{5,9},{9,13},{13,1},{2,6},{6,10},{... | collective-permute-start | bytes 393224 | tf_op jit(solution)/shard_map/ppermute | solution.py:514
  140.1 1.9 %collective-permute-start.47 = (bf16[1,4,16,1024]{3,2,1,0:T(8,128)(2,1)S(1)}, bf16[1,4,16,1024]{3,2,1,0:T(8,128)(2,1)S(1)}, u32[]{:S(2)}, u32[]{:S(2)}) collective-permute-start(bf16[1,4,16,1024]{3,2,1,0:T(8,128)(2,1)S(1)} %get-tuple-element.109.refs_5_), channel_id=1, source_target_pairs={{0,12},{4,0},{8,4},{12,8},{1,13},{5,1},{9,5},{13,9},{2,14},{6,2},{... | collective-permute-start | bytes 393224 | tf_op jit(solution)/shard_map/ppermute | solution.py:514
  142.0 4.0 %output.6 = (bf16[2,4,16,1024]{3,2,1,0:T(8,128)(2,1)S(1)}, bf16[2,4,16,1024]{3,2,1,0:T(8,128)(2,1)S(1)}) custom-call(s32[4]{0:T(128)S(1)} %fusion.3.order_ref, bf16[4,16,2048]{2,1,0:T(8,128)(2,1)S(1)} %bitcast.39, bf16[4,16,2048]{2,1,0:T(8,128)(2,1)S(1)} %bitcast.37, bf16[4,16,2048]{2,1,0:T(8,128)(2,1)S(1)} %bitcast.43, bf16[4,16,2048]{2,1,0:T(8,128)(2,1)S(1)} %bitcast.45, ...), custom_call_target="tpu_custom_call" | custom-call | flops 1000 | bytes 1000 | tf_op jit(solution)/shard_map/output/pallas_call | solution.py:418
  146.0 3.8 %collective-permute-done.45.refs_1_ = bf16[1,4,16,1024]{3,2,1,0:T(8,128)(2,1)S(1)} collective-permute-done((bf16[1,4,16,1024]{3,2,1,0:T(8,128)(2,1)S(1)}, bf16[1,4,16,1024]{3,2,1,0:T(8,128)(2,1)S(1)}, u32[]{:S(2)}, u32[]{:S(2)}) %collective-permute-start.45) | collective-permute-done | bytes 131104 | tf_op jit(solution)/shard_map/ppermute | solution.py:514
  149.7 2.6 %collective-permute-done.47.refs_3_ = bf16[1,4,16,1024]{3,2,1,0:T(8,128)(2,1)S(1)} collective-permute-done((bf16[1,4,16,1024]{3,2,1,0:T(8,128)(2,1)S(1)}, bf16[1,4,16,1024]{3,2,1,0:T(8,128)(2,1)S(1)}, u32[]{:S(2)}, u32[]{:S(2)}) %collective-permute-start.47) | collective-permute-done | bytes 131104 | tf_op jit(solution)/shard_map/ppermute | solution.py:514
  152.5 2.7 %collective-permute-start.49 = (bf16[1,4,16,1024]{3,2,1,0:T(8,128)(2,1)S(1)}, bf16[1,4,16,1024]{3,2,1,0:T(8,128)(2,1)S(1)}, u32[]{:S(2)}, u32[]{:S(2)}) collective-permute-start(bf16[1,4,16,1024]{3,2,1,0:T(8,128)(2,1)S(1)} %fold.20), channel_id=1, source_target_pairs={{0,8},{4,12},{8,0},{12,4},{1,9},{5,13},{9,1},{13,5},{2,10},{6,14},... | collective-permute-start | bytes 393224 | tf_op jit(solution)/shard_map/ppermute | solution.py:490
  155.2 4.0 %output.7 = (bf16[1,4,16,1024]{3,2,1,0:T(8,128)(2,1)S(1)}, bf16[1,4,16,1024]{3,2,1,0:T(8,128)(2,1)S(1)}, bf16[1,4,16,1024]{3,2,1,0:T(8,128)(2,1)S(1)}, bf16[1,4,16,1024]{3,2,1,0:T(8,128)(2,1)S(1)}) custom-call(s32[4]{0:T(128)S(1)} %and_select_fusion.order_ref, bf16[4,16,2048]{2,1,0:T(8,128)(2,1)S(1)} %bitcast.40, bf16[4,16,2048]{2,1,0:T(8,128)(2,1)S(1)} %bitcast.38, ...), custom_call_target="tpu_custom_call" | custom-call | flops 1000 | bytes 1000 | tf_op jit(solution)/shard_map/output/pallas_call | solution.py:418
  159.2 1.7 collective-permute-done.49.refs_1_.refs_6_
  160.9 2.3 %collective-permute-start.57 = (bf16[1,4,16,1024]{3,2,1,0:T(8,128)(2,1)S(1)}, bf16[1,4,16,1024]{3,2,1,0:T(8,128)(2,1)S(1)}, u32[]{:S(2)}, u32[]{:S(2)}) collective-permute-start(bf16[1,4,16,1024]{3,2,1,0:T(8,128)(2,1)S(1)} %tie.25), channel_id=1, source_target_pairs={{0,12},{4,0},{8,4},{12,8},{1,13},{5,1},{9,5},{13,9},{2,14},{6,2},{... | collective-permute-start | bytes 393224 | tf_op jit(solution)/shard_map/ppermute | solution.py:514
  163.2 2.5 %collective-permute-start.56 = (bf16[1,4,16,1024]{3,2,1,0:T(8,128)(2,1)S(1)}, bf16[1,4,16,1024]{3,2,1,0:T(8,128)(2,1)S(1)}, u32[]{:S(2)}, u32[]{:S(2)}) collective-permute-start(bf16[1,4,16,1024]{3,2,1,0:T(8,128)(2,1)S(1)} %tie.24), channel_id=1, source_target_pairs={{0,8},{4,12},{8,0},{12,4},{1,9},{5,13},{9,1},{13,5},{2,10},{6,14},... | collective-permute-start | bytes 393224 | tf_op jit(solution)/shard_map/ppermute | solution.py:514
  167.4 13.6 %collective-permute-done.56.refs_12_ = bf16[1,4,16,1024]{3,2,1,0:T(8,128)(2,1)S(1)} collective-permute-done((bf16[1,4,16,1024]{3,2,1,0:T(8,128)(2,1)S(1)}, bf16[1,4,16,1024]{3,2,1,0:T(8,128)(2,1)S(1)}, u32[]{:S(2)}, u32[]{:S(2)}) %collective-permute-start.56) | collective-permute-done | bytes 131104 | tf_op jit(solution)/shard_map/ppermute | solution.py:514
  181.1 1.4 collective-permute-done.54.refs_9_
  182.5 2.7 %close.1 = bf16[8,16,2048]{2,1,0:T(8,128)(2,1)} custom-call(s32[2]{0:T(128)S(1)} %pad_add_fusion.at_ref, bf16[32,16,2048]{2,1,0:T(8,128)(2,1)} %bitcast.75, bf16[1,4,16,1024]{3,2,1,0:T(8,128)(2,1)S(1)} %get-tuple-element.106.refs_0_, bf16[1,4,16,1024]{3,2,1,0:T(8,128)(2,1)S(1)} %collective-permute-done.45.refs_1_, ...), custom_call_target="tpu_custom_call" | custom-call | flops 1000 | bytes 1000 | tf_op jit(solution)/shard_map/close/pallas_call | solution.py:459
  (139 shorter events, 21.1 us)
Async XLA Ops:
  5.5 9.4 %collective-permute-start = (bf16[1,4,128,256]{3,2,1,0:T(8,128)(2,1)S(1)}, bf16[1,4,128,256]{3,2,1,0:T(8,128)(2,1)S(1)}, u32[]{:S(2)}, u32[]{:S(2)}) collective-permute-start(bf16[1,4,128,256]{3,2,1,0:T(8,128)(2,1)S(1)} %get-tuple-element.65), channel_id=1, source_target_pairs={{0,1},{1,0},{2,3},{3,2},{4,5},{5,4},{6,7},{7,6},{8,9},{9,8},{10,11... | collective-permute-start | bytes 786440 | tf_op jit(solution)/shard_map/ppermute | solution.py:490
  6.1 8.8 %collective-permute-start.1 = (bf16[1,4,128,256]{3,2,1,0:T(8,128)(2,1)S(1)}, bf16[1,4,128,256]{3,2,1,0:T(8,128)(2,1)S(1)}, u32[]{:S(2)}, u32[]{:S(2)}) collective-permute-start(bf16[1,4,128,256]{3,2,1,0:T(8,128)(2,1)S(1)} %get-tuple-element.66), channel_id=1, source_target_pairs={{0,1},{1,0},{2,3},{3,2},{4,5},{5,4},{6,7},{7,6},{8,9},{9,8},{10,11... | collective-permute-start | bytes 786440 | tf_op jit(solution)/shard_map/ppermute | solution.py:490
  14.9 12.6 %collective-permute-start.3 = (bf16[1,4,128,512]{3,2,1,0:T(8,128)(2,1)S(1)}, bf16[1,4,128,512]{3,2,1,0:T(8,128)(2,1)S(1)}, u32[]{:S(2)}, u32[]{:S(2)}) collective-permute-start(bf16[1,4,128,512]{3,2,1,0:T(8,128)(2,1)S(1)} %tie.14), channel_id=1, source_target_pairs={{0,1},{1,0},{2,3},{3,2},{4,5},{5,4},{6,7},{7,6},{8,9},{9,8},{10,11... | collective-permute-start | bytes 1572872 | tf_op jit(solution)/shard_map/ppermute | solution.py:490
  15.4 12.1 %collective-permute-start.2 = (bf16[1,4,128,512]{3,2,1,0:T(8,128)(2,1)S(1)}, bf16[1,4,128,512]{3,2,1,0:T(8,128)(2,1)S(1)}, u32[]{:S(2)}, u32[]{:S(2)}) collective-permute-start(bf16[1,4,128,512]{3,2,1,0:T(8,128)(2,1)S(1)} %tie.13), channel_id=1, source_target_pairs={{0,1},{1,0},{2,3},{3,2},{4,5},{5,4},{6,7},{7,6},{8,9},{9,8},{10,11... | collective-permute-start | bytes 1572872 | tf_op jit(solution)/shard_map/ppermute | solution.py:490
  15.8 11.7 %collective-permute-start.4 = (bf16[1,4,128,256]{3,2,1,0:T(8,128)(2,1)S(1)}, bf16[1,4,128,256]{3,2,1,0:T(8,128)(2,1)S(1)}, u32[]{:S(2)}, u32[]{:S(2)}) collective-permute-start(bf16[1,4,128,256]{3,2,1,0:T(8,128)(2,1)S(1)} %fold.11.refs_8_), channel_id=1, source_target_pairs={{0,2},{1,3},{2,0},{3,1},{4,6},{5,7},{6,4},{7,5},{8,10},{9,11},{10,... | collective-permute-start | bytes 786440 | tf_op jit(solution)/shard_map/ppermute | solution.py:490
  27.5 9.8 %collective-permute-start.6 = (bf16[1,4,128,512]{3,2,1,0:T(8,128)(2,1)S(1)}, bf16[1,4,128,512]{3,2,1,0:T(8,128)(2,1)S(1)}, u32[]{:S(2)}, u32[]{:S(2)}) collective-permute-start(bf16[1,4,128,512]{3,2,1,0:T(8,128)(2,1)S(1)} %tie.16), channel_id=1, source_target_pairs={{0,1},{1,0},{2,3},{3,2},{4,5},{5,4},{6,7},{7,6},{8,9},{9,8},{10,11... | collective-permute-start | bytes 1572872 | tf_op jit(solution)/shard_map/ppermute | solution.py:490
  27.6 9.7 %collective-permute-start.5 = (bf16[1,4,128,512]{3,2,1,0:T(8,128)(2,1)S(1)}, bf16[1,4,128,512]{3,2,1,0:T(8,128)(2,1)S(1)}, u32[]{:S(2)}, u32[]{:S(2)}) collective-permute-start(bf16[1,4,128,512]{3,2,1,0:T(8,128)(2,1)S(1)} %tie.15), channel_id=1, source_target_pairs={{0,1},{1,0},{2,3},{3,2},{4,5},{5,4},{6,7},{7,6},{8,9},{9,8},{10,11... | collective-permute-start | bytes 1572872 | tf_op jit(solution)/shard_map/ppermute | solution.py:490
  28.4 14.0 %collective-permute-start.8 = (bf16[1,4,128,512]{3,2,1,0:T(8,128)(2,1)S(1)}, bf16[1,4,128,512]{3,2,1,0:T(8,128)(2,1)S(1)}, u32[]{:S(2)}, u32[]{:S(2)}) collective-permute-start(bf16[1,4,128,512]{3,2,1,0:T(8,128)(2,1)S(1)} %fold.12.refs_8_), channel_id=1, source_target_pairs={{0,2},{1,3},{2,0},{3,1},{4,6},{5,7},{6,4},{7,5},{8,10},{9,11},{10,... | collective-permute-start | bytes 1572872 | tf_op jit(solution)/shard_map/ppermute | solution.py:490
  37.3 5.9 %collective-permute-start.7 = (bf16[1,4,128,512]{3,2,1,0:T(8,128)(2,1)S(1)}, bf16[1,4,128,512]{3,2,1,0:T(8,128)(2,1)S(1)}, u32[]{:S(2)}, u32[]{:S(2)}) collective-permute-start(bf16[1,4,128,512]{3,2,1,0:T(8,128)(2,1)S(1)} %tie.17), channel_id=1, source_target_pairs={{0,1},{1,0},{2,3},{3,2},{4,5},{5,4},{6,7},{7,6},{8,9},{9,8},{10,11... | collective-permute-start | bytes 1572872 | tf_op jit(solution)/shard_map/ppermute | solution.py:490
  38.1 13.0 %collective-permute-start.9 = (bf16[1,4,128,512]{3,2,1,0:T(8,128)(2,1)S(1)}, bf16[1,4,128,512]{3,2,1,0:T(8,128)(2,1)S(1)}, u32[]{:S(2)}, u32[]{:S(2)}) collective-permute-start(bf16[1,4,128,512]{3,2,1,0:T(8,128)(2,1)S(1)} %tie.18), channel_id=1, source_target_pairs={{0,1},{1,0},{2,3},{3,2},{4,5},{5,4},{6,7},{7,6},{8,9},{9,8},{10,11... | collective-permute-start | bytes 1572872 | tf_op jit(solution)/shard_map/ppermute | solution.py:490
  39.1 19.4 %collective-permute-start.12 = (bf16[1,4,128,512]{3,2,1,0:T(8,128)(2,1)}, bf16[1,4,128,512]{3,2,1,0:T(8,128)(2,1)}, u32[]{:S(2)}, u32[]{:S(2)}) collective-permute-start(bf16[1,4,128,512]{3,2,1,0:T(8,128)(2,1)} %fold.13.refs_6_), channel_id=1, source_target_pairs={{0,2},{1,3},{2,0},{3,1},{4,6},{5,7},{6,4},{7,5},{8,10},{9,11},{10,... | collective-permute-start | bytes 1572872 | tf_op jit(solution)/shard_map/ppermute | solution.py:490
  42.9 15.5 %collective-permute-start.18 = (bf16[128,768]{1,0:T(8,128)(2,1)S(1)}, bf16[128,768]{1,0:T(8,128)(2,1)S(1)}, u32[]{:S(2)}, u32[]{:S(2)}) collective-permute-start(bf16[128,768]{1,0:T(8,128)(2,1)S(1)} %get-tuple-element.73.refs_2_.refs_0_.q_ref), channel_id=1, source_target_pairs={{0,2},{1,3},{2,0},{3,1},{4,6},{5,7},{6,4},{7,5},{8,10},{9,11},{10,... | collective-permute-start | bytes 589832 | tf_op jit(solution)/shard_map/ppermute | solution.py:490
  51.1 9.8 %collective-permute-start.11 = (bf16[1,4,128,256]{3,2,1,0:T(8,128)(2,1)}, bf16[1,4,128,256]{3,2,1,0:T(8,128)(2,1)}, u32[]{:S(2)}, u32[]{:S(2)}) collective-permute-start(bf16[1,4,128,256]{3,2,1,0:T(8,128)(2,1)} %tie.20), channel_id=1, source_target_pairs={{0,1},{1,0},{2,3},{3,2},{4,5},{5,4},{6,7},{7,6},{8,9},{9,8},{10,11... | collective-permute-start | bytes 786440 | tf_op jit(solution)/shard_map/ppermute | solution.py:490
  51.1 22.4 %collective-permute-start.17 = (bf16[1,4,128,512]{3,2,1,0:T(8,128)(2,1)}, bf16[1,4,128,512]{3,2,1,0:T(8,128)(2,1)}, u32[]{:S(2)}, u32[]{:S(2)}) collective-permute-start(bf16[1,4,128,512]{3,2,1,0:T(8,128)(2,1)} %fold.14.refs_8_), channel_id=1, source_target_pairs={{0,2},{1,3},{2,0},{3,1},{4,6},{5,7},{6,4},{7,5},{8,10},{9,11},{10,... | collective-permute-start | bytes 1572872 | tf_op jit(solution)/shard_map/ppermute | solution.py:490
  52.9 9.1 %collective-permute-start.19 = (bf16[128,768]{1,0:T(8,128)(2,1)S(1)}, bf16[128,768]{1,0:T(8,128)(2,1)}, u32[]{:S(2)}, u32[]{:S(2)}) collective-permute-start(bf16[128,768]{1,0:T(8,128)(2,1)S(1)} %get-tuple-element.73.refs_2_.refs_0_.q_ref), channel_id=1, source_target_pairs={{0,1},{1,0},{2,3},{3,2},{4,5},{5,4},{6,7},{7,6},{8,9},{9,8},{10,11... | collective-permute-start | bytes 589832 | tf_op jit(solution)/shard_map/ppermute | solution.py:490
  66.1 6.7 %collective-permute-start.21 = (bf16[1,128,768]{2,1,0:T(8,128)(2,1)S(1)}, bf16[1,128,768]{2,1,0:T(8,128)(2,1)S(1)}, u32[]{:S(2)}, u32[]{:S(2)}) collective-permute-start(bf16[1,128,768]{2,1,0:T(8,128)(2,1)S(1)} %get-tuple-element.80), channel_id=1, source_target_pairs={{0,1},{1,0},{2,3},{3,2},{4,5},{5,4},{6,7},{7,6},{8,9},{9,8},{10,11... | collective-permute-start | bytes 589832 | tf_op jit(solution)/shard_map/ppermute | solution.py:490
  66.7 6.1 %collective-permute-start.14 = (bf16[128,512]{1,0:T(8,128)(2,1)S(1)}, bf16[128,512]{1,0:T(8,128)(2,1)S(1)}, u32[]{:S(2)}, u32[]{:S(2)}) collective-permute-start(bf16[128,512]{1,0:T(8,128)(2,1)S(1)} %get-tuple-element.78.refs_2_.refs_0_.q_ref), channel_id=1, source_target_pairs={{0,2},{1,3},{2,0},{3,1},{4,6},{5,7},{6,4},{7,5},{8,10},{9,11},{10,... | collective-permute-start | bytes 393224 | tf_op jit(solution)/shard_map/ppermute | solution.py:490
  68.5 11.8 %collective-permute-start.10 = (bf16[1,4,128,256]{3,2,1,0:T(8,128)(2,1)S(1)}, bf16[1,4,128,256]{3,2,1,0:T(8,128)(2,1)S(1)}, u32[]{:S(2)}, u32[]{:S(2)}) collective-permute-start(bf16[1,4,128,256]{3,2,1,0:T(8,128)(2,1)S(1)} %tie.19), channel_id=1, source_target_pairs={{0,1},{1,0},{2,3},{3,2},{4,5},{5,4},{6,7},{7,6},{8,9},{9,8},{10,11... | collective-permute-start | bytes 786440 | tf_op jit(solution)/shard_map/ppermute | solution.py:490
  68.5 12.2 %collective-permute-start.13 = (bf16[1,4,128,256]{3,2,1,0:T(8,128)(2,1)S(1)}, bf16[1,4,128,256]{3,2,1,0:T(8,128)(2,1)S(1)}, u32[]{:S(2)}, u32[]{:S(2)}) collective-permute-start(bf16[1,4,128,256]{3,2,1,0:T(8,128)(2,1)S(1)} %fold.15.refs_10_), channel_id=1, source_target_pairs={{0,2},{1,3},{2,0},{3,1},{4,6},{5,7},{6,4},{7,5},{8,10},{9,11},{10,... | collective-permute-start | bytes 786440 | tf_op jit(solution)/shard_map/ppermute | solution.py:490
  74.9 6.3 %collective-permute-start.25 = (bf16[128,512]{1,0:T(8,128)(2,1)S(1)}, bf16[128,512]{1,0:T(8,128)(2,1)S(1)}, u32[]{:S(2)}, u32[]{:S(2)}) collective-permute-start(bf16[128,512]{1,0:T(8,128)(2,1)S(1)} %get-tuple-element.81.refs_10_.refs_0_.q_ref), channel_id=1, source_target_pairs={{0,2},{1,3},{2,0},{3,1},{4,6},{5,7},{6,4},{7,5},{8,10},{9,11},{10,... | collective-permute-start | bytes 393224 | tf_op jit(solution)/shard_map/ppermute | solution.py:490
  77.0 4.9 %collective-permute-start.28 = (bf16[1,128,768]{2,1,0:T(8,128)(2,1)S(1)}, bf16[1,128,768]{2,1,0:T(8,128)(2,1)S(1)}, u32[]{:S(2)}, u32[]{:S(2)}) collective-permute-start(bf16[1,128,768]{2,1,0:T(8,128)(2,1)S(1)} %get-tuple-element.86), channel_id=1, source_target_pairs={{0,1},{1,0},{2,3},{3,2},{4,5},{5,4},{6,7},{7,6},{8,9},{9,8},{10,11... | collective-permute-start | bytes 589832 | tf_op jit(solution)/shard_map/ppermute | solution.py:490
  77.0 7.9 %collective-permute-start.29 = (bf16[1,128,768]{2,1,0:T(8,128)(2,1)S(1)}, bf16[1,128,768]{2,1,0:T(8,128)(2,1)S(1)}, u32[]{:S(2)}, u32[]{:S(2)}) collective-permute-start(bf16[1,128,768]{2,1,0:T(8,128)(2,1)S(1)} %fold.16.refs_3_), channel_id=1, source_target_pairs={{0,2},{1,3},{2,0},{3,1},{4,6},{5,7},{6,4},{7,5},{8,10},{9,11},{10,... | collective-permute-start | bytes 589832 | tf_op jit(solution)/shard_map/ppermute | solution.py:490
  80.8 4.7 %collective-permute-start.26 = (bf16[128,512]{1,0:T(8,128)(2,1)S(1)}, bf16[128,512]{1,0:T(8,128)(2,1)S(1)}, u32[]{:S(2)}, u32[]{:S(2)}) collective-permute-start(bf16[128,512]{1,0:T(8,128)(2,1)S(1)} %get-tuple-element.81.refs_10_.refs_0_.q_ref), channel_id=1, source_target_pairs={{0,1},{1,0},{2,3},{3,2},{4,5},{5,4},{6,7},{7,6},{8,9},{9,8},{10,11... | collective-permute-start | bytes 393224 | tf_op jit(solution)/shard_map/ppermute | solution.py:490
  88.6 4.6 %collective-permute-start.31 = (bf16[1,128,512]{2,1,0:T(8,128)(2,1)S(1)}, bf16[1,128,512]{2,1,0:T(8,128)(2,1)S(1)}, u32[]{:S(2)}, u32[]{:S(2)}) collective-permute-start(bf16[1,128,512]{2,1,0:T(8,128)(2,1)S(1)} %get-tuple-element.90), channel_id=1, source_target_pairs={{0,1},{1,0},{2,3},{3,2},{4,5},{5,4},{6,7},{7,6},{8,9},{9,8},{10,11... | collective-permute-start | bytes 393224 | tf_op jit(solution)/shard_map/ppermute | solution.py:490
  88.7 4.5 %collective-permute-start.22 = (bf16[128,256]{1,0:T(8,128)(2,1)S(1)}, bf16[128,256]{1,0:T(8,128)(2,1)S(1)}, u32[]{:S(2)}, u32[]{:S(2)}) collective-permute-start(bf16[128,256]{1,0:T(8,128)(2,1)S(1)} %get-tuple-element.83.refs_2_.refs_0_.q_ref), channel_id=1, source_target_pairs={{0,2},{1,3},{2,0},{3,1},{4,6},{5,7},{6,4},{7,5},{8,10},{9,11},{10,... | collective-permute-start | bytes 196616 | tf_op jit(solution)/shard_map/ppermute | solution.py:490
  90.5 7.7 %collective-permute-start.34 = (bf16[1,128,512]{2,1,0:T(8,128)(2,1)S(1)}, bf16[1,128,512]{2,1,0:T(8,128)(2,1)S(1)}, u32[]{:S(2)}, u32[]{:S(2)}) collective-permute-start(bf16[1,128,512]{2,1,0:T(8,128)(2,1)S(1)} %get-tuple-element.95), channel_id=1, source_target_pairs={{0,1},{1,0},{2,3},{3,2},{4,5},{5,4},{6,7},{7,6},{8,9},{9,8},{10,11... | collective-permute-start | bytes 393224 | tf_op jit(solution)/shard_map/ppermute | solution.py:490
  91.0 7.7 %collective-permute-start.35 = (bf16[1,128,512]{2,1,0:T(8,128)(2,1)S(1)}, bf16[1,128,512]{2,1,0:T(8,128)(2,1)S(1)}, u32[]{:S(2)}, u32[]{:S(2)}) collective-permute-start(bf16[1,128,512]{2,1,0:T(8,128)(2,1)S(1)} %fold.17.refs_3_), channel_id=1, source_target_pairs={{0,2},{1,3},{2,0},{3,1},{4,6},{5,7},{6,4},{7,5},{8,10},{9,11},{10,... | collective-permute-start | bytes 393224 | tf_op jit(solution)/shard_map/ppermute | solution.py:490
  93.2 7.0 %collective-permute-start.37 = (bf16[1,128,512]{2,1,0:T(8,128)(2,1)S(1)}, bf16[1,128,512]{2,1,0:T(8,128)(2,1)S(1)}, u32[]{:S(2)}, u32[]{:S(2)}) collective-permute-start(bf16[1,128,512]{2,1,0:T(8,128)(2,1)S(1)} %get-tuple-element.100), channel_id=1, source_target_pairs={{0,1},{1,0},{2,3},{3,2},{4,5},{5,4},{6,7},{7,6},{8,9},{9,8},{10,11... | collective-permute-start | bytes 393224 | tf_op jit(solution)/shard_map/ppermute | solution.py:490
  93.9 6.3 %collective-permute-start.38 = (bf16[1,128,512]{2,1,0:T(8,128)(2,1)S(1)}, bf16[1,128,512]{2,1,0:T(8,128)(2,1)S(1)}, u32[]{:S(2)}, u32[]{:S(2)}) collective-permute-start(bf16[1,128,512]{2,1,0:T(8,128)(2,1)S(1)} %fold.18.refs_10_), channel_id=1, source_target_pairs={{0,2},{1,3},{2,0},{3,1},{4,6},{5,7},{6,4},{7,5},{8,10},{9,11},{10,... | collective-permute-start | bytes 393224 | tf_op jit(solution)/shard_map/ppermute | solution.py:490
  99.6 4.3 %collective-permute-start.36 = (bf16[1,128,256]{2,1,0:T(8,128)(2,1)S(1)}, bf16[1,128,256]{2,1,0:T(8,128)(2,1)S(1)}, u32[]{:S(2)}, u32[]{:S(2)}) collective-permute-start(bf16[1,128,256]{2,1,0:T(8,128)(2,1)S(1)} %fold.19.refs_3_), channel_id=1, source_target_pairs={{0,2},{1,3},{2,0},{3,1},{4,6},{5,7},{6,4},{7,5},{8,10},{9,11},{10,... | collective-permute-start | bytes 196616 | tf_op jit(solution)/shard_map/ppermute | solution.py:490
  104.4 5.0 %collective-permute-start.41 = (f32[8,128]{1,0:T(8,128)S(1)}, f32[8,128]{1,0:T(8,128)S(1)}, u32[]{:S(2)}, u32[]{:S(2)}) collective-permute-start(f32[8,128]{1,0:T(8,128)S(1)} %get-tuple-element.103.refs_0_), channel_id=1, source_target_pairs={{0,12},{4,0},{8,4},{12,8},{1,13},{5,1},{9,5},{13,9},{2,14},{6,2},{... | collective-permute-start | bytes 12296 | tf_op jit(solution)/shard_map/ppermute | solution.py:514
  108.1 4.5 %collective-permute-start.40 = (f32[8,128]{1,0:T(8,128)S(1)}, f32[8,128]{1,0:T(8,128)S(1)}, u32[]{:S(2)}, u32[]{:S(2)}) collective-permute-start(f32[8,128]{1,0:T(8,128)S(1)} %get-tuple-element.103.refs_0_), channel_id=1, source_target_pairs={{0,8},{4,12},{8,0},{12,4},{1,9},{5,13},{9,1},{13,5},{2,10},{6,14},... | collective-permute-start | bytes 12296 | tf_op jit(solution)/shard_map/ppermute | solution.py:514
  108.1 5.4 %collective-permute-start.39 = (f32[8,128]{1,0:T(8,128)S(1)}, f32[8,128]{1,0:T(8,128)S(1)}, u32[]{:S(2)}, u32[]{:S(2)}) collective-permute-start(f32[8,128]{1,0:T(8,128)S(1)} %get-tuple-element.103.refs_0_), channel_id=1, source_target_pairs={{0,4},{4,8},{8,12},{12,0},{1,5},{5,9},{9,13},{13,1},{2,6},{6,10},{... | collective-permute-start | bytes 12296 | tf_op jit(solution)/shard_map/ppermute | solution.py:514
  113.9 6.4 %collective-permute-start.42 = (bf16[64,2048]{1,0:T(8,128)(2,1)S(1)}, bf16[64,2048]{1,0:T(8,128)(2,1)S(1)}, u32[]{:S(2)}, u32[]{:S(2)}) collective-permute-start(bf16[64,2048]{1,0:T(8,128)(2,1)S(1)} %get-tuple-element.105), channel_id=1, source_target_pairs={{0,2},{1,3},{2,0},{3,1},{4,6},{5,7},{6,4},{7,5},{8,10},{9,11},{10,... | collective-permute-start | bytes 786440 | tf_op jit(solution)/shard_map/ppermute | solution.py:490
  114.5 6.4 %collective-permute-start.43 = (bf16[64,2048]{1,0:T(8,128)(2,1)S(1)}, bf16[64,2048]{1,0:T(8,128)(2,1)S(1)}, u32[]{:S(2)}, u32[]{:S(2)}) collective-permute-start(bf16[64,2048]{1,0:T(8,128)(2,1)S(1)} %get-tuple-element.105), channel_id=1, source_target_pairs={{0,1},{1,0},{2,3},{3,2},{4,5},{5,4},{6,7},{7,6},{8,9},{9,8},{10,11... | collective-permute-start | bytes 786440 | tf_op jit(solution)/shard_map/ppermute | solution.py:490
  120.3 8.7 %collective-permute-start.50 = (bf16[64,2048]{1,0:T(8,128)(2,1)S(1)}, bf16[64,2048]{1,0:T(8,128)(2,1)S(1)}, u32[]{:S(2)}, u32[]{:S(2)}) collective-permute-start(bf16[64,2048]{1,0:T(8,128)(2,1)S(1)} %get-tuple-element.112), channel_id=1, source_target_pairs={{0,2},{1,3},{2,0},{3,1},{4,6},{5,7},{6,4},{7,5},{8,10},{9,11},{10,... | collective-permute-start | bytes 786440 | tf_op jit(solution)/shard_map/ppermute | solution.py:490
  125.8 8.2 %collective-permute-start.46 = (bf16[1,4,16,1024]{3,2,1,0:T(8,128)(2,1)S(1)}, bf16[1,4,16,1024]{3,2,1,0:T(8,128)(2,1)S(1)}, u32[]{:S(2)}, u32[]{:S(2)}) collective-permute-start(bf16[1,4,16,1024]{3,2,1,0:T(8,128)(2,1)S(1)} %get-tuple-element.108), channel_id=1, source_target_pairs={{0,8},{4,12},{8,0},{12,4},{1,9},{5,13},{9,1},{13,5},{2,10},{6,14},... | collective-permute-start | bytes 393224 | tf_op jit(solution)/shard_map/ppermute | solution.py:514
  127.0 14.9 %collective-permute-start.51 = (bf16[64,2048]{1,0:T(8,128)(2,1)S(1)}, bf16[64,2048]{1,0:T(8,128)(2,1)S(1)}, u32[]{:S(2)}, u32[]{:S(2)}) collective-permute-start(bf16[64,2048]{1,0:T(8,128)(2,1)S(1)} %get-tuple-element.112), channel_id=1, source_target_pairs={{0,1},{1,0},{2,3},{3,2},{4,5},{5,4},{6,7},{7,6},{8,9},{9,8},{10,11... | collective-permute-start | bytes 786440 | tf_op jit(solution)/shard_map/ppermute | solution.py:490
  134.0 8.0 %collective-permute-start.52 = (bf16[64,2048]{1,0:T(8,128)(2,1)S(1)}, bf16[64,2048]{1,0:T(8,128)(2,1)S(1)}, u32[]{:S(2)}, u32[]{:S(2)}) collective-permute-start(bf16[64,2048]{1,0:T(8,128)(2,1)S(1)} %tie.21), channel_id=1, source_target_pairs={{0,1},{1,0},{2,3},{3,2},{4,5},{5,4},{6,7},{7,6},{8,9},{9,8},{10,11... | collective-permute-start | bytes 786440 | tf_op jit(solution)/shard_map/ppermute | solution.py:490
  138.0 14.4 %collective-permute-start.48 = (bf16[2,4,16,1024]{3,2,1,0:T(8,128)(2,1)S(1)}, bf16[2,4,16,1024]{3,2,1,0:T(8,128)(2,1)S(1)}, u32[]{:S(2)}, u32[]{:S(2)}) collective-permute-start(bf16[2,4,16,1024]{3,2,1,0:T(8,128)(2,1)S(1)} %get-tuple-element.111.refs_5_), channel_id=1, source_target_pairs={{0,4},{4,0},{8,12},{12,8},{1,5},{5,1},{9,13},{13,9},{2,6},{6,2},{1... | collective-permute-start | bytes 786440 | tf_op jit(solution)/shard_map/ppermute | solution.py:490
  138.1 11.6 %collective-permute-start.45 = (bf16[1,4,16,1024]{3,2,1,0:T(8,128)(2,1)S(1)}, bf16[1,4,16,1024]{3,2,1,0:T(8,128)(2,1)S(1)}, u32[]{:S(2)}, u32[]{:S(2)}) collective-permute-start(bf16[1,4,16,1024]{3,2,1,0:T(8,128)(2,1)S(1)} %get-tuple-element.107), channel_id=1, source_target_pairs={{0,4},{4,8},{8,12},{12,0},{1,5},{5,9},{9,13},{13,1},{2,6},{6,10},{... | collective-permute-start | bytes 393224 | tf_op jit(solution)/shard_map/ppermute | solution.py:514
  140.1 12.3 %collective-permute-start.47 = (bf16[1,4,16,1024]{3,2,1,0:T(8,128)(2,1)S(1)}, bf16[1,4,16,1024]{3,2,1,0:T(8,128)(2,1)S(1)}, u32[]{:S(2)}, u32[]{:S(2)}) collective-permute-start(bf16[1,4,16,1024]{3,2,1,0:T(8,128)(2,1)S(1)} %get-tuple-element.109.refs_5_), channel_id=1, source_target_pairs={{0,12},{4,0},{8,4},{12,8},{1,13},{5,1},{9,5},{13,9},{2,14},{6,2},{... | collective-permute-start | bytes 393224 | tf_op jit(solution)/shard_map/ppermute | solution.py:514
  152.4 13.9 %collective-permute-start.53 = (bf16[2,4,16,1024]{3,2,1,0:T(8,128)(2,1)S(1)}, bf16[2,4,16,1024]{3,2,1,0:T(8,128)(2,1)S(1)}, u32[]{:S(2)}, u32[]{:S(2)}) collective-permute-start(bf16[2,4,16,1024]{3,2,1,0:T(8,128)(2,1)S(1)} %tie.22.refs_5_), channel_id=1, source_target_pairs={{0,4},{4,0},{8,12},{12,8},{1,5},{5,1},{9,13},{13,9},{2,6},{6,2},{1... | collective-permute-start | bytes 786440 | tf_op jit(solution)/shard_map/ppermute | solution.py:490
  152.5 8.4 %collective-permute-start.49 = (bf16[1,4,16,1024]{3,2,1,0:T(8,128)(2,1)S(1)}, bf16[1,4,16,1024]{3,2,1,0:T(8,128)(2,1)S(1)}, u32[]{:S(2)}, u32[]{:S(2)}) collective-permute-start(bf16[1,4,16,1024]{3,2,1,0:T(8,128)(2,1)S(1)} %fold.20), channel_id=1, source_target_pairs={{0,8},{4,12},{8,0},{12,4},{1,9},{5,13},{9,1},{13,5},{2,10},{6,14},... | collective-permute-start | bytes 393224 | tf_op jit(solution)/shard_map/ppermute | solution.py:490
  160.9 6.5 %collective-permute-start.57 = (bf16[1,4,16,1024]{3,2,1,0:T(8,128)(2,1)S(1)}, bf16[1,4,16,1024]{3,2,1,0:T(8,128)(2,1)S(1)}, u32[]{:S(2)}, u32[]{:S(2)}) collective-permute-start(bf16[1,4,16,1024]{3,2,1,0:T(8,128)(2,1)S(1)} %tie.25), channel_id=1, source_target_pairs={{0,12},{4,0},{8,4},{12,8},{1,13},{5,1},{9,5},{13,9},{2,14},{6,2},{... | collective-permute-start | bytes 393224 | tf_op jit(solution)/shard_map/ppermute | solution.py:514
  163.2 17.8 %collective-permute-start.56 = (bf16[1,4,16,1024]{3,2,1,0:T(8,128)(2,1)S(1)}, bf16[1,4,16,1024]{3,2,1,0:T(8,128)(2,1)S(1)}, u32[]{:S(2)}, u32[]{:S(2)}) collective-permute-start(bf16[1,4,16,1024]{3,2,1,0:T(8,128)(2,1)S(1)} %tie.24), channel_id=1, source_target_pairs={{0,8},{4,12},{8,0},{12,4},{1,9},{5,13},{9,1},{13,5},{2,10},{6,14},... | collective-permute-start | bytes 393224 | tf_op jit(solution)/shard_map/ppermute | solution.py:514
  165.7 15.4 %collective-permute-start.55 = (bf16[1,4,16,1024]{3,2,1,0:T(8,128)(2,1)S(1)}, bf16[1,4,16,1024]{3,2,1,0:T(8,128)(2,1)S(1)}, u32[]{:S(2)}, u32[]{:S(2)}) collective-permute-start(bf16[1,4,16,1024]{3,2,1,0:T(8,128)(2,1)S(1)} %tie.23), channel_id=1, source_target_pairs={{0,4},{4,8},{8,12},{12,0},{1,5},{5,9},{9,13},{13,1},{2,6},{6,10},{... | collective-permute-start | bytes 393224 | tf_op jit(solution)/shard_map/ppermute | solution.py:514
  166.5 16.0 %collective-permute-start.54 = (bf16[1,4,16,1024]{3,2,1,0:T(8,128)(2,1)S(1)}, bf16[1,4,16,1024]{3,2,1,0:T(8,128)(2,1)S(1)}, u32[]{:S(2)}, u32[]{:S(2)}) collective-permute-start(bf16[1,4,16,1024]{3,2,1,0:T(8,128)(2,1)S(1)} %fold.21), channel_id=1, source_target_pairs={{0,8},{4,12},{8,0},{12,4},{1,9},{5,13},{9,1},{13,5},{2,10},{6,14},... | collective-permute-start | bytes 393224 | tf_op jit(solution)/shard_map/ppermute | solution.py:490
  (20 other events, 92.8 us)

commit v10 on v9

--- a/solution.py
+++ b/solution.py
@@ -25,6 +25,7 @@
 
 
 LIGHT = pl.CostEstimate(flops=1000, bytes_accessed=1000, transcendentals=0)
+STEP = pl.CostEstimate(flops=1000, bytes_accessed=4_000_000, transcendentals=0)
 
 
 def far(x):
@@ -129,7 +130,7 @@
     refs[-1][...] = sum(r[...].astype(f32) for r in refs[:count]).astype(bf16)
 
 
-def fold(terms, after=()):
+def fold(terms, after=(), told=LIGHT):
     half = terms[0].shape[0] // 2 if len(terms) == 2 else terms[-1].shape[0] // 2
     tail = terms[0].shape[1:]
     steps = 2 if tail[-1] % 256 == 0 else 1
@@ -144,7 +145,7 @@
         out_specs=pl.BlockSpec(block, lambda j: (0,) + middle + (j,)),
         out_shape=jax.ShapeDtypeStruct((half,) + tail, bf16),
         compiler_params=params(),
-        cost_estimate=LIGHT,
+        cost_estimate=told,
         name="fold",
     )(*terms, *after)
 
@@ -435,45 +436,42 @@
     )(order, *[b.reshape(zs, piece, width) for b in blocks], far(w_out), *after)
 
 
-def close_kernel(counts, at_ref, t_ref, *refs):
-    out_ref, first = refs[-1], 0
-    owners = refs[0].shape[1]
-    for r, row in enumerate(counts):
-        column = 0
-        for count in row:
-            terms = refs[first:first + count]
-            first += count
-            span = terms[0].shape[-1]
-            for p in range(owners):
-                total = t_ref[r * owners + p, :, column:column + span].astype(f32)
-                for term in terms:
-                    total = total + term[0, p ^ at_ref[0]].astype(f32)
-                out_ref[r * owners + p, :, column:column + span] = total.astype(bf16)
-            column += span
-
-
-def close(place, index, tokens, chunks):
-    _, owners, piece, _ = chunks[0][0][0].shape
-    blocks, width = len(chunks) * owners, sum(terms[0].shape[-1] for terms in chunks[0])
-    flat = [term for row in chunks for terms in row for term in terms]
-    return pl.pallas_call(
-        functools.partial(close_kernel, [[len(terms) for terms in row] for row in chunks]),
+def close_kernel(count, at_ref, t_ref, *refs):
+    out_ref, mark_ref = refs[-2:]
+    mark_ref[...] = jnp.zeros_like(mark_ref)
+    for p in range(out_ref.shape[0]):
+        total = t_ref[p].astype(f32)
+        for term in refs[:count]:
+            total = total + term[0, p ^ at_ref[0]].astype(f32)
+        out_ref[p] = total.astype(bf16)
+
+
+def close(place, index, tokens, chunks, r, g, terms, out, after):
+    _, owners, piece, span = terms[0].shape
+    at = jnp.stack([place, index * chunks + r]).astype(jnp.int32)
+    into = [] if out is None else [out]
+    return pl.pallas_call(
+        functools.partial(close_kernel, len(terms)),
         grid_spec=pltpu.PrefetchScalarGridSpec(
             num_scalar_prefetch=1,
             grid=(1,),
-            in_specs=[pl.BlockSpec((blocks, piece, width), lambda j, at: (at[1], 0, 0))]
-            + [pl.BlockSpec((1,) + t.shape[1:], lambda j, at: (0, 0, 0, 0)) for t in flat],
-            out_specs=pl.BlockSpec((blocks, piece, width), lambda j, at: (0, 0, 0)),
-        ),
-        out_shape=jax.ShapeDtypeStruct((blocks, piece, width), bf16),
-        compiler_params=params(),
-        cost_estimate=LIGHT,
+            in_specs=[pl.BlockSpec((owners, piece, span), lambda j, at: (at[1], 0, g))]
+            + [pl.BlockSpec((1,) + t.shape[1:], lambda j, at: (0, 0, 0, 0)) for t in terms]
+            + anywhere(into) + anywhere(after),
+            out_specs=(
+                pl.BlockSpec((owners, piece, span), lambda j, at: (r, 0, g)),
+                pl.BlockSpec((8, DH), lambda j, at: (0, 0)),
+            ),
+        ),
+        out_shape=(
+            jax.ShapeDtypeStruct((chunks * owners, piece, tokens.shape[1]), bf16),
+            jax.ShapeDtypeStruct((8, DH), f32),
+        ),
+        input_output_aliases={} if out is None else {2 + len(terms): 0},
+        compiler_params=params(),
+        cost_estimate=STEP,
         name="close",
-    )(
-        jnp.stack([place, index]).astype(jnp.int32),
-        far(tokens.reshape(-1, piece, width)),
-        *flat,
-    )
+    )(at, far(tokens.reshape(-1, piece, tokens.shape[1])), *terms, *into, *after)
 
 
 def bits_of(axis):
@@ -492,10 +490,10 @@
     )
 
 
-def scatter(keep, gots, axis, after=()):
+def scatter(keep, gots, axis, after=(), told=LIGHT):
     terms, sent = [keep, gots[0]], gots[-1]
     for b in range(1, bits_of(axis)):
-        sent = fold([keep, gots[-1]] if b == 1 else terms, after)
+        sent = fold([keep, gots[-1]] if b == 1 else terms, after, told)
         terms.append(swap(sent, axis, b))
     return terms, sent
 
@@ -604,42 +602,35 @@
     gated = gate_rows(all_stats(stats[last], "head"), atts, rests, chunks)
     columns = w_out.shape[1]
     straight = piece % 16 == 0 and zs & (zs - 1) == 0
-    steps = jnp.arange(zs, dtype=jnp.int32)
-    shifted = (index + steps) % zs
-    halved = index ^ reverse(steps, bits_of("head")) if straight else shifted
-    results, last_sent, before = [], [], {}
+    out, last_out = None, []
+    if not straight:
+        for r, rows in enumerate(gated):
+            whole = jnp.concatenate(gather(rows, "hist"))
+            whole = jnp.dot(whole, w_out, preferred_element_type=f32).astype(bf16)
+            whole = whole.reshape(owners, zs, piece, -1).swapaxes(0, 1)
+            whole = lax.psum_scatter(whole, "head", scatter_dimension=0, tiled=True)
+            out, _ = close(place, index, tokens, chunks, r, 0, [whole], out, [])
+        return out.reshape(cand // zs, -1)
+    halved = index ^ reverse(jnp.arange(zs, dtype=jnp.int32), bits_of("head"))
+    groups = 2 if columns % 1024 == 0 else 1
+    span = columns // groups
+    pieces, first_out, counts = [], [], [zs // 2] * 2 if zs > 1 else [1]
     for r, rows in enumerate(gated):
-        results.append([])
-        if not straight:
-            blocks = gather(rows, "hist")
-            whole = jnp.dot(jnp.concatenate(blocks), w_out, preferred_element_type=f32)
-            whole = whole.astype(bf16).reshape(owners, zs, piece, -1).swapaxes(0, 1)
-            whole = lax.psum_scatter(whole, "head", scatter_dimension=0, tiled=True)
-            results[-1].append([whole])
-            continue
-        blocks = gather(rows, "hist", before.get(r, []))
-        spans = [columns // 2] * 2 if columns % 1024 == 0 else [columns]
-        for g, span in enumerate(spans):
-            direct = len(spans) == 1 or g == r
-            order = shifted if direct else halved
-            counts = [1] * zs if direct else [zs // 2] * 2
-            own, *others = output(order, counts, blocks, w_out, g * span, span, last_sent)
-            others = [tie(x, before.get((r, g), [])) for x in others]
-            last_sent = others[-1:]
-            if direct:
-                arrived = [shift(x, "head", k + 1) for k, x in enumerate(others)]
-                terms = [own] + arrived
-                if r == 0:
-                    before[1] = arrived[zs // 2 - 1:zs // 2]
-                    before[1, 0] = arrived
-            else:
-                arrived = swap(others[0], "head", 0)
-                terms, _ = scatter(own, [arrived], "head")
-                if r == 0:
-                    before[1, 0] = before.get((1, 0), []) + [arrived]
-                    before[1, 1] = [terms[-1]]
-            results[-1].append(terms)
-    out = close(place, index, tokens, results)
+        blocks = gather(rows, "hist", first_out)
+        for g in range(groups):
+            own, *others = output(halved, counts, blocks, w_out, g * span, span, last_out)
+            pieces.append((r, g, own, [swap(x, "head", 0) for x in others]))
+            last_out, first_out = [own], first_out or [own]
+    closing, chain = [], last_out
+    for r, g, own, arrived in pieces:
+        terms, sent = scatter(own, arrived, "head", chain, STEP) if arrived else ([own], own)
+        chain = [sent]
+        closing.append((r, g, terms))
+        if len(closing) > 1:
+            out, mark = close(place, index, tokens, chunks, *closing.pop(0), out, chain)
+            chain = [mark]
+    for last_piece in closing:
+        out, _ = close(place, index, tokens, chunks, *last_piece, out, [])
     return out.reshape(cand // zs, -1)
 
 

time: 186 us -> 176 us (0.946)
  waiting for transfers between devices: 61.1 us -> 47.9 us
  Pallas kernels: 79.1 us -> 85.3 us
  starting transfers between devices: 42 us -> 38.8 us
    ppermute x9 -> x3, waiting for transfers between devices: 29.4 us -> 4.39 us  [shift(): return lax.ppermute(x, axis, [(i, (i + k) % count) for i in range(count)])]
    ppermute x49 -> x53, waiting for transfers between devices: 31.7 us -> 43.5 us  [swap(): lax.ppermute(x, axis, [(i, i ^ 1 << bit) for i in range(lax.axis_size(axi...]
    ppermute x9 -> x3, starting transfers between devices: 15.1 us -> 4.64 us  [shift(): return lax.ppermute(x, axis, [(i, (i + k) % count) for i in range(count)])]
    ppermute x49 -> x53, starting transfers between devices: 26.8 us -> 34.2 us  [swap(): lax.ppermute(x, axis, [(i, i ^ 1 << bit) for i in range(lax.axis_size(axi...]
    pallas_call x1 -> x4, Pallas kernels: 2.68 us -> 8.68 us  [close(): pl.pallas_call(functools.partial(close_kernel, len(terms)), grid_spec=plt...]
    pallas_call x11 -> x13, Pallas kernels: 4.29 us -> 4.54 us  [fold(): pl.pallas_call(functools.partial(fold_kernel, len(terms)), grid=(steps,),...]
  transfers between devices with their start and end apart: 58 -> 56, of which waited for: 21 -> 17; matrix products, arithmetic and copies ran while one was open for 0% -> 0% of each run, Pallas kernels for 36% -> 42%
where the time goes in v10:
time: 176 us; the launch traced here: 175 us
  Pallas kernels  85.3 us (48%)
  waiting for transfers between devices  47.9 us (27%)
  starting transfers between devices  38.8 us (22%)
  local copies, waits for them, and re-layouts  2.4 us (1%)
    ppermute x53, waiting for transfers between devices, swap(): lax.ppermute(x, axis, [(i, i ^ 1 << bit) for i in range(lax.axis_size(axi...  43.5 us
    pallas_call x5, Pallas kernels, project(): pl.pallas_call(functools.partial(project_kernel, parts, owners, len(after...  37.9 us
    ppermute x53, starting transfers between devices, swap(): lax.ppermute(x, axis, [(i, i ^ 1 << bit) for i in range(lax.axis_size(axi...  34.2 us
    pallas_call x4, Pallas kernels, output(): pl.pallas_call(functools.partial(output_kernel, owners, len(after)), grid...  15.9 us
    pallas_call x4, Pallas kernels, attend(): pl.pallas_call(functools.partial(attend_kernel, owners, len(counts)), gri...  12.4 us
    pallas_call x4, Pallas kernels, close(): pl.pallas_call(functools.partial(close_kernel, len(terms)), grid_spec=plt...  8.68 us
    ppermute x3, starting transfers between devices, shift(): return lax.ppermute(x, axis, [(i, (i + k) % count) for i in range(count)])  4.64 us
    pallas_call x13, Pallas kernels, fold(): pl.pallas_call(functools.partial(fold_kernel, len(terms)), grid=(steps,),...  4.54 us
  transfers between devices with their start and end apart: 56, of which 17 were waited for; matrix products, arithmetic and copies ran while one was open for 0% of the time, Pallas kernels for 42%

profile of v10, /device:TPU:0, one launch (start us, length us, event | category | flops | bytes accessed | tf_op | source)
XLA Modules:
  0.0 175.1 jit_solution(1566373612827567604)
XLA Ops:
  0.0 5.5 %project.5 = (bf16[2,4,128,256]{3,2,1,0:T(8,128)(2,1)S(1)}, bf16[1,4,128,256]{3,2,1,0:T(8,128)(2,1)S(1)}, bf16[1,4,128,256]{3,2,1,0:T(8,128)(2,1)S(1)}) custom-call(s32[1]{0:T(128)} %bitcast.at_ref, bf16[4,2,4,16,2048]{4,3,2,1,0:T(8,128)(2,1)} %bitcast.56, bf16[4,2,4,16,2048]{4,3,2,1,0:T(8,128)(2,1)} %bitcast.57, bf16[4,2,4,16,2048]{4,3,2,1,0:T(8,128)(2,1)} %bitcast.58, ...), custom_call_target="tpu_custom_call" | custom-call | flops 1000 | bytes 1000 | tf_op jit(solution)/shard_map/project/pallas_call | solution.py:81
  6.1 8.7 %project.6 = (bf16[2,4,128,512]{3,2,1,0:T(8,128)(2,1)S(1)}, bf16[1,4,128,512]{3,2,1,0:T(8,128)(2,1)S(1)}, bf16[1,4,128,512]{3,2,1,0:T(8,128)(2,1)S(1)}) custom-call(s32[1]{0:T(128)} %bitcast.at_ref, bf16[4,2,4,16,2048]{4,3,2,1,0:T(8,128)(2,1)} %bitcast.60, bf16[4,2,4,16,2048]{4,3,2,1,0:T(8,128)(2,1)} %bitcast.61, bf16[4,2,4,16,2048]{4,3,2,1,0:T(8,128)(2,1)} %bitcast.62, ...), custom_call_target="tpu_custom_call" | custom-call | flops 1000 | bytes 1000 | tf_op jit(solution)/shard_map/project/pallas_call | solution.py:81
  15.8 3.0 %collective-permute-start.4 = (bf16[1,4,128,256]{3,2,1,0:T(8,128)(2,1)S(1)}, bf16[1,4,128,256]{3,2,1,0:T(8,128)(2,1)S(1)}, u32[]{:S(2)}, u32[]{:S(2)}) collective-permute-start(bf16[1,4,128,256]{3,2,1,0:T(8,128)(2,1)S(1)} %fold.13.refs_8_), channel_id=1, source_target_pairs={{0,2},{1,3},{2,0},{3,1},{4,6},{5,7},{6,4},{7,5},{8,10},{9,11},{10,... | collective-permute-start | bytes 786440 | tf_op jit(solution)/shard_map/ppermute | solution.py:488
  18.7 8.7 %project.7 = (bf16[2,4,128,512]{3,2,1,0:T(8,128)(2,1)S(1)}, bf16[1,4,128,512]{3,2,1,0:T(8,128)(2,1)S(1)}, bf16[1,4,128,512]{3,2,1,0:T(8,128)(2,1)S(1)}) custom-call(s32[1]{0:T(128)} %bitcast.at_ref, bf16[4,2,4,16,2048]{4,3,2,1,0:T(8,128)(2,1)} %bitcast.64, bf16[4,2,4,16,2048]{4,3,2,1,0:T(8,128)(2,1)} %bitcast.65, bf16[4,2,4,16,2048]{4,3,2,1,0:T(8,128)(2,1)} %bitcast.66, ...), custom_call_target="tpu_custom_call" | custom-call | flops 1000 | bytes 1000 | tf_op jit(solution)/shard_map/project/pallas_call | solution.py:81
  28.5 8.8 %project.8 = (bf16[2,4,128,512]{3,2,1,0:T(8,128)(2,1)S(1)}, bf16[1,4,128,512]{3,2,1,0:T(8,128)(2,1)S(1)}, bf16[1,4,128,512]{3,2,1,0:T(8,128)(2,1)S(1)}) custom-call(s32[1]{0:T(128)} %bitcast.at_ref, bf16[4,2,4,16,2048]{4,3,2,1,0:T(8,128)(2,1)} %bitcast.68, bf16[4,2,4,16,2048]{4,3,2,1,0:T(8,128)(2,1)} %bitcast.69, bf16[4,2,4,16,2048]{4,3,2,1,0:T(8,128)(2,1)} %bitcast.70, ...), custom_call_target="tpu_custom_call" | custom-call | flops 1000 | bytes 1000 | tf_op jit(solution)/shard_map/project/pallas_call | solution.py:81
  38.2 0.9 fold.15.refs_6_
  39.1 1.9 %collective-permute-start.12 = (bf16[1,4,128,512]{3,2,1,0:T(8,128)(2,1)}, bf16[1,4,128,512]{3,2,1,0:T(8,128)(2,1)}, u32[]{:S(2)}, u32[]{:S(2)}) collective-permute-start(bf16[1,4,128,512]{3,2,1,0:T(8,128)(2,1)} %fold.15.refs_6_), channel_id=1, source_target_pairs={{0,2},{1,3},{2,0},{3,1},{4,6},{5,7},{6,4},{7,5},{8,10},{9,11},{10,... | collective-permute-start | bytes 1572872 | tf_op jit(solution)/shard_map/ppermute | solution.py:488
  41.0 1.4 collective-permute-done.8.refs_5_
  43.2 1.0 fold.16.refs_8_
  44.2 6.2 %project.9 = (bf16[2,4,128,256]{3,2,1,0:T(8,128)(2,1)S(1)}, bf16[1,4,128,256]{3,2,1,0:T(8,128)(2,1)S(1)}, bf16[1,4,128,256]{3,2,1,0:T(8,128)(2,1)}) custom-call(s32[1]{0:T(128)} %bitcast.at_ref, bf16[4,2,4,16,2048]{4,3,2,1,0:T(8,128)(2,1)} %bitcast.72, bf16[4,2,4,16,2048]{4,3,2,1,0:T(8,128)(2,1)} %bitcast.73, bf16[4,2,4,16,2048]{4,3,2,1,0:T(8,128)(2,1)} %bitcast.74, ...), custom_call_target="tpu_custom_call" | custom-call | flops 1000 | bytes 1000 | tf_op jit(solution)/shard_map/project/pallas_call | solution.py:81
  51.1 1.8 %collective-permute-start.17 = (bf16[1,4,128,512]{3,2,1,0:T(8,128)(2,1)}, bf16[1,4,128,512]{3,2,1,0:T(8,128)(2,1)}, u32[]{:S(2)}, u32[]{:S(2)}) collective-permute-start(bf16[1,4,128,512]{3,2,1,0:T(8,128)(2,1)} %fold.16.refs_8_), channel_id=1, source_target_pairs={{0,2},{1,3},{2,0},{3,1},{4,6},{5,7},{6,4},{7,5},{8,10},{9,11},{10,... | collective-permute-start | bytes 1572872 | tf_op jit(solution)/shard_map/ppermute | solution.py:488
  53.1 5.3 %collective-permute-done.18.refs_1_ = bf16[128,768]{1,0:T(8,128)(2,1)S(1)} collective-permute-done((bf16[128,768]{1,0:T(8,128)(2,1)S(1)}, bf16[128,768]{1,0:T(8,128)(2,1)S(1)}, u32[]{:S(2)}, u32[]{:S(2)}) %collective-permute-start.18) | collective-permute-done | bytes 196640 | tf_op jit(solution)/shard_map/ppermute | solution.py:488
  58.5 1.0 copy-done.3
  59.5 1.4 activate.5
  60.9 1.1 fold.17.refs_10_
  62.1 4.1 %attend.4 = (bf16[2,128,768]{2,1,0:T(8,128)(2,1)S(1)}, bf16[1,128,768]{2,1,0:T(8,128)(2,1)S(1)}, bf16[1,128,768]{2,1,0:T(8,128)(2,1)S(1)}) custom-call(s32[1]{0:T(128)} %bitcast.at_ref, bf16[128,768]{1,0:T(8,128)(2,1)S(1)} %get-tuple-element.75.refs_2_.refs_0_.q_ref, bf16[128,768]{1,0:T(8,128)(2,1)S(1)} %collective-permute-done.18.refs_1_, ...), custom_call_target="tpu_custom_call" | custom-call | flops 1000 | bytes 1000 | tf_op jit(solution)/shard_map/attend/pallas_call | solution.py:263
  66.7 1.8 %collective-permute-start.14 = (bf16[128,512]{1,0:T(8,128)(2,1)S(1)}, bf16[128,512]{1,0:T(8,128)(2,1)S(1)}, u32[]{:S(2)}, u32[]{:S(2)}) collective-permute-start(bf16[128,512]{1,0:T(8,128)(2,1)S(1)} %get-tuple-element.80.refs_2_.refs_0_.q_ref), channel_id=1, source_target_pairs={{0,2},{1,3},{2,0},{3,1},{4,6},{5,7},{6,4},{7,5},{8,10},{9,11},{10,... | collective-permute-start | bytes 393224 | tf_op jit(solution)/shard_map/ppermute | solution.py:488
  68.8 4.0 %collective-permute-done.14.refs_1_ = bf16[128,512]{1,0:T(8,128)(2,1)S(1)} collective-permute-done((bf16[128,512]{1,0:T(8,128)(2,1)S(1)}, bf16[128,512]{1,0:T(8,128)(2,1)S(1)}, u32[]{:S(2)}, u32[]{:S(2)}) %collective-permute-start.14) | collective-permute-done | bytes 131104 | tf_op jit(solution)/shard_map/ppermute | solution.py:488
  73.5 1.4 activate.6
  74.9 2.1 %collective-permute-start.25 = (bf16[128,512]{1,0:T(8,128)(2,1)S(1)}, bf16[128,512]{1,0:T(8,128)(2,1)S(1)}, u32[]{:S(2)}, u32[]{:S(2)}) collective-permute-start(bf16[128,512]{1,0:T(8,128)(2,1)S(1)} %get-tuple-element.83.refs_10_.refs_0_.q_ref), channel_id=1, source_target_pairs={{0,2},{1,3},{2,0},{3,1},{4,6},{5,7},{6,4},{7,5},{8,10},{9,11},{10,... | collective-permute-start | bytes 393224 | tf_op jit(solution)/shard_map/ppermute | solution.py:488
  77.2 3.1 %attend.5 = (bf16[2,128,512]{2,1,0:T(8,128)(2,1)S(1)}, bf16[1,128,512]{2,1,0:T(8,128)(2,1)S(1)}, bf16[1,128,512]{2,1,0:T(8,128)(2,1)S(1)}) custom-call(s32[1]{0:T(128)} %bitcast.at_ref, bf16[128,512]{1,0:T(8,128)(2,1)S(1)} %get-tuple-element.80.refs_2_.refs_0_.q_ref, bf16[128,512]{1,0:T(8,128)(2,1)S(1)} %collective-permute-done.14.refs_1_, ...), custom_call_target="tpu_custom_call" | custom-call | flops 1000 | bytes 1000 | tf_op jit(solution)/shard_map/attend/pallas_call | solution.py:263
  81.9 3.0 %collective-permute-done.29.refs_2_ = bf16[1,128,768]{2,1,0:T(8,128)(2,1)S(1)} collective-permute-done((bf16[1,128,768]{2,1,0:T(8,128)(2,1)S(1)}, bf16[1,128,768]{2,1,0:T(8,128)(2,1)S(1)}, u32[]{:S(2)}, u32[]{:S(2)}) %collective-permute-start.29) | collective-permute-done | bytes 196640 | tf_op jit(solution)/shard_map/ppermute | solution.py:488
  85.5 3.2 %attend.6 = (bf16[2,128,512]{2,1,0:T(8,128)(2,1)S(1)}, bf16[1,128,512]{2,1,0:T(8,128)(2,1)S(1)}, bf16[1,128,512]{2,1,0:T(8,128)(2,1)S(1)}) custom-call(s32[1]{0:T(128)} %bitcast.at_ref, bf16[128,512]{1,0:T(8,128)(2,1)S(1)} %get-tuple-element.83.refs_10_.refs_0_.q_ref, bf16[128,512]{1,0:T(8,128)(2,1)S(1)} %collective-permute-done.25.refs_1_, ...), custom_call_target="tpu_custom_call" | custom-call | flops 1000 | bytes 1000 | tf_op jit(solution)/shard_map/attend/pallas_call | solution.py:263
  88.7 1.8 %collective-permute-start.22 = (bf16[128,256]{1,0:T(8,128)(2,1)S(1)}, bf16[128,256]{1,0:T(8,128)(2,1)S(1)}, u32[]{:S(2)}, u32[]{:S(2)}) collective-permute-start(bf16[128,256]{1,0:T(8,128)(2,1)S(1)} %get-tuple-element.85.refs_2_.refs_0_.q_ref), channel_id=1, source_target_pairs={{0,2},{1,3},{2,0},{3,1},{4,6},{5,7},{6,4},{7,5},{8,10},{9,11},{10,... | collective-permute-start | bytes 196616 | tf_op jit(solution)/shard_map/ppermute | solution.py:488
  91.3 1.9 %collective-permute-done.22.refs_1_ = bf16[128,256]{1,0:T(8,128)(2,1)S(1)} collective-permute-done((bf16[128,256]{1,0:T(8,128)(2,1)S(1)}, bf16[128,256]{1,0:T(8,128)(2,1)S(1)}, u32[]{:S(2)}, u32[]{:S(2)}) %collective-permute-start.22) | collective-permute-done | bytes 65568 | tf_op jit(solution)/shard_map/ppermute | solution.py:488
  93.9 2.3 %collective-permute-start.38 = (bf16[1,128,512]{2,1,0:T(8,128)(2,1)S(1)}, bf16[1,128,512]{2,1,0:T(8,128)(2,1)S(1)}, u32[]{:S(2)}, u32[]{:S(2)}) collective-permute-start(bf16[1,128,512]{2,1,0:T(8,128)(2,1)S(1)} %fold.20.refs_10_), channel_id=1, source_target_pairs={{0,2},{1,3},{2,0},{3,1},{4,6},{5,7},{6,4},{7,5},{8,10},{9,11},{10,... | collective-permute-start | bytes 393224 | tf_op jit(solution)/shard_map/ppermute | solution.py:488
  96.1 2.0 %attend.7 = (bf16[2,128,256]{2,1,0:T(8,128)(2,1)S(1)}, bf16[1,128,256]{2,1,0:T(8,128)(2,1)S(1)}, bf16[1,128,256]{2,1,0:T(8,128)(2,1)S(1)}) custom-call(s32[1]{0:T(128)} %bitcast.at_ref, bf16[128,256]{1,0:T(8,128)(2,1)S(1)} %get-tuple-element.85.refs_2_.refs_0_.q_ref, bf16[128,256]{1,0:T(8,128)(2,1)S(1)} %collective-permute-done.22.refs_1_, ...), custom_call_target="tpu_custom_call" | custom-call | flops 1000 | bytes 1000 | tf_op jit(solution)/shard_map/attend/pallas_call | solution.py:263
  100.7 3.3 %collective-permute-done.36.refs_2_ = bf16[1,128,256]{2,1,0:T(8,128)(2,1)S(1)} collective-permute-done((bf16[1,128,256]{2,1,0:T(8,128)(2,1)S(1)}, bf16[1,128,256]{2,1,0:T(8,128)(2,1)S(1)}, u32[]{:S(2)}, u32[]{:S(2)}) %collective-permute-start.36) | collective-permute-done | bytes 65568 | tf_op jit(solution)/shard_map/ppermute | solution.py:488
  104.4 3.6 %collective-permute-start.41 = (f32[8,128]{1,0:T(8,128)S(1)}, f32[8,128]{1,0:T(8,128)S(1)}, u32[]{:S(2)}, u32[]{:S(2)}) collective-permute-start(f32[8,128]{1,0:T(8,128)S(1)} %get-tuple-element.105.refs_0_), channel_id=1, source_target_pairs={{0,12},{4,0},{8,4},{12,8},{1,13},{5,1},{9,5},{13,9},{2,14},{6,2},{... | collective-permute-start | bytes 12296 | tf_op jit(solution)/shard_map/ppermute | solution.py:512
  108.1 1.0 collective-permute-start.39
  109.4 3.2 %collective-permute-done.40.refs_2_ = f32[8,128]{1,0:T(8,128)S(1)} collective-permute-done((f32[8,128]{1,0:T(8,128)S(1)}, f32[8,128]{1,0:T(8,128)S(1)}, u32[]{:S(2)}, u32[]{:S(2)}) %collective-permute-start.40) | collective-permute-done | bytes 4128 | tf_op jit(solution)/shard_map/ppermute | solution.py:512
  114.5 5.8 %collective-permute-done.43 = bf16[64,2048]{1,0:T(8,128)(2,1)S(1)} collective-permute-done((bf16[64,2048]{1,0:T(8,128)(2,1)S(1)}, bf16[64,2048]{1,0:T(8,128)(2,1)S(1)}, u32[]{:S(2)}, u32[]{:S(2)}) %collective-permute-start.43) | collective-permute-done | bytes 262176 | tf_op jit(solution)/shard_map/ppermute | solution.py:488
  121.9 4.0 %output.4 = (bf16[2,4,16,1024]{3,2,1,0:T(8,128)(2,1)S(1)}, bf16[2,4,16,1024]{3,2,1,0:T(8,128)(2,1)S(1)}) custom-call(s32[4]{0:T(128)S(1)} %fusion.3.order_ref, bf16[4,16,2048]{2,1,0:T(8,128)(2,1)S(1)} %bitcast.42, bf16[4,16,2048]{2,1,0:T(8,128)(2,1)S(1)} %bitcast.44, bf16[4,16,2048]{2,1,0:T(8,128)(2,1)S(1)} %bitcast.48, bf16[4,16,2048]{2,1,0:T(8,128)(2,1)S(1)} %bitcast.50, ...), custom_call_target="tpu_custom_call" | custom-call | flops 1000 | bytes 1000 | tf_op jit(solution)/shard_map/output/pallas_call | solution.py:419
  125.8 3.2 %collective-permute-done.42.refs_0_ = bf16[64,2048]{1,0:T(8,128)(2,1)S(1)} collective-permute-done((bf16[64,2048]{1,0:T(8,128)(2,1)S(1)}, bf16[64,2048]{1,0:T(8,128)(2,1)S(1)}, u32[]{:S(2)}, u32[]{:S(2)}) %collective-permute-start.42) | collective-permute-done | bytes 262176 | tf_op jit(solution)/shard_map/ppermute | solution.py:488
  129.1 4.0 %output.5 = (bf16[2,4,16,1024]{3,2,1,0:T(8,128)(2,1)S(1)}, bf16[2,4,16,1024]{3,2,1,0:T(8,128)(2,1)S(1)}) custom-call(s32[4]{0:T(128)S(1)} %fusion.3.order_ref, bf16[4,16,2048]{2,1,0:T(8,128)(2,1)S(1)} %bitcast.43, bf16[4,16,2048]{2,1,0:T(8,128)(2,1)S(1)} %bitcast.45, bf16[4,16,2048]{2,1,0:T(8,128)(2,1)S(1)} %bitcast.49, bf16[4,16,2048]{2,1,0:T(8,128)(2,1)S(1)} %bitcast.51, ...), custom_call_target="tpu_custom_call" | custom-call | flops 1000 | bytes 1000 | tf_op jit(solution)/shard_map/output/pallas_call | solution.py:419
  133.0 2.1 %collective-permute-start.49 = (bf16[2,4,16,1024]{3,2,1,0:T(8,128)(2,1)S(1)}, bf16[2,4,16,1024]{3,2,1,0:T(8,128)(2,1)S(1)}, u32[]{:S(2)}, u32[]{:S(2)}) collective-permute-start(bf16[2,4,16,1024]{3,2,1,0:T(8,128)(2,1)S(1)} %get-tuple-element.114), channel_id=1, source_target_pairs={{0,4},{4,0},{8,12},{12,8},{1,5},{5,1},{9,13},{13,9},{2,6},{6,2},{1... | collective-permute-start | bytes 786440 | tf_op jit(solution)/shard_map/ppermute | solution.py:488
  135.1 4.0 %output.6 = (bf16[2,4,16,1024]{3,2,1,0:T(8,128)(2,1)S(1)}, bf16[2,4,16,1024]{3,2,1,0:T(8,128)(2,1)S(1)}) custom-call(s32[4]{0:T(128)S(1)} %fusion.3.order_ref, bf16[4,16,2048]{2,1,0:T(8,128)(2,1)S(1)} %bitcast.40, bf16[4,16,2048]{2,1,0:T(8,128)(2,1)S(1)} %bitcast.38, bf16[4,16,2048]{2,1,0:T(8,128)(2,1)S(1)} %bitcast.46, bf16[4,16,2048]{2,1,0:T(8,128)(2,1)S(1)} %bitcast.52, ...), custom_call_target="tpu_custom_call" | custom-call | flops 1000 | bytes 1000 | tf_op jit(solution)/shard_map/output/pallas_call | solution.py:419
  139.2 4.0 %output.7 = (bf16[2,4,16,1024]{3,2,1,0:T(8,128)(2,1)S(1)}, bf16[2,4,16,1024]{3,2,1,0:T(8,128)(2,1)S(1)}) custom-call(s32[4]{0:T(128)S(1)} %fusion.3.order_ref, bf16[4,16,2048]{2,1,0:T(8,128)(2,1)S(1)} %bitcast.41, bf16[4,16,2048]{2,1,0:T(8,128)(2,1)S(1)} %bitcast.39, bf16[4,16,2048]{2,1,0:T(8,128)(2,1)S(1)} %bitcast.47, bf16[4,16,2048]{2,1,0:T(8,128)(2,1)S(1)} %bitcast.53, ...), custom_call_target="tpu_custom_call" | custom-call | flops 1000 | bytes 1000 | tf_op jit(solution)/shard_map/output/pallas_call | solution.py:419
  143.2 2.1 %collective-permute-start.48 = (bf16[2,4,16,1024]{3,2,1,0:T(8,128)(2,1)S(1)}, bf16[2,4,16,1024]{3,2,1,0:T(8,128)(2,1)S(1)}, u32[]{:S(2)}, u32[]{:S(2)}) collective-permute-start(bf16[2,4,16,1024]{3,2,1,0:T(8,128)(2,1)S(1)} %get-tuple-element.113), channel_id=1, source_target_pairs={{0,4},{4,0},{8,12},{12,8},{1,5},{5,1},{9,13},{13,9},{2,6},{6,2},{1... | collective-permute-start | bytes 786440 | tf_op jit(solution)/shard_map/ppermute | solution.py:488
  145.4 1.2 collective-permute-start.52
  146.7 1.9 %collective-permute-start.51 = (bf16[1,4,16,1024]{3,2,1,0:T(8,128)(2,1)S(1)}, bf16[1,4,16,1024]{3,2,1,0:T(8,128)(2,1)S(1)}, u32[]{:S(2)}, u32[]{:S(2)}) collective-permute-start(bf16[1,4,16,1024]{3,2,1,0:T(8,128)(2,1)S(1)} %fold.23.refs_3_), channel_id=1, source_target_pairs={{0,8},{4,12},{8,0},{12,4},{1,9},{5,13},{9,1},{13,5},{2,10},{6,14},... | collective-permute-start | bytes 393224 | tf_op jit(solution)/shard_map/ppermute | solution.py:488
  148.7 7.2 %collective-permute-done.52.refs_2_ = bf16[1,4,16,1024]{3,2,1,0:T(8,128)(2,1)S(1)} collective-permute-done((bf16[1,4,16,1024]{3,2,1,0:T(8,128)(2,1)S(1)}, bf16[1,4,16,1024]{3,2,1,0:T(8,128)(2,1)S(1)}, u32[]{:S(2)}, u32[]{:S(2)}) %collective-permute-start.52) | collective-permute-done | bytes 131104 | tf_op jit(solution)/shard_map/ppermute | solution.py:488
  155.8 2.2 %close.4 = (bf16[8,16,2048]{2,1,0:T(8,128)(2,1)}, f32[8,128]{1,0:T(8,128)S(1)}) custom-call(s32[2]{0:T(128)S(1)} %pad_add_fusion.1.at_ref, bf16[32,16,2048]{2,1,0:T(8,128)(2,1)} %bitcast.76, bf16[2,4,16,1024]{3,2,1,0:T(8,128)(2,1)S(1)} %get-tuple-element.109.refs_1_.refs_5_.refs_0_, bf16[2,4,16,1024]{3,2,1,0:T(8,128)(2,1)S(1)} %collective-permute-done.50.refs_1_, ...), custom_call_target="tpu_custom_call" | custom-call | flops 1000 | bytes 4000000 | tf_op jit(solution)/shard_map/close/pallas_call | solution.py:453
  158.1 3.4 %collective-permute-start.55 = (bf16[1,4,16,1024]{3,2,1,0:T(8,128)(2,1)S(1)}, bf16[1,4,16,1024]{3,2,1,0:T(8,128)(2,1)S(1)}, u32[]{:S(2)}, u32[]{:S(2)}) collective-permute-start(bf16[1,4,16,1024]{3,2,1,0:T(8,128)(2,1)S(1)} %fold.24.refs_4_), channel_id=1, source_target_pairs={{0,8},{4,12},{8,0},{12,4},{1,9},{5,13},{9,1},{13,5},{2,10},{6,14},... | collective-permute-start | bytes 393224 | tf_op jit(solution)/shard_map/ppermute | solution.py:488
  161.6 2.2 %close.5 = (bf16[8,16,2048]{2,1,0:T(8,128)(2,1)}, f32[8,128]{1,0:T(8,128)S(1)}) custom-call(s32[2]{0:T(128)S(1)} %pad_add_fusion.1.at_ref, bf16[32,16,2048]{2,1,0:T(8,128)(2,1)} %bitcast.77, bf16[2,4,16,1024]{3,2,1,0:T(8,128)(2,1)S(1)} %get-tuple-element.110.refs_5_.refs_0_, ...), custom_call_target="tpu_custom_call", output_to_operand_aliasing={{0}: (5, {})} | custom-call | flops 1000 | bytes 4000000 | tf_op jit(solution)/shard_map/close/pallas_call | solution.py:453
  164.1 6.7 %collective-permute-done.55.refs_2_ = bf16[1,4,16,1024]{3,2,1,0:T(8,128)(2,1)S(1)} collective-permute-done((bf16[1,4,16,1024]{3,2,1,0:T(8,128)(2,1)S(1)}, bf16[1,4,16,1024]{3,2,1,0:T(8,128)(2,1)S(1)}, u32[]{:S(2)}, u32[]{:S(2)}) %collective-permute-start.55) | collective-permute-done | bytes 131104 | tf_op jit(solution)/shard_map/ppermute | solution.py:488
  170.8 2.2 %close.6 = (bf16[8,16,2048]{2,1,0:T(8,128)(2,1)}, f32[8,128]{1,0:T(8,128)}) custom-call(s32[2]{0:T(128)S(1)} %pad_add_fusion.at_ref, bf16[32,16,2048]{2,1,0:T(8,128)(2,1)} %bitcast.78, bf16[2,4,16,1024]{3,2,1,0:T(8,128)(2,1)S(1)} %get-tuple-element.111.refs_5_.refs_0_, ...), custom_call_target="tpu_custom_call", output_to_operand_aliasing={{0}: (5, {})} | custom-call | flops 1000 | bytes 4000000 | tf_op jit(solution)/shard_map/close/pallas_call | solution.py:453
  173.0 2.2 %close.7 = (bf16[8,16,2048]{2,1,0:T(8,128)(2,1)}, f32[8,128]{1,0:T(8,128)}) custom-call(s32[2]{0:T(128)S(1)} %pad_add_fusion.at_ref, bf16[32,16,2048]{2,1,0:T(8,128)(2,1)} %bitcast.79, bf16[2,4,16,1024]{3,2,1,0:T(8,128)(2,1)S(1)} %get-tuple-element.112.refs_2_.refs_0_, ...), custom_call_target="tpu_custom_call", output_to_operand_aliasing={{0}: (5, {})} | custom-call | flops 1000 | bytes 4000000 | tf_op jit(solution)/shard_map/close/pallas_call | solution.py:453
  (136 shorter events, 18.0 us)
Async XLA Ops:
  5.5 9.4 %collective-permute-start = (bf16[1,4,128,256]{3,2,1,0:T(8,128)(2,1)S(1)}, bf16[1,4,128,256]{3,2,1,0:T(8,128)(2,1)S(1)}, u32[]{:S(2)}, u32[]{:S(2)}) collective-permute-start(bf16[1,4,128,256]{3,2,1,0:T(8,128)(2,1)S(1)} %get-tuple-element.67), channel_id=1, source_target_pairs={{0,1},{1,0},{2,3},{3,2},{4,5},{5,4},{6,7},{7,6},{8,9},{9,8},{10,11... | collective-permute-start | bytes 786440 | tf_op jit(solution)/shard_map/ppermute | solution.py:488
  6.1 8.8 %collective-permute-start.1 = (bf16[1,4,128,256]{3,2,1,0:T(8,128)(2,1)S(1)}, bf16[1,4,128,256]{3,2,1,0:T(8,128)(2,1)S(1)}, u32[]{:S(2)}, u32[]{:S(2)}) collective-permute-start(bf16[1,4,128,256]{3,2,1,0:T(8,128)(2,1)S(1)} %get-tuple-element.68), channel_id=1, source_target_pairs={{0,1},{1,0},{2,3},{3,2},{4,5},{5,4},{6,7},{7,6},{8,9},{9,8},{10,11... | collective-permute-start | bytes 786440 | tf_op jit(solution)/shard_map/ppermute | solution.py:488
  14.9 12.6 %collective-permute-start.3 = (bf16[1,4,128,512]{3,2,1,0:T(8,128)(2,1)S(1)}, bf16[1,4,128,512]{3,2,1,0:T(8,128)(2,1)S(1)}, u32[]{:S(2)}, u32[]{:S(2)}) collective-permute-start(bf16[1,4,128,512]{3,2,1,0:T(8,128)(2,1)S(1)} %tie.10), channel_id=1, source_target_pairs={{0,1},{1,0},{2,3},{3,2},{4,5},{5,4},{6,7},{7,6},{8,9},{9,8},{10,11... | collective-permute-start | bytes 1572872 | tf_op jit(solution)/shard_map/ppermute | solution.py:488
  15.4 12.1 %collective-permute-start.2 = (bf16[1,4,128,512]{3,2,1,0:T(8,128)(2,1)S(1)}, bf16[1,4,128,512]{3,2,1,0:T(8,128)(2,1)S(1)}, u32[]{:S(2)}, u32[]{:S(2)}) collective-permute-start(bf16[1,4,128,512]{3,2,1,0:T(8,128)(2,1)S(1)} %tie.9), channel_id=1, source_target_pairs={{0,1},{1,0},{2,3},{3,2},{4,5},{5,4},{6,7},{7,6},{8,9},{9,8},{10,11... | collective-permute-start | bytes 1572872 | tf_op jit(solution)/shard_map/ppermute | solution.py:488
  15.8 11.7 %collective-permute-start.4 = (bf16[1,4,128,256]{3,2,1,0:T(8,128)(2,1)S(1)}, bf16[1,4,128,256]{3,2,1,0:T(8,128)(2,1)S(1)}, u32[]{:S(2)}, u32[]{:S(2)}) collective-permute-start(bf16[1,4,128,256]{3,2,1,0:T(8,128)(2,1)S(1)} %fold.13.refs_8_), channel_id=1, source_target_pairs={{0,2},{1,3},{2,0},{3,1},{4,6},{5,7},{6,4},{7,5},{8,10},{9,11},{10,... | collective-permute-start | bytes 786440 | tf_op jit(solution)/shard_map/ppermute | solution.py:488
  27.5 9.8 %collective-permute-start.6 = (bf16[1,4,128,512]{3,2,1,0:T(8,128)(2,1)S(1)}, bf16[1,4,128,512]{3,2,1,0:T(8,128)(2,1)S(1)}, u32[]{:S(2)}, u32[]{:S(2)}) collective-permute-start(bf16[1,4,128,512]{3,2,1,0:T(8,128)(2,1)S(1)} %tie.12), channel_id=1, source_target_pairs={{0,1},{1,0},{2,3},{3,2},{4,5},{5,4},{6,7},{7,6},{8,9},{9,8},{10,11... | collective-permute-start | bytes 1572872 | tf_op jit(solution)/shard_map/ppermute | solution.py:488
  27.6 9.7 %collective-permute-start.5 = (bf16[1,4,128,512]{3,2,1,0:T(8,128)(2,1)S(1)}, bf16[1,4,128,512]{3,2,1,0:T(8,128)(2,1)S(1)}, u32[]{:S(2)}, u32[]{:S(2)}) collective-permute-start(bf16[1,4,128,512]{3,2,1,0:T(8,128)(2,1)S(1)} %tie.11), channel_id=1, source_target_pairs={{0,1},{1,0},{2,3},{3,2},{4,5},{5,4},{6,7},{7,6},{8,9},{9,8},{10,11... | collective-permute-start | bytes 1572872 | tf_op jit(solution)/shard_map/ppermute | solution.py:488
  28.4 14.0 %collective-permute-start.8 = (bf16[1,4,128,512]{3,2,1,0:T(8,128)(2,1)S(1)}, bf16[1,4,128,512]{3,2,1,0:T(8,128)(2,1)S(1)}, u32[]{:S(2)}, u32[]{:S(2)}) collective-permute-start(bf16[1,4,128,512]{3,2,1,0:T(8,128)(2,1)S(1)} %fold.14.refs_8_), channel_id=1, source_target_pairs={{0,2},{1,3},{2,0},{3,1},{4,6},{5,7},{6,4},{7,5},{8,10},{9,11},{10,... | collective-permute-start | bytes 1572872 | tf_op jit(solution)/shard_map/ppermute | solution.py:488
  37.3 5.9 %collective-permute-start.7 = (bf16[1,4,128,512]{3,2,1,0:T(8,128)(2,1)S(1)}, bf16[1,4,128,512]{3,2,1,0:T(8,128)(2,1)S(1)}, u32[]{:S(2)}, u32[]{:S(2)}) collective-permute-start(bf16[1,4,128,512]{3,2,1,0:T(8,128)(2,1)S(1)} %tie.13), channel_id=1, source_target_pairs={{0,1},{1,0},{2,3},{3,2},{4,5},{5,4},{6,7},{7,6},{8,9},{9,8},{10,11... | collective-permute-start | bytes 1572872 | tf_op jit(solution)/shard_map/ppermute | solution.py:488
  38.1 13.0 %collective-permute-start.9 = (bf16[1,4,128,512]{3,2,1,0:T(8,128)(2,1)S(1)}, bf16[1,4,128,512]{3,2,1,0:T(8,128)(2,1)S(1)}, u32[]{:S(2)}, u32[]{:S(2)}) collective-permute-start(bf16[1,4,128,512]{3,2,1,0:T(8,128)(2,1)S(1)} %tie.14), channel_id=1, source_target_pairs={{0,1},{1,0},{2,3},{3,2},{4,5},{5,4},{6,7},{7,6},{8,9},{9,8},{10,11... | collective-permute-start | bytes 1572872 | tf_op jit(solution)/shard_map/ppermute | solution.py:488
  39.1 19.4 %collective-permute-start.12 = (bf16[1,4,128,512]{3,2,1,0:T(8,128)(2,1)}, bf16[1,4,128,512]{3,2,1,0:T(8,128)(2,1)}, u32[]{:S(2)}, u32[]{:S(2)}) collective-permute-start(bf16[1,4,128,512]{3,2,1,0:T(8,128)(2,1)} %fold.15.refs_6_), channel_id=1, source_target_pairs={{0,2},{1,3},{2,0},{3,1},{4,6},{5,7},{6,4},{7,5},{8,10},{9,11},{10,... | collective-permute-start | bytes 1572872 | tf_op jit(solution)/shard_map/ppermute | solution.py:488
  42.9 15.5 %collective-permute-start.18 = (bf16[128,768]{1,0:T(8,128)(2,1)S(1)}, bf16[128,768]{1,0:T(8,128)(2,1)S(1)}, u32[]{:S(2)}, u32[]{:S(2)}) collective-permute-start(bf16[128,768]{1,0:T(8,128)(2,1)S(1)} %get-tuple-element.75.refs_2_.refs_0_.q_ref), channel_id=1, source_target_pairs={{0,2},{1,3},{2,0},{3,1},{4,6},{5,7},{6,4},{7,5},{8,10},{9,11},{10,... | collective-permute-start | bytes 589832 | tf_op jit(solution)/shard_map/ppermute | solution.py:488
  51.1 9.8 %collective-permute-start.11 = (bf16[1,4,128,256]{3,2,1,0:T(8,128)(2,1)}, bf16[1,4,128,256]{3,2,1,0:T(8,128)(2,1)}, u32[]{:S(2)}, u32[]{:S(2)}) collective-permute-start(bf16[1,4,128,256]{3,2,1,0:T(8,128)(2,1)} %tie.16), channel_id=1, source_target_pairs={{0,1},{1,0},{2,3},{3,2},{4,5},{5,4},{6,7},{7,6},{8,9},{9,8},{10,11... | collective-permute-start | bytes 786440 | tf_op jit(solution)/shard_map/ppermute | solution.py:488
  51.1 22.4 %collective-permute-start.17 = (bf16[1,4,128,512]{3,2,1,0:T(8,128)(2,1)}, bf16[1,4,128,512]{3,2,1,0:T(8,128)(2,1)}, u32[]{:S(2)}, u32[]{:S(2)}) collective-permute-start(bf16[1,4,128,512]{3,2,1,0:T(8,128)(2,1)} %fold.16.refs_8_), channel_id=1, source_target_pairs={{0,2},{1,3},{2,0},{3,1},{4,6},{5,7},{6,4},{7,5},{8,10},{9,11},{10,... | collective-permute-start | bytes 1572872 | tf_op jit(solution)/shard_map/ppermute | solution.py:488
  52.9 9.1 %collective-permute-start.19 = (bf16[128,768]{1,0:T(8,128)(2,1)S(1)}, bf16[128,768]{1,0:T(8,128)(2,1)}, u32[]{:S(2)}, u32[]{:S(2)}) collective-permute-start(bf16[128,768]{1,0:T(8,128)(2,1)S(1)} %get-tuple-element.75.refs_2_.refs_0_.q_ref), channel_id=1, source_target_pairs={{0,1},{1,0},{2,3},{3,2},{4,5},{5,4},{6,7},{7,6},{8,9},{9,8},{10,11... | collective-permute-start | bytes 589832 | tf_op jit(solution)/shard_map/ppermute | solution.py:488
  66.1 6.7 %collective-permute-start.21 = (bf16[1,128,768]{2,1,0:T(8,128)(2,1)S(1)}, bf16[1,128,768]{2,1,0:T(8,128)(2,1)S(1)}, u32[]{:S(2)}, u32[]{:S(2)}) collective-permute-start(bf16[1,128,768]{2,1,0:T(8,128)(2,1)S(1)} %get-tuple-element.82), channel_id=1, source_target_pairs={{0,1},{1,0},{2,3},{3,2},{4,5},{5,4},{6,7},{7,6},{8,9},{9,8},{10,11... | collective-permute-start | bytes 589832 | tf_op jit(solution)/shard_map/ppermute | solution.py:488
  66.7 6.1 %collective-permute-start.14 = (bf16[128,512]{1,0:T(8,128)(2,1)S(1)}, bf16[128,512]{1,0:T(8,128)(2,1)S(1)}, u32[]{:S(2)}, u32[]{:S(2)}) collective-permute-start(bf16[128,512]{1,0:T(8,128)(2,1)S(1)} %get-tuple-element.80.refs_2_.refs_0_.q_ref), channel_id=1, source_target_pairs={{0,2},{1,3},{2,0},{3,1},{4,6},{5,7},{6,4},{7,5},{8,10},{9,11},{10,... | collective-permute-start | bytes 393224 | tf_op jit(solution)/shard_map/ppermute | solution.py:488
  68.5 11.8 %collective-permute-start.10 = (bf16[1,4,128,256]{3,2,1,0:T(8,128)(2,1)S(1)}, bf16[1,4,128,256]{3,2,1,0:T(8,128)(2,1)S(1)}, u32[]{:S(2)}, u32[]{:S(2)}) collective-permute-start(bf16[1,4,128,256]{3,2,1,0:T(8,128)(2,1)S(1)} %tie.15), channel_id=1, source_target_pairs={{0,1},{1,0},{2,3},{3,2},{4,5},{5,4},{6,7},{7,6},{8,9},{9,8},{10,11... | collective-permute-start | bytes 786440 | tf_op jit(solution)/shard_map/ppermute | solution.py:488
  68.5 12.2 %collective-permute-start.13 = (bf16[1,4,128,256]{3,2,1,0:T(8,128)(2,1)S(1)}, bf16[1,4,128,256]{3,2,1,0:T(8,128)(2,1)S(1)}, u32[]{:S(2)}, u32[]{:S(2)}) collective-permute-start(bf16[1,4,128,256]{3,2,1,0:T(8,128)(2,1)S(1)} %fold.17.refs_10_), channel_id=1, source_target_pairs={{0,2},{1,3},{2,0},{3,1},{4,6},{5,7},{6,4},{7,5},{8,10},{9,11},{10,... | collective-permute-start | bytes 786440 | tf_op jit(solution)/shard_map/ppermute | solution.py:488
  72.8 4.2 %collective-permute-start.15 = (bf16[128,512]{1,0:T(8,128)(2,1)S(1)}, bf16[128,512]{1,0:T(8,128)(2,1)S(1)}, u32[]{:S(2)}, u32[]{:S(2)}) collective-permute-start(bf16[128,512]{1,0:T(8,128)(2,1)S(1)} %get-tuple-element.80.refs_2_.refs_0_.q_ref), channel_id=1, source_target_pairs={{0,1},{1,0},{2,3},{3,2},{4,5},{5,4},{6,7},{7,6},{8,9},{9,8},{10,11... | collective-permute-start | bytes 393224 | tf_op jit(solution)/shard_map/ppermute | solution.py:488
  74.9 6.3 %collective-permute-start.25 = (bf16[128,512]{1,0:T(8,128)(2,1)S(1)}, bf16[128,512]{1,0:T(8,128)(2,1)S(1)}, u32[]{:S(2)}, u32[]{:S(2)}) collective-permute-start(bf16[128,512]{1,0:T(8,128)(2,1)S(1)} %get-tuple-element.83.refs_10_.refs_0_.q_ref), channel_id=1, source_target_pairs={{0,2},{1,3},{2,0},{3,1},{4,6},{5,7},{6,4},{7,5},{8,10},{9,11},{10,... | collective-permute-start | bytes 393224 | tf_op jit(solution)/shard_map/ppermute | solution.py:488
  77.0 4.9 %collective-permute-start.28 = (bf16[1,128,768]{2,1,0:T(8,128)(2,1)S(1)}, bf16[1,128,768]{2,1,0:T(8,128)(2,1)S(1)}, u32[]{:S(2)}, u32[]{:S(2)}) collective-permute-start(bf16[1,128,768]{2,1,0:T(8,128)(2,1)S(1)} %get-tuple-element.88), channel_id=1, source_target_pairs={{0,1},{1,0},{2,3},{3,2},{4,5},{5,4},{6,7},{7,6},{8,9},{9,8},{10,11... | collective-permute-start | bytes 589832 | tf_op jit(solution)/shard_map/ppermute | solution.py:488
  77.0 7.9 %collective-permute-start.29 = (bf16[1,128,768]{2,1,0:T(8,128)(2,1)S(1)}, bf16[1,128,768]{2,1,0:T(8,128)(2,1)S(1)}, u32[]{:S(2)}, u32[]{:S(2)}) collective-permute-start(bf16[1,128,768]{2,1,0:T(8,128)(2,1)S(1)} %fold.18.refs_3_), channel_id=1, source_target_pairs={{0,2},{1,3},{2,0},{3,1},{4,6},{5,7},{6,4},{7,5},{8,10},{9,11},{10,... | collective-permute-start | bytes 589832 | tf_op jit(solution)/shard_map/ppermute | solution.py:488
  80.8 4.7 %collective-permute-start.26 = (bf16[128,512]{1,0:T(8,128)(2,1)S(1)}, bf16[128,512]{1,0:T(8,128)(2,1)S(1)}, u32[]{:S(2)}, u32[]{:S(2)}) collective-permute-start(bf16[128,512]{1,0:T(8,128)(2,1)S(1)} %get-tuple-element.83.refs_10_.refs_0_.q_ref), channel_id=1, source_target_pairs={{0,1},{1,0},{2,3},{3,2},{4,5},{5,4},{6,7},{7,6},{8,9},{9,8},{10,11... | collective-permute-start | bytes 393224 | tf_op jit(solution)/shard_map/ppermute | solution.py:488
  81.2 4.3 %collective-permute-start.27 = (bf16[128,512]{1,0:T(8,128)(2,1)S(1)}, bf16[128,512]{1,0:T(8,128)(2,1)S(1)}, u32[]{:S(2)}, u32[]{:S(2)}) collective-permute-start(bf16[128,512]{1,0:T(8,128)(2,1)S(1)} %collective-permute-done.25.refs_1_), channel_id=1, source_target_pairs={{0,1},{1,0},{2,3},{3,2},{4,5},{5,4},{6,7},{7,6},{8,9},{9,8},{10,11... | collective-permute-start | bytes 393224 | tf_op jit(solution)/shard_map/ppermute | solution.py:488
  88.6 4.6 %collective-permute-start.31 = (bf16[1,128,512]{2,1,0:T(8,128)(2,1)S(1)}, bf16[1,128,512]{2,1,0:T(8,128)(2,1)S(1)}, u32[]{:S(2)}, u32[]{:S(2)}) collective-permute-start(bf16[1,128,512]{2,1,0:T(8,128)(2,1)S(1)} %get-tuple-element.92), channel_id=1, source_target_pairs={{0,1},{1,0},{2,3},{3,2},{4,5},{5,4},{6,7},{7,6},{8,9},{9,8},{10,11... | collective-permute-start | bytes 393224 | tf_op jit(solution)/shard_map/ppermute | solution.py:488
  88.7 4.5 %collective-permute-start.22 = (bf16[128,256]{1,0:T(8,128)(2,1)S(1)}, bf16[128,256]{1,0:T(8,128)(2,1)S(1)}, u32[]{:S(2)}, u32[]{:S(2)}) collective-permute-start(bf16[128,256]{1,0:T(8,128)(2,1)S(1)} %get-tuple-element.85.refs_2_.refs_0_.q_ref), channel_id=1, source_target_pairs={{0,2},{1,3},{2,0},{3,1},{4,6},{5,7},{6,4},{7,5},{8,10},{9,11},{10,... | collective-permute-start | bytes 196616 | tf_op jit(solution)/shard_map/ppermute | solution.py:488
  90.5 7.7 %collective-permute-start.34 = (bf16[1,128,512]{2,1,0:T(8,128)(2,1)S(1)}, bf16[1,128,512]{2,1,0:T(8,128)(2,1)S(1)}, u32[]{:S(2)}, u32[]{:S(2)}) collective-permute-start(bf16[1,128,512]{2,1,0:T(8,128)(2,1)S(1)} %get-tuple-element.97), channel_id=1, source_target_pairs={{0,1},{1,0},{2,3},{3,2},{4,5},{5,4},{6,7},{7,6},{8,9},{9,8},{10,11... | collective-permute-start | bytes 393224 | tf_op jit(solution)/shard_map/ppermute | solution.py:488
  91.0 7.7 %collective-permute-start.35 = (bf16[1,128,512]{2,1,0:T(8,128)(2,1)S(1)}, bf16[1,128,512]{2,1,0:T(8,128)(2,1)S(1)}, u32[]{:S(2)}, u32[]{:S(2)}) collective-permute-start(bf16[1,128,512]{2,1,0:T(8,128)(2,1)S(1)} %fold.19.refs_3_), channel_id=1, source_target_pairs={{0,2},{1,3},{2,0},{3,1},{4,6},{5,7},{6,4},{7,5},{8,10},{9,11},{10,... | collective-permute-start | bytes 393224 | tf_op jit(solution)/shard_map/ppermute | solution.py:488
  93.2 7.0 %collective-permute-start.37 = (bf16[1,128,512]{2,1,0:T(8,128)(2,1)S(1)}, bf16[1,128,512]{2,1,0:T(8,128)(2,1)S(1)}, u32[]{:S(2)}, u32[]{:S(2)}) collective-permute-start(bf16[1,128,512]{2,1,0:T(8,128)(2,1)S(1)} %get-tuple-element.102), channel_id=1, source_target_pairs={{0,1},{1,0},{2,3},{3,2},{4,5},{5,4},{6,7},{7,6},{8,9},{9,8},{10,11... | collective-permute-start | bytes 393224 | tf_op jit(solution)/shard_map/ppermute | solution.py:488
  93.9 6.3 %collective-permute-start.38 = (bf16[1,128,512]{2,1,0:T(8,128)(2,1)S(1)}, bf16[1,128,512]{2,1,0:T(8,128)(2,1)S(1)}, u32[]{:S(2)}, u32[]{:S(2)}) collective-permute-start(bf16[1,128,512]{2,1,0:T(8,128)(2,1)S(1)} %fold.20.refs_10_), channel_id=1, source_target_pairs={{0,2},{1,3},{2,0},{3,1},{4,6},{5,7},{6,4},{7,5},{8,10},{9,11},{10,... | collective-permute-start | bytes 393224 | tf_op jit(solution)/shard_map/ppermute | solution.py:488
  99.6 4.3 %collective-permute-start.36 = (bf16[1,128,256]{2,1,0:T(8,128)(2,1)S(1)}, bf16[1,128,256]{2,1,0:T(8,128)(2,1)S(1)}, u32[]{:S(2)}, u32[]{:S(2)}) collective-permute-start(bf16[1,128,256]{2,1,0:T(8,128)(2,1)S(1)} %fold.21.refs_3_), channel_id=1, source_target_pairs={{0,2},{1,3},{2,0},{3,1},{4,6},{5,7},{6,4},{7,5},{8,10},{9,11},{10,... | collective-permute-start | bytes 196616 | tf_op jit(solution)/shard_map/ppermute | solution.py:488
  104.4 5.0 %collective-permute-start.41 = (f32[8,128]{1,0:T(8,128)S(1)}, f32[8,128]{1,0:T(8,128)S(1)}, u32[]{:S(2)}, u32[]{:S(2)}) collective-permute-start(f32[8,128]{1,0:T(8,128)S(1)} %get-tuple-element.105.refs_0_), channel_id=1, source_target_pairs={{0,12},{4,0},{8,4},{12,8},{1,13},{5,1},{9,5},{13,9},{2,14},{6,2},{... | collective-permute-start | bytes 12296 | tf_op jit(solution)/shard_map/ppermute | solution.py:512
  108.1 4.5 %collective-permute-start.40 = (f32[8,128]{1,0:T(8,128)S(1)}, f32[8,128]{1,0:T(8,128)S(1)}, u32[]{:S(2)}, u32[]{:S(2)}) collective-permute-start(f32[8,128]{1,0:T(8,128)S(1)} %get-tuple-element.105.refs_0_), channel_id=1, source_target_pairs={{0,8},{4,12},{8,0},{12,4},{1,9},{5,13},{9,1},{13,5},{2,10},{6,14},... | collective-permute-start | bytes 12296 | tf_op jit(solution)/shard_map/ppermute | solution.py:512
  108.1 5.4 %collective-permute-start.39 = (f32[8,128]{1,0:T(8,128)S(1)}, f32[8,128]{1,0:T(8,128)S(1)}, u32[]{:S(2)}, u32[]{:S(2)}) collective-permute-start(f32[8,128]{1,0:T(8,128)S(1)} %get-tuple-element.105.refs_0_), channel_id=1, source_target_pairs={{0,4},{4,8},{8,12},{12,0},{1,5},{5,9},{9,13},{13,1},{2,6},{6,10},{... | collective-permute-start | bytes 12296 | tf_op jit(solution)/shard_map/ppermute | solution.py:512
  113.9 6.4 %collective-permute-start.43 = (bf16[64,2048]{1,0:T(8,128)(2,1)S(1)}, bf16[64,2048]{1,0:T(8,128)(2,1)S(1)}, u32[]{:S(2)}, u32[]{:S(2)}) collective-permute-start(bf16[64,2048]{1,0:T(8,128)(2,1)S(1)} %get-tuple-element.108), channel_id=1, source_target_pairs={{0,2},{1,3},{2,0},{3,1},{4,6},{5,7},{6,4},{7,5},{8,10},{9,11},{10,... | collective-permute-start | bytes 786440 | tf_op jit(solution)/shard_map/ppermute | solution.py:488
  114.5 6.6 %collective-permute-start.44 = (bf16[64,2048]{1,0:T(8,128)(2,1)S(1)}, bf16[64,2048]{1,0:T(8,128)(2,1)S(1)}, u32[]{:S(2)}, u32[]{:S(2)}) collective-permute-start(bf16[64,2048]{1,0:T(8,128)(2,1)S(1)} %get-tuple-element.108), channel_id=1, source_target_pairs={{0,1},{1,0},{2,3},{3,2},{4,5},{5,4},{6,7},{7,6},{8,9},{9,8},{10,11... | collective-permute-start | bytes 786440 | tf_op jit(solution)/shard_map/ppermute | solution.py:488
  120.3 8.7 %collective-permute-start.42 = (bf16[64,2048]{1,0:T(8,128)(2,1)S(1)}, bf16[64,2048]{1,0:T(8,128)(2,1)S(1)}, u32[]{:S(2)}, u32[]{:S(2)}) collective-permute-start(bf16[64,2048]{1,0:T(8,128)(2,1)S(1)} %get-tuple-element.107), channel_id=1, source_target_pairs={{0,2},{1,3},{2,0},{3,1},{4,6},{5,7},{6,4},{7,5},{8,10},{9,11},{10,... | collective-permute-start | bytes 786440 | tf_op jit(solution)/shard_map/ppermute | solution.py:488
  120.9 14.3 %collective-permute-start.46 = (bf16[64,2048]{1,0:T(8,128)(2,1)S(1)}, bf16[64,2048]{1,0:T(8,128)(2,1)S(1)}, u32[]{:S(2)}, u32[]{:S(2)}) collective-permute-start(bf16[64,2048]{1,0:T(8,128)(2,1)S(1)} %get-tuple-element.107), channel_id=1, source_target_pairs={{0,1},{1,0},{2,3},{3,2},{4,5},{5,4},{6,7},{7,6},{8,9},{9,8},{10,11... | collective-permute-start | bytes 786440 | tf_op jit(solution)/shard_map/ppermute | solution.py:488
  129.1 6.1 %collective-permute-start.47 = (bf16[64,2048]{1,0:T(8,128)(2,1)S(1)}, bf16[64,2048]{1,0:T(8,128)(2,1)S(1)}, u32[]{:S(2)}, u32[]{:S(2)}) collective-permute-start(bf16[64,2048]{1,0:T(8,128)(2,1)S(1)} %tie.17), channel_id=1, source_target_pairs={{0,1},{1,0},{2,3},{3,2},{4,5},{5,4},{6,7},{7,6},{8,9},{9,8},{10,11... | collective-permute-start | bytes 786440 | tf_op jit(solution)/shard_map/ppermute | solution.py:488
  129.1 16.2 %collective-permute-start.50 = (bf16[2,4,16,1024]{3,2,1,0:T(8,128)(2,1)S(1)}, bf16[2,4,16,1024]{3,2,1,0:T(8,128)(2,1)S(1)}, u32[]{:S(2)}, u32[]{:S(2)}) collective-permute-start(bf16[2,4,16,1024]{3,2,1,0:T(8,128)(2,1)S(1)} %get-tuple-element.115), channel_id=1, source_target_pairs={{0,4},{4,0},{8,12},{12,8},{1,5},{5,1},{9,13},{13,9},{2,6},{6,2},{1... | collective-permute-start | bytes 786440 | tf_op jit(solution)/shard_map/ppermute | solution.py:488
  133.0 13.5 %collective-permute-start.49 = (bf16[2,4,16,1024]{3,2,1,0:T(8,128)(2,1)S(1)}, bf16[2,4,16,1024]{3,2,1,0:T(8,128)(2,1)S(1)}, u32[]{:S(2)}, u32[]{:S(2)}) collective-permute-start(bf16[2,4,16,1024]{3,2,1,0:T(8,128)(2,1)S(1)} %get-tuple-element.114), channel_id=1, source_target_pairs={{0,4},{4,0},{8,12},{12,8},{1,5},{5,1},{9,13},{13,9},{2,6},{6,2},{1... | collective-permute-start | bytes 786440 | tf_op jit(solution)/shard_map/ppermute | solution.py:488
  139.1 18.9 %collective-permute-start.53 = (bf16[2,4,16,1024]{3,2,1,0:T(8,128)(2,1)S(1)}, bf16[2,4,16,1024]{3,2,1,0:T(8,128)(2,1)S(1)}, u32[]{:S(2)}, u32[]{:S(2)}) collective-permute-start(bf16[2,4,16,1024]{3,2,1,0:T(8,128)(2,1)S(1)} %get-tuple-element.117), channel_id=1, source_target_pairs={{0,4},{4,0},{8,12},{12,8},{1,5},{5,1},{9,13},{13,9},{2,6},{6,2},{1... | collective-permute-start | bytes 786440 | tf_op jit(solution)/shard_map/ppermute | solution.py:488
  143.2 20.6 %collective-permute-start.48 = (bf16[2,4,16,1024]{3,2,1,0:T(8,128)(2,1)S(1)}, bf16[2,4,16,1024]{3,2,1,0:T(8,128)(2,1)S(1)}, u32[]{:S(2)}, u32[]{:S(2)}) collective-permute-start(bf16[2,4,16,1024]{3,2,1,0:T(8,128)(2,1)S(1)} %get-tuple-element.113), channel_id=1, source_target_pairs={{0,4},{4,0},{8,12},{12,8},{1,5},{5,1},{9,13},{13,9},{2,6},{6,2},{1... | collective-permute-start | bytes 786440 | tf_op jit(solution)/shard_map/ppermute | solution.py:488
  145.4 10.4 %collective-permute-start.52 = (bf16[1,4,16,1024]{3,2,1,0:T(8,128)(2,1)S(1)}, bf16[1,4,16,1024]{3,2,1,0:T(8,128)(2,1)S(1)}, u32[]{:S(2)}, u32[]{:S(2)}) collective-permute-start(bf16[1,4,16,1024]{3,2,1,0:T(8,128)(2,1)S(1)} %fold.22.refs_2_), channel_id=1, source_target_pairs={{0,8},{4,12},{8,0},{12,4},{1,9},{5,13},{9,1},{13,5},{2,10},{6,14},... | collective-permute-start | bytes 393224 | tf_op jit(solution)/shard_map/ppermute | solution.py:488
  146.7 14.9 %collective-permute-start.51 = (bf16[1,4,16,1024]{3,2,1,0:T(8,128)(2,1)S(1)}, bf16[1,4,16,1024]{3,2,1,0:T(8,128)(2,1)S(1)}, u32[]{:S(2)}, u32[]{:S(2)}) collective-permute-start(bf16[1,4,16,1024]{3,2,1,0:T(8,128)(2,1)S(1)} %fold.23.refs_3_), channel_id=1, source_target_pairs={{0,8},{4,12},{8,0},{12,4},{1,9},{5,13},{9,1},{13,5},{2,10},{6,14},... | collective-permute-start | bytes 393224 | tf_op jit(solution)/shard_map/ppermute | solution.py:488
  158.1 12.7 %collective-permute-start.55 = (bf16[1,4,16,1024]{3,2,1,0:T(8,128)(2,1)S(1)}, bf16[1,4,16,1024]{3,2,1,0:T(8,128)(2,1)S(1)}, u32[]{:S(2)}, u32[]{:S(2)}) collective-permute-start(bf16[1,4,16,1024]{3,2,1,0:T(8,128)(2,1)S(1)} %fold.24.refs_4_), channel_id=1, source_target_pairs={{0,8},{4,12},{8,0},{12,4},{1,9},{5,13},{9,1},{13,5},{2,10},{6,14},... | collective-permute-start | bytes 393224 | tf_op jit(solution)/shard_map/ppermute | solution.py:488
  163.9 9.1 %collective-permute-start.54 = (bf16[1,4,16,1024]{3,2,1,0:T(8,128)(2,1)S(1)}, bf16[1,4,16,1024]{3,2,1,0:T(8,128)(2,1)S(1)}, u32[]{:S(2)}, u32[]{:S(2)}) collective-permute-start(bf16[1,4,16,1024]{3,2,1,0:T(8,128)(2,1)S(1)} %fold.25.refs_4_), channel_id=1, source_target_pairs={{0,8},{4,12},{8,0},{12,4},{1,9},{5,13},{9,1},{13,5},{2,10},{6,14},... | collective-permute-start | bytes 393224 | tf_op jit(solution)/shard_map/ppermute | solution.py:488
  (18 other events, 84.4 us)

commit v11 on v10

--- a/solution.py
+++ b/solution.py
@@ -25,7 +25,6 @@
 
 
 LIGHT = pl.CostEstimate(flops=1000, bytes_accessed=1000, transcendentals=0)
-STEP = pl.CostEstimate(flops=1000, bytes_accessed=4_000_000, transcendentals=0)
 
 
 def far(x):
@@ -130,7 +129,7 @@
     refs[-1][...] = sum(r[...].astype(f32) for r in refs[:count]).astype(bf16)
 
 
-def fold(terms, after=(), told=LIGHT):
+def fold(terms, after=()):
     half = terms[0].shape[0] // 2 if len(terms) == 2 else terms[-1].shape[0] // 2
     tail = terms[0].shape[1:]
     steps = 2 if tail[-1] % 256 == 0 else 1
@@ -145,7 +144,7 @@
         out_specs=pl.BlockSpec(block, lambda j: (0,) + middle + (j,)),
         out_shape=jax.ShapeDtypeStruct((half,) + tail, bf16),
         compiler_params=params(),
-        cost_estimate=told,
+        cost_estimate=LIGHT,
         name="fold",
     )(*terms, *after)
 
@@ -436,42 +435,51 @@
     )(order, *[b.reshape(zs, piece, width) for b in blocks], far(w_out), *after)
 
 
-def close_kernel(count, at_ref, t_ref, *refs):
+def close_kernel(counts, at_ref, t_ref, *refs):
     out_ref, mark_ref = refs[-2:]
     mark_ref[...] = jnp.zeros_like(mark_ref)
-    for p in range(out_ref.shape[0]):
-        total = t_ref[p].astype(f32)
-        for term in refs[:count]:
-            total = total + term[0, p ^ at_ref[0]].astype(f32)
-        out_ref[p] = total.astype(bf16)
-
-
-def close(place, index, tokens, chunks, r, g, terms, out, after):
-    _, owners, piece, span = terms[0].shape
+    first, column = 0, 0
+    for count in counts:
+        terms = refs[first:first + count]
+        span = terms[0].shape[-1]
+        at = slice(column, column + span)
+        for p in range(out_ref.shape[0]):
+            total = t_ref[p, :, at].astype(f32)
+            for term in terms:
+                total = total + term[0, p ^ at_ref[0]].astype(f32)
+            out_ref[p, :, at] = total.astype(bf16)
+        first += count
+        column += span
+
+
+def close(place, index, tokens, chunks, r, groups, out, after):
+    _, owners, piece, _ = groups[0][0].shape
+    width = tokens.shape[1]
     at = jnp.stack([place, index * chunks + r]).astype(jnp.int32)
+    flat = [term for terms in groups for term in terms]
     into = [] if out is None else [out]
     return pl.pallas_call(
-        functools.partial(close_kernel, len(terms)),
+        functools.partial(close_kernel, [len(terms) for terms in groups]),
         grid_spec=pltpu.PrefetchScalarGridSpec(
             num_scalar_prefetch=1,
             grid=(1,),
-            in_specs=[pl.BlockSpec((owners, piece, span), lambda j, at: (at[1], 0, g))]
-            + [pl.BlockSpec((1,) + t.shape[1:], lambda j, at: (0, 0, 0, 0)) for t in terms]
+            in_specs=[pl.BlockSpec((owners, piece, width), lambda j, at: (at[1], 0, 0))]
+            + [pl.BlockSpec((1,) + t.shape[1:], lambda j, at: (0, 0, 0, 0)) for t in flat]
             + anywhere(into) + anywhere(after),
             out_specs=(
-                pl.BlockSpec((owners, piece, span), lambda j, at: (r, 0, g)),
+                pl.BlockSpec((owners, piece, width), lambda j, at: (r, 0, 0)),
                 pl.BlockSpec((8, DH), lambda j, at: (0, 0)),
             ),
         ),
         out_shape=(
-            jax.ShapeDtypeStruct((chunks * owners, piece, tokens.shape[1]), bf16),
+            jax.ShapeDtypeStruct((chunks * owners, piece, width), bf16),
             jax.ShapeDtypeStruct((8, DH), f32),
         ),
-        input_output_aliases={} if out is None else {2 + len(terms): 0},
-        compiler_params=params(),
-        cost_estimate=STEP,
+        input_output_aliases={} if out is None else {2 + len(flat): 0},
+        compiler_params=params(),
+        cost_estimate=LIGHT,
         name="close",
-    )(at, far(tokens.reshape(-1, piece, tokens.shape[1])), *terms, *into, *after)
+    )(at, far(tokens.reshape(-1, piece, width)), *flat, *into, *after)
 
 
 def bits_of(axis):
@@ -490,10 +498,10 @@
     )
 
 
-def scatter(keep, gots, axis, after=(), told=LIGHT):
+def scatter(keep, gots, axis, after=()):
     terms, sent = [keep, gots[0]], gots[-1]
     for b in range(1, bits_of(axis)):
-        sent = fold([keep, gots[-1]] if b == 1 else terms, after, told)
+        sent = fold([keep, gots[-1]] if b == 1 else terms, after)
         terms.append(swap(sent, axis, b))
     return terms, sent
 
@@ -602,35 +610,41 @@
     gated = gate_rows(all_stats(stats[last], "head"), atts, rests, chunks)
     columns = w_out.shape[1]
     straight = piece % 16 == 0 and zs & (zs - 1) == 0
-    out, last_out = None, []
+    out = None
     if not straight:
         for r, rows in enumerate(gated):
             whole = jnp.concatenate(gather(rows, "hist"))
             whole = jnp.dot(whole, w_out, preferred_element_type=f32).astype(bf16)
             whole = whole.reshape(owners, zs, piece, -1).swapaxes(0, 1)
             whole = lax.psum_scatter(whole, "head", scatter_dimension=0, tiled=True)
-            out, _ = close(place, index, tokens, chunks, r, 0, [whole], out, [])
+            out, _ = close(place, index, tokens, chunks, r, [[whole]], out, [])
         return out.reshape(cand // zs, -1)
     halved = index ^ reverse(jnp.arange(zs, dtype=jnp.int32), bits_of("head"))
-    groups = 2 if columns % 1024 == 0 else 1
-    span = columns // groups
-    pieces, first_out, counts = [], [], [zs // 2] * 2 if zs > 1 else [1]
-    for r, rows in enumerate(gated):
-        blocks = gather(rows, "hist", first_out)
-        for g in range(groups):
-            own, *others = output(halved, counts, blocks, w_out, g * span, span, last_out)
-            pieces.append((r, g, own, [swap(x, "head", 0) for x in others]))
-            last_out, first_out = [own], first_out or [own]
-    closing, chain = [], last_out
-    for r, g, own, arrived in pieces:
-        terms, sent = scatter(own, arrived, "head", chain, STEP) if arrived else ([own], own)
-        chain = [sent]
-        closing.append((r, g, terms))
-        if len(closing) > 1:
-            out, mark = close(place, index, tokens, chunks, *closing.pop(0), out, chain)
-            chain = [mark]
-    for last_piece in closing:
-        out, _ = close(place, index, tokens, chunks, *last_piece, out, [])
+    spans = [columns // 2] * 2 if columns % 1024 == 0 else [columns]
+    counts = [zs // 2] * 2 if zs > 1 else [1]
+    pieces = [(r, sum(spans[:g]), span) for r in range(chunks) for g, span in enumerate(spans)]
+    chain, made, groups, blocks = [], [], [[] for _ in range(chunks)], {}
+
+    def sum_next():
+        r, own, arrived = made.pop(0)
+        terms, sent = scatter(own, arrived, "head", chain) if arrived else ([own], own)
+        groups[r].append(terms)
+        return [sent]
+
+    first_out = []
+    for r, column, span in pieces:
+        if r not in blocks:
+            blocks[r] = gather(gated[r], "hist", first_out)
+        own, *others = output(halved, counts, blocks[r], w_out, column, span, chain)
+        made.append((r, own, [swap(x, "head", 0) for x in others]))
+        chain, first_out = [own], first_out or [own]
+    while len(made) > 1:
+        chain = sum_next()
+    for r in range(chunks):
+        if r == chunks - 1:
+            sum_next()
+        out, mark = close(place, index, tokens, chunks, r, groups[r], out, chain)
+        chain = [mark]
     return out.reshape(cand // zs, -1)
 
 

time: 176 us -> 179 us (1.017)
  waiting for transfers between devices: 47.9 us -> 54.8 us
  Pallas kernels: 85.3 us -> 81.2 us
    ppermute x53, waiting for transfers between devices: 43.5 us -> 50.4 us  [swap(): lax.ppermute(x, axis, [(i, i ^ 1 << bit) for i in range(lax.axis_size(axi...]
    pallas_call x4 -> x2, Pallas kernels: 8.68 us -> 4.65 us  [close(): pl.pallas_call(functools.partial(close_kernel, [len(terms) for terms in g...]
  transfers between devices with their start and end apart: 56 -> 56, of which waited for: 17 -> 20; matrix products, arithmetic and copies ran while one was open for 0% -> 0% of each run, Pallas kernels for 42% -> 39%
where the time goes in v11:
time: 179 us; the launch traced here: 178 us
  Pallas kernels  81.2 us (45%)
  waiting for transfers between devices  54.8 us (31%)
  starting transfers between devices  38.8 us (22%)
  local copies, waits for them, and re-layouts  2.39 us (1%)
    ppermute x53, waiting for transfers between devices, swap(): lax.ppermute(x, axis, [(i, i ^ 1 << bit) for i in range(lax.axis_size(axi...  50.4 us
    pallas_call x5, Pallas kernels, project(): pl.pallas_call(functools.partial(project_kernel, parts, owners, len(after...  37.9 us
    ppermute x53, starting transfers between devices, swap(): lax.ppermute(x, axis, [(i, i ^ 1 << bit) for i in range(lax.axis_size(axi...  34.1 us
    pallas_call x4, Pallas kernels, output(): pl.pallas_call(functools.partial(output_kernel, owners, len(after)), grid...  15.9 us
    pallas_call x4, Pallas kernels, attend(): pl.pallas_call(functools.partial(attend_kernel, owners, len(counts)), gri...  12.4 us
    pallas_call x2, Pallas kernels, close(): pl.pallas_call(functools.partial(close_kernel, [len(terms) for terms in g...  4.65 us
    ppermute x3, starting transfers between devices, shift(): return lax.ppermute(x, axis, [(i, (i + k) % count) for i in range(count)])  4.64 us
    pallas_call x13, Pallas kernels, fold(): pl.pallas_call(functools.partial(fold_kernel, len(terms)), grid=(steps,),...  4.54 us
  transfers between devices with their start and end apart: 56, of which 20 were waited for; matrix products, arithmetic and copies ran while one was open for 0% of the time, Pallas kernels for 39%

profile of v11, /device:TPU:0, one launch (start us, length us, event | category | flops | bytes accessed | tf_op | source)
XLA Modules:
  0.0 177.9 jit_solution(2323684227046167034)
XLA Ops:
  0.0 5.5 %project.5 = (bf16[2,4,128,256]{3,2,1,0:T(8,128)(2,1)S(1)}, bf16[1,4,128,256]{3,2,1,0:T(8,128)(2,1)S(1)}, bf16[1,4,128,256]{3,2,1,0:T(8,128)(2,1)S(1)}) custom-call(s32[1]{0:T(128)} %bitcast.at_ref, bf16[4,2,4,16,2048]{4,3,2,1,0:T(8,128)(2,1)} %bitcast.56, bf16[4,2,4,16,2048]{4,3,2,1,0:T(8,128)(2,1)} %bitcast.57, bf16[4,2,4,16,2048]{4,3,2,1,0:T(8,128)(2,1)} %bitcast.58, ...), custom_call_target="tpu_custom_call" | custom-call | flops 1000 | bytes 1000 | tf_op jit(solution)/shard_map/project/pallas_call | solution.py:80
  6.1 8.7 %project.6 = (bf16[2,4,128,512]{3,2,1,0:T(8,128)(2,1)S(1)}, bf16[1,4,128,512]{3,2,1,0:T(8,128)(2,1)S(1)}, bf16[1,4,128,512]{3,2,1,0:T(8,128)(2,1)S(1)}) custom-call(s32[1]{0:T(128)} %bitcast.at_ref, bf16[4,2,4,16,2048]{4,3,2,1,0:T(8,128)(2,1)} %bitcast.60, bf16[4,2,4,16,2048]{4,3,2,1,0:T(8,128)(2,1)} %bitcast.61, bf16[4,2,4,16,2048]{4,3,2,1,0:T(8,128)(2,1)} %bitcast.62, ...), custom_call_target="tpu_custom_call" | custom-call | flops 1000 | bytes 1000 | tf_op jit(solution)/shard_map/project/pallas_call | solution.py:80
  15.8 3.0 %collective-permute-start.4 = (bf16[1,4,128,256]{3,2,1,0:T(8,128)(2,1)S(1)}, bf16[1,4,128,256]{3,2,1,0:T(8,128)(2,1)S(1)}, u32[]{:S(2)}, u32[]{:S(2)}) collective-permute-start(bf16[1,4,128,256]{3,2,1,0:T(8,128)(2,1)S(1)} %fold.13.refs_8_), channel_id=1, source_target_pairs={{0,2},{1,3},{2,0},{3,1},{4,6},{5,7},{6,4},{7,5},{8,10},{9,11},{10,... | collective-permute-start | bytes 786440 | tf_op jit(solution)/shard_map/ppermute | solution.py:496
  18.7 8.7 %project.7 = (bf16[2,4,128,512]{3,2,1,0:T(8,128)(2,1)S(1)}, bf16[1,4,128,512]{3,2,1,0:T(8,128)(2,1)S(1)}, bf16[1,4,128,512]{3,2,1,0:T(8,128)(2,1)S(1)}) custom-call(s32[1]{0:T(128)} %bitcast.at_ref, bf16[4,2,4,16,2048]{4,3,2,1,0:T(8,128)(2,1)} %bitcast.67, bf16[4,2,4,16,2048]{4,3,2,1,0:T(8,128)(2,1)} %bitcast.65, bf16[4,2,4,16,2048]{4,3,2,1,0:T(8,128)(2,1)} %bitcast.66, ...), custom_call_target="tpu_custom_call" | custom-call | flops 1000 | bytes 1000 | tf_op jit(solution)/shard_map/project/pallas_call | solution.py:80
  28.5 8.8 %project.8 = (bf16[2,4,128,512]{3,2,1,0:T(8,128)(2,1)S(1)}, bf16[1,4,128,512]{3,2,1,0:T(8,128)(2,1)S(1)}, bf16[1,4,128,512]{3,2,1,0:T(8,128)(2,1)S(1)}) custom-call(s32[1]{0:T(128)} %bitcast.at_ref, bf16[4,2,4,16,2048]{4,3,2,1,0:T(8,128)(2,1)} %bitcast.68, bf16[4,2,4,16,2048]{4,3,2,1,0:T(8,128)(2,1)} %bitcast.69, bf16[4,2,4,16,2048]{4,3,2,1,0:T(8,128)(2,1)} %bitcast.70, ...), custom_call_target="tpu_custom_call" | custom-call | flops 1000 | bytes 1000 | tf_op jit(solution)/shard_map/project/pallas_call | solution.py:80
  38.2 0.9 fold.15.refs_6_
  39.1 1.9 %collective-permute-start.12 = (bf16[1,4,128,512]{3,2,1,0:T(8,128)(2,1)}, bf16[1,4,128,512]{3,2,1,0:T(8,128)(2,1)}, u32[]{:S(2)}, u32[]{:S(2)}) collective-permute-start(bf16[1,4,128,512]{3,2,1,0:T(8,128)(2,1)} %fold.15.refs_6_), channel_id=1, source_target_pairs={{0,2},{1,3},{2,0},{3,1},{4,6},{5,7},{6,4},{7,5},{8,10},{9,11},{10,... | collective-permute-start | bytes 1572872 | tf_op jit(solution)/shard_map/ppermute | solution.py:496
  41.0 1.4 collective-permute-done.8.refs_5_
  43.2 1.0 fold.16.refs_8_
  44.2 6.2 %project.9 = (bf16[2,4,128,256]{3,2,1,0:T(8,128)(2,1)S(1)}, bf16[1,4,128,256]{3,2,1,0:T(8,128)(2,1)S(1)}, bf16[1,4,128,256]{3,2,1,0:T(8,128)(2,1)}) custom-call(s32[1]{0:T(128)} %bitcast.at_ref, bf16[4,2,4,16,2048]{4,3,2,1,0:T(8,128)(2,1)} %bitcast.72, bf16[4,2,4,16,2048]{4,3,2,1,0:T(8,128)(2,1)} %bitcast.73, bf16[4,2,4,16,2048]{4,3,2,1,0:T(8,128)(2,1)} %bitcast.74, ...), custom_call_target="tpu_custom_call" | custom-call | flops 1000 | bytes 1000 | tf_op jit(solution)/shard_map/project/pallas_call | solution.py:80
  51.1 1.8 %collective-permute-start.17 = (bf16[1,4,128,512]{3,2,1,0:T(8,128)(2,1)}, bf16[1,4,128,512]{3,2,1,0:T(8,128)(2,1)}, u32[]{:S(2)}, u32[]{:S(2)}) collective-permute-start(bf16[1,4,128,512]{3,2,1,0:T(8,128)(2,1)} %fold.16.refs_8_), channel_id=1, source_target_pairs={{0,2},{1,3},{2,0},{3,1},{4,6},{5,7},{6,4},{7,5},{8,10},{9,11},{10,... | collective-permute-start | bytes 1572872 | tf_op jit(solution)/shard_map/ppermute | solution.py:496
  53.1 5.3 %collective-permute-done.18.refs_1_ = bf16[128,768]{1,0:T(8,128)(2,1)S(1)} collective-permute-done((bf16[128,768]{1,0:T(8,128)(2,1)S(1)}, bf16[128,768]{1,0:T(8,128)(2,1)S(1)}, u32[]{:S(2)}, u32[]{:S(2)}) %collective-permute-start.18) | collective-permute-done | bytes 196640 | tf_op jit(solution)/shard_map/ppermute | solution.py:496
  58.5 1.0 copy-done.3
  59.6 1.4 activate.5
  60.9 1.1 fold.17.refs_10_
  62.1 4.1 %attend.4 = (bf16[2,128,768]{2,1,0:T(8,128)(2,1)S(1)}, bf16[1,128,768]{2,1,0:T(8,128)(2,1)S(1)}, bf16[1,128,768]{2,1,0:T(8,128)(2,1)S(1)}) custom-call(s32[1]{0:T(128)} %bitcast.at_ref, bf16[128,768]{1,0:T(8,128)(2,1)S(1)} %get-tuple-element.72.refs_2_.refs_0_.q_ref, bf16[128,768]{1,0:T(8,128)(2,1)S(1)} %collective-permute-done.18.refs_1_, ...), custom_call_target="tpu_custom_call" | custom-call | flops 1000 | bytes 1000 | tf_op jit(solution)/shard_map/attend/pallas_call | solution.py:262
  66.7 1.8 %collective-permute-start.14 = (bf16[128,512]{1,0:T(8,128)(2,1)S(1)}, bf16[128,512]{1,0:T(8,128)(2,1)S(1)}, u32[]{:S(2)}, u32[]{:S(2)}) collective-permute-start(bf16[128,512]{1,0:T(8,128)(2,1)S(1)} %get-tuple-element.77.refs_2_.refs_0_.q_ref), channel_id=1, source_target_pairs={{0,2},{1,3},{2,0},{3,1},{4,6},{5,7},{6,4},{7,5},{8,10},{9,11},{10,... | collective-permute-start | bytes 393224 | tf_op jit(solution)/shard_map/ppermute | solution.py:496
  68.8 4.0 %collective-permute-done.14.refs_1_ = bf16[128,512]{1,0:T(8,128)(2,1)S(1)} collective-permute-done((bf16[128,512]{1,0:T(8,128)(2,1)S(1)}, bf16[128,512]{1,0:T(8,128)(2,1)S(1)}, u32[]{:S(2)}, u32[]{:S(2)}) %collective-permute-start.14) | collective-permute-done | bytes 131104 | tf_op jit(solution)/shard_map/ppermute | solution.py:496
  73.5 1.4 activate.6
  74.9 2.1 %collective-permute-start.25 = (bf16[128,512]{1,0:T(8,128)(2,1)S(1)}, bf16[128,512]{1,0:T(8,128)(2,1)S(1)}, u32[]{:S(2)}, u32[]{:S(2)}) collective-permute-start(bf16[128,512]{1,0:T(8,128)(2,1)S(1)} %get-tuple-element.80.refs_10_.refs_0_.q_ref), channel_id=1, source_target_pairs={{0,2},{1,3},{2,0},{3,1},{4,6},{5,7},{6,4},{7,5},{8,10},{9,11},{10,... | collective-permute-start | bytes 393224 | tf_op jit(solution)/shard_map/ppermute | solution.py:496
  77.2 3.1 %attend.5 = (bf16[2,128,512]{2,1,0:T(8,128)(2,1)S(1)}, bf16[1,128,512]{2,1,0:T(8,128)(2,1)S(1)}, bf16[1,128,512]{2,1,0:T(8,128)(2,1)S(1)}) custom-call(s32[1]{0:T(128)} %bitcast.at_ref, bf16[128,512]{1,0:T(8,128)(2,1)S(1)} %get-tuple-element.77.refs_2_.refs_0_.q_ref, bf16[128,512]{1,0:T(8,128)(2,1)S(1)} %collective-permute-done.14.refs_1_, ...), custom_call_target="tpu_custom_call" | custom-call | flops 1000 | bytes 1000 | tf_op jit(solution)/shard_map/attend/pallas_call | solution.py:262
  81.9 3.0 %collective-permute-done.29.refs_2_ = bf16[1,128,768]{2,1,0:T(8,128)(2,1)S(1)} collective-permute-done((bf16[1,128,768]{2,1,0:T(8,128)(2,1)S(1)}, bf16[1,128,768]{2,1,0:T(8,128)(2,1)S(1)}, u32[]{:S(2)}, u32[]{:S(2)}) %collective-permute-start.29) | collective-permute-done | bytes 196640 | tf_op jit(solution)/shard_map/ppermute | solution.py:496
  85.5 3.2 %attend.6 = (bf16[2,128,512]{2,1,0:T(8,128)(2,1)S(1)}, bf16[1,128,512]{2,1,0:T(8,128)(2,1)S(1)}, bf16[1,128,512]{2,1,0:T(8,128)(2,1)S(1)}) custom-call(s32[1]{0:T(128)} %bitcast.at_ref, bf16[128,512]{1,0:T(8,128)(2,1)S(1)} %get-tuple-element.80.refs_10_.refs_0_.q_ref, bf16[128,512]{1,0:T(8,128)(2,1)S(1)} %collective-permute-done.25.refs_1_, ...), custom_call_target="tpu_custom_call" | custom-call | flops 1000 | bytes 1000 | tf_op jit(solution)/shard_map/attend/pallas_call | solution.py:262
  88.7 1.8 %collective-permute-start.22 = (bf16[128,256]{1,0:T(8,128)(2,1)S(1)}, bf16[128,256]{1,0:T(8,128)(2,1)S(1)}, u32[]{:S(2)}, u32[]{:S(2)}) collective-permute-start(bf16[128,256]{1,0:T(8,128)(2,1)S(1)} %get-tuple-element.82.refs_2_.refs_0_.q_ref), channel_id=1, source_target_pairs={{0,2},{1,3},{2,0},{3,1},{4,6},{5,7},{6,4},{7,5},{8,10},{9,11},{10,... | collective-permute-start | bytes 196616 | tf_op jit(solution)/shard_map/ppermute | solution.py:496
  91.3 1.9 %collective-permute-done.22.refs_1_ = bf16[128,256]{1,0:T(8,128)(2,1)S(1)} collective-permute-done((bf16[128,256]{1,0:T(8,128)(2,1)S(1)}, bf16[128,256]{1,0:T(8,128)(2,1)S(1)}, u32[]{:S(2)}, u32[]{:S(2)}) %collective-permute-start.22) | collective-permute-done | bytes 65568 | tf_op jit(solution)/shard_map/ppermute | solution.py:496
  93.9 2.3 %collective-permute-start.38 = (bf16[1,128,512]{2,1,0:T(8,128)(2,1)S(1)}, bf16[1,128,512]{2,1,0:T(8,128)(2,1)S(1)}, u32[]{:S(2)}, u32[]{:S(2)}) collective-permute-start(bf16[1,128,512]{2,1,0:T(8,128)(2,1)S(1)} %fold.20.refs_10_), channel_id=1, source_target_pairs={{0,2},{1,3},{2,0},{3,1},{4,6},{5,7},{6,4},{7,5},{8,10},{9,11},{10,... | collective-permute-start | bytes 393224 | tf_op jit(solution)/shard_map/ppermute | solution.py:496
  96.1 2.0 %attend.7 = (bf16[2,128,256]{2,1,0:T(8,128)(2,1)S(1)}, bf16[1,128,256]{2,1,0:T(8,128)(2,1)S(1)}, bf16[1,128,256]{2,1,0:T(8,128)(2,1)S(1)}) custom-call(s32[1]{0:T(128)} %bitcast.at_ref, bf16[128,256]{1,0:T(8,128)(2,1)S(1)} %get-tuple-element.82.refs_2_.refs_0_.q_ref, bf16[128,256]{1,0:T(8,128)(2,1)S(1)} %collective-permute-done.22.refs_1_, ...), custom_call_target="tpu_custom_call" | custom-call | flops 1000 | bytes 1000 | tf_op jit(solution)/shard_map/attend/pallas_call | solution.py:262
  100.7 3.3 %collective-permute-done.36.refs_2_ = bf16[1,128,256]{2,1,0:T(8,128)(2,1)S(1)} collective-permute-done((bf16[1,128,256]{2,1,0:T(8,128)(2,1)S(1)}, bf16[1,128,256]{2,1,0:T(8,128)(2,1)S(1)}, u32[]{:S(2)}, u32[]{:S(2)}) %collective-permute-start.36) | collective-permute-done | bytes 65568 | tf_op jit(solution)/shard_map/ppermute | solution.py:496
  104.4 3.6 %collective-permute-start.41 = (f32[8,128]{1,0:T(8,128)S(1)}, f32[8,128]{1,0:T(8,128)S(1)}, u32[]{:S(2)}, u32[]{:S(2)}) collective-permute-start(f32[8,128]{1,0:T(8,128)S(1)} %get-tuple-element.102.refs_0_), channel_id=1, source_target_pairs={{0,12},{4,0},{8,4},{12,8},{1,13},{5,1},{9,5},{13,9},{2,14},{6,2},{... | collective-permute-start | bytes 12296 | tf_op jit(solution)/shard_map/ppermute | solution.py:520
  108.1 1.0 collective-permute-start.39
  109.4 3.2 %collective-permute-done.40.refs_2_ = f32[8,128]{1,0:T(8,128)S(1)} collective-permute-done((f32[8,128]{1,0:T(8,128)S(1)}, f32[8,128]{1,0:T(8,128)S(1)}, u32[]{:S(2)}, u32[]{:S(2)}) %collective-permute-start.40) | collective-permute-done | bytes 4128 | tf_op jit(solution)/shard_map/ppermute | solution.py:520
  114.5 5.8 %collective-permute-done.43 = bf16[64,2048]{1,0:T(8,128)(2,1)S(1)} collective-permute-done((bf16[64,2048]{1,0:T(8,128)(2,1)S(1)}, bf16[64,2048]{1,0:T(8,128)(2,1)S(1)}, u32[]{:S(2)}, u32[]{:S(2)}) %collective-permute-start.43) | collective-permute-done | bytes 262176 | tf_op jit(solution)/shard_map/ppermute | solution.py:496
  121.9 4.0 %output.4 = (bf16[2,4,16,1024]{3,2,1,0:T(8,128)(2,1)S(1)}, bf16[2,4,16,1024]{3,2,1,0:T(8,128)(2,1)S(1)}) custom-call(s32[4]{0:T(128)S(1)} %fusion.3.order_ref, bf16[4,16,2048]{2,1,0:T(8,128)(2,1)S(1)} %bitcast.42, bf16[4,16,2048]{2,1,0:T(8,128)(2,1)S(1)} %bitcast.44, bf16[4,16,2048]{2,1,0:T(8,128)(2,1)S(1)} %bitcast.48, bf16[4,16,2048]{2,1,0:T(8,128)(2,1)S(1)} %bitcast.50, ...), custom_call_target="tpu_custom_call" | custom-call | flops 1000 | bytes 1000 | tf_op jit(solution)/shard_map/output/pallas_call | solution.py:418
  125.8 3.2 %collective-permute-done.42.refs_0_ = bf16[64,2048]{1,0:T(8,128)(2,1)S(1)} collective-permute-done((bf16[64,2048]{1,0:T(8,128)(2,1)S(1)}, bf16[64,2048]{1,0:T(8,128)(2,1)S(1)}, u32[]{:S(2)}, u32[]{:S(2)}) %collective-permute-start.42) | collective-permute-done | bytes 262176 | tf_op jit(solution)/shard_map/ppermute | solution.py:496
  129.1 4.0 %output.5 = (bf16[2,4,16,1024]{3,2,1,0:T(8,128)(2,1)S(1)}, bf16[2,4,16,1024]{3,2,1,0:T(8,128)(2,1)S(1)}) custom-call(s32[4]{0:T(128)S(1)} %fusion.3.order_ref, bf16[4,16,2048]{2,1,0:T(8,128)(2,1)S(1)} %bitcast.43, bf16[4,16,2048]{2,1,0:T(8,128)(2,1)S(1)} %bitcast.45, bf16[4,16,2048]{2,1,0:T(8,128)(2,1)S(1)} %bitcast.49, bf16[4,16,2048]{2,1,0:T(8,128)(2,1)S(1)} %bitcast.51, ...), custom_call_target="tpu_custom_call" | custom-call | flops 1000 | bytes 1000 | tf_op jit(solution)/shard_map/output/pallas_call | solution.py:418
  133.0 2.1 %collective-permute-start.49 = (bf16[2,4,16,1024]{3,2,1,0:T(8,128)(2,1)S(1)}, bf16[2,4,16,1024]{3,2,1,0:T(8,128)(2,1)S(1)}, u32[]{:S(2)}, u32[]{:S(2)}) collective-permute-start(bf16[2,4,16,1024]{3,2,1,0:T(8,128)(2,1)S(1)} %get-tuple-element.110), channel_id=1, source_target_pairs={{0,4},{4,0},{8,12},{12,8},{1,5},{5,1},{9,13},{13,9},{2,6},{6,2},{1... | collective-permute-start | bytes 786440 | tf_op jit(solution)/shard_map/ppermute | solution.py:496
  135.1 4.0 %output.6 = (bf16[2,4,16,1024]{3,2,1,0:T(8,128)(2,1)S(1)}, bf16[2,4,16,1024]{3,2,1,0:T(8,128)(2,1)S(1)}) custom-call(s32[4]{0:T(128)S(1)} %fusion.3.order_ref, bf16[4,16,2048]{2,1,0:T(8,128)(2,1)S(1)} %bitcast.40, bf16[4,16,2048]{2,1,0:T(8,128)(2,1)S(1)} %bitcast.38, bf16[4,16,2048]{2,1,0:T(8,128)(2,1)S(1)} %bitcast.46, bf16[4,16,2048]{2,1,0:T(8,128)(2,1)S(1)} %bitcast.52, ...), custom_call_target="tpu_custom_call" | custom-call | flops 1000 | bytes 1000 | tf_op jit(solution)/shard_map/output/pallas_call | solution.py:418
  139.2 4.0 %output.7 = (bf16[2,4,16,1024]{3,2,1,0:T(8,128)(2,1)S(1)}, bf16[2,4,16,1024]{3,2,1,0:T(8,128)(2,1)S(1)}) custom-call(s32[4]{0:T(128)S(1)} %fusion.3.order_ref, bf16[4,16,2048]{2,1,0:T(8,128)(2,1)S(1)} %bitcast.41, bf16[4,16,2048]{2,1,0:T(8,128)(2,1)S(1)} %bitcast.39, bf16[4,16,2048]{2,1,0:T(8,128)(2,1)S(1)} %bitcast.47, bf16[4,16,2048]{2,1,0:T(8,128)(2,1)S(1)} %bitcast.53, ...), custom_call_target="tpu_custom_call" | custom-call | flops 1000 | bytes 1000 | tf_op jit(solution)/shard_map/output/pallas_call | solution.py:418
  143.2 2.1 %collective-permute-start.52 = (bf16[2,4,16,1024]{3,2,1,0:T(8,128)(2,1)S(1)}, bf16[2,4,16,1024]{3,2,1,0:T(8,128)(2,1)S(1)}, u32[]{:S(2)}, u32[]{:S(2)}) collective-permute-start(bf16[2,4,16,1024]{3,2,1,0:T(8,128)(2,1)S(1)} %get-tuple-element.113), channel_id=1, source_target_pairs={{0,4},{4,0},{8,12},{12,8},{1,5},{5,1},{9,13},{13,9},{2,6},{6,2},{1... | collective-permute-start | bytes 786440 | tf_op jit(solution)/shard_map/ppermute | solution.py:496
  145.5 1.2 collective-permute-start.54
  146.7 1.8 %collective-permute-start.53 = (bf16[1,4,16,1024]{3,2,1,0:T(8,128)(2,1)S(1)}, bf16[1,4,16,1024]{3,2,1,0:T(8,128)(2,1)S(1)}, u32[]{:S(2)}, u32[]{:S(2)}) collective-permute-start(bf16[1,4,16,1024]{3,2,1,0:T(8,128)(2,1)S(1)} %fold.22.refs_2_), channel_id=1, source_target_pairs={{0,8},{4,12},{8,0},{12,4},{1,9},{5,13},{9,1},{13,5},{2,10},{6,14},... | collective-permute-start | bytes 393224 | tf_op jit(solution)/shard_map/ppermute | solution.py:496
  148.6 6.4 %collective-permute-done.48.refs_1_ = bf16[2,4,16,1024]{3,2,1,0:T(8,128)(2,1)S(1)} collective-permute-done((bf16[2,4,16,1024]{3,2,1,0:T(8,128)(2,1)S(1)}, bf16[2,4,16,1024]{3,2,1,0:T(8,128)(2,1)S(1)}, u32[]{:S(2)}, u32[]{:S(2)}) %collective-permute-start.48) | collective-permute-done | bytes 262176 | tf_op jit(solution)/shard_map/ppermute | solution.py:496
  155.8 2.2 %collective-permute-done.53.refs_2_ = bf16[1,4,16,1024]{3,2,1,0:T(8,128)(2,1)S(1)} collective-permute-done((bf16[1,4,16,1024]{3,2,1,0:T(8,128)(2,1)S(1)}, bf16[1,4,16,1024]{3,2,1,0:T(8,128)(2,1)S(1)}, u32[]{:S(2)}, u32[]{:S(2)}) %collective-permute-start.53) | collective-permute-done | bytes 131104 | tf_op jit(solution)/shard_map/ppermute | solution.py:496
  158.1 2.3 %close.2 = (bf16[8,16,2048]{2,1,0:T(8,128)(2,1)}, f32[8,128]{1,0:T(8,128)S(1)}) custom-call(s32[2]{0:T(128)S(1)} %pad_add_fusion.1.at_ref, bf16[32,16,2048]{2,1,0:T(8,128)(2,1)} %bitcast.76, bf16[2,4,16,1024]{3,2,1,0:T(8,128)(2,1)S(1)} %get-tuple-element.106.refs_1_.refs_5_.refs_0_, bf16[2,4,16,1024]{3,2,1,0:T(8,128)(2,1)S(1)} %collective-permute-done.50.refs_1_, ...), custom_call_target="tpu_custom_call" | custom-call | flops 1000 | bytes 1000 | tf_op jit(solution)/shard_map/close/pallas_call | solution.py:461
  160.5 3.4 %collective-permute-start.55 = (bf16[1,4,16,1024]{3,2,1,0:T(8,128)(2,1)S(1)}, bf16[1,4,16,1024]{3,2,1,0:T(8,128)(2,1)S(1)}, u32[]{:S(2)}, u32[]{:S(2)}) collective-permute-start(bf16[1,4,16,1024]{3,2,1,0:T(8,128)(2,1)S(1)} %fold.25), channel_id=1, source_target_pairs={{0,8},{4,12},{8,0},{12,4},{1,9},{5,13},{9,1},{13,5},{2,10},{6,14},... | collective-permute-start | bytes 393224 | tf_op jit(solution)/shard_map/ppermute | solution.py:496
  164.1 9.1 %collective-permute-done.55.refs_5_ = bf16[1,4,16,1024]{3,2,1,0:T(8,128)(2,1)S(1)} collective-permute-done((bf16[1,4,16,1024]{3,2,1,0:T(8,128)(2,1)S(1)}, bf16[1,4,16,1024]{3,2,1,0:T(8,128)(2,1)S(1)}, u32[]{:S(2)}, u32[]{:S(2)}) %collective-permute-start.55) | collective-permute-done | bytes 131104 | tf_op jit(solution)/shard_map/ppermute | solution.py:496
  173.2 2.3 %collective-permute-done.51.refs_2_ = bf16[1,4,16,1024]{3,2,1,0:T(8,128)(2,1)S(1)} collective-permute-done((bf16[1,4,16,1024]{3,2,1,0:T(8,128)(2,1)S(1)}, bf16[1,4,16,1024]{3,2,1,0:T(8,128)(2,1)S(1)}, u32[]{:S(2)}, u32[]{:S(2)}) %collective-permute-start.51) | collective-permute-done | bytes 131104 | tf_op jit(solution)/shard_map/ppermute | solution.py:496
  175.6 2.3 %close.3 = (bf16[8,16,2048]{2,1,0:T(8,128)(2,1)}, f32[8,128]{1,0:T(8,128)}) custom-call(s32[2]{0:T(128)S(1)} %pad_add_fusion.at_ref, bf16[32,16,2048]{2,1,0:T(8,128)(2,1)} %bitcast.77, bf16[2,4,16,1024]{3,2,1,0:T(8,128)(2,1)S(1)} %get-tuple-element.108.refs_5_.refs_0_, ...), custom_call_target="tpu_custom_call", output_to_operand_aliasing={{0}: (8, {})} | custom-call | flops 1000 | bytes 1000 | tf_op jit(solution)/shard_map/close/pallas_call | solution.py:461
  (134 shorter events, 18.7 us)
Async XLA Ops:
  5.5 9.4 %collective-permute-start = (bf16[1,4,128,256]{3,2,1,0:T(8,128)(2,1)S(1)}, bf16[1,4,128,256]{3,2,1,0:T(8,128)(2,1)S(1)}, u32[]{:S(2)}, u32[]{:S(2)}) collective-permute-start(bf16[1,4,128,256]{3,2,1,0:T(8,128)(2,1)S(1)} %get-tuple-element.64), channel_id=1, source_target_pairs={{0,1},{1,0},{2,3},{3,2},{4,5},{5,4},{6,7},{7,6},{8,9},{9,8},{10,11... | collective-permute-start | bytes 786440 | tf_op jit(solution)/shard_map/ppermute | solution.py:496
  6.1 8.8 %collective-permute-start.1 = (bf16[1,4,128,256]{3,2,1,0:T(8,128)(2,1)S(1)}, bf16[1,4,128,256]{3,2,1,0:T(8,128)(2,1)S(1)}, u32[]{:S(2)}, u32[]{:S(2)}) collective-permute-start(bf16[1,4,128,256]{3,2,1,0:T(8,128)(2,1)S(1)} %get-tuple-element.65), channel_id=1, source_target_pairs={{0,1},{1,0},{2,3},{3,2},{4,5},{5,4},{6,7},{7,6},{8,9},{9,8},{10,11... | collective-permute-start | bytes 786440 | tf_op jit(solution)/shard_map/ppermute | solution.py:496
  14.9 12.6 %collective-permute-start.3 = (bf16[1,4,128,512]{3,2,1,0:T(8,128)(2,1)S(1)}, bf16[1,4,128,512]{3,2,1,0:T(8,128)(2,1)S(1)}, u32[]{:S(2)}, u32[]{:S(2)}) collective-permute-start(bf16[1,4,128,512]{3,2,1,0:T(8,128)(2,1)S(1)} %tie.10), channel_id=1, source_target_pairs={{0,1},{1,0},{2,3},{3,2},{4,5},{5,4},{6,7},{7,6},{8,9},{9,8},{10,11... | collective-permute-start | bytes 1572872 | tf_op jit(solution)/shard_map/ppermute | solution.py:496
  15.4 12.1 %collective-permute-start.2 = (bf16[1,4,128,512]{3,2,1,0:T(8,128)(2,1)S(1)}, bf16[1,4,128,512]{3,2,1,0:T(8,128)(2,1)S(1)}, u32[]{:S(2)}, u32[]{:S(2)}) collective-permute-start(bf16[1,4,128,512]{3,2,1,0:T(8,128)(2,1)S(1)} %tie.9), channel_id=1, source_target_pairs={{0,1},{1,0},{2,3},{3,2},{4,5},{5,4},{6,7},{7,6},{8,9},{9,8},{10,11... | collective-permute-start | bytes 1572872 | tf_op jit(solution)/shard_map/ppermute | solution.py:496
  15.8 11.7 %collective-permute-start.4 = (bf16[1,4,128,256]{3,2,1,0:T(8,128)(2,1)S(1)}, bf16[1,4,128,256]{3,2,1,0:T(8,128)(2,1)S(1)}, u32[]{:S(2)}, u32[]{:S(2)}) collective-permute-start(bf16[1,4,128,256]{3,2,1,0:T(8,128)(2,1)S(1)} %fold.13.refs_8_), channel_id=1, source_target_pairs={{0,2},{1,3},{2,0},{3,1},{4,6},{5,7},{6,4},{7,5},{8,10},{9,11},{10,... | collective-permute-start | bytes 786440 | tf_op jit(solution)/shard_map/ppermute | solution.py:496
  27.5 9.8 %collective-permute-start.6 = (bf16[1,4,128,512]{3,2,1,0:T(8,128)(2,1)S(1)}, bf16[1,4,128,512]{3,2,1,0:T(8,128)(2,1)S(1)}, u32[]{:S(2)}, u32[]{:S(2)}) collective-permute-start(bf16[1,4,128,512]{3,2,1,0:T(8,128)(2,1)S(1)} %tie.12), channel_id=1, source_target_pairs={{0,1},{1,0},{2,3},{3,2},{4,5},{5,4},{6,7},{7,6},{8,9},{9,8},{10,11... | collective-permute-start | bytes 1572872 | tf_op jit(solution)/shard_map/ppermute | solution.py:496
  27.6 9.7 %collective-permute-start.5 = (bf16[1,4,128,512]{3,2,1,0:T(8,128)(2,1)S(1)}, bf16[1,4,128,512]{3,2,1,0:T(8,128)(2,1)S(1)}, u32[]{:S(2)}, u32[]{:S(2)}) collective-permute-start(bf16[1,4,128,512]{3,2,1,0:T(8,128)(2,1)S(1)} %tie.11), channel_id=1, source_target_pairs={{0,1},{1,0},{2,3},{3,2},{4,5},{5,4},{6,7},{7,6},{8,9},{9,8},{10,11... | collective-permute-start | bytes 1572872 | tf_op jit(solution)/shard_map/ppermute | solution.py:496
  28.4 14.0 %collective-permute-start.8 = (bf16[1,4,128,512]{3,2,1,0:T(8,128)(2,1)S(1)}, bf16[1,4,128,512]{3,2,1,0:T(8,128)(2,1)S(1)}, u32[]{:S(2)}, u32[]{:S(2)}) collective-permute-start(bf16[1,4,128,512]{3,2,1,0:T(8,128)(2,1)S(1)} %fold.14.refs_8_), channel_id=1, source_target_pairs={{0,2},{1,3},{2,0},{3,1},{4,6},{5,7},{6,4},{7,5},{8,10},{9,11},{10,... | collective-permute-start | bytes 1572872 | tf_op jit(solution)/shard_map/ppermute | solution.py:496
  37.3 5.9 %collective-permute-start.7 = (bf16[1,4,128,512]{3,2,1,0:T(8,128)(2,1)S(1)}, bf16[1,4,128,512]{3,2,1,0:T(8,128)(2,1)S(1)}, u32[]{:S(2)}, u32[]{:S(2)}) collective-permute-start(bf16[1,4,128,512]{3,2,1,0:T(8,128)(2,1)S(1)} %tie.13), channel_id=1, source_target_pairs={{0,1},{1,0},{2,3},{3,2},{4,5},{5,4},{6,7},{7,6},{8,9},{9,8},{10,11... | collective-permute-start | bytes 1572872 | tf_op jit(solution)/shard_map/ppermute | solution.py:496
  38.1 13.0 %collective-permute-start.9 = (bf16[1,4,128,512]{3,2,1,0:T(8,128)(2,1)S(1)}, bf16[1,4,128,512]{3,2,1,0:T(8,128)(2,1)S(1)}, u32[]{:S(2)}, u32[]{:S(2)}) collective-permute-start(bf16[1,4,128,512]{3,2,1,0:T(8,128)(2,1)S(1)} %tie.14), channel_id=1, source_target_pairs={{0,1},{1,0},{2,3},{3,2},{4,5},{5,4},{6,7},{7,6},{8,9},{9,8},{10,11... | collective-permute-start | bytes 1572872 | tf_op jit(solution)/shard_map/ppermute | solution.py:496
  39.1 19.4 %collective-permute-start.12 = (bf16[1,4,128,512]{3,2,1,0:T(8,128)(2,1)}, bf16[1,4,128,512]{3,2,1,0:T(8,128)(2,1)}, u32[]{:S(2)}, u32[]{:S(2)}) collective-permute-start(bf16[1,4,128,512]{3,2,1,0:T(8,128)(2,1)} %fold.15.refs_6_), channel_id=1, source_target_pairs={{0,2},{1,3},{2,0},{3,1},{4,6},{5,7},{6,4},{7,5},{8,10},{9,11},{10,... | collective-permute-start | bytes 1572872 | tf_op jit(solution)/shard_map/ppermute | solution.py:496
  42.9 15.5 %collective-permute-start.18 = (bf16[128,768]{1,0:T(8,128)(2,1)S(1)}, bf16[128,768]{1,0:T(8,128)(2,1)S(1)}, u32[]{:S(2)}, u32[]{:S(2)}) collective-permute-start(bf16[128,768]{1,0:T(8,128)(2,1)S(1)} %get-tuple-element.72.refs_2_.refs_0_.q_ref), channel_id=1, source_target_pairs={{0,2},{1,3},{2,0},{3,1},{4,6},{5,7},{6,4},{7,5},{8,10},{9,11},{10,... | collective-permute-start | bytes 589832 | tf_op jit(solution)/shard_map/ppermute | solution.py:496
  51.1 9.8 %collective-permute-start.11 = (bf16[1,4,128,256]{3,2,1,0:T(8,128)(2,1)}, bf16[1,4,128,256]{3,2,1,0:T(8,128)(2,1)}, u32[]{:S(2)}, u32[]{:S(2)}) collective-permute-start(bf16[1,4,128,256]{3,2,1,0:T(8,128)(2,1)} %tie.16), channel_id=1, source_target_pairs={{0,1},{1,0},{2,3},{3,2},{4,5},{5,4},{6,7},{7,6},{8,9},{9,8},{10,11... | collective-permute-start | bytes 786440 | tf_op jit(solution)/shard_map/ppermute | solution.py:496
  51.1 22.4 %collective-permute-start.17 = (bf16[1,4,128,512]{3,2,1,0:T(8,128)(2,1)}, bf16[1,4,128,512]{3,2,1,0:T(8,128)(2,1)}, u32[]{:S(2)}, u32[]{:S(2)}) collective-permute-start(bf16[1,4,128,512]{3,2,1,0:T(8,128)(2,1)} %fold.16.refs_8_), channel_id=1, source_target_pairs={{0,2},{1,3},{2,0},{3,1},{4,6},{5,7},{6,4},{7,5},{8,10},{9,11},{10,... | collective-permute-start | bytes 1572872 | tf_op jit(solution)/shard_map/ppermute | solution.py:496
  52.9 9.1 %collective-permute-start.19 = (bf16[128,768]{1,0:T(8,128)(2,1)S(1)}, bf16[128,768]{1,0:T(8,128)(2,1)}, u32[]{:S(2)}, u32[]{:S(2)}) collective-permute-start(bf16[128,768]{1,0:T(8,128)(2,1)S(1)} %get-tuple-element.72.refs_2_.refs_0_.q_ref), channel_id=1, source_target_pairs={{0,1},{1,0},{2,3},{3,2},{4,5},{5,4},{6,7},{7,6},{8,9},{9,8},{10,11... | collective-permute-start | bytes 589832 | tf_op jit(solution)/shard_map/ppermute | solution.py:496
  66.1 6.7 %collective-permute-start.21 = (bf16[1,128,768]{2,1,0:T(8,128)(2,1)S(1)}, bf16[1,128,768]{2,1,0:T(8,128)(2,1)S(1)}, u32[]{:S(2)}, u32[]{:S(2)}) collective-permute-start(bf16[1,128,768]{2,1,0:T(8,128)(2,1)S(1)} %get-tuple-element.79), channel_id=1, source_target_pairs={{0,1},{1,0},{2,3},{3,2},{4,5},{5,4},{6,7},{7,6},{8,9},{9,8},{10,11... | collective-permute-start | bytes 589832 | tf_op jit(solution)/shard_map/ppermute | solution.py:496
  66.7 6.1 %collective-permute-start.14 = (bf16[128,512]{1,0:T(8,128)(2,1)S(1)}, bf16[128,512]{1,0:T(8,128)(2,1)S(1)}, u32[]{:S(2)}, u32[]{:S(2)}) collective-permute-start(bf16[128,512]{1,0:T(8,128)(2,1)S(1)} %get-tuple-element.77.refs_2_.refs_0_.q_ref), channel_id=1, source_target_pairs={{0,2},{1,3},{2,0},{3,1},{4,6},{5,7},{6,4},{7,5},{8,10},{9,11},{10,... | collective-permute-start | bytes 393224 | tf_op jit(solution)/shard_map/ppermute | solution.py:496
  68.5 11.8 %collective-permute-start.10 = (bf16[1,4,128,256]{3,2,1,0:T(8,128)(2,1)S(1)}, bf16[1,4,128,256]{3,2,1,0:T(8,128)(2,1)S(1)}, u32[]{:S(2)}, u32[]{:S(2)}) collective-permute-start(bf16[1,4,128,256]{3,2,1,0:T(8,128)(2,1)S(1)} %tie.15), channel_id=1, source_target_pairs={{0,1},{1,0},{2,3},{3,2},{4,5},{5,4},{6,7},{7,6},{8,9},{9,8},{10,11... | collective-permute-start | bytes 786440 | tf_op jit(solution)/shard_map/ppermute | solution.py:496
  68.5 12.2 %collective-permute-start.13 = (bf16[1,4,128,256]{3,2,1,0:T(8,128)(2,1)S(1)}, bf16[1,4,128,256]{3,2,1,0:T(8,128)(2,1)S(1)}, u32[]{:S(2)}, u32[]{:S(2)}) collective-permute-start(bf16[1,4,128,256]{3,2,1,0:T(8,128)(2,1)S(1)} %fold.17.refs_10_), channel_id=1, source_target_pairs={{0,2},{1,3},{2,0},{3,1},{4,6},{5,7},{6,4},{7,5},{8,10},{9,11},{10,... | collective-permute-start | bytes 786440 | tf_op jit(solution)/shard_map/ppermute | solution.py:496
  72.8 4.2 %collective-permute-start.15 = (bf16[128,512]{1,0:T(8,128)(2,1)S(1)}, bf16[128,512]{1,0:T(8,128)(2,1)S(1)}, u32[]{:S(2)}, u32[]{:S(2)}) collective-permute-start(bf16[128,512]{1,0:T(8,128)(2,1)S(1)} %get-tuple-element.77.refs_2_.refs_0_.q_ref), channel_id=1, source_target_pairs={{0,1},{1,0},{2,3},{3,2},{4,5},{5,4},{6,7},{7,6},{8,9},{9,8},{10,11... | collective-permute-start | bytes 393224 | tf_op jit(solution)/shard_map/ppermute | solution.py:496
  74.9 6.3 %collective-permute-start.25 = (bf16[128,512]{1,0:T(8,128)(2,1)S(1)}, bf16[128,512]{1,0:T(8,128)(2,1)S(1)}, u32[]{:S(2)}, u32[]{:S(2)}) collective-permute-start(bf16[128,512]{1,0:T(8,128)(2,1)S(1)} %get-tuple-element.80.refs_10_.refs_0_.q_ref), channel_id=1, source_target_pairs={{0,2},{1,3},{2,0},{3,1},{4,6},{5,7},{6,4},{7,5},{8,10},{9,11},{10,... | collective-permute-start | bytes 393224 | tf_op jit(solution)/shard_map/ppermute | solution.py:496
  77.0 4.9 %collective-permute-start.28 = (bf16[1,128,768]{2,1,0:T(8,128)(2,1)S(1)}, bf16[1,128,768]{2,1,0:T(8,128)(2,1)S(1)}, u32[]{:S(2)}, u32[]{:S(2)}) collective-permute-start(bf16[1,128,768]{2,1,0:T(8,128)(2,1)S(1)} %get-tuple-element.85), channel_id=1, source_target_pairs={{0,1},{1,0},{2,3},{3,2},{4,5},{5,4},{6,7},{7,6},{8,9},{9,8},{10,11... | collective-permute-start | bytes 589832 | tf_op jit(solution)/shard_map/ppermute | solution.py:496
  77.0 7.9 %collective-permute-start.29 = (bf16[1,128,768]{2,1,0:T(8,128)(2,1)S(1)}, bf16[1,128,768]{2,1,0:T(8,128)(2,1)S(1)}, u32[]{:S(2)}, u32[]{:S(2)}) collective-permute-start(bf16[1,128,768]{2,1,0:T(8,128)(2,1)S(1)} %fold.18.refs_3_), channel_id=1, source_target_pairs={{0,2},{1,3},{2,0},{3,1},{4,6},{5,7},{6,4},{7,5},{8,10},{9,11},{10,... | collective-permute-start | bytes 589832 | tf_op jit(solution)/shard_map/ppermute | solution.py:496
  80.8 4.7 %collective-permute-start.26 = (bf16[128,512]{1,0:T(8,128)(2,1)S(1)}, bf16[128,512]{1,0:T(8,128)(2,1)S(1)}, u32[]{:S(2)}, u32[]{:S(2)}) collective-permute-start(bf16[128,512]{1,0:T(8,128)(2,1)S(1)} %get-tuple-element.80.refs_10_.refs_0_.q_ref), channel_id=1, source_target_pairs={{0,1},{1,0},{2,3},{3,2},{4,5},{5,4},{6,7},{7,6},{8,9},{9,8},{10,11... | collective-permute-start | bytes 393224 | tf_op jit(solution)/shard_map/ppermute | solution.py:496
  81.2 4.3 %collective-permute-start.27 = (bf16[128,512]{1,0:T(8,128)(2,1)S(1)}, bf16[128,512]{1,0:T(8,128)(2,1)S(1)}, u32[]{:S(2)}, u32[]{:S(2)}) collective-permute-start(bf16[128,512]{1,0:T(8,128)(2,1)S(1)} %collective-permute-done.25.refs_1_), channel_id=1, source_target_pairs={{0,1},{1,0},{2,3},{3,2},{4,5},{5,4},{6,7},{7,6},{8,9},{9,8},{10,11... | collective-permute-start | bytes 393224 | tf_op jit(solution)/shard_map/ppermute | solution.py:496
  88.6 4.6 %collective-permute-start.31 = (bf16[1,128,512]{2,1,0:T(8,128)(2,1)S(1)}, bf16[1,128,512]{2,1,0:T(8,128)(2,1)S(1)}, u32[]{:S(2)}, u32[]{:S(2)}) collective-permute-start(bf16[1,128,512]{2,1,0:T(8,128)(2,1)S(1)} %get-tuple-element.89), channel_id=1, source_target_pairs={{0,1},{1,0},{2,3},{3,2},{4,5},{5,4},{6,7},{7,6},{8,9},{9,8},{10,11... | collective-permute-start | bytes 393224 | tf_op jit(solution)/shard_map/ppermute | solution.py:496
  88.7 4.5 %collective-permute-start.22 = (bf16[128,256]{1,0:T(8,128)(2,1)S(1)}, bf16[128,256]{1,0:T(8,128)(2,1)S(1)}, u32[]{:S(2)}, u32[]{:S(2)}) collective-permute-start(bf16[128,256]{1,0:T(8,128)(2,1)S(1)} %get-tuple-element.82.refs_2_.refs_0_.q_ref), channel_id=1, source_target_pairs={{0,2},{1,3},{2,0},{3,1},{4,6},{5,7},{6,4},{7,5},{8,10},{9,11},{10,... | collective-permute-start | bytes 196616 | tf_op jit(solution)/shard_map/ppermute | solution.py:496
  90.5 7.7 %collective-permute-start.34 = (bf16[1,128,512]{2,1,0:T(8,128)(2,1)S(1)}, bf16[1,128,512]{2,1,0:T(8,128)(2,1)S(1)}, u32[]{:S(2)}, u32[]{:S(2)}) collective-permute-start(bf16[1,128,512]{2,1,0:T(8,128)(2,1)S(1)} %get-tuple-element.94), channel_id=1, source_target_pairs={{0,1},{1,0},{2,3},{3,2},{4,5},{5,4},{6,7},{7,6},{8,9},{9,8},{10,11... | collective-permute-start | bytes 393224 | tf_op jit(solution)/shard_map/ppermute | solution.py:496
  91.0 7.7 %collective-permute-start.35 = (bf16[1,128,512]{2,1,0:T(8,128)(2,1)S(1)}, bf16[1,128,512]{2,1,0:T(8,128)(2,1)S(1)}, u32[]{:S(2)}, u32[]{:S(2)}) collective-permute-start(bf16[1,128,512]{2,1,0:T(8,128)(2,1)S(1)} %fold.19.refs_3_), channel_id=1, source_target_pairs={{0,2},{1,3},{2,0},{3,1},{4,6},{5,7},{6,4},{7,5},{8,10},{9,11},{10,... | collective-permute-start | bytes 393224 | tf_op jit(solution)/shard_map/ppermute | solution.py:496
  93.2 7.0 %collective-permute-start.37 = (bf16[1,128,512]{2,1,0:T(8,128)(2,1)S(1)}, bf16[1,128,512]{2,1,0:T(8,128)(2,1)S(1)}, u32[]{:S(2)}, u32[]{:S(2)}) collective-permute-start(bf16[1,128,512]{2,1,0:T(8,128)(2,1)S(1)} %get-tuple-element.99), channel_id=1, source_target_pairs={{0,1},{1,0},{2,3},{3,2},{4,5},{5,4},{6,7},{7,6},{8,9},{9,8},{10,11... | collective-permute-start | bytes 393224 | tf_op jit(solution)/shard_map/ppermute | solution.py:496
  93.9 6.3 %collective-permute-start.38 = (bf16[1,128,512]{2,1,0:T(8,128)(2,1)S(1)}, bf16[1,128,512]{2,1,0:T(8,128)(2,1)S(1)}, u32[]{:S(2)}, u32[]{:S(2)}) collective-permute-start(bf16[1,128,512]{2,1,0:T(8,128)(2,1)S(1)} %fold.20.refs_10_), channel_id=1, source_target_pairs={{0,2},{1,3},{2,0},{3,1},{4,6},{5,7},{6,4},{7,5},{8,10},{9,11},{10,... | collective-permute-start | bytes 393224 | tf_op jit(solution)/shard_map/ppermute | solution.py:496
  99.6 4.3 %collective-permute-start.36 = (bf16[1,128,256]{2,1,0:T(8,128)(2,1)S(1)}, bf16[1,128,256]{2,1,0:T(8,128)(2,1)S(1)}, u32[]{:S(2)}, u32[]{:S(2)}) collective-permute-start(bf16[1,128,256]{2,1,0:T(8,128)(2,1)S(1)} %fold.21.refs_3_), channel_id=1, source_target_pairs={{0,2},{1,3},{2,0},{3,1},{4,6},{5,7},{6,4},{7,5},{8,10},{9,11},{10,... | collective-permute-start | bytes 196616 | tf_op jit(solution)/shard_map/ppermute | solution.py:496
  104.4 5.0 %collective-permute-start.41 = (f32[8,128]{1,0:T(8,128)S(1)}, f32[8,128]{1,0:T(8,128)S(1)}, u32[]{:S(2)}, u32[]{:S(2)}) collective-permute-start(f32[8,128]{1,0:T(8,128)S(1)} %get-tuple-element.102.refs_0_), channel_id=1, source_target_pairs={{0,12},{4,0},{8,4},{12,8},{1,13},{5,1},{9,5},{13,9},{2,14},{6,2},{... | collective-permute-start | bytes 12296 | tf_op jit(solution)/shard_map/ppermute | solution.py:520
  108.1 4.5 %collective-permute-start.40 = (f32[8,128]{1,0:T(8,128)S(1)}, f32[8,128]{1,0:T(8,128)S(1)}, u32[]{:S(2)}, u32[]{:S(2)}) collective-permute-start(f32[8,128]{1,0:T(8,128)S(1)} %get-tuple-element.102.refs_0_), channel_id=1, source_target_pairs={{0,8},{4,12},{8,0},{12,4},{1,9},{5,13},{9,1},{13,5},{2,10},{6,14},... | collective-permute-start | bytes 12296 | tf_op jit(solution)/shard_map/ppermute | solution.py:520
  108.1 5.4 %collective-permute-start.39 = (f32[8,128]{1,0:T(8,128)S(1)}, f32[8,128]{1,0:T(8,128)S(1)}, u32[]{:S(2)}, u32[]{:S(2)}) collective-permute-start(f32[8,128]{1,0:T(8,128)S(1)} %get-tuple-element.102.refs_0_), channel_id=1, source_target_pairs={{0,4},{4,8},{8,12},{12,0},{1,5},{5,9},{9,13},{13,1},{2,6},{6,10},{... | collective-permute-start | bytes 12296 | tf_op jit(solution)/shard_map/ppermute | solution.py:520
  113.9 6.4 %collective-permute-start.43 = (bf16[64,2048]{1,0:T(8,128)(2,1)S(1)}, bf16[64,2048]{1,0:T(8,128)(2,1)S(1)}, u32[]{:S(2)}, u32[]{:S(2)}) collective-permute-start(bf16[64,2048]{1,0:T(8,128)(2,1)S(1)} %get-tuple-element.105), channel_id=1, source_target_pairs={{0,2},{1,3},{2,0},{3,1},{4,6},{5,7},{6,4},{7,5},{8,10},{9,11},{10,... | collective-permute-start | bytes 786440 | tf_op jit(solution)/shard_map/ppermute | solution.py:496
  114.5 6.6 %collective-permute-start.44 = (bf16[64,2048]{1,0:T(8,128)(2,1)S(1)}, bf16[64,2048]{1,0:T(8,128)(2,1)S(1)}, u32[]{:S(2)}, u32[]{:S(2)}) collective-permute-start(bf16[64,2048]{1,0:T(8,128)(2,1)S(1)} %get-tuple-element.105), channel_id=1, source_target_pairs={{0,1},{1,0},{2,3},{3,2},{4,5},{5,4},{6,7},{7,6},{8,9},{9,8},{10,11... | collective-permute-start | bytes 786440 | tf_op jit(solution)/shard_map/ppermute | solution.py:496
  120.3 8.7 %collective-permute-start.42 = (bf16[64,2048]{1,0:T(8,128)(2,1)S(1)}, bf16[64,2048]{1,0:T(8,128)(2,1)S(1)}, u32[]{:S(2)}, u32[]{:S(2)}) collective-permute-start(bf16[64,2048]{1,0:T(8,128)(2,1)S(1)} %get-tuple-element.104), channel_id=1, source_target_pairs={{0,2},{1,3},{2,0},{3,1},{4,6},{5,7},{6,4},{7,5},{8,10},{9,11},{10,... | collective-permute-start | bytes 786440 | tf_op jit(solution)/shard_map/ppermute | solution.py:496
  120.9 14.3 %collective-permute-start.46 = (bf16[64,2048]{1,0:T(8,128)(2,1)S(1)}, bf16[64,2048]{1,0:T(8,128)(2,1)S(1)}, u32[]{:S(2)}, u32[]{:S(2)}) collective-permute-start(bf16[64,2048]{1,0:T(8,128)(2,1)S(1)} %get-tuple-element.104), channel_id=1, source_target_pairs={{0,1},{1,0},{2,3},{3,2},{4,5},{5,4},{6,7},{7,6},{8,9},{9,8},{10,11... | collective-permute-start | bytes 786440 | tf_op jit(solution)/shard_map/ppermute | solution.py:496
  129.1 6.1 %collective-permute-start.47 = (bf16[64,2048]{1,0:T(8,128)(2,1)S(1)}, bf16[64,2048]{1,0:T(8,128)(2,1)S(1)}, u32[]{:S(2)}, u32[]{:S(2)}) collective-permute-start(bf16[64,2048]{1,0:T(8,128)(2,1)S(1)} %tie.17), channel_id=1, source_target_pairs={{0,1},{1,0},{2,3},{3,2},{4,5},{5,4},{6,7},{7,6},{8,9},{9,8},{10,11... | collective-permute-start | bytes 786440 | tf_op jit(solution)/shard_map/ppermute | solution.py:496
  129.1 16.2 %collective-permute-start.50 = (bf16[2,4,16,1024]{3,2,1,0:T(8,128)(2,1)S(1)}, bf16[2,4,16,1024]{3,2,1,0:T(8,128)(2,1)S(1)}, u32[]{:S(2)}, u32[]{:S(2)}) collective-permute-start(bf16[2,4,16,1024]{3,2,1,0:T(8,128)(2,1)S(1)} %get-tuple-element.111), channel_id=1, source_target_pairs={{0,4},{4,0},{8,12},{12,8},{1,5},{5,1},{9,13},{13,9},{2,6},{6,2},{1... | collective-permute-start | bytes 786440 | tf_op jit(solution)/shard_map/ppermute | solution.py:496
  133.0 12.3 %collective-permute-start.49 = (bf16[2,4,16,1024]{3,2,1,0:T(8,128)(2,1)S(1)}, bf16[2,4,16,1024]{3,2,1,0:T(8,128)(2,1)S(1)}, u32[]{:S(2)}, u32[]{:S(2)}) collective-permute-start(bf16[2,4,16,1024]{3,2,1,0:T(8,128)(2,1)S(1)} %get-tuple-element.110), channel_id=1, source_target_pairs={{0,4},{4,0},{8,12},{12,8},{1,5},{5,1},{9,13},{13,9},{2,6},{6,2},{1... | collective-permute-start | bytes 786440 | tf_op jit(solution)/shard_map/ppermute | solution.py:496
  139.1 15.9 %collective-permute-start.48 = (bf16[2,4,16,1024]{3,2,1,0:T(8,128)(2,1)S(1)}, bf16[2,4,16,1024]{3,2,1,0:T(8,128)(2,1)S(1)}, u32[]{:S(2)}, u32[]{:S(2)}) collective-permute-start(bf16[2,4,16,1024]{3,2,1,0:T(8,128)(2,1)S(1)} %get-tuple-element.109), channel_id=1, source_target_pairs={{0,4},{4,0},{8,12},{12,8},{1,5},{5,1},{9,13},{13,9},{2,6},{6,2},{1... | collective-permute-start | bytes 786440 | tf_op jit(solution)/shard_map/ppermute | solution.py:496
  143.2 17.2 %collective-permute-start.52 = (bf16[2,4,16,1024]{3,2,1,0:T(8,128)(2,1)S(1)}, bf16[2,4,16,1024]{3,2,1,0:T(8,128)(2,1)S(1)}, u32[]{:S(2)}, u32[]{:S(2)}) collective-permute-start(bf16[2,4,16,1024]{3,2,1,0:T(8,128)(2,1)S(1)} %get-tuple-element.113), channel_id=1, source_target_pairs={{0,4},{4,0},{8,12},{12,8},{1,5},{5,1},{9,13},{13,9},{2,6},{6,2},{1... | collective-permute-start | bytes 786440 | tf_op jit(solution)/shard_map/ppermute | solution.py:496
  145.5 10.3 %collective-permute-start.54 = (bf16[1,4,16,1024]{3,2,1,0:T(8,128)(2,1)S(1)}, bf16[1,4,16,1024]{3,2,1,0:T(8,128)(2,1)S(1)}, u32[]{:S(2)}, u32[]{:S(2)}) collective-permute-start(bf16[1,4,16,1024]{3,2,1,0:T(8,128)(2,1)S(1)} %fold.23.refs_2_), channel_id=1, source_target_pairs={{0,8},{4,12},{8,0},{12,4},{1,9},{5,13},{9,1},{13,5},{2,10},{6,14},... | collective-permute-start | bytes 393224 | tf_op jit(solution)/shard_map/ppermute | solution.py:496
  146.7 11.3 %collective-permute-start.53 = (bf16[1,4,16,1024]{3,2,1,0:T(8,128)(2,1)S(1)}, bf16[1,4,16,1024]{3,2,1,0:T(8,128)(2,1)S(1)}, u32[]{:S(2)}, u32[]{:S(2)}) collective-permute-start(bf16[1,4,16,1024]{3,2,1,0:T(8,128)(2,1)S(1)} %fold.22.refs_2_), channel_id=1, source_target_pairs={{0,8},{4,12},{8,0},{12,4},{1,9},{5,13},{9,1},{13,5},{2,10},{6,14},... | collective-permute-start | bytes 393224 | tf_op jit(solution)/shard_map/ppermute | solution.py:496
  160.5 12.7 %collective-permute-start.55 = (bf16[1,4,16,1024]{3,2,1,0:T(8,128)(2,1)S(1)}, bf16[1,4,16,1024]{3,2,1,0:T(8,128)(2,1)S(1)}, u32[]{:S(2)}, u32[]{:S(2)}) collective-permute-start(bf16[1,4,16,1024]{3,2,1,0:T(8,128)(2,1)S(1)} %fold.25), channel_id=1, source_target_pairs={{0,8},{4,12},{8,0},{12,4},{1,9},{5,13},{9,1},{13,5},{2,10},{6,14},... | collective-permute-start | bytes 393224 | tf_op jit(solution)/shard_map/ppermute | solution.py:496
  164.0 11.6 %collective-permute-start.51 = (bf16[1,4,16,1024]{3,2,1,0:T(8,128)(2,1)S(1)}, bf16[1,4,16,1024]{3,2,1,0:T(8,128)(2,1)S(1)}, u32[]{:S(2)}, u32[]{:S(2)}) collective-permute-start(bf16[1,4,16,1024]{3,2,1,0:T(8,128)(2,1)S(1)} %fold.24.refs_6_), channel_id=1, source_target_pairs={{0,8},{4,12},{8,0},{12,4},{1,9},{5,13},{9,1},{13,5},{2,10},{6,14},... | collective-permute-start | bytes 393224 | tf_op jit(solution)/shard_map/ppermute | solution.py:496
  (18 other events, 84.4 us)

commit v12 on v10

--- a/solution.py
+++ b/solution.py
@@ -355,12 +355,34 @@
     )(at, edges, query, rest, *sums, *others, *after)
 
 
-def gate_kernel(count, parts, *refs):
+def merge_kernel(width, *refs):
+    (m, n), (s, t) = (
+        [r[:4] if r.shape[0] == 8 else r[:, :4] for r in refs[:2]],
+        [r[4:] if r.shape[0] == 8 else r[:, 4:8] for r in refs[:2]],
+    )
+    mean, square = merge([m, n], [s, t], [width] * 2)
+    if refs[2].shape[0] == 8:
+        refs[2][:4], refs[2][4:] = mean, square
+    else:
+        lane = lax.broadcasted_iota(jnp.int32, refs[2].shape, 1)
+        refs[2][...] = jnp.where(lane < 4, mean[:, :1], square[:, :1])
+
+
+def merge_stats(stats, width):
+    return pl.pallas_call(
+        functools.partial(merge_kernel, width),
+        out_shape=jax.ShapeDtypeStruct(stats[0].shape, f32),
+        compiler_params=params(),
+        cost_estimate=LIGHT,
+        name="merge",
+    )(*stats)
+
+
+def gate_kernel(count, parts, width, *refs):
     stats, atts, rests, outs = (
         refs[:count], refs[count:count + parts],
         refs[count + parts:count + 2 * parts], refs[count + 2 * parts:],
     )
-    width = sum(a.shape[1] for a in atts)
     means, squares = stat_columns(stats)
     mean, square = merge(means, squares, [width] * count)
     scale = lax.rsqrt(square / (width * count) + EPSILON)
@@ -374,10 +396,10 @@
         column += span
 
 
-def gate_rows(stats, atts, rests, chunks):
+def gate_rows(stats, stat_width, atts, rests, chunks):
     rows, width = atts[0].shape[0], sum(a.shape[1] for a in atts)
     return pl.pallas_call(
-        functools.partial(gate_kernel, len(stats), len(atts)),
+        functools.partial(gate_kernel, len(stats), len(atts), stat_width),
         grid=(1,),
         in_specs=[pl.BlockSpec(s.shape, lambda j: (0, 0)) for s in stats]
         + [pl.BlockSpec((rows, a.shape[1]), lambda j: (0, 0)) for a in atts]
@@ -390,16 +412,16 @@
     )(*stats, *atts, *rests)
 
 
-def output_kernel(owners, after, order_ref, *refs):
+def output_kernel(owners, slots, after, index_ref, *refs):
     rows, w_ref, outs, lhs_ref = refs[:owners], refs[owners], refs[owners + 1 + after:-1], refs[-1]
     piece = rows[0].shape[1]
 
     @pl.when(pl.program_id(0) == 0)
     def _():
         first = 0
-        for k in range(rows[0].shape[0]):
+        for slot in slots:
             for p in range(owners):
-                lhs_ref[first:first + piece, :] = rows[p][order_ref[k]]
+                lhs_ref[first:first + piece, :] = rows[p][index_ref[0] ^ slot]
                 first += piece
 
     sums = jnp.dot(lhs_ref[...], w_ref[...], preferred_element_type=f32).astype(bf16)
@@ -411,13 +433,13 @@
                 first += piece
 
 
-def output(order, counts, blocks, w_out, column, columns, after):
+def output(index, slots, counts, blocks, w_out, column, columns, after):
     owners, (each, width), zs = len(blocks), blocks[0].shape, sum(counts)
     piece = each // zs
     span = max(c for c in (512, 256, columns) if columns % c == 0 and column % c == 0)
     row_spec = pl.BlockSpec((zs, piece, width), lambda j, at: (0, 0, 0))
     return pl.pallas_call(
-        functools.partial(output_kernel, owners, len(after)),
+        functools.partial(output_kernel, owners, slots, len(after)),
         grid_spec=pltpu.PrefetchScalarGridSpec(
             num_scalar_prefetch=1,
             grid=(columns // span,),
@@ -433,7 +455,10 @@
         compiler_params=params(),
         cost_estimate=LIGHT,
         name="output",
-    )(order, *[b.reshape(zs, piece, width) for b in blocks], far(w_out), *after)
+    )(
+        index.reshape(1).astype(jnp.int32),
+        *[b.reshape(zs, piece, width) for b in blocks], far(w_out), *after,
+    )
 
 
 def close_kernel(count, at_ref, t_ref, *refs):
@@ -507,17 +532,17 @@
     return blocks
 
 
-def shift(x, axis, k):
+def all_stats(stat, width, axis):
     count = lax.axis_size(axis)
-    return lax.ppermute(x, axis, [(i, (i + k) % count) for i in range(count)])
-
-
-def all_stats(stat, axis):
-    count = lax.axis_size(axis)
-    if count > 8:
+    if count > 8 or count & (count - 1):
         every = lax.all_gather(stat, axis)
-        return [every[i] for i in range(count)]
-    return [stat] + [shift(stat, axis, k) for k in range(1, count)]
+        return [every[i] for i in range(count)], width
+    stats = [stat]
+    for b in range(bits_of(axis)):
+        if b:
+            width, stats = 2 * width, [merge_stats(stats, width)]
+        stats.append(swap(stats[0], axis, b))
+    return stats, width
 
 
 def head_chunks(heads):
@@ -530,7 +555,7 @@
 GROUPS = [[0, 1], [2], [3], [4]]
 ORDER = [
     "P0", "P1", "F0", "P2", "F1", "P3", "F2", "A0", "F3", "P4", "A1", "F4", "T0", "G0", "A2",
-    "T1", "A3", "G1", "E0", "T2", "G2", "T3", "E1", "G3", "E2", "E3",
+    "T1", "A3", "G1", "T2", "E0", "G2", "T3", "G3", "E1", "E2", "E3",
 ]
 
 
@@ -599,7 +624,8 @@
 
     atts = [atts[c] for c in range(last + 1)]
     rests = [parts[c][1] for c in range(last + 1)]
-    gated = gate_rows(all_stats(stats[last], "head"), atts, rests, chunks)
+    every, stat_width = all_stats(stats[last], width, "head")
+    gated = gate_rows(every, stat_width, atts, rests, chunks)
     columns = w_out.shape[1]
     straight = piece % 16 == 0 and zs & (zs - 1) == 0
     out, last_out = None, []
@@ -611,14 +637,16 @@
             whole = lax.psum_scatter(whole, "head", scatter_dimension=0, tiled=True)
             out, _ = close(place, index, tokens, chunks, r, 0, [whole], out, [])
         return out.reshape(cand // zs, -1)
-    halved = index ^ reverse(jnp.arange(zs, dtype=jnp.int32), bits_of("head"))
+    slots = [reverse(k, bits_of("head")) for k in range(zs)]
     groups = 2 if columns % 1024 == 0 else 1
     span = columns // groups
     pieces, first_out, counts = [], [], [zs // 2] * 2 if zs > 1 else [1]
     for r, rows in enumerate(gated):
         blocks = gather(rows, "hist", first_out)
         for g in range(groups):
-            own, *others = output(halved, counts, blocks, w_out, g * span, span, last_out)
+            own, *others = output(
+                index, slots, counts, blocks, w_out, g * span, span, last_out
+            )
             pieces.append((r, g, own, [swap(x, "head", 0) for x in others]))
             last_out, first_out = [own], first_out or [own]
     closing, chain = [], last_out

time: 176 us -> 174 us (0.989)
  starting transfers between devices: 38.8 us -> 41.3 us
  waiting for transfers between devices: 47.9 us -> 45.9 us
  Pallas kernels: 85.3 us -> 83.4 us
    ppermute x53 -> x55, starting transfers between devices: 34.2 us -> 41.3 us  [swap(): lax.ppermute(x, axis, [(i, i ^ 1 << bit) for i in range(lax.axis_size(axi...]
    ppermute x3 -> x0, starting transfers between devices: 4.64 us -> none  [shift(): return lax.ppermute(x, axis, [(i, (i + k) % count) for i in range(count)])]
    ppermute x3 -> x0, waiting for transfers between devices: 4.39 us -> none  [shift(): return lax.ppermute(x, axis, [(i, (i + k) % count) for i in range(count)])]
    ppermute x53 -> x55, waiting for transfers between devices: 43.5 us -> 45.9 us  [swap(): lax.ppermute(x, axis, [(i, i ^ 1 << bit) for i in range(lax.axis_size(axi...]
    pallas_call x5 -> x6, Pallas kernels: 16.3 us -> 14.1 us  [the longest x4 13.7 us: output(): pl.pallas_call(functools.partial(output_kernel, owners, slots, len(after)...]
  transfers between devices with their start and end apart: 56 -> 55, of which waited for: 17 -> 13; matrix products, arithmetic and copies ran while one was open for 0% -> 0% of each run, Pallas kernels for 42% -> 43%
where the time goes in v12:
time: 174 us
  Pallas kernels  83.4 us (48%)
  waiting for transfers between devices  45.9 us (26%)
  starting transfers between devices  41.3 us (24%)
  local copies, waits for them, and re-layouts  2.43 us (1%)
    ppermute x55, waiting for transfers between devices, swap(): lax.ppermute(x, axis, [(i, i ^ 1 << bit) for i in range(lax.axis_size(axi...  45.9 us
    ppermute x55, starting transfers between devices, swap(): lax.ppermute(x, axis, [(i, i ^ 1 << bit) for i in range(lax.axis_size(axi...  41.3 us
    pallas_call x5, Pallas kernels, project(): pl.pallas_call(functools.partial(project_kernel, parts, owners, len(after...  37.9 us
    pallas_call x4, Pallas kernels, output(): pl.pallas_call(functools.partial(output_kernel, owners, slots, len(after)...  13.7 us
    pallas_call x4, Pallas kernels, attend(): pl.pallas_call(functools.partial(attend_kernel, owners, len(counts)), gri...  12.5 us
    pallas_call x4, Pallas kernels, close(): pl.pallas_call(functools.partial(close_kernel, len(terms)), grid_spec=plt...  8.68 us
    pallas_call x13, Pallas kernels, fold(): pl.pallas_call(functools.partial(fold_kernel, len(terms)), grid=(steps,),...  4.77 us
  transfers between devices with their start and end apart: 55, of which 13 were waited for; matrix products, arithmetic and copies ran while one was open for 0% of the time, Pallas kernels for 43%

profile of v12, /device:TPU:0, one launch (start us, length us, event | category | flops | bytes accessed | tf_op | source)
XLA Modules:
  0.0 173.8 jit_solution(12533630122517461555)
XLA Ops:
  0.0 5.5 %project.5 = (bf16[2,4,128,256]{3,2,1,0:T(8,128)(2,1)S(1)}, bf16[1,4,128,256]{3,2,1,0:T(8,128)(2,1)S(1)}, bf16[1,4,128,256]{3,2,1,0:T(8,128)(2,1)S(1)}) custom-call(s32[1]{0:T(128)} %bitcast.at_ref, bf16[4,2,4,16,2048]{4,3,2,1,0:T(8,128)(2,1)} %bitcast.57, bf16[4,2,4,16,2048]{4,3,2,1,0:T(8,128)(2,1)} %bitcast.58, bf16[4,2,4,16,2048]{4,3,2,1,0:T(8,128)(2,1)} %bitcast.59, ...), custom_call_target="tpu_custom_call" | custom-call | flops 1000 | bytes 1000 | tf_op jit(solution)/shard_map/project/pallas_call | solution.py:81
  6.1 8.7 %project.6 = (bf16[2,4,128,512]{3,2,1,0:T(8,128)(2,1)S(1)}, bf16[1,4,128,512]{3,2,1,0:T(8,128)(2,1)S(1)}, bf16[1,4,128,512]{3,2,1,0:T(8,128)(2,1)S(1)}) custom-call(s32[1]{0:T(128)} %bitcast.at_ref, bf16[4,2,4,16,2048]{4,3,2,1,0:T(8,128)(2,1)} %bitcast.61, bf16[4,2,4,16,2048]{4,3,2,1,0:T(8,128)(2,1)} %bitcast.62, bf16[4,2,4,16,2048]{4,3,2,1,0:T(8,128)(2,1)} %bitcast.63, ...), custom_call_target="tpu_custom_call" | custom-call | flops 1000 | bytes 1000 | tf_op jit(solution)/shard_map/project/pallas_call | solution.py:81
  15.8 3.0 %collective-permute-start.4 = (bf16[1,4,128,256]{3,2,1,0:T(8,128)(2,1)S(1)}, bf16[1,4,128,256]{3,2,1,0:T(8,128)(2,1)S(1)}, u32[]{:S(2)}, u32[]{:S(2)}) collective-permute-start(bf16[1,4,128,256]{3,2,1,0:T(8,128)(2,1)S(1)} %fold.13.refs_8_), channel_id=1, source_target_pairs={{0,2},{1,3},{2,0},{3,1},{4,6},{5,7},{6,4},{7,5},{8,10},{9,11},{10,... | collective-permute-start | bytes 786440 | tf_op jit(solution)/shard_map/ppermute | solution.py:513
  18.7 8.7 %project.7 = (bf16[2,4,128,512]{3,2,1,0:T(8,128)(2,1)S(1)}, bf16[1,4,128,512]{3,2,1,0:T(8,128)(2,1)S(1)}, bf16[1,4,128,512]{3,2,1,0:T(8,128)(2,1)S(1)}) custom-call(s32[1]{0:T(128)} %bitcast.at_ref, bf16[4,2,4,16,2048]{4,3,2,1,0:T(8,128)(2,1)} %bitcast.65, bf16[4,2,4,16,2048]{4,3,2,1,0:T(8,128)(2,1)} %bitcast.66, bf16[4,2,4,16,2048]{4,3,2,1,0:T(8,128)(2,1)} %bitcast.67, ...), custom_call_target="tpu_custom_call" | custom-call | flops 1000 | bytes 1000 | tf_op jit(solution)/shard_map/project/pallas_call | solution.py:81
  28.5 8.8 %project.8 = (bf16[2,4,128,512]{3,2,1,0:T(8,128)(2,1)S(1)}, bf16[1,4,128,512]{3,2,1,0:T(8,128)(2,1)S(1)}, bf16[1,4,128,512]{3,2,1,0:T(8,128)(2,1)S(1)}) custom-call(s32[1]{0:T(128)} %bitcast.at_ref, bf16[4,2,4,16,2048]{4,3,2,1,0:T(8,128)(2,1)} %bitcast.69, bf16[4,2,4,16,2048]{4,3,2,1,0:T(8,128)(2,1)} %bitcast.70, bf16[4,2,4,16,2048]{4,3,2,1,0:T(8,128)(2,1)} %bitcast.71, ...), custom_call_target="tpu_custom_call" | custom-call | flops 1000 | bytes 1000 | tf_op jit(solution)/shard_map/project/pallas_call | solution.py:81
  39.1 1.9 %collective-permute-start.12 = (bf16[1,4,128,512]{3,2,1,0:T(8,128)(2,1)}, bf16[1,4,128,512]{3,2,1,0:T(8,128)(2,1)}, u32[]{:S(2)}, u32[]{:S(2)}) collective-permute-start(bf16[1,4,128,512]{3,2,1,0:T(8,128)(2,1)} %fold.15.refs_6_), channel_id=1, source_target_pairs={{0,2},{1,3},{2,0},{3,1},{4,6},{5,7},{6,4},{7,5},{8,10},{9,11},{10,... | collective-permute-start | bytes 1572872 | tf_op jit(solution)/shard_map/ppermute | solution.py:513
  41.0 1.4 collective-permute-done.8.refs_5_
  43.2 1.0 fold.16.refs_8_
  44.2 1.7 %collective-permute-start.17 = (bf16[1,4,128,512]{3,2,1,0:T(8,128)(2,1)}, bf16[1,4,128,512]{3,2,1,0:T(8,128)(2,1)}, u32[]{:S(2)}, u32[]{:S(2)}) collective-permute-start(bf16[1,4,128,512]{3,2,1,0:T(8,128)(2,1)} %fold.16.refs_8_), channel_id=1, source_target_pairs={{0,2},{1,3},{2,0},{3,1},{4,6},{5,7},{6,4},{7,5},{8,10},{9,11},{10,... | collective-permute-start | bytes 1572872 | tf_op jit(solution)/shard_map/ppermute | solution.py:513
  46.0 6.2 %project.9 = (bf16[2,4,128,256]{3,2,1,0:T(8,128)(2,1)S(1)}, bf16[1,4,128,256]{3,2,1,0:T(8,128)(2,1)S(1)}, bf16[1,4,128,256]{3,2,1,0:T(8,128)(2,1)}) custom-call(s32[1]{0:T(128)} %bitcast.at_ref, bf16[4,2,4,16,2048]{4,3,2,1,0:T(8,128)(2,1)} %bitcast.73, bf16[4,2,4,16,2048]{4,3,2,1,0:T(8,128)(2,1)} %bitcast.74, bf16[4,2,4,16,2048]{4,3,2,1,0:T(8,128)(2,1)} %bitcast.75, ...), custom_call_target="tpu_custom_call" | custom-call | flops 1000 | bytes 1000 | tf_op jit(solution)/shard_map/project/pallas_call | solution.py:81
  53.4 5.0 %collective-permute-done.18.refs_1_ = bf16[128,768]{1,0:T(8,128)(2,1)S(1)} collective-permute-done((bf16[128,768]{1,0:T(8,128)(2,1)S(1)}, bf16[128,768]{1,0:T(8,128)(2,1)S(1)}, u32[]{:S(2)}, u32[]{:S(2)}) %collective-permute-start.18) | collective-permute-done | bytes 196640 | tf_op jit(solution)/shard_map/ppermute | solution.py:513
  58.5 1.0 copy-done.3
  59.6 1.4 activate.5
  61.0 1.1 fold.17.refs_10_
  62.1 4.1 %attend.4 = (bf16[2,128,768]{2,1,0:T(8,128)(2,1)S(1)}, bf16[1,128,768]{2,1,0:T(8,128)(2,1)S(1)}, bf16[1,128,768]{2,1,0:T(8,128)(2,1)S(1)}) custom-call(s32[1]{0:T(128)} %bitcast.at_ref, bf16[128,768]{1,0:T(8,128)(2,1)S(1)} %get-tuple-element.75.refs_2_.refs_0_.q_ref, bf16[128,768]{1,0:T(8,128)(2,1)S(1)} %collective-permute-done.18.refs_1_, ...), custom_call_target="tpu_custom_call" | custom-call | flops 1000 | bytes 1000 | tf_op jit(solution)/shard_map/attend/pallas_call | solution.py:263
  66.7 1.8 %collective-permute-start.14 = (bf16[128,512]{1,0:T(8,128)(2,1)S(1)}, bf16[128,512]{1,0:T(8,128)(2,1)S(1)}, u32[]{:S(2)}, u32[]{:S(2)}) collective-permute-start(bf16[128,512]{1,0:T(8,128)(2,1)S(1)} %get-tuple-element.80.refs_2_.refs_0_.q_ref), channel_id=1, source_target_pairs={{0,2},{1,3},{2,0},{3,1},{4,6},{5,7},{6,4},{7,5},{8,10},{9,11},{10,... | collective-permute-start | bytes 393224 | tf_op jit(solution)/shard_map/ppermute | solution.py:513
  68.8 4.0 %collective-permute-done.14.refs_1_ = bf16[128,512]{1,0:T(8,128)(2,1)S(1)} collective-permute-done((bf16[128,512]{1,0:T(8,128)(2,1)S(1)}, bf16[128,512]{1,0:T(8,128)(2,1)S(1)}, u32[]{:S(2)}, u32[]{:S(2)}) %collective-permute-start.14) | collective-permute-done | bytes 131104 | tf_op jit(solution)/shard_map/ppermute | solution.py:513
  73.6 1.4 activate.6
  74.9 2.1 %collective-permute-start.25 = (bf16[128,512]{1,0:T(8,128)(2,1)S(1)}, bf16[128,512]{1,0:T(8,128)(2,1)S(1)}, u32[]{:S(2)}, u32[]{:S(2)}) collective-permute-start(bf16[128,512]{1,0:T(8,128)(2,1)S(1)} %get-tuple-element.83.refs_10_.refs_0_.q_ref), channel_id=1, source_target_pairs={{0,2},{1,3},{2,0},{3,1},{4,6},{5,7},{6,4},{7,5},{8,10},{9,11},{10,... | collective-permute-start | bytes 393224 | tf_op jit(solution)/shard_map/ppermute | solution.py:513
  77.0 3.1 %attend.5 = (bf16[2,128,512]{2,1,0:T(8,128)(2,1)S(1)}, bf16[1,128,512]{2,1,0:T(8,128)(2,1)S(1)}, bf16[1,128,512]{2,1,0:T(8,128)(2,1)S(1)}) custom-call(s32[1]{0:T(128)} %bitcast.at_ref, bf16[128,512]{1,0:T(8,128)(2,1)S(1)} %get-tuple-element.80.refs_2_.refs_0_.q_ref, bf16[128,512]{1,0:T(8,128)(2,1)S(1)} %collective-permute-done.14.refs_1_, ...), custom_call_target="tpu_custom_call" | custom-call | flops 1000 | bytes 1000 | tf_op jit(solution)/shard_map/attend/pallas_call | solution.py:263
  81.3 1.7 collective-permute-start.31
  83.3 3.2 %attend.6 = (bf16[2,128,512]{2,1,0:T(8,128)(2,1)S(1)}, bf16[1,128,512]{2,1,0:T(8,128)(2,1)S(1)}, bf16[1,128,512]{2,1,0:T(8,128)(2,1)S(1)}) custom-call(s32[1]{0:T(128)} %bitcast.at_ref, bf16[128,512]{1,0:T(8,128)(2,1)S(1)} %get-tuple-element.83.refs_10_.refs_0_.q_ref, bf16[128,512]{1,0:T(8,128)(2,1)S(1)} %collective-permute-done.25.refs_1_, ...), custom_call_target="tpu_custom_call" | custom-call | flops 1000 | bytes 1000 | tf_op jit(solution)/shard_map/attend/pallas_call | solution.py:263
  87.2 3.9 %collective-permute-done.22.refs_1_ = bf16[128,256]{1,0:T(8,128)(2,1)S(1)} collective-permute-done((bf16[128,256]{1,0:T(8,128)(2,1)S(1)}, bf16[128,256]{1,0:T(8,128)(2,1)S(1)}, u32[]{:S(2)}, u32[]{:S(2)}) %collective-permute-start.22) | collective-permute-done | bytes 65568 | tf_op jit(solution)/shard_map/ppermute | solution.py:513
  92.8 2.0 %attend.7 = (bf16[2,128,256]{2,1,0:T(8,128)(2,1)S(1)}, bf16[1,128,256]{2,1,0:T(8,128)(2,1)S(1)}, bf16[1,128,256]{2,1,0:T(8,128)(2,1)S(1)}) custom-call(s32[1]{0:T(128)} %bitcast.at_ref, bf16[128,256]{1,0:T(8,128)(2,1)S(1)} %get-tuple-element.85.refs_2_.refs_0_.q_ref, bf16[128,256]{1,0:T(8,128)(2,1)S(1)} %collective-permute-done.22.refs_1_, ...), custom_call_target="tpu_custom_call" | custom-call | flops 1000 | bytes 1000 | tf_op jit(solution)/shard_map/attend/pallas_call | solution.py:263
  95.4 1.7 collective-permute-start.38
  98.8 2.3 %collective-permute-done.38.refs_2_ = bf16[1,128,512]{2,1,0:T(8,128)(2,1)S(1)} collective-permute-done((bf16[1,128,512]{2,1,0:T(8,128)(2,1)S(1)}, bf16[1,128,512]{2,1,0:T(8,128)(2,1)S(1)}, u32[]{:S(2)}, u32[]{:S(2)}) %collective-permute-start.38) | collective-permute-done | bytes 131104 | tf_op jit(solution)/shard_map/ppermute | solution.py:513
  102.7 1.8 %collective-permute-start.39 = (f32[8,128]{1,0:T(8,128)S(1)}, f32[8,128]{1,0:T(8,128)S(1)}, u32[]{:S(2)}, u32[]{:S(2)}) collective-permute-start(f32[8,128]{1,0:T(8,128)S(1)} %get-tuple-element.105.refs_0_), channel_id=1, source_target_pairs={{0,4},{4,0},{8,12},{12,8},{1,5},{5,1},{9,13},{13,9},{2,6},{6,2},{1... | collective-permute-start | bytes 12296 | tf_op jit(solution)/shard_map/ppermute | solution.py:513
  104.5 1.9 %collective-permute-done.39.refs_1_ = f32[8,128]{1,0:T(8,128)S(1)} collective-permute-done((f32[8,128]{1,0:T(8,128)S(1)}, f32[8,128]{1,0:T(8,128)S(1)}, u32[]{:S(2)}, u32[]{:S(2)}) %collective-permute-start.39) | collective-permute-done | bytes 4128 | tf_op jit(solution)/shard_map/ppermute | solution.py:513
  106.4 2.8 %collective-permute-start.40 = (f32[8,128]{1,0:T(8,128)S(1)}, f32[8,128]{1,0:T(8,128)S(1)}, u32[]{:S(2)}, u32[]{:S(2)}) collective-permute-start(f32[8,128]{1,0:T(8,128)S(1)} %merge.1.refs_0_), channel_id=1, source_target_pairs={{0,8},{4,12},{8,0},{12,4},{1,9},{5,13},{9,1},{13,5},{2,10},{6,14},... | collective-permute-start | bytes 12296 | tf_op jit(solution)/shard_map/ppermute | solution.py:513
  109.2 1.7 %collective-permute-done.40.refs_1_ = f32[8,128]{1,0:T(8,128)S(1)} collective-permute-done((f32[8,128]{1,0:T(8,128)S(1)}, f32[8,128]{1,0:T(8,128)S(1)}, u32[]{:S(2)}, u32[]{:S(2)}) %collective-permute-start.40) | collective-permute-done | bytes 4128 | tf_op jit(solution)/shard_map/ppermute | solution.py:513
  111.3 1.7 collective-permute-start.42
  113.0 4.7 %collective-permute-done.42 = bf16[64,2048]{1,0:T(8,128)(2,1)S(1)} collective-permute-done((bf16[64,2048]{1,0:T(8,128)(2,1)S(1)}, bf16[64,2048]{1,0:T(8,128)(2,1)S(1)}, u32[]{:S(2)}, u32[]{:S(2)}) %collective-permute-start.42) | collective-permute-done | bytes 262176 | tf_op jit(solution)/shard_map/ppermute | solution.py:513
  117.7 1.7 collective-permute-start.41
  119.6 3.4 %output.4 = (bf16[2,4,16,1024]{3,2,1,0:T(8,128)(2,1)S(1)}, bf16[2,4,16,1024]{3,2,1,0:T(8,128)(2,1)S(1)}) custom-call(s32[1]{0:T(128)} %bitcast.3.index_ref, bf16[4,16,2048]{2,1,0:T(8,128)(2,1)S(1)} %bitcast.43, bf16[4,16,2048]{2,1,0:T(8,128)(2,1)S(1)} %bitcast.45, bf16[4,16,2048]{2,1,0:T(8,128)(2,1)S(1)} %bitcast.49, bf16[4,16,2048]{2,1,0:T(8,128)(2,1)S(1)} %bitcast.51, ...), custom_call_target="tpu_custom_call" | custom-call | flops 1000 | bytes 1000 | tf_op jit(solution)/shard_map/output/pallas_call | solution.py:441
  123.1 3.4 %collective-permute-done.41.refs_0_ = bf16[64,2048]{1,0:T(8,128)(2,1)S(1)} collective-permute-done((bf16[64,2048]{1,0:T(8,128)(2,1)S(1)}, bf16[64,2048]{1,0:T(8,128)(2,1)S(1)}, u32[]{:S(2)}, u32[]{:S(2)}) %collective-permute-start.41) | collective-permute-done | bytes 262176 | tf_op jit(solution)/shard_map/ppermute | solution.py:513
  126.5 1.7 %collective-permute-start.49 = (bf16[2,4,16,1024]{3,2,1,0:T(8,128)(2,1)S(1)}, bf16[2,4,16,1024]{3,2,1,0:T(8,128)(2,1)S(1)}, u32[]{:S(2)}, u32[]{:S(2)}) collective-permute-start(bf16[2,4,16,1024]{3,2,1,0:T(8,128)(2,1)S(1)} %get-tuple-element.115), channel_id=1, source_target_pairs={{0,4},{4,0},{8,12},{12,8},{1,5},{5,1},{9,13},{13,9},{2,6},{6,2},{1... | collective-permute-start | bytes 786440 | tf_op jit(solution)/shard_map/ppermute | solution.py:513
  128.2 3.4 %output.5 = (bf16[2,4,16,1024]{3,2,1,0:T(8,128)(2,1)S(1)}, bf16[2,4,16,1024]{3,2,1,0:T(8,128)(2,1)S(1)}) custom-call(s32[1]{0:T(128)} %bitcast.3.index_ref, bf16[4,16,2048]{2,1,0:T(8,128)(2,1)S(1)} %bitcast.44, bf16[4,16,2048]{2,1,0:T(8,128)(2,1)S(1)} %bitcast.46, bf16[4,16,2048]{2,1,0:T(8,128)(2,1)S(1)} %bitcast.50, bf16[4,16,2048]{2,1,0:T(8,128)(2,1)S(1)} %bitcast.52, ...), custom_call_target="tpu_custom_call" | custom-call | flops 1000 | bytes 1000 | tf_op jit(solution)/shard_map/output/pallas_call | solution.py:441
  132.0 3.4 %output.6 = (bf16[2,4,16,1024]{3,2,1,0:T(8,128)(2,1)S(1)}, bf16[2,4,16,1024]{3,2,1,0:T(8,128)(2,1)S(1)}) custom-call(s32[1]{0:T(128)} %bitcast.3.index_ref, bf16[4,16,2048]{2,1,0:T(8,128)(2,1)S(1)} %bitcast.41, bf16[4,16,2048]{2,1,0:T(8,128)(2,1)S(1)} %bitcast.39, bf16[4,16,2048]{2,1,0:T(8,128)(2,1)S(1)} %bitcast.47, bf16[4,16,2048]{2,1,0:T(8,128)(2,1)S(1)} %bitcast.53, ...), custom_call_target="tpu_custom_call" | custom-call | flops 1000 | bytes 1000 | tf_op jit(solution)/shard_map/output/pallas_call | solution.py:441
  135.4 1.8 %collective-permute-start.52 = (bf16[2,4,16,1024]{3,2,1,0:T(8,128)(2,1)S(1)}, bf16[2,4,16,1024]{3,2,1,0:T(8,128)(2,1)S(1)}, u32[]{:S(2)}, u32[]{:S(2)}) collective-permute-start(bf16[2,4,16,1024]{3,2,1,0:T(8,128)(2,1)S(1)} %get-tuple-element.117), channel_id=1, source_target_pairs={{0,4},{4,0},{8,12},{12,8},{1,5},{5,1},{9,13},{13,9},{2,6},{6,2},{1... | collective-permute-start | bytes 786440 | tf_op jit(solution)/shard_map/ppermute | solution.py:513
  137.2 3.4 %output.7 = (bf16[2,4,16,1024]{3,2,1,0:T(8,128)(2,1)S(1)}, bf16[2,4,16,1024]{3,2,1,0:T(8,128)(2,1)S(1)}) custom-call(s32[1]{0:T(128)} %bitcast.3.index_ref, bf16[4,16,2048]{2,1,0:T(8,128)(2,1)S(1)} %bitcast.42, bf16[4,16,2048]{2,1,0:T(8,128)(2,1)S(1)} %bitcast.40, bf16[4,16,2048]{2,1,0:T(8,128)(2,1)S(1)} %bitcast.48, bf16[4,16,2048]{2,1,0:T(8,128)(2,1)S(1)} %bitcast.54, ...), custom_call_target="tpu_custom_call" | custom-call | flops 1000 | bytes 1000 | tf_op jit(solution)/shard_map/output/pallas_call | solution.py:441
  141.2 2.8 %collective-permute-start.51 = (bf16[1,4,16,1024]{3,2,1,0:T(8,128)(2,1)S(1)}, bf16[1,4,16,1024]{3,2,1,0:T(8,128)(2,1)S(1)}, u32[]{:S(2)}, u32[]{:S(2)}) collective-permute-start(bf16[1,4,16,1024]{3,2,1,0:T(8,128)(2,1)S(1)} %fold.22.refs_2_), channel_id=1, source_target_pairs={{0,8},{4,12},{8,0},{12,4},{1,9},{5,13},{9,1},{13,5},{2,10},{6,14},... | collective-permute-start | bytes 393224 | tf_op jit(solution)/shard_map/ppermute | solution.py:513
  144.4 10.1 %collective-permute-done.51.refs_2_ = bf16[1,4,16,1024]{3,2,1,0:T(8,128)(2,1)S(1)} collective-permute-done((bf16[1,4,16,1024]{3,2,1,0:T(8,128)(2,1)S(1)}, bf16[1,4,16,1024]{3,2,1,0:T(8,128)(2,1)S(1)}, u32[]{:S(2)}, u32[]{:S(2)}) %collective-permute-start.51) | collective-permute-done | bytes 131104 | tf_op jit(solution)/shard_map/ppermute | solution.py:513
  154.5 2.2 %close.4 = (bf16[8,16,2048]{2,1,0:T(8,128)(2,1)}, f32[8,128]{1,0:T(8,128)S(1)}) custom-call(s32[2]{0:T(128)S(1)} %pad_add_fusion.1.at_ref, bf16[32,16,2048]{2,1,0:T(8,128)(2,1)} %bitcast.77, bf16[2,4,16,1024]{3,2,1,0:T(8,128)(2,1)S(1)} %get-tuple-element.109.refs_1_.refs_5_.refs_0_, bf16[2,4,16,1024]{3,2,1,0:T(8,128)(2,1)S(1)} %collective-permute-done.49.refs_1_, ...), custom_call_target="tpu_custom_call" | custom-call | flops 1000 | bytes 4000000 | tf_op jit(solution)/shard_map/close/pallas_call | solution.py:478
  156.8 3.4 %collective-permute-start.54 = (bf16[1,4,16,1024]{3,2,1,0:T(8,128)(2,1)S(1)}, bf16[1,4,16,1024]{3,2,1,0:T(8,128)(2,1)S(1)}, u32[]{:S(2)}, u32[]{:S(2)}) collective-permute-start(bf16[1,4,16,1024]{3,2,1,0:T(8,128)(2,1)S(1)} %fold.24.refs_4_), channel_id=1, source_target_pairs={{0,8},{4,12},{8,0},{12,4},{1,9},{5,13},{9,1},{13,5},{2,10},{6,14},... | collective-permute-start | bytes 393224 | tf_op jit(solution)/shard_map/ppermute | solution.py:513
  160.2 2.2 %close.5 = (bf16[8,16,2048]{2,1,0:T(8,128)(2,1)}, f32[8,128]{1,0:T(8,128)S(1)}) custom-call(s32[2]{0:T(128)S(1)} %pad_add_fusion.1.at_ref, bf16[32,16,2048]{2,1,0:T(8,128)(2,1)} %bitcast.78, bf16[2,4,16,1024]{3,2,1,0:T(8,128)(2,1)S(1)} %get-tuple-element.110.refs_5_.refs_0_, ...), custom_call_target="tpu_custom_call", output_to_operand_aliasing={{0}: (5, {})} | custom-call | flops 1000 | bytes 4000000 | tf_op jit(solution)/shard_map/close/pallas_call | solution.py:478
  162.7 6.4 %collective-permute-done.54.refs_2_ = bf16[1,4,16,1024]{3,2,1,0:T(8,128)(2,1)S(1)} collective-permute-done((bf16[1,4,16,1024]{3,2,1,0:T(8,128)(2,1)S(1)}, bf16[1,4,16,1024]{3,2,1,0:T(8,128)(2,1)S(1)}, u32[]{:S(2)}, u32[]{:S(2)}) %collective-permute-start.54) | collective-permute-done | bytes 131104 | tf_op jit(solution)/shard_map/ppermute | solution.py:513
  169.2 2.2 %close.6 = (bf16[8,16,2048]{2,1,0:T(8,128)(2,1)}, f32[8,128]{1,0:T(8,128)}) custom-call(s32[2]{0:T(128)S(1)} %pad_add_fusion.at_ref, bf16[32,16,2048]{2,1,0:T(8,128)(2,1)} %bitcast.79, bf16[2,4,16,1024]{3,2,1,0:T(8,128)(2,1)S(1)} %get-tuple-element.111.refs_5_.refs_0_, ...), custom_call_target="tpu_custom_call", output_to_operand_aliasing={{0}: (5, {})} | custom-call | flops 1000 | bytes 4000000 | tf_op jit(solution)/shard_map/close/pallas_call | solution.py:478
  171.7 2.2 %close.7 = (bf16[8,16,2048]{2,1,0:T(8,128)(2,1)}, f32[8,128]{1,0:T(8,128)}) custom-call(s32[2]{0:T(128)S(1)} %pad_add_fusion.at_ref, bf16[32,16,2048]{2,1,0:T(8,128)(2,1)} %bitcast.80, bf16[2,4,16,1024]{3,2,1,0:T(8,128)(2,1)S(1)} %get-tuple-element.112.refs_2_.refs_0_, ...), custom_call_target="tpu_custom_call", output_to_operand_aliasing={{0}: (5, {})} | custom-call | flops 1000 | bytes 4000000 | tf_op jit(solution)/shard_map/close/pallas_call | solution.py:478
  (134 shorter events, 18.3 us)
Async XLA Ops:
  5.5 9.4 %collective-permute-start = (bf16[1,4,128,256]{3,2,1,0:T(8,128)(2,1)S(1)}, bf16[1,4,128,256]{3,2,1,0:T(8,128)(2,1)S(1)}, u32[]{:S(2)}, u32[]{:S(2)}) collective-permute-start(bf16[1,4,128,256]{3,2,1,0:T(8,128)(2,1)S(1)} %get-tuple-element.67), channel_id=1, source_target_pairs={{0,1},{1,0},{2,3},{3,2},{4,5},{5,4},{6,7},{7,6},{8,9},{9,8},{10,11... | collective-permute-start | bytes 786440 | tf_op jit(solution)/shard_map/ppermute | solution.py:513
  6.1 8.8 %collective-permute-start.1 = (bf16[1,4,128,256]{3,2,1,0:T(8,128)(2,1)S(1)}, bf16[1,4,128,256]{3,2,1,0:T(8,128)(2,1)S(1)}, u32[]{:S(2)}, u32[]{:S(2)}) collective-permute-start(bf16[1,4,128,256]{3,2,1,0:T(8,128)(2,1)S(1)} %get-tuple-element.68), channel_id=1, source_target_pairs={{0,1},{1,0},{2,3},{3,2},{4,5},{5,4},{6,7},{7,6},{8,9},{9,8},{10,11... | collective-permute-start | bytes 786440 | tf_op jit(solution)/shard_map/ppermute | solution.py:513
  14.9 12.6 %collective-permute-start.3 = (bf16[1,4,128,512]{3,2,1,0:T(8,128)(2,1)S(1)}, bf16[1,4,128,512]{3,2,1,0:T(8,128)(2,1)S(1)}, u32[]{:S(2)}, u32[]{:S(2)}) collective-permute-start(bf16[1,4,128,512]{3,2,1,0:T(8,128)(2,1)S(1)} %tie.10), channel_id=1, source_target_pairs={{0,1},{1,0},{2,3},{3,2},{4,5},{5,4},{6,7},{7,6},{8,9},{9,8},{10,11... | collective-permute-start | bytes 1572872 | tf_op jit(solution)/shard_map/ppermute | solution.py:513
  15.4 12.1 %collective-permute-start.2 = (bf16[1,4,128,512]{3,2,1,0:T(8,128)(2,1)S(1)}, bf16[1,4,128,512]{3,2,1,0:T(8,128)(2,1)S(1)}, u32[]{:S(2)}, u32[]{:S(2)}) collective-permute-start(bf16[1,4,128,512]{3,2,1,0:T(8,128)(2,1)S(1)} %tie.9), channel_id=1, source_target_pairs={{0,1},{1,0},{2,3},{3,2},{4,5},{5,4},{6,7},{7,6},{8,9},{9,8},{10,11... | collective-permute-start | bytes 1572872 | tf_op jit(solution)/shard_map/ppermute | solution.py:513
  15.8 11.7 %collective-permute-start.4 = (bf16[1,4,128,256]{3,2,1,0:T(8,128)(2,1)S(1)}, bf16[1,4,128,256]{3,2,1,0:T(8,128)(2,1)S(1)}, u32[]{:S(2)}, u32[]{:S(2)}) collective-permute-start(bf16[1,4,128,256]{3,2,1,0:T(8,128)(2,1)S(1)} %fold.13.refs_8_), channel_id=1, source_target_pairs={{0,2},{1,3},{2,0},{3,1},{4,6},{5,7},{6,4},{7,5},{8,10},{9,11},{10,... | collective-permute-start | bytes 786440 | tf_op jit(solution)/shard_map/ppermute | solution.py:513
  27.5 9.8 %collective-permute-start.6 = (bf16[1,4,128,512]{3,2,1,0:T(8,128)(2,1)S(1)}, bf16[1,4,128,512]{3,2,1,0:T(8,128)(2,1)S(1)}, u32[]{:S(2)}, u32[]{:S(2)}) collective-permute-start(bf16[1,4,128,512]{3,2,1,0:T(8,128)(2,1)S(1)} %tie.12), channel_id=1, source_target_pairs={{0,1},{1,0},{2,3},{3,2},{4,5},{5,4},{6,7},{7,6},{8,9},{9,8},{10,11... | collective-permute-start | bytes 1572872 | tf_op jit(solution)/shard_map/ppermute | solution.py:513
  27.6 9.7 %collective-permute-start.5 = (bf16[1,4,128,512]{3,2,1,0:T(8,128)(2,1)S(1)}, bf16[1,4,128,512]{3,2,1,0:T(8,128)(2,1)S(1)}, u32[]{:S(2)}, u32[]{:S(2)}) collective-permute-start(bf16[1,4,128,512]{3,2,1,0:T(8,128)(2,1)S(1)} %tie.11), channel_id=1, source_target_pairs={{0,1},{1,0},{2,3},{3,2},{4,5},{5,4},{6,7},{7,6},{8,9},{9,8},{10,11... | collective-permute-start | bytes 1572872 | tf_op jit(solution)/shard_map/ppermute | solution.py:513
  28.4 14.0 %collective-permute-start.8 = (bf16[1,4,128,512]{3,2,1,0:T(8,128)(2,1)S(1)}, bf16[1,4,128,512]{3,2,1,0:T(8,128)(2,1)S(1)}, u32[]{:S(2)}, u32[]{:S(2)}) collective-permute-start(bf16[1,4,128,512]{3,2,1,0:T(8,128)(2,1)S(1)} %fold.14.refs_8_), channel_id=1, source_target_pairs={{0,2},{1,3},{2,0},{3,1},{4,6},{5,7},{6,4},{7,5},{8,10},{9,11},{10,... | collective-permute-start | bytes 1572872 | tf_op jit(solution)/shard_map/ppermute | solution.py:513
  37.3 5.9 %collective-permute-start.7 = (bf16[1,4,128,512]{3,2,1,0:T(8,128)(2,1)S(1)}, bf16[1,4,128,512]{3,2,1,0:T(8,128)(2,1)S(1)}, u32[]{:S(2)}, u32[]{:S(2)}) collective-permute-start(bf16[1,4,128,512]{3,2,1,0:T(8,128)(2,1)S(1)} %tie.13), channel_id=1, source_target_pairs={{0,1},{1,0},{2,3},{3,2},{4,5},{5,4},{6,7},{7,6},{8,9},{9,8},{10,11... | collective-permute-start | bytes 1572872 | tf_op jit(solution)/shard_map/ppermute | solution.py:513
  38.1 14.7 %collective-permute-start.9 = (bf16[1,4,128,512]{3,2,1,0:T(8,128)(2,1)S(1)}, bf16[1,4,128,512]{3,2,1,0:T(8,128)(2,1)S(1)}, u32[]{:S(2)}, u32[]{:S(2)}) collective-permute-start(bf16[1,4,128,512]{3,2,1,0:T(8,128)(2,1)S(1)} %tie.14), channel_id=1, source_target_pairs={{0,1},{1,0},{2,3},{3,2},{4,5},{5,4},{6,7},{7,6},{8,9},{9,8},{10,11... | collective-permute-start | bytes 1572872 | tf_op jit(solution)/shard_map/ppermute | solution.py:513
  39.1 19.4 %collective-permute-start.12 = (bf16[1,4,128,512]{3,2,1,0:T(8,128)(2,1)}, bf16[1,4,128,512]{3,2,1,0:T(8,128)(2,1)}, u32[]{:S(2)}, u32[]{:S(2)}) collective-permute-start(bf16[1,4,128,512]{3,2,1,0:T(8,128)(2,1)} %fold.15.refs_6_), channel_id=1, source_target_pairs={{0,2},{1,3},{2,0},{3,1},{4,6},{5,7},{6,4},{7,5},{8,10},{9,11},{10,... | collective-permute-start | bytes 1572872 | tf_op jit(solution)/shard_map/ppermute | solution.py:513
  42.9 15.5 %collective-permute-start.18 = (bf16[128,768]{1,0:T(8,128)(2,1)S(1)}, bf16[128,768]{1,0:T(8,128)(2,1)S(1)}, u32[]{:S(2)}, u32[]{:S(2)}) collective-permute-start(bf16[128,768]{1,0:T(8,128)(2,1)S(1)} %get-tuple-element.75.refs_2_.refs_0_.q_ref), channel_id=1, source_target_pairs={{0,2},{1,3},{2,0},{3,1},{4,6},{5,7},{6,4},{7,5},{8,10},{9,11},{10,... | collective-permute-start | bytes 589832 | tf_op jit(solution)/shard_map/ppermute | solution.py:513
  44.2 29.3 %collective-permute-start.17 = (bf16[1,4,128,512]{3,2,1,0:T(8,128)(2,1)}, bf16[1,4,128,512]{3,2,1,0:T(8,128)(2,1)}, u32[]{:S(2)}, u32[]{:S(2)}) collective-permute-start(bf16[1,4,128,512]{3,2,1,0:T(8,128)(2,1)} %fold.16.refs_8_), channel_id=1, source_target_pairs={{0,2},{1,3},{2,0},{3,1},{4,6},{5,7},{6,4},{7,5},{8,10},{9,11},{10,... | collective-permute-start | bytes 1572872 | tf_op jit(solution)/shard_map/ppermute | solution.py:513
  52.8 8.1 %collective-permute-start.11 = (bf16[1,4,128,256]{3,2,1,0:T(8,128)(2,1)}, bf16[1,4,128,256]{3,2,1,0:T(8,128)(2,1)}, u32[]{:S(2)}, u32[]{:S(2)}) collective-permute-start(bf16[1,4,128,256]{3,2,1,0:T(8,128)(2,1)} %tie.16), channel_id=1, source_target_pairs={{0,1},{1,0},{2,3},{3,2},{4,5},{5,4},{6,7},{7,6},{8,9},{9,8},{10,11... | collective-permute-start | bytes 786440 | tf_op jit(solution)/shard_map/ppermute | solution.py:513
  52.8 9.2 %collective-permute-start.19 = (bf16[128,768]{1,0:T(8,128)(2,1)S(1)}, bf16[128,768]{1,0:T(8,128)(2,1)}, u32[]{:S(2)}, u32[]{:S(2)}) collective-permute-start(bf16[128,768]{1,0:T(8,128)(2,1)S(1)} %get-tuple-element.75.refs_2_.refs_0_.q_ref), channel_id=1, source_target_pairs={{0,1},{1,0},{2,3},{3,2},{4,5},{5,4},{6,7},{7,6},{8,9},{9,8},{10,11... | collective-permute-start | bytes 589832 | tf_op jit(solution)/shard_map/ppermute | solution.py:513
  58.4 3.7 %collective-permute-start.20 = (bf16[128,768]{1,0:T(8,128)(2,1)S(1)}, bf16[128,768]{1,0:T(8,128)(2,1)}, u32[]{:S(2)}, u32[]{:S(2)}) collective-permute-start(bf16[128,768]{1,0:T(8,128)(2,1)S(1)} %collective-permute-done.18.refs_1_), channel_id=1, source_target_pairs={{0,1},{1,0},{2,3},{3,2},{4,5},{5,4},{6,7},{7,6},{8,9},{9,8},{10,11... | collective-permute-start | bytes 589832 | tf_op jit(solution)/shard_map/ppermute | solution.py:513
  66.2 6.7 %collective-permute-start.21 = (bf16[1,128,768]{2,1,0:T(8,128)(2,1)S(1)}, bf16[1,128,768]{2,1,0:T(8,128)(2,1)S(1)}, u32[]{:S(2)}, u32[]{:S(2)}) collective-permute-start(bf16[1,128,768]{2,1,0:T(8,128)(2,1)S(1)} %get-tuple-element.82), channel_id=1, source_target_pairs={{0,1},{1,0},{2,3},{3,2},{4,5},{5,4},{6,7},{7,6},{8,9},{9,8},{10,11... | collective-permute-start | bytes 589832 | tf_op jit(solution)/shard_map/ppermute | solution.py:513
  66.7 6.1 %collective-permute-start.14 = (bf16[128,512]{1,0:T(8,128)(2,1)S(1)}, bf16[128,512]{1,0:T(8,128)(2,1)S(1)}, u32[]{:S(2)}, u32[]{:S(2)}) collective-permute-start(bf16[128,512]{1,0:T(8,128)(2,1)S(1)} %get-tuple-element.80.refs_2_.refs_0_.q_ref), channel_id=1, source_target_pairs={{0,2},{1,3},{2,0},{3,1},{4,6},{5,7},{6,4},{7,5},{8,10},{9,11},{10,... | collective-permute-start | bytes 393224 | tf_op jit(solution)/shard_map/ppermute | solution.py:513
  68.5 12.3 %collective-permute-start.10 = (bf16[1,4,128,256]{3,2,1,0:T(8,128)(2,1)S(1)}, bf16[1,4,128,256]{3,2,1,0:T(8,128)(2,1)S(1)}, u32[]{:S(2)}, u32[]{:S(2)}) collective-permute-start(bf16[1,4,128,256]{3,2,1,0:T(8,128)(2,1)S(1)} %tie.15), channel_id=1, source_target_pairs={{0,1},{1,0},{2,3},{3,2},{4,5},{5,4},{6,7},{7,6},{8,9},{9,8},{10,11... | collective-permute-start | bytes 786440 | tf_op jit(solution)/shard_map/ppermute | solution.py:513
  68.6 12.7 %collective-permute-start.13 = (bf16[1,4,128,256]{3,2,1,0:T(8,128)(2,1)S(1)}, bf16[1,4,128,256]{3,2,1,0:T(8,128)(2,1)S(1)}, u32[]{:S(2)}, u32[]{:S(2)}) collective-permute-start(bf16[1,4,128,256]{3,2,1,0:T(8,128)(2,1)S(1)} %fold.17.refs_10_), channel_id=1, source_target_pairs={{0,2},{1,3},{2,0},{3,1},{4,6},{5,7},{6,4},{7,5},{8,10},{9,11},{10,... | collective-permute-start | bytes 786440 | tf_op jit(solution)/shard_map/ppermute | solution.py:513
  72.9 4.2 %collective-permute-start.15 = (bf16[128,512]{1,0:T(8,128)(2,1)S(1)}, bf16[128,512]{1,0:T(8,128)(2,1)S(1)}, u32[]{:S(2)}, u32[]{:S(2)}) collective-permute-start(bf16[128,512]{1,0:T(8,128)(2,1)S(1)} %get-tuple-element.80.refs_2_.refs_0_.q_ref), channel_id=1, source_target_pairs={{0,1},{1,0},{2,3},{3,2},{4,5},{5,4},{6,7},{7,6},{8,9},{9,8},{10,11... | collective-permute-start | bytes 393224 | tf_op jit(solution)/shard_map/ppermute | solution.py:513
  72.9 4.2 %collective-permute-start.16 = (bf16[128,512]{1,0:T(8,128)(2,1)S(1)}, bf16[128,512]{1,0:T(8,128)(2,1)S(1)}, u32[]{:S(2)}, u32[]{:S(2)}) collective-permute-start(bf16[128,512]{1,0:T(8,128)(2,1)S(1)} %collective-permute-done.14.refs_1_), channel_id=1, source_target_pairs={{0,1},{1,0},{2,3},{3,2},{4,5},{5,4},{6,7},{7,6},{8,9},{9,8},{10,11... | collective-permute-start | bytes 393224 | tf_op jit(solution)/shard_map/ppermute | solution.py:513
  74.9 5.8 %collective-permute-start.25 = (bf16[128,512]{1,0:T(8,128)(2,1)S(1)}, bf16[128,512]{1,0:T(8,128)(2,1)S(1)}, u32[]{:S(2)}, u32[]{:S(2)}) collective-permute-start(bf16[128,512]{1,0:T(8,128)(2,1)S(1)} %get-tuple-element.83.refs_10_.refs_0_.q_ref), channel_id=1, source_target_pairs={{0,2},{1,3},{2,0},{3,1},{4,6},{5,7},{6,4},{7,5},{8,10},{9,11},{10,... | collective-permute-start | bytes 393224 | tf_op jit(solution)/shard_map/ppermute | solution.py:513
  80.8 10.3 %collective-permute-start.30 = (bf16[1,128,768]{2,1,0:T(8,128)(2,1)S(1)}, bf16[1,128,768]{2,1,0:T(8,128)(2,1)S(1)}, u32[]{:S(2)}, u32[]{:S(2)}) collective-permute-start(bf16[1,128,768]{2,1,0:T(8,128)(2,1)S(1)} %get-tuple-element.91), channel_id=1, source_target_pairs={{0,1},{1,0},{2,3},{3,2},{4,5},{5,4},{6,7},{7,6},{8,9},{9,8},{10,11... | collective-permute-start | bytes 589832 | tf_op jit(solution)/shard_map/ppermute | solution.py:513
  81.3 10.4 %collective-permute-start.31 = (bf16[1,128,768]{2,1,0:T(8,128)(2,1)S(1)}, bf16[1,128,768]{2,1,0:T(8,128)(2,1)S(1)}, u32[]{:S(2)}, u32[]{:S(2)}) collective-permute-start(bf16[1,128,768]{2,1,0:T(8,128)(2,1)S(1)} %fold.18.refs_3_), channel_id=1, source_target_pairs={{0,2},{1,3},{2,0},{3,1},{4,6},{5,7},{6,4},{7,5},{8,10},{9,11},{10,... | collective-permute-start | bytes 589832 | tf_op jit(solution)/shard_map/ppermute | solution.py:513
  86.6 6.0 %collective-permute-start.29 = (bf16[1,128,512]{2,1,0:T(8,128)(2,1)S(1)}, bf16[1,128,512]{2,1,0:T(8,128)(2,1)S(1)}, u32[]{:S(2)}, u32[]{:S(2)}) collective-permute-start(bf16[1,128,512]{2,1,0:T(8,128)(2,1)S(1)} %get-tuple-element.89), channel_id=1, source_target_pairs={{0,1},{1,0},{2,3},{3,2},{4,5},{5,4},{6,7},{7,6},{8,9},{9,8},{10,11... | collective-permute-start | bytes 393224 | tf_op jit(solution)/shard_map/ppermute | solution.py:513
  86.6 4.5 %collective-permute-start.22 = (bf16[128,256]{1,0:T(8,128)(2,1)S(1)}, bf16[128,256]{1,0:T(8,128)(2,1)S(1)}, u32[]{:S(2)}, u32[]{:S(2)}) collective-permute-start(bf16[128,256]{1,0:T(8,128)(2,1)S(1)} %get-tuple-element.85.refs_2_.refs_0_.q_ref), channel_id=1, source_target_pairs={{0,2},{1,3},{2,0},{3,1},{4,6},{5,7},{6,4},{7,5},{8,10},{9,11},{10,... | collective-permute-start | bytes 196616 | tf_op jit(solution)/shard_map/ppermute | solution.py:513
  87.2 5.6 %collective-permute-start.23 = (bf16[128,256]{1,0:T(8,128)(2,1)S(1)}, bf16[128,256]{1,0:T(8,128)(2,1)S(1)}, u32[]{:S(2)}, u32[]{:S(2)}) collective-permute-start(bf16[128,256]{1,0:T(8,128)(2,1)S(1)} %get-tuple-element.85.refs_2_.refs_0_.q_ref), channel_id=1, source_target_pairs={{0,1},{1,0},{2,3},{3,2},{4,5},{5,4},{6,7},{7,6},{8,9},{9,8},{10,11... | collective-permute-start | bytes 196616 | tf_op jit(solution)/shard_map/ppermute | solution.py:513
  91.2 6.2 %collective-permute-start.35 = (bf16[1,128,512]{2,1,0:T(8,128)(2,1)S(1)}, bf16[1,128,512]{2,1,0:T(8,128)(2,1)S(1)}, u32[]{:S(2)}, u32[]{:S(2)}) collective-permute-start(bf16[1,128,512]{2,1,0:T(8,128)(2,1)S(1)} %get-tuple-element.98), channel_id=1, source_target_pairs={{0,1},{1,0},{2,3},{3,2},{4,5},{5,4},{6,7},{7,6},{8,9},{9,8},{10,11... | collective-permute-start | bytes 393224 | tf_op jit(solution)/shard_map/ppermute | solution.py:513
  91.7 6.7 %collective-permute-start.36 = (bf16[1,128,512]{2,1,0:T(8,128)(2,1)S(1)}, bf16[1,128,512]{2,1,0:T(8,128)(2,1)S(1)}, u32[]{:S(2)}, u32[]{:S(2)}) collective-permute-start(bf16[1,128,512]{2,1,0:T(8,128)(2,1)S(1)} %fold.19.refs_10_), channel_id=1, source_target_pairs={{0,2},{1,3},{2,0},{3,1},{4,6},{5,7},{6,4},{7,5},{8,10},{9,11},{10,... | collective-permute-start | bytes 393224 | tf_op jit(solution)/shard_map/ppermute | solution.py:513
  94.9 3.9 %collective-permute-start.37 = (bf16[1,128,512]{2,1,0:T(8,128)(2,1)S(1)}, bf16[1,128,512]{2,1,0:T(8,128)(2,1)S(1)}, u32[]{:S(2)}, u32[]{:S(2)}) collective-permute-start(bf16[1,128,512]{2,1,0:T(8,128)(2,1)S(1)} %get-tuple-element.101), channel_id=1, source_target_pairs={{0,1},{1,0},{2,3},{3,2},{4,5},{5,4},{6,7},{7,6},{8,9},{9,8},{10,11... | collective-permute-start | bytes 393224 | tf_op jit(solution)/shard_map/ppermute | solution.py:513
  95.4 5.7 %collective-permute-start.38 = (bf16[1,128,512]{2,1,0:T(8,128)(2,1)S(1)}, bf16[1,128,512]{2,1,0:T(8,128)(2,1)S(1)}, u32[]{:S(2)}, u32[]{:S(2)}) collective-permute-start(bf16[1,128,512]{2,1,0:T(8,128)(2,1)S(1)} %fold.20.refs_10_), channel_id=1, source_target_pairs={{0,2},{1,3},{2,0},{3,1},{4,6},{5,7},{6,4},{7,5},{8,10},{9,11},{10,... | collective-permute-start | bytes 393224 | tf_op jit(solution)/shard_map/ppermute | solution.py:513
  97.0 4.5 %collective-permute-start.32 = (bf16[1,128,256]{2,1,0:T(8,128)(2,1)S(1)}, bf16[1,128,256]{2,1,0:T(8,128)(2,1)S(1)}, u32[]{:S(2)}, u32[]{:S(2)}) collective-permute-start(bf16[1,128,256]{2,1,0:T(8,128)(2,1)S(1)} %get-tuple-element.94), channel_id=1, source_target_pairs={{0,1},{1,0},{2,3},{3,2},{4,5},{5,4},{6,7},{7,6},{8,9},{9,8},{10,11... | collective-permute-start | bytes 196616 | tf_op jit(solution)/shard_map/ppermute | solution.py:513
  97.4 4.9 %collective-permute-start.34 = (bf16[1,128,256]{2,1,0:T(8,128)(2,1)S(1)}, bf16[1,128,256]{2,1,0:T(8,128)(2,1)S(1)}, u32[]{:S(2)}, u32[]{:S(2)}) collective-permute-start(bf16[1,128,256]{2,1,0:T(8,128)(2,1)S(1)} %fold.21.refs_3_), channel_id=1, source_target_pairs={{0,2},{1,3},{2,0},{3,1},{4,6},{5,7},{6,4},{7,5},{8,10},{9,11},{10,... | collective-permute-start | bytes 196616 | tf_op jit(solution)/shard_map/ppermute | solution.py:513
  106.4 4.5 %collective-permute-start.40 = (f32[8,128]{1,0:T(8,128)S(1)}, f32[8,128]{1,0:T(8,128)S(1)}, u32[]{:S(2)}, u32[]{:S(2)}) collective-permute-start(f32[8,128]{1,0:T(8,128)S(1)} %merge.1.refs_0_), channel_id=1, source_target_pairs={{0,8},{4,12},{8,0},{12,4},{1,9},{5,13},{9,1},{13,5},{2,10},{6,14},... | collective-permute-start | bytes 12296 | tf_op jit(solution)/shard_map/ppermute | solution.py:513
  111.3 6.4 %collective-permute-start.42 = (bf16[64,2048]{1,0:T(8,128)(2,1)S(1)}, bf16[64,2048]{1,0:T(8,128)(2,1)S(1)}, u32[]{:S(2)}, u32[]{:S(2)}) collective-permute-start(bf16[64,2048]{1,0:T(8,128)(2,1)S(1)} %get-tuple-element.108), channel_id=1, source_target_pairs={{0,2},{1,3},{2,0},{3,1},{4,6},{5,7},{6,4},{7,5},{8,10},{9,11},{10,... | collective-permute-start | bytes 786440 | tf_op jit(solution)/shard_map/ppermute | solution.py:513
  113.0 6.6 %collective-permute-start.43 = (bf16[64,2048]{1,0:T(8,128)(2,1)S(1)}, bf16[64,2048]{1,0:T(8,128)(2,1)S(1)}, u32[]{:S(2)}, u32[]{:S(2)}) collective-permute-start(bf16[64,2048]{1,0:T(8,128)(2,1)S(1)} %get-tuple-element.108), channel_id=1, source_target_pairs={{0,1},{1,0},{2,3},{3,2},{4,5},{5,4},{6,7},{7,6},{8,9},{9,8},{10,11... | collective-permute-start | bytes 786440 | tf_op jit(solution)/shard_map/ppermute | solution.py:513
  117.7 8.7 %collective-permute-start.41 = (bf16[64,2048]{1,0:T(8,128)(2,1)S(1)}, bf16[64,2048]{1,0:T(8,128)(2,1)S(1)}, u32[]{:S(2)}, u32[]{:S(2)}) collective-permute-start(bf16[64,2048]{1,0:T(8,128)(2,1)S(1)} %get-tuple-element.107), channel_id=1, source_target_pairs={{0,2},{1,3},{2,0},{3,1},{4,6},{5,7},{6,4},{7,5},{8,10},{9,11},{10,... | collective-permute-start | bytes 786440 | tf_op jit(solution)/shard_map/ppermute | solution.py:513
  119.4 12.6 %collective-permute-start.45 = (bf16[64,2048]{1,0:T(8,128)(2,1)S(1)}, bf16[64,2048]{1,0:T(8,128)(2,1)S(1)}, u32[]{:S(2)}, u32[]{:S(2)}) collective-permute-start(bf16[64,2048]{1,0:T(8,128)(2,1)S(1)} %get-tuple-element.107), channel_id=1, source_target_pairs={{0,1},{1,0},{2,3},{3,2},{4,5},{5,4},{6,7},{7,6},{8,9},{9,8},{10,11... | collective-permute-start | bytes 786440 | tf_op jit(solution)/shard_map/ppermute | solution.py:513
  126.4 5.5 %collective-permute-start.46 = (bf16[64,2048]{1,0:T(8,128)(2,1)S(1)}, bf16[64,2048]{1,0:T(8,128)(2,1)S(1)}, u32[]{:S(2)}, u32[]{:S(2)}) collective-permute-start(bf16[64,2048]{1,0:T(8,128)(2,1)S(1)} %tie.17), channel_id=1, source_target_pairs={{0,1},{1,0},{2,3},{3,2},{4,5},{5,4},{6,7},{7,6},{8,9},{9,8},{10,11... | collective-permute-start | bytes 786440 | tf_op jit(solution)/shard_map/ppermute | solution.py:513
  126.5 14.6 %collective-permute-start.49 = (bf16[2,4,16,1024]{3,2,1,0:T(8,128)(2,1)S(1)}, bf16[2,4,16,1024]{3,2,1,0:T(8,128)(2,1)S(1)}, u32[]{:S(2)}, u32[]{:S(2)}) collective-permute-start(bf16[2,4,16,1024]{3,2,1,0:T(8,128)(2,1)S(1)} %get-tuple-element.115), channel_id=1, source_target_pairs={{0,4},{4,0},{8,12},{12,8},{1,5},{5,1},{9,13},{13,9},{2,6},{6,2},{1... | collective-permute-start | bytes 786440 | tf_op jit(solution)/shard_map/ppermute | solution.py:513
  131.6 12.4 %collective-permute-start.48 = (bf16[2,4,16,1024]{3,2,1,0:T(8,128)(2,1)S(1)}, bf16[2,4,16,1024]{3,2,1,0:T(8,128)(2,1)S(1)}, u32[]{:S(2)}, u32[]{:S(2)}) collective-permute-start(bf16[2,4,16,1024]{3,2,1,0:T(8,128)(2,1)S(1)} %get-tuple-element.114), channel_id=1, source_target_pairs={{0,4},{4,0},{8,12},{12,8},{1,5},{5,1},{9,13},{13,9},{2,6},{6,2},{1... | collective-permute-start | bytes 786440 | tf_op jit(solution)/shard_map/ppermute | solution.py:513
  135.4 21.2 %collective-permute-start.52 = (bf16[2,4,16,1024]{3,2,1,0:T(8,128)(2,1)S(1)}, bf16[2,4,16,1024]{3,2,1,0:T(8,128)(2,1)S(1)}, u32[]{:S(2)}, u32[]{:S(2)}) collective-permute-start(bf16[2,4,16,1024]{3,2,1,0:T(8,128)(2,1)S(1)} %get-tuple-element.117), channel_id=1, source_target_pairs={{0,4},{4,0},{8,12},{12,8},{1,5},{5,1},{9,13},{13,9},{2,6},{6,2},{1... | collective-permute-start | bytes 786440 | tf_op jit(solution)/shard_map/ppermute | solution.py:513
  140.7 21.7 %collective-permute-start.47 = (bf16[2,4,16,1024]{3,2,1,0:T(8,128)(2,1)S(1)}, bf16[2,4,16,1024]{3,2,1,0:T(8,128)(2,1)S(1)}, u32[]{:S(2)}, u32[]{:S(2)}) collective-permute-start(bf16[2,4,16,1024]{3,2,1,0:T(8,128)(2,1)S(1)} %get-tuple-element.113), channel_id=1, source_target_pairs={{0,4},{4,0},{8,12},{12,8},{1,5},{5,1},{9,13},{13,9},{2,6},{6,2},{1... | collective-permute-start | bytes 786440 | tf_op jit(solution)/shard_map/ppermute | solution.py:513
  141.2 13.3 %collective-permute-start.51 = (bf16[1,4,16,1024]{3,2,1,0:T(8,128)(2,1)S(1)}, bf16[1,4,16,1024]{3,2,1,0:T(8,128)(2,1)S(1)}, u32[]{:S(2)}, u32[]{:S(2)}) collective-permute-start(bf16[1,4,16,1024]{3,2,1,0:T(8,128)(2,1)S(1)} %fold.22.refs_2_), channel_id=1, source_target_pairs={{0,8},{4,12},{8,0},{12,4},{1,9},{5,13},{9,1},{13,5},{2,10},{6,14},... | collective-permute-start | bytes 393224 | tf_op jit(solution)/shard_map/ppermute | solution.py:513
  144.1 16.1 %collective-permute-start.50 = (bf16[1,4,16,1024]{3,2,1,0:T(8,128)(2,1)S(1)}, bf16[1,4,16,1024]{3,2,1,0:T(8,128)(2,1)S(1)}, u32[]{:S(2)}, u32[]{:S(2)}) collective-permute-start(bf16[1,4,16,1024]{3,2,1,0:T(8,128)(2,1)S(1)} %fold.23.refs_3_), channel_id=1, source_target_pairs={{0,8},{4,12},{8,0},{12,4},{1,9},{5,13},{9,1},{13,5},{2,10},{6,14},... | collective-permute-start | bytes 393224 | tf_op jit(solution)/shard_map/ppermute | solution.py:513
  156.8 12.4 %collective-permute-start.54 = (bf16[1,4,16,1024]{3,2,1,0:T(8,128)(2,1)S(1)}, bf16[1,4,16,1024]{3,2,1,0:T(8,128)(2,1)S(1)}, u32[]{:S(2)}, u32[]{:S(2)}) collective-permute-start(bf16[1,4,16,1024]{3,2,1,0:T(8,128)(2,1)S(1)} %fold.24.refs_4_), channel_id=1, source_target_pairs={{0,8},{4,12},{8,0},{12,4},{1,9},{5,13},{9,1},{13,5},{2,10},{6,14},... | collective-permute-start | bytes 393224 | tf_op jit(solution)/shard_map/ppermute | solution.py:513
  162.5 9.1 %collective-permute-start.53 = (bf16[1,4,16,1024]{3,2,1,0:T(8,128)(2,1)S(1)}, bf16[1,4,16,1024]{3,2,1,0:T(8,128)(2,1)S(1)}, u32[]{:S(2)}, u32[]{:S(2)}) collective-permute-start(bf16[1,4,16,1024]{3,2,1,0:T(8,128)(2,1)S(1)} %fold.25.refs_4_), channel_id=1, source_target_pairs={{0,8},{4,12},{8,0},{12,4},{1,9},{5,13},{9,1},{13,5},{2,10},{6,14},... | collective-permute-start | bytes 393224 | tf_op jit(solution)/shard_map/ppermute | solution.py:513
  (17 other events, 89.4 us)

commit v13 on v12

--- a/solution.py
+++ b/solution.py
@@ -25,7 +25,6 @@
 
 
 LIGHT = pl.CostEstimate(flops=1000, bytes_accessed=1000, transcendentals=0)
-STEP = pl.CostEstimate(flops=1000, bytes_accessed=4_000_000, transcendentals=0)
 
 
 def far(x):
@@ -130,7 +129,7 @@
     refs[-1][...] = sum(r[...].astype(f32) for r in refs[:count]).astype(bf16)
 
 
-def fold(terms, after=(), told=LIGHT):
+def fold(terms, after=()):
     half = terms[0].shape[0] // 2 if len(terms) == 2 else terms[-1].shape[0] // 2
     tail = terms[0].shape[1:]
     steps = 2 if tail[-1] % 256 == 0 else 1
@@ -145,7 +144,7 @@
         out_specs=pl.BlockSpec(block, lambda j: (0,) + middle + (j,)),
         out_shape=jax.ShapeDtypeStruct((half,) + tail, bf16),
         compiler_params=params(),
-        cost_estimate=told,
+        cost_estimate=LIGHT,
         name="fold",
     )(*terms, *after)
 
@@ -394,18 +393,22 @@
         for r, out in enumerate(outs):
             out[:, column:column + span] = gated[r * rows:(r + 1) * rows]
         column += span
+    for out in outs:
+        if out.shape[1] > column:
+            out[:, column:] = jnp.zeros((rows, out.shape[1] - column), bf16)
 
 
 def gate_rows(stats, stat_width, atts, rests, chunks):
     rows, width = atts[0].shape[0], sum(a.shape[1] for a in atts)
+    widths = [width + DH * min(r, 1) for r in range(chunks)]
     return pl.pallas_call(
         functools.partial(gate_kernel, len(stats), len(atts), stat_width),
         grid=(1,),
         in_specs=[pl.BlockSpec(s.shape, lambda j: (0, 0)) for s in stats]
         + [pl.BlockSpec((rows, a.shape[1]), lambda j: (0, 0)) for a in atts]
         + [pl.BlockSpec((1, rows, r.shape[2]), lambda j: (2, 0, 0)) for r in rests],
-        out_specs=[pl.BlockSpec((rows // chunks, width), lambda j: (0, 0))] * chunks,
-        out_shape=[jax.ShapeDtypeStruct((rows // chunks, width), bf16)] * chunks,
+        out_specs=[pl.BlockSpec((rows // chunks, w), lambda j: (0, 0)) for w in widths],
+        out_shape=[jax.ShapeDtypeStruct((rows // chunks, w), bf16) for w in widths],
         compiler_params=params(),
         cost_estimate=LIGHT,
         name="gate",
@@ -434,8 +437,8 @@
 
 
 def output(index, slots, counts, blocks, w_out, column, columns, after):
-    owners, (each, width), zs = len(blocks), blocks[0].shape, sum(counts)
-    piece = each // zs
+    owners, each, zs = len(blocks), blocks[0].shape[0], sum(counts)
+    width, piece = w_out.shape[0], each // zs
     span = max(c for c in (512, 256, columns) if columns % c == 0 and column % c == 0)
     row_spec = pl.BlockSpec((zs, piece, width), lambda j, at: (0, 0, 0))
     return pl.pallas_call(
@@ -457,7 +460,7 @@
         name="output",
     )(
         index.reshape(1).astype(jnp.int32),
-        *[b.reshape(zs, piece, width) for b in blocks], far(w_out), *after,
+        *[b.reshape(zs, piece, b.shape[1]) for b in blocks], far(w_out), *after,
     )
 
 
@@ -494,7 +497,7 @@
         ),
         input_output_aliases={} if out is None else {2 + len(terms): 0},
         compiler_params=params(),
-        cost_estimate=STEP,
+        cost_estimate=LIGHT,
         name="close",
     )(at, far(tokens.reshape(-1, piece, tokens.shape[1])), *terms, *into, *after)
 
@@ -515,10 +518,10 @@
     )
 
 
-def scatter(keep, gots, axis, after=(), told=LIGHT):
+def scatter(keep, gots, axis, after=()):
     terms, sent = [keep, gots[0]], gots[-1]
     for b in range(1, bits_of(axis)):
-        sent = fold([keep, gots[-1]] if b == 1 else terms, after, told)
+        sent = fold([keep, gots[-1]] if b == 1 else terms, after)
         terms.append(swap(sent, axis, b))
     return terms, sent
 
@@ -631,7 +634,7 @@
     out, last_out = None, []
     if not straight:
         for r, rows in enumerate(gated):
-            whole = jnp.concatenate(gather(rows, "hist"))
+            whole = jnp.concatenate(gather(rows, "hist"))[:, :width]
             whole = jnp.dot(whole, w_out, preferred_element_type=f32).astype(bf16)
             whole = whole.reshape(owners, zs, piece, -1).swapaxes(0, 1)
             whole = lax.psum_scatter(whole, "head", scatter_dimension=0, tiled=True)
@@ -647,18 +650,20 @@
             own, *others = output(
                 index, slots, counts, blocks, w_out, g * span, span, last_out
             )
-            pieces.append((r, g, own, [swap(x, "head", 0) for x in others]))
+            before = pieces[-2][3] if len(pieces) > 1 else []
+            pieces.append((r, g, own, [swap(tie(x, before), "head", 0) for x in others]))
             last_out, first_out = [own], first_out or [own]
     closing, chain = [], last_out
     for r, g, own, arrived in pieces:
-        terms, sent = scatter(own, arrived, "head", chain, STEP) if arrived else ([own], own)
+        terms, sent = scatter(own, arrived, "head", chain) if arrived else ([own], own)
         chain = [sent]
         closing.append((r, g, terms))
-        if len(closing) > 1:
+        if len(closing) > 2:
             out, mark = close(place, index, tokens, chunks, *closing.pop(0), out, chain)
             chain = [mark]
     for last_piece in closing:
-        out, _ = close(place, index, tokens, chunks, *last_piece, out, [])
+        out, mark = close(place, index, tokens, chunks, *last_piece, out, chain)
+        chain = [mark]
     return out.reshape(cand // zs, -1)
 
 

time: 174 us -> 172 us (0.989)
  waiting for transfers between devices: 45.9 us -> 43.1 us
    ppermute x55, waiting for transfers between devices: 45.9 us -> 43.1 us  [swap(): lax.ppermute(x, axis, [(i, i ^ 1 << bit) for i in range(lax.axis_size(axi...]
  transfers between devices with their start and end apart: 55 -> 55, of which waited for: 13 -> 16; matrix products, arithmetic and copies ran while one was open for 0% -> 0% of each run, Pallas kernels for 43% -> 44%
where the time goes in v13:
time: 172 us
  Pallas kernels  83.5 us (49%)
  waiting for transfers between devices  43.1 us (25%)
  starting transfers between devices  41.9 us (24%)
  local copies, waits for them, and re-layouts  2.43 us (1%)
    ppermute x55, waiting for transfers between devices, swap(): lax.ppermute(x, axis, [(i, i ^ 1 << bit) for i in range(lax.axis_size(axi...  43.1 us
    ppermute x55, starting transfers between devices, swap(): lax.ppermute(x, axis, [(i, i ^ 1 << bit) for i in range(lax.axis_size(axi...  41.9 us
    pallas_call x5, Pallas kernels, project(): pl.pallas_call(functools.partial(project_kernel, parts, owners, len(after...  37.9 us
    pallas_call x4, Pallas kernels, output(): pl.pallas_call(functools.partial(output_kernel, owners, slots, len(after)...  13.9 us
    pallas_call x4, Pallas kernels, attend(): pl.pallas_call(functools.partial(attend_kernel, owners, len(counts)), gri...  12.5 us
    pallas_call x4, Pallas kernels, close(): pl.pallas_call(functools.partial(close_kernel, len(terms)), grid_spec=plt...  8.68 us
    pallas_call x13, Pallas kernels, fold(): pl.pallas_call(functools.partial(fold_kernel, len(terms)), grid=(steps,),...  4.77 us
  transfers between devices with their start and end apart: 55, of which 16 were waited for; matrix products, arithmetic and copies ran while one was open for 0% of the time, Pallas kernels for 44%

profile of v13, /device:TPU:0, one launch (start us, length us, event | category | flops | bytes accessed | tf_op | source)
XLA Modules:
  0.0 171.7 jit_solution(6446552527016142598)
XLA Ops:
  0.0 5.5 %project.5 = (bf16[2,4,128,256]{3,2,1,0:T(8,128)(2,1)S(1)}, bf16[1,4,128,256]{3,2,1,0:T(8,128)(2,1)S(1)}, bf16[1,4,128,256]{3,2,1,0:T(8,128)(2,1)S(1)}) custom-call(s32[1]{0:T(128)} %bitcast.at_ref, bf16[4,2,4,16,2048]{4,3,2,1,0:T(8,128)(2,1)} %bitcast.57, bf16[4,2,4,16,2048]{4,3,2,1,0:T(8,128)(2,1)} %bitcast.58, bf16[4,2,4,16,2048]{4,3,2,1,0:T(8,128)(2,1)} %bitcast.59, ...), custom_call_target="tpu_custom_call" | custom-call | flops 1000 | bytes 1000 | tf_op jit(solution)/shard_map/project/pallas_call | solution.py:80
  6.1 8.7 %project.6 = (bf16[2,4,128,512]{3,2,1,0:T(8,128)(2,1)S(1)}, bf16[1,4,128,512]{3,2,1,0:T(8,128)(2,1)S(1)}, bf16[1,4,128,512]{3,2,1,0:T(8,128)(2,1)S(1)}) custom-call(s32[1]{0:T(128)} %bitcast.at_ref, bf16[4,2,4,16,2048]{4,3,2,1,0:T(8,128)(2,1)} %bitcast.61, bf16[4,2,4,16,2048]{4,3,2,1,0:T(8,128)(2,1)} %bitcast.62, bf16[4,2,4,16,2048]{4,3,2,1,0:T(8,128)(2,1)} %bitcast.63, ...), custom_call_target="tpu_custom_call" | custom-call | flops 1000 | bytes 1000 | tf_op jit(solution)/shard_map/project/pallas_call | solution.py:80
  15.8 3.0 %collective-permute-start.4 = (bf16[1,4,128,256]{3,2,1,0:T(8,128)(2,1)S(1)}, bf16[1,4,128,256]{3,2,1,0:T(8,128)(2,1)S(1)}, u32[]{:S(2)}, u32[]{:S(2)}) collective-permute-start(bf16[1,4,128,256]{3,2,1,0:T(8,128)(2,1)S(1)} %fold.13.refs_8_), channel_id=1, source_target_pairs={{0,2},{1,3},{2,0},{3,1},{4,6},{5,7},{6,4},{7,5},{8,10},{9,11},{10,... | collective-permute-start | bytes 786440 | tf_op jit(solution)/shard_map/ppermute | solution.py:516
  18.7 8.7 %project.7 = (bf16[2,4,128,512]{3,2,1,0:T(8,128)(2,1)S(1)}, bf16[1,4,128,512]{3,2,1,0:T(8,128)(2,1)S(1)}, bf16[1,4,128,512]{3,2,1,0:T(8,128)(2,1)S(1)}) custom-call(s32[1]{0:T(128)} %bitcast.at_ref, bf16[4,2,4,16,2048]{4,3,2,1,0:T(8,128)(2,1)} %bitcast.65, bf16[4,2,4,16,2048]{4,3,2,1,0:T(8,128)(2,1)} %bitcast.66, bf16[4,2,4,16,2048]{4,3,2,1,0:T(8,128)(2,1)} %bitcast.67, ...), custom_call_target="tpu_custom_call" | custom-call | flops 1000 | bytes 1000 | tf_op jit(solution)/shard_map/project/pallas_call | solution.py:80
  28.5 8.8 %project.8 = (bf16[2,4,128,512]{3,2,1,0:T(8,128)(2,1)S(1)}, bf16[1,4,128,512]{3,2,1,0:T(8,128)(2,1)S(1)}, bf16[1,4,128,512]{3,2,1,0:T(8,128)(2,1)S(1)}) custom-call(s32[1]{0:T(128)} %bitcast.at_ref, bf16[4,2,4,16,2048]{4,3,2,1,0:T(8,128)(2,1)} %bitcast.69, bf16[4,2,4,16,2048]{4,3,2,1,0:T(8,128)(2,1)} %bitcast.70, bf16[4,2,4,16,2048]{4,3,2,1,0:T(8,128)(2,1)} %bitcast.71, ...), custom_call_target="tpu_custom_call" | custom-call | flops 1000 | bytes 1000 | tf_op jit(solution)/shard_map/project/pallas_call | solution.py:80
  39.1 1.9 %collective-permute-start.12 = (bf16[1,4,128,512]{3,2,1,0:T(8,128)(2,1)}, bf16[1,4,128,512]{3,2,1,0:T(8,128)(2,1)}, u32[]{:S(2)}, u32[]{:S(2)}) collective-permute-start(bf16[1,4,128,512]{3,2,1,0:T(8,128)(2,1)} %fold.15.refs_6_), channel_id=1, source_target_pairs={{0,2},{1,3},{2,0},{3,1},{4,6},{5,7},{6,4},{7,5},{8,10},{9,11},{10,... | collective-permute-start | bytes 1572872 | tf_op jit(solution)/shard_map/ppermute | solution.py:516
  41.0 1.4 collective-permute-done.8.refs_5_
  44.2 1.7 %collective-permute-start.17 = (bf16[1,4,128,512]{3,2,1,0:T(8,128)(2,1)}, bf16[1,4,128,512]{3,2,1,0:T(8,128)(2,1)}, u32[]{:S(2)}, u32[]{:S(2)}) collective-permute-start(bf16[1,4,128,512]{3,2,1,0:T(8,128)(2,1)} %fold.16.refs_8_), channel_id=1, source_target_pairs={{0,2},{1,3},{2,0},{3,1},{4,6},{5,7},{6,4},{7,5},{8,10},{9,11},{10,... | collective-permute-start | bytes 1572872 | tf_op jit(solution)/shard_map/ppermute | solution.py:516
  46.0 6.2 %project.9 = (bf16[2,4,128,256]{3,2,1,0:T(8,128)(2,1)S(1)}, bf16[1,4,128,256]{3,2,1,0:T(8,128)(2,1)S(1)}, bf16[1,4,128,256]{3,2,1,0:T(8,128)(2,1)}) custom-call(s32[1]{0:T(128)} %bitcast.at_ref, bf16[4,2,4,16,2048]{4,3,2,1,0:T(8,128)(2,1)} %bitcast.73, bf16[4,2,4,16,2048]{4,3,2,1,0:T(8,128)(2,1)} %bitcast.74, bf16[4,2,4,16,2048]{4,3,2,1,0:T(8,128)(2,1)} %bitcast.75, ...), custom_call_target="tpu_custom_call" | custom-call | flops 1000 | bytes 1000 | tf_op jit(solution)/shard_map/project/pallas_call | solution.py:80
  53.4 5.0 %collective-permute-done.18.refs_1_ = bf16[128,768]{1,0:T(8,128)(2,1)S(1)} collective-permute-done((bf16[128,768]{1,0:T(8,128)(2,1)S(1)}, bf16[128,768]{1,0:T(8,128)(2,1)S(1)}, u32[]{:S(2)}, u32[]{:S(2)}) %collective-permute-start.18) | collective-permute-done | bytes 196640 | tf_op jit(solution)/shard_map/ppermute | solution.py:516
  58.5 1.0 copy-done.3
  59.6 1.4 activate.5
  61.0 1.1 fold.17.refs_10_
  62.1 4.1 %attend.4 = (bf16[2,128,768]{2,1,0:T(8,128)(2,1)S(1)}, bf16[1,128,768]{2,1,0:T(8,128)(2,1)S(1)}, bf16[1,128,768]{2,1,0:T(8,128)(2,1)S(1)}) custom-call(s32[1]{0:T(128)} %bitcast.at_ref, bf16[128,768]{1,0:T(8,128)(2,1)S(1)} %get-tuple-element.76.refs_2_.refs_0_.q_ref, bf16[128,768]{1,0:T(8,128)(2,1)S(1)} %collective-permute-done.18.refs_1_, ...), custom_call_target="tpu_custom_call" | custom-call | flops 1000 | bytes 1000 | tf_op jit(solution)/shard_map/attend/pallas_call | solution.py:262
  66.7 1.8 %collective-permute-start.14 = (bf16[128,512]{1,0:T(8,128)(2,1)S(1)}, bf16[128,512]{1,0:T(8,128)(2,1)S(1)}, u32[]{:S(2)}, u32[]{:S(2)}) collective-permute-start(bf16[128,512]{1,0:T(8,128)(2,1)S(1)} %get-tuple-element.81.refs_2_.refs_0_.q_ref), channel_id=1, source_target_pairs={{0,2},{1,3},{2,0},{3,1},{4,6},{5,7},{6,4},{7,5},{8,10},{9,11},{10,... | collective-permute-start | bytes 393224 | tf_op jit(solution)/shard_map/ppermute | solution.py:516
  68.8 4.0 %collective-permute-done.14.refs_1_ = bf16[128,512]{1,0:T(8,128)(2,1)S(1)} collective-permute-done((bf16[128,512]{1,0:T(8,128)(2,1)S(1)}, bf16[128,512]{1,0:T(8,128)(2,1)S(1)}, u32[]{:S(2)}, u32[]{:S(2)}) %collective-permute-start.14) | collective-permute-done | bytes 131104 | tf_op jit(solution)/shard_map/ppermute | solution.py:516
  73.6 1.4 activate.6
  74.9 2.1 %collective-permute-start.25 = (bf16[128,512]{1,0:T(8,128)(2,1)S(1)}, bf16[128,512]{1,0:T(8,128)(2,1)S(1)}, u32[]{:S(2)}, u32[]{:S(2)}) collective-permute-start(bf16[128,512]{1,0:T(8,128)(2,1)S(1)} %get-tuple-element.84.refs_10_.refs_0_.q_ref), channel_id=1, source_target_pairs={{0,2},{1,3},{2,0},{3,1},{4,6},{5,7},{6,4},{7,5},{8,10},{9,11},{10,... | collective-permute-start | bytes 393224 | tf_op jit(solution)/shard_map/ppermute | solution.py:516
  77.0 3.1 %attend.5 = (bf16[2,128,512]{2,1,0:T(8,128)(2,1)S(1)}, bf16[1,128,512]{2,1,0:T(8,128)(2,1)S(1)}, bf16[1,128,512]{2,1,0:T(8,128)(2,1)S(1)}) custom-call(s32[1]{0:T(128)} %bitcast.at_ref, bf16[128,512]{1,0:T(8,128)(2,1)S(1)} %get-tuple-element.81.refs_2_.refs_0_.q_ref, bf16[128,512]{1,0:T(8,128)(2,1)S(1)} %collective-permute-done.14.refs_1_, ...), custom_call_target="tpu_custom_call" | custom-call | flops 1000 | bytes 1000 | tf_op jit(solution)/shard_map/attend/pallas_call | solution.py:262
  81.3 1.7 collective-permute-start.31
  83.3 3.2 %attend.6 = (bf16[2,128,512]{2,1,0:T(8,128)(2,1)S(1)}, bf16[1,128,512]{2,1,0:T(8,128)(2,1)S(1)}, bf16[1,128,512]{2,1,0:T(8,128)(2,1)S(1)}) custom-call(s32[1]{0:T(128)} %bitcast.at_ref, bf16[128,512]{1,0:T(8,128)(2,1)S(1)} %get-tuple-element.84.refs_10_.refs_0_.q_ref, bf16[128,512]{1,0:T(8,128)(2,1)S(1)} %collective-permute-done.25.refs_1_, ...), custom_call_target="tpu_custom_call" | custom-call | flops 1000 | bytes 1000 | tf_op jit(solution)/shard_map/attend/pallas_call | solution.py:262
  87.2 3.9 %collective-permute-done.22.refs_1_ = bf16[128,256]{1,0:T(8,128)(2,1)S(1)} collective-permute-done((bf16[128,256]{1,0:T(8,128)(2,1)S(1)}, bf16[128,256]{1,0:T(8,128)(2,1)S(1)}, u32[]{:S(2)}, u32[]{:S(2)}) %collective-permute-start.22) | collective-permute-done | bytes 65568 | tf_op jit(solution)/shard_map/ppermute | solution.py:516
  92.8 2.0 %attend.7 = (bf16[2,128,256]{2,1,0:T(8,128)(2,1)S(1)}, bf16[1,128,256]{2,1,0:T(8,128)(2,1)S(1)}, bf16[1,128,256]{2,1,0:T(8,128)(2,1)S(1)}) custom-call(s32[1]{0:T(128)} %bitcast.at_ref, bf16[128,256]{1,0:T(8,128)(2,1)S(1)} %get-tuple-element.86.refs_2_.refs_0_.q_ref, bf16[128,256]{1,0:T(8,128)(2,1)S(1)} %collective-permute-done.22.refs_1_, ...), custom_call_target="tpu_custom_call" | custom-call | flops 1000 | bytes 1000 | tf_op jit(solution)/shard_map/attend/pallas_call | solution.py:262
  95.4 1.7 collective-permute-start.38
  98.8 2.3 %collective-permute-done.38.refs_2_ = bf16[1,128,512]{2,1,0:T(8,128)(2,1)S(1)} collective-permute-done((bf16[1,128,512]{2,1,0:T(8,128)(2,1)S(1)}, bf16[1,128,512]{2,1,0:T(8,128)(2,1)S(1)}, u32[]{:S(2)}, u32[]{:S(2)}) %collective-permute-start.38) | collective-permute-done | bytes 131104 | tf_op jit(solution)/shard_map/ppermute | solution.py:516
  102.7 1.8 %collective-permute-start.39 = (f32[8,128]{1,0:T(8,128)S(1)}, f32[8,128]{1,0:T(8,128)S(1)}, u32[]{:S(2)}, u32[]{:S(2)}) collective-permute-start(f32[8,128]{1,0:T(8,128)S(1)} %get-tuple-element.106.refs_0_), channel_id=1, source_target_pairs={{0,4},{4,0},{8,12},{12,8},{1,5},{5,1},{9,13},{13,9},{2,6},{6,2},{1... | collective-permute-start | bytes 12296 | tf_op jit(solution)/shard_map/ppermute | solution.py:516
  104.5 1.9 %collective-permute-done.39.refs_1_ = f32[8,128]{1,0:T(8,128)S(1)} collective-permute-done((f32[8,128]{1,0:T(8,128)S(1)}, f32[8,128]{1,0:T(8,128)S(1)}, u32[]{:S(2)}, u32[]{:S(2)}) %collective-permute-start.39) | collective-permute-done | bytes 4128 | tf_op jit(solution)/shard_map/ppermute | solution.py:516
  106.4 2.8 %collective-permute-start.40 = (f32[8,128]{1,0:T(8,128)S(1)}, f32[8,128]{1,0:T(8,128)S(1)}, u32[]{:S(2)}, u32[]{:S(2)}) collective-permute-start(f32[8,128]{1,0:T(8,128)S(1)} %merge.1.refs_0_), channel_id=1, source_target_pairs={{0,8},{4,12},{8,0},{12,4},{1,9},{5,13},{9,1},{13,5},{2,10},{6,14},... | collective-permute-start | bytes 12296 | tf_op jit(solution)/shard_map/ppermute | solution.py:516
  109.2 1.7 %collective-permute-done.40.refs_1_ = f32[8,128]{1,0:T(8,128)S(1)} collective-permute-done((f32[8,128]{1,0:T(8,128)S(1)}, f32[8,128]{1,0:T(8,128)S(1)}, u32[]{:S(2)}, u32[]{:S(2)}) %collective-permute-start.40) | collective-permute-done | bytes 4128 | tf_op jit(solution)/shard_map/ppermute | solution.py:516
  111.3 1.7 %collective-permute-start.42 = (bf16[64,2048]{1,0:T(8,128)(2,1)S(1)}, bf16[64,2048]{1,0:T(8,128)(2,1)S(1)}, u32[]{:S(2)}, u32[]{:S(2)}) collective-permute-start(bf16[64,2048]{1,0:T(8,128)(2,1)S(1)} %get-tuple-element.109), channel_id=1, source_target_pairs={{0,2},{1,3},{2,0},{3,1},{4,6},{5,7},{6,4},{7,5},{8,10},{9,11},{10,... | collective-permute-start | bytes 786440 | tf_op jit(solution)/shard_map/ppermute | solution.py:516
  113.4 6.7 %collective-permute-done.42 = bf16[64,2048]{1,0:T(8,128)(2,1)S(1)} collective-permute-done((bf16[64,2048]{1,0:T(8,128)(2,1)S(1)}, bf16[64,2048]{1,0:T(8,128)(2,1)S(1)}, u32[]{:S(2)}, u32[]{:S(2)}) %collective-permute-start.42) | collective-permute-done | bytes 262176 | tf_op jit(solution)/shard_map/ppermute | solution.py:516
  121.7 3.4 %output.4 = (bf16[2,4,16,1024]{3,2,1,0:T(8,128)(2,1)S(1)}, bf16[2,4,16,1024]{3,2,1,0:T(8,128)(2,1)S(1)}) custom-call(s32[1]{0:T(128)} %bitcast.3.index_ref, bf16[4,16,2048]{2,1,0:T(8,128)(2,1)S(1)} %bitcast.47, bf16[4,16,2048]{2,1,0:T(8,128)(2,1)S(1)} %bitcast.49, bf16[4,16,2048]{2,1,0:T(8,128)(2,1)S(1)} %bitcast.51, bf16[4,16,2048]{2,1,0:T(8,128)(2,1)S(1)} %bitcast.53, ...), custom_call_target="tpu_custom_call" | custom-call | flops 1000 | bytes 1000 | tf_op jit(solution)/shard_map/output/pallas_call | solution.py:444
  125.3 1.6 collective-permute-start.49
  126.9 3.4 %output.5 = (bf16[2,4,16,1024]{3,2,1,0:T(8,128)(2,1)S(1)}, bf16[2,4,16,1024]{3,2,1,0:T(8,128)(2,1)S(1)}) custom-call(s32[1]{0:T(128)} %bitcast.3.index_ref, bf16[4,16,2048]{2,1,0:T(8,128)(2,1)S(1)} %bitcast.48, bf16[4,16,2048]{2,1,0:T(8,128)(2,1)S(1)} %bitcast.50, bf16[4,16,2048]{2,1,0:T(8,128)(2,1)S(1)} %bitcast.52, bf16[4,16,2048]{2,1,0:T(8,128)(2,1)S(1)} %bitcast.54, ...), custom_call_target="tpu_custom_call" | custom-call | flops 1000 | bytes 1000 | tf_op jit(solution)/shard_map/output/pallas_call | solution.py:444
  130.9 3.5 %output.6 = (bf16[2,4,16,1024]{3,2,1,0:T(8,128)(2,1)S(1)}, bf16[2,4,16,1024]{3,2,1,0:T(8,128)(2,1)S(1)}) custom-call(s32[1]{0:T(128)} %bitcast.3.index_ref, bf16[4,16,2176]{2,1,0:T(8,128)(2,1)S(1)} %bitcast.41, bf16[4,16,2176]{2,1,0:T(8,128)(2,1)S(1)} %bitcast.39, bf16[4,16,2176]{2,1,0:T(8,128)(2,1)S(1)} %bitcast.43, bf16[4,16,2176]{2,1,0:T(8,128)(2,1)S(1)} %bitcast.45, ...), custom_call_target="tpu_custom_call" | custom-call | flops 1000 | bytes 1000 | tf_op jit(solution)/shard_map/output/pallas_call | solution.py:444
  134.5 1.6 collective-permute-start.51
  136.0 3.5 %output.7 = (bf16[2,4,16,1024]{3,2,1,0:T(8,128)(2,1)S(1)}, bf16[2,4,16,1024]{3,2,1,0:T(8,128)(2,1)S(1)}) custom-call(s32[1]{0:T(128)} %bitcast.3.index_ref, bf16[4,16,2176]{2,1,0:T(8,128)(2,1)S(1)} %bitcast.42, bf16[4,16,2176]{2,1,0:T(8,128)(2,1)S(1)} %bitcast.40, bf16[4,16,2176]{2,1,0:T(8,128)(2,1)S(1)} %bitcast.44, bf16[4,16,2176]{2,1,0:T(8,128)(2,1)S(1)} %bitcast.46, ...), custom_call_target="tpu_custom_call" | custom-call | flops 1000 | bytes 1000 | tf_op jit(solution)/shard_map/output/pallas_call | solution.py:444
  140.1 1.6 collective-permute-start.48
  141.8 2.7 %collective-permute-start.50 = (bf16[1,4,16,1024]{3,2,1,0:T(8,128)(2,1)S(1)}, bf16[1,4,16,1024]{3,2,1,0:T(8,128)(2,1)S(1)}, u32[]{:S(2)}, u32[]{:S(2)}) collective-permute-start(bf16[1,4,16,1024]{3,2,1,0:T(8,128)(2,1)S(1)} %fold.22.refs_2_), channel_id=1, source_target_pairs={{0,8},{4,12},{8,0},{12,4},{1,9},{5,13},{9,1},{13,5},{2,10},{6,14},... | collective-permute-start | bytes 393224 | tf_op jit(solution)/shard_map/ppermute | solution.py:516
  145.0 6.3 %collective-permute-done.51.refs_1_ = bf16[2,4,16,1024]{3,2,1,0:T(8,128)(2,1)S(1)} collective-permute-done((bf16[2,4,16,1024]{3,2,1,0:T(8,128)(2,1)S(1)}, bf16[2,4,16,1024]{3,2,1,0:T(8,128)(2,1)S(1)}, u32[]{:S(2)}, u32[]{:S(2)}) %collective-permute-start.51) | collective-permute-done | bytes 262176 | tf_op jit(solution)/shard_map/ppermute | solution.py:516
  151.4 1.7 %collective-permute-start.53 = (bf16[1,4,16,1024]{3,2,1,0:T(8,128)(2,1)S(1)}, bf16[1,4,16,1024]{3,2,1,0:T(8,128)(2,1)S(1)}, u32[]{:S(2)}, u32[]{:S(2)}) collective-permute-start(bf16[1,4,16,1024]{3,2,1,0:T(8,128)(2,1)S(1)} %fold.24.refs_3_), channel_id=1, source_target_pairs={{0,8},{4,12},{8,0},{12,4},{1,9},{5,13},{9,1},{13,5},{2,10},{6,14},... | collective-permute-start | bytes 393224 | tf_op jit(solution)/shard_map/ppermute | solution.py:516
  153.2 2.2 %close.4 = (bf16[8,16,2048]{2,1,0:T(8,128)(2,1)}, f32[8,128]{1,0:T(8,128)S(1)}) custom-call(s32[2]{0:T(128)S(1)} %pad_add_fusion.1.at_ref, bf16[32,16,2048]{2,1,0:T(8,128)(2,1)} %bitcast.77, bf16[2,4,16,1024]{3,2,1,0:T(8,128)(2,1)S(1)} %get-tuple-element.110.refs_1_.refs_5_.refs_0_, bf16[2,4,16,1024]{3,2,1,0:T(8,128)(2,1)S(1)} %collective-permute-done.49.refs_1_, ...), custom_call_target="tpu_custom_call" | custom-call | flops 1000 | bytes 1000 | tf_op jit(solution)/shard_map/close/pallas_call | solution.py:481
  155.4 1.2 collective-permute-done.48.refs_1_
  156.8 2.2 %collective-permute-start.52 = (bf16[1,4,16,1024]{3,2,1,0:T(8,128)(2,1)S(1)}, bf16[1,4,16,1024]{3,2,1,0:T(8,128)(2,1)S(1)}, u32[]{:S(2)}, u32[]{:S(2)}) collective-permute-start(bf16[1,4,16,1024]{3,2,1,0:T(8,128)(2,1)S(1)} %fold.25.refs_4_), channel_id=1, source_target_pairs={{0,8},{4,12},{8,0},{12,4},{1,9},{5,13},{9,1},{13,5},{2,10},{6,14},... | collective-permute-start | bytes 393224 | tf_op jit(solution)/shard_map/ppermute | solution.py:516
  159.0 2.2 %close.5 = (bf16[8,16,2048]{2,1,0:T(8,128)(2,1)}, f32[8,128]{1,0:T(8,128)S(1)}) custom-call(s32[2]{0:T(128)S(1)} %pad_add_fusion.1.at_ref, bf16[32,16,2048]{2,1,0:T(8,128)(2,1)} %bitcast.78, bf16[2,4,16,1024]{3,2,1,0:T(8,128)(2,1)S(1)} %get-tuple-element.111.refs_5_.refs_0_, ...), custom_call_target="tpu_custom_call", output_to_operand_aliasing={{0}: (5, {})} | custom-call | flops 1000 | bytes 1000 | tf_op jit(solution)/shard_map/close/pallas_call | solution.py:481
  161.2 5.7 %collective-permute-done.53.refs_2_ = bf16[1,4,16,1024]{3,2,1,0:T(8,128)(2,1)S(1)} collective-permute-done((bf16[1,4,16,1024]{3,2,1,0:T(8,128)(2,1)S(1)}, bf16[1,4,16,1024]{3,2,1,0:T(8,128)(2,1)S(1)}, u32[]{:S(2)}, u32[]{:S(2)}) %collective-permute-start.53) | collective-permute-done | bytes 131104 | tf_op jit(solution)/shard_map/ppermute | solution.py:516
  166.9 2.2 %close.6 = (bf16[8,16,2048]{2,1,0:T(8,128)(2,1)}, f32[8,128]{1,0:T(8,128)S(1)}) custom-call(s32[2]{0:T(128)S(1)} %pad_add_fusion.at_ref, bf16[32,16,2048]{2,1,0:T(8,128)(2,1)} %bitcast.79, bf16[2,4,16,1024]{3,2,1,0:T(8,128)(2,1)S(1)} %get-tuple-element.112.refs_5_.refs_0_, ...), custom_call_target="tpu_custom_call", output_to_operand_aliasing={{0}: (5, {})} | custom-call | flops 1000 | bytes 1000 | tf_op jit(solution)/shard_map/close/pallas_call | solution.py:481
  169.5 2.2 %close.7 = (bf16[8,16,2048]{2,1,0:T(8,128)(2,1)}, f32[8,128]{1,0:T(8,128)}) custom-call(s32[2]{0:T(128)S(1)} %pad_add_fusion.at_ref, bf16[32,16,2048]{2,1,0:T(8,128)(2,1)} %bitcast.80, bf16[2,4,16,1024]{3,2,1,0:T(8,128)(2,1)S(1)} %get-tuple-element.113.refs_2_.refs_0_, ...), custom_call_target="tpu_custom_call", output_to_operand_aliasing={{0}: (5, {})} | custom-call | flops 1000 | bytes 1000 | tf_op jit(solution)/shard_map/close/pallas_call | solution.py:481
  (136 shorter events, 21.7 us)
Async XLA Ops:
  5.5 9.4 %collective-permute-start = (bf16[1,4,128,256]{3,2,1,0:T(8,128)(2,1)S(1)}, bf16[1,4,128,256]{3,2,1,0:T(8,128)(2,1)S(1)}, u32[]{:S(2)}, u32[]{:S(2)}) collective-permute-start(bf16[1,4,128,256]{3,2,1,0:T(8,128)(2,1)S(1)} %get-tuple-element.68), channel_id=1, source_target_pairs={{0,1},{1,0},{2,3},{3,2},{4,5},{5,4},{6,7},{7,6},{8,9},{9,8},{10,11... | collective-permute-start | bytes 786440 | tf_op jit(solution)/shard_map/ppermute | solution.py:516
  6.1 8.8 %collective-permute-start.1 = (bf16[1,4,128,256]{3,2,1,0:T(8,128)(2,1)S(1)}, bf16[1,4,128,256]{3,2,1,0:T(8,128)(2,1)S(1)}, u32[]{:S(2)}, u32[]{:S(2)}) collective-permute-start(bf16[1,4,128,256]{3,2,1,0:T(8,128)(2,1)S(1)} %get-tuple-element.69), channel_id=1, source_target_pairs={{0,1},{1,0},{2,3},{3,2},{4,5},{5,4},{6,7},{7,6},{8,9},{9,8},{10,11... | collective-permute-start | bytes 786440 | tf_op jit(solution)/shard_map/ppermute | solution.py:516
  14.9 12.6 %collective-permute-start.3 = (bf16[1,4,128,512]{3,2,1,0:T(8,128)(2,1)S(1)}, bf16[1,4,128,512]{3,2,1,0:T(8,128)(2,1)S(1)}, u32[]{:S(2)}, u32[]{:S(2)}) collective-permute-start(bf16[1,4,128,512]{3,2,1,0:T(8,128)(2,1)S(1)} %tie.12), channel_id=1, source_target_pairs={{0,1},{1,0},{2,3},{3,2},{4,5},{5,4},{6,7},{7,6},{8,9},{9,8},{10,11... | collective-permute-start | bytes 1572872 | tf_op jit(solution)/shard_map/ppermute | solution.py:516
  15.4 12.1 %collective-permute-start.2 = (bf16[1,4,128,512]{3,2,1,0:T(8,128)(2,1)S(1)}, bf16[1,4,128,512]{3,2,1,0:T(8,128)(2,1)S(1)}, u32[]{:S(2)}, u32[]{:S(2)}) collective-permute-start(bf16[1,4,128,512]{3,2,1,0:T(8,128)(2,1)S(1)} %tie.11), channel_id=1, source_target_pairs={{0,1},{1,0},{2,3},{3,2},{4,5},{5,4},{6,7},{7,6},{8,9},{9,8},{10,11... | collective-permute-start | bytes 1572872 | tf_op jit(solution)/shard_map/ppermute | solution.py:516
  15.8 11.7 %collective-permute-start.4 = (bf16[1,4,128,256]{3,2,1,0:T(8,128)(2,1)S(1)}, bf16[1,4,128,256]{3,2,1,0:T(8,128)(2,1)S(1)}, u32[]{:S(2)}, u32[]{:S(2)}) collective-permute-start(bf16[1,4,128,256]{3,2,1,0:T(8,128)(2,1)S(1)} %fold.13.refs_8_), channel_id=1, source_target_pairs={{0,2},{1,3},{2,0},{3,1},{4,6},{5,7},{6,4},{7,5},{8,10},{9,11},{10,... | collective-permute-start | bytes 786440 | tf_op jit(solution)/shard_map/ppermute | solution.py:516
  27.5 9.8 %collective-permute-start.6 = (bf16[1,4,128,512]{3,2,1,0:T(8,128)(2,1)S(1)}, bf16[1,4,128,512]{3,2,1,0:T(8,128)(2,1)S(1)}, u32[]{:S(2)}, u32[]{:S(2)}) collective-permute-start(bf16[1,4,128,512]{3,2,1,0:T(8,128)(2,1)S(1)} %tie.14), channel_id=1, source_target_pairs={{0,1},{1,0},{2,3},{3,2},{4,5},{5,4},{6,7},{7,6},{8,9},{9,8},{10,11... | collective-permute-start | bytes 1572872 | tf_op jit(solution)/shard_map/ppermute | solution.py:516
  27.6 9.7 %collective-permute-start.5 = (bf16[1,4,128,512]{3,2,1,0:T(8,128)(2,1)S(1)}, bf16[1,4,128,512]{3,2,1,0:T(8,128)(2,1)S(1)}, u32[]{:S(2)}, u32[]{:S(2)}) collective-permute-start(bf16[1,4,128,512]{3,2,1,0:T(8,128)(2,1)S(1)} %tie.13), channel_id=1, source_target_pairs={{0,1},{1,0},{2,3},{3,2},{4,5},{5,4},{6,7},{7,6},{8,9},{9,8},{10,11... | collective-permute-start | bytes 1572872 | tf_op jit(solution)/shard_map/ppermute | solution.py:516
  28.4 14.0 %collective-permute-start.8 = (bf16[1,4,128,512]{3,2,1,0:T(8,128)(2,1)S(1)}, bf16[1,4,128,512]{3,2,1,0:T(8,128)(2,1)S(1)}, u32[]{:S(2)}, u32[]{:S(2)}) collective-permute-start(bf16[1,4,128,512]{3,2,1,0:T(8,128)(2,1)S(1)} %fold.14.refs_8_), channel_id=1, source_target_pairs={{0,2},{1,3},{2,0},{3,1},{4,6},{5,7},{6,4},{7,5},{8,10},{9,11},{10,... | collective-permute-start | bytes 1572872 | tf_op jit(solution)/shard_map/ppermute | solution.py:516
  37.3 5.9 %collective-permute-start.7 = (bf16[1,4,128,512]{3,2,1,0:T(8,128)(2,1)S(1)}, bf16[1,4,128,512]{3,2,1,0:T(8,128)(2,1)S(1)}, u32[]{:S(2)}, u32[]{:S(2)}) collective-permute-start(bf16[1,4,128,512]{3,2,1,0:T(8,128)(2,1)S(1)} %tie.15), channel_id=1, source_target_pairs={{0,1},{1,0},{2,3},{3,2},{4,5},{5,4},{6,7},{7,6},{8,9},{9,8},{10,11... | collective-permute-start | bytes 1572872 | tf_op jit(solution)/shard_map/ppermute | solution.py:516
  38.1 14.7 %collective-permute-start.9 = (bf16[1,4,128,512]{3,2,1,0:T(8,128)(2,1)S(1)}, bf16[1,4,128,512]{3,2,1,0:T(8,128)(2,1)S(1)}, u32[]{:S(2)}, u32[]{:S(2)}) collective-permute-start(bf16[1,4,128,512]{3,2,1,0:T(8,128)(2,1)S(1)} %tie.16), channel_id=1, source_target_pairs={{0,1},{1,0},{2,3},{3,2},{4,5},{5,4},{6,7},{7,6},{8,9},{9,8},{10,11... | collective-permute-start | bytes 1572872 | tf_op jit(solution)/shard_map/ppermute | solution.py:516
  39.1 19.4 %collective-permute-start.12 = (bf16[1,4,128,512]{3,2,1,0:T(8,128)(2,1)}, bf16[1,4,128,512]{3,2,1,0:T(8,128)(2,1)}, u32[]{:S(2)}, u32[]{:S(2)}) collective-permute-start(bf16[1,4,128,512]{3,2,1,0:T(8,128)(2,1)} %fold.15.refs_6_), channel_id=1, source_target_pairs={{0,2},{1,3},{2,0},{3,1},{4,6},{5,7},{6,4},{7,5},{8,10},{9,11},{10,... | collective-permute-start | bytes 1572872 | tf_op jit(solution)/shard_map/ppermute | solution.py:516
  42.9 15.5 %collective-permute-start.18 = (bf16[128,768]{1,0:T(8,128)(2,1)S(1)}, bf16[128,768]{1,0:T(8,128)(2,1)S(1)}, u32[]{:S(2)}, u32[]{:S(2)}) collective-permute-start(bf16[128,768]{1,0:T(8,128)(2,1)S(1)} %get-tuple-element.76.refs_2_.refs_0_.q_ref), channel_id=1, source_target_pairs={{0,2},{1,3},{2,0},{3,1},{4,6},{5,7},{6,4},{7,5},{8,10},{9,11},{10,... | collective-permute-start | bytes 589832 | tf_op jit(solution)/shard_map/ppermute | solution.py:516
  44.2 29.3 %collective-permute-start.17 = (bf16[1,4,128,512]{3,2,1,0:T(8,128)(2,1)}, bf16[1,4,128,512]{3,2,1,0:T(8,128)(2,1)}, u32[]{:S(2)}, u32[]{:S(2)}) collective-permute-start(bf16[1,4,128,512]{3,2,1,0:T(8,128)(2,1)} %fold.16.refs_8_), channel_id=1, source_target_pairs={{0,2},{1,3},{2,0},{3,1},{4,6},{5,7},{6,4},{7,5},{8,10},{9,11},{10,... | collective-permute-start | bytes 1572872 | tf_op jit(solution)/shard_map/ppermute | solution.py:516
  52.8 8.1 %collective-permute-start.11 = (bf16[1,4,128,256]{3,2,1,0:T(8,128)(2,1)}, bf16[1,4,128,256]{3,2,1,0:T(8,128)(2,1)}, u32[]{:S(2)}, u32[]{:S(2)}) collective-permute-start(bf16[1,4,128,256]{3,2,1,0:T(8,128)(2,1)} %tie.18), channel_id=1, source_target_pairs={{0,1},{1,0},{2,3},{3,2},{4,5},{5,4},{6,7},{7,6},{8,9},{9,8},{10,11... | collective-permute-start | bytes 786440 | tf_op jit(solution)/shard_map/ppermute | solution.py:516
  52.8 9.2 %collective-permute-start.19 = (bf16[128,768]{1,0:T(8,128)(2,1)S(1)}, bf16[128,768]{1,0:T(8,128)(2,1)}, u32[]{:S(2)}, u32[]{:S(2)}) collective-permute-start(bf16[128,768]{1,0:T(8,128)(2,1)S(1)} %get-tuple-element.76.refs_2_.refs_0_.q_ref), channel_id=1, source_target_pairs={{0,1},{1,0},{2,3},{3,2},{4,5},{5,4},{6,7},{7,6},{8,9},{9,8},{10,11... | collective-permute-start | bytes 589832 | tf_op jit(solution)/shard_map/ppermute | solution.py:516
  58.4 3.7 %collective-permute-start.20 = (bf16[128,768]{1,0:T(8,128)(2,1)S(1)}, bf16[128,768]{1,0:T(8,128)(2,1)}, u32[]{:S(2)}, u32[]{:S(2)}) collective-permute-start(bf16[128,768]{1,0:T(8,128)(2,1)S(1)} %collective-permute-done.18.refs_1_), channel_id=1, source_target_pairs={{0,1},{1,0},{2,3},{3,2},{4,5},{5,4},{6,7},{7,6},{8,9},{9,8},{10,11... | collective-permute-start | bytes 589832 | tf_op jit(solution)/shard_map/ppermute | solution.py:516
  66.2 6.7 %collective-permute-start.21 = (bf16[1,128,768]{2,1,0:T(8,128)(2,1)S(1)}, bf16[1,128,768]{2,1,0:T(8,128)(2,1)S(1)}, u32[]{:S(2)}, u32[]{:S(2)}) collective-permute-start(bf16[1,128,768]{2,1,0:T(8,128)(2,1)S(1)} %get-tuple-element.83), channel_id=1, source_target_pairs={{0,1},{1,0},{2,3},{3,2},{4,5},{5,4},{6,7},{7,6},{8,9},{9,8},{10,11... | collective-permute-start | bytes 589832 | tf_op jit(solution)/shard_map/ppermute | solution.py:516
  66.7 6.1 %collective-permute-start.14 = (bf16[128,512]{1,0:T(8,128)(2,1)S(1)}, bf16[128,512]{1,0:T(8,128)(2,1)S(1)}, u32[]{:S(2)}, u32[]{:S(2)}) collective-permute-start(bf16[128,512]{1,0:T(8,128)(2,1)S(1)} %get-tuple-element.81.refs_2_.refs_0_.q_ref), channel_id=1, source_target_pairs={{0,2},{1,3},{2,0},{3,1},{4,6},{5,7},{6,4},{7,5},{8,10},{9,11},{10,... | collective-permute-start | bytes 393224 | tf_op jit(solution)/shard_map/ppermute | solution.py:516
  68.5 12.3 %collective-permute-start.10 = (bf16[1,4,128,256]{3,2,1,0:T(8,128)(2,1)S(1)}, bf16[1,4,128,256]{3,2,1,0:T(8,128)(2,1)S(1)}, u32[]{:S(2)}, u32[]{:S(2)}) collective-permute-start(bf16[1,4,128,256]{3,2,1,0:T(8,128)(2,1)S(1)} %tie.17), channel_id=1, source_target_pairs={{0,1},{1,0},{2,3},{3,2},{4,5},{5,4},{6,7},{7,6},{8,9},{9,8},{10,11... | collective-permute-start | bytes 786440 | tf_op jit(solution)/shard_map/ppermute | solution.py:516
  68.6 12.7 %collective-permute-start.13 = (bf16[1,4,128,256]{3,2,1,0:T(8,128)(2,1)S(1)}, bf16[1,4,128,256]{3,2,1,0:T(8,128)(2,1)S(1)}, u32[]{:S(2)}, u32[]{:S(2)}) collective-permute-start(bf16[1,4,128,256]{3,2,1,0:T(8,128)(2,1)S(1)} %fold.17.refs_10_), channel_id=1, source_target_pairs={{0,2},{1,3},{2,0},{3,1},{4,6},{5,7},{6,4},{7,5},{8,10},{9,11},{10,... | collective-permute-start | bytes 786440 | tf_op jit(solution)/shard_map/ppermute | solution.py:516
  72.9 4.2 %collective-permute-start.15 = (bf16[128,512]{1,0:T(8,128)(2,1)S(1)}, bf16[128,512]{1,0:T(8,128)(2,1)S(1)}, u32[]{:S(2)}, u32[]{:S(2)}) collective-permute-start(bf16[128,512]{1,0:T(8,128)(2,1)S(1)} %get-tuple-element.81.refs_2_.refs_0_.q_ref), channel_id=1, source_target_pairs={{0,1},{1,0},{2,3},{3,2},{4,5},{5,4},{6,7},{7,6},{8,9},{9,8},{10,11... | collective-permute-start | bytes 393224 | tf_op jit(solution)/shard_map/ppermute | solution.py:516
  72.9 4.2 %collective-permute-start.16 = (bf16[128,512]{1,0:T(8,128)(2,1)S(1)}, bf16[128,512]{1,0:T(8,128)(2,1)S(1)}, u32[]{:S(2)}, u32[]{:S(2)}) collective-permute-start(bf16[128,512]{1,0:T(8,128)(2,1)S(1)} %collective-permute-done.14.refs_1_), channel_id=1, source_target_pairs={{0,1},{1,0},{2,3},{3,2},{4,5},{5,4},{6,7},{7,6},{8,9},{9,8},{10,11... | collective-permute-start | bytes 393224 | tf_op jit(solution)/shard_map/ppermute | solution.py:516
  74.9 5.8 %collective-permute-start.25 = (bf16[128,512]{1,0:T(8,128)(2,1)S(1)}, bf16[128,512]{1,0:T(8,128)(2,1)S(1)}, u32[]{:S(2)}, u32[]{:S(2)}) collective-permute-start(bf16[128,512]{1,0:T(8,128)(2,1)S(1)} %get-tuple-element.84.refs_10_.refs_0_.q_ref), channel_id=1, source_target_pairs={{0,2},{1,3},{2,0},{3,1},{4,6},{5,7},{6,4},{7,5},{8,10},{9,11},{10,... | collective-permute-start | bytes 393224 | tf_op jit(solution)/shard_map/ppermute | solution.py:516
  80.8 10.3 %collective-permute-start.30 = (bf16[1,128,768]{2,1,0:T(8,128)(2,1)S(1)}, bf16[1,128,768]{2,1,0:T(8,128)(2,1)S(1)}, u32[]{:S(2)}, u32[]{:S(2)}) collective-permute-start(bf16[1,128,768]{2,1,0:T(8,128)(2,1)S(1)} %get-tuple-element.92), channel_id=1, source_target_pairs={{0,1},{1,0},{2,3},{3,2},{4,5},{5,4},{6,7},{7,6},{8,9},{9,8},{10,11... | collective-permute-start | bytes 589832 | tf_op jit(solution)/shard_map/ppermute | solution.py:516
  81.3 10.4 %collective-permute-start.31 = (bf16[1,128,768]{2,1,0:T(8,128)(2,1)S(1)}, bf16[1,128,768]{2,1,0:T(8,128)(2,1)S(1)}, u32[]{:S(2)}, u32[]{:S(2)}) collective-permute-start(bf16[1,128,768]{2,1,0:T(8,128)(2,1)S(1)} %fold.18.refs_3_), channel_id=1, source_target_pairs={{0,2},{1,3},{2,0},{3,1},{4,6},{5,7},{6,4},{7,5},{8,10},{9,11},{10,... | collective-permute-start | bytes 589832 | tf_op jit(solution)/shard_map/ppermute | solution.py:516
  86.6 6.0 %collective-permute-start.29 = (bf16[1,128,512]{2,1,0:T(8,128)(2,1)S(1)}, bf16[1,128,512]{2,1,0:T(8,128)(2,1)S(1)}, u32[]{:S(2)}, u32[]{:S(2)}) collective-permute-start(bf16[1,128,512]{2,1,0:T(8,128)(2,1)S(1)} %get-tuple-element.90), channel_id=1, source_target_pairs={{0,1},{1,0},{2,3},{3,2},{4,5},{5,4},{6,7},{7,6},{8,9},{9,8},{10,11... | collective-permute-start | bytes 393224 | tf_op jit(solution)/shard_map/ppermute | solution.py:516
  86.6 4.5 %collective-permute-start.22 = (bf16[128,256]{1,0:T(8,128)(2,1)S(1)}, bf16[128,256]{1,0:T(8,128)(2,1)S(1)}, u32[]{:S(2)}, u32[]{:S(2)}) collective-permute-start(bf16[128,256]{1,0:T(8,128)(2,1)S(1)} %get-tuple-element.86.refs_2_.refs_0_.q_ref), channel_id=1, source_target_pairs={{0,2},{1,3},{2,0},{3,1},{4,6},{5,7},{6,4},{7,5},{8,10},{9,11},{10,... | collective-permute-start | bytes 196616 | tf_op jit(solution)/shard_map/ppermute | solution.py:516
  87.2 5.6 %collective-permute-start.23 = (bf16[128,256]{1,0:T(8,128)(2,1)S(1)}, bf16[128,256]{1,0:T(8,128)(2,1)S(1)}, u32[]{:S(2)}, u32[]{:S(2)}) collective-permute-start(bf16[128,256]{1,0:T(8,128)(2,1)S(1)} %get-tuple-element.86.refs_2_.refs_0_.q_ref), channel_id=1, source_target_pairs={{0,1},{1,0},{2,3},{3,2},{4,5},{5,4},{6,7},{7,6},{8,9},{9,8},{10,11... | collective-permute-start | bytes 196616 | tf_op jit(solution)/shard_map/ppermute | solution.py:516
  91.2 6.2 %collective-permute-start.35 = (bf16[1,128,512]{2,1,0:T(8,128)(2,1)S(1)}, bf16[1,128,512]{2,1,0:T(8,128)(2,1)S(1)}, u32[]{:S(2)}, u32[]{:S(2)}) collective-permute-start(bf16[1,128,512]{2,1,0:T(8,128)(2,1)S(1)} %get-tuple-element.99), channel_id=1, source_target_pairs={{0,1},{1,0},{2,3},{3,2},{4,5},{5,4},{6,7},{7,6},{8,9},{9,8},{10,11... | collective-permute-start | bytes 393224 | tf_op jit(solution)/shard_map/ppermute | solution.py:516
  91.7 6.7 %collective-permute-start.36 = (bf16[1,128,512]{2,1,0:T(8,128)(2,1)S(1)}, bf16[1,128,512]{2,1,0:T(8,128)(2,1)S(1)}, u32[]{:S(2)}, u32[]{:S(2)}) collective-permute-start(bf16[1,128,512]{2,1,0:T(8,128)(2,1)S(1)} %fold.19.refs_10_), channel_id=1, source_target_pairs={{0,2},{1,3},{2,0},{3,1},{4,6},{5,7},{6,4},{7,5},{8,10},{9,11},{10,... | collective-permute-start | bytes 393224 | tf_op jit(solution)/shard_map/ppermute | solution.py:516
  94.9 3.9 %collective-permute-start.37 = (bf16[1,128,512]{2,1,0:T(8,128)(2,1)S(1)}, bf16[1,128,512]{2,1,0:T(8,128)(2,1)S(1)}, u32[]{:S(2)}, u32[]{:S(2)}) collective-permute-start(bf16[1,128,512]{2,1,0:T(8,128)(2,1)S(1)} %get-tuple-element.102), channel_id=1, source_target_pairs={{0,1},{1,0},{2,3},{3,2},{4,5},{5,4},{6,7},{7,6},{8,9},{9,8},{10,11... | collective-permute-start | bytes 393224 | tf_op jit(solution)/shard_map/ppermute | solution.py:516
  95.4 5.7 %collective-permute-start.38 = (bf16[1,128,512]{2,1,0:T(8,128)(2,1)S(1)}, bf16[1,128,512]{2,1,0:T(8,128)(2,1)S(1)}, u32[]{:S(2)}, u32[]{:S(2)}) collective-permute-start(bf16[1,128,512]{2,1,0:T(8,128)(2,1)S(1)} %fold.20.refs_10_), channel_id=1, source_target_pairs={{0,2},{1,3},{2,0},{3,1},{4,6},{5,7},{6,4},{7,5},{8,10},{9,11},{10,... | collective-permute-start | bytes 393224 | tf_op jit(solution)/shard_map/ppermute | solution.py:516
  97.0 4.5 %collective-permute-start.32 = (bf16[1,128,256]{2,1,0:T(8,128)(2,1)S(1)}, bf16[1,128,256]{2,1,0:T(8,128)(2,1)S(1)}, u32[]{:S(2)}, u32[]{:S(2)}) collective-permute-start(bf16[1,128,256]{2,1,0:T(8,128)(2,1)S(1)} %get-tuple-element.95), channel_id=1, source_target_pairs={{0,1},{1,0},{2,3},{3,2},{4,5},{5,4},{6,7},{7,6},{8,9},{9,8},{10,11... | collective-permute-start | bytes 196616 | tf_op jit(solution)/shard_map/ppermute | solution.py:516
  97.4 4.9 %collective-permute-start.34 = (bf16[1,128,256]{2,1,0:T(8,128)(2,1)S(1)}, bf16[1,128,256]{2,1,0:T(8,128)(2,1)S(1)}, u32[]{:S(2)}, u32[]{:S(2)}) collective-permute-start(bf16[1,128,256]{2,1,0:T(8,128)(2,1)S(1)} %fold.21.refs_3_), channel_id=1, source_target_pairs={{0,2},{1,3},{2,0},{3,1},{4,6},{5,7},{6,4},{7,5},{8,10},{9,11},{10,... | collective-permute-start | bytes 196616 | tf_op jit(solution)/shard_map/ppermute | solution.py:516
  106.4 4.5 %collective-permute-start.40 = (f32[8,128]{1,0:T(8,128)S(1)}, f32[8,128]{1,0:T(8,128)S(1)}, u32[]{:S(2)}, u32[]{:S(2)}) collective-permute-start(f32[8,128]{1,0:T(8,128)S(1)} %merge.1.refs_0_), channel_id=1, source_target_pairs={{0,8},{4,12},{8,0},{12,4},{1,9},{5,13},{9,1},{13,5},{2,10},{6,14},... | collective-permute-start | bytes 12296 | tf_op jit(solution)/shard_map/ppermute | solution.py:516
  111.3 8.8 %collective-permute-start.42 = (bf16[64,2048]{1,0:T(8,128)(2,1)S(1)}, bf16[64,2048]{1,0:T(8,128)(2,1)S(1)}, u32[]{:S(2)}, u32[]{:S(2)}) collective-permute-start(bf16[64,2048]{1,0:T(8,128)(2,1)S(1)} %get-tuple-element.109), channel_id=1, source_target_pairs={{0,2},{1,3},{2,0},{3,1},{4,6},{5,7},{6,4},{7,5},{8,10},{9,11},{10,... | collective-permute-start | bytes 786440 | tf_op jit(solution)/shard_map/ppermute | solution.py:516
  113.0 12.1 %collective-permute-start.41 = (bf16[64,2176]{1,0:T(8,128)(2,1)S(1)}, bf16[64,2176]{1,0:T(8,128)(2,1)S(1)}, u32[]{:S(2)}, u32[]{:S(2)}) collective-permute-start(bf16[64,2176]{1,0:T(8,128)(2,1)S(1)} %get-tuple-element.108), channel_id=1, source_target_pairs={{0,2},{1,3},{2,0},{3,1},{4,6},{5,7},{6,4},{7,5},{8,10},{9,11},{10,... | collective-permute-start | bytes 835592 | tf_op jit(solution)/shard_map/ppermute | solution.py:516
  113.4 7.3 %collective-permute-start.43 = (bf16[64,2048]{1,0:T(8,128)(2,1)S(1)}, bf16[64,2048]{1,0:T(8,128)(2,1)S(1)}, u32[]{:S(2)}, u32[]{:S(2)}) collective-permute-start(bf16[64,2048]{1,0:T(8,128)(2,1)S(1)} %get-tuple-element.109), channel_id=1, source_target_pairs={{0,1},{1,0},{2,3},{3,2},{4,5},{5,4},{6,7},{7,6},{8,9},{9,8},{10,11... | collective-permute-start | bytes 786440 | tf_op jit(solution)/shard_map/ppermute | solution.py:516
  120.1 10.7 %collective-permute-start.45 = (bf16[64,2176]{1,0:T(8,128)(2,1)S(1)}, bf16[64,2176]{1,0:T(8,128)(2,1)S(1)}, u32[]{:S(2)}, u32[]{:S(2)}) collective-permute-start(bf16[64,2176]{1,0:T(8,128)(2,1)S(1)} %get-tuple-element.108), channel_id=1, source_target_pairs={{0,1},{1,0},{2,3},{3,2},{4,5},{5,4},{6,7},{7,6},{8,9},{9,8},{10,11... | collective-permute-start | bytes 835592 | tf_op jit(solution)/shard_map/ppermute | solution.py:516
  125.1 5.8 %collective-permute-start.46 = (bf16[64,2176]{1,0:T(8,128)(2,1)S(1)}, bf16[64,2176]{1,0:T(8,128)(2,1)S(1)}, u32[]{:S(2)}, u32[]{:S(2)}) collective-permute-start(bf16[64,2176]{1,0:T(8,128)(2,1)S(1)} %tie.19), channel_id=1, source_target_pairs={{0,1},{1,0},{2,3},{3,2},{4,5},{5,4},{6,7},{7,6},{8,9},{9,8},{10,11... | collective-permute-start | bytes 835592 | tf_op jit(solution)/shard_map/ppermute | solution.py:516
  125.3 9.1 %collective-permute-start.49 = (bf16[2,4,16,1024]{3,2,1,0:T(8,128)(2,1)S(1)}, bf16[2,4,16,1024]{3,2,1,0:T(8,128)(2,1)S(1)}, u32[]{:S(2)}, u32[]{:S(2)}) collective-permute-start(bf16[2,4,16,1024]{3,2,1,0:T(8,128)(2,1)S(1)} %get-tuple-element.116), channel_id=1, source_target_pairs={{0,4},{4,0},{8,12},{12,8},{1,5},{5,1},{9,13},{13,9},{2,6},{6,2},{1... | collective-permute-start | bytes 786440 | tf_op jit(solution)/shard_map/ppermute | solution.py:516
  130.3 9.7 %collective-permute-start.47 = (bf16[2,4,16,1024]{3,2,1,0:T(8,128)(2,1)S(1)}, bf16[2,4,16,1024]{3,2,1,0:T(8,128)(2,1)S(1)}, u32[]{:S(2)}, u32[]{:S(2)}) collective-permute-start(bf16[2,4,16,1024]{3,2,1,0:T(8,128)(2,1)S(1)} %get-tuple-element.115), channel_id=1, source_target_pairs={{0,4},{4,0},{8,12},{12,8},{1,5},{5,1},{9,13},{13,9},{2,6},{6,2},{1... | collective-permute-start | bytes 786440 | tf_op jit(solution)/shard_map/ppermute | solution.py:516
  134.5 16.9 %collective-permute-start.51 = (bf16[2,4,16,1024]{3,2,1,0:T(8,128)(2,1)S(1)}, bf16[2,4,16,1024]{3,2,1,0:T(8,128)(2,1)S(1)}, u32[]{:S(2)}, u32[]{:S(2)}) collective-permute-start(bf16[2,4,16,1024]{3,2,1,0:T(8,128)(2,1)S(1)} %tie.21), channel_id=1, source_target_pairs={{0,4},{4,0},{8,12},{12,8},{1,5},{5,1},{9,13},{13,9},{2,6},{6,2},{1... | collective-permute-start | bytes 786440 | tf_op jit(solution)/shard_map/ppermute | solution.py:516
  140.1 16.5 %collective-permute-start.48 = (bf16[2,4,16,1024]{3,2,1,0:T(8,128)(2,1)S(1)}, bf16[2,4,16,1024]{3,2,1,0:T(8,128)(2,1)S(1)}, u32[]{:S(2)}, u32[]{:S(2)}) collective-permute-start(bf16[2,4,16,1024]{3,2,1,0:T(8,128)(2,1)S(1)} %tie.20), channel_id=1, source_target_pairs={{0,4},{4,0},{8,12},{12,8},{1,5},{5,1},{9,13},{13,9},{2,6},{6,2},{1... | collective-permute-start | bytes 786440 | tf_op jit(solution)/shard_map/ppermute | solution.py:516
  141.8 11.4 %collective-permute-start.50 = (bf16[1,4,16,1024]{3,2,1,0:T(8,128)(2,1)S(1)}, bf16[1,4,16,1024]{3,2,1,0:T(8,128)(2,1)S(1)}, u32[]{:S(2)}, u32[]{:S(2)}) collective-permute-start(bf16[1,4,16,1024]{3,2,1,0:T(8,128)(2,1)S(1)} %fold.22.refs_2_), channel_id=1, source_target_pairs={{0,8},{4,12},{8,0},{12,4},{1,9},{5,13},{9,1},{13,5},{2,10},{6,14},... | collective-permute-start | bytes 393224 | tf_op jit(solution)/shard_map/ppermute | solution.py:516
  144.6 14.4 %collective-permute-start.54 = (bf16[1,4,16,1024]{3,2,1,0:T(8,128)(2,1)S(1)}, bf16[1,4,16,1024]{3,2,1,0:T(8,128)(2,1)S(1)}, u32[]{:S(2)}, u32[]{:S(2)}) collective-permute-start(bf16[1,4,16,1024]{3,2,1,0:T(8,128)(2,1)S(1)} %fold.23.refs_2_), channel_id=1, source_target_pairs={{0,8},{4,12},{8,0},{12,4},{1,9},{5,13},{9,1},{13,5},{2,10},{6,14},... | collective-permute-start | bytes 393224 | tf_op jit(solution)/shard_map/ppermute | solution.py:516
  151.4 15.5 %collective-permute-start.53 = (bf16[1,4,16,1024]{3,2,1,0:T(8,128)(2,1)S(1)}, bf16[1,4,16,1024]{3,2,1,0:T(8,128)(2,1)S(1)}, u32[]{:S(2)}, u32[]{:S(2)}) collective-permute-start(bf16[1,4,16,1024]{3,2,1,0:T(8,128)(2,1)S(1)} %fold.24.refs_3_), channel_id=1, source_target_pairs={{0,8},{4,12},{8,0},{12,4},{1,9},{5,13},{9,1},{13,5},{2,10},{6,14},... | collective-permute-start | bytes 393224 | tf_op jit(solution)/shard_map/ppermute | solution.py:516
  156.8 12.7 %collective-permute-start.52 = (bf16[1,4,16,1024]{3,2,1,0:T(8,128)(2,1)S(1)}, bf16[1,4,16,1024]{3,2,1,0:T(8,128)(2,1)S(1)}, u32[]{:S(2)}, u32[]{:S(2)}) collective-permute-start(bf16[1,4,16,1024]{3,2,1,0:T(8,128)(2,1)S(1)} %fold.25.refs_4_), channel_id=1, source_target_pairs={{0,8},{4,12},{8,0},{12,4},{1,9},{5,13},{9,1},{13,5},{2,10},{6,14},... | collective-permute-start | bytes 393224 | tf_op jit(solution)/shard_map/ppermute | solution.py:516
  (17 other events, 89.0 us)

commit v14 on v13

--- a/solution.py
+++ b/solution.py
@@ -631,7 +631,7 @@
     gated = gate_rows(every, stat_width, atts, rests, chunks)
     columns = w_out.shape[1]
     straight = piece % 16 == 0 and zs & (zs - 1) == 0
-    out, last_out = None, []
+    out = None
     if not straight:
         for r, rows in enumerate(gated):
             whole = jnp.concatenate(gather(rows, "hist"))[:, :width]
@@ -643,27 +643,34 @@
     slots = [reverse(k, bits_of("head")) for k in range(zs)]
     groups = 2 if columns % 1024 == 0 else 1
     span = columns // groups
-    pieces, first_out, counts = [], [], [zs // 2] * 2 if zs > 1 else [1]
-    for r, rows in enumerate(gated):
-        blocks = gather(rows, "hist", first_out)
-        for g in range(groups):
-            own, *others = output(
-                index, slots, counts, blocks, w_out, g * span, span, last_out
-            )
-            before = pieces[-2][3] if len(pieces) > 1 else []
-            pieces.append((r, g, own, [swap(tie(x, before), "head", 0) for x in others]))
-            last_out, first_out = [own], first_out or [own]
-    closing, chain = [], last_out
-    for r, g, own, arrived in pieces:
+    counts = [zs // 2] * 2 if zs > 1 else [1]
+    plan = [(r, g) for r in range(chunks) for g in range(groups)]
+    chain, first_out, blocks, made, folded = [], [], {}, [], []
+
+    def fold_next():
+        own, arrived = made[len(folded)]
         terms, sent = scatter(own, arrived, "head", chain) if arrived else ([own], own)
-        chain = [sent]
-        closing.append((r, g, terms))
-        if len(closing) > 2:
-            out, mark = close(place, index, tokens, chunks, *closing.pop(0), out, chain)
-            chain = [mark]
-    for last_piece in closing:
-        out, mark = close(place, index, tokens, chunks, *last_piece, out, chain)
-        chain = [mark]
+        folded.append(terms)
+        return [sent]
+
+    for n, (r, g) in enumerate(plan):
+        if r not in blocks:
+            blocks[r] = gather(gated[r], "hist", first_out)
+        own, *others = output(index, slots, counts, blocks[r], w_out, g * span, span, chain)
+        before = made[n - 2][1] if n > 1 else []
+        before = before + [folded[0][-1]] if folded else before
+        made.append((own, [swap(tie(x, before), "head", 0) for x in others]))
+        chain, first_out = [own], first_out or [own]
+        if n == 2:
+            chain = fold_next()
+    closed = 0
+    while closed < len(plan):
+        if len(folded) < len(plan):
+            chain = fold_next()
+        if len(folded) > closed + 2 or len(folded) == len(plan):
+            r, g = plan[closed]
+            out, mark = close(place, index, tokens, chunks, r, g, folded[closed], out, chain)
+            chain, closed = [mark], closed + 1
     return out.reshape(cand // zs, -1)
 
 

time: 172 us -> 170 us (0.988)
  waiting for transfers between devices: 43.1 us -> 38.7 us
  starting transfers between devices: 41.9 us -> 44.2 us
    ppermute x55, waiting for transfers between devices: 43.1 us -> 38.7 us  [swap(): lax.ppermute(x, axis, [(i, i ^ 1 << bit) for i in range(lax.axis_size(axi...]
    ppermute x55, starting transfers between devices: 41.9 us -> 44.2 us  [swap(): lax.ppermute(x, axis, [(i, i ^ 1 << bit) for i in range(lax.axis_size(axi...]
where the time goes in v14:
time: 170 us
  Pallas kernels  83.5 us (49%)
  starting transfers between devices  44.2 us (26%)
  waiting for transfers between devices  38.7 us (23%)
  local copies, waits for them, and re-layouts  2.43 us (1%)
    ppermute x55, starting transfers between devices, swap(): lax.ppermute(x, axis, [(i, i ^ 1 << bit) for i in range(lax.axis_size(axi...  44.2 us
    ppermute x55, waiting for transfers between devices, swap(): lax.ppermute(x, axis, [(i, i ^ 1 << bit) for i in range(lax.axis_size(axi...  38.7 us
    pallas_call x5, Pallas kernels, project(): pl.pallas_call(functools.partial(project_kernel, parts, owners, len(after...  37.9 us
    pallas_call x4, Pallas kernels, output(): pl.pallas_call(functools.partial(output_kernel, owners, slots, len(after)...  13.9 us
    pallas_call x4, Pallas kernels, attend(): pl.pallas_call(functools.partial(attend_kernel, owners, len(counts)), gri...  12.5 us
    pallas_call x4, Pallas kernels, close(): pl.pallas_call(functools.partial(close_kernel, len(terms)), grid_spec=plt...  8.68 us
    pallas_call x13, Pallas kernels, fold(): pl.pallas_call(functools.partial(fold_kernel, len(terms)), grid=(steps,),...  4.77 us
    pallas_call x4, Pallas kernels, activate(): pl.pallas_call(functools.partial(activate_kernel, [len(terms) for terms i...  3.41 us
  transfers between devices with their start and end apart: 55, of which 16 were waited for; matrix products, arithmetic and copies ran while one was open for 0% of the time, Pallas kernels for 44%

profile of v14, /device:TPU:0, one launch (start us, length us, event | category | flops | bytes accessed | tf_op | source)
XLA Modules:
  0.0 169.5 jit_solution(1727719887503622244)
XLA Ops:
  0.0 5.5 %project.5 = (bf16[2,4,128,256]{3,2,1,0:T(8,128)(2,1)S(1)}, bf16[1,4,128,256]{3,2,1,0:T(8,128)(2,1)S(1)}, bf16[1,4,128,256]{3,2,1,0:T(8,128)(2,1)S(1)}) custom-call(s32[1]{0:T(128)} %bitcast.at_ref, bf16[4,2,4,16,2048]{4,3,2,1,0:T(8,128)(2,1)} %bitcast.57, bf16[4,2,4,16,2048]{4,3,2,1,0:T(8,128)(2,1)} %bitcast.58, bf16[4,2,4,16,2048]{4,3,2,1,0:T(8,128)(2,1)} %bitcast.59, ...), custom_call_target="tpu_custom_call" | custom-call | flops 1000 | bytes 1000 | tf_op jit(solution)/shard_map/project/pallas_call | solution.py:80
  6.1 8.7 %project.6 = (bf16[2,4,128,512]{3,2,1,0:T(8,128)(2,1)S(1)}, bf16[1,4,128,512]{3,2,1,0:T(8,128)(2,1)S(1)}, bf16[1,4,128,512]{3,2,1,0:T(8,128)(2,1)S(1)}) custom-call(s32[1]{0:T(128)} %bitcast.at_ref, bf16[4,2,4,16,2048]{4,3,2,1,0:T(8,128)(2,1)} %bitcast.61, bf16[4,2,4,16,2048]{4,3,2,1,0:T(8,128)(2,1)} %bitcast.62, bf16[4,2,4,16,2048]{4,3,2,1,0:T(8,128)(2,1)} %bitcast.63, ...), custom_call_target="tpu_custom_call" | custom-call | flops 1000 | bytes 1000 | tf_op jit(solution)/shard_map/project/pallas_call | solution.py:80
  15.8 3.0 %collective-permute-start.4 = (bf16[1,4,128,256]{3,2,1,0:T(8,128)(2,1)S(1)}, bf16[1,4,128,256]{3,2,1,0:T(8,128)(2,1)S(1)}, u32[]{:S(2)}, u32[]{:S(2)}) collective-permute-start(bf16[1,4,128,256]{3,2,1,0:T(8,128)(2,1)S(1)} %fold.13.refs_8_), channel_id=1, source_target_pairs={{0,2},{1,3},{2,0},{3,1},{4,6},{5,7},{6,4},{7,5},{8,10},{9,11},{10,... | collective-permute-start | bytes 786440 | tf_op jit(solution)/shard_map/ppermute | solution.py:516
  18.7 8.7 %project.7 = (bf16[2,4,128,512]{3,2,1,0:T(8,128)(2,1)S(1)}, bf16[1,4,128,512]{3,2,1,0:T(8,128)(2,1)S(1)}, bf16[1,4,128,512]{3,2,1,0:T(8,128)(2,1)S(1)}) custom-call(s32[1]{0:T(128)} %bitcast.at_ref, bf16[4,2,4,16,2048]{4,3,2,1,0:T(8,128)(2,1)} %bitcast.65, bf16[4,2,4,16,2048]{4,3,2,1,0:T(8,128)(2,1)} %bitcast.66, bf16[4,2,4,16,2048]{4,3,2,1,0:T(8,128)(2,1)} %bitcast.67, ...), custom_call_target="tpu_custom_call" | custom-call | flops 1000 | bytes 1000 | tf_op jit(solution)/shard_map/project/pallas_call | solution.py:80
  28.5 8.8 %project.8 = (bf16[2,4,128,512]{3,2,1,0:T(8,128)(2,1)S(1)}, bf16[1,4,128,512]{3,2,1,0:T(8,128)(2,1)S(1)}, bf16[1,4,128,512]{3,2,1,0:T(8,128)(2,1)S(1)}) custom-call(s32[1]{0:T(128)} %bitcast.at_ref, bf16[4,2,4,16,2048]{4,3,2,1,0:T(8,128)(2,1)} %bitcast.69, bf16[4,2,4,16,2048]{4,3,2,1,0:T(8,128)(2,1)} %bitcast.70, bf16[4,2,4,16,2048]{4,3,2,1,0:T(8,128)(2,1)} %bitcast.71, ...), custom_call_target="tpu_custom_call" | custom-call | flops 1000 | bytes 1000 | tf_op jit(solution)/shard_map/project/pallas_call | solution.py:80
  39.1 1.9 %collective-permute-start.12 = (bf16[1,4,128,512]{3,2,1,0:T(8,128)(2,1)}, bf16[1,4,128,512]{3,2,1,0:T(8,128)(2,1)}, u32[]{:S(2)}, u32[]{:S(2)}) collective-permute-start(bf16[1,4,128,512]{3,2,1,0:T(8,128)(2,1)} %fold.15.refs_6_), channel_id=1, source_target_pairs={{0,2},{1,3},{2,0},{3,1},{4,6},{5,7},{6,4},{7,5},{8,10},{9,11},{10,... | collective-permute-start | bytes 1572872 | tf_op jit(solution)/shard_map/ppermute | solution.py:516
  41.0 1.4 collective-permute-done.8.refs_5_
  44.2 1.7 %collective-permute-start.17 = (bf16[1,4,128,512]{3,2,1,0:T(8,128)(2,1)}, bf16[1,4,128,512]{3,2,1,0:T(8,128)(2,1)}, u32[]{:S(2)}, u32[]{:S(2)}) collective-permute-start(bf16[1,4,128,512]{3,2,1,0:T(8,128)(2,1)} %fold.16.refs_8_), channel_id=1, source_target_pairs={{0,2},{1,3},{2,0},{3,1},{4,6},{5,7},{6,4},{7,5},{8,10},{9,11},{10,... | collective-permute-start | bytes 1572872 | tf_op jit(solution)/shard_map/ppermute | solution.py:516
  46.0 6.2 %project.9 = (bf16[2,4,128,256]{3,2,1,0:T(8,128)(2,1)S(1)}, bf16[1,4,128,256]{3,2,1,0:T(8,128)(2,1)S(1)}, bf16[1,4,128,256]{3,2,1,0:T(8,128)(2,1)}) custom-call(s32[1]{0:T(128)} %bitcast.at_ref, bf16[4,2,4,16,2048]{4,3,2,1,0:T(8,128)(2,1)} %bitcast.73, bf16[4,2,4,16,2048]{4,3,2,1,0:T(8,128)(2,1)} %bitcast.74, bf16[4,2,4,16,2048]{4,3,2,1,0:T(8,128)(2,1)} %bitcast.75, ...), custom_call_target="tpu_custom_call" | custom-call | flops 1000 | bytes 1000 | tf_op jit(solution)/shard_map/project/pallas_call | solution.py:80
  53.4 5.0 %collective-permute-done.18.refs_1_ = bf16[128,768]{1,0:T(8,128)(2,1)S(1)} collective-permute-done((bf16[128,768]{1,0:T(8,128)(2,1)S(1)}, bf16[128,768]{1,0:T(8,128)(2,1)S(1)}, u32[]{:S(2)}, u32[]{:S(2)}) %collective-permute-start.18) | collective-permute-done | bytes 196640 | tf_op jit(solution)/shard_map/ppermute | solution.py:516
  58.5 1.0 copy-done.3
  59.6 1.4 activate.5
  61.0 1.1 fold.17.refs_10_
  62.1 4.1 %attend.4 = (bf16[2,128,768]{2,1,0:T(8,128)(2,1)S(1)}, bf16[1,128,768]{2,1,0:T(8,128)(2,1)S(1)}, bf16[1,128,768]{2,1,0:T(8,128)(2,1)S(1)}) custom-call(s32[1]{0:T(128)} %bitcast.at_ref, bf16[128,768]{1,0:T(8,128)(2,1)S(1)} %get-tuple-element.76.refs_2_.refs_0_.q_ref, bf16[128,768]{1,0:T(8,128)(2,1)S(1)} %collective-permute-done.18.refs_1_, ...), custom_call_target="tpu_custom_call" | custom-call | flops 1000 | bytes 1000 | tf_op jit(solution)/shard_map/attend/pallas_call | solution.py:262
  66.7 1.8 %collective-permute-start.14 = (bf16[128,512]{1,0:T(8,128)(2,1)S(1)}, bf16[128,512]{1,0:T(8,128)(2,1)S(1)}, u32[]{:S(2)}, u32[]{:S(2)}) collective-permute-start(bf16[128,512]{1,0:T(8,128)(2,1)S(1)} %get-tuple-element.81.refs_2_.refs_0_.q_ref), channel_id=1, source_target_pairs={{0,2},{1,3},{2,0},{3,1},{4,6},{5,7},{6,4},{7,5},{8,10},{9,11},{10,... | collective-permute-start | bytes 393224 | tf_op jit(solution)/shard_map/ppermute | solution.py:516
  68.8 4.0 %collective-permute-done.14.refs_1_ = bf16[128,512]{1,0:T(8,128)(2,1)S(1)} collective-permute-done((bf16[128,512]{1,0:T(8,128)(2,1)S(1)}, bf16[128,512]{1,0:T(8,128)(2,1)S(1)}, u32[]{:S(2)}, u32[]{:S(2)}) %collective-permute-start.14) | collective-permute-done | bytes 131104 | tf_op jit(solution)/shard_map/ppermute | solution.py:516
  73.6 1.4 activate.6
  74.9 2.1 %collective-permute-start.25 = (bf16[128,512]{1,0:T(8,128)(2,1)S(1)}, bf16[128,512]{1,0:T(8,128)(2,1)S(1)}, u32[]{:S(2)}, u32[]{:S(2)}) collective-permute-start(bf16[128,512]{1,0:T(8,128)(2,1)S(1)} %get-tuple-element.84.refs_10_.refs_0_.q_ref), channel_id=1, source_target_pairs={{0,2},{1,3},{2,0},{3,1},{4,6},{5,7},{6,4},{7,5},{8,10},{9,11},{10,... | collective-permute-start | bytes 393224 | tf_op jit(solution)/shard_map/ppermute | solution.py:516
  77.0 3.1 %attend.5 = (bf16[2,128,512]{2,1,0:T(8,128)(2,1)S(1)}, bf16[1,128,512]{2,1,0:T(8,128)(2,1)S(1)}, bf16[1,128,512]{2,1,0:T(8,128)(2,1)S(1)}) custom-call(s32[1]{0:T(128)} %bitcast.at_ref, bf16[128,512]{1,0:T(8,128)(2,1)S(1)} %get-tuple-element.81.refs_2_.refs_0_.q_ref, bf16[128,512]{1,0:T(8,128)(2,1)S(1)} %collective-permute-done.14.refs_1_, ...), custom_call_target="tpu_custom_call" | custom-call | flops 1000 | bytes 1000 | tf_op jit(solution)/shard_map/attend/pallas_call | solution.py:262
  81.3 1.7 collective-permute-start.31
  83.3 3.2 %attend.6 = (bf16[2,128,512]{2,1,0:T(8,128)(2,1)S(1)}, bf16[1,128,512]{2,1,0:T(8,128)(2,1)S(1)}, bf16[1,128,512]{2,1,0:T(8,128)(2,1)S(1)}) custom-call(s32[1]{0:T(128)} %bitcast.at_ref, bf16[128,512]{1,0:T(8,128)(2,1)S(1)} %get-tuple-element.84.refs_10_.refs_0_.q_ref, bf16[128,512]{1,0:T(8,128)(2,1)S(1)} %collective-permute-done.25.refs_1_, ...), custom_call_target="tpu_custom_call" | custom-call | flops 1000 | bytes 1000 | tf_op jit(solution)/shard_map/attend/pallas_call | solution.py:262
  87.2 3.9 %collective-permute-done.22.refs_1_ = bf16[128,256]{1,0:T(8,128)(2,1)S(1)} collective-permute-done((bf16[128,256]{1,0:T(8,128)(2,1)S(1)}, bf16[128,256]{1,0:T(8,128)(2,1)S(1)}, u32[]{:S(2)}, u32[]{:S(2)}) %collective-permute-start.22) | collective-permute-done | bytes 65568 | tf_op jit(solution)/shard_map/ppermute | solution.py:516
  92.8 2.0 %attend.7 = (bf16[2,128,256]{2,1,0:T(8,128)(2,1)S(1)}, bf16[1,128,256]{2,1,0:T(8,128)(2,1)S(1)}, bf16[1,128,256]{2,1,0:T(8,128)(2,1)S(1)}) custom-call(s32[1]{0:T(128)} %bitcast.at_ref, bf16[128,256]{1,0:T(8,128)(2,1)S(1)} %get-tuple-element.86.refs_2_.refs_0_.q_ref, bf16[128,256]{1,0:T(8,128)(2,1)S(1)} %collective-permute-done.22.refs_1_, ...), custom_call_target="tpu_custom_call" | custom-call | flops 1000 | bytes 1000 | tf_op jit(solution)/shard_map/attend/pallas_call | solution.py:262
  95.4 1.7 collective-permute-start.38
  98.8 2.3 %collective-permute-done.38.refs_2_ = bf16[1,128,512]{2,1,0:T(8,128)(2,1)S(1)} collective-permute-done((bf16[1,128,512]{2,1,0:T(8,128)(2,1)S(1)}, bf16[1,128,512]{2,1,0:T(8,128)(2,1)S(1)}, u32[]{:S(2)}, u32[]{:S(2)}) %collective-permute-start.38) | collective-permute-done | bytes 131104 | tf_op jit(solution)/shard_map/ppermute | solution.py:516
  102.7 1.8 %collective-permute-start.39 = (f32[8,128]{1,0:T(8,128)S(1)}, f32[8,128]{1,0:T(8,128)S(1)}, u32[]{:S(2)}, u32[]{:S(2)}) collective-permute-start(f32[8,128]{1,0:T(8,128)S(1)} %get-tuple-element.106.refs_0_), channel_id=1, source_target_pairs={{0,4},{4,0},{8,12},{12,8},{1,5},{5,1},{9,13},{13,9},{2,6},{6,2},{1... | collective-permute-start | bytes 12296 | tf_op jit(solution)/shard_map/ppermute | solution.py:516
  104.5 1.9 %collective-permute-done.39.refs_1_ = f32[8,128]{1,0:T(8,128)S(1)} collective-permute-done((f32[8,128]{1,0:T(8,128)S(1)}, f32[8,128]{1,0:T(8,128)S(1)}, u32[]{:S(2)}, u32[]{:S(2)}) %collective-permute-start.39) | collective-permute-done | bytes 4128 | tf_op jit(solution)/shard_map/ppermute | solution.py:516
  106.4 2.8 %collective-permute-start.40 = (f32[8,128]{1,0:T(8,128)S(1)}, f32[8,128]{1,0:T(8,128)S(1)}, u32[]{:S(2)}, u32[]{:S(2)}) collective-permute-start(f32[8,128]{1,0:T(8,128)S(1)} %merge.1.refs_0_), channel_id=1, source_target_pairs={{0,8},{4,12},{8,0},{12,4},{1,9},{5,13},{9,1},{13,5},{2,10},{6,14},... | collective-permute-start | bytes 12296 | tf_op jit(solution)/shard_map/ppermute | solution.py:516
  109.2 1.7 %collective-permute-done.40.refs_1_ = f32[8,128]{1,0:T(8,128)S(1)} collective-permute-done((f32[8,128]{1,0:T(8,128)S(1)}, f32[8,128]{1,0:T(8,128)S(1)}, u32[]{:S(2)}, u32[]{:S(2)}) %collective-permute-start.40) | collective-permute-done | bytes 4128 | tf_op jit(solution)/shard_map/ppermute | solution.py:516
  111.3 1.7 %collective-permute-start.42 = (bf16[64,2048]{1,0:T(8,128)(2,1)S(1)}, bf16[64,2048]{1,0:T(8,128)(2,1)S(1)}, u32[]{:S(2)}, u32[]{:S(2)}) collective-permute-start(bf16[64,2048]{1,0:T(8,128)(2,1)S(1)} %get-tuple-element.109), channel_id=1, source_target_pairs={{0,2},{1,3},{2,0},{3,1},{4,6},{5,7},{6,4},{7,5},{8,10},{9,11},{10,... | collective-permute-start | bytes 786440 | tf_op jit(solution)/shard_map/ppermute | solution.py:516
  113.4 6.7 %collective-permute-done.42 = bf16[64,2048]{1,0:T(8,128)(2,1)S(1)} collective-permute-done((bf16[64,2048]{1,0:T(8,128)(2,1)S(1)}, bf16[64,2048]{1,0:T(8,128)(2,1)S(1)}, u32[]{:S(2)}, u32[]{:S(2)}) %collective-permute-start.42) | collective-permute-done | bytes 262176 | tf_op jit(solution)/shard_map/ppermute | solution.py:516
  121.7 3.4 %output.4 = (bf16[2,4,16,1024]{3,2,1,0:T(8,128)(2,1)S(1)}, bf16[2,4,16,1024]{3,2,1,0:T(8,128)(2,1)S(1)}) custom-call(s32[1]{0:T(128)} %bitcast.3.index_ref, bf16[4,16,2048]{2,1,0:T(8,128)(2,1)S(1)} %bitcast.47, bf16[4,16,2048]{2,1,0:T(8,128)(2,1)S(1)} %bitcast.49, bf16[4,16,2048]{2,1,0:T(8,128)(2,1)S(1)} %bitcast.51, bf16[4,16,2048]{2,1,0:T(8,128)(2,1)S(1)} %bitcast.53, ...), custom_call_target="tpu_custom_call" | custom-call | flops 1000 | bytes 1000 | tf_op jit(solution)/shard_map/output/pallas_call | solution.py:444
  125.3 1.6 collective-permute-start.47
  126.9 3.4 %output.5 = (bf16[2,4,16,1024]{3,2,1,0:T(8,128)(2,1)S(1)}, bf16[2,4,16,1024]{3,2,1,0:T(8,128)(2,1)S(1)}) custom-call(s32[1]{0:T(128)} %bitcast.3.index_ref, bf16[4,16,2048]{2,1,0:T(8,128)(2,1)S(1)} %bitcast.48, bf16[4,16,2048]{2,1,0:T(8,128)(2,1)S(1)} %bitcast.50, bf16[4,16,2048]{2,1,0:T(8,128)(2,1)S(1)} %bitcast.52, bf16[4,16,2048]{2,1,0:T(8,128)(2,1)S(1)} %bitcast.54, ...), custom_call_target="tpu_custom_call" | custom-call | flops 1000 | bytes 1000 | tf_op jit(solution)/shard_map/output/pallas_call | solution.py:444
  130.9 3.5 %output.6 = (bf16[2,4,16,1024]{3,2,1,0:T(8,128)(2,1)S(1)}, bf16[2,4,16,1024]{3,2,1,0:T(8,128)(2,1)S(1)}) custom-call(s32[1]{0:T(128)} %bitcast.3.index_ref, bf16[4,16,2176]{2,1,0:T(8,128)(2,1)S(1)} %bitcast.41, bf16[4,16,2176]{2,1,0:T(8,128)(2,1)S(1)} %bitcast.39, bf16[4,16,2176]{2,1,0:T(8,128)(2,1)S(1)} %bitcast.43, bf16[4,16,2176]{2,1,0:T(8,128)(2,1)S(1)} %bitcast.45, ...), custom_call_target="tpu_custom_call" | custom-call | flops 1000 | bytes 1000 | tf_op jit(solution)/shard_map/output/pallas_call | solution.py:444
  134.6 2.6 %collective-permute-start.49 = (bf16[1,4,16,1024]{3,2,1,0:T(8,128)(2,1)S(1)}, bf16[1,4,16,1024]{3,2,1,0:T(8,128)(2,1)S(1)}, u32[]{:S(2)}, u32[]{:S(2)}) collective-permute-start(bf16[1,4,16,1024]{3,2,1,0:T(8,128)(2,1)S(1)} %fold.22.refs_5_), channel_id=1, source_target_pairs={{0,8},{4,12},{8,0},{12,4},{1,9},{5,13},{9,1},{13,5},{2,10},{6,14},... | collective-permute-start | bytes 393224 | tf_op jit(solution)/shard_map/ppermute | solution.py:516
  137.2 1.6 collective-permute-start.51
  138.8 3.5 %output.7 = (bf16[2,4,16,1024]{3,2,1,0:T(8,128)(2,1)S(1)}, bf16[2,4,16,1024]{3,2,1,0:T(8,128)(2,1)S(1)}) custom-call(s32[1]{0:T(128)} %bitcast.3.index_ref, bf16[4,16,2176]{2,1,0:T(8,128)(2,1)S(1)} %bitcast.42, bf16[4,16,2176]{2,1,0:T(8,128)(2,1)S(1)} %bitcast.40, bf16[4,16,2176]{2,1,0:T(8,128)(2,1)S(1)} %bitcast.44, bf16[4,16,2176]{2,1,0:T(8,128)(2,1)S(1)} %bitcast.46, ...), custom_call_target="tpu_custom_call" | custom-call | flops 1000 | bytes 1000 | tf_op jit(solution)/shard_map/output/pallas_call | solution.py:444
  142.9 2.6 %collective-permute-start.50 = (bf16[2,4,16,1024]{3,2,1,0:T(8,128)(2,1)S(1)}, bf16[2,4,16,1024]{3,2,1,0:T(8,128)(2,1)S(1)}, u32[]{:S(2)}, u32[]{:S(2)}) collective-permute-start(bf16[2,4,16,1024]{3,2,1,0:T(8,128)(2,1)S(1)} %tie.20), channel_id=1, source_target_pairs={{0,4},{4,0},{8,12},{12,8},{1,5},{5,1},{9,13},{13,9},{2,6},{6,2},{1... | collective-permute-start | bytes 786440 | tf_op jit(solution)/shard_map/ppermute | solution.py:516
  145.7 2.4 %collective-permute-start.54 = (bf16[1,4,16,1024]{3,2,1,0:T(8,128)(2,1)S(1)}, bf16[1,4,16,1024]{3,2,1,0:T(8,128)(2,1)S(1)}, u32[]{:S(2)}, u32[]{:S(2)}) collective-permute-start(bf16[1,4,16,1024]{3,2,1,0:T(8,128)(2,1)S(1)} %fold.23.refs_2_), channel_id=1, source_target_pairs={{0,8},{4,12},{8,0},{12,4},{1,9},{5,13},{9,1},{13,5},{2,10},{6,14},... | collective-permute-start | bytes 393224 | tf_op jit(solution)/shard_map/ppermute | solution.py:516
  148.1 1.9 %collective-permute-done.51.refs_1_ = bf16[2,4,16,1024]{3,2,1,0:T(8,128)(2,1)S(1)} collective-permute-done((bf16[2,4,16,1024]{3,2,1,0:T(8,128)(2,1)S(1)}, bf16[2,4,16,1024]{3,2,1,0:T(8,128)(2,1)S(1)}, u32[]{:S(2)}, u32[]{:S(2)}) %collective-permute-start.51) | collective-permute-done | bytes 262176 | tf_op jit(solution)/shard_map/ppermute | solution.py:516
  150.0 3.1 %collective-permute-start.53 = (bf16[1,4,16,1024]{3,2,1,0:T(8,128)(2,1)S(1)}, bf16[1,4,16,1024]{3,2,1,0:T(8,128)(2,1)S(1)}, u32[]{:S(2)}, u32[]{:S(2)}) collective-permute-start(bf16[1,4,16,1024]{3,2,1,0:T(8,128)(2,1)S(1)} %fold.24.refs_3_), channel_id=1, source_target_pairs={{0,8},{4,12},{8,0},{12,4},{1,9},{5,13},{9,1},{13,5},{2,10},{6,14},... | collective-permute-start | bytes 393224 | tf_op jit(solution)/shard_map/ppermute | solution.py:516
  153.2 2.2 %close.4 = (bf16[8,16,2048]{2,1,0:T(8,128)(2,1)}, f32[8,128]{1,0:T(8,128)S(1)}) custom-call(s32[2]{0:T(128)S(1)} %pad_add_fusion.1.at_ref, bf16[32,16,2048]{2,1,0:T(8,128)(2,1)} %bitcast.77, bf16[2,4,16,1024]{3,2,1,0:T(8,128)(2,1)S(1)} %get-tuple-element.110.refs_1_.refs_5_.refs_0_, bf16[2,4,16,1024]{3,2,1,0:T(8,128)(2,1)S(1)} %collective-permute-done.47.refs_1_, ...), custom_call_target="tpu_custom_call" | custom-call | flops 1000 | bytes 1000 | tf_op jit(solution)/shard_map/close/pallas_call | solution.py:481
  155.4 3.4 %collective-permute-done.50.refs_1_ = bf16[2,4,16,1024]{3,2,1,0:T(8,128)(2,1)S(1)} collective-permute-done((bf16[2,4,16,1024]{3,2,1,0:T(8,128)(2,1)S(1)}, bf16[2,4,16,1024]{3,2,1,0:T(8,128)(2,1)S(1)}, u32[]{:S(2)}, u32[]{:S(2)}) %collective-permute-start.50) | collective-permute-done | bytes 262176 | tf_op jit(solution)/shard_map/ppermute | solution.py:516
  159.0 2.2 %close.5 = (bf16[8,16,2048]{2,1,0:T(8,128)(2,1)}, f32[8,128]{1,0:T(8,128)S(1)}) custom-call(s32[2]{0:T(128)S(1)} %pad_add_fusion.1.at_ref, bf16[32,16,2048]{2,1,0:T(8,128)(2,1)} %bitcast.78, bf16[2,4,16,1024]{3,2,1,0:T(8,128)(2,1)S(1)} %get-tuple-element.112.refs_5_.refs_0_, ...), custom_call_target="tpu_custom_call", output_to_operand_aliasing={{0}: (5, {})} | custom-call | flops 1000 | bytes 1000 | tf_op jit(solution)/shard_map/close/pallas_call | solution.py:481
  161.2 3.7 %collective-permute-done.53.refs_2_ = bf16[1,4,16,1024]{3,2,1,0:T(8,128)(2,1)S(1)} collective-permute-done((bf16[1,4,16,1024]{3,2,1,0:T(8,128)(2,1)S(1)}, bf16[1,4,16,1024]{3,2,1,0:T(8,128)(2,1)S(1)}, u32[]{:S(2)}, u32[]{:S(2)}) %collective-permute-start.53) | collective-permute-done | bytes 131104 | tf_op jit(solution)/shard_map/ppermute | solution.py:516
  165.0 2.2 %close.6 = (bf16[8,16,2048]{2,1,0:T(8,128)(2,1)}, f32[8,128]{1,0:T(8,128)S(1)}) custom-call(s32[2]{0:T(128)S(1)} %pad_add_fusion.at_ref, bf16[32,16,2048]{2,1,0:T(8,128)(2,1)} %bitcast.79, bf16[2,4,16,1024]{3,2,1,0:T(8,128)(2,1)S(1)} %get-tuple-element.113.refs_2_.refs_0_, ...), custom_call_target="tpu_custom_call", output_to_operand_aliasing={{0}: (5, {})} | custom-call | flops 1000 | bytes 1000 | tf_op jit(solution)/shard_map/close/pallas_call | solution.py:481
  167.4 2.2 %close.7 = (bf16[8,16,2048]{2,1,0:T(8,128)(2,1)}, f32[8,128]{1,0:T(8,128)}) custom-call(s32[2]{0:T(128)S(1)} %pad_add_fusion.at_ref, bf16[32,16,2048]{2,1,0:T(8,128)(2,1)} %bitcast.80, bf16[2,4,16,1024]{3,2,1,0:T(8,128)(2,1)S(1)} %get-tuple-element.114.refs_2_.refs_0_, ...), custom_call_target="tpu_custom_call", output_to_operand_aliasing={{0}: (5, {})} | custom-call | flops 1000 | bytes 1000 | tf_op jit(solution)/shard_map/close/pallas_call | solution.py:481
  (136 shorter events, 21.2 us)
Async XLA Ops:
  5.5 9.4 %collective-permute-start = (bf16[1,4,128,256]{3,2,1,0:T(8,128)(2,1)S(1)}, bf16[1,4,128,256]{3,2,1,0:T(8,128)(2,1)S(1)}, u32[]{:S(2)}, u32[]{:S(2)}) collective-permute-start(bf16[1,4,128,256]{3,2,1,0:T(8,128)(2,1)S(1)} %get-tuple-element.68), channel_id=1, source_target_pairs={{0,1},{1,0},{2,3},{3,2},{4,5},{5,4},{6,7},{7,6},{8,9},{9,8},{10,11... | collective-permute-start | bytes 786440 | tf_op jit(solution)/shard_map/ppermute | solution.py:516
  6.1 8.8 %collective-permute-start.1 = (bf16[1,4,128,256]{3,2,1,0:T(8,128)(2,1)S(1)}, bf16[1,4,128,256]{3,2,1,0:T(8,128)(2,1)S(1)}, u32[]{:S(2)}, u32[]{:S(2)}) collective-permute-start(bf16[1,4,128,256]{3,2,1,0:T(8,128)(2,1)S(1)} %get-tuple-element.69), channel_id=1, source_target_pairs={{0,1},{1,0},{2,3},{3,2},{4,5},{5,4},{6,7},{7,6},{8,9},{9,8},{10,11... | collective-permute-start | bytes 786440 | tf_op jit(solution)/shard_map/ppermute | solution.py:516
  14.9 12.6 %collective-permute-start.3 = (bf16[1,4,128,512]{3,2,1,0:T(8,128)(2,1)S(1)}, bf16[1,4,128,512]{3,2,1,0:T(8,128)(2,1)S(1)}, u32[]{:S(2)}, u32[]{:S(2)}) collective-permute-start(bf16[1,4,128,512]{3,2,1,0:T(8,128)(2,1)S(1)} %tie.12), channel_id=1, source_target_pairs={{0,1},{1,0},{2,3},{3,2},{4,5},{5,4},{6,7},{7,6},{8,9},{9,8},{10,11... | collective-permute-start | bytes 1572872 | tf_op jit(solution)/shard_map/ppermute | solution.py:516
  15.4 12.1 %collective-permute-start.2 = (bf16[1,4,128,512]{3,2,1,0:T(8,128)(2,1)S(1)}, bf16[1,4,128,512]{3,2,1,0:T(8,128)(2,1)S(1)}, u32[]{:S(2)}, u32[]{:S(2)}) collective-permute-start(bf16[1,4,128,512]{3,2,1,0:T(8,128)(2,1)S(1)} %tie.11), channel_id=1, source_target_pairs={{0,1},{1,0},{2,3},{3,2},{4,5},{5,4},{6,7},{7,6},{8,9},{9,8},{10,11... | collective-permute-start | bytes 1572872 | tf_op jit(solution)/shard_map/ppermute | solution.py:516
  15.8 11.7 %collective-permute-start.4 = (bf16[1,4,128,256]{3,2,1,0:T(8,128)(2,1)S(1)}, bf16[1,4,128,256]{3,2,1,0:T(8,128)(2,1)S(1)}, u32[]{:S(2)}, u32[]{:S(2)}) collective-permute-start(bf16[1,4,128,256]{3,2,1,0:T(8,128)(2,1)S(1)} %fold.13.refs_8_), channel_id=1, source_target_pairs={{0,2},{1,3},{2,0},{3,1},{4,6},{5,7},{6,4},{7,5},{8,10},{9,11},{10,... | collective-permute-start | bytes 786440 | tf_op jit(solution)/shard_map/ppermute | solution.py:516
  27.5 9.8 %collective-permute-start.6 = (bf16[1,4,128,512]{3,2,1,0:T(8,128)(2,1)S(1)}, bf16[1,4,128,512]{3,2,1,0:T(8,128)(2,1)S(1)}, u32[]{:S(2)}, u32[]{:S(2)}) collective-permute-start(bf16[1,4,128,512]{3,2,1,0:T(8,128)(2,1)S(1)} %tie.14), channel_id=1, source_target_pairs={{0,1},{1,0},{2,3},{3,2},{4,5},{5,4},{6,7},{7,6},{8,9},{9,8},{10,11... | collective-permute-start | bytes 1572872 | tf_op jit(solution)/shard_map/ppermute | solution.py:516
  27.6 9.7 %collective-permute-start.5 = (bf16[1,4,128,512]{3,2,1,0:T(8,128)(2,1)S(1)}, bf16[1,4,128,512]{3,2,1,0:T(8,128)(2,1)S(1)}, u32[]{:S(2)}, u32[]{:S(2)}) collective-permute-start(bf16[1,4,128,512]{3,2,1,0:T(8,128)(2,1)S(1)} %tie.13), channel_id=1, source_target_pairs={{0,1},{1,0},{2,3},{3,2},{4,5},{5,4},{6,7},{7,6},{8,9},{9,8},{10,11... | collective-permute-start | bytes 1572872 | tf_op jit(solution)/shard_map/ppermute | solution.py:516
  28.4 14.0 %collective-permute-start.8 = (bf16[1,4,128,512]{3,2,1,0:T(8,128)(2,1)S(1)}, bf16[1,4,128,512]{3,2,1,0:T(8,128)(2,1)S(1)}, u32[]{:S(2)}, u32[]{:S(2)}) collective-permute-start(bf16[1,4,128,512]{3,2,1,0:T(8,128)(2,1)S(1)} %fold.14.refs_8_), channel_id=1, source_target_pairs={{0,2},{1,3},{2,0},{3,1},{4,6},{5,7},{6,4},{7,5},{8,10},{9,11},{10,... | collective-permute-start | bytes 1572872 | tf_op jit(solution)/shard_map/ppermute | solution.py:516
  37.3 5.9 %collective-permute-start.7 = (bf16[1,4,128,512]{3,2,1,0:T(8,128)(2,1)S(1)}, bf16[1,4,128,512]{3,2,1,0:T(8,128)(2,1)S(1)}, u32[]{:S(2)}, u32[]{:S(2)}) collective-permute-start(bf16[1,4,128,512]{3,2,1,0:T(8,128)(2,1)S(1)} %tie.15), channel_id=1, source_target_pairs={{0,1},{1,0},{2,3},{3,2},{4,5},{5,4},{6,7},{7,6},{8,9},{9,8},{10,11... | collective-permute-start | bytes 1572872 | tf_op jit(solution)/shard_map/ppermute | solution.py:516
  38.1 14.7 %collective-permute-start.9 = (bf16[1,4,128,512]{3,2,1,0:T(8,128)(2,1)S(1)}, bf16[1,4,128,512]{3,2,1,0:T(8,128)(2,1)S(1)}, u32[]{:S(2)}, u32[]{:S(2)}) collective-permute-start(bf16[1,4,128,512]{3,2,1,0:T(8,128)(2,1)S(1)} %tie.16), channel_id=1, source_target_pairs={{0,1},{1,0},{2,3},{3,2},{4,5},{5,4},{6,7},{7,6},{8,9},{9,8},{10,11... | collective-permute-start | bytes 1572872 | tf_op jit(solution)/shard_map/ppermute | solution.py:516
  39.1 19.4 %collective-permute-start.12 = (bf16[1,4,128,512]{3,2,1,0:T(8,128)(2,1)}, bf16[1,4,128,512]{3,2,1,0:T(8,128)(2,1)}, u32[]{:S(2)}, u32[]{:S(2)}) collective-permute-start(bf16[1,4,128,512]{3,2,1,0:T(8,128)(2,1)} %fold.15.refs_6_), channel_id=1, source_target_pairs={{0,2},{1,3},{2,0},{3,1},{4,6},{5,7},{6,4},{7,5},{8,10},{9,11},{10,... | collective-permute-start | bytes 1572872 | tf_op jit(solution)/shard_map/ppermute | solution.py:516
  42.9 15.5 %collective-permute-start.18 = (bf16[128,768]{1,0:T(8,128)(2,1)S(1)}, bf16[128,768]{1,0:T(8,128)(2,1)S(1)}, u32[]{:S(2)}, u32[]{:S(2)}) collective-permute-start(bf16[128,768]{1,0:T(8,128)(2,1)S(1)} %get-tuple-element.76.refs_2_.refs_0_.q_ref), channel_id=1, source_target_pairs={{0,2},{1,3},{2,0},{3,1},{4,6},{5,7},{6,4},{7,5},{8,10},{9,11},{10,... | collective-permute-start | bytes 589832 | tf_op jit(solution)/shard_map/ppermute | solution.py:516
  44.2 29.3 %collective-permute-start.17 = (bf16[1,4,128,512]{3,2,1,0:T(8,128)(2,1)}, bf16[1,4,128,512]{3,2,1,0:T(8,128)(2,1)}, u32[]{:S(2)}, u32[]{:S(2)}) collective-permute-start(bf16[1,4,128,512]{3,2,1,0:T(8,128)(2,1)} %fold.16.refs_8_), channel_id=1, source_target_pairs={{0,2},{1,3},{2,0},{3,1},{4,6},{5,7},{6,4},{7,5},{8,10},{9,11},{10,... | collective-permute-start | bytes 1572872 | tf_op jit(solution)/shard_map/ppermute | solution.py:516
  52.8 8.1 %collective-permute-start.11 = (bf16[1,4,128,256]{3,2,1,0:T(8,128)(2,1)}, bf16[1,4,128,256]{3,2,1,0:T(8,128)(2,1)}, u32[]{:S(2)}, u32[]{:S(2)}) collective-permute-start(bf16[1,4,128,256]{3,2,1,0:T(8,128)(2,1)} %tie.18), channel_id=1, source_target_pairs={{0,1},{1,0},{2,3},{3,2},{4,5},{5,4},{6,7},{7,6},{8,9},{9,8},{10,11... | collective-permute-start | bytes 786440 | tf_op jit(solution)/shard_map/ppermute | solution.py:516
  52.8 9.2 %collective-permute-start.19 = (bf16[128,768]{1,0:T(8,128)(2,1)S(1)}, bf16[128,768]{1,0:T(8,128)(2,1)}, u32[]{:S(2)}, u32[]{:S(2)}) collective-permute-start(bf16[128,768]{1,0:T(8,128)(2,1)S(1)} %get-tuple-element.76.refs_2_.refs_0_.q_ref), channel_id=1, source_target_pairs={{0,1},{1,0},{2,3},{3,2},{4,5},{5,4},{6,7},{7,6},{8,9},{9,8},{10,11... | collective-permute-start | bytes 589832 | tf_op jit(solution)/shard_map/ppermute | solution.py:516
  58.4 3.7 %collective-permute-start.20 = (bf16[128,768]{1,0:T(8,128)(2,1)S(1)}, bf16[128,768]{1,0:T(8,128)(2,1)}, u32[]{:S(2)}, u32[]{:S(2)}) collective-permute-start(bf16[128,768]{1,0:T(8,128)(2,1)S(1)} %collective-permute-done.18.refs_1_), channel_id=1, source_target_pairs={{0,1},{1,0},{2,3},{3,2},{4,5},{5,4},{6,7},{7,6},{8,9},{9,8},{10,11... | collective-permute-start | bytes 589832 | tf_op jit(solution)/shard_map/ppermute | solution.py:516
  66.2 6.7 %collective-permute-start.21 = (bf16[1,128,768]{2,1,0:T(8,128)(2,1)S(1)}, bf16[1,128,768]{2,1,0:T(8,128)(2,1)S(1)}, u32[]{:S(2)}, u32[]{:S(2)}) collective-permute-start(bf16[1,128,768]{2,1,0:T(8,128)(2,1)S(1)} %get-tuple-element.83), channel_id=1, source_target_pairs={{0,1},{1,0},{2,3},{3,2},{4,5},{5,4},{6,7},{7,6},{8,9},{9,8},{10,11... | collective-permute-start | bytes 589832 | tf_op jit(solution)/shard_map/ppermute | solution.py:516
  66.7 6.1 %collective-permute-start.14 = (bf16[128,512]{1,0:T(8,128)(2,1)S(1)}, bf16[128,512]{1,0:T(8,128)(2,1)S(1)}, u32[]{:S(2)}, u32[]{:S(2)}) collective-permute-start(bf16[128,512]{1,0:T(8,128)(2,1)S(1)} %get-tuple-element.81.refs_2_.refs_0_.q_ref), channel_id=1, source_target_pairs={{0,2},{1,3},{2,0},{3,1},{4,6},{5,7},{6,4},{7,5},{8,10},{9,11},{10,... | collective-permute-start | bytes 393224 | tf_op jit(solution)/shard_map/ppermute | solution.py:516
  68.5 12.3 %collective-permute-start.10 = (bf16[1,4,128,256]{3,2,1,0:T(8,128)(2,1)S(1)}, bf16[1,4,128,256]{3,2,1,0:T(8,128)(2,1)S(1)}, u32[]{:S(2)}, u32[]{:S(2)}) collective-permute-start(bf16[1,4,128,256]{3,2,1,0:T(8,128)(2,1)S(1)} %tie.17), channel_id=1, source_target_pairs={{0,1},{1,0},{2,3},{3,2},{4,5},{5,4},{6,7},{7,6},{8,9},{9,8},{10,11... | collective-permute-start | bytes 786440 | tf_op jit(solution)/shard_map/ppermute | solution.py:516
  68.6 12.7 %collective-permute-start.13 = (bf16[1,4,128,256]{3,2,1,0:T(8,128)(2,1)S(1)}, bf16[1,4,128,256]{3,2,1,0:T(8,128)(2,1)S(1)}, u32[]{:S(2)}, u32[]{:S(2)}) collective-permute-start(bf16[1,4,128,256]{3,2,1,0:T(8,128)(2,1)S(1)} %fold.17.refs_10_), channel_id=1, source_target_pairs={{0,2},{1,3},{2,0},{3,1},{4,6},{5,7},{6,4},{7,5},{8,10},{9,11},{10,... | collective-permute-start | bytes 786440 | tf_op jit(solution)/shard_map/ppermute | solution.py:516
  72.9 4.2 %collective-permute-start.15 = (bf16[128,512]{1,0:T(8,128)(2,1)S(1)}, bf16[128,512]{1,0:T(8,128)(2,1)S(1)}, u32[]{:S(2)}, u32[]{:S(2)}) collective-permute-start(bf16[128,512]{1,0:T(8,128)(2,1)S(1)} %get-tuple-element.81.refs_2_.refs_0_.q_ref), channel_id=1, source_target_pairs={{0,1},{1,0},{2,3},{3,2},{4,5},{5,4},{6,7},{7,6},{8,9},{9,8},{10,11... | collective-permute-start | bytes 393224 | tf_op jit(solution)/shard_map/ppermute | solution.py:516
  72.9 4.2 %collective-permute-start.16 = (bf16[128,512]{1,0:T(8,128)(2,1)S(1)}, bf16[128,512]{1,0:T(8,128)(2,1)S(1)}, u32[]{:S(2)}, u32[]{:S(2)}) collective-permute-start(bf16[128,512]{1,0:T(8,128)(2,1)S(1)} %collective-permute-done.14.refs_1_), channel_id=1, source_target_pairs={{0,1},{1,0},{2,3},{3,2},{4,5},{5,4},{6,7},{7,6},{8,9},{9,8},{10,11... | collective-permute-start | bytes 393224 | tf_op jit(solution)/shard_map/ppermute | solution.py:516
  74.9 5.8 %collective-permute-start.25 = (bf16[128,512]{1,0:T(8,128)(2,1)S(1)}, bf16[128,512]{1,0:T(8,128)(2,1)S(1)}, u32[]{:S(2)}, u32[]{:S(2)}) collective-permute-start(bf16[128,512]{1,0:T(8,128)(2,1)S(1)} %get-tuple-element.84.refs_10_.refs_0_.q_ref), channel_id=1, source_target_pairs={{0,2},{1,3},{2,0},{3,1},{4,6},{5,7},{6,4},{7,5},{8,10},{9,11},{10,... | collective-permute-start | bytes 393224 | tf_op jit(solution)/shard_map/ppermute | solution.py:516
  80.8 10.3 %collective-permute-start.30 = (bf16[1,128,768]{2,1,0:T(8,128)(2,1)S(1)}, bf16[1,128,768]{2,1,0:T(8,128)(2,1)S(1)}, u32[]{:S(2)}, u32[]{:S(2)}) collective-permute-start(bf16[1,128,768]{2,1,0:T(8,128)(2,1)S(1)} %get-tuple-element.92), channel_id=1, source_target_pairs={{0,1},{1,0},{2,3},{3,2},{4,5},{5,4},{6,7},{7,6},{8,9},{9,8},{10,11... | collective-permute-start | bytes 589832 | tf_op jit(solution)/shard_map/ppermute | solution.py:516
  81.3 10.4 %collective-permute-start.31 = (bf16[1,128,768]{2,1,0:T(8,128)(2,1)S(1)}, bf16[1,128,768]{2,1,0:T(8,128)(2,1)S(1)}, u32[]{:S(2)}, u32[]{:S(2)}) collective-permute-start(bf16[1,128,768]{2,1,0:T(8,128)(2,1)S(1)} %fold.18.refs_3_), channel_id=1, source_target_pairs={{0,2},{1,3},{2,0},{3,1},{4,6},{5,7},{6,4},{7,5},{8,10},{9,11},{10,... | collective-permute-start | bytes 589832 | tf_op jit(solution)/shard_map/ppermute | solution.py:516
  86.6 6.0 %collective-permute-start.29 = (bf16[1,128,512]{2,1,0:T(8,128)(2,1)S(1)}, bf16[1,128,512]{2,1,0:T(8,128)(2,1)S(1)}, u32[]{:S(2)}, u32[]{:S(2)}) collective-permute-start(bf16[1,128,512]{2,1,0:T(8,128)(2,1)S(1)} %get-tuple-element.90), channel_id=1, source_target_pairs={{0,1},{1,0},{2,3},{3,2},{4,5},{5,4},{6,7},{7,6},{8,9},{9,8},{10,11... | collective-permute-start | bytes 393224 | tf_op jit(solution)/shard_map/ppermute | solution.py:516
  86.6 4.5 %collective-permute-start.22 = (bf16[128,256]{1,0:T(8,128)(2,1)S(1)}, bf16[128,256]{1,0:T(8,128)(2,1)S(1)}, u32[]{:S(2)}, u32[]{:S(2)}) collective-permute-start(bf16[128,256]{1,0:T(8,128)(2,1)S(1)} %get-tuple-element.86.refs_2_.refs_0_.q_ref), channel_id=1, source_target_pairs={{0,2},{1,3},{2,0},{3,1},{4,6},{5,7},{6,4},{7,5},{8,10},{9,11},{10,... | collective-permute-start | bytes 196616 | tf_op jit(solution)/shard_map/ppermute | solution.py:516
  87.2 5.6 %collective-permute-start.23 = (bf16[128,256]{1,0:T(8,128)(2,1)S(1)}, bf16[128,256]{1,0:T(8,128)(2,1)S(1)}, u32[]{:S(2)}, u32[]{:S(2)}) collective-permute-start(bf16[128,256]{1,0:T(8,128)(2,1)S(1)} %get-tuple-element.86.refs_2_.refs_0_.q_ref), channel_id=1, source_target_pairs={{0,1},{1,0},{2,3},{3,2},{4,5},{5,4},{6,7},{7,6},{8,9},{9,8},{10,11... | collective-permute-start | bytes 196616 | tf_op jit(solution)/shard_map/ppermute | solution.py:516
  91.2 6.2 %collective-permute-start.35 = (bf16[1,128,512]{2,1,0:T(8,128)(2,1)S(1)}, bf16[1,128,512]{2,1,0:T(8,128)(2,1)S(1)}, u32[]{:S(2)}, u32[]{:S(2)}) collective-permute-start(bf16[1,128,512]{2,1,0:T(8,128)(2,1)S(1)} %get-tuple-element.99), channel_id=1, source_target_pairs={{0,1},{1,0},{2,3},{3,2},{4,5},{5,4},{6,7},{7,6},{8,9},{9,8},{10,11... | collective-permute-start | bytes 393224 | tf_op jit(solution)/shard_map/ppermute | solution.py:516
  91.7 6.7 %collective-permute-start.36 = (bf16[1,128,512]{2,1,0:T(8,128)(2,1)S(1)}, bf16[1,128,512]{2,1,0:T(8,128)(2,1)S(1)}, u32[]{:S(2)}, u32[]{:S(2)}) collective-permute-start(bf16[1,128,512]{2,1,0:T(8,128)(2,1)S(1)} %fold.19.refs_10_), channel_id=1, source_target_pairs={{0,2},{1,3},{2,0},{3,1},{4,6},{5,7},{6,4},{7,5},{8,10},{9,11},{10,... | collective-permute-start | bytes 393224 | tf_op jit(solution)/shard_map/ppermute | solution.py:516
  94.9 3.9 %collective-permute-start.37 = (bf16[1,128,512]{2,1,0:T(8,128)(2,1)S(1)}, bf16[1,128,512]{2,1,0:T(8,128)(2,1)S(1)}, u32[]{:S(2)}, u32[]{:S(2)}) collective-permute-start(bf16[1,128,512]{2,1,0:T(8,128)(2,1)S(1)} %get-tuple-element.102), channel_id=1, source_target_pairs={{0,1},{1,0},{2,3},{3,2},{4,5},{5,4},{6,7},{7,6},{8,9},{9,8},{10,11... | collective-permute-start | bytes 393224 | tf_op jit(solution)/shard_map/ppermute | solution.py:516
  95.4 5.7 %collective-permute-start.38 = (bf16[1,128,512]{2,1,0:T(8,128)(2,1)S(1)}, bf16[1,128,512]{2,1,0:T(8,128)(2,1)S(1)}, u32[]{:S(2)}, u32[]{:S(2)}) collective-permute-start(bf16[1,128,512]{2,1,0:T(8,128)(2,1)S(1)} %fold.20.refs_10_), channel_id=1, source_target_pairs={{0,2},{1,3},{2,0},{3,1},{4,6},{5,7},{6,4},{7,5},{8,10},{9,11},{10,... | collective-permute-start | bytes 393224 | tf_op jit(solution)/shard_map/ppermute | solution.py:516
  97.0 4.5 %collective-permute-start.32 = (bf16[1,128,256]{2,1,0:T(8,128)(2,1)S(1)}, bf16[1,128,256]{2,1,0:T(8,128)(2,1)S(1)}, u32[]{:S(2)}, u32[]{:S(2)}) collective-permute-start(bf16[1,128,256]{2,1,0:T(8,128)(2,1)S(1)} %get-tuple-element.95), channel_id=1, source_target_pairs={{0,1},{1,0},{2,3},{3,2},{4,5},{5,4},{6,7},{7,6},{8,9},{9,8},{10,11... | collective-permute-start | bytes 196616 | tf_op jit(solution)/shard_map/ppermute | solution.py:516
  97.4 4.9 %collective-permute-start.34 = (bf16[1,128,256]{2,1,0:T(8,128)(2,1)S(1)}, bf16[1,128,256]{2,1,0:T(8,128)(2,1)S(1)}, u32[]{:S(2)}, u32[]{:S(2)}) collective-permute-start(bf16[1,128,256]{2,1,0:T(8,128)(2,1)S(1)} %fold.21.refs_3_), channel_id=1, source_target_pairs={{0,2},{1,3},{2,0},{3,1},{4,6},{5,7},{6,4},{7,5},{8,10},{9,11},{10,... | collective-permute-start | bytes 196616 | tf_op jit(solution)/shard_map/ppermute | solution.py:516
  106.4 4.5 %collective-permute-start.40 = (f32[8,128]{1,0:T(8,128)S(1)}, f32[8,128]{1,0:T(8,128)S(1)}, u32[]{:S(2)}, u32[]{:S(2)}) collective-permute-start(f32[8,128]{1,0:T(8,128)S(1)} %merge.1.refs_0_), channel_id=1, source_target_pairs={{0,8},{4,12},{8,0},{12,4},{1,9},{5,13},{9,1},{13,5},{2,10},{6,14},... | collective-permute-start | bytes 12296 | tf_op jit(solution)/shard_map/ppermute | solution.py:516
  111.3 8.8 %collective-permute-start.42 = (bf16[64,2048]{1,0:T(8,128)(2,1)S(1)}, bf16[64,2048]{1,0:T(8,128)(2,1)S(1)}, u32[]{:S(2)}, u32[]{:S(2)}) collective-permute-start(bf16[64,2048]{1,0:T(8,128)(2,1)S(1)} %get-tuple-element.109), channel_id=1, source_target_pairs={{0,2},{1,3},{2,0},{3,1},{4,6},{5,7},{6,4},{7,5},{8,10},{9,11},{10,... | collective-permute-start | bytes 786440 | tf_op jit(solution)/shard_map/ppermute | solution.py:516
  113.0 12.1 %collective-permute-start.41 = (bf16[64,2176]{1,0:T(8,128)(2,1)S(1)}, bf16[64,2176]{1,0:T(8,128)(2,1)S(1)}, u32[]{:S(2)}, u32[]{:S(2)}) collective-permute-start(bf16[64,2176]{1,0:T(8,128)(2,1)S(1)} %get-tuple-element.108), channel_id=1, source_target_pairs={{0,2},{1,3},{2,0},{3,1},{4,6},{5,7},{6,4},{7,5},{8,10},{9,11},{10,... | collective-permute-start | bytes 835592 | tf_op jit(solution)/shard_map/ppermute | solution.py:516
  113.4 7.3 %collective-permute-start.43 = (bf16[64,2048]{1,0:T(8,128)(2,1)S(1)}, bf16[64,2048]{1,0:T(8,128)(2,1)S(1)}, u32[]{:S(2)}, u32[]{:S(2)}) collective-permute-start(bf16[64,2048]{1,0:T(8,128)(2,1)S(1)} %get-tuple-element.109), channel_id=1, source_target_pairs={{0,1},{1,0},{2,3},{3,2},{4,5},{5,4},{6,7},{7,6},{8,9},{9,8},{10,11... | collective-permute-start | bytes 786440 | tf_op jit(solution)/shard_map/ppermute | solution.py:516
  120.1 10.7 %collective-permute-start.45 = (bf16[64,2176]{1,0:T(8,128)(2,1)S(1)}, bf16[64,2176]{1,0:T(8,128)(2,1)S(1)}, u32[]{:S(2)}, u32[]{:S(2)}) collective-permute-start(bf16[64,2176]{1,0:T(8,128)(2,1)S(1)} %get-tuple-element.108), channel_id=1, source_target_pairs={{0,1},{1,0},{2,3},{3,2},{4,5},{5,4},{6,7},{7,6},{8,9},{9,8},{10,11... | collective-permute-start | bytes 835592 | tf_op jit(solution)/shard_map/ppermute | solution.py:516
  125.1 5.8 %collective-permute-start.46 = (bf16[64,2176]{1,0:T(8,128)(2,1)S(1)}, bf16[64,2176]{1,0:T(8,128)(2,1)S(1)}, u32[]{:S(2)}, u32[]{:S(2)}) collective-permute-start(bf16[64,2176]{1,0:T(8,128)(2,1)S(1)} %tie.19), channel_id=1, source_target_pairs={{0,1},{1,0},{2,3},{3,2},{4,5},{5,4},{6,7},{7,6},{8,9},{9,8},{10,11... | collective-permute-start | bytes 835592 | tf_op jit(solution)/shard_map/ppermute | solution.py:516
  125.3 9.1 %collective-permute-start.47 = (bf16[2,4,16,1024]{3,2,1,0:T(8,128)(2,1)S(1)}, bf16[2,4,16,1024]{3,2,1,0:T(8,128)(2,1)S(1)}, u32[]{:S(2)}, u32[]{:S(2)}) collective-permute-start(bf16[2,4,16,1024]{3,2,1,0:T(8,128)(2,1)S(1)} %get-tuple-element.111), channel_id=1, source_target_pairs={{0,4},{4,0},{8,12},{12,8},{1,5},{5,1},{9,13},{13,9},{2,6},{6,2},{1... | collective-permute-start | bytes 786440 | tf_op jit(solution)/shard_map/ppermute | solution.py:516
  130.3 12.5 %collective-permute-start.48 = (bf16[2,4,16,1024]{3,2,1,0:T(8,128)(2,1)S(1)}, bf16[2,4,16,1024]{3,2,1,0:T(8,128)(2,1)S(1)}, u32[]{:S(2)}, u32[]{:S(2)}) collective-permute-start(bf16[2,4,16,1024]{3,2,1,0:T(8,128)(2,1)S(1)} %get-tuple-element.116), channel_id=1, source_target_pairs={{0,4},{4,0},{8,12},{12,8},{1,5},{5,1},{9,13},{13,9},{2,6},{6,2},{1... | collective-permute-start | bytes 786440 | tf_op jit(solution)/shard_map/ppermute | solution.py:516
  134.6 8.3 %collective-permute-start.49 = (bf16[1,4,16,1024]{3,2,1,0:T(8,128)(2,1)S(1)}, bf16[1,4,16,1024]{3,2,1,0:T(8,128)(2,1)S(1)}, u32[]{:S(2)}, u32[]{:S(2)}) collective-permute-start(bf16[1,4,16,1024]{3,2,1,0:T(8,128)(2,1)S(1)} %fold.22.refs_5_), channel_id=1, source_target_pairs={{0,8},{4,12},{8,0},{12,4},{1,9},{5,13},{9,1},{13,5},{2,10},{6,14},... | collective-permute-start | bytes 393224 | tf_op jit(solution)/shard_map/ppermute | solution.py:516
  137.2 12.7 %collective-permute-start.51 = (bf16[2,4,16,1024]{3,2,1,0:T(8,128)(2,1)S(1)}, bf16[2,4,16,1024]{3,2,1,0:T(8,128)(2,1)S(1)}, u32[]{:S(2)}, u32[]{:S(2)}) collective-permute-start(bf16[2,4,16,1024]{3,2,1,0:T(8,128)(2,1)S(1)} %tie.21), channel_id=1, source_target_pairs={{0,4},{4,0},{8,12},{12,8},{1,5},{5,1},{9,13},{13,9},{2,6},{6,2},{1... | collective-permute-start | bytes 786440 | tf_op jit(solution)/shard_map/ppermute | solution.py:516
  142.9 15.8 %collective-permute-start.50 = (bf16[2,4,16,1024]{3,2,1,0:T(8,128)(2,1)S(1)}, bf16[2,4,16,1024]{3,2,1,0:T(8,128)(2,1)S(1)}, u32[]{:S(2)}, u32[]{:S(2)}) collective-permute-start(bf16[2,4,16,1024]{3,2,1,0:T(8,128)(2,1)S(1)} %tie.20), channel_id=1, source_target_pairs={{0,4},{4,0},{8,12},{12,8},{1,5},{5,1},{9,13},{13,9},{2,6},{6,2},{1... | collective-permute-start | bytes 786440 | tf_op jit(solution)/shard_map/ppermute | solution.py:516
  145.7 13.4 %collective-permute-start.54 = (bf16[1,4,16,1024]{3,2,1,0:T(8,128)(2,1)S(1)}, bf16[1,4,16,1024]{3,2,1,0:T(8,128)(2,1)S(1)}, u32[]{:S(2)}, u32[]{:S(2)}) collective-permute-start(bf16[1,4,16,1024]{3,2,1,0:T(8,128)(2,1)S(1)} %fold.23.refs_2_), channel_id=1, source_target_pairs={{0,8},{4,12},{8,0},{12,4},{1,9},{5,13},{9,1},{13,5},{2,10},{6,14},... | collective-permute-start | bytes 393224 | tf_op jit(solution)/shard_map/ppermute | solution.py:516
  150.0 14.9 %collective-permute-start.53 = (bf16[1,4,16,1024]{3,2,1,0:T(8,128)(2,1)S(1)}, bf16[1,4,16,1024]{3,2,1,0:T(8,128)(2,1)S(1)}, u32[]{:S(2)}, u32[]{:S(2)}) collective-permute-start(bf16[1,4,16,1024]{3,2,1,0:T(8,128)(2,1)S(1)} %fold.24.refs_3_), channel_id=1, source_target_pairs={{0,8},{4,12},{8,0},{12,4},{1,9},{5,13},{9,1},{13,5},{2,10},{6,14},... | collective-permute-start | bytes 393224 | tf_op jit(solution)/shard_map/ppermute | solution.py:516
  158.9 8.5 %collective-permute-start.52 = (bf16[1,4,16,1024]{3,2,1,0:T(8,128)(2,1)S(1)}, bf16[1,4,16,1024]{3,2,1,0:T(8,128)(2,1)S(1)}, u32[]{:S(2)}, u32[]{:S(2)}) collective-permute-start(bf16[1,4,16,1024]{3,2,1,0:T(8,128)(2,1)S(1)} %fold.25.refs_4_), channel_id=1, source_target_pairs={{0,8},{4,12},{8,0},{12,4},{1,9},{5,13},{9,1},{13,5},{2,10},{6,14},... | collective-permute-start | bytes 393224 | tf_op jit(solution)/shard_map/ppermute | solution.py:516
  (17 other events, 89.0 us)

commit v15 on v14

--- a/solution.py
+++ b/solution.py
@@ -464,42 +464,51 @@
     )
 
 
-def close_kernel(count, at_ref, t_ref, *refs):
+def close_kernel(counts, at_ref, t_ref, *refs):
     out_ref, mark_ref = refs[-2:]
     mark_ref[...] = jnp.zeros_like(mark_ref)
-    for p in range(out_ref.shape[0]):
-        total = t_ref[p].astype(f32)
-        for term in refs[:count]:
-            total = total + term[0, p ^ at_ref[0]].astype(f32)
-        out_ref[p] = total.astype(bf16)
-
-
-def close(place, index, tokens, chunks, r, g, terms, out, after):
-    _, owners, piece, span = terms[0].shape
+    first, column = 0, 0
+    for count in counts:
+        terms = refs[first:first + count]
+        span = terms[0].shape[-1]
+        at = slice(column, column + span)
+        for p in range(out_ref.shape[0]):
+            total = t_ref[p, :, at].astype(f32)
+            for term in terms:
+                total = total + term[0, p ^ at_ref[0]].astype(f32)
+            out_ref[p, :, at] = total.astype(bf16)
+        first += count
+        column += span
+
+
+def close(place, index, tokens, chunks, r, groups, out, after):
+    _, owners, piece, _ = groups[0][0].shape
+    width = tokens.shape[1]
     at = jnp.stack([place, index * chunks + r]).astype(jnp.int32)
+    flat = [term for terms in groups for term in terms]
     into = [] if out is None else [out]
     return pl.pallas_call(
-        functools.partial(close_kernel, len(terms)),
+        functools.partial(close_kernel, [len(terms) for terms in groups]),
         grid_spec=pltpu.PrefetchScalarGridSpec(
             num_scalar_prefetch=1,
             grid=(1,),
-            in_specs=[pl.BlockSpec((owners, piece, span), lambda j, at: (at[1], 0, g))]
-            + [pl.BlockSpec((1,) + t.shape[1:], lambda j, at: (0, 0, 0, 0)) for t in terms]
+            in_specs=[pl.BlockSpec((owners, piece, width), lambda j, at: (at[1], 0, 0))]
+            + [pl.BlockSpec((1,) + t.shape[1:], lambda j, at: (0, 0, 0, 0)) for t in flat]
             + anywhere(into) + anywhere(after),
             out_specs=(
-                pl.BlockSpec((owners, piece, span), lambda j, at: (r, 0, g)),
+                pl.BlockSpec((owners, piece, width), lambda j, at: (r, 0, 0)),
                 pl.BlockSpec((8, DH), lambda j, at: (0, 0)),
             ),
         ),
         out_shape=(
-            jax.ShapeDtypeStruct((chunks * owners, piece, tokens.shape[1]), bf16),
+            jax.ShapeDtypeStruct((chunks * owners, piece, width), bf16),
             jax.ShapeDtypeStruct((8, DH), f32),
         ),
-        input_output_aliases={} if out is None else {2 + len(terms): 0},
+        input_output_aliases={} if out is None else {2 + len(flat): 0},
         compiler_params=params(),
         cost_estimate=LIGHT,
         name="close",
-    )(at, far(tokens.reshape(-1, piece, tokens.shape[1])), *terms, *into, *after)
+    )(at, far(tokens.reshape(-1, piece, width)), *flat, *into, *after)
 
 
 def bits_of(axis):
@@ -638,13 +647,15 @@
             whole = jnp.dot(whole, w_out, preferred_element_type=f32).astype(bf16)
             whole = whole.reshape(owners, zs, piece, -1).swapaxes(0, 1)
             whole = lax.psum_scatter(whole, "head", scatter_dimension=0, tiled=True)
-            out, _ = close(place, index, tokens, chunks, r, 0, [whole], out, [])
+            out, _ = close(place, index, tokens, chunks, r, [[whole]], out, [])
         return out.reshape(cand // zs, -1)
     slots = [reverse(k, bits_of("head")) for k in range(zs)]
-    groups = 2 if columns % 1024 == 0 else 1
-    span = columns // groups
+    unit = columns // 8
+    spans = [[columns]] * chunks
+    if unit % (2 * DH) == 0 and chunks == 2:
+        spans = [[4 * unit, 4 * unit], [5 * unit, 3 * unit]]
     counts = [zs // 2] * 2 if zs > 1 else [1]
-    plan = [(r, g) for r in range(chunks) for g in range(groups)]
+    plan = [(r, sum(row[:g]), span) for r, row in enumerate(spans) for g, span in enumerate(row)]
     chain, first_out, blocks, made, folded = [], [], {}, [], []
 
     def fold_next():
@@ -653,24 +664,23 @@
         folded.append(terms)
         return [sent]
 
-    for n, (r, g) in enumerate(plan):
+    for n, (r, column, span) in enumerate(plan):
         if r not in blocks:
             blocks[r] = gather(gated[r], "hist", first_out)
-        own, *others = output(index, slots, counts, blocks[r], w_out, g * span, span, chain)
+        own, *others = output(index, slots, counts, blocks[r], w_out, column, span, chain)
         before = made[n - 2][1] if n > 1 else []
         before = before + [folded[0][-1]] if folded else before
         made.append((own, [swap(tie(x, before), "head", 0) for x in others]))
         chain, first_out = [own], first_out or [own]
         if n == 2:
             chain = fold_next()
-    closed = 0
-    while closed < len(plan):
-        if len(folded) < len(plan):
+    done = 0
+    for r, row in enumerate(spans):
+        while len(folded) < min(len(plan), done + len(row) + 2):
             chain = fold_next()
-        if len(folded) > closed + 2 or len(folded) == len(plan):
-            r, g = plan[closed]
-            out, mark = close(place, index, tokens, chunks, r, g, folded[closed], out, chain)
-            chain, closed = [mark], closed + 1
+        terms, done = folded[done:done + len(row)], done + len(row)
+        out, mark = close(place, index, tokens, chunks, r, terms, out, chain)
+        chain = [mark]
     return out.reshape(cand // zs, -1)
 
 

time: 170 us -> 175 us (1.029)
  waiting for transfers between devices: 38.7 us -> 47.8 us
  Pallas kernels: 83.5 us -> 80.1 us
    ppermute x55, waiting for transfers between devices: 38.7 us -> 47.8 us  [swap(): lax.ppermute(x, axis, [(i, i ^ 1 << bit) for i in range(lax.axis_size(axi...]
    pallas_call x4 -> x2, Pallas kernels: 8.68 us -> 4.65 us  [close(): pl.pallas_call(functools.partial(close_kernel, [len(terms) for terms in g...]
  transfers between devices with their start and end apart: 55 -> 55, of which waited for: 16 -> 14; matrix products, arithmetic and copies ran while one was open for 0% -> 0% of each run, Pallas kernels for 44% -> 41%
where the time goes in v15:
time: 175 us; the launch traced here: 174 us
  Pallas kernels  80.1 us (46%)
  waiting for transfers between devices  47.8 us (27%)
  starting transfers between devices  43.1 us (25%)
  local copies, waits for them, and re-layouts  2.42 us (1%)
    ppermute x55, waiting for transfers between devices, swap(): lax.ppermute(x, axis, [(i, i ^ 1 << bit) for i in range(lax.axis_size(axi...  47.8 us
    ppermute x55, starting transfers between devices, swap(): lax.ppermute(x, axis, [(i, i ^ 1 << bit) for i in range(lax.axis_size(axi...  43.1 us
    pallas_call x5, Pallas kernels, project(): pl.pallas_call(functools.partial(project_kernel, parts, owners, len(after...  37.9 us
    pallas_call x4, Pallas kernels, output(): pl.pallas_call(functools.partial(output_kernel, owners, slots, len(after)...  14.4 us
    pallas_call x4, Pallas kernels, attend(): pl.pallas_call(functools.partial(attend_kernel, owners, len(counts)), gri...  12.5 us
    pallas_call x13, Pallas kernels, fold(): pl.pallas_call(functools.partial(fold_kernel, len(terms)), grid=(steps,),...  4.8 us
    pallas_call x2, Pallas kernels, close(): pl.pallas_call(functools.partial(close_kernel, [len(terms) for terms in g...  4.65 us
  transfers between devices with their start and end apart: 55, of which 14 were waited for; matrix products, arithmetic and copies ran while one was open for 0% of the time, Pallas kernels for 41%

profile of v15, /device:TPU:0, one launch (start us, length us, event | category | flops | bytes accessed | tf_op | source)
XLA Modules:
  0.0 174.1 jit_solution(17755466824508550396)
XLA Ops:
  0.0 5.5 %project.5 = (bf16[2,4,128,256]{3,2,1,0:T(8,128)(2,1)S(1)}, bf16[1,4,128,256]{3,2,1,0:T(8,128)(2,1)S(1)}, bf16[1,4,128,256]{3,2,1,0:T(8,128)(2,1)S(1)}) custom-call(s32[1]{0:T(128)} %bitcast.at_ref, bf16[4,2,4,16,2048]{4,3,2,1,0:T(8,128)(2,1)} %bitcast.57, bf16[4,2,4,16,2048]{4,3,2,1,0:T(8,128)(2,1)} %bitcast.58, bf16[4,2,4,16,2048]{4,3,2,1,0:T(8,128)(2,1)} %bitcast.59, ...), custom_call_target="tpu_custom_call" | custom-call | flops 1000 | bytes 1000 | tf_op jit(solution)/shard_map/project/pallas_call | solution.py:80
  6.1 8.7 %project.6 = (bf16[2,4,128,512]{3,2,1,0:T(8,128)(2,1)S(1)}, bf16[1,4,128,512]{3,2,1,0:T(8,128)(2,1)S(1)}, bf16[1,4,128,512]{3,2,1,0:T(8,128)(2,1)S(1)}) custom-call(s32[1]{0:T(128)} %bitcast.at_ref, bf16[4,2,4,16,2048]{4,3,2,1,0:T(8,128)(2,1)} %bitcast.61, bf16[4,2,4,16,2048]{4,3,2,1,0:T(8,128)(2,1)} %bitcast.62, bf16[4,2,4,16,2048]{4,3,2,1,0:T(8,128)(2,1)} %bitcast.63, ...), custom_call_target="tpu_custom_call" | custom-call | flops 1000 | bytes 1000 | tf_op jit(solution)/shard_map/project/pallas_call | solution.py:80
  15.8 3.0 %collective-permute-start.4 = (bf16[1,4,128,256]{3,2,1,0:T(8,128)(2,1)S(1)}, bf16[1,4,128,256]{3,2,1,0:T(8,128)(2,1)S(1)}, u32[]{:S(2)}, u32[]{:S(2)}) collective-permute-start(bf16[1,4,128,256]{3,2,1,0:T(8,128)(2,1)S(1)} %fold.13.refs_8_), channel_id=1, source_target_pairs={{0,2},{1,3},{2,0},{3,1},{4,6},{5,7},{6,4},{7,5},{8,10},{9,11},{10,... | collective-permute-start | bytes 786440 | tf_op jit(solution)/shard_map/ppermute | solution.py:525
  18.7 8.7 %project.7 = (bf16[2,4,128,512]{3,2,1,0:T(8,128)(2,1)S(1)}, bf16[1,4,128,512]{3,2,1,0:T(8,128)(2,1)S(1)}, bf16[1,4,128,512]{3,2,1,0:T(8,128)(2,1)S(1)}) custom-call(s32[1]{0:T(128)} %bitcast.at_ref, bf16[4,2,4,16,2048]{4,3,2,1,0:T(8,128)(2,1)} %bitcast.68, bf16[4,2,4,16,2048]{4,3,2,1,0:T(8,128)(2,1)} %bitcast.66, bf16[4,2,4,16,2048]{4,3,2,1,0:T(8,128)(2,1)} %bitcast.67, ...), custom_call_target="tpu_custom_call" | custom-call | flops 1000 | bytes 1000 | tf_op jit(solution)/shard_map/project/pallas_call | solution.py:80
  28.5 8.8 %project.8 = (bf16[2,4,128,512]{3,2,1,0:T(8,128)(2,1)S(1)}, bf16[1,4,128,512]{3,2,1,0:T(8,128)(2,1)S(1)}, bf16[1,4,128,512]{3,2,1,0:T(8,128)(2,1)S(1)}) custom-call(s32[1]{0:T(128)} %bitcast.at_ref, bf16[4,2,4,16,2048]{4,3,2,1,0:T(8,128)(2,1)} %bitcast.69, bf16[4,2,4,16,2048]{4,3,2,1,0:T(8,128)(2,1)} %bitcast.70, bf16[4,2,4,16,2048]{4,3,2,1,0:T(8,128)(2,1)} %bitcast.71, ...), custom_call_target="tpu_custom_call" | custom-call | flops 1000 | bytes 1000 | tf_op jit(solution)/shard_map/project/pallas_call | solution.py:80
  39.1 1.9 %collective-permute-start.12 = (bf16[1,4,128,512]{3,2,1,0:T(8,128)(2,1)}, bf16[1,4,128,512]{3,2,1,0:T(8,128)(2,1)}, u32[]{:S(2)}, u32[]{:S(2)}) collective-permute-start(bf16[1,4,128,512]{3,2,1,0:T(8,128)(2,1)} %fold.15.refs_6_), channel_id=1, source_target_pairs={{0,2},{1,3},{2,0},{3,1},{4,6},{5,7},{6,4},{7,5},{8,10},{9,11},{10,... | collective-permute-start | bytes 1572872 | tf_op jit(solution)/shard_map/ppermute | solution.py:525
  41.0 1.4 collective-permute-done.8.refs_5_
  43.2 1.0 fold.16.refs_8_
  44.2 1.7 collective-permute-start.17
  45.9 6.1 %project.9 = (bf16[2,4,128,256]{3,2,1,0:T(8,128)(2,1)S(1)}, bf16[1,4,128,256]{3,2,1,0:T(8,128)(2,1)S(1)}, bf16[1,4,128,256]{3,2,1,0:T(8,128)(2,1)}) custom-call(s32[1]{0:T(128)} %bitcast.at_ref, bf16[4,2,4,16,2048]{4,3,2,1,0:T(8,128)(2,1)} %bitcast.73, bf16[4,2,4,16,2048]{4,3,2,1,0:T(8,128)(2,1)} %bitcast.74, bf16[4,2,4,16,2048]{4,3,2,1,0:T(8,128)(2,1)} %bitcast.75, ...), custom_call_target="tpu_custom_call" | custom-call | flops 1000 | bytes 1000 | tf_op jit(solution)/shard_map/project/pallas_call | solution.py:80
  53.3 5.0 %collective-permute-done.18.refs_1_ = bf16[128,768]{1,0:T(8,128)(2,1)S(1)} collective-permute-done((bf16[128,768]{1,0:T(8,128)(2,1)S(1)}, bf16[128,768]{1,0:T(8,128)(2,1)S(1)}, u32[]{:S(2)}, u32[]{:S(2)}) %collective-permute-start.18) | collective-permute-done | bytes 196640 | tf_op jit(solution)/shard_map/ppermute | solution.py:525
  58.5 1.0 copy-done.3
  59.6 1.4 activate.5
  61.0 1.1 fold.17.refs_10_
  62.1 4.1 %attend.4 = (bf16[2,128,768]{2,1,0:T(8,128)(2,1)S(1)}, bf16[1,128,768]{2,1,0:T(8,128)(2,1)S(1)}, bf16[1,128,768]{2,1,0:T(8,128)(2,1)S(1)}) custom-call(s32[1]{0:T(128)} %bitcast.at_ref, bf16[128,768]{1,0:T(8,128)(2,1)S(1)} %get-tuple-element.72.refs_2_.refs_0_.q_ref, bf16[128,768]{1,0:T(8,128)(2,1)S(1)} %collective-permute-done.18.refs_1_, ...), custom_call_target="tpu_custom_call" | custom-call | flops 1000 | bytes 1000 | tf_op jit(solution)/shard_map/attend/pallas_call | solution.py:262
  66.7 1.8 %collective-permute-start.14 = (bf16[128,512]{1,0:T(8,128)(2,1)S(1)}, bf16[128,512]{1,0:T(8,128)(2,1)S(1)}, u32[]{:S(2)}, u32[]{:S(2)}) collective-permute-start(bf16[128,512]{1,0:T(8,128)(2,1)S(1)} %get-tuple-element.77.refs_2_.refs_0_.q_ref), channel_id=1, source_target_pairs={{0,2},{1,3},{2,0},{3,1},{4,6},{5,7},{6,4},{7,5},{8,10},{9,11},{10,... | collective-permute-start | bytes 393224 | tf_op jit(solution)/shard_map/ppermute | solution.py:525
  68.8 4.0 %collective-permute-done.14.refs_1_ = bf16[128,512]{1,0:T(8,128)(2,1)S(1)} collective-permute-done((bf16[128,512]{1,0:T(8,128)(2,1)S(1)}, bf16[128,512]{1,0:T(8,128)(2,1)S(1)}, u32[]{:S(2)}, u32[]{:S(2)}) %collective-permute-start.14) | collective-permute-done | bytes 131104 | tf_op jit(solution)/shard_map/ppermute | solution.py:525
  73.5 1.4 activate.6
  74.9 2.1 %collective-permute-start.25 = (bf16[128,512]{1,0:T(8,128)(2,1)S(1)}, bf16[128,512]{1,0:T(8,128)(2,1)S(1)}, u32[]{:S(2)}, u32[]{:S(2)}) collective-permute-start(bf16[128,512]{1,0:T(8,128)(2,1)S(1)} %get-tuple-element.80.refs_10_.refs_0_.q_ref), channel_id=1, source_target_pairs={{0,2},{1,3},{2,0},{3,1},{4,6},{5,7},{6,4},{7,5},{8,10},{9,11},{10,... | collective-permute-start | bytes 393224 | tf_op jit(solution)/shard_map/ppermute | solution.py:525
  77.0 3.1 %attend.5 = (bf16[2,128,512]{2,1,0:T(8,128)(2,1)S(1)}, bf16[1,128,512]{2,1,0:T(8,128)(2,1)S(1)}, bf16[1,128,512]{2,1,0:T(8,128)(2,1)S(1)}) custom-call(s32[1]{0:T(128)} %bitcast.at_ref, bf16[128,512]{1,0:T(8,128)(2,1)S(1)} %get-tuple-element.77.refs_2_.refs_0_.q_ref, bf16[128,512]{1,0:T(8,128)(2,1)S(1)} %collective-permute-done.14.refs_1_, ...), custom_call_target="tpu_custom_call" | custom-call | flops 1000 | bytes 1000 | tf_op jit(solution)/shard_map/attend/pallas_call | solution.py:262
  81.3 1.7 collective-permute-start.31
  83.3 3.2 %attend.6 = (bf16[2,128,512]{2,1,0:T(8,128)(2,1)S(1)}, bf16[1,128,512]{2,1,0:T(8,128)(2,1)S(1)}, bf16[1,128,512]{2,1,0:T(8,128)(2,1)S(1)}) custom-call(s32[1]{0:T(128)} %bitcast.at_ref, bf16[128,512]{1,0:T(8,128)(2,1)S(1)} %get-tuple-element.80.refs_10_.refs_0_.q_ref, bf16[128,512]{1,0:T(8,128)(2,1)S(1)} %collective-permute-done.25.refs_1_, ...), custom_call_target="tpu_custom_call" | custom-call | flops 1000 | bytes 1000 | tf_op jit(solution)/shard_map/attend/pallas_call | solution.py:262
  87.2 3.9 %collective-permute-done.22.refs_1_ = bf16[128,256]{1,0:T(8,128)(2,1)S(1)} collective-permute-done((bf16[128,256]{1,0:T(8,128)(2,1)S(1)}, bf16[128,256]{1,0:T(8,128)(2,1)S(1)}, u32[]{:S(2)}, u32[]{:S(2)}) %collective-permute-start.22) | collective-permute-done | bytes 65568 | tf_op jit(solution)/shard_map/ppermute | solution.py:525
  92.8 2.0 %attend.7 = (bf16[2,128,256]{2,1,0:T(8,128)(2,1)S(1)}, bf16[1,128,256]{2,1,0:T(8,128)(2,1)S(1)}, bf16[1,128,256]{2,1,0:T(8,128)(2,1)S(1)}) custom-call(s32[1]{0:T(128)} %bitcast.at_ref, bf16[128,256]{1,0:T(8,128)(2,1)S(1)} %get-tuple-element.82.refs_2_.refs_0_.q_ref, bf16[128,256]{1,0:T(8,128)(2,1)S(1)} %collective-permute-done.22.refs_1_, ...), custom_call_target="tpu_custom_call" | custom-call | flops 1000 | bytes 1000 | tf_op jit(solution)/shard_map/attend/pallas_call | solution.py:262
  95.3 1.7 collective-permute-start.38
  98.8 2.3 %collective-permute-done.38.refs_2_ = bf16[1,128,512]{2,1,0:T(8,128)(2,1)S(1)} collective-permute-done((bf16[1,128,512]{2,1,0:T(8,128)(2,1)S(1)}, bf16[1,128,512]{2,1,0:T(8,128)(2,1)S(1)}, u32[]{:S(2)}, u32[]{:S(2)}) %collective-permute-start.38) | collective-permute-done | bytes 131104 | tf_op jit(solution)/shard_map/ppermute | solution.py:525
  102.7 1.8 %collective-permute-start.39 = (f32[8,128]{1,0:T(8,128)S(1)}, f32[8,128]{1,0:T(8,128)S(1)}, u32[]{:S(2)}, u32[]{:S(2)}) collective-permute-start(f32[8,128]{1,0:T(8,128)S(1)} %get-tuple-element.102.refs_0_), channel_id=1, source_target_pairs={{0,4},{4,0},{8,12},{12,8},{1,5},{5,1},{9,13},{13,9},{2,6},{6,2},{1... | collective-permute-start | bytes 12296 | tf_op jit(solution)/shard_map/ppermute | solution.py:525
  104.5 1.9 %collective-permute-done.39.refs_1_ = f32[8,128]{1,0:T(8,128)S(1)} collective-permute-done((f32[8,128]{1,0:T(8,128)S(1)}, f32[8,128]{1,0:T(8,128)S(1)}, u32[]{:S(2)}, u32[]{:S(2)}) %collective-permute-start.39) | collective-permute-done | bytes 4128 | tf_op jit(solution)/shard_map/ppermute | solution.py:525
  106.4 2.8 %collective-permute-start.40 = (f32[8,128]{1,0:T(8,128)S(1)}, f32[8,128]{1,0:T(8,128)S(1)}, u32[]{:S(2)}, u32[]{:S(2)}) collective-permute-start(f32[8,128]{1,0:T(8,128)S(1)} %merge.1.refs_0_), channel_id=1, source_target_pairs={{0,8},{4,12},{8,0},{12,4},{1,9},{5,13},{9,1},{13,5},{2,10},{6,14},... | collective-permute-start | bytes 12296 | tf_op jit(solution)/shard_map/ppermute | solution.py:525
  109.2 1.7 %collective-permute-done.40.refs_1_ = f32[8,128]{1,0:T(8,128)S(1)} collective-permute-done((f32[8,128]{1,0:T(8,128)S(1)}, f32[8,128]{1,0:T(8,128)S(1)}, u32[]{:S(2)}, u32[]{:S(2)}) %collective-permute-start.40) | collective-permute-done | bytes 4128 | tf_op jit(solution)/shard_map/ppermute | solution.py:525
  111.3 1.7 collective-permute-start.42
  113.4 6.7 %collective-permute-done.42 = bf16[64,2048]{1,0:T(8,128)(2,1)S(1)} collective-permute-done((bf16[64,2048]{1,0:T(8,128)(2,1)S(1)}, bf16[64,2048]{1,0:T(8,128)(2,1)S(1)}, u32[]{:S(2)}, u32[]{:S(2)}) %collective-permute-start.42) | collective-permute-done | bytes 262176 | tf_op jit(solution)/shard_map/ppermute | solution.py:525
  120.6 1.0 collective-permute-done.44
  121.7 3.4 %output.4 = (bf16[2,4,16,1024]{3,2,1,0:T(8,128)(2,1)S(1)}, bf16[2,4,16,1024]{3,2,1,0:T(8,128)(2,1)S(1)}) custom-call(s32[1]{0:T(128)} %bitcast.3.index_ref, bf16[4,16,2048]{2,1,0:T(8,128)(2,1)S(1)} %bitcast.47, bf16[4,16,2048]{2,1,0:T(8,128)(2,1)S(1)} %bitcast.49, bf16[4,16,2048]{2,1,0:T(8,128)(2,1)S(1)} %bitcast.51, bf16[4,16,2048]{2,1,0:T(8,128)(2,1)S(1)} %bitcast.53, ...), custom_call_target="tpu_custom_call" | custom-call | flops 1000 | bytes 1000 | tf_op jit(solution)/shard_map/output/pallas_call | solution.py:444
  125.3 1.6 collective-permute-start.47
  126.9 3.4 %output.5 = (bf16[2,4,16,1024]{3,2,1,0:T(8,128)(2,1)S(1)}, bf16[2,4,16,1024]{3,2,1,0:T(8,128)(2,1)S(1)}) custom-call(s32[1]{0:T(128)} %bitcast.3.index_ref, bf16[4,16,2048]{2,1,0:T(8,128)(2,1)S(1)} %bitcast.48, bf16[4,16,2048]{2,1,0:T(8,128)(2,1)S(1)} %bitcast.50, bf16[4,16,2048]{2,1,0:T(8,128)(2,1)S(1)} %bitcast.52, bf16[4,16,2048]{2,1,0:T(8,128)(2,1)S(1)} %bitcast.54, ...), custom_call_target="tpu_custom_call" | custom-call | flops 1000 | bytes 1000 | tf_op jit(solution)/shard_map/output/pallas_call | solution.py:444
  130.9 4.1 %output.6 = (bf16[2,4,16,1280]{3,2,1,0:T(8,128)(2,1)S(1)}, bf16[2,4,16,1280]{3,2,1,0:T(8,128)(2,1)S(1)}) custom-call(s32[1]{0:T(128)} %bitcast.3.index_ref, bf16[4,16,2176]{2,1,0:T(8,128)(2,1)S(1)} %bitcast.41, bf16[4,16,2176]{2,1,0:T(8,128)(2,1)S(1)} %bitcast.39, bf16[4,16,2176]{2,1,0:T(8,128)(2,1)S(1)} %bitcast.43, bf16[4,16,2176]{2,1,0:T(8,128)(2,1)S(1)} %bitcast.45, ...), custom_call_target="tpu_custom_call" | custom-call | flops 1000 | bytes 1000 | tf_op jit(solution)/shard_map/output/pallas_call | solution.py:444
  135.0 1.6 collective-permute-start.48
  136.7 2.7 %collective-permute-start.51 = (bf16[1,4,16,1024]{3,2,1,0:T(8,128)(2,1)S(1)}, bf16[1,4,16,1024]{3,2,1,0:T(8,128)(2,1)S(1)}, u32[]{:S(2)}, u32[]{:S(2)}) collective-permute-start(bf16[1,4,16,1024]{3,2,1,0:T(8,128)(2,1)S(1)} %fold.22.refs_5_), channel_id=1, source_target_pairs={{0,8},{4,12},{8,0},{12,4},{1,9},{5,13},{9,1},{13,5},{2,10},{6,14},... | collective-permute-start | bytes 393224 | tf_op jit(solution)/shard_map/ppermute | solution.py:525
  139.4 3.5 %output.7 = (bf16[2,4,16,768]{3,2,1,0:T(8,128)(2,1)S(1)}, bf16[2,4,16,768]{3,2,1,0:T(8,128)(2,1)S(1)}) custom-call(s32[1]{0:T(128)} %bitcast.3.index_ref, bf16[4,16,2176]{2,1,0:T(8,128)(2,1)S(1)} %bitcast.42, bf16[4,16,2176]{2,1,0:T(8,128)(2,1)S(1)} %bitcast.40, bf16[4,16,2176]{2,1,0:T(8,128)(2,1)S(1)} %bitcast.44, bf16[4,16,2176]{2,1,0:T(8,128)(2,1)S(1)} %bitcast.46, ...), custom_call_target="tpu_custom_call" | custom-call | flops 1000 | bytes 1000 | tf_op jit(solution)/shard_map/output/pallas_call | solution.py:444
  142.9 5.6 %collective-permute-done.51.refs_2_ = bf16[1,4,16,1024]{3,2,1,0:T(8,128)(2,1)S(1)} collective-permute-done((bf16[1,4,16,1024]{3,2,1,0:T(8,128)(2,1)S(1)}, bf16[1,4,16,1024]{3,2,1,0:T(8,128)(2,1)S(1)}, u32[]{:S(2)}, u32[]{:S(2)}) %collective-permute-start.51) | collective-permute-done | bytes 131104 | tf_op jit(solution)/shard_map/ppermute | solution.py:525
  148.4 3.5 %collective-permute-start.52 = (bf16[2,4,16,768]{3,2,1,0:T(8,128)(2,1)S(1)}, bf16[2,4,16,768]{3,2,1,0:T(8,128)(2,1)S(1)}, u32[]{:S(2)}, u32[]{:S(2)}) collective-permute-start(bf16[2,4,16,768]{3,2,1,0:T(8,128)(2,1)S(1)} %tie.21), channel_id=1, source_target_pairs={{0,4},{4,0},{8,12},{12,8},{1,5},{5,1},{9,13},{13,9},{2,6},{6,2},{1... | collective-permute-start | bytes 589832 | tf_op jit(solution)/shard_map/ppermute | solution.py:525
  152.3 3.0 %collective-permute-start.50 = (bf16[1,4,16,1280]{3,2,1,0:T(8,128)(2,1)S(1)}, bf16[1,4,16,1280]{3,2,1,0:T(8,128)(2,1)S(1)}, u32[]{:S(2)}, u32[]{:S(2)}) collective-permute-start(bf16[1,4,16,1280]{3,2,1,0:T(8,128)(2,1)S(1)} %fold.24.refs_2_), channel_id=1, source_target_pairs={{0,8},{4,12},{8,0},{12,4},{1,9},{5,13},{9,1},{13,5},{2,10},{6,14},... | collective-permute-start | bytes 491528 | tf_op jit(solution)/shard_map/ppermute | solution.py:525
  155.4 4.0 %collective-permute-done.52.refs_1_.refs_4_ = bf16[2,4,16,768]{3,2,1,0:T(8,128)(2,1)S(1)} collective-permute-done((bf16[2,4,16,768]{3,2,1,0:T(8,128)(2,1)S(1)}, bf16[2,4,16,768]{3,2,1,0:T(8,128)(2,1)S(1)}, u32[]{:S(2)}, u32[]{:S(2)}) %collective-permute-start.52) | collective-permute-done | bytes 196640 | tf_op jit(solution)/shard_map/ppermute | solution.py:525
  160.1 7.6 %collective-permute-done.54.refs_5_ = bf16[1,4,16,1024]{3,2,1,0:T(8,128)(2,1)S(1)} collective-permute-done((bf16[1,4,16,1024]{3,2,1,0:T(8,128)(2,1)S(1)}, bf16[1,4,16,1024]{3,2,1,0:T(8,128)(2,1)S(1)}, u32[]{:S(2)}, u32[]{:S(2)}) %collective-permute-start.54) | collective-permute-done | bytes 131104 | tf_op jit(solution)/shard_map/ppermute | solution.py:525
  167.7 2.3 %close.2 = (bf16[8,16,2048]{2,1,0:T(8,128)(2,1)}, f32[8,128]{1,0:T(8,128)S(1)}) custom-call(s32[2]{0:T(128)S(1)} %pad_add_fusion.1.at_ref, bf16[32,16,2048]{2,1,0:T(8,128)(2,1)} %bitcast.77, bf16[2,4,16,1024]{3,2,1,0:T(8,128)(2,1)S(1)} %get-tuple-element.106.refs_1_.refs_5_.refs_0_, bf16[2,4,16,1024]{3,2,1,0:T(8,128)(2,1)S(1)} %collective-permute-done.47.refs_1_, ...), custom_call_target="tpu_custom_call" | custom-call | flops 1000 | bytes 1000 | tf_op jit(solution)/shard_map/close/pallas_call | solution.py:490
  170.0 1.8 %collective-permute-done.53.refs_5_ = bf16[1,4,16,768]{3,2,1,0:T(8,128)(2,1)S(1)} collective-permute-done((bf16[1,4,16,768]{3,2,1,0:T(8,128)(2,1)S(1)}, bf16[1,4,16,768]{3,2,1,0:T(8,128)(2,1)S(1)}, u32[]{:S(2)}, u32[]{:S(2)}) %collective-permute-start.53) | collective-permute-done | bytes 98336 | tf_op jit(solution)/shard_map/ppermute | solution.py:525
  171.8 2.3 %close.3 = (bf16[8,16,2048]{2,1,0:T(8,128)(2,1)}, f32[8,128]{1,0:T(8,128)}) custom-call(s32[2]{0:T(128)S(1)} %pad_add_fusion.at_ref, bf16[32,16,2048]{2,1,0:T(8,128)(2,1)} %bitcast.78, bf16[2,4,16,1280]{3,2,1,0:T(8,128)(2,1)S(1)} %get-tuple-element.108.refs_2_.refs_0_, ...), custom_call_target="tpu_custom_call", output_to_operand_aliasing={{0}: (8, {})} | custom-call | flops 1000 | bytes 1000 | tf_op jit(solution)/shard_map/close/pallas_call | solution.py:490
  (134 shorter events, 18.9 us)
Async XLA Ops:
  5.5 9.4 %collective-permute-start = (bf16[1,4,128,256]{3,2,1,0:T(8,128)(2,1)S(1)}, bf16[1,4,128,256]{3,2,1,0:T(8,128)(2,1)S(1)}, u32[]{:S(2)}, u32[]{:S(2)}) collective-permute-start(bf16[1,4,128,256]{3,2,1,0:T(8,128)(2,1)S(1)} %get-tuple-element.64), channel_id=1, source_target_pairs={{0,1},{1,0},{2,3},{3,2},{4,5},{5,4},{6,7},{7,6},{8,9},{9,8},{10,11... | collective-permute-start | bytes 786440 | tf_op jit(solution)/shard_map/ppermute | solution.py:525
  6.1 8.8 %collective-permute-start.1 = (bf16[1,4,128,256]{3,2,1,0:T(8,128)(2,1)S(1)}, bf16[1,4,128,256]{3,2,1,0:T(8,128)(2,1)S(1)}, u32[]{:S(2)}, u32[]{:S(2)}) collective-permute-start(bf16[1,4,128,256]{3,2,1,0:T(8,128)(2,1)S(1)} %get-tuple-element.65), channel_id=1, source_target_pairs={{0,1},{1,0},{2,3},{3,2},{4,5},{5,4},{6,7},{7,6},{8,9},{9,8},{10,11... | collective-permute-start | bytes 786440 | tf_op jit(solution)/shard_map/ppermute | solution.py:525
  14.9 12.6 %collective-permute-start.3 = (bf16[1,4,128,512]{3,2,1,0:T(8,128)(2,1)S(1)}, bf16[1,4,128,512]{3,2,1,0:T(8,128)(2,1)S(1)}, u32[]{:S(2)}, u32[]{:S(2)}) collective-permute-start(bf16[1,4,128,512]{3,2,1,0:T(8,128)(2,1)S(1)} %tie.12), channel_id=1, source_target_pairs={{0,1},{1,0},{2,3},{3,2},{4,5},{5,4},{6,7},{7,6},{8,9},{9,8},{10,11... | collective-permute-start | bytes 1572872 | tf_op jit(solution)/shard_map/ppermute | solution.py:525
  15.4 12.1 %collective-permute-start.2 = (bf16[1,4,128,512]{3,2,1,0:T(8,128)(2,1)S(1)}, bf16[1,4,128,512]{3,2,1,0:T(8,128)(2,1)S(1)}, u32[]{:S(2)}, u32[]{:S(2)}) collective-permute-start(bf16[1,4,128,512]{3,2,1,0:T(8,128)(2,1)S(1)} %tie.11), channel_id=1, source_target_pairs={{0,1},{1,0},{2,3},{3,2},{4,5},{5,4},{6,7},{7,6},{8,9},{9,8},{10,11... | collective-permute-start | bytes 1572872 | tf_op jit(solution)/shard_map/ppermute | solution.py:525
  15.8 11.7 %collective-permute-start.4 = (bf16[1,4,128,256]{3,2,1,0:T(8,128)(2,1)S(1)}, bf16[1,4,128,256]{3,2,1,0:T(8,128)(2,1)S(1)}, u32[]{:S(2)}, u32[]{:S(2)}) collective-permute-start(bf16[1,4,128,256]{3,2,1,0:T(8,128)(2,1)S(1)} %fold.13.refs_8_), channel_id=1, source_target_pairs={{0,2},{1,3},{2,0},{3,1},{4,6},{5,7},{6,4},{7,5},{8,10},{9,11},{10,... | collective-permute-start | bytes 786440 | tf_op jit(solution)/shard_map/ppermute | solution.py:525
  27.5 9.8 %collective-permute-start.6 = (bf16[1,4,128,512]{3,2,1,0:T(8,128)(2,1)S(1)}, bf16[1,4,128,512]{3,2,1,0:T(8,128)(2,1)S(1)}, u32[]{:S(2)}, u32[]{:S(2)}) collective-permute-start(bf16[1,4,128,512]{3,2,1,0:T(8,128)(2,1)S(1)} %tie.14), channel_id=1, source_target_pairs={{0,1},{1,0},{2,3},{3,2},{4,5},{5,4},{6,7},{7,6},{8,9},{9,8},{10,11... | collective-permute-start | bytes 1572872 | tf_op jit(solution)/shard_map/ppermute | solution.py:525
  27.6 9.7 %collective-permute-start.5 = (bf16[1,4,128,512]{3,2,1,0:T(8,128)(2,1)S(1)}, bf16[1,4,128,512]{3,2,1,0:T(8,128)(2,1)S(1)}, u32[]{:S(2)}, u32[]{:S(2)}) collective-permute-start(bf16[1,4,128,512]{3,2,1,0:T(8,128)(2,1)S(1)} %tie.13), channel_id=1, source_target_pairs={{0,1},{1,0},{2,3},{3,2},{4,5},{5,4},{6,7},{7,6},{8,9},{9,8},{10,11... | collective-permute-start | bytes 1572872 | tf_op jit(solution)/shard_map/ppermute | solution.py:525
  28.4 14.0 %collective-permute-start.8 = (bf16[1,4,128,512]{3,2,1,0:T(8,128)(2,1)S(1)}, bf16[1,4,128,512]{3,2,1,0:T(8,128)(2,1)S(1)}, u32[]{:S(2)}, u32[]{:S(2)}) collective-permute-start(bf16[1,4,128,512]{3,2,1,0:T(8,128)(2,1)S(1)} %fold.14.refs_8_), channel_id=1, source_target_pairs={{0,2},{1,3},{2,0},{3,1},{4,6},{5,7},{6,4},{7,5},{8,10},{9,11},{10,... | collective-permute-start | bytes 1572872 | tf_op jit(solution)/shard_map/ppermute | solution.py:525
  37.3 5.9 %collective-permute-start.7 = (bf16[1,4,128,512]{3,2,1,0:T(8,128)(2,1)S(1)}, bf16[1,4,128,512]{3,2,1,0:T(8,128)(2,1)S(1)}, u32[]{:S(2)}, u32[]{:S(2)}) collective-permute-start(bf16[1,4,128,512]{3,2,1,0:T(8,128)(2,1)S(1)} %tie.15), channel_id=1, source_target_pairs={{0,1},{1,0},{2,3},{3,2},{4,5},{5,4},{6,7},{7,6},{8,9},{9,8},{10,11... | collective-permute-start | bytes 1572872 | tf_op jit(solution)/shard_map/ppermute | solution.py:525
  38.1 14.7 %collective-permute-start.9 = (bf16[1,4,128,512]{3,2,1,0:T(8,128)(2,1)S(1)}, bf16[1,4,128,512]{3,2,1,0:T(8,128)(2,1)S(1)}, u32[]{:S(2)}, u32[]{:S(2)}) collective-permute-start(bf16[1,4,128,512]{3,2,1,0:T(8,128)(2,1)S(1)} %tie.16), channel_id=1, source_target_pairs={{0,1},{1,0},{2,3},{3,2},{4,5},{5,4},{6,7},{7,6},{8,9},{9,8},{10,11... | collective-permute-start | bytes 1572872 | tf_op jit(solution)/shard_map/ppermute | solution.py:525
  39.1 19.4 %collective-permute-start.12 = (bf16[1,4,128,512]{3,2,1,0:T(8,128)(2,1)}, bf16[1,4,128,512]{3,2,1,0:T(8,128)(2,1)}, u32[]{:S(2)}, u32[]{:S(2)}) collective-permute-start(bf16[1,4,128,512]{3,2,1,0:T(8,128)(2,1)} %fold.15.refs_6_), channel_id=1, source_target_pairs={{0,2},{1,3},{2,0},{3,1},{4,6},{5,7},{6,4},{7,5},{8,10},{9,11},{10,... | collective-permute-start | bytes 1572872 | tf_op jit(solution)/shard_map/ppermute | solution.py:525
  42.9 15.5 %collective-permute-start.18 = (bf16[128,768]{1,0:T(8,128)(2,1)S(1)}, bf16[128,768]{1,0:T(8,128)(2,1)S(1)}, u32[]{:S(2)}, u32[]{:S(2)}) collective-permute-start(bf16[128,768]{1,0:T(8,128)(2,1)S(1)} %get-tuple-element.72.refs_2_.refs_0_.q_ref), channel_id=1, source_target_pairs={{0,2},{1,3},{2,0},{3,1},{4,6},{5,7},{6,4},{7,5},{8,10},{9,11},{10,... | collective-permute-start | bytes 589832 | tf_op jit(solution)/shard_map/ppermute | solution.py:525
  44.2 29.3 %collective-permute-start.17 = (bf16[1,4,128,512]{3,2,1,0:T(8,128)(2,1)}, bf16[1,4,128,512]{3,2,1,0:T(8,128)(2,1)}, u32[]{:S(2)}, u32[]{:S(2)}) collective-permute-start(bf16[1,4,128,512]{3,2,1,0:T(8,128)(2,1)} %fold.16.refs_8_), channel_id=1, source_target_pairs={{0,2},{1,3},{2,0},{3,1},{4,6},{5,7},{6,4},{7,5},{8,10},{9,11},{10,... | collective-permute-start | bytes 1572872 | tf_op jit(solution)/shard_map/ppermute | solution.py:525
  52.8 8.1 %collective-permute-start.11 = (bf16[1,4,128,256]{3,2,1,0:T(8,128)(2,1)}, bf16[1,4,128,256]{3,2,1,0:T(8,128)(2,1)}, u32[]{:S(2)}, u32[]{:S(2)}) collective-permute-start(bf16[1,4,128,256]{3,2,1,0:T(8,128)(2,1)} %tie.18), channel_id=1, source_target_pairs={{0,1},{1,0},{2,3},{3,2},{4,5},{5,4},{6,7},{7,6},{8,9},{9,8},{10,11... | collective-permute-start | bytes 786440 | tf_op jit(solution)/shard_map/ppermute | solution.py:525
  52.8 9.2 %collective-permute-start.19 = (bf16[128,768]{1,0:T(8,128)(2,1)S(1)}, bf16[128,768]{1,0:T(8,128)(2,1)}, u32[]{:S(2)}, u32[]{:S(2)}) collective-permute-start(bf16[128,768]{1,0:T(8,128)(2,1)S(1)} %get-tuple-element.72.refs_2_.refs_0_.q_ref), channel_id=1, source_target_pairs={{0,1},{1,0},{2,3},{3,2},{4,5},{5,4},{6,7},{7,6},{8,9},{9,8},{10,11... | collective-permute-start | bytes 589832 | tf_op jit(solution)/shard_map/ppermute | solution.py:525
  58.4 3.7 %collective-permute-start.20 = (bf16[128,768]{1,0:T(8,128)(2,1)S(1)}, bf16[128,768]{1,0:T(8,128)(2,1)}, u32[]{:S(2)}, u32[]{:S(2)}) collective-permute-start(bf16[128,768]{1,0:T(8,128)(2,1)S(1)} %collective-permute-done.18.refs_1_), channel_id=1, source_target_pairs={{0,1},{1,0},{2,3},{3,2},{4,5},{5,4},{6,7},{7,6},{8,9},{9,8},{10,11... | collective-permute-start | bytes 589832 | tf_op jit(solution)/shard_map/ppermute | solution.py:525
  66.2 6.7 %collective-permute-start.21 = (bf16[1,128,768]{2,1,0:T(8,128)(2,1)S(1)}, bf16[1,128,768]{2,1,0:T(8,128)(2,1)S(1)}, u32[]{:S(2)}, u32[]{:S(2)}) collective-permute-start(bf16[1,128,768]{2,1,0:T(8,128)(2,1)S(1)} %get-tuple-element.79), channel_id=1, source_target_pairs={{0,1},{1,0},{2,3},{3,2},{4,5},{5,4},{6,7},{7,6},{8,9},{9,8},{10,11... | collective-permute-start | bytes 589832 | tf_op jit(solution)/shard_map/ppermute | solution.py:525
  66.7 6.1 %collective-permute-start.14 = (bf16[128,512]{1,0:T(8,128)(2,1)S(1)}, bf16[128,512]{1,0:T(8,128)(2,1)S(1)}, u32[]{:S(2)}, u32[]{:S(2)}) collective-permute-start(bf16[128,512]{1,0:T(8,128)(2,1)S(1)} %get-tuple-element.77.refs_2_.refs_0_.q_ref), channel_id=1, source_target_pairs={{0,2},{1,3},{2,0},{3,1},{4,6},{5,7},{6,4},{7,5},{8,10},{9,11},{10,... | collective-permute-start | bytes 393224 | tf_op jit(solution)/shard_map/ppermute | solution.py:525
  68.5 12.3 %collective-permute-start.10 = (bf16[1,4,128,256]{3,2,1,0:T(8,128)(2,1)S(1)}, bf16[1,4,128,256]{3,2,1,0:T(8,128)(2,1)S(1)}, u32[]{:S(2)}, u32[]{:S(2)}) collective-permute-start(bf16[1,4,128,256]{3,2,1,0:T(8,128)(2,1)S(1)} %tie.17), channel_id=1, source_target_pairs={{0,1},{1,0},{2,3},{3,2},{4,5},{5,4},{6,7},{7,6},{8,9},{9,8},{10,11... | collective-permute-start | bytes 786440 | tf_op jit(solution)/shard_map/ppermute | solution.py:525
  68.5 12.7 %collective-permute-start.13 = (bf16[1,4,128,256]{3,2,1,0:T(8,128)(2,1)S(1)}, bf16[1,4,128,256]{3,2,1,0:T(8,128)(2,1)S(1)}, u32[]{:S(2)}, u32[]{:S(2)}) collective-permute-start(bf16[1,4,128,256]{3,2,1,0:T(8,128)(2,1)S(1)} %fold.17.refs_10_), channel_id=1, source_target_pairs={{0,2},{1,3},{2,0},{3,1},{4,6},{5,7},{6,4},{7,5},{8,10},{9,11},{10,... | collective-permute-start | bytes 786440 | tf_op jit(solution)/shard_map/ppermute | solution.py:525
  72.9 4.2 %collective-permute-start.15 = (bf16[128,512]{1,0:T(8,128)(2,1)S(1)}, bf16[128,512]{1,0:T(8,128)(2,1)S(1)}, u32[]{:S(2)}, u32[]{:S(2)}) collective-permute-start(bf16[128,512]{1,0:T(8,128)(2,1)S(1)} %get-tuple-element.77.refs_2_.refs_0_.q_ref), channel_id=1, source_target_pairs={{0,1},{1,0},{2,3},{3,2},{4,5},{5,4},{6,7},{7,6},{8,9},{9,8},{10,11... | collective-permute-start | bytes 393224 | tf_op jit(solution)/shard_map/ppermute | solution.py:525
  72.9 4.2 %collective-permute-start.16 = (bf16[128,512]{1,0:T(8,128)(2,1)S(1)}, bf16[128,512]{1,0:T(8,128)(2,1)S(1)}, u32[]{:S(2)}, u32[]{:S(2)}) collective-permute-start(bf16[128,512]{1,0:T(8,128)(2,1)S(1)} %collective-permute-done.14.refs_1_), channel_id=1, source_target_pairs={{0,1},{1,0},{2,3},{3,2},{4,5},{5,4},{6,7},{7,6},{8,9},{9,8},{10,11... | collective-permute-start | bytes 393224 | tf_op jit(solution)/shard_map/ppermute | solution.py:525
  74.9 5.8 %collective-permute-start.25 = (bf16[128,512]{1,0:T(8,128)(2,1)S(1)}, bf16[128,512]{1,0:T(8,128)(2,1)S(1)}, u32[]{:S(2)}, u32[]{:S(2)}) collective-permute-start(bf16[128,512]{1,0:T(8,128)(2,1)S(1)} %get-tuple-element.80.refs_10_.refs_0_.q_ref), channel_id=1, source_target_pairs={{0,2},{1,3},{2,0},{3,1},{4,6},{5,7},{6,4},{7,5},{8,10},{9,11},{10,... | collective-permute-start | bytes 393224 | tf_op jit(solution)/shard_map/ppermute | solution.py:525
  80.8 10.3 %collective-permute-start.30 = (bf16[1,128,768]{2,1,0:T(8,128)(2,1)S(1)}, bf16[1,128,768]{2,1,0:T(8,128)(2,1)S(1)}, u32[]{:S(2)}, u32[]{:S(2)}) collective-permute-start(bf16[1,128,768]{2,1,0:T(8,128)(2,1)S(1)} %get-tuple-element.88), channel_id=1, source_target_pairs={{0,1},{1,0},{2,3},{3,2},{4,5},{5,4},{6,7},{7,6},{8,9},{9,8},{10,11... | collective-permute-start | bytes 589832 | tf_op jit(solution)/shard_map/ppermute | solution.py:525
  81.3 10.4 %collective-permute-start.31 = (bf16[1,128,768]{2,1,0:T(8,128)(2,1)S(1)}, bf16[1,128,768]{2,1,0:T(8,128)(2,1)S(1)}, u32[]{:S(2)}, u32[]{:S(2)}) collective-permute-start(bf16[1,128,768]{2,1,0:T(8,128)(2,1)S(1)} %fold.18.refs_3_), channel_id=1, source_target_pairs={{0,2},{1,3},{2,0},{3,1},{4,6},{5,7},{6,4},{7,5},{8,10},{9,11},{10,... | collective-permute-start | bytes 589832 | tf_op jit(solution)/shard_map/ppermute | solution.py:525
  86.6 6.0 %collective-permute-start.29 = (bf16[1,128,512]{2,1,0:T(8,128)(2,1)S(1)}, bf16[1,128,512]{2,1,0:T(8,128)(2,1)S(1)}, u32[]{:S(2)}, u32[]{:S(2)}) collective-permute-start(bf16[1,128,512]{2,1,0:T(8,128)(2,1)S(1)} %get-tuple-element.86), channel_id=1, source_target_pairs={{0,1},{1,0},{2,3},{3,2},{4,5},{5,4},{6,7},{7,6},{8,9},{9,8},{10,11... | collective-permute-start | bytes 393224 | tf_op jit(solution)/shard_map/ppermute | solution.py:525
  86.6 4.5 %collective-permute-start.22 = (bf16[128,256]{1,0:T(8,128)(2,1)S(1)}, bf16[128,256]{1,0:T(8,128)(2,1)S(1)}, u32[]{:S(2)}, u32[]{:S(2)}) collective-permute-start(bf16[128,256]{1,0:T(8,128)(2,1)S(1)} %get-tuple-element.82.refs_2_.refs_0_.q_ref), channel_id=1, source_target_pairs={{0,2},{1,3},{2,0},{3,1},{4,6},{5,7},{6,4},{7,5},{8,10},{9,11},{10,... | collective-permute-start | bytes 196616 | tf_op jit(solution)/shard_map/ppermute | solution.py:525
  87.1 5.6 %collective-permute-start.23 = (bf16[128,256]{1,0:T(8,128)(2,1)S(1)}, bf16[128,256]{1,0:T(8,128)(2,1)S(1)}, u32[]{:S(2)}, u32[]{:S(2)}) collective-permute-start(bf16[128,256]{1,0:T(8,128)(2,1)S(1)} %get-tuple-element.82.refs_2_.refs_0_.q_ref), channel_id=1, source_target_pairs={{0,1},{1,0},{2,3},{3,2},{4,5},{5,4},{6,7},{7,6},{8,9},{9,8},{10,11... | collective-permute-start | bytes 196616 | tf_op jit(solution)/shard_map/ppermute | solution.py:525
  91.1 6.2 %collective-permute-start.35 = (bf16[1,128,512]{2,1,0:T(8,128)(2,1)S(1)}, bf16[1,128,512]{2,1,0:T(8,128)(2,1)S(1)}, u32[]{:S(2)}, u32[]{:S(2)}) collective-permute-start(bf16[1,128,512]{2,1,0:T(8,128)(2,1)S(1)} %get-tuple-element.95), channel_id=1, source_target_pairs={{0,1},{1,0},{2,3},{3,2},{4,5},{5,4},{6,7},{7,6},{8,9},{9,8},{10,11... | collective-permute-start | bytes 393224 | tf_op jit(solution)/shard_map/ppermute | solution.py:525
  91.7 6.7 %collective-permute-start.36 = (bf16[1,128,512]{2,1,0:T(8,128)(2,1)S(1)}, bf16[1,128,512]{2,1,0:T(8,128)(2,1)S(1)}, u32[]{:S(2)}, u32[]{:S(2)}) collective-permute-start(bf16[1,128,512]{2,1,0:T(8,128)(2,1)S(1)} %fold.19.refs_10_), channel_id=1, source_target_pairs={{0,2},{1,3},{2,0},{3,1},{4,6},{5,7},{6,4},{7,5},{8,10},{9,11},{10,... | collective-permute-start | bytes 393224 | tf_op jit(solution)/shard_map/ppermute | solution.py:525
  94.9 3.9 %collective-permute-start.37 = (bf16[1,128,512]{2,1,0:T(8,128)(2,1)S(1)}, bf16[1,128,512]{2,1,0:T(8,128)(2,1)S(1)}, u32[]{:S(2)}, u32[]{:S(2)}) collective-permute-start(bf16[1,128,512]{2,1,0:T(8,128)(2,1)S(1)} %get-tuple-element.98), channel_id=1, source_target_pairs={{0,1},{1,0},{2,3},{3,2},{4,5},{5,4},{6,7},{7,6},{8,9},{9,8},{10,11... | collective-permute-start | bytes 393224 | tf_op jit(solution)/shard_map/ppermute | solution.py:525
  95.3 5.7 %collective-permute-start.38 = (bf16[1,128,512]{2,1,0:T(8,128)(2,1)S(1)}, bf16[1,128,512]{2,1,0:T(8,128)(2,1)S(1)}, u32[]{:S(2)}, u32[]{:S(2)}) collective-permute-start(bf16[1,128,512]{2,1,0:T(8,128)(2,1)S(1)} %fold.20.refs_10_), channel_id=1, source_target_pairs={{0,2},{1,3},{2,0},{3,1},{4,6},{5,7},{6,4},{7,5},{8,10},{9,11},{10,... | collective-permute-start | bytes 393224 | tf_op jit(solution)/shard_map/ppermute | solution.py:525
  97.0 4.5 %collective-permute-start.32 = (bf16[1,128,256]{2,1,0:T(8,128)(2,1)S(1)}, bf16[1,128,256]{2,1,0:T(8,128)(2,1)S(1)}, u32[]{:S(2)}, u32[]{:S(2)}) collective-permute-start(bf16[1,128,256]{2,1,0:T(8,128)(2,1)S(1)} %get-tuple-element.91), channel_id=1, source_target_pairs={{0,1},{1,0},{2,3},{3,2},{4,5},{5,4},{6,7},{7,6},{8,9},{9,8},{10,11... | collective-permute-start | bytes 196616 | tf_op jit(solution)/shard_map/ppermute | solution.py:525
  97.4 4.9 %collective-permute-start.34 = (bf16[1,128,256]{2,1,0:T(8,128)(2,1)S(1)}, bf16[1,128,256]{2,1,0:T(8,128)(2,1)S(1)}, u32[]{:S(2)}, u32[]{:S(2)}) collective-permute-start(bf16[1,128,256]{2,1,0:T(8,128)(2,1)S(1)} %fold.21.refs_3_), channel_id=1, source_target_pairs={{0,2},{1,3},{2,0},{3,1},{4,6},{5,7},{6,4},{7,5},{8,10},{9,11},{10,... | collective-permute-start | bytes 196616 | tf_op jit(solution)/shard_map/ppermute | solution.py:525
  106.4 4.5 %collective-permute-start.40 = (f32[8,128]{1,0:T(8,128)S(1)}, f32[8,128]{1,0:T(8,128)S(1)}, u32[]{:S(2)}, u32[]{:S(2)}) collective-permute-start(f32[8,128]{1,0:T(8,128)S(1)} %merge.1.refs_0_), channel_id=1, source_target_pairs={{0,8},{4,12},{8,0},{12,4},{1,9},{5,13},{9,1},{13,5},{2,10},{6,14},... | collective-permute-start | bytes 12296 | tf_op jit(solution)/shard_map/ppermute | solution.py:525
  111.3 8.8 %collective-permute-start.42 = (bf16[64,2048]{1,0:T(8,128)(2,1)S(1)}, bf16[64,2048]{1,0:T(8,128)(2,1)S(1)}, u32[]{:S(2)}, u32[]{:S(2)}) collective-permute-start(bf16[64,2048]{1,0:T(8,128)(2,1)S(1)} %get-tuple-element.105), channel_id=1, source_target_pairs={{0,2},{1,3},{2,0},{3,1},{4,6},{5,7},{6,4},{7,5},{8,10},{9,11},{10,... | collective-permute-start | bytes 786440 | tf_op jit(solution)/shard_map/ppermute | solution.py:525
  113.0 12.1 %collective-permute-start.41 = (bf16[64,2176]{1,0:T(8,128)(2,1)S(1)}, bf16[64,2176]{1,0:T(8,128)(2,1)S(1)}, u32[]{:S(2)}, u32[]{:S(2)}) collective-permute-start(bf16[64,2176]{1,0:T(8,128)(2,1)S(1)} %get-tuple-element.104), channel_id=1, source_target_pairs={{0,2},{1,3},{2,0},{3,1},{4,6},{5,7},{6,4},{7,5},{8,10},{9,11},{10,... | collective-permute-start | bytes 835592 | tf_op jit(solution)/shard_map/ppermute | solution.py:525
  113.4 7.3 %collective-permute-start.43 = (bf16[64,2048]{1,0:T(8,128)(2,1)S(1)}, bf16[64,2048]{1,0:T(8,128)(2,1)S(1)}, u32[]{:S(2)}, u32[]{:S(2)}) collective-permute-start(bf16[64,2048]{1,0:T(8,128)(2,1)S(1)} %get-tuple-element.105), channel_id=1, source_target_pairs={{0,1},{1,0},{2,3},{3,2},{4,5},{5,4},{6,7},{7,6},{8,9},{9,8},{10,11... | collective-permute-start | bytes 786440 | tf_op jit(solution)/shard_map/ppermute | solution.py:525
  120.1 10.7 %collective-permute-start.45 = (bf16[64,2176]{1,0:T(8,128)(2,1)S(1)}, bf16[64,2176]{1,0:T(8,128)(2,1)S(1)}, u32[]{:S(2)}, u32[]{:S(2)}) collective-permute-start(bf16[64,2176]{1,0:T(8,128)(2,1)S(1)} %get-tuple-element.104), channel_id=1, source_target_pairs={{0,1},{1,0},{2,3},{3,2},{4,5},{5,4},{6,7},{7,6},{8,9},{9,8},{10,11... | collective-permute-start | bytes 835592 | tf_op jit(solution)/shard_map/ppermute | solution.py:525
  125.1 5.8 %collective-permute-start.46 = (bf16[64,2176]{1,0:T(8,128)(2,1)S(1)}, bf16[64,2176]{1,0:T(8,128)(2,1)S(1)}, u32[]{:S(2)}, u32[]{:S(2)}) collective-permute-start(bf16[64,2176]{1,0:T(8,128)(2,1)S(1)} %tie.19), channel_id=1, source_target_pairs={{0,1},{1,0},{2,3},{3,2},{4,5},{5,4},{6,7},{7,6},{8,9},{9,8},{10,11... | collective-permute-start | bytes 835592 | tf_op jit(solution)/shard_map/ppermute | solution.py:525
  125.3 9.6 %collective-permute-start.47 = (bf16[2,4,16,1024]{3,2,1,0:T(8,128)(2,1)S(1)}, bf16[2,4,16,1024]{3,2,1,0:T(8,128)(2,1)S(1)}, u32[]{:S(2)}, u32[]{:S(2)}) collective-permute-start(bf16[2,4,16,1024]{3,2,1,0:T(8,128)(2,1)S(1)} %get-tuple-element.110), channel_id=1, source_target_pairs={{0,4},{4,0},{8,12},{12,8},{1,5},{5,1},{9,13},{13,9},{2,6},{6,2},{1... | collective-permute-start | bytes 786440 | tf_op jit(solution)/shard_map/ppermute | solution.py:525
  130.3 12.5 %collective-permute-start.49 = (bf16[2,4,16,1024]{3,2,1,0:T(8,128)(2,1)S(1)}, bf16[2,4,16,1024]{3,2,1,0:T(8,128)(2,1)S(1)}, u32[]{:S(2)}, u32[]{:S(2)}) collective-permute-start(bf16[2,4,16,1024]{3,2,1,0:T(8,128)(2,1)S(1)} %get-tuple-element.111), channel_id=1, source_target_pairs={{0,4},{4,0},{8,12},{12,8},{1,5},{5,1},{9,13},{13,9},{2,6},{6,2},{1... | collective-permute-start | bytes 786440 | tf_op jit(solution)/shard_map/ppermute | solution.py:525
  135.0 17.2 %collective-permute-start.48 = (bf16[2,4,16,1280]{3,2,1,0:T(8,128)(2,1)S(1)}, bf16[2,4,16,1280]{3,2,1,0:T(8,128)(2,1)S(1)}, u32[]{:S(2)}, u32[]{:S(2)}) collective-permute-start(bf16[2,4,16,1280]{3,2,1,0:T(8,128)(2,1)S(1)} %tie.20), channel_id=1, source_target_pairs={{0,4},{4,0},{8,12},{12,8},{1,5},{5,1},{9,13},{13,9},{2,6},{6,2},{1... | collective-permute-start | bytes 983048 | tf_op jit(solution)/shard_map/ppermute | solution.py:525
  136.7 11.7 %collective-permute-start.51 = (bf16[1,4,16,1024]{3,2,1,0:T(8,128)(2,1)S(1)}, bf16[1,4,16,1024]{3,2,1,0:T(8,128)(2,1)S(1)}, u32[]{:S(2)}, u32[]{:S(2)}) collective-permute-start(bf16[1,4,16,1024]{3,2,1,0:T(8,128)(2,1)S(1)} %fold.22.refs_5_), channel_id=1, source_target_pairs={{0,8},{4,12},{8,0},{12,4},{1,9},{5,13},{9,1},{13,5},{2,10},{6,14},... | collective-permute-start | bytes 393224 | tf_op jit(solution)/shard_map/ppermute | solution.py:525
  148.4 10.9 %collective-permute-start.52 = (bf16[2,4,16,768]{3,2,1,0:T(8,128)(2,1)S(1)}, bf16[2,4,16,768]{3,2,1,0:T(8,128)(2,1)S(1)}, u32[]{:S(2)}, u32[]{:S(2)}) collective-permute-start(bf16[2,4,16,768]{3,2,1,0:T(8,128)(2,1)S(1)} %tie.21), channel_id=1, source_target_pairs={{0,4},{4,0},{8,12},{12,8},{1,5},{5,1},{9,13},{13,9},{2,6},{6,2},{1... | collective-permute-start | bytes 589832 | tf_op jit(solution)/shard_map/ppermute | solution.py:525
  152.1 15.6 %collective-permute-start.54 = (bf16[1,4,16,1024]{3,2,1,0:T(8,128)(2,1)S(1)}, bf16[1,4,16,1024]{3,2,1,0:T(8,128)(2,1)S(1)}, u32[]{:S(2)}, u32[]{:S(2)}) collective-permute-start(bf16[1,4,16,1024]{3,2,1,0:T(8,128)(2,1)S(1)} %fold.23.refs_2_), channel_id=1, source_target_pairs={{0,8},{4,12},{8,0},{12,4},{1,9},{5,13},{9,1},{13,5},{2,10},{6,14},... | collective-permute-start | bytes 393224 | tf_op jit(solution)/shard_map/ppermute | solution.py:525
  152.3 19.5 %collective-permute-start.50 = (bf16[1,4,16,1280]{3,2,1,0:T(8,128)(2,1)S(1)}, bf16[1,4,16,1280]{3,2,1,0:T(8,128)(2,1)S(1)}, u32[]{:S(2)}, u32[]{:S(2)}) collective-permute-start(bf16[1,4,16,1280]{3,2,1,0:T(8,128)(2,1)S(1)} %fold.24.refs_2_), channel_id=1, source_target_pairs={{0,8},{4,12},{8,0},{12,4},{1,9},{5,13},{9,1},{13,5},{2,10},{6,14},... | collective-permute-start | bytes 491528 | tf_op jit(solution)/shard_map/ppermute | solution.py:525
  159.5 12.3 %collective-permute-start.53 = (bf16[1,4,16,768]{3,2,1,0:T(8,128)(2,1)S(1)}, bf16[1,4,16,768]{3,2,1,0:T(8,128)(2,1)S(1)}, u32[]{:S(2)}, u32[]{:S(2)}) collective-permute-start(bf16[1,4,16,768]{3,2,1,0:T(8,128)(2,1)S(1)} %fold.25.refs_6_), channel_id=1, source_target_pairs={{0,8},{4,12},{8,0},{12,4},{1,9},{5,13},{9,1},{13,5},{2,10},{6,14},... | collective-permute-start | bytes 294920 | tf_op jit(solution)/shard_map/ppermute | solution.py:525
  (17 other events, 88.9 us)

commit v16 on v15

--- a/solution.py
+++ b/solution.py
@@ -481,9 +481,9 @@
         column += span
 
 
-def close(place, index, tokens, chunks, r, groups, out, after):
+def close(place, index, tokens, chunks, r, g, groups, out, after):
     _, owners, piece, _ = groups[0][0].shape
-    width = tokens.shape[1]
+    span, width = sum(terms[0].shape[-1] for terms in groups), tokens.shape[1]
     at = jnp.stack([place, index * chunks + r]).astype(jnp.int32)
     flat = [term for terms in groups for term in terms]
     into = [] if out is None else [out]
@@ -492,11 +492,11 @@
         grid_spec=pltpu.PrefetchScalarGridSpec(
             num_scalar_prefetch=1,
             grid=(1,),
-            in_specs=[pl.BlockSpec((owners, piece, width), lambda j, at: (at[1], 0, 0))]
+            in_specs=[pl.BlockSpec((owners, piece, span), lambda j, at: (at[1], 0, g))]
             + [pl.BlockSpec((1,) + t.shape[1:], lambda j, at: (0, 0, 0, 0)) for t in flat]
             + anywhere(into) + anywhere(after),
             out_specs=(
-                pl.BlockSpec((owners, piece, width), lambda j, at: (r, 0, 0)),
+                pl.BlockSpec((owners, piece, span), lambda j, at: (r, 0, g)),
                 pl.BlockSpec((8, DH), lambda j, at: (0, 0)),
             ),
         ),
@@ -647,15 +647,13 @@
             whole = jnp.dot(whole, w_out, preferred_element_type=f32).astype(bf16)
             whole = whole.reshape(owners, zs, piece, -1).swapaxes(0, 1)
             whole = lax.psum_scatter(whole, "head", scatter_dimension=0, tiled=True)
-            out, _ = close(place, index, tokens, chunks, r, [[whole]], out, [])
+            out, _ = close(place, index, tokens, chunks, r, 0, [[whole]], out, [])
         return out.reshape(cand // zs, -1)
     slots = [reverse(k, bits_of("head")) for k in range(zs)]
-    unit = columns // 8
-    spans = [[columns]] * chunks
-    if unit % (2 * DH) == 0 and chunks == 2:
-        spans = [[4 * unit, 4 * unit], [5 * unit, 3 * unit]]
+    groups = 2 if columns % 1024 == 0 else 1
+    span = columns // groups
     counts = [zs // 2] * 2 if zs > 1 else [1]
-    plan = [(r, sum(row[:g]), span) for r, row in enumerate(spans) for g, span in enumerate(row)]
+    plan = [(r, g) for r in range(chunks) for g in range(groups)]
     chain, first_out, blocks, made, folded = [], [], {}, [], []
 
     def fold_next():
@@ -664,23 +662,27 @@
         folded.append(terms)
         return [sent]
 
-    for n, (r, column, span) in enumerate(plan):
+    for n, (r, g) in enumerate(plan):
         if r not in blocks:
             blocks[r] = gather(gated[r], "hist", first_out)
-        own, *others = output(index, slots, counts, blocks[r], w_out, column, span, chain)
+        own, *others = output(index, slots, counts, blocks[r], w_out, g * span, span, chain)
         before = made[n - 2][1] if n > 1 else []
         before = before + [folded[0][-1]] if folded else before
         made.append((own, [swap(tie(x, before), "head", 0) for x in others]))
         chain, first_out = [own], first_out or [own]
         if n == 2:
             chain = fold_next()
-    done = 0
-    for r, row in enumerate(spans):
-        while len(folded) < min(len(plan), done + len(row) + 2):
+    closed = 0
+    while closed < len(plan):
+        if len(folded) < len(plan):
             chain = fold_next()
-        terms, done = folded[done:done + len(row)], done + len(row)
-        out, mark = close(place, index, tokens, chunks, r, terms, out, chain)
-        chain = [mark]
+        if len(folded) > closed + 2 or len(folded) == len(plan):
+            r, g = plan[closed]
+            some = 1 if r < chunks - 1 else groups
+            out, mark = close(
+                place, index, tokens, chunks, r, g, folded[closed:closed + some], out, chain
+            )
+            chain, closed = [mark], closed + some
     return out.reshape(cand // zs, -1)
 
 

time: 175 us -> 170 us (0.971)
  waiting for transfers between devices: 47.8 us -> 40.9 us
    ppermute x55, waiting for transfers between devices: 47.8 us -> 40.9 us  [swap(): lax.ppermute(x, axis, [(i, i ^ 1 << bit) for i in range(lax.axis_size(axi...]
    pallas_call x2 -> x3, Pallas kernels: 4.65 us -> 6.66 us  [close(): pl.pallas_call(functools.partial(close_kernel, [len(terms) for terms in g...]
  transfers between devices with their start and end apart: 55 -> 55, of which waited for: 14 -> 16; matrix products, arithmetic and copies ran while one was open for 0% -> 0% of each run, Pallas kernels for 41% -> 43%
where the time goes in v16:
time: 170 us
  Pallas kernels  81.5 us (48%)
  starting transfers between devices  44.1 us (26%)
  waiting for transfers between devices  40.9 us (24%)
  local copies, waits for them, and re-layouts  2.4 us (1%)
    ppermute x55, starting transfers between devices, swap(): lax.ppermute(x, axis, [(i, i ^ 1 << bit) for i in range(lax.axis_size(axi...  44.1 us
    ppermute x55, waiting for transfers between devices, swap(): lax.ppermute(x, axis, [(i, i ^ 1 << bit) for i in range(lax.axis_size(axi...  40.9 us
    pallas_call x5, Pallas kernels, project(): pl.pallas_call(functools.partial(project_kernel, parts, owners, len(after...  37.9 us
    pallas_call x4, Pallas kernels, output(): pl.pallas_call(functools.partial(output_kernel, owners, slots, len(after)...  13.9 us
    pallas_call x4, Pallas kernels, attend(): pl.pallas_call(functools.partial(attend_kernel, owners, len(counts)), gri...  12.5 us
    pallas_call x3, Pallas kernels, close(): pl.pallas_call(functools.partial(close_kernel, [len(terms) for terms in g...  6.66 us
    pallas_call x13, Pallas kernels, fold(): pl.pallas_call(functools.partial(fold_kernel, len(terms)), grid=(steps,),...  4.76 us
    pallas_call x4, Pallas kernels, activate(): pl.pallas_call(functools.partial(activate_kernel, [len(terms) for terms i...  3.41 us
  transfers between devices with their start and end apart: 55, of which 16 were waited for; matrix products, arithmetic and copies ran while one was open for 0% of the time, Pallas kernels for 43%

profile of v16, /device:TPU:0, one launch (start us, length us, event | category | flops | bytes accessed | tf_op | source)
XLA Modules:
  0.0 169.7 jit_solution(13475464973092866684)
XLA Ops:
  0.0 5.5 %project.5 = (bf16[2,4,128,256]{3,2,1,0:T(8,128)(2,1)S(1)}, bf16[1,4,128,256]{3,2,1,0:T(8,128)(2,1)S(1)}, bf16[1,4,128,256]{3,2,1,0:T(8,128)(2,1)S(1)}) custom-call(s32[1]{0:T(128)} %bitcast.at_ref, bf16[4,2,4,16,2048]{4,3,2,1,0:T(8,128)(2,1)} %bitcast.57, bf16[4,2,4,16,2048]{4,3,2,1,0:T(8,128)(2,1)} %bitcast.58, bf16[4,2,4,16,2048]{4,3,2,1,0:T(8,128)(2,1)} %bitcast.59, ...), custom_call_target="tpu_custom_call" | custom-call | flops 1000 | bytes 1000 | tf_op jit(solution)/shard_map/project/pallas_call | solution.py:80
  6.1 8.7 %project.6 = (bf16[2,4,128,512]{3,2,1,0:T(8,128)(2,1)S(1)}, bf16[1,4,128,512]{3,2,1,0:T(8,128)(2,1)S(1)}, bf16[1,4,128,512]{3,2,1,0:T(8,128)(2,1)S(1)}) custom-call(s32[1]{0:T(128)} %bitcast.at_ref, bf16[4,2,4,16,2048]{4,3,2,1,0:T(8,128)(2,1)} %bitcast.61, bf16[4,2,4,16,2048]{4,3,2,1,0:T(8,128)(2,1)} %bitcast.62, bf16[4,2,4,16,2048]{4,3,2,1,0:T(8,128)(2,1)} %bitcast.63, ...), custom_call_target="tpu_custom_call" | custom-call | flops 1000 | bytes 1000 | tf_op jit(solution)/shard_map/project/pallas_call | solution.py:80
  15.8 3.0 %collective-permute-start.4 = (bf16[1,4,128,256]{3,2,1,0:T(8,128)(2,1)S(1)}, bf16[1,4,128,256]{3,2,1,0:T(8,128)(2,1)S(1)}, u32[]{:S(2)}, u32[]{:S(2)}) collective-permute-start(bf16[1,4,128,256]{3,2,1,0:T(8,128)(2,1)S(1)} %fold.13.refs_8_), channel_id=1, source_target_pairs={{0,2},{1,3},{2,0},{3,1},{4,6},{5,7},{6,4},{7,5},{8,10},{9,11},{10,... | collective-permute-start | bytes 786440 | tf_op jit(solution)/shard_map/ppermute | solution.py:525
  18.7 8.7 %project.7 = (bf16[2,4,128,512]{3,2,1,0:T(8,128)(2,1)S(1)}, bf16[1,4,128,512]{3,2,1,0:T(8,128)(2,1)S(1)}, bf16[1,4,128,512]{3,2,1,0:T(8,128)(2,1)S(1)}) custom-call(s32[1]{0:T(128)} %bitcast.at_ref, bf16[4,2,4,16,2048]{4,3,2,1,0:T(8,128)(2,1)} %bitcast.68, bf16[4,2,4,16,2048]{4,3,2,1,0:T(8,128)(2,1)} %bitcast.66, bf16[4,2,4,16,2048]{4,3,2,1,0:T(8,128)(2,1)} %bitcast.67, ...), custom_call_target="tpu_custom_call" | custom-call | flops 1000 | bytes 1000 | tf_op jit(solution)/shard_map/project/pallas_call | solution.py:80
  28.5 8.8 %project.8 = (bf16[2,4,128,512]{3,2,1,0:T(8,128)(2,1)S(1)}, bf16[1,4,128,512]{3,2,1,0:T(8,128)(2,1)S(1)}, bf16[1,4,128,512]{3,2,1,0:T(8,128)(2,1)S(1)}) custom-call(s32[1]{0:T(128)} %bitcast.at_ref, bf16[4,2,4,16,2048]{4,3,2,1,0:T(8,128)(2,1)} %bitcast.69, bf16[4,2,4,16,2048]{4,3,2,1,0:T(8,128)(2,1)} %bitcast.70, bf16[4,2,4,16,2048]{4,3,2,1,0:T(8,128)(2,1)} %bitcast.71, ...), custom_call_target="tpu_custom_call" | custom-call | flops 1000 | bytes 1000 | tf_op jit(solution)/shard_map/project/pallas_call | solution.py:80
  39.1 1.9 %collective-permute-start.12 = (bf16[1,4,128,512]{3,2,1,0:T(8,128)(2,1)}, bf16[1,4,128,512]{3,2,1,0:T(8,128)(2,1)}, u32[]{:S(2)}, u32[]{:S(2)}) collective-permute-start(bf16[1,4,128,512]{3,2,1,0:T(8,128)(2,1)} %fold.15.refs_6_), channel_id=1, source_target_pairs={{0,2},{1,3},{2,0},{3,1},{4,6},{5,7},{6,4},{7,5},{8,10},{9,11},{10,... | collective-permute-start | bytes 1572872 | tf_op jit(solution)/shard_map/ppermute | solution.py:525
  41.0 1.4 collective-permute-done.8.refs_5_
  44.2 1.7 %collective-permute-start.17 = (bf16[1,4,128,512]{3,2,1,0:T(8,128)(2,1)}, bf16[1,4,128,512]{3,2,1,0:T(8,128)(2,1)}, u32[]{:S(2)}, u32[]{:S(2)}) collective-permute-start(bf16[1,4,128,512]{3,2,1,0:T(8,128)(2,1)} %fold.16.refs_8_), channel_id=1, source_target_pairs={{0,2},{1,3},{2,0},{3,1},{4,6},{5,7},{6,4},{7,5},{8,10},{9,11},{10,... | collective-permute-start | bytes 1572872 | tf_op jit(solution)/shard_map/ppermute | solution.py:525
  45.9 6.1 %project.9 = (bf16[2,4,128,256]{3,2,1,0:T(8,128)(2,1)S(1)}, bf16[1,4,128,256]{3,2,1,0:T(8,128)(2,1)S(1)}, bf16[1,4,128,256]{3,2,1,0:T(8,128)(2,1)}) custom-call(s32[1]{0:T(128)} %bitcast.at_ref, bf16[4,2,4,16,2048]{4,3,2,1,0:T(8,128)(2,1)} %bitcast.73, bf16[4,2,4,16,2048]{4,3,2,1,0:T(8,128)(2,1)} %bitcast.74, bf16[4,2,4,16,2048]{4,3,2,1,0:T(8,128)(2,1)} %bitcast.75, ...), custom_call_target="tpu_custom_call" | custom-call | flops 1000 | bytes 1000 | tf_op jit(solution)/shard_map/project/pallas_call | solution.py:80
  53.3 5.0 %collective-permute-done.18.refs_1_ = bf16[128,768]{1,0:T(8,128)(2,1)S(1)} collective-permute-done((bf16[128,768]{1,0:T(8,128)(2,1)S(1)}, bf16[128,768]{1,0:T(8,128)(2,1)S(1)}, u32[]{:S(2)}, u32[]{:S(2)}) %collective-permute-start.18) | collective-permute-done | bytes 196640 | tf_op jit(solution)/shard_map/ppermute | solution.py:525
  58.5 1.0 copy-done.3
  59.6 1.4 activate.5
  60.9 1.1 fold.17.refs_10_
  62.1 4.1 %attend.4 = (bf16[2,128,768]{2,1,0:T(8,128)(2,1)S(1)}, bf16[1,128,768]{2,1,0:T(8,128)(2,1)S(1)}, bf16[1,128,768]{2,1,0:T(8,128)(2,1)S(1)}) custom-call(s32[1]{0:T(128)} %bitcast.at_ref, bf16[128,768]{1,0:T(8,128)(2,1)S(1)} %get-tuple-element.74.refs_2_.refs_0_.q_ref, bf16[128,768]{1,0:T(8,128)(2,1)S(1)} %collective-permute-done.18.refs_1_, ...), custom_call_target="tpu_custom_call" | custom-call | flops 1000 | bytes 1000 | tf_op jit(solution)/shard_map/attend/pallas_call | solution.py:262
  66.7 1.8 %collective-permute-start.14 = (bf16[128,512]{1,0:T(8,128)(2,1)S(1)}, bf16[128,512]{1,0:T(8,128)(2,1)S(1)}, u32[]{:S(2)}, u32[]{:S(2)}) collective-permute-start(bf16[128,512]{1,0:T(8,128)(2,1)S(1)} %get-tuple-element.79.refs_2_.refs_0_.q_ref), channel_id=1, source_target_pairs={{0,2},{1,3},{2,0},{3,1},{4,6},{5,7},{6,4},{7,5},{8,10},{9,11},{10,... | collective-permute-start | bytes 393224 | tf_op jit(solution)/shard_map/ppermute | solution.py:525
  68.8 4.0 %collective-permute-done.14.refs_1_ = bf16[128,512]{1,0:T(8,128)(2,1)S(1)} collective-permute-done((bf16[128,512]{1,0:T(8,128)(2,1)S(1)}, bf16[128,512]{1,0:T(8,128)(2,1)S(1)}, u32[]{:S(2)}, u32[]{:S(2)}) %collective-permute-start.14) | collective-permute-done | bytes 131104 | tf_op jit(solution)/shard_map/ppermute | solution.py:525
  73.5 1.4 activate.6
  74.9 2.1 %collective-permute-start.25 = (bf16[128,512]{1,0:T(8,128)(2,1)S(1)}, bf16[128,512]{1,0:T(8,128)(2,1)S(1)}, u32[]{:S(2)}, u32[]{:S(2)}) collective-permute-start(bf16[128,512]{1,0:T(8,128)(2,1)S(1)} %get-tuple-element.82.refs_10_.refs_0_.q_ref), channel_id=1, source_target_pairs={{0,2},{1,3},{2,0},{3,1},{4,6},{5,7},{6,4},{7,5},{8,10},{9,11},{10,... | collective-permute-start | bytes 393224 | tf_op jit(solution)/shard_map/ppermute | solution.py:525
  77.0 3.1 %attend.5 = (bf16[2,128,512]{2,1,0:T(8,128)(2,1)S(1)}, bf16[1,128,512]{2,1,0:T(8,128)(2,1)S(1)}, bf16[1,128,512]{2,1,0:T(8,128)(2,1)S(1)}) custom-call(s32[1]{0:T(128)} %bitcast.at_ref, bf16[128,512]{1,0:T(8,128)(2,1)S(1)} %get-tuple-element.79.refs_2_.refs_0_.q_ref, bf16[128,512]{1,0:T(8,128)(2,1)S(1)} %collective-permute-done.14.refs_1_, ...), custom_call_target="tpu_custom_call" | custom-call | flops 1000 | bytes 1000 | tf_op jit(solution)/shard_map/attend/pallas_call | solution.py:262
  81.3 1.7 collective-permute-start.31
  83.3 3.2 %attend.6 = (bf16[2,128,512]{2,1,0:T(8,128)(2,1)S(1)}, bf16[1,128,512]{2,1,0:T(8,128)(2,1)S(1)}, bf16[1,128,512]{2,1,0:T(8,128)(2,1)S(1)}) custom-call(s32[1]{0:T(128)} %bitcast.at_ref, bf16[128,512]{1,0:T(8,128)(2,1)S(1)} %get-tuple-element.82.refs_10_.refs_0_.q_ref, bf16[128,512]{1,0:T(8,128)(2,1)S(1)} %collective-permute-done.25.refs_1_, ...), custom_call_target="tpu_custom_call" | custom-call | flops 1000 | bytes 1000 | tf_op jit(solution)/shard_map/attend/pallas_call | solution.py:262
  87.2 3.9 %collective-permute-done.22.refs_1_ = bf16[128,256]{1,0:T(8,128)(2,1)S(1)} collective-permute-done((bf16[128,256]{1,0:T(8,128)(2,1)S(1)}, bf16[128,256]{1,0:T(8,128)(2,1)S(1)}, u32[]{:S(2)}, u32[]{:S(2)}) %collective-permute-start.22) | collective-permute-done | bytes 65568 | tf_op jit(solution)/shard_map/ppermute | solution.py:525
  92.7 2.0 %attend.7 = (bf16[2,128,256]{2,1,0:T(8,128)(2,1)S(1)}, bf16[1,128,256]{2,1,0:T(8,128)(2,1)S(1)}, bf16[1,128,256]{2,1,0:T(8,128)(2,1)S(1)}) custom-call(s32[1]{0:T(128)} %bitcast.at_ref, bf16[128,256]{1,0:T(8,128)(2,1)S(1)} %get-tuple-element.84.refs_2_.refs_0_.q_ref, bf16[128,256]{1,0:T(8,128)(2,1)S(1)} %collective-permute-done.22.refs_1_, ...), custom_call_target="tpu_custom_call" | custom-call | flops 1000 | bytes 1000 | tf_op jit(solution)/shard_map/attend/pallas_call | solution.py:262
  95.3 1.7 collective-permute-start.38
  98.8 2.3 %collective-permute-done.38.refs_2_ = bf16[1,128,512]{2,1,0:T(8,128)(2,1)S(1)} collective-permute-done((bf16[1,128,512]{2,1,0:T(8,128)(2,1)S(1)}, bf16[1,128,512]{2,1,0:T(8,128)(2,1)S(1)}, u32[]{:S(2)}, u32[]{:S(2)}) %collective-permute-start.38) | collective-permute-done | bytes 131104 | tf_op jit(solution)/shard_map/ppermute | solution.py:525
  102.7 1.8 %collective-permute-start.39 = (f32[8,128]{1,0:T(8,128)S(1)}, f32[8,128]{1,0:T(8,128)S(1)}, u32[]{:S(2)}, u32[]{:S(2)}) collective-permute-start(f32[8,128]{1,0:T(8,128)S(1)} %get-tuple-element.104.refs_0_), channel_id=1, source_target_pairs={{0,4},{4,0},{8,12},{12,8},{1,5},{5,1},{9,13},{13,9},{2,6},{6,2},{1... | collective-permute-start | bytes 12296 | tf_op jit(solution)/shard_map/ppermute | solution.py:525
  104.5 1.9 %collective-permute-done.39.refs_1_ = f32[8,128]{1,0:T(8,128)S(1)} collective-permute-done((f32[8,128]{1,0:T(8,128)S(1)}, f32[8,128]{1,0:T(8,128)S(1)}, u32[]{:S(2)}, u32[]{:S(2)}) %collective-permute-start.39) | collective-permute-done | bytes 4128 | tf_op jit(solution)/shard_map/ppermute | solution.py:525
  106.4 2.8 %collective-permute-start.40 = (f32[8,128]{1,0:T(8,128)S(1)}, f32[8,128]{1,0:T(8,128)S(1)}, u32[]{:S(2)}, u32[]{:S(2)}) collective-permute-start(f32[8,128]{1,0:T(8,128)S(1)} %merge.1.refs_0_), channel_id=1, source_target_pairs={{0,8},{4,12},{8,0},{12,4},{1,9},{5,13},{9,1},{13,5},{2,10},{6,14},... | collective-permute-start | bytes 12296 | tf_op jit(solution)/shard_map/ppermute | solution.py:525
  109.1 1.7 %collective-permute-done.40.refs_1_ = f32[8,128]{1,0:T(8,128)S(1)} collective-permute-done((f32[8,128]{1,0:T(8,128)S(1)}, f32[8,128]{1,0:T(8,128)S(1)}, u32[]{:S(2)}, u32[]{:S(2)}) %collective-permute-start.40) | collective-permute-done | bytes 4128 | tf_op jit(solution)/shard_map/ppermute | solution.py:525
  111.3 1.7 %collective-permute-start.42 = (bf16[64,2048]{1,0:T(8,128)(2,1)S(1)}, bf16[64,2048]{1,0:T(8,128)(2,1)S(1)}, u32[]{:S(2)}, u32[]{:S(2)}) collective-permute-start(bf16[64,2048]{1,0:T(8,128)(2,1)S(1)} %get-tuple-element.107), channel_id=1, source_target_pairs={{0,2},{1,3},{2,0},{3,1},{4,6},{5,7},{6,4},{7,5},{8,10},{9,11},{10,... | collective-permute-start | bytes 786440 | tf_op jit(solution)/shard_map/ppermute | solution.py:525
  113.4 6.7 %collective-permute-done.42 = bf16[64,2048]{1,0:T(8,128)(2,1)S(1)} collective-permute-done((bf16[64,2048]{1,0:T(8,128)(2,1)S(1)}, bf16[64,2048]{1,0:T(8,128)(2,1)S(1)}, u32[]{:S(2)}, u32[]{:S(2)}) %collective-permute-start.42) | collective-permute-done | bytes 262176 | tf_op jit(solution)/shard_map/ppermute | solution.py:525
  121.7 3.4 %output.4 = (bf16[2,4,16,1024]{3,2,1,0:T(8,128)(2,1)S(1)}, bf16[2,4,16,1024]{3,2,1,0:T(8,128)(2,1)S(1)}) custom-call(s32[1]{0:T(128)} %bitcast.3.index_ref, bf16[4,16,2048]{2,1,0:T(8,128)(2,1)S(1)} %bitcast.47, bf16[4,16,2048]{2,1,0:T(8,128)(2,1)S(1)} %bitcast.49, bf16[4,16,2048]{2,1,0:T(8,128)(2,1)S(1)} %bitcast.51, bf16[4,16,2048]{2,1,0:T(8,128)(2,1)S(1)} %bitcast.53, ...), custom_call_target="tpu_custom_call" | custom-call | flops 1000 | bytes 1000 | tf_op jit(solution)/shard_map/output/pallas_call | solution.py:444
  125.3 1.6 collective-permute-start.47
  126.9 3.4 %output.5 = (bf16[2,4,16,1024]{3,2,1,0:T(8,128)(2,1)S(1)}, bf16[2,4,16,1024]{3,2,1,0:T(8,128)(2,1)S(1)}) custom-call(s32[1]{0:T(128)} %bitcast.3.index_ref, bf16[4,16,2048]{2,1,0:T(8,128)(2,1)S(1)} %bitcast.48, bf16[4,16,2048]{2,1,0:T(8,128)(2,1)S(1)} %bitcast.50, bf16[4,16,2048]{2,1,0:T(8,128)(2,1)S(1)} %bitcast.52, bf16[4,16,2048]{2,1,0:T(8,128)(2,1)S(1)} %bitcast.54, ...), custom_call_target="tpu_custom_call" | custom-call | flops 1000 | bytes 1000 | tf_op jit(solution)/shard_map/output/pallas_call | solution.py:444
  130.9 3.5 %output.6 = (bf16[2,4,16,1024]{3,2,1,0:T(8,128)(2,1)S(1)}, bf16[2,4,16,1024]{3,2,1,0:T(8,128)(2,1)S(1)}) custom-call(s32[1]{0:T(128)} %bitcast.3.index_ref, bf16[4,16,2176]{2,1,0:T(8,128)(2,1)S(1)} %bitcast.41, bf16[4,16,2176]{2,1,0:T(8,128)(2,1)S(1)} %bitcast.39, bf16[4,16,2176]{2,1,0:T(8,128)(2,1)S(1)} %bitcast.43, bf16[4,16,2176]{2,1,0:T(8,128)(2,1)S(1)} %bitcast.45, ...), custom_call_target="tpu_custom_call" | custom-call | flops 1000 | bytes 1000 | tf_op jit(solution)/shard_map/output/pallas_call | solution.py:444
  134.6 2.6 %collective-permute-start.51 = (bf16[1,4,16,1024]{3,2,1,0:T(8,128)(2,1)S(1)}, bf16[1,4,16,1024]{3,2,1,0:T(8,128)(2,1)S(1)}, u32[]{:S(2)}, u32[]{:S(2)}) collective-permute-start(bf16[1,4,16,1024]{3,2,1,0:T(8,128)(2,1)S(1)} %fold.22.refs_5_), channel_id=1, source_target_pairs={{0,8},{4,12},{8,0},{12,4},{1,9},{5,13},{9,1},{13,5},{2,10},{6,14},... | collective-permute-start | bytes 393224 | tf_op jit(solution)/shard_map/ppermute | solution.py:525
  137.2 1.6 collective-permute-start.48
  138.8 3.5 %output.7 = (bf16[2,4,16,1024]{3,2,1,0:T(8,128)(2,1)S(1)}, bf16[2,4,16,1024]{3,2,1,0:T(8,128)(2,1)S(1)}) custom-call(s32[1]{0:T(128)} %bitcast.3.index_ref, bf16[4,16,2176]{2,1,0:T(8,128)(2,1)S(1)} %bitcast.42, bf16[4,16,2176]{2,1,0:T(8,128)(2,1)S(1)} %bitcast.40, bf16[4,16,2176]{2,1,0:T(8,128)(2,1)S(1)} %bitcast.44, bf16[4,16,2176]{2,1,0:T(8,128)(2,1)S(1)} %bitcast.46, ...), custom_call_target="tpu_custom_call" | custom-call | flops 1000 | bytes 1000 | tf_op jit(solution)/shard_map/output/pallas_call | solution.py:444
  142.9 2.6 %collective-permute-start.52 = (bf16[2,4,16,1024]{3,2,1,0:T(8,128)(2,1)S(1)}, bf16[2,4,16,1024]{3,2,1,0:T(8,128)(2,1)S(1)}, u32[]{:S(2)}, u32[]{:S(2)}) collective-permute-start(bf16[2,4,16,1024]{3,2,1,0:T(8,128)(2,1)S(1)} %tie.21), channel_id=1, source_target_pairs={{0,4},{4,0},{8,12},{12,8},{1,5},{5,1},{9,13},{13,9},{2,6},{6,2},{1... | collective-permute-start | bytes 786440 | tf_op jit(solution)/shard_map/ppermute | solution.py:525
  145.7 2.4 %collective-permute-start.54 = (bf16[1,4,16,1024]{3,2,1,0:T(8,128)(2,1)S(1)}, bf16[1,4,16,1024]{3,2,1,0:T(8,128)(2,1)S(1)}, u32[]{:S(2)}, u32[]{:S(2)}) collective-permute-start(bf16[1,4,16,1024]{3,2,1,0:T(8,128)(2,1)S(1)} %fold.23.refs_2_), channel_id=1, source_target_pairs={{0,8},{4,12},{8,0},{12,4},{1,9},{5,13},{9,1},{13,5},{2,10},{6,14},... | collective-permute-start | bytes 393224 | tf_op jit(solution)/shard_map/ppermute | solution.py:525
  148.0 1.9 %collective-permute-done.48.refs_1_ = bf16[2,4,16,1024]{3,2,1,0:T(8,128)(2,1)S(1)} collective-permute-done((bf16[2,4,16,1024]{3,2,1,0:T(8,128)(2,1)S(1)}, bf16[2,4,16,1024]{3,2,1,0:T(8,128)(2,1)S(1)}, u32[]{:S(2)}, u32[]{:S(2)}) %collective-permute-start.48) | collective-permute-done | bytes 262176 | tf_op jit(solution)/shard_map/ppermute | solution.py:525
  150.0 3.1 %collective-permute-start.50 = (bf16[1,4,16,1024]{3,2,1,0:T(8,128)(2,1)S(1)}, bf16[1,4,16,1024]{3,2,1,0:T(8,128)(2,1)S(1)}, u32[]{:S(2)}, u32[]{:S(2)}) collective-permute-start(bf16[1,4,16,1024]{3,2,1,0:T(8,128)(2,1)S(1)} %fold.24.refs_3_), channel_id=1, source_target_pairs={{0,8},{4,12},{8,0},{12,4},{1,9},{5,13},{9,1},{13,5},{2,10},{6,14},... | collective-permute-start | bytes 393224 | tf_op jit(solution)/shard_map/ppermute | solution.py:525
  153.2 2.2 %close.3 = (bf16[8,16,2048]{2,1,0:T(8,128)(2,1)}, f32[8,128]{1,0:T(8,128)S(1)}) custom-call(s32[2]{0:T(128)S(1)} %pad_add_fusion.1.at_ref, bf16[32,16,2048]{2,1,0:T(8,128)(2,1)} %bitcast.77, bf16[2,4,16,1024]{3,2,1,0:T(8,128)(2,1)S(1)} %get-tuple-element.108.refs_1_.refs_5_.refs_0_, bf16[2,4,16,1024]{3,2,1,0:T(8,128)(2,1)S(1)} %collective-permute-done.47.refs_1_, ...), custom_call_target="tpu_custom_call" | custom-call | flops 1000 | bytes 1000 | tf_op jit(solution)/shard_map/close/pallas_call | solution.py:490
  155.3 3.4 %collective-permute-done.52.refs_1_.refs_4_ = bf16[2,4,16,1024]{3,2,1,0:T(8,128)(2,1)S(1)} collective-permute-done((bf16[2,4,16,1024]{3,2,1,0:T(8,128)(2,1)S(1)}, bf16[2,4,16,1024]{3,2,1,0:T(8,128)(2,1)S(1)}, u32[]{:S(2)}, u32[]{:S(2)}) %collective-permute-start.52) | collective-permute-done | bytes 262176 | tf_op jit(solution)/shard_map/ppermute | solution.py:525
  159.0 2.2 %close.4 = (bf16[8,16,2048]{2,1,0:T(8,128)(2,1)}, f32[8,128]{1,0:T(8,128)S(1)}) custom-call(s32[2]{0:T(128)S(1)} %pad_add_fusion.1.at_ref, bf16[32,16,2048]{2,1,0:T(8,128)(2,1)} %bitcast.78, bf16[2,4,16,1024]{3,2,1,0:T(8,128)(2,1)S(1)} %get-tuple-element.109.refs_5_.refs_0_, ...), custom_call_target="tpu_custom_call", output_to_operand_aliasing={{0}: (5, {})} | custom-call | flops 1000 | bytes 1000 | tf_op jit(solution)/shard_map/close/pallas_call | solution.py:490
  161.2 3.7 %collective-permute-done.50.refs_2_ = bf16[1,4,16,1024]{3,2,1,0:T(8,128)(2,1)S(1)} collective-permute-done((bf16[1,4,16,1024]{3,2,1,0:T(8,128)(2,1)S(1)}, bf16[1,4,16,1024]{3,2,1,0:T(8,128)(2,1)S(1)}, u32[]{:S(2)}, u32[]{:S(2)}) %collective-permute-start.50) | collective-permute-done | bytes 131104 | tf_op jit(solution)/shard_map/ppermute | solution.py:525
  164.9 2.4 %collective-permute-done.53.refs_5_ = bf16[1,4,16,1024]{3,2,1,0:T(8,128)(2,1)S(1)} collective-permute-done((bf16[1,4,16,1024]{3,2,1,0:T(8,128)(2,1)S(1)}, bf16[1,4,16,1024]{3,2,1,0:T(8,128)(2,1)S(1)}, u32[]{:S(2)}, u32[]{:S(2)}) %collective-permute-start.53) | collective-permute-done | bytes 131104 | tf_op jit(solution)/shard_map/ppermute | solution.py:525
  167.4 2.3 %close.5 = (bf16[8,16,2048]{2,1,0:T(8,128)(2,1)}, f32[8,128]{1,0:T(8,128)}) custom-call(s32[2]{0:T(128)S(1)} %pad_add_fusion.at_ref, bf16[32,16,2048]{2,1,0:T(8,128)(2,1)} %bitcast.79, bf16[2,4,16,1024]{3,2,1,0:T(8,128)(2,1)S(1)} %get-tuple-element.110.refs_2_.refs_0_, ...), custom_call_target="tpu_custom_call", output_to_operand_aliasing={{0}: (8, {})} | custom-call | flops 1000 | bytes 1000 | tf_op jit(solution)/shard_map/close/pallas_call | solution.py:490
  (135 shorter events, 20.9 us)
Async XLA Ops:
  5.5 9.4 %collective-permute-start = (bf16[1,4,128,256]{3,2,1,0:T(8,128)(2,1)S(1)}, bf16[1,4,128,256]{3,2,1,0:T(8,128)(2,1)S(1)}, u32[]{:S(2)}, u32[]{:S(2)}) collective-permute-start(bf16[1,4,128,256]{3,2,1,0:T(8,128)(2,1)S(1)} %get-tuple-element.66), channel_id=1, source_target_pairs={{0,1},{1,0},{2,3},{3,2},{4,5},{5,4},{6,7},{7,6},{8,9},{9,8},{10,11... | collective-permute-start | bytes 786440 | tf_op jit(solution)/shard_map/ppermute | solution.py:525
  6.1 8.8 %collective-permute-start.1 = (bf16[1,4,128,256]{3,2,1,0:T(8,128)(2,1)S(1)}, bf16[1,4,128,256]{3,2,1,0:T(8,128)(2,1)S(1)}, u32[]{:S(2)}, u32[]{:S(2)}) collective-permute-start(bf16[1,4,128,256]{3,2,1,0:T(8,128)(2,1)S(1)} %get-tuple-element.67), channel_id=1, source_target_pairs={{0,1},{1,0},{2,3},{3,2},{4,5},{5,4},{6,7},{7,6},{8,9},{9,8},{10,11... | collective-permute-start | bytes 786440 | tf_op jit(solution)/shard_map/ppermute | solution.py:525
  14.9 12.6 %collective-permute-start.3 = (bf16[1,4,128,512]{3,2,1,0:T(8,128)(2,1)S(1)}, bf16[1,4,128,512]{3,2,1,0:T(8,128)(2,1)S(1)}, u32[]{:S(2)}, u32[]{:S(2)}) collective-permute-start(bf16[1,4,128,512]{3,2,1,0:T(8,128)(2,1)S(1)} %tie.12), channel_id=1, source_target_pairs={{0,1},{1,0},{2,3},{3,2},{4,5},{5,4},{6,7},{7,6},{8,9},{9,8},{10,11... | collective-permute-start | bytes 1572872 | tf_op jit(solution)/shard_map/ppermute | solution.py:525
  15.4 12.1 %collective-permute-start.2 = (bf16[1,4,128,512]{3,2,1,0:T(8,128)(2,1)S(1)}, bf16[1,4,128,512]{3,2,1,0:T(8,128)(2,1)S(1)}, u32[]{:S(2)}, u32[]{:S(2)}) collective-permute-start(bf16[1,4,128,512]{3,2,1,0:T(8,128)(2,1)S(1)} %tie.11), channel_id=1, source_target_pairs={{0,1},{1,0},{2,3},{3,2},{4,5},{5,4},{6,7},{7,6},{8,9},{9,8},{10,11... | collective-permute-start | bytes 1572872 | tf_op jit(solution)/shard_map/ppermute | solution.py:525
  15.8 11.7 %collective-permute-start.4 = (bf16[1,4,128,256]{3,2,1,0:T(8,128)(2,1)S(1)}, bf16[1,4,128,256]{3,2,1,0:T(8,128)(2,1)S(1)}, u32[]{:S(2)}, u32[]{:S(2)}) collective-permute-start(bf16[1,4,128,256]{3,2,1,0:T(8,128)(2,1)S(1)} %fold.13.refs_8_), channel_id=1, source_target_pairs={{0,2},{1,3},{2,0},{3,1},{4,6},{5,7},{6,4},{7,5},{8,10},{9,11},{10,... | collective-permute-start | bytes 786440 | tf_op jit(solution)/shard_map/ppermute | solution.py:525
  27.5 9.8 %collective-permute-start.6 = (bf16[1,4,128,512]{3,2,1,0:T(8,128)(2,1)S(1)}, bf16[1,4,128,512]{3,2,1,0:T(8,128)(2,1)S(1)}, u32[]{:S(2)}, u32[]{:S(2)}) collective-permute-start(bf16[1,4,128,512]{3,2,1,0:T(8,128)(2,1)S(1)} %tie.14), channel_id=1, source_target_pairs={{0,1},{1,0},{2,3},{3,2},{4,5},{5,4},{6,7},{7,6},{8,9},{9,8},{10,11... | collective-permute-start | bytes 1572872 | tf_op jit(solution)/shard_map/ppermute | solution.py:525
  27.6 9.7 %collective-permute-start.5 = (bf16[1,4,128,512]{3,2,1,0:T(8,128)(2,1)S(1)}, bf16[1,4,128,512]{3,2,1,0:T(8,128)(2,1)S(1)}, u32[]{:S(2)}, u32[]{:S(2)}) collective-permute-start(bf16[1,4,128,512]{3,2,1,0:T(8,128)(2,1)S(1)} %tie.13), channel_id=1, source_target_pairs={{0,1},{1,0},{2,3},{3,2},{4,5},{5,4},{6,7},{7,6},{8,9},{9,8},{10,11... | collective-permute-start | bytes 1572872 | tf_op jit(solution)/shard_map/ppermute | solution.py:525
  28.4 14.0 %collective-permute-start.8 = (bf16[1,4,128,512]{3,2,1,0:T(8,128)(2,1)S(1)}, bf16[1,4,128,512]{3,2,1,0:T(8,128)(2,1)S(1)}, u32[]{:S(2)}, u32[]{:S(2)}) collective-permute-start(bf16[1,4,128,512]{3,2,1,0:T(8,128)(2,1)S(1)} %fold.14.refs_8_), channel_id=1, source_target_pairs={{0,2},{1,3},{2,0},{3,1},{4,6},{5,7},{6,4},{7,5},{8,10},{9,11},{10,... | collective-permute-start | bytes 1572872 | tf_op jit(solution)/shard_map/ppermute | solution.py:525
  37.3 5.9 %collective-permute-start.7 = (bf16[1,4,128,512]{3,2,1,0:T(8,128)(2,1)S(1)}, bf16[1,4,128,512]{3,2,1,0:T(8,128)(2,1)S(1)}, u32[]{:S(2)}, u32[]{:S(2)}) collective-permute-start(bf16[1,4,128,512]{3,2,1,0:T(8,128)(2,1)S(1)} %tie.15), channel_id=1, source_target_pairs={{0,1},{1,0},{2,3},{3,2},{4,5},{5,4},{6,7},{7,6},{8,9},{9,8},{10,11... | collective-permute-start | bytes 1572872 | tf_op jit(solution)/shard_map/ppermute | solution.py:525
  38.1 14.7 %collective-permute-start.9 = (bf16[1,4,128,512]{3,2,1,0:T(8,128)(2,1)S(1)}, bf16[1,4,128,512]{3,2,1,0:T(8,128)(2,1)S(1)}, u32[]{:S(2)}, u32[]{:S(2)}) collective-permute-start(bf16[1,4,128,512]{3,2,1,0:T(8,128)(2,1)S(1)} %tie.16), channel_id=1, source_target_pairs={{0,1},{1,0},{2,3},{3,2},{4,5},{5,4},{6,7},{7,6},{8,9},{9,8},{10,11... | collective-permute-start | bytes 1572872 | tf_op jit(solution)/shard_map/ppermute | solution.py:525
  39.1 19.4 %collective-permute-start.12 = (bf16[1,4,128,512]{3,2,1,0:T(8,128)(2,1)}, bf16[1,4,128,512]{3,2,1,0:T(8,128)(2,1)}, u32[]{:S(2)}, u32[]{:S(2)}) collective-permute-start(bf16[1,4,128,512]{3,2,1,0:T(8,128)(2,1)} %fold.15.refs_6_), channel_id=1, source_target_pairs={{0,2},{1,3},{2,0},{3,1},{4,6},{5,7},{6,4},{7,5},{8,10},{9,11},{10,... | collective-permute-start | bytes 1572872 | tf_op jit(solution)/shard_map/ppermute | solution.py:525
  42.9 15.5 %collective-permute-start.18 = (bf16[128,768]{1,0:T(8,128)(2,1)S(1)}, bf16[128,768]{1,0:T(8,128)(2,1)S(1)}, u32[]{:S(2)}, u32[]{:S(2)}) collective-permute-start(bf16[128,768]{1,0:T(8,128)(2,1)S(1)} %get-tuple-element.74.refs_2_.refs_0_.q_ref), channel_id=1, source_target_pairs={{0,2},{1,3},{2,0},{3,1},{4,6},{5,7},{6,4},{7,5},{8,10},{9,11},{10,... | collective-permute-start | bytes 589832 | tf_op jit(solution)/shard_map/ppermute | solution.py:525
  44.2 29.3 %collective-permute-start.17 = (bf16[1,4,128,512]{3,2,1,0:T(8,128)(2,1)}, bf16[1,4,128,512]{3,2,1,0:T(8,128)(2,1)}, u32[]{:S(2)}, u32[]{:S(2)}) collective-permute-start(bf16[1,4,128,512]{3,2,1,0:T(8,128)(2,1)} %fold.16.refs_8_), channel_id=1, source_target_pairs={{0,2},{1,3},{2,0},{3,1},{4,6},{5,7},{6,4},{7,5},{8,10},{9,11},{10,... | collective-permute-start | bytes 1572872 | tf_op jit(solution)/shard_map/ppermute | solution.py:525
  52.8 8.1 %collective-permute-start.11 = (bf16[1,4,128,256]{3,2,1,0:T(8,128)(2,1)}, bf16[1,4,128,256]{3,2,1,0:T(8,128)(2,1)}, u32[]{:S(2)}, u32[]{:S(2)}) collective-permute-start(bf16[1,4,128,256]{3,2,1,0:T(8,128)(2,1)} %tie.18), channel_id=1, source_target_pairs={{0,1},{1,0},{2,3},{3,2},{4,5},{5,4},{6,7},{7,6},{8,9},{9,8},{10,11... | collective-permute-start | bytes 786440 | tf_op jit(solution)/shard_map/ppermute | solution.py:525
  52.8 9.2 %collective-permute-start.19 = (bf16[128,768]{1,0:T(8,128)(2,1)S(1)}, bf16[128,768]{1,0:T(8,128)(2,1)}, u32[]{:S(2)}, u32[]{:S(2)}) collective-permute-start(bf16[128,768]{1,0:T(8,128)(2,1)S(1)} %get-tuple-element.74.refs_2_.refs_0_.q_ref), channel_id=1, source_target_pairs={{0,1},{1,0},{2,3},{3,2},{4,5},{5,4},{6,7},{7,6},{8,9},{9,8},{10,11... | collective-permute-start | bytes 589832 | tf_op jit(solution)/shard_map/ppermute | solution.py:525
  58.4 3.7 %collective-permute-start.20 = (bf16[128,768]{1,0:T(8,128)(2,1)S(1)}, bf16[128,768]{1,0:T(8,128)(2,1)}, u32[]{:S(2)}, u32[]{:S(2)}) collective-permute-start(bf16[128,768]{1,0:T(8,128)(2,1)S(1)} %collective-permute-done.18.refs_1_), channel_id=1, source_target_pairs={{0,1},{1,0},{2,3},{3,2},{4,5},{5,4},{6,7},{7,6},{8,9},{9,8},{10,11... | collective-permute-start | bytes 589832 | tf_op jit(solution)/shard_map/ppermute | solution.py:525
  66.2 6.7 %collective-permute-start.21 = (bf16[1,128,768]{2,1,0:T(8,128)(2,1)S(1)}, bf16[1,128,768]{2,1,0:T(8,128)(2,1)S(1)}, u32[]{:S(2)}, u32[]{:S(2)}) collective-permute-start(bf16[1,128,768]{2,1,0:T(8,128)(2,1)S(1)} %get-tuple-element.81), channel_id=1, source_target_pairs={{0,1},{1,0},{2,3},{3,2},{4,5},{5,4},{6,7},{7,6},{8,9},{9,8},{10,11... | collective-permute-start | bytes 589832 | tf_op jit(solution)/shard_map/ppermute | solution.py:525
  66.7 6.1 %collective-permute-start.14 = (bf16[128,512]{1,0:T(8,128)(2,1)S(1)}, bf16[128,512]{1,0:T(8,128)(2,1)S(1)}, u32[]{:S(2)}, u32[]{:S(2)}) collective-permute-start(bf16[128,512]{1,0:T(8,128)(2,1)S(1)} %get-tuple-element.79.refs_2_.refs_0_.q_ref), channel_id=1, source_target_pairs={{0,2},{1,3},{2,0},{3,1},{4,6},{5,7},{6,4},{7,5},{8,10},{9,11},{10,... | collective-permute-start | bytes 393224 | tf_op jit(solution)/shard_map/ppermute | solution.py:525
  68.5 12.3 %collective-permute-start.10 = (bf16[1,4,128,256]{3,2,1,0:T(8,128)(2,1)S(1)}, bf16[1,4,128,256]{3,2,1,0:T(8,128)(2,1)S(1)}, u32[]{:S(2)}, u32[]{:S(2)}) collective-permute-start(bf16[1,4,128,256]{3,2,1,0:T(8,128)(2,1)S(1)} %tie.17), channel_id=1, source_target_pairs={{0,1},{1,0},{2,3},{3,2},{4,5},{5,4},{6,7},{7,6},{8,9},{9,8},{10,11... | collective-permute-start | bytes 786440 | tf_op jit(solution)/shard_map/ppermute | solution.py:525
  68.5 12.7 %collective-permute-start.13 = (bf16[1,4,128,256]{3,2,1,0:T(8,128)(2,1)S(1)}, bf16[1,4,128,256]{3,2,1,0:T(8,128)(2,1)S(1)}, u32[]{:S(2)}, u32[]{:S(2)}) collective-permute-start(bf16[1,4,128,256]{3,2,1,0:T(8,128)(2,1)S(1)} %fold.17.refs_10_), channel_id=1, source_target_pairs={{0,2},{1,3},{2,0},{3,1},{4,6},{5,7},{6,4},{7,5},{8,10},{9,11},{10,... | collective-permute-start | bytes 786440 | tf_op jit(solution)/shard_map/ppermute | solution.py:525
  72.8 4.2 %collective-permute-start.15 = (bf16[128,512]{1,0:T(8,128)(2,1)S(1)}, bf16[128,512]{1,0:T(8,128)(2,1)S(1)}, u32[]{:S(2)}, u32[]{:S(2)}) collective-permute-start(bf16[128,512]{1,0:T(8,128)(2,1)S(1)} %get-tuple-element.79.refs_2_.refs_0_.q_ref), channel_id=1, source_target_pairs={{0,1},{1,0},{2,3},{3,2},{4,5},{5,4},{6,7},{7,6},{8,9},{9,8},{10,11... | collective-permute-start | bytes 393224 | tf_op jit(solution)/shard_map/ppermute | solution.py:525
  72.9 4.2 %collective-permute-start.16 = (bf16[128,512]{1,0:T(8,128)(2,1)S(1)}, bf16[128,512]{1,0:T(8,128)(2,1)S(1)}, u32[]{:S(2)}, u32[]{:S(2)}) collective-permute-start(bf16[128,512]{1,0:T(8,128)(2,1)S(1)} %collective-permute-done.14.refs_1_), channel_id=1, source_target_pairs={{0,1},{1,0},{2,3},{3,2},{4,5},{5,4},{6,7},{7,6},{8,9},{9,8},{10,11... | collective-permute-start | bytes 393224 | tf_op jit(solution)/shard_map/ppermute | solution.py:525
  74.9 5.8 %collective-permute-start.25 = (bf16[128,512]{1,0:T(8,128)(2,1)S(1)}, bf16[128,512]{1,0:T(8,128)(2,1)S(1)}, u32[]{:S(2)}, u32[]{:S(2)}) collective-permute-start(bf16[128,512]{1,0:T(8,128)(2,1)S(1)} %get-tuple-element.82.refs_10_.refs_0_.q_ref), channel_id=1, source_target_pairs={{0,2},{1,3},{2,0},{3,1},{4,6},{5,7},{6,4},{7,5},{8,10},{9,11},{10,... | collective-permute-start | bytes 393224 | tf_op jit(solution)/shard_map/ppermute | solution.py:525
  80.8 10.3 %collective-permute-start.30 = (bf16[1,128,768]{2,1,0:T(8,128)(2,1)S(1)}, bf16[1,128,768]{2,1,0:T(8,128)(2,1)S(1)}, u32[]{:S(2)}, u32[]{:S(2)}) collective-permute-start(bf16[1,128,768]{2,1,0:T(8,128)(2,1)S(1)} %get-tuple-element.90), channel_id=1, source_target_pairs={{0,1},{1,0},{2,3},{3,2},{4,5},{5,4},{6,7},{7,6},{8,9},{9,8},{10,11... | collective-permute-start | bytes 589832 | tf_op jit(solution)/shard_map/ppermute | solution.py:525
  81.3 10.4 %collective-permute-start.31 = (bf16[1,128,768]{2,1,0:T(8,128)(2,1)S(1)}, bf16[1,128,768]{2,1,0:T(8,128)(2,1)S(1)}, u32[]{:S(2)}, u32[]{:S(2)}) collective-permute-start(bf16[1,128,768]{2,1,0:T(8,128)(2,1)S(1)} %fold.18.refs_3_), channel_id=1, source_target_pairs={{0,2},{1,3},{2,0},{3,1},{4,6},{5,7},{6,4},{7,5},{8,10},{9,11},{10,... | collective-permute-start | bytes 589832 | tf_op jit(solution)/shard_map/ppermute | solution.py:525
  86.5 6.0 %collective-permute-start.29 = (bf16[1,128,512]{2,1,0:T(8,128)(2,1)S(1)}, bf16[1,128,512]{2,1,0:T(8,128)(2,1)S(1)}, u32[]{:S(2)}, u32[]{:S(2)}) collective-permute-start(bf16[1,128,512]{2,1,0:T(8,128)(2,1)S(1)} %get-tuple-element.88), channel_id=1, source_target_pairs={{0,1},{1,0},{2,3},{3,2},{4,5},{5,4},{6,7},{7,6},{8,9},{9,8},{10,11... | collective-permute-start | bytes 393224 | tf_op jit(solution)/shard_map/ppermute | solution.py:525
  86.6 4.5 %collective-permute-start.22 = (bf16[128,256]{1,0:T(8,128)(2,1)S(1)}, bf16[128,256]{1,0:T(8,128)(2,1)S(1)}, u32[]{:S(2)}, u32[]{:S(2)}) collective-permute-start(bf16[128,256]{1,0:T(8,128)(2,1)S(1)} %get-tuple-element.84.refs_2_.refs_0_.q_ref), channel_id=1, source_target_pairs={{0,2},{1,3},{2,0},{3,1},{4,6},{5,7},{6,4},{7,5},{8,10},{9,11},{10,... | collective-permute-start | bytes 196616 | tf_op jit(solution)/shard_map/ppermute | solution.py:525
  87.1 5.6 %collective-permute-start.23 = (bf16[128,256]{1,0:T(8,128)(2,1)S(1)}, bf16[128,256]{1,0:T(8,128)(2,1)S(1)}, u32[]{:S(2)}, u32[]{:S(2)}) collective-permute-start(bf16[128,256]{1,0:T(8,128)(2,1)S(1)} %get-tuple-element.84.refs_2_.refs_0_.q_ref), channel_id=1, source_target_pairs={{0,1},{1,0},{2,3},{3,2},{4,5},{5,4},{6,7},{7,6},{8,9},{9,8},{10,11... | collective-permute-start | bytes 196616 | tf_op jit(solution)/shard_map/ppermute | solution.py:525
  91.1 6.2 %collective-permute-start.35 = (bf16[1,128,512]{2,1,0:T(8,128)(2,1)S(1)}, bf16[1,128,512]{2,1,0:T(8,128)(2,1)S(1)}, u32[]{:S(2)}, u32[]{:S(2)}) collective-permute-start(bf16[1,128,512]{2,1,0:T(8,128)(2,1)S(1)} %get-tuple-element.97), channel_id=1, source_target_pairs={{0,1},{1,0},{2,3},{3,2},{4,5},{5,4},{6,7},{7,6},{8,9},{9,8},{10,11... | collective-permute-start | bytes 393224 | tf_op jit(solution)/shard_map/ppermute | solution.py:525
  91.7 6.7 %collective-permute-start.36 = (bf16[1,128,512]{2,1,0:T(8,128)(2,1)S(1)}, bf16[1,128,512]{2,1,0:T(8,128)(2,1)S(1)}, u32[]{:S(2)}, u32[]{:S(2)}) collective-permute-start(bf16[1,128,512]{2,1,0:T(8,128)(2,1)S(1)} %fold.19.refs_10_), channel_id=1, source_target_pairs={{0,2},{1,3},{2,0},{3,1},{4,6},{5,7},{6,4},{7,5},{8,10},{9,11},{10,... | collective-permute-start | bytes 393224 | tf_op jit(solution)/shard_map/ppermute | solution.py:525
  94.8 3.9 %collective-permute-start.37 = (bf16[1,128,512]{2,1,0:T(8,128)(2,1)S(1)}, bf16[1,128,512]{2,1,0:T(8,128)(2,1)S(1)}, u32[]{:S(2)}, u32[]{:S(2)}) collective-permute-start(bf16[1,128,512]{2,1,0:T(8,128)(2,1)S(1)} %get-tuple-element.100), channel_id=1, source_target_pairs={{0,1},{1,0},{2,3},{3,2},{4,5},{5,4},{6,7},{7,6},{8,9},{9,8},{10,11... | collective-permute-start | bytes 393224 | tf_op jit(solution)/shard_map/ppermute | solution.py:525
  95.3 5.7 %collective-permute-start.38 = (bf16[1,128,512]{2,1,0:T(8,128)(2,1)S(1)}, bf16[1,128,512]{2,1,0:T(8,128)(2,1)S(1)}, u32[]{:S(2)}, u32[]{:S(2)}) collective-permute-start(bf16[1,128,512]{2,1,0:T(8,128)(2,1)S(1)} %fold.20.refs_10_), channel_id=1, source_target_pairs={{0,2},{1,3},{2,0},{3,1},{4,6},{5,7},{6,4},{7,5},{8,10},{9,11},{10,... | collective-permute-start | bytes 393224 | tf_op jit(solution)/shard_map/ppermute | solution.py:525
  97.0 4.5 %collective-permute-start.32 = (bf16[1,128,256]{2,1,0:T(8,128)(2,1)S(1)}, bf16[1,128,256]{2,1,0:T(8,128)(2,1)S(1)}, u32[]{:S(2)}, u32[]{:S(2)}) collective-permute-start(bf16[1,128,256]{2,1,0:T(8,128)(2,1)S(1)} %get-tuple-element.93), channel_id=1, source_target_pairs={{0,1},{1,0},{2,3},{3,2},{4,5},{5,4},{6,7},{7,6},{8,9},{9,8},{10,11... | collective-permute-start | bytes 196616 | tf_op jit(solution)/shard_map/ppermute | solution.py:525
  97.4 4.9 %collective-permute-start.34 = (bf16[1,128,256]{2,1,0:T(8,128)(2,1)S(1)}, bf16[1,128,256]{2,1,0:T(8,128)(2,1)S(1)}, u32[]{:S(2)}, u32[]{:S(2)}) collective-permute-start(bf16[1,128,256]{2,1,0:T(8,128)(2,1)S(1)} %fold.21.refs_3_), channel_id=1, source_target_pairs={{0,2},{1,3},{2,0},{3,1},{4,6},{5,7},{6,4},{7,5},{8,10},{9,11},{10,... | collective-permute-start | bytes 196616 | tf_op jit(solution)/shard_map/ppermute | solution.py:525
  106.4 4.5 %collective-permute-start.40 = (f32[8,128]{1,0:T(8,128)S(1)}, f32[8,128]{1,0:T(8,128)S(1)}, u32[]{:S(2)}, u32[]{:S(2)}) collective-permute-start(f32[8,128]{1,0:T(8,128)S(1)} %merge.1.refs_0_), channel_id=1, source_target_pairs={{0,8},{4,12},{8,0},{12,4},{1,9},{5,13},{9,1},{13,5},{2,10},{6,14},... | collective-permute-start | bytes 12296 | tf_op jit(solution)/shard_map/ppermute | solution.py:525
  111.3 8.8 %collective-permute-start.42 = (bf16[64,2048]{1,0:T(8,128)(2,1)S(1)}, bf16[64,2048]{1,0:T(8,128)(2,1)S(1)}, u32[]{:S(2)}, u32[]{:S(2)}) collective-permute-start(bf16[64,2048]{1,0:T(8,128)(2,1)S(1)} %get-tuple-element.107), channel_id=1, source_target_pairs={{0,2},{1,3},{2,0},{3,1},{4,6},{5,7},{6,4},{7,5},{8,10},{9,11},{10,... | collective-permute-start | bytes 786440 | tf_op jit(solution)/shard_map/ppermute | solution.py:525
  113.0 12.1 %collective-permute-start.41 = (bf16[64,2176]{1,0:T(8,128)(2,1)S(1)}, bf16[64,2176]{1,0:T(8,128)(2,1)S(1)}, u32[]{:S(2)}, u32[]{:S(2)}) collective-permute-start(bf16[64,2176]{1,0:T(8,128)(2,1)S(1)} %get-tuple-element.106), channel_id=1, source_target_pairs={{0,2},{1,3},{2,0},{3,1},{4,6},{5,7},{6,4},{7,5},{8,10},{9,11},{10,... | collective-permute-start | bytes 835592 | tf_op jit(solution)/shard_map/ppermute | solution.py:525
  113.4 7.3 %collective-permute-start.43 = (bf16[64,2048]{1,0:T(8,128)(2,1)S(1)}, bf16[64,2048]{1,0:T(8,128)(2,1)S(1)}, u32[]{:S(2)}, u32[]{:S(2)}) collective-permute-start(bf16[64,2048]{1,0:T(8,128)(2,1)S(1)} %get-tuple-element.107), channel_id=1, source_target_pairs={{0,1},{1,0},{2,3},{3,2},{4,5},{5,4},{6,7},{7,6},{8,9},{9,8},{10,11... | collective-permute-start | bytes 786440 | tf_op jit(solution)/shard_map/ppermute | solution.py:525
  120.1 10.7 %collective-permute-start.45 = (bf16[64,2176]{1,0:T(8,128)(2,1)S(1)}, bf16[64,2176]{1,0:T(8,128)(2,1)S(1)}, u32[]{:S(2)}, u32[]{:S(2)}) collective-permute-start(bf16[64,2176]{1,0:T(8,128)(2,1)S(1)} %get-tuple-element.106), channel_id=1, source_target_pairs={{0,1},{1,0},{2,3},{3,2},{4,5},{5,4},{6,7},{7,6},{8,9},{9,8},{10,11... | collective-permute-start | bytes 835592 | tf_op jit(solution)/shard_map/ppermute | solution.py:525
  125.1 5.8 %collective-permute-start.46 = (bf16[64,2176]{1,0:T(8,128)(2,1)S(1)}, bf16[64,2176]{1,0:T(8,128)(2,1)S(1)}, u32[]{:S(2)}, u32[]{:S(2)}) collective-permute-start(bf16[64,2176]{1,0:T(8,128)(2,1)S(1)} %tie.19), channel_id=1, source_target_pairs={{0,1},{1,0},{2,3},{3,2},{4,5},{5,4},{6,7},{7,6},{8,9},{9,8},{10,11... | collective-permute-start | bytes 835592 | tf_op jit(solution)/shard_map/ppermute | solution.py:525
  125.3 9.1 %collective-permute-start.47 = (bf16[2,4,16,1024]{3,2,1,0:T(8,128)(2,1)S(1)}, bf16[2,4,16,1024]{3,2,1,0:T(8,128)(2,1)S(1)}, u32[]{:S(2)}, u32[]{:S(2)}) collective-permute-start(bf16[2,4,16,1024]{3,2,1,0:T(8,128)(2,1)S(1)} %get-tuple-element.112), channel_id=1, source_target_pairs={{0,4},{4,0},{8,12},{12,8},{1,5},{5,1},{9,13},{13,9},{2,6},{6,2},{1... | collective-permute-start | bytes 786440 | tf_op jit(solution)/shard_map/ppermute | solution.py:525
  130.3 12.5 %collective-permute-start.49 = (bf16[2,4,16,1024]{3,2,1,0:T(8,128)(2,1)S(1)}, bf16[2,4,16,1024]{3,2,1,0:T(8,128)(2,1)S(1)}, u32[]{:S(2)}, u32[]{:S(2)}) collective-permute-start(bf16[2,4,16,1024]{3,2,1,0:T(8,128)(2,1)S(1)} %get-tuple-element.113), channel_id=1, source_target_pairs={{0,4},{4,0},{8,12},{12,8},{1,5},{5,1},{9,13},{13,9},{2,6},{6,2},{1... | collective-permute-start | bytes 786440 | tf_op jit(solution)/shard_map/ppermute | solution.py:525
  134.6 8.3 %collective-permute-start.51 = (bf16[1,4,16,1024]{3,2,1,0:T(8,128)(2,1)S(1)}, bf16[1,4,16,1024]{3,2,1,0:T(8,128)(2,1)S(1)}, u32[]{:S(2)}, u32[]{:S(2)}) collective-permute-start(bf16[1,4,16,1024]{3,2,1,0:T(8,128)(2,1)S(1)} %fold.22.refs_5_), channel_id=1, source_target_pairs={{0,8},{4,12},{8,0},{12,4},{1,9},{5,13},{9,1},{13,5},{2,10},{6,14},... | collective-permute-start | bytes 393224 | tf_op jit(solution)/shard_map/ppermute | solution.py:525
  137.2 12.7 %collective-permute-start.48 = (bf16[2,4,16,1024]{3,2,1,0:T(8,128)(2,1)S(1)}, bf16[2,4,16,1024]{3,2,1,0:T(8,128)(2,1)S(1)}, u32[]{:S(2)}, u32[]{:S(2)}) collective-permute-start(bf16[2,4,16,1024]{3,2,1,0:T(8,128)(2,1)S(1)} %tie.20), channel_id=1, source_target_pairs={{0,4},{4,0},{8,12},{12,8},{1,5},{5,1},{9,13},{13,9},{2,6},{6,2},{1... | collective-permute-start | bytes 786440 | tf_op jit(solution)/shard_map/ppermute | solution.py:525
  142.9 15.8 %collective-permute-start.52 = (bf16[2,4,16,1024]{3,2,1,0:T(8,128)(2,1)S(1)}, bf16[2,4,16,1024]{3,2,1,0:T(8,128)(2,1)S(1)}, u32[]{:S(2)}, u32[]{:S(2)}) collective-permute-start(bf16[2,4,16,1024]{3,2,1,0:T(8,128)(2,1)S(1)} %tie.21), channel_id=1, source_target_pairs={{0,4},{4,0},{8,12},{12,8},{1,5},{5,1},{9,13},{13,9},{2,6},{6,2},{1... | collective-permute-start | bytes 786440 | tf_op jit(solution)/shard_map/ppermute | solution.py:525
  145.7 13.4 %collective-permute-start.54 = (bf16[1,4,16,1024]{3,2,1,0:T(8,128)(2,1)S(1)}, bf16[1,4,16,1024]{3,2,1,0:T(8,128)(2,1)S(1)}, u32[]{:S(2)}, u32[]{:S(2)}) collective-permute-start(bf16[1,4,16,1024]{3,2,1,0:T(8,128)(2,1)S(1)} %fold.23.refs_2_), channel_id=1, source_target_pairs={{0,8},{4,12},{8,0},{12,4},{1,9},{5,13},{9,1},{13,5},{2,10},{6,14},... | collective-permute-start | bytes 393224 | tf_op jit(solution)/shard_map/ppermute | solution.py:525
  150.0 14.9 %collective-permute-start.50 = (bf16[1,4,16,1024]{3,2,1,0:T(8,128)(2,1)S(1)}, bf16[1,4,16,1024]{3,2,1,0:T(8,128)(2,1)S(1)}, u32[]{:S(2)}, u32[]{:S(2)}) collective-permute-start(bf16[1,4,16,1024]{3,2,1,0:T(8,128)(2,1)S(1)} %fold.24.refs_3_), channel_id=1, source_target_pairs={{0,8},{4,12},{8,0},{12,4},{1,9},{5,13},{9,1},{13,5},{2,10},{6,14},... | collective-permute-start | bytes 393224 | tf_op jit(solution)/shard_map/ppermute | solution.py:525
  158.9 8.5 %collective-permute-start.53 = (bf16[1,4,16,1024]{3,2,1,0:T(8,128)(2,1)S(1)}, bf16[1,4,16,1024]{3,2,1,0:T(8,128)(2,1)S(1)}, u32[]{:S(2)}, u32[]{:S(2)}) collective-permute-start(bf16[1,4,16,1024]{3,2,1,0:T(8,128)(2,1)S(1)} %fold.25.refs_4_), channel_id=1, source_target_pairs={{0,8},{4,12},{8,0},{12,4},{1,9},{5,13},{9,1},{13,5},{2,10},{6,14},... | collective-permute-start | bytes 393224 | tf_op jit(solution)/shard_map/ppermute | solution.py:525
  (17 other events, 88.9 us)

commit v17 on v16

--- a/solution.py
+++ b/solution.py
@@ -9,7 +9,7 @@
 
 DH = 128
 EPSILON = 1e-05
-VMEM_LIMIT = 28 * 1024 * 1024
+VMEM_LIMIT = 20 * 1024 * 1024
 
 bf16 = jnp.bfloat16
 f32 = jnp.float32

time: 170 us -> 170 us (level)
  no operation moved by 1% of the time
where the time goes in v17:
time: 170 us
  Pallas kernels  81.5 us (48%)
  starting transfers between devices  44.1 us (26%)
  waiting for transfers between devices  40.9 us (24%)
  local copies, waits for them, and re-layouts  2.4 us (1%)
    ppermute x55, starting transfers between devices, swap(): lax.ppermute(x, axis, [(i, i ^ 1 << bit) for i in range(lax.axis_size(axi...  44.1 us
    ppermute x55, waiting for transfers between devices, swap(): lax.ppermute(x, axis, [(i, i ^ 1 << bit) for i in range(lax.axis_size(axi...  40.9 us
    pallas_call x5, Pallas kernels, project(): pl.pallas_call(functools.partial(project_kernel, parts, owners, len(after...  37.9 us
    pallas_call x4, Pallas kernels, output(): pl.pallas_call(functools.partial(output_kernel, owners, slots, len(after)...  13.9 us
    pallas_call x4, Pallas kernels, attend(): pl.pallas_call(functools.partial(attend_kernel, owners, len(counts)), gri...  12.5 us
    pallas_call x3, Pallas kernels, close(): pl.pallas_call(functools.partial(close_kernel, [len(terms) for terms in g...  6.66 us
    pallas_call x13, Pallas kernels, fold(): pl.pallas_call(functools.partial(fold_kernel, len(terms)), grid=(steps,),...  4.76 us
    pallas_call x4, Pallas kernels, activate(): pl.pallas_call(functools.partial(activate_kernel, [len(terms) for terms i...  3.41 us
  transfers between devices with their start and end apart: 55, of which 16 were waited for; matrix products, arithmetic and copies ran while one was open for 0% of the time, Pallas kernels for 43%

profile of v17, /device:TPU:0, one launch (start us, length us, event | category | flops | bytes accessed | tf_op | source)
XLA Modules:
  0.0 169.7 jit_solution(3875543815313092943)
XLA Ops:
  0.0 5.5 %project.5 = (bf16[2,4,128,256]{3,2,1,0:T(8,128)(2,1)S(1)}, bf16[1,4,128,256]{3,2,1,0:T(8,128)(2,1)S(1)}, bf16[1,4,128,256]{3,2,1,0:T(8,128)(2,1)S(1)}) custom-call(s32[1]{0:T(128)} %bitcast.at_ref, bf16[4,2,4,16,2048]{4,3,2,1,0:T(8,128)(2,1)} %bitcast.57, bf16[4,2,4,16,2048]{4,3,2,1,0:T(8,128)(2,1)} %bitcast.58, bf16[4,2,4,16,2048]{4,3,2,1,0:T(8,128)(2,1)} %bitcast.59, ...), custom_call_target="tpu_custom_call" | custom-call | flops 1000 | bytes 1000 | tf_op jit(solution)/shard_map/project/pallas_call | solution.py:80
  6.1 8.7 %project.6 = (bf16[2,4,128,512]{3,2,1,0:T(8,128)(2,1)S(1)}, bf16[1,4,128,512]{3,2,1,0:T(8,128)(2,1)S(1)}, bf16[1,4,128,512]{3,2,1,0:T(8,128)(2,1)S(1)}) custom-call(s32[1]{0:T(128)} %bitcast.at_ref, bf16[4,2,4,16,2048]{4,3,2,1,0:T(8,128)(2,1)} %bitcast.61, bf16[4,2,4,16,2048]{4,3,2,1,0:T(8,128)(2,1)} %bitcast.62, bf16[4,2,4,16,2048]{4,3,2,1,0:T(8,128)(2,1)} %bitcast.63, ...), custom_call_target="tpu_custom_call" | custom-call | flops 1000 | bytes 1000 | tf_op jit(solution)/shard_map/project/pallas_call | solution.py:80
  15.8 3.0 %collective-permute-start.4 = (bf16[1,4,128,256]{3,2,1,0:T(8,128)(2,1)S(1)}, bf16[1,4,128,256]{3,2,1,0:T(8,128)(2,1)S(1)}, u32[]{:S(2)}, u32[]{:S(2)}) collective-permute-start(bf16[1,4,128,256]{3,2,1,0:T(8,128)(2,1)S(1)} %fold.13.refs_8_), channel_id=1, source_target_pairs={{0,2},{1,3},{2,0},{3,1},{4,6},{5,7},{6,4},{7,5},{8,10},{9,11},{10,... | collective-permute-start | bytes 786440 | tf_op jit(solution)/shard_map/ppermute | solution.py:525
  18.7 8.7 %project.7 = (bf16[2,4,128,512]{3,2,1,0:T(8,128)(2,1)S(1)}, bf16[1,4,128,512]{3,2,1,0:T(8,128)(2,1)S(1)}, bf16[1,4,128,512]{3,2,1,0:T(8,128)(2,1)S(1)}) custom-call(s32[1]{0:T(128)} %bitcast.at_ref, bf16[4,2,4,16,2048]{4,3,2,1,0:T(8,128)(2,1)} %bitcast.68, bf16[4,2,4,16,2048]{4,3,2,1,0:T(8,128)(2,1)} %bitcast.66, bf16[4,2,4,16,2048]{4,3,2,1,0:T(8,128)(2,1)} %bitcast.67, ...), custom_call_target="tpu_custom_call" | custom-call | flops 1000 | bytes 1000 | tf_op jit(solution)/shard_map/project/pallas_call | solution.py:80
  28.5 8.8 %project.8 = (bf16[2,4,128,512]{3,2,1,0:T(8,128)(2,1)S(1)}, bf16[1,4,128,512]{3,2,1,0:T(8,128)(2,1)S(1)}, bf16[1,4,128,512]{3,2,1,0:T(8,128)(2,1)S(1)}) custom-call(s32[1]{0:T(128)} %bitcast.at_ref, bf16[4,2,4,16,2048]{4,3,2,1,0:T(8,128)(2,1)} %bitcast.69, bf16[4,2,4,16,2048]{4,3,2,1,0:T(8,128)(2,1)} %bitcast.70, bf16[4,2,4,16,2048]{4,3,2,1,0:T(8,128)(2,1)} %bitcast.71, ...), custom_call_target="tpu_custom_call" | custom-call | flops 1000 | bytes 1000 | tf_op jit(solution)/shard_map/project/pallas_call | solution.py:80
  39.1 1.9 %collective-permute-start.12 = (bf16[1,4,128,512]{3,2,1,0:T(8,128)(2,1)}, bf16[1,4,128,512]{3,2,1,0:T(8,128)(2,1)}, u32[]{:S(2)}, u32[]{:S(2)}) collective-permute-start(bf16[1,4,128,512]{3,2,1,0:T(8,128)(2,1)} %fold.15.refs_6_), channel_id=1, source_target_pairs={{0,2},{1,3},{2,0},{3,1},{4,6},{5,7},{6,4},{7,5},{8,10},{9,11},{10,... | collective-permute-start | bytes 1572872 | tf_op jit(solution)/shard_map/ppermute | solution.py:525
  41.0 1.4 collective-permute-done.8.refs_5_
  44.2 1.7 %collective-permute-start.17 = (bf16[1,4,128,512]{3,2,1,0:T(8,128)(2,1)}, bf16[1,4,128,512]{3,2,1,0:T(8,128)(2,1)}, u32[]{:S(2)}, u32[]{:S(2)}) collective-permute-start(bf16[1,4,128,512]{3,2,1,0:T(8,128)(2,1)} %fold.16.refs_8_), channel_id=1, source_target_pairs={{0,2},{1,3},{2,0},{3,1},{4,6},{5,7},{6,4},{7,5},{8,10},{9,11},{10,... | collective-permute-start | bytes 1572872 | tf_op jit(solution)/shard_map/ppermute | solution.py:525
  45.9 6.1 %project.9 = (bf16[2,4,128,256]{3,2,1,0:T(8,128)(2,1)S(1)}, bf16[1,4,128,256]{3,2,1,0:T(8,128)(2,1)S(1)}, bf16[1,4,128,256]{3,2,1,0:T(8,128)(2,1)}) custom-call(s32[1]{0:T(128)} %bitcast.at_ref, bf16[4,2,4,16,2048]{4,3,2,1,0:T(8,128)(2,1)} %bitcast.73, bf16[4,2,4,16,2048]{4,3,2,1,0:T(8,128)(2,1)} %bitcast.74, bf16[4,2,4,16,2048]{4,3,2,1,0:T(8,128)(2,1)} %bitcast.75, ...), custom_call_target="tpu_custom_call" | custom-call | flops 1000 | bytes 1000 | tf_op jit(solution)/shard_map/project/pallas_call | solution.py:80
  53.3 5.0 %collective-permute-done.18.refs_1_ = bf16[128,768]{1,0:T(8,128)(2,1)S(1)} collective-permute-done((bf16[128,768]{1,0:T(8,128)(2,1)S(1)}, bf16[128,768]{1,0:T(8,128)(2,1)S(1)}, u32[]{:S(2)}, u32[]{:S(2)}) %collective-permute-start.18) | collective-permute-done | bytes 196640 | tf_op jit(solution)/shard_map/ppermute | solution.py:525
  58.5 1.0 copy-done.3
  59.6 1.4 activate.5
  60.9 1.1 fold.17.refs_10_
  62.1 4.1 %attend.4 = (bf16[2,128,768]{2,1,0:T(8,128)(2,1)S(1)}, bf16[1,128,768]{2,1,0:T(8,128)(2,1)S(1)}, bf16[1,128,768]{2,1,0:T(8,128)(2,1)S(1)}) custom-call(s32[1]{0:T(128)} %bitcast.at_ref, bf16[128,768]{1,0:T(8,128)(2,1)S(1)} %get-tuple-element.74.refs_2_.refs_0_.q_ref, bf16[128,768]{1,0:T(8,128)(2,1)S(1)} %collective-permute-done.18.refs_1_, ...), custom_call_target="tpu_custom_call" | custom-call | flops 1000 | bytes 1000 | tf_op jit(solution)/shard_map/attend/pallas_call | solution.py:262
  66.7 1.8 %collective-permute-start.14 = (bf16[128,512]{1,0:T(8,128)(2,1)S(1)}, bf16[128,512]{1,0:T(8,128)(2,1)S(1)}, u32[]{:S(2)}, u32[]{:S(2)}) collective-permute-start(bf16[128,512]{1,0:T(8,128)(2,1)S(1)} %get-tuple-element.79.refs_2_.refs_0_.q_ref), channel_id=1, source_target_pairs={{0,2},{1,3},{2,0},{3,1},{4,6},{5,7},{6,4},{7,5},{8,10},{9,11},{10,... | collective-permute-start | bytes 393224 | tf_op jit(solution)/shard_map/ppermute | solution.py:525
  68.8 4.0 %collective-permute-done.14.refs_1_ = bf16[128,512]{1,0:T(8,128)(2,1)S(1)} collective-permute-done((bf16[128,512]{1,0:T(8,128)(2,1)S(1)}, bf16[128,512]{1,0:T(8,128)(2,1)S(1)}, u32[]{:S(2)}, u32[]{:S(2)}) %collective-permute-start.14) | collective-permute-done | bytes 131104 | tf_op jit(solution)/shard_map/ppermute | solution.py:525
  73.5 1.4 activate.6
  74.9 2.1 %collective-permute-start.25 = (bf16[128,512]{1,0:T(8,128)(2,1)S(1)}, bf16[128,512]{1,0:T(8,128)(2,1)S(1)}, u32[]{:S(2)}, u32[]{:S(2)}) collective-permute-start(bf16[128,512]{1,0:T(8,128)(2,1)S(1)} %get-tuple-element.82.refs_10_.refs_0_.q_ref), channel_id=1, source_target_pairs={{0,2},{1,3},{2,0},{3,1},{4,6},{5,7},{6,4},{7,5},{8,10},{9,11},{10,... | collective-permute-start | bytes 393224 | tf_op jit(solution)/shard_map/ppermute | solution.py:525
  77.0 3.1 %attend.5 = (bf16[2,128,512]{2,1,0:T(8,128)(2,1)S(1)}, bf16[1,128,512]{2,1,0:T(8,128)(2,1)S(1)}, bf16[1,128,512]{2,1,0:T(8,128)(2,1)S(1)}) custom-call(s32[1]{0:T(128)} %bitcast.at_ref, bf16[128,512]{1,0:T(8,128)(2,1)S(1)} %get-tuple-element.79.refs_2_.refs_0_.q_ref, bf16[128,512]{1,0:T(8,128)(2,1)S(1)} %collective-permute-done.14.refs_1_, ...), custom_call_target="tpu_custom_call" | custom-call | flops 1000 | bytes 1000 | tf_op jit(solution)/shard_map/attend/pallas_call | solution.py:262
  81.3 1.7 collective-permute-start.31
  83.3 3.2 %attend.6 = (bf16[2,128,512]{2,1,0:T(8,128)(2,1)S(1)}, bf16[1,128,512]{2,1,0:T(8,128)(2,1)S(1)}, bf16[1,128,512]{2,1,0:T(8,128)(2,1)S(1)}) custom-call(s32[1]{0:T(128)} %bitcast.at_ref, bf16[128,512]{1,0:T(8,128)(2,1)S(1)} %get-tuple-element.82.refs_10_.refs_0_.q_ref, bf16[128,512]{1,0:T(8,128)(2,1)S(1)} %collective-permute-done.25.refs_1_, ...), custom_call_target="tpu_custom_call" | custom-call | flops 1000 | bytes 1000 | tf_op jit(solution)/shard_map/attend/pallas_call | solution.py:262
  87.2 3.9 %collective-permute-done.22.refs_1_ = bf16[128,256]{1,0:T(8,128)(2,1)S(1)} collective-permute-done((bf16[128,256]{1,0:T(8,128)(2,1)S(1)}, bf16[128,256]{1,0:T(8,128)(2,1)S(1)}, u32[]{:S(2)}, u32[]{:S(2)}) %collective-permute-start.22) | collective-permute-done | bytes 65568 | tf_op jit(solution)/shard_map/ppermute | solution.py:525
  92.7 2.0 %attend.7 = (bf16[2,128,256]{2,1,0:T(8,128)(2,1)S(1)}, bf16[1,128,256]{2,1,0:T(8,128)(2,1)S(1)}, bf16[1,128,256]{2,1,0:T(8,128)(2,1)S(1)}) custom-call(s32[1]{0:T(128)} %bitcast.at_ref, bf16[128,256]{1,0:T(8,128)(2,1)S(1)} %get-tuple-element.84.refs_2_.refs_0_.q_ref, bf16[128,256]{1,0:T(8,128)(2,1)S(1)} %collective-permute-done.22.refs_1_, ...), custom_call_target="tpu_custom_call" | custom-call | flops 1000 | bytes 1000 | tf_op jit(solution)/shard_map/attend/pallas_call | solution.py:262
  95.3 1.7 collective-permute-start.38
  98.8 2.3 %collective-permute-done.38.refs_2_ = bf16[1,128,512]{2,1,0:T(8,128)(2,1)S(1)} collective-permute-done((bf16[1,128,512]{2,1,0:T(8,128)(2,1)S(1)}, bf16[1,128,512]{2,1,0:T(8,128)(2,1)S(1)}, u32[]{:S(2)}, u32[]{:S(2)}) %collective-permute-start.38) | collective-permute-done | bytes 131104 | tf_op jit(solution)/shard_map/ppermute | solution.py:525
  102.7 1.8 %collective-permute-start.39 = (f32[8,128]{1,0:T(8,128)S(1)}, f32[8,128]{1,0:T(8,128)S(1)}, u32[]{:S(2)}, u32[]{:S(2)}) collective-permute-start(f32[8,128]{1,0:T(8,128)S(1)} %get-tuple-element.104.refs_0_), channel_id=1, source_target_pairs={{0,4},{4,0},{8,12},{12,8},{1,5},{5,1},{9,13},{13,9},{2,6},{6,2},{1... | collective-permute-start | bytes 12296 | tf_op jit(solution)/shard_map/ppermute | solution.py:525
  104.5 1.9 %collective-permute-done.39.refs_1_ = f32[8,128]{1,0:T(8,128)S(1)} collective-permute-done((f32[8,128]{1,0:T(8,128)S(1)}, f32[8,128]{1,0:T(8,128)S(1)}, u32[]{:S(2)}, u32[]{:S(2)}) %collective-permute-start.39) | collective-permute-done | bytes 4128 | tf_op jit(solution)/shard_map/ppermute | solution.py:525
  106.4 2.8 %collective-permute-start.40 = (f32[8,128]{1,0:T(8,128)S(1)}, f32[8,128]{1,0:T(8,128)S(1)}, u32[]{:S(2)}, u32[]{:S(2)}) collective-permute-start(f32[8,128]{1,0:T(8,128)S(1)} %merge.1.refs_0_), channel_id=1, source_target_pairs={{0,8},{4,12},{8,0},{12,4},{1,9},{5,13},{9,1},{13,5},{2,10},{6,14},... | collective-permute-start | bytes 12296 | tf_op jit(solution)/shard_map/ppermute | solution.py:525
  109.1 1.7 %collective-permute-done.40.refs_1_ = f32[8,128]{1,0:T(8,128)S(1)} collective-permute-done((f32[8,128]{1,0:T(8,128)S(1)}, f32[8,128]{1,0:T(8,128)S(1)}, u32[]{:S(2)}, u32[]{:S(2)}) %collective-permute-start.40) | collective-permute-done | bytes 4128 | tf_op jit(solution)/shard_map/ppermute | solution.py:525
  111.3 1.7 %collective-permute-start.42 = (bf16[64,2048]{1,0:T(8,128)(2,1)S(1)}, bf16[64,2048]{1,0:T(8,128)(2,1)S(1)}, u32[]{:S(2)}, u32[]{:S(2)}) collective-permute-start(bf16[64,2048]{1,0:T(8,128)(2,1)S(1)} %get-tuple-element.107), channel_id=1, source_target_pairs={{0,2},{1,3},{2,0},{3,1},{4,6},{5,7},{6,4},{7,5},{8,10},{9,11},{10,... | collective-permute-start | bytes 786440 | tf_op jit(solution)/shard_map/ppermute | solution.py:525
  113.4 6.7 %collective-permute-done.42 = bf16[64,2048]{1,0:T(8,128)(2,1)S(1)} collective-permute-done((bf16[64,2048]{1,0:T(8,128)(2,1)S(1)}, bf16[64,2048]{1,0:T(8,128)(2,1)S(1)}, u32[]{:S(2)}, u32[]{:S(2)}) %collective-permute-start.42) | collective-permute-done | bytes 262176 | tf_op jit(solution)/shard_map/ppermute | solution.py:525
  121.7 3.4 %output.4 = (bf16[2,4,16,1024]{3,2,1,0:T(8,128)(2,1)S(1)}, bf16[2,4,16,1024]{3,2,1,0:T(8,128)(2,1)S(1)}) custom-call(s32[1]{0:T(128)} %bitcast.3.index_ref, bf16[4,16,2048]{2,1,0:T(8,128)(2,1)S(1)} %bitcast.47, bf16[4,16,2048]{2,1,0:T(8,128)(2,1)S(1)} %bitcast.49, bf16[4,16,2048]{2,1,0:T(8,128)(2,1)S(1)} %bitcast.51, bf16[4,16,2048]{2,1,0:T(8,128)(2,1)S(1)} %bitcast.53, ...), custom_call_target="tpu_custom_call" | custom-call | flops 1000 | bytes 1000 | tf_op jit(solution)/shard_map/output/pallas_call | solution.py:444
  125.3 1.6 collective-permute-start.47
  126.9 3.4 %output.5 = (bf16[2,4,16,1024]{3,2,1,0:T(8,128)(2,1)S(1)}, bf16[2,4,16,1024]{3,2,1,0:T(8,128)(2,1)S(1)}) custom-call(s32[1]{0:T(128)} %bitcast.3.index_ref, bf16[4,16,2048]{2,1,0:T(8,128)(2,1)S(1)} %bitcast.48, bf16[4,16,2048]{2,1,0:T(8,128)(2,1)S(1)} %bitcast.50, bf16[4,16,2048]{2,1,0:T(8,128)(2,1)S(1)} %bitcast.52, bf16[4,16,2048]{2,1,0:T(8,128)(2,1)S(1)} %bitcast.54, ...), custom_call_target="tpu_custom_call" | custom-call | flops 1000 | bytes 1000 | tf_op jit(solution)/shard_map/output/pallas_call | solution.py:444
  130.9 3.5 %output.6 = (bf16[2,4,16,1024]{3,2,1,0:T(8,128)(2,1)S(1)}, bf16[2,4,16,1024]{3,2,1,0:T(8,128)(2,1)S(1)}) custom-call(s32[1]{0:T(128)} %bitcast.3.index_ref, bf16[4,16,2176]{2,1,0:T(8,128)(2,1)S(1)} %bitcast.41, bf16[4,16,2176]{2,1,0:T(8,128)(2,1)S(1)} %bitcast.39, bf16[4,16,2176]{2,1,0:T(8,128)(2,1)S(1)} %bitcast.43, bf16[4,16,2176]{2,1,0:T(8,128)(2,1)S(1)} %bitcast.45, ...), custom_call_target="tpu_custom_call" | custom-call | flops 1000 | bytes 1000 | tf_op jit(solution)/shard_map/output/pallas_call | solution.py:444
  134.6 2.6 %collective-permute-start.51 = (bf16[1,4,16,1024]{3,2,1,0:T(8,128)(2,1)S(1)}, bf16[1,4,16,1024]{3,2,1,0:T(8,128)(2,1)S(1)}, u32[]{:S(2)}, u32[]{:S(2)}) collective-permute-start(bf16[1,4,16,1024]{3,2,1,0:T(8,128)(2,1)S(1)} %fold.22.refs_5_), channel_id=1, source_target_pairs={{0,8},{4,12},{8,0},{12,4},{1,9},{5,13},{9,1},{13,5},{2,10},{6,14},... | collective-permute-start | bytes 393224 | tf_op jit(solution)/shard_map/ppermute | solution.py:525
  137.2 1.6 collective-permute-start.48
  138.8 3.5 %output.7 = (bf16[2,4,16,1024]{3,2,1,0:T(8,128)(2,1)S(1)}, bf16[2,4,16,1024]{3,2,1,0:T(8,128)(2,1)S(1)}) custom-call(s32[1]{0:T(128)} %bitcast.3.index_ref, bf16[4,16,2176]{2,1,0:T(8,128)(2,1)S(1)} %bitcast.42, bf16[4,16,2176]{2,1,0:T(8,128)(2,1)S(1)} %bitcast.40, bf16[4,16,2176]{2,1,0:T(8,128)(2,1)S(1)} %bitcast.44, bf16[4,16,2176]{2,1,0:T(8,128)(2,1)S(1)} %bitcast.46, ...), custom_call_target="tpu_custom_call" | custom-call | flops 1000 | bytes 1000 | tf_op jit(solution)/shard_map/output/pallas_call | solution.py:444
  142.9 2.6 %collective-permute-start.52 = (bf16[2,4,16,1024]{3,2,1,0:T(8,128)(2,1)S(1)}, bf16[2,4,16,1024]{3,2,1,0:T(8,128)(2,1)S(1)}, u32[]{:S(2)}, u32[]{:S(2)}) collective-permute-start(bf16[2,4,16,1024]{3,2,1,0:T(8,128)(2,1)S(1)} %tie.21), channel_id=1, source_target_pairs={{0,4},{4,0},{8,12},{12,8},{1,5},{5,1},{9,13},{13,9},{2,6},{6,2},{1... | collective-permute-start | bytes 786440 | tf_op jit(solution)/shard_map/ppermute | solution.py:525
  145.7 2.4 %collective-permute-start.54 = (bf16[1,4,16,1024]{3,2,1,0:T(8,128)(2,1)S(1)}, bf16[1,4,16,1024]{3,2,1,0:T(8,128)(2,1)S(1)}, u32[]{:S(2)}, u32[]{:S(2)}) collective-permute-start(bf16[1,4,16,1024]{3,2,1,0:T(8,128)(2,1)S(1)} %fold.23.refs_2_), channel_id=1, source_target_pairs={{0,8},{4,12},{8,0},{12,4},{1,9},{5,13},{9,1},{13,5},{2,10},{6,14},... | collective-permute-start | bytes 393224 | tf_op jit(solution)/shard_map/ppermute | solution.py:525
  148.0 1.9 %collective-permute-done.48.refs_1_ = bf16[2,4,16,1024]{3,2,1,0:T(8,128)(2,1)S(1)} collective-permute-done((bf16[2,4,16,1024]{3,2,1,0:T(8,128)(2,1)S(1)}, bf16[2,4,16,1024]{3,2,1,0:T(8,128)(2,1)S(1)}, u32[]{:S(2)}, u32[]{:S(2)}) %collective-permute-start.48) | collective-permute-done | bytes 262176 | tf_op jit(solution)/shard_map/ppermute | solution.py:525
  150.0 3.1 %collective-permute-start.50 = (bf16[1,4,16,1024]{3,2,1,0:T(8,128)(2,1)S(1)}, bf16[1,4,16,1024]{3,2,1,0:T(8,128)(2,1)S(1)}, u32[]{:S(2)}, u32[]{:S(2)}) collective-permute-start(bf16[1,4,16,1024]{3,2,1,0:T(8,128)(2,1)S(1)} %fold.24.refs_3_), channel_id=1, source_target_pairs={{0,8},{4,12},{8,0},{12,4},{1,9},{5,13},{9,1},{13,5},{2,10},{6,14},... | collective-permute-start | bytes 393224 | tf_op jit(solution)/shard_map/ppermute | solution.py:525
  153.2 2.2 %close.3 = (bf16[8,16,2048]{2,1,0:T(8,128)(2,1)}, f32[8,128]{1,0:T(8,128)S(1)}) custom-call(s32[2]{0:T(128)S(1)} %pad_add_fusion.1.at_ref, bf16[32,16,2048]{2,1,0:T(8,128)(2,1)} %bitcast.77, bf16[2,4,16,1024]{3,2,1,0:T(8,128)(2,1)S(1)} %get-tuple-element.108.refs_1_.refs_5_.refs_0_, bf16[2,4,16,1024]{3,2,1,0:T(8,128)(2,1)S(1)} %collective-permute-done.47.refs_1_, ...), custom_call_target="tpu_custom_call" | custom-call | flops 1000 | bytes 1000 | tf_op jit(solution)/shard_map/close/pallas_call | solution.py:490
  155.3 3.4 %collective-permute-done.52.refs_1_.refs_4_ = bf16[2,4,16,1024]{3,2,1,0:T(8,128)(2,1)S(1)} collective-permute-done((bf16[2,4,16,1024]{3,2,1,0:T(8,128)(2,1)S(1)}, bf16[2,4,16,1024]{3,2,1,0:T(8,128)(2,1)S(1)}, u32[]{:S(2)}, u32[]{:S(2)}) %collective-permute-start.52) | collective-permute-done | bytes 262176 | tf_op jit(solution)/shard_map/ppermute | solution.py:525
  159.0 2.2 %close.4 = (bf16[8,16,2048]{2,1,0:T(8,128)(2,1)}, f32[8,128]{1,0:T(8,128)S(1)}) custom-call(s32[2]{0:T(128)S(1)} %pad_add_fusion.1.at_ref, bf16[32,16,2048]{2,1,0:T(8,128)(2,1)} %bitcast.78, bf16[2,4,16,1024]{3,2,1,0:T(8,128)(2,1)S(1)} %get-tuple-element.109.refs_5_.refs_0_, ...), custom_call_target="tpu_custom_call", output_to_operand_aliasing={{0}: (5, {})} | custom-call | flops 1000 | bytes 1000 | tf_op jit(solution)/shard_map/close/pallas_call | solution.py:490
  161.2 3.7 %collective-permute-done.50.refs_2_ = bf16[1,4,16,1024]{3,2,1,0:T(8,128)(2,1)S(1)} collective-permute-done((bf16[1,4,16,1024]{3,2,1,0:T(8,128)(2,1)S(1)}, bf16[1,4,16,1024]{3,2,1,0:T(8,128)(2,1)S(1)}, u32[]{:S(2)}, u32[]{:S(2)}) %collective-permute-start.50) | collective-permute-done | bytes 131104 | tf_op jit(solution)/shard_map/ppermute | solution.py:525
  164.9 2.4 %collective-permute-done.53.refs_5_ = bf16[1,4,16,1024]{3,2,1,0:T(8,128)(2,1)S(1)} collective-permute-done((bf16[1,4,16,1024]{3,2,1,0:T(8,128)(2,1)S(1)}, bf16[1,4,16,1024]{3,2,1,0:T(8,128)(2,1)S(1)}, u32[]{:S(2)}, u32[]{:S(2)}) %collective-permute-start.53) | collective-permute-done | bytes 131104 | tf_op jit(solution)/shard_map/ppermute | solution.py:525
  167.4 2.3 %close.5 = (bf16[8,16,2048]{2,1,0:T(8,128)(2,1)}, f32[8,128]{1,0:T(8,128)}) custom-call(s32[2]{0:T(128)S(1)} %pad_add_fusion.at_ref, bf16[32,16,2048]{2,1,0:T(8,128)(2,1)} %bitcast.79, bf16[2,4,16,1024]{3,2,1,0:T(8,128)(2,1)S(1)} %get-tuple-element.110.refs_2_.refs_0_, ...), custom_call_target="tpu_custom_call", output_to_operand_aliasing={{0}: (8, {})} | custom-call | flops 1000 | bytes 1000 | tf_op jit(solution)/shard_map/close/pallas_call | solution.py:490
  (135 shorter events, 20.9 us)
Async XLA Ops:
  5.5 9.4 %collective-permute-start = (bf16[1,4,128,256]{3,2,1,0:T(8,128)(2,1)S(1)}, bf16[1,4,128,256]{3,2,1,0:T(8,128)(2,1)S(1)}, u32[]{:S(2)}, u32[]{:S(2)}) collective-permute-start(bf16[1,4,128,256]{3,2,1,0:T(8,128)(2,1)S(1)} %get-tuple-element.66), channel_id=1, source_target_pairs={{0,1},{1,0},{2,3},{3,2},{4,5},{5,4},{6,7},{7,6},{8,9},{9,8},{10,11... | collective-permute-start | bytes 786440 | tf_op jit(solution)/shard_map/ppermute | solution.py:525
  6.1 8.8 %collective-permute-start.1 = (bf16[1,4,128,256]{3,2,1,0:T(8,128)(2,1)S(1)}, bf16[1,4,128,256]{3,2,1,0:T(8,128)(2,1)S(1)}, u32[]{:S(2)}, u32[]{:S(2)}) collective-permute-start(bf16[1,4,128,256]{3,2,1,0:T(8,128)(2,1)S(1)} %get-tuple-element.67), channel_id=1, source_target_pairs={{0,1},{1,0},{2,3},{3,2},{4,5},{5,4},{6,7},{7,6},{8,9},{9,8},{10,11... | collective-permute-start | bytes 786440 | tf_op jit(solution)/shard_map/ppermute | solution.py:525
  14.9 12.6 %collective-permute-start.3 = (bf16[1,4,128,512]{3,2,1,0:T(8,128)(2,1)S(1)}, bf16[1,4,128,512]{3,2,1,0:T(8,128)(2,1)S(1)}, u32[]{:S(2)}, u32[]{:S(2)}) collective-permute-start(bf16[1,4,128,512]{3,2,1,0:T(8,128)(2,1)S(1)} %tie.12), channel_id=1, source_target_pairs={{0,1},{1,0},{2,3},{3,2},{4,5},{5,4},{6,7},{7,6},{8,9},{9,8},{10,11... | collective-permute-start | bytes 1572872 | tf_op jit(solution)/shard_map/ppermute | solution.py:525
  15.4 12.1 %collective-permute-start.2 = (bf16[1,4,128,512]{3,2,1,0:T(8,128)(2,1)S(1)}, bf16[1,4,128,512]{3,2,1,0:T(8,128)(2,1)S(1)}, u32[]{:S(2)}, u32[]{:S(2)}) collective-permute-start(bf16[1,4,128,512]{3,2,1,0:T(8,128)(2,1)S(1)} %tie.11), channel_id=1, source_target_pairs={{0,1},{1,0},{2,3},{3,2},{4,5},{5,4},{6,7},{7,6},{8,9},{9,8},{10,11... | collective-permute-start | bytes 1572872 | tf_op jit(solution)/shard_map/ppermute | solution.py:525
  15.8 11.7 %collective-permute-start.4 = (bf16[1,4,128,256]{3,2,1,0:T(8,128)(2,1)S(1)}, bf16[1,4,128,256]{3,2,1,0:T(8,128)(2,1)S(1)}, u32[]{:S(2)}, u32[]{:S(2)}) collective-permute-start(bf16[1,4,128,256]{3,2,1,0:T(8,128)(2,1)S(1)} %fold.13.refs_8_), channel_id=1, source_target_pairs={{0,2},{1,3},{2,0},{3,1},{4,6},{5,7},{6,4},{7,5},{8,10},{9,11},{10,... | collective-permute-start | bytes 786440 | tf_op jit(solution)/shard_map/ppermute | solution.py:525
  27.5 9.8 %collective-permute-start.6 = (bf16[1,4,128,512]{3,2,1,0:T(8,128)(2,1)S(1)}, bf16[1,4,128,512]{3,2,1,0:T(8,128)(2,1)S(1)}, u32[]{:S(2)}, u32[]{:S(2)}) collective-permute-start(bf16[1,4,128,512]{3,2,1,0:T(8,128)(2,1)S(1)} %tie.14), channel_id=1, source_target_pairs={{0,1},{1,0},{2,3},{3,2},{4,5},{5,4},{6,7},{7,6},{8,9},{9,8},{10,11... | collective-permute-start | bytes 1572872 | tf_op jit(solution)/shard_map/ppermute | solution.py:525
  27.6 9.7 %collective-permute-start.5 = (bf16[1,4,128,512]{3,2,1,0:T(8,128)(2,1)S(1)}, bf16[1,4,128,512]{3,2,1,0:T(8,128)(2,1)S(1)}, u32[]{:S(2)}, u32[]{:S(2)}) collective-permute-start(bf16[1,4,128,512]{3,2,1,0:T(8,128)(2,1)S(1)} %tie.13), channel_id=1, source_target_pairs={{0,1},{1,0},{2,3},{3,2},{4,5},{5,4},{6,7},{7,6},{8,9},{9,8},{10,11... | collective-permute-start | bytes 1572872 | tf_op jit(solution)/shard_map/ppermute | solution.py:525
  28.4 14.0 %collective-permute-start.8 = (bf16[1,4,128,512]{3,2,1,0:T(8,128)(2,1)S(1)}, bf16[1,4,128,512]{3,2,1,0:T(8,128)(2,1)S(1)}, u32[]{:S(2)}, u32[]{:S(2)}) collective-permute-start(bf16[1,4,128,512]{3,2,1,0:T(8,128)(2,1)S(1)} %fold.14.refs_8_), channel_id=1, source_target_pairs={{0,2},{1,3},{2,0},{3,1},{4,6},{5,7},{6,4},{7,5},{8,10},{9,11},{10,... | collective-permute-start | bytes 1572872 | tf_op jit(solution)/shard_map/ppermute | solution.py:525
  37.3 5.9 %collective-permute-start.7 = (bf16[1,4,128,512]{3,2,1,0:T(8,128)(2,1)S(1)}, bf16[1,4,128,512]{3,2,1,0:T(8,128)(2,1)S(1)}, u32[]{:S(2)}, u32[]{:S(2)}) collective-permute-start(bf16[1,4,128,512]{3,2,1,0:T(8,128)(2,1)S(1)} %tie.15), channel_id=1, source_target_pairs={{0,1},{1,0},{2,3},{3,2},{4,5},{5,4},{6,7},{7,6},{8,9},{9,8},{10,11... | collective-permute-start | bytes 1572872 | tf_op jit(solution)/shard_map/ppermute | solution.py:525
  38.1 14.7 %collective-permute-start.9 = (bf16[1,4,128,512]{3,2,1,0:T(8,128)(2,1)S(1)}, bf16[1,4,128,512]{3,2,1,0:T(8,128)(2,1)S(1)}, u32[]{:S(2)}, u32[]{:S(2)}) collective-permute-start(bf16[1,4,128,512]{3,2,1,0:T(8,128)(2,1)S(1)} %tie.16), channel_id=1, source_target_pairs={{0,1},{1,0},{2,3},{3,2},{4,5},{5,4},{6,7},{7,6},{8,9},{9,8},{10,11... | collective-permute-start | bytes 1572872 | tf_op jit(solution)/shard_map/ppermute | solution.py:525
  39.1 19.4 %collective-permute-start.12 = (bf16[1,4,128,512]{3,2,1,0:T(8,128)(2,1)}, bf16[1,4,128,512]{3,2,1,0:T(8,128)(2,1)}, u32[]{:S(2)}, u32[]{:S(2)}) collective-permute-start(bf16[1,4,128,512]{3,2,1,0:T(8,128)(2,1)} %fold.15.refs_6_), channel_id=1, source_target_pairs={{0,2},{1,3},{2,0},{3,1},{4,6},{5,7},{6,4},{7,5},{8,10},{9,11},{10,... | collective-permute-start | bytes 1572872 | tf_op jit(solution)/shard_map/ppermute | solution.py:525
  42.9 15.5 %collective-permute-start.18 = (bf16[128,768]{1,0:T(8,128)(2,1)S(1)}, bf16[128,768]{1,0:T(8,128)(2,1)S(1)}, u32[]{:S(2)}, u32[]{:S(2)}) collective-permute-start(bf16[128,768]{1,0:T(8,128)(2,1)S(1)} %get-tuple-element.74.refs_2_.refs_0_.q_ref), channel_id=1, source_target_pairs={{0,2},{1,3},{2,0},{3,1},{4,6},{5,7},{6,4},{7,5},{8,10},{9,11},{10,... | collective-permute-start | bytes 589832 | tf_op jit(solution)/shard_map/ppermute | solution.py:525
  44.2 29.3 %collective-permute-start.17 = (bf16[1,4,128,512]{3,2,1,0:T(8,128)(2,1)}, bf16[1,4,128,512]{3,2,1,0:T(8,128)(2,1)}, u32[]{:S(2)}, u32[]{:S(2)}) collective-permute-start(bf16[1,4,128,512]{3,2,1,0:T(8,128)(2,1)} %fold.16.refs_8_), channel_id=1, source_target_pairs={{0,2},{1,3},{2,0},{3,1},{4,6},{5,7},{6,4},{7,5},{8,10},{9,11},{10,... | collective-permute-start | bytes 1572872 | tf_op jit(solution)/shard_map/ppermute | solution.py:525
  52.8 8.1 %collective-permute-start.11 = (bf16[1,4,128,256]{3,2,1,0:T(8,128)(2,1)}, bf16[1,4,128,256]{3,2,1,0:T(8,128)(2,1)}, u32[]{:S(2)}, u32[]{:S(2)}) collective-permute-start(bf16[1,4,128,256]{3,2,1,0:T(8,128)(2,1)} %tie.18), channel_id=1, source_target_pairs={{0,1},{1,0},{2,3},{3,2},{4,5},{5,4},{6,7},{7,6},{8,9},{9,8},{10,11... | collective-permute-start | bytes 786440 | tf_op jit(solution)/shard_map/ppermute | solution.py:525
  52.8 9.2 %collective-permute-start.19 = (bf16[128,768]{1,0:T(8,128)(2,1)S(1)}, bf16[128,768]{1,0:T(8,128)(2,1)}, u32[]{:S(2)}, u32[]{:S(2)}) collective-permute-start(bf16[128,768]{1,0:T(8,128)(2,1)S(1)} %get-tuple-element.74.refs_2_.refs_0_.q_ref), channel_id=1, source_target_pairs={{0,1},{1,0},{2,3},{3,2},{4,5},{5,4},{6,7},{7,6},{8,9},{9,8},{10,11... | collective-permute-start | bytes 589832 | tf_op jit(solution)/shard_map/ppermute | solution.py:525
  58.4 3.7 %collective-permute-start.20 = (bf16[128,768]{1,0:T(8,128)(2,1)S(1)}, bf16[128,768]{1,0:T(8,128)(2,1)}, u32[]{:S(2)}, u32[]{:S(2)}) collective-permute-start(bf16[128,768]{1,0:T(8,128)(2,1)S(1)} %collective-permute-done.18.refs_1_), channel_id=1, source_target_pairs={{0,1},{1,0},{2,3},{3,2},{4,5},{5,4},{6,7},{7,6},{8,9},{9,8},{10,11... | collective-permute-start | bytes 589832 | tf_op jit(solution)/shard_map/ppermute | solution.py:525
  66.2 6.7 %collective-permute-start.21 = (bf16[1,128,768]{2,1,0:T(8,128)(2,1)S(1)}, bf16[1,128,768]{2,1,0:T(8,128)(2,1)S(1)}, u32[]{:S(2)}, u32[]{:S(2)}) collective-permute-start(bf16[1,128,768]{2,1,0:T(8,128)(2,1)S(1)} %get-tuple-element.81), channel_id=1, source_target_pairs={{0,1},{1,0},{2,3},{3,2},{4,5},{5,4},{6,7},{7,6},{8,9},{9,8},{10,11... | collective-permute-start | bytes 589832 | tf_op jit(solution)/shard_map/ppermute | solution.py:525
  66.7 6.1 %collective-permute-start.14 = (bf16[128,512]{1,0:T(8,128)(2,1)S(1)}, bf16[128,512]{1,0:T(8,128)(2,1)S(1)}, u32[]{:S(2)}, u32[]{:S(2)}) collective-permute-start(bf16[128,512]{1,0:T(8,128)(2,1)S(1)} %get-tuple-element.79.refs_2_.refs_0_.q_ref), channel_id=1, source_target_pairs={{0,2},{1,3},{2,0},{3,1},{4,6},{5,7},{6,4},{7,5},{8,10},{9,11},{10,... | collective-permute-start | bytes 393224 | tf_op jit(solution)/shard_map/ppermute | solution.py:525
  68.5 12.3 %collective-permute-start.10 = (bf16[1,4,128,256]{3,2,1,0:T(8,128)(2,1)S(1)}, bf16[1,4,128,256]{3,2,1,0:T(8,128)(2,1)S(1)}, u32[]{:S(2)}, u32[]{:S(2)}) collective-permute-start(bf16[1,4,128,256]{3,2,1,0:T(8,128)(2,1)S(1)} %tie.17), channel_id=1, source_target_pairs={{0,1},{1,0},{2,3},{3,2},{4,5},{5,4},{6,7},{7,6},{8,9},{9,8},{10,11... | collective-permute-start | bytes 786440 | tf_op jit(solution)/shard_map/ppermute | solution.py:525
  68.5 12.7 %collective-permute-start.13 = (bf16[1,4,128,256]{3,2,1,0:T(8,128)(2,1)S(1)}, bf16[1,4,128,256]{3,2,1,0:T(8,128)(2,1)S(1)}, u32[]{:S(2)}, u32[]{:S(2)}) collective-permute-start(bf16[1,4,128,256]{3,2,1,0:T(8,128)(2,1)S(1)} %fold.17.refs_10_), channel_id=1, source_target_pairs={{0,2},{1,3},{2,0},{3,1},{4,6},{5,7},{6,4},{7,5},{8,10},{9,11},{10,... | collective-permute-start | bytes 786440 | tf_op jit(solution)/shard_map/ppermute | solution.py:525
  72.8 4.2 %collective-permute-start.15 = (bf16[128,512]{1,0:T(8,128)(2,1)S(1)}, bf16[128,512]{1,0:T(8,128)(2,1)S(1)}, u32[]{:S(2)}, u32[]{:S(2)}) collective-permute-start(bf16[128,512]{1,0:T(8,128)(2,1)S(1)} %get-tuple-element.79.refs_2_.refs_0_.q_ref), channel_id=1, source_target_pairs={{0,1},{1,0},{2,3},{3,2},{4,5},{5,4},{6,7},{7,6},{8,9},{9,8},{10,11... | collective-permute-start | bytes 393224 | tf_op jit(solution)/shard_map/ppermute | solution.py:525
  72.9 4.2 %collective-permute-start.16 = (bf16[128,512]{1,0:T(8,128)(2,1)S(1)}, bf16[128,512]{1,0:T(8,128)(2,1)S(1)}, u32[]{:S(2)}, u32[]{:S(2)}) collective-permute-start(bf16[128,512]{1,0:T(8,128)(2,1)S(1)} %collective-permute-done.14.refs_1_), channel_id=1, source_target_pairs={{0,1},{1,0},{2,3},{3,2},{4,5},{5,4},{6,7},{7,6},{8,9},{9,8},{10,11... | collective-permute-start | bytes 393224 | tf_op jit(solution)/shard_map/ppermute | solution.py:525
  74.9 5.8 %collective-permute-start.25 = (bf16[128,512]{1,0:T(8,128)(2,1)S(1)}, bf16[128,512]{1,0:T(8,128)(2,1)S(1)}, u32[]{:S(2)}, u32[]{:S(2)}) collective-permute-start(bf16[128,512]{1,0:T(8,128)(2,1)S(1)} %get-tuple-element.82.refs_10_.refs_0_.q_ref), channel_id=1, source_target_pairs={{0,2},{1,3},{2,0},{3,1},{4,6},{5,7},{6,4},{7,5},{8,10},{9,11},{10,... | collective-permute-start | bytes 393224 | tf_op jit(solution)/shard_map/ppermute | solution.py:525
  80.8 10.3 %collective-permute-start.30 = (bf16[1,128,768]{2,1,0:T(8,128)(2,1)S(1)}, bf16[1,128,768]{2,1,0:T(8,128)(2,1)S(1)}, u32[]{:S(2)}, u32[]{:S(2)}) collective-permute-start(bf16[1,128,768]{2,1,0:T(8,128)(2,1)S(1)} %get-tuple-element.90), channel_id=1, source_target_pairs={{0,1},{1,0},{2,3},{3,2},{4,5},{5,4},{6,7},{7,6},{8,9},{9,8},{10,11... | collective-permute-start | bytes 589832 | tf_op jit(solution)/shard_map/ppermute | solution.py:525
  81.3 10.4 %collective-permute-start.31 = (bf16[1,128,768]{2,1,0:T(8,128)(2,1)S(1)}, bf16[1,128,768]{2,1,0:T(8,128)(2,1)S(1)}, u32[]{:S(2)}, u32[]{:S(2)}) collective-permute-start(bf16[1,128,768]{2,1,0:T(8,128)(2,1)S(1)} %fold.18.refs_3_), channel_id=1, source_target_pairs={{0,2},{1,3},{2,0},{3,1},{4,6},{5,7},{6,4},{7,5},{8,10},{9,11},{10,... | collective-permute-start | bytes 589832 | tf_op jit(solution)/shard_map/ppermute | solution.py:525
  86.5 6.0 %collective-permute-start.29 = (bf16[1,128,512]{2,1,0:T(8,128)(2,1)S(1)}, bf16[1,128,512]{2,1,0:T(8,128)(2,1)S(1)}, u32[]{:S(2)}, u32[]{:S(2)}) collective-permute-start(bf16[1,128,512]{2,1,0:T(8,128)(2,1)S(1)} %get-tuple-element.88), channel_id=1, source_target_pairs={{0,1},{1,0},{2,3},{3,2},{4,5},{5,4},{6,7},{7,6},{8,9},{9,8},{10,11... | collective-permute-start | bytes 393224 | tf_op jit(solution)/shard_map/ppermute | solution.py:525
  86.6 4.5 %collective-permute-start.22 = (bf16[128,256]{1,0:T(8,128)(2,1)S(1)}, bf16[128,256]{1,0:T(8,128)(2,1)S(1)}, u32[]{:S(2)}, u32[]{:S(2)}) collective-permute-start(bf16[128,256]{1,0:T(8,128)(2,1)S(1)} %get-tuple-element.84.refs_2_.refs_0_.q_ref), channel_id=1, source_target_pairs={{0,2},{1,3},{2,0},{3,1},{4,6},{5,7},{6,4},{7,5},{8,10},{9,11},{10,... | collective-permute-start | bytes 196616 | tf_op jit(solution)/shard_map/ppermute | solution.py:525
  87.1 5.6 %collective-permute-start.23 = (bf16[128,256]{1,0:T(8,128)(2,1)S(1)}, bf16[128,256]{1,0:T(8,128)(2,1)S(1)}, u32[]{:S(2)}, u32[]{:S(2)}) collective-permute-start(bf16[128,256]{1,0:T(8,128)(2,1)S(1)} %get-tuple-element.84.refs_2_.refs_0_.q_ref), channel_id=1, source_target_pairs={{0,1},{1,0},{2,3},{3,2},{4,5},{5,4},{6,7},{7,6},{8,9},{9,8},{10,11... | collective-permute-start | bytes 196616 | tf_op jit(solution)/shard_map/ppermute | solution.py:525
  91.1 6.2 %collective-permute-start.35 = (bf16[1,128,512]{2,1,0:T(8,128)(2,1)S(1)}, bf16[1,128,512]{2,1,0:T(8,128)(2,1)S(1)}, u32[]{:S(2)}, u32[]{:S(2)}) collective-permute-start(bf16[1,128,512]{2,1,0:T(8,128)(2,1)S(1)} %get-tuple-element.97), channel_id=1, source_target_pairs={{0,1},{1,0},{2,3},{3,2},{4,5},{5,4},{6,7},{7,6},{8,9},{9,8},{10,11... | collective-permute-start | bytes 393224 | tf_op jit(solution)/shard_map/ppermute | solution.py:525
  91.7 6.7 %collective-permute-start.36 = (bf16[1,128,512]{2,1,0:T(8,128)(2,1)S(1)}, bf16[1,128,512]{2,1,0:T(8,128)(2,1)S(1)}, u32[]{:S(2)}, u32[]{:S(2)}) collective-permute-start(bf16[1,128,512]{2,1,0:T(8,128)(2,1)S(1)} %fold.19.refs_10_), channel_id=1, source_target_pairs={{0,2},{1,3},{2,0},{3,1},{4,6},{5,7},{6,4},{7,5},{8,10},{9,11},{10,... | collective-permute-start | bytes 393224 | tf_op jit(solution)/shard_map/ppermute | solution.py:525
  94.8 3.9 %collective-permute-start.37 = (bf16[1,128,512]{2,1,0:T(8,128)(2,1)S(1)}, bf16[1,128,512]{2,1,0:T(8,128)(2,1)S(1)}, u32[]{:S(2)}, u32[]{:S(2)}) collective-permute-start(bf16[1,128,512]{2,1,0:T(8,128)(2,1)S(1)} %get-tuple-element.100), channel_id=1, source_target_pairs={{0,1},{1,0},{2,3},{3,2},{4,5},{5,4},{6,7},{7,6},{8,9},{9,8},{10,11... | collective-permute-start | bytes 393224 | tf_op jit(solution)/shard_map/ppermute | solution.py:525
  95.3 5.7 %collective-permute-start.38 = (bf16[1,128,512]{2,1,0:T(8,128)(2,1)S(1)}, bf16[1,128,512]{2,1,0:T(8,128)(2,1)S(1)}, u32[]{:S(2)}, u32[]{:S(2)}) collective-permute-start(bf16[1,128,512]{2,1,0:T(8,128)(2,1)S(1)} %fold.20.refs_10_), channel_id=1, source_target_pairs={{0,2},{1,3},{2,0},{3,1},{4,6},{5,7},{6,4},{7,5},{8,10},{9,11},{10,... | collective-permute-start | bytes 393224 | tf_op jit(solution)/shard_map/ppermute | solution.py:525
  97.0 4.5 %collective-permute-start.32 = (bf16[1,128,256]{2,1,0:T(8,128)(2,1)S(1)}, bf16[1,128,256]{2,1,0:T(8,128)(2,1)S(1)}, u32[]{:S(2)}, u32[]{:S(2)}) collective-permute-start(bf16[1,128,256]{2,1,0:T(8,128)(2,1)S(1)} %get-tuple-element.93), channel_id=1, source_target_pairs={{0,1},{1,0},{2,3},{3,2},{4,5},{5,4},{6,7},{7,6},{8,9},{9,8},{10,11... | collective-permute-start | bytes 196616 | tf_op jit(solution)/shard_map/ppermute | solution.py:525
  97.4 4.9 %collective-permute-start.34 = (bf16[1,128,256]{2,1,0:T(8,128)(2,1)S(1)}, bf16[1,128,256]{2,1,0:T(8,128)(2,1)S(1)}, u32[]{:S(2)}, u32[]{:S(2)}) collective-permute-start(bf16[1,128,256]{2,1,0:T(8,128)(2,1)S(1)} %fold.21.refs_3_), channel_id=1, source_target_pairs={{0,2},{1,3},{2,0},{3,1},{4,6},{5,7},{6,4},{7,5},{8,10},{9,11},{10,... | collective-permute-start | bytes 196616 | tf_op jit(solution)/shard_map/ppermute | solution.py:525
  106.4 4.5 %collective-permute-start.40 = (f32[8,128]{1,0:T(8,128)S(1)}, f32[8,128]{1,0:T(8,128)S(1)}, u32[]{:S(2)}, u32[]{:S(2)}) collective-permute-start(f32[8,128]{1,0:T(8,128)S(1)} %merge.1.refs_0_), channel_id=1, source_target_pairs={{0,8},{4,12},{8,0},{12,4},{1,9},{5,13},{9,1},{13,5},{2,10},{6,14},... | collective-permute-start | bytes 12296 | tf_op jit(solution)/shard_map/ppermute | solution.py:525
  111.3 8.8 %collective-permute-start.42 = (bf16[64,2048]{1,0:T(8,128)(2,1)S(1)}, bf16[64,2048]{1,0:T(8,128)(2,1)S(1)}, u32[]{:S(2)}, u32[]{:S(2)}) collective-permute-start(bf16[64,2048]{1,0:T(8,128)(2,1)S(1)} %get-tuple-element.107), channel_id=1, source_target_pairs={{0,2},{1,3},{2,0},{3,1},{4,6},{5,7},{6,4},{7,5},{8,10},{9,11},{10,... | collective-permute-start | bytes 786440 | tf_op jit(solution)/shard_map/ppermute | solution.py:525
  113.0 12.1 %collective-permute-start.41 = (bf16[64,2176]{1,0:T(8,128)(2,1)S(1)}, bf16[64,2176]{1,0:T(8,128)(2,1)S(1)}, u32[]{:S(2)}, u32[]{:S(2)}) collective-permute-start(bf16[64,2176]{1,0:T(8,128)(2,1)S(1)} %get-tuple-element.106), channel_id=1, source_target_pairs={{0,2},{1,3},{2,0},{3,1},{4,6},{5,7},{6,4},{7,5},{8,10},{9,11},{10,... | collective-permute-start | bytes 835592 | tf_op jit(solution)/shard_map/ppermute | solution.py:525
  113.4 7.3 %collective-permute-start.43 = (bf16[64,2048]{1,0:T(8,128)(2,1)S(1)}, bf16[64,2048]{1,0:T(8,128)(2,1)S(1)}, u32[]{:S(2)}, u32[]{:S(2)}) collective-permute-start(bf16[64,2048]{1,0:T(8,128)(2,1)S(1)} %get-tuple-element.107), channel_id=1, source_target_pairs={{0,1},{1,0},{2,3},{3,2},{4,5},{5,4},{6,7},{7,6},{8,9},{9,8},{10,11... | collective-permute-start | bytes 786440 | tf_op jit(solution)/shard_map/ppermute | solution.py:525
  120.1 10.7 %collective-permute-start.45 = (bf16[64,2176]{1,0:T(8,128)(2,1)S(1)}, bf16[64,2176]{1,0:T(8,128)(2,1)S(1)}, u32[]{:S(2)}, u32[]{:S(2)}) collective-permute-start(bf16[64,2176]{1,0:T(8,128)(2,1)S(1)} %get-tuple-element.106), channel_id=1, source_target_pairs={{0,1},{1,0},{2,3},{3,2},{4,5},{5,4},{6,7},{7,6},{8,9},{9,8},{10,11... | collective-permute-start | bytes 835592 | tf_op jit(solution)/shard_map/ppermute | solution.py:525
  125.1 5.8 %collective-permute-start.46 = (bf16[64,2176]{1,0:T(8,128)(2,1)S(1)}, bf16[64,2176]{1,0:T(8,128)(2,1)S(1)}, u32[]{:S(2)}, u32[]{:S(2)}) collective-permute-start(bf16[64,2176]{1,0:T(8,128)(2,1)S(1)} %tie.19), channel_id=1, source_target_pairs={{0,1},{1,0},{2,3},{3,2},{4,5},{5,4},{6,7},{7,6},{8,9},{9,8},{10,11... | collective-permute-start | bytes 835592 | tf_op jit(solution)/shard_map/ppermute | solution.py:525
  125.3 9.1 %collective-permute-start.47 = (bf16[2,4,16,1024]{3,2,1,0:T(8,128)(2,1)S(1)}, bf16[2,4,16,1024]{3,2,1,0:T(8,128)(2,1)S(1)}, u32[]{:S(2)}, u32[]{:S(2)}) collective-permute-start(bf16[2,4,16,1024]{3,2,1,0:T(8,128)(2,1)S(1)} %get-tuple-element.112), channel_id=1, source_target_pairs={{0,4},{4,0},{8,12},{12,8},{1,5},{5,1},{9,13},{13,9},{2,6},{6,2},{1... | collective-permute-start | bytes 786440 | tf_op jit(solution)/shard_map/ppermute | solution.py:525
  130.3 12.5 %collective-permute-start.49 = (bf16[2,4,16,1024]{3,2,1,0:T(8,128)(2,1)S(1)}, bf16[2,4,16,1024]{3,2,1,0:T(8,128)(2,1)S(1)}, u32[]{:S(2)}, u32[]{:S(2)}) collective-permute-start(bf16[2,4,16,1024]{3,2,1,0:T(8,128)(2,1)S(1)} %get-tuple-element.113), channel_id=1, source_target_pairs={{0,4},{4,0},{8,12},{12,8},{1,5},{5,1},{9,13},{13,9},{2,6},{6,2},{1... | collective-permute-start | bytes 786440 | tf_op jit(solution)/shard_map/ppermute | solution.py:525
  134.6 8.3 %collective-permute-start.51 = (bf16[1,4,16,1024]{3,2,1,0:T(8,128)(2,1)S(1)}, bf16[1,4,16,1024]{3,2,1,0:T(8,128)(2,1)S(1)}, u32[]{:S(2)}, u32[]{:S(2)}) collective-permute-start(bf16[1,4,16,1024]{3,2,1,0:T(8,128)(2,1)S(1)} %fold.22.refs_5_), channel_id=1, source_target_pairs={{0,8},{4,12},{8,0},{12,4},{1,9},{5,13},{9,1},{13,5},{2,10},{6,14},... | collective-permute-start | bytes 393224 | tf_op jit(solution)/shard_map/ppermute | solution.py:525
  137.2 12.7 %collective-permute-start.48 = (bf16[2,4,16,1024]{3,2,1,0:T(8,128)(2,1)S(1)}, bf16[2,4,16,1024]{3,2,1,0:T(8,128)(2,1)S(1)}, u32[]{:S(2)}, u32[]{:S(2)}) collective-permute-start(bf16[2,4,16,1024]{3,2,1,0:T(8,128)(2,1)S(1)} %tie.20), channel_id=1, source_target_pairs={{0,4},{4,0},{8,12},{12,8},{1,5},{5,1},{9,13},{13,9},{2,6},{6,2},{1... | collective-permute-start | bytes 786440 | tf_op jit(solution)/shard_map/ppermute | solution.py:525
  142.9 15.8 %collective-permute-start.52 = (bf16[2,4,16,1024]{3,2,1,0:T(8,128)(2,1)S(1)}, bf16[2,4,16,1024]{3,2,1,0:T(8,128)(2,1)S(1)}, u32[]{:S(2)}, u32[]{:S(2)}) collective-permute-start(bf16[2,4,16,1024]{3,2,1,0:T(8,128)(2,1)S(1)} %tie.21), channel_id=1, source_target_pairs={{0,4},{4,0},{8,12},{12,8},{1,5},{5,1},{9,13},{13,9},{2,6},{6,2},{1... | collective-permute-start | bytes 786440 | tf_op jit(solution)/shard_map/ppermute | solution.py:525
  145.7 13.4 %collective-permute-start.54 = (bf16[1,4,16,1024]{3,2,1,0:T(8,128)(2,1)S(1)}, bf16[1,4,16,1024]{3,2,1,0:T(8,128)(2,1)S(1)}, u32[]{:S(2)}, u32[]{:S(2)}) collective-permute-start(bf16[1,4,16,1024]{3,2,1,0:T(8,128)(2,1)S(1)} %fold.23.refs_2_), channel_id=1, source_target_pairs={{0,8},{4,12},{8,0},{12,4},{1,9},{5,13},{9,1},{13,5},{2,10},{6,14},... | collective-permute-start | bytes 393224 | tf_op jit(solution)/shard_map/ppermute | solution.py:525
  150.0 14.9 %collective-permute-start.50 = (bf16[1,4,16,1024]{3,2,1,0:T(8,128)(2,1)S(1)}, bf16[1,4,16,1024]{3,2,1,0:T(8,128)(2,1)S(1)}, u32[]{:S(2)}, u32[]{:S(2)}) collective-permute-start(bf16[1,4,16,1024]{3,2,1,0:T(8,128)(2,1)S(1)} %fold.24.refs_3_), channel_id=1, source_target_pairs={{0,8},{4,12},{8,0},{12,4},{1,9},{5,13},{9,1},{13,5},{2,10},{6,14},... | collective-permute-start | bytes 393224 | tf_op jit(solution)/shard_map/ppermute | solution.py:525
  158.9 8.5 %collective-permute-start.53 = (bf16[1,4,16,1024]{3,2,1,0:T(8,128)(2,1)S(1)}, bf16[1,4,16,1024]{3,2,1,0:T(8,128)(2,1)S(1)}, u32[]{:S(2)}, u32[]{:S(2)}) collective-permute-start(bf16[1,4,16,1024]{3,2,1,0:T(8,128)(2,1)S(1)} %fold.25.refs_4_), channel_id=1, source_target_pairs={{0,8},{4,12},{8,0},{12,4},{1,9},{5,13},{9,1},{13,5},{2,10},{6,14},... | collective-permute-start | bytes 393224 | tf_op jit(solution)/shard_map/ppermute | solution.py:525
  (17 other events, 88.9 us)

commit v18 on v16

--- a/solution.py
+++ b/solution.py
@@ -567,7 +567,7 @@
 GROUPS = [[0, 1], [2], [3], [4]]
 ORDER = [
     "P0", "P1", "F0", "P2", "F1", "P3", "F2", "A0", "F3", "P4", "A1", "F4", "T0", "G0", "A2",
-    "T1", "A3", "G1", "T2", "E0", "G2", "T3", "G3", "E1", "E2", "E3",
+    "T1", "A3", "G1", "T2", "T3", "G2", "E0", "G3", "E1", "E2", "E3",
 ]
 
 
@@ -623,7 +623,8 @@
         elif step == "T":
             first = firsts[groups[c][0]]
             keep, *sends = attend(at, queries[c], k_cache, v_cache, edges, first, after)
-            halves[c] = keep, [swap(send, "hist", 0) for send in sends]
+            before = queries[last][1:2] if c == last - 1 and last in queries else []
+            halves[c] = keep, [swap(tie(send, before), "hist", 0) for send in sends]
             chain.append(keep)
         elif step == "G":
             sums[c], sent = scatter(*halves[c], "hist", after)

time: 170 us -> 167 us (0.982)
  waiting for transfers between devices: 40.9 us -> 37.3 us
    ppermute x55, waiting for transfers between devices: 40.9 us -> 37.3 us  [swap(): lax.ppermute(x, axis, [(i, i ^ 1 << bit) for i in range(lax.axis_size(axi...]
  transfers between devices with their start and end apart: 55 -> 55, of which waited for: 16 -> 16; matrix products, arithmetic and copies ran while one was open for 0% -> 0% of each run, Pallas kernels for 43% -> 44%
where the time goes in v18:
time: 167 us
  Pallas kernels  81.5 us (49%)
  starting transfers between devices  44.8 us (27%)
  waiting for transfers between devices  37.3 us (22%)
  local copies, waits for them, and re-layouts  2.4 us (1%)
    ppermute x55, starting transfers between devices, swap(): lax.ppermute(x, axis, [(i, i ^ 1 << bit) for i in range(lax.axis_size(axi...  44.8 us
    pallas_call x5, Pallas kernels, project(): pl.pallas_call(functools.partial(project_kernel, parts, owners, len(after...  37.9 us
    ppermute x55, waiting for transfers between devices, swap(): lax.ppermute(x, axis, [(i, i ^ 1 << bit) for i in range(lax.axis_size(axi...  37.3 us
    pallas_call x4, Pallas kernels, output(): pl.pallas_call(functools.partial(output_kernel, owners, slots, len(after)...  13.9 us
    pallas_call x4, Pallas kernels, attend(): pl.pallas_call(functools.partial(attend_kernel, owners, len(counts)), gri...  12.5 us
    pallas_call x3, Pallas kernels, close(): pl.pallas_call(functools.partial(close_kernel, [len(terms) for terms in g...  6.66 us
    pallas_call x13, Pallas kernels, fold(): pl.pallas_call(functools.partial(fold_kernel, len(terms)), grid=(steps,),...  4.75 us
    pallas_call x4, Pallas kernels, activate(): pl.pallas_call(functools.partial(activate_kernel, [len(terms) for terms i...  3.41 us
  transfers between devices with their start and end apart: 55, of which 16 were waited for; matrix products, arithmetic and copies ran while one was open for 0% of the time, Pallas kernels for 44%

profile of v18, /device:TPU:0, one launch (start us, length us, event | category | flops | bytes accessed | tf_op | source)
XLA Modules:
  0.0 166.8 jit_solution(2350930117738434125)
XLA Ops:
  0.0 5.5 %project.5 = (bf16[2,4,128,256]{3,2,1,0:T(8,128)(2,1)S(1)}, bf16[1,4,128,256]{3,2,1,0:T(8,128)(2,1)S(1)}, bf16[1,4,128,256]{3,2,1,0:T(8,128)(2,1)S(1)}) custom-call(s32[1]{0:T(128)} %bitcast.at_ref, bf16[4,2,4,16,2048]{4,3,2,1,0:T(8,128)(2,1)} %bitcast.57, bf16[4,2,4,16,2048]{4,3,2,1,0:T(8,128)(2,1)} %bitcast.58, bf16[4,2,4,16,2048]{4,3,2,1,0:T(8,128)(2,1)} %bitcast.59, ...), custom_call_target="tpu_custom_call" | custom-call | flops 1000 | bytes 1000 | tf_op jit(solution)/shard_map/project/pallas_call | solution.py:80
  6.1 8.7 %project.6 = (bf16[2,4,128,512]{3,2,1,0:T(8,128)(2,1)S(1)}, bf16[1,4,128,512]{3,2,1,0:T(8,128)(2,1)S(1)}, bf16[1,4,128,512]{3,2,1,0:T(8,128)(2,1)S(1)}) custom-call(s32[1]{0:T(128)} %bitcast.at_ref, bf16[4,2,4,16,2048]{4,3,2,1,0:T(8,128)(2,1)} %bitcast.61, bf16[4,2,4,16,2048]{4,3,2,1,0:T(8,128)(2,1)} %bitcast.62, bf16[4,2,4,16,2048]{4,3,2,1,0:T(8,128)(2,1)} %bitcast.63, ...), custom_call_target="tpu_custom_call" | custom-call | flops 1000 | bytes 1000 | tf_op jit(solution)/shard_map/project/pallas_call | solution.py:80
  15.8 3.0 %collective-permute-start.4 = (bf16[1,4,128,256]{3,2,1,0:T(8,128)(2,1)S(1)}, bf16[1,4,128,256]{3,2,1,0:T(8,128)(2,1)S(1)}, u32[]{:S(2)}, u32[]{:S(2)}) collective-permute-start(bf16[1,4,128,256]{3,2,1,0:T(8,128)(2,1)S(1)} %fold.13.refs_8_), channel_id=1, source_target_pairs={{0,2},{1,3},{2,0},{3,1},{4,6},{5,7},{6,4},{7,5},{8,10},{9,11},{10,... | collective-permute-start | bytes 786440 | tf_op jit(solution)/shard_map/ppermute | solution.py:525
  18.7 8.7 %project.7 = (bf16[2,4,128,512]{3,2,1,0:T(8,128)(2,1)S(1)}, bf16[1,4,128,512]{3,2,1,0:T(8,128)(2,1)S(1)}, bf16[1,4,128,512]{3,2,1,0:T(8,128)(2,1)S(1)}) custom-call(s32[1]{0:T(128)} %bitcast.at_ref, bf16[4,2,4,16,2048]{4,3,2,1,0:T(8,128)(2,1)} %bitcast.68, bf16[4,2,4,16,2048]{4,3,2,1,0:T(8,128)(2,1)} %bitcast.66, bf16[4,2,4,16,2048]{4,3,2,1,0:T(8,128)(2,1)} %bitcast.67, ...), custom_call_target="tpu_custom_call" | custom-call | flops 1000 | bytes 1000 | tf_op jit(solution)/shard_map/project/pallas_call | solution.py:80
  28.5 8.8 %project.8 = (bf16[2,4,128,512]{3,2,1,0:T(8,128)(2,1)S(1)}, bf16[1,4,128,512]{3,2,1,0:T(8,128)(2,1)S(1)}, bf16[1,4,128,512]{3,2,1,0:T(8,128)(2,1)S(1)}) custom-call(s32[1]{0:T(128)} %bitcast.at_ref, bf16[4,2,4,16,2048]{4,3,2,1,0:T(8,128)(2,1)} %bitcast.69, bf16[4,2,4,16,2048]{4,3,2,1,0:T(8,128)(2,1)} %bitcast.70, bf16[4,2,4,16,2048]{4,3,2,1,0:T(8,128)(2,1)} %bitcast.71, ...), custom_call_target="tpu_custom_call" | custom-call | flops 1000 | bytes 1000 | tf_op jit(solution)/shard_map/project/pallas_call | solution.py:80
  39.1 1.9 %collective-permute-start.12 = (bf16[1,4,128,512]{3,2,1,0:T(8,128)(2,1)}, bf16[1,4,128,512]{3,2,1,0:T(8,128)(2,1)}, u32[]{:S(2)}, u32[]{:S(2)}) collective-permute-start(bf16[1,4,128,512]{3,2,1,0:T(8,128)(2,1)} %fold.15.refs_6_), channel_id=1, source_target_pairs={{0,2},{1,3},{2,0},{3,1},{4,6},{5,7},{6,4},{7,5},{8,10},{9,11},{10,... | collective-permute-start | bytes 1572872 | tf_op jit(solution)/shard_map/ppermute | solution.py:525
  41.0 1.4 collective-permute-done.8.refs_5_
  44.2 1.7 %collective-permute-start.17 = (bf16[1,4,128,512]{3,2,1,0:T(8,128)(2,1)}, bf16[1,4,128,512]{3,2,1,0:T(8,128)(2,1)}, u32[]{:S(2)}, u32[]{:S(2)}) collective-permute-start(bf16[1,4,128,512]{3,2,1,0:T(8,128)(2,1)} %fold.16.refs_8_), channel_id=1, source_target_pairs={{0,2},{1,3},{2,0},{3,1},{4,6},{5,7},{6,4},{7,5},{8,10},{9,11},{10,... | collective-permute-start | bytes 1572872 | tf_op jit(solution)/shard_map/ppermute | solution.py:525
  45.9 6.1 %project.9 = (bf16[2,4,128,256]{3,2,1,0:T(8,128)(2,1)S(1)}, bf16[1,4,128,256]{3,2,1,0:T(8,128)(2,1)S(1)}, bf16[1,4,128,256]{3,2,1,0:T(8,128)(2,1)}) custom-call(s32[1]{0:T(128)} %bitcast.at_ref, bf16[4,2,4,16,2048]{4,3,2,1,0:T(8,128)(2,1)} %bitcast.73, bf16[4,2,4,16,2048]{4,3,2,1,0:T(8,128)(2,1)} %bitcast.74, bf16[4,2,4,16,2048]{4,3,2,1,0:T(8,128)(2,1)} %bitcast.75, ...), custom_call_target="tpu_custom_call" | custom-call | flops 1000 | bytes 1000 | tf_op jit(solution)/shard_map/project/pallas_call | solution.py:80
  53.3 5.0 %collective-permute-done.18.refs_1_ = bf16[128,768]{1,0:T(8,128)(2,1)S(1)} collective-permute-done((bf16[128,768]{1,0:T(8,128)(2,1)S(1)}, bf16[128,768]{1,0:T(8,128)(2,1)S(1)}, u32[]{:S(2)}, u32[]{:S(2)}) %collective-permute-start.18) | collective-permute-done | bytes 196640 | tf_op jit(solution)/shard_map/ppermute | solution.py:525
  58.5 1.0 copy-done.3
  59.6 1.4 activate.5
  60.9 1.1 fold.17.refs_10_
  62.1 4.1 %attend.4 = (bf16[2,128,768]{2,1,0:T(8,128)(2,1)S(1)}, bf16[1,128,768]{2,1,0:T(8,128)(2,1)S(1)}, bf16[1,128,768]{2,1,0:T(8,128)(2,1)S(1)}) custom-call(s32[1]{0:T(128)} %bitcast.at_ref, bf16[128,768]{1,0:T(8,128)(2,1)S(1)} %get-tuple-element.74.refs_2_.refs_0_.q_ref, bf16[128,768]{1,0:T(8,128)(2,1)S(1)} %collective-permute-done.18.refs_1_, ...), custom_call_target="tpu_custom_call" | custom-call | flops 1000 | bytes 1000 | tf_op jit(solution)/shard_map/attend/pallas_call | solution.py:262
  66.7 1.8 %collective-permute-start.14 = (bf16[128,512]{1,0:T(8,128)(2,1)S(1)}, bf16[128,512]{1,0:T(8,128)(2,1)S(1)}, u32[]{:S(2)}, u32[]{:S(2)}) collective-permute-start(bf16[128,512]{1,0:T(8,128)(2,1)S(1)} %get-tuple-element.79.refs_2_.refs_0_.q_ref), channel_id=1, source_target_pairs={{0,2},{1,3},{2,0},{3,1},{4,6},{5,7},{6,4},{7,5},{8,10},{9,11},{10,... | collective-permute-start | bytes 393224 | tf_op jit(solution)/shard_map/ppermute | solution.py:525
  68.8 4.0 %collective-permute-done.14.refs_1_ = bf16[128,512]{1,0:T(8,128)(2,1)S(1)} collective-permute-done((bf16[128,512]{1,0:T(8,128)(2,1)S(1)}, bf16[128,512]{1,0:T(8,128)(2,1)S(1)}, u32[]{:S(2)}, u32[]{:S(2)}) %collective-permute-start.14) | collective-permute-done | bytes 131104 | tf_op jit(solution)/shard_map/ppermute | solution.py:525
  73.5 1.4 activate.6
  74.9 2.1 %collective-permute-start.25 = (bf16[128,512]{1,0:T(8,128)(2,1)S(1)}, bf16[128,512]{1,0:T(8,128)(2,1)S(1)}, u32[]{:S(2)}, u32[]{:S(2)}) collective-permute-start(bf16[128,512]{1,0:T(8,128)(2,1)S(1)} %get-tuple-element.82.refs_10_.refs_0_.q_ref), channel_id=1, source_target_pairs={{0,2},{1,3},{2,0},{3,1},{4,6},{5,7},{6,4},{7,5},{8,10},{9,11},{10,... | collective-permute-start | bytes 393224 | tf_op jit(solution)/shard_map/ppermute | solution.py:525
  77.0 3.1 %attend.5 = (bf16[2,128,512]{2,1,0:T(8,128)(2,1)S(1)}, bf16[1,128,512]{2,1,0:T(8,128)(2,1)S(1)}, bf16[1,128,512]{2,1,0:T(8,128)(2,1)S(1)}) custom-call(s32[1]{0:T(128)} %bitcast.at_ref, bf16[128,512]{1,0:T(8,128)(2,1)S(1)} %get-tuple-element.79.refs_2_.refs_0_.q_ref, bf16[128,512]{1,0:T(8,128)(2,1)S(1)} %collective-permute-done.14.refs_1_, ...), custom_call_target="tpu_custom_call" | custom-call | flops 1000 | bytes 1000 | tf_op jit(solution)/shard_map/attend/pallas_call | solution.py:262
  81.0 1.7 %collective-permute-start.22 = (bf16[128,256]{1,0:T(8,128)(2,1)S(1)}, bf16[128,256]{1,0:T(8,128)(2,1)S(1)}, u32[]{:S(2)}, u32[]{:S(2)}) collective-permute-start(bf16[128,256]{1,0:T(8,128)(2,1)S(1)} %get-tuple-element.84.refs_2_.refs_0_.q_ref), channel_id=1, source_target_pairs={{0,2},{1,3},{2,0},{3,1},{4,6},{5,7},{6,4},{7,5},{8,10},{9,11},{10,... | collective-permute-start | bytes 196616 | tf_op jit(solution)/shard_map/ppermute | solution.py:525
  83.4 3.2 %attend.6 = (bf16[2,128,512]{2,1,0:T(8,128)(2,1)S(1)}, bf16[1,128,512]{2,1,0:T(8,128)(2,1)S(1)}, bf16[1,128,512]{2,1,0:T(8,128)(2,1)S(1)}) custom-call(s32[1]{0:T(128)} %bitcast.at_ref, bf16[128,512]{1,0:T(8,128)(2,1)S(1)} %get-tuple-element.82.refs_10_.refs_0_.q_ref, bf16[128,512]{1,0:T(8,128)(2,1)S(1)} %collective-permute-done.25.refs_1_, ...), custom_call_target="tpu_custom_call" | custom-call | flops 1000 | bytes 1000 | tf_op jit(solution)/shard_map/attend/pallas_call | solution.py:262
  88.5 1.7 collective-permute-start.36
  90.1 2.1 %attend.7 = (bf16[2,128,256]{2,1,0:T(8,128)(2,1)S(1)}, bf16[1,128,256]{2,1,0:T(8,128)(2,1)S(1)}, bf16[1,128,256]{2,1,0:T(8,128)(2,1)S(1)}) custom-call(s32[1]{0:T(128)} %bitcast.at_ref, bf16[128,256]{1,0:T(8,128)(2,1)S(1)} %get-tuple-element.84.refs_2_.refs_0_.q_ref, bf16[128,256]{1,0:T(8,128)(2,1)S(1)} %collective-permute-done.22.refs_1_, ...), custom_call_target="tpu_custom_call" | custom-call | flops 1000 | bytes 1000 | tf_op jit(solution)/shard_map/attend/pallas_call | solution.py:262
  94.4 1.7 %collective-permute-start.34 = (bf16[1,128,256]{2,1,0:T(8,128)(2,1)S(1)}, bf16[1,128,256]{2,1,0:T(8,128)(2,1)S(1)}, u32[]{:S(2)}, u32[]{:S(2)}) collective-permute-start(bf16[1,128,256]{2,1,0:T(8,128)(2,1)S(1)} %fold.21.refs_3_), channel_id=1, source_target_pairs={{0,2},{1,3},{2,0},{3,1},{4,6},{5,7},{6,4},{7,5},{8,10},{9,11},{10,... | collective-permute-start | bytes 196616 | tf_op jit(solution)/shard_map/ppermute | solution.py:525
  96.5 2.6 %collective-permute-done.38.refs_2_ = bf16[1,128,512]{2,1,0:T(8,128)(2,1)S(1)} collective-permute-done((bf16[1,128,512]{2,1,0:T(8,128)(2,1)S(1)}, bf16[1,128,512]{2,1,0:T(8,128)(2,1)S(1)}, u32[]{:S(2)}, u32[]{:S(2)}) %collective-permute-start.38) | collective-permute-done | bytes 131104 | tf_op jit(solution)/shard_map/ppermute | solution.py:525
  100.4 1.6 collective-permute-start.39
  102.0 2.0 %collective-permute-done.39.refs_1_ = f32[8,128]{1,0:T(8,128)S(1)} collective-permute-done((f32[8,128]{1,0:T(8,128)S(1)}, f32[8,128]{1,0:T(8,128)S(1)}, u32[]{:S(2)}, u32[]{:S(2)}) %collective-permute-start.39) | collective-permute-done | bytes 4128 | tf_op jit(solution)/shard_map/ppermute | solution.py:525
  104.0 2.6 %collective-permute-start.40 = (f32[8,128]{1,0:T(8,128)S(1)}, f32[8,128]{1,0:T(8,128)S(1)}, u32[]{:S(2)}, u32[]{:S(2)}) collective-permute-start(f32[8,128]{1,0:T(8,128)S(1)} %merge.1.refs_0_), channel_id=1, source_target_pairs={{0,8},{4,12},{8,0},{12,4},{1,9},{5,13},{9,1},{13,5},{2,10},{6,14},... | collective-permute-start | bytes 12296 | tf_op jit(solution)/shard_map/ppermute | solution.py:525
  106.6 1.9 %collective-permute-done.40.refs_1_ = f32[8,128]{1,0:T(8,128)S(1)} collective-permute-done((f32[8,128]{1,0:T(8,128)S(1)}, f32[8,128]{1,0:T(8,128)S(1)}, u32[]{:S(2)}, u32[]{:S(2)}) %collective-permute-start.40) | collective-permute-done | bytes 4128 | tf_op jit(solution)/shard_map/ppermute | solution.py:525
  109.7 1.3 collective-permute-start.41
  111.0 6.1 %collective-permute-done.42 = bf16[64,2048]{1,0:T(8,128)(2,1)S(1)} collective-permute-done((bf16[64,2048]{1,0:T(8,128)(2,1)S(1)}, bf16[64,2048]{1,0:T(8,128)(2,1)S(1)}, u32[]{:S(2)}, u32[]{:S(2)}) %collective-permute-start.42) | collective-permute-done | bytes 262176 | tf_op jit(solution)/shard_map/ppermute | solution.py:525
  118.7 3.4 %output.4 = (bf16[2,4,16,1024]{3,2,1,0:T(8,128)(2,1)S(1)}, bf16[2,4,16,1024]{3,2,1,0:T(8,128)(2,1)S(1)}) custom-call(s32[1]{0:T(128)} %bitcast.3.index_ref, bf16[4,16,2048]{2,1,0:T(8,128)(2,1)S(1)} %bitcast.47, bf16[4,16,2048]{2,1,0:T(8,128)(2,1)S(1)} %bitcast.49, bf16[4,16,2048]{2,1,0:T(8,128)(2,1)S(1)} %bitcast.51, bf16[4,16,2048]{2,1,0:T(8,128)(2,1)S(1)} %bitcast.53, ...), custom_call_target="tpu_custom_call" | custom-call | flops 1000 | bytes 1000 | tf_op jit(solution)/shard_map/output/pallas_call | solution.py:444
  122.4 1.6 collective-permute-start.47
  124.0 3.4 %output.5 = (bf16[2,4,16,1024]{3,2,1,0:T(8,128)(2,1)S(1)}, bf16[2,4,16,1024]{3,2,1,0:T(8,128)(2,1)S(1)}) custom-call(s32[1]{0:T(128)} %bitcast.3.index_ref, bf16[4,16,2048]{2,1,0:T(8,128)(2,1)S(1)} %bitcast.48, bf16[4,16,2048]{2,1,0:T(8,128)(2,1)S(1)} %bitcast.50, bf16[4,16,2048]{2,1,0:T(8,128)(2,1)S(1)} %bitcast.52, bf16[4,16,2048]{2,1,0:T(8,128)(2,1)S(1)} %bitcast.54, ...), custom_call_target="tpu_custom_call" | custom-call | flops 1000 | bytes 1000 | tf_op jit(solution)/shard_map/output/pallas_call | solution.py:444
  127.9 3.5 %output.6 = (bf16[2,4,16,1024]{3,2,1,0:T(8,128)(2,1)S(1)}, bf16[2,4,16,1024]{3,2,1,0:T(8,128)(2,1)S(1)}) custom-call(s32[1]{0:T(128)} %bitcast.3.index_ref, bf16[4,16,2176]{2,1,0:T(8,128)(2,1)S(1)} %bitcast.41, bf16[4,16,2176]{2,1,0:T(8,128)(2,1)S(1)} %bitcast.39, bf16[4,16,2176]{2,1,0:T(8,128)(2,1)S(1)} %bitcast.43, bf16[4,16,2176]{2,1,0:T(8,128)(2,1)S(1)} %bitcast.45, ...), custom_call_target="tpu_custom_call" | custom-call | flops 1000 | bytes 1000 | tf_op jit(solution)/shard_map/output/pallas_call | solution.py:444
  131.6 2.7 %collective-permute-start.51 = (bf16[1,4,16,1024]{3,2,1,0:T(8,128)(2,1)S(1)}, bf16[1,4,16,1024]{3,2,1,0:T(8,128)(2,1)S(1)}, u32[]{:S(2)}, u32[]{:S(2)}) collective-permute-start(bf16[1,4,16,1024]{3,2,1,0:T(8,128)(2,1)S(1)} %fold.22.refs_5_), channel_id=1, source_target_pairs={{0,8},{4,12},{8,0},{12,4},{1,9},{5,13},{9,1},{13,5},{2,10},{6,14},... | collective-permute-start | bytes 393224 | tf_op jit(solution)/shard_map/ppermute | solution.py:525
  134.4 1.6 collective-permute-start.48
  135.9 3.5 %output.7 = (bf16[2,4,16,1024]{3,2,1,0:T(8,128)(2,1)S(1)}, bf16[2,4,16,1024]{3,2,1,0:T(8,128)(2,1)S(1)}) custom-call(s32[1]{0:T(128)} %bitcast.3.index_ref, bf16[4,16,2176]{2,1,0:T(8,128)(2,1)S(1)} %bitcast.42, bf16[4,16,2176]{2,1,0:T(8,128)(2,1)S(1)} %bitcast.40, bf16[4,16,2176]{2,1,0:T(8,128)(2,1)S(1)} %bitcast.44, bf16[4,16,2176]{2,1,0:T(8,128)(2,1)S(1)} %bitcast.46, ...), custom_call_target="tpu_custom_call" | custom-call | flops 1000 | bytes 1000 | tf_op jit(solution)/shard_map/output/pallas_call | solution.py:444
  139.9 2.6 %collective-permute-start.52 = (bf16[2,4,16,1024]{3,2,1,0:T(8,128)(2,1)S(1)}, bf16[2,4,16,1024]{3,2,1,0:T(8,128)(2,1)S(1)}, u32[]{:S(2)}, u32[]{:S(2)}) collective-permute-start(bf16[2,4,16,1024]{3,2,1,0:T(8,128)(2,1)S(1)} %tie.25), channel_id=1, source_target_pairs={{0,4},{4,0},{8,12},{12,8},{1,5},{5,1},{9,13},{13,9},{2,6},{6,2},{1... | collective-permute-start | bytes 786440 | tf_op jit(solution)/shard_map/ppermute | solution.py:525
  142.8 2.4 %collective-permute-start.54 = (bf16[1,4,16,1024]{3,2,1,0:T(8,128)(2,1)S(1)}, bf16[1,4,16,1024]{3,2,1,0:T(8,128)(2,1)S(1)}, u32[]{:S(2)}, u32[]{:S(2)}) collective-permute-start(bf16[1,4,16,1024]{3,2,1,0:T(8,128)(2,1)S(1)} %fold.23.refs_2_), channel_id=1, source_target_pairs={{0,8},{4,12},{8,0},{12,4},{1,9},{5,13},{9,1},{13,5},{2,10},{6,14},... | collective-permute-start | bytes 393224 | tf_op jit(solution)/shard_map/ppermute | solution.py:525
  145.2 1.8 %collective-permute-done.48.refs_1_ = bf16[2,4,16,1024]{3,2,1,0:T(8,128)(2,1)S(1)} collective-permute-done((bf16[2,4,16,1024]{3,2,1,0:T(8,128)(2,1)S(1)}, bf16[2,4,16,1024]{3,2,1,0:T(8,128)(2,1)S(1)}, u32[]{:S(2)}, u32[]{:S(2)}) %collective-permute-start.48) | collective-permute-done | bytes 262176 | tf_op jit(solution)/shard_map/ppermute | solution.py:525
  147.1 3.2 %collective-permute-start.50 = (bf16[1,4,16,1024]{3,2,1,0:T(8,128)(2,1)S(1)}, bf16[1,4,16,1024]{3,2,1,0:T(8,128)(2,1)S(1)}, u32[]{:S(2)}, u32[]{:S(2)}) collective-permute-start(bf16[1,4,16,1024]{3,2,1,0:T(8,128)(2,1)S(1)} %fold.24.refs_3_), channel_id=1, source_target_pairs={{0,8},{4,12},{8,0},{12,4},{1,9},{5,13},{9,1},{13,5},{2,10},{6,14},... | collective-permute-start | bytes 393224 | tf_op jit(solution)/shard_map/ppermute | solution.py:525
  150.3 2.2 %close.3 = (bf16[8,16,2048]{2,1,0:T(8,128)(2,1)}, f32[8,128]{1,0:T(8,128)S(1)}) custom-call(s32[2]{0:T(128)S(1)} %pad_add_fusion.1.at_ref, bf16[32,16,2048]{2,1,0:T(8,128)(2,1)} %bitcast.77, bf16[2,4,16,1024]{3,2,1,0:T(8,128)(2,1)S(1)} %get-tuple-element.108.refs_1_.refs_5_.refs_0_, bf16[2,4,16,1024]{3,2,1,0:T(8,128)(2,1)S(1)} %collective-permute-done.47.refs_1_, ...), custom_call_target="tpu_custom_call" | custom-call | flops 1000 | bytes 1000 | tf_op jit(solution)/shard_map/close/pallas_call | solution.py:490
  152.5 3.3 %collective-permute-done.52.refs_1_.refs_4_ = bf16[2,4,16,1024]{3,2,1,0:T(8,128)(2,1)S(1)} collective-permute-done((bf16[2,4,16,1024]{3,2,1,0:T(8,128)(2,1)S(1)}, bf16[2,4,16,1024]{3,2,1,0:T(8,128)(2,1)S(1)}, u32[]{:S(2)}, u32[]{:S(2)}) %collective-permute-start.52) | collective-permute-done | bytes 262176 | tf_op jit(solution)/shard_map/ppermute | solution.py:525
  156.1 2.2 %close.4 = (bf16[8,16,2048]{2,1,0:T(8,128)(2,1)}, f32[8,128]{1,0:T(8,128)S(1)}) custom-call(s32[2]{0:T(128)S(1)} %pad_add_fusion.1.at_ref, bf16[32,16,2048]{2,1,0:T(8,128)(2,1)} %bitcast.78, bf16[2,4,16,1024]{3,2,1,0:T(8,128)(2,1)S(1)} %get-tuple-element.109.refs_5_.refs_0_, ...), custom_call_target="tpu_custom_call", output_to_operand_aliasing={{0}: (5, {})} | custom-call | flops 1000 | bytes 1000 | tf_op jit(solution)/shard_map/close/pallas_call | solution.py:490
  158.3 3.8 %collective-permute-done.50.refs_2_ = bf16[1,4,16,1024]{3,2,1,0:T(8,128)(2,1)S(1)} collective-permute-done((bf16[1,4,16,1024]{3,2,1,0:T(8,128)(2,1)S(1)}, bf16[1,4,16,1024]{3,2,1,0:T(8,128)(2,1)S(1)}, u32[]{:S(2)}, u32[]{:S(2)}) %collective-permute-start.50) | collective-permute-done | bytes 131104 | tf_op jit(solution)/shard_map/ppermute | solution.py:525
  162.0 2.4 %collective-permute-done.53.refs_5_ = bf16[1,4,16,1024]{3,2,1,0:T(8,128)(2,1)S(1)} collective-permute-done((bf16[1,4,16,1024]{3,2,1,0:T(8,128)(2,1)S(1)}, bf16[1,4,16,1024]{3,2,1,0:T(8,128)(2,1)S(1)}, u32[]{:S(2)}, u32[]{:S(2)}) %collective-permute-start.53) | collective-permute-done | bytes 131104 | tf_op jit(solution)/shard_map/ppermute | solution.py:525
  164.5 2.3 %close.5 = (bf16[8,16,2048]{2,1,0:T(8,128)(2,1)}, f32[8,128]{1,0:T(8,128)}) custom-call(s32[2]{0:T(128)S(1)} %pad_add_fusion.at_ref, bf16[32,16,2048]{2,1,0:T(8,128)(2,1)} %bitcast.79, bf16[2,4,16,1024]{3,2,1,0:T(8,128)(2,1)S(1)} %get-tuple-element.110.refs_2_.refs_0_, ...), custom_call_target="tpu_custom_call", output_to_operand_aliasing={{0}: (8, {})} | custom-call | flops 1000 | bytes 1000 | tf_op jit(solution)/shard_map/close/pallas_call | solution.py:490
  (137 shorter events, 20.7 us)
Async XLA Ops:
  5.5 9.4 %collective-permute-start = (bf16[1,4,128,256]{3,2,1,0:T(8,128)(2,1)S(1)}, bf16[1,4,128,256]{3,2,1,0:T(8,128)(2,1)S(1)}, u32[]{:S(2)}, u32[]{:S(2)}) collective-permute-start(bf16[1,4,128,256]{3,2,1,0:T(8,128)(2,1)S(1)} %get-tuple-element.66), channel_id=1, source_target_pairs={{0,1},{1,0},{2,3},{3,2},{4,5},{5,4},{6,7},{7,6},{8,9},{9,8},{10,11... | collective-permute-start | bytes 786440 | tf_op jit(solution)/shard_map/ppermute | solution.py:525
  6.1 8.8 %collective-permute-start.1 = (bf16[1,4,128,256]{3,2,1,0:T(8,128)(2,1)S(1)}, bf16[1,4,128,256]{3,2,1,0:T(8,128)(2,1)S(1)}, u32[]{:S(2)}, u32[]{:S(2)}) collective-permute-start(bf16[1,4,128,256]{3,2,1,0:T(8,128)(2,1)S(1)} %get-tuple-element.67), channel_id=1, source_target_pairs={{0,1},{1,0},{2,3},{3,2},{4,5},{5,4},{6,7},{7,6},{8,9},{9,8},{10,11... | collective-permute-start | bytes 786440 | tf_op jit(solution)/shard_map/ppermute | solution.py:525
  14.9 12.6 %collective-permute-start.3 = (bf16[1,4,128,512]{3,2,1,0:T(8,128)(2,1)S(1)}, bf16[1,4,128,512]{3,2,1,0:T(8,128)(2,1)S(1)}, u32[]{:S(2)}, u32[]{:S(2)}) collective-permute-start(bf16[1,4,128,512]{3,2,1,0:T(8,128)(2,1)S(1)} %tie.14), channel_id=1, source_target_pairs={{0,1},{1,0},{2,3},{3,2},{4,5},{5,4},{6,7},{7,6},{8,9},{9,8},{10,11... | collective-permute-start | bytes 1572872 | tf_op jit(solution)/shard_map/ppermute | solution.py:525
  15.4 12.1 %collective-permute-start.2 = (bf16[1,4,128,512]{3,2,1,0:T(8,128)(2,1)S(1)}, bf16[1,4,128,512]{3,2,1,0:T(8,128)(2,1)S(1)}, u32[]{:S(2)}, u32[]{:S(2)}) collective-permute-start(bf16[1,4,128,512]{3,2,1,0:T(8,128)(2,1)S(1)} %tie.13), channel_id=1, source_target_pairs={{0,1},{1,0},{2,3},{3,2},{4,5},{5,4},{6,7},{7,6},{8,9},{9,8},{10,11... | collective-permute-start | bytes 1572872 | tf_op jit(solution)/shard_map/ppermute | solution.py:525
  15.8 11.7 %collective-permute-start.4 = (bf16[1,4,128,256]{3,2,1,0:T(8,128)(2,1)S(1)}, bf16[1,4,128,256]{3,2,1,0:T(8,128)(2,1)S(1)}, u32[]{:S(2)}, u32[]{:S(2)}) collective-permute-start(bf16[1,4,128,256]{3,2,1,0:T(8,128)(2,1)S(1)} %fold.13.refs_8_), channel_id=1, source_target_pairs={{0,2},{1,3},{2,0},{3,1},{4,6},{5,7},{6,4},{7,5},{8,10},{9,11},{10,... | collective-permute-start | bytes 786440 | tf_op jit(solution)/shard_map/ppermute | solution.py:525
  27.5 9.8 %collective-permute-start.6 = (bf16[1,4,128,512]{3,2,1,0:T(8,128)(2,1)S(1)}, bf16[1,4,128,512]{3,2,1,0:T(8,128)(2,1)S(1)}, u32[]{:S(2)}, u32[]{:S(2)}) collective-permute-start(bf16[1,4,128,512]{3,2,1,0:T(8,128)(2,1)S(1)} %tie.16), channel_id=1, source_target_pairs={{0,1},{1,0},{2,3},{3,2},{4,5},{5,4},{6,7},{7,6},{8,9},{9,8},{10,11... | collective-permute-start | bytes 1572872 | tf_op jit(solution)/shard_map/ppermute | solution.py:525
  27.6 9.7 %collective-permute-start.5 = (bf16[1,4,128,512]{3,2,1,0:T(8,128)(2,1)S(1)}, bf16[1,4,128,512]{3,2,1,0:T(8,128)(2,1)S(1)}, u32[]{:S(2)}, u32[]{:S(2)}) collective-permute-start(bf16[1,4,128,512]{3,2,1,0:T(8,128)(2,1)S(1)} %tie.15), channel_id=1, source_target_pairs={{0,1},{1,0},{2,3},{3,2},{4,5},{5,4},{6,7},{7,6},{8,9},{9,8},{10,11... | collective-permute-start | bytes 1572872 | tf_op jit(solution)/shard_map/ppermute | solution.py:525
  28.4 14.0 %collective-permute-start.8 = (bf16[1,4,128,512]{3,2,1,0:T(8,128)(2,1)S(1)}, bf16[1,4,128,512]{3,2,1,0:T(8,128)(2,1)S(1)}, u32[]{:S(2)}, u32[]{:S(2)}) collective-permute-start(bf16[1,4,128,512]{3,2,1,0:T(8,128)(2,1)S(1)} %fold.14.refs_8_), channel_id=1, source_target_pairs={{0,2},{1,3},{2,0},{3,1},{4,6},{5,7},{6,4},{7,5},{8,10},{9,11},{10,... | collective-permute-start | bytes 1572872 | tf_op jit(solution)/shard_map/ppermute | solution.py:525
  37.3 5.9 %collective-permute-start.7 = (bf16[1,4,128,512]{3,2,1,0:T(8,128)(2,1)S(1)}, bf16[1,4,128,512]{3,2,1,0:T(8,128)(2,1)S(1)}, u32[]{:S(2)}, u32[]{:S(2)}) collective-permute-start(bf16[1,4,128,512]{3,2,1,0:T(8,128)(2,1)S(1)} %tie.17), channel_id=1, source_target_pairs={{0,1},{1,0},{2,3},{3,2},{4,5},{5,4},{6,7},{7,6},{8,9},{9,8},{10,11... | collective-permute-start | bytes 1572872 | tf_op jit(solution)/shard_map/ppermute | solution.py:525
  38.1 14.7 %collective-permute-start.9 = (bf16[1,4,128,512]{3,2,1,0:T(8,128)(2,1)S(1)}, bf16[1,4,128,512]{3,2,1,0:T(8,128)(2,1)S(1)}, u32[]{:S(2)}, u32[]{:S(2)}) collective-permute-start(bf16[1,4,128,512]{3,2,1,0:T(8,128)(2,1)S(1)} %tie.18), channel_id=1, source_target_pairs={{0,1},{1,0},{2,3},{3,2},{4,5},{5,4},{6,7},{7,6},{8,9},{9,8},{10,11... | collective-permute-start | bytes 1572872 | tf_op jit(solution)/shard_map/ppermute | solution.py:525
  39.1 19.4 %collective-permute-start.12 = (bf16[1,4,128,512]{3,2,1,0:T(8,128)(2,1)}, bf16[1,4,128,512]{3,2,1,0:T(8,128)(2,1)}, u32[]{:S(2)}, u32[]{:S(2)}) collective-permute-start(bf16[1,4,128,512]{3,2,1,0:T(8,128)(2,1)} %fold.15.refs_6_), channel_id=1, source_target_pairs={{0,2},{1,3},{2,0},{3,1},{4,6},{5,7},{6,4},{7,5},{8,10},{9,11},{10,... | collective-permute-start | bytes 1572872 | tf_op jit(solution)/shard_map/ppermute | solution.py:525
  42.9 15.5 %collective-permute-start.18 = (bf16[128,768]{1,0:T(8,128)(2,1)S(1)}, bf16[128,768]{1,0:T(8,128)(2,1)S(1)}, u32[]{:S(2)}, u32[]{:S(2)}) collective-permute-start(bf16[128,768]{1,0:T(8,128)(2,1)S(1)} %get-tuple-element.74.refs_2_.refs_0_.q_ref), channel_id=1, source_target_pairs={{0,2},{1,3},{2,0},{3,1},{4,6},{5,7},{6,4},{7,5},{8,10},{9,11},{10,... | collective-permute-start | bytes 589832 | tf_op jit(solution)/shard_map/ppermute | solution.py:525
  44.2 29.3 %collective-permute-start.17 = (bf16[1,4,128,512]{3,2,1,0:T(8,128)(2,1)}, bf16[1,4,128,512]{3,2,1,0:T(8,128)(2,1)}, u32[]{:S(2)}, u32[]{:S(2)}) collective-permute-start(bf16[1,4,128,512]{3,2,1,0:T(8,128)(2,1)} %fold.16.refs_8_), channel_id=1, source_target_pairs={{0,2},{1,3},{2,0},{3,1},{4,6},{5,7},{6,4},{7,5},{8,10},{9,11},{10,... | collective-permute-start | bytes 1572872 | tf_op jit(solution)/shard_map/ppermute | solution.py:525
  52.8 8.1 %collective-permute-start.11 = (bf16[1,4,128,256]{3,2,1,0:T(8,128)(2,1)}, bf16[1,4,128,256]{3,2,1,0:T(8,128)(2,1)}, u32[]{:S(2)}, u32[]{:S(2)}) collective-permute-start(bf16[1,4,128,256]{3,2,1,0:T(8,128)(2,1)} %tie.20), channel_id=1, source_target_pairs={{0,1},{1,0},{2,3},{3,2},{4,5},{5,4},{6,7},{7,6},{8,9},{9,8},{10,11... | collective-permute-start | bytes 786440 | tf_op jit(solution)/shard_map/ppermute | solution.py:525
  52.8 9.2 %collective-permute-start.19 = (bf16[128,768]{1,0:T(8,128)(2,1)S(1)}, bf16[128,768]{1,0:T(8,128)(2,1)}, u32[]{:S(2)}, u32[]{:S(2)}) collective-permute-start(bf16[128,768]{1,0:T(8,128)(2,1)S(1)} %get-tuple-element.74.refs_2_.refs_0_.q_ref), channel_id=1, source_target_pairs={{0,1},{1,0},{2,3},{3,2},{4,5},{5,4},{6,7},{7,6},{8,9},{9,8},{10,11... | collective-permute-start | bytes 589832 | tf_op jit(solution)/shard_map/ppermute | solution.py:525
  58.4 3.7 %collective-permute-start.20 = (bf16[128,768]{1,0:T(8,128)(2,1)S(1)}, bf16[128,768]{1,0:T(8,128)(2,1)}, u32[]{:S(2)}, u32[]{:S(2)}) collective-permute-start(bf16[128,768]{1,0:T(8,128)(2,1)S(1)} %collective-permute-done.18.refs_1_), channel_id=1, source_target_pairs={{0,1},{1,0},{2,3},{3,2},{4,5},{5,4},{6,7},{7,6},{8,9},{9,8},{10,11... | collective-permute-start | bytes 589832 | tf_op jit(solution)/shard_map/ppermute | solution.py:525
  66.2 6.7 %collective-permute-start.21 = (bf16[1,128,768]{2,1,0:T(8,128)(2,1)S(1)}, bf16[1,128,768]{2,1,0:T(8,128)(2,1)S(1)}, u32[]{:S(2)}, u32[]{:S(2)}) collective-permute-start(bf16[1,128,768]{2,1,0:T(8,128)(2,1)S(1)} %get-tuple-element.81), channel_id=1, source_target_pairs={{0,1},{1,0},{2,3},{3,2},{4,5},{5,4},{6,7},{7,6},{8,9},{9,8},{10,11... | collective-permute-start | bytes 589832 | tf_op jit(solution)/shard_map/ppermute | solution.py:525
  66.7 6.1 %collective-permute-start.14 = (bf16[128,512]{1,0:T(8,128)(2,1)S(1)}, bf16[128,512]{1,0:T(8,128)(2,1)S(1)}, u32[]{:S(2)}, u32[]{:S(2)}) collective-permute-start(bf16[128,512]{1,0:T(8,128)(2,1)S(1)} %get-tuple-element.79.refs_2_.refs_0_.q_ref), channel_id=1, source_target_pairs={{0,2},{1,3},{2,0},{3,1},{4,6},{5,7},{6,4},{7,5},{8,10},{9,11},{10,... | collective-permute-start | bytes 393224 | tf_op jit(solution)/shard_map/ppermute | solution.py:525
  68.5 12.3 %collective-permute-start.10 = (bf16[1,4,128,256]{3,2,1,0:T(8,128)(2,1)S(1)}, bf16[1,4,128,256]{3,2,1,0:T(8,128)(2,1)S(1)}, u32[]{:S(2)}, u32[]{:S(2)}) collective-permute-start(bf16[1,4,128,256]{3,2,1,0:T(8,128)(2,1)S(1)} %tie.19), channel_id=1, source_target_pairs={{0,1},{1,0},{2,3},{3,2},{4,5},{5,4},{6,7},{7,6},{8,9},{9,8},{10,11... | collective-permute-start | bytes 786440 | tf_op jit(solution)/shard_map/ppermute | solution.py:525
  68.5 12.3 %collective-permute-start.13 = (bf16[1,4,128,256]{3,2,1,0:T(8,128)(2,1)S(1)}, bf16[1,4,128,256]{3,2,1,0:T(8,128)(2,1)S(1)}, u32[]{:S(2)}, u32[]{:S(2)}) collective-permute-start(bf16[1,4,128,256]{3,2,1,0:T(8,128)(2,1)S(1)} %fold.17.refs_10_), channel_id=1, source_target_pairs={{0,2},{1,3},{2,0},{3,1},{4,6},{5,7},{6,4},{7,5},{8,10},{9,11},{10,... | collective-permute-start | bytes 786440 | tf_op jit(solution)/shard_map/ppermute | solution.py:525
  72.8 4.2 %collective-permute-start.15 = (bf16[128,512]{1,0:T(8,128)(2,1)S(1)}, bf16[128,512]{1,0:T(8,128)(2,1)S(1)}, u32[]{:S(2)}, u32[]{:S(2)}) collective-permute-start(bf16[128,512]{1,0:T(8,128)(2,1)S(1)} %get-tuple-element.79.refs_2_.refs_0_.q_ref), channel_id=1, source_target_pairs={{0,1},{1,0},{2,3},{3,2},{4,5},{5,4},{6,7},{7,6},{8,9},{9,8},{10,11... | collective-permute-start | bytes 393224 | tf_op jit(solution)/shard_map/ppermute | solution.py:525
  72.9 4.2 %collective-permute-start.16 = (bf16[128,512]{1,0:T(8,128)(2,1)S(1)}, bf16[128,512]{1,0:T(8,128)(2,1)S(1)}, u32[]{:S(2)}, u32[]{:S(2)}) collective-permute-start(bf16[128,512]{1,0:T(8,128)(2,1)S(1)} %collective-permute-done.14.refs_1_), channel_id=1, source_target_pairs={{0,1},{1,0},{2,3},{3,2},{4,5},{5,4},{6,7},{7,6},{8,9},{9,8},{10,11... | collective-permute-start | bytes 393224 | tf_op jit(solution)/shard_map/ppermute | solution.py:525
  74.9 5.8 %collective-permute-start.25 = (bf16[128,512]{1,0:T(8,128)(2,1)S(1)}, bf16[128,512]{1,0:T(8,128)(2,1)S(1)}, u32[]{:S(2)}, u32[]{:S(2)}) collective-permute-start(bf16[128,512]{1,0:T(8,128)(2,1)S(1)} %get-tuple-element.82.refs_10_.refs_0_.q_ref), channel_id=1, source_target_pairs={{0,2},{1,3},{2,0},{3,1},{4,6},{5,7},{6,4},{7,5},{8,10},{9,11},{10,... | collective-permute-start | bytes 393224 | tf_op jit(solution)/shard_map/ppermute | solution.py:525
  81.0 5.6 %collective-permute-start.22 = (bf16[128,256]{1,0:T(8,128)(2,1)S(1)}, bf16[128,256]{1,0:T(8,128)(2,1)S(1)}, u32[]{:S(2)}, u32[]{:S(2)}) collective-permute-start(bf16[128,256]{1,0:T(8,128)(2,1)S(1)} %get-tuple-element.84.refs_2_.refs_0_.q_ref), channel_id=1, source_target_pairs={{0,2},{1,3},{2,0},{3,1},{4,6},{5,7},{6,4},{7,5},{8,10},{9,11},{10,... | collective-permute-start | bytes 196616 | tf_op jit(solution)/shard_map/ppermute | solution.py:525
  82.7 9.7 %collective-permute-start.31 = (bf16[1,128,768]{2,1,0:T(8,128)(2,1)S(1)}, bf16[1,128,768]{2,1,0:T(8,128)(2,1)S(1)}, u32[]{:S(2)}, u32[]{:S(2)}) collective-permute-start(bf16[1,128,768]{2,1,0:T(8,128)(2,1)S(1)} %get-tuple-element.92), channel_id=1, source_target_pairs={{0,1},{1,0},{2,3},{3,2},{4,5},{5,4},{6,7},{7,6},{8,9},{9,8},{10,11... | collective-permute-start | bytes 589832 | tf_op jit(solution)/shard_map/ppermute | solution.py:525
  82.9 10.1 %collective-permute-start.32 = (bf16[1,128,768]{2,1,0:T(8,128)(2,1)S(1)}, bf16[1,128,768]{2,1,0:T(8,128)(2,1)S(1)}, u32[]{:S(2)}, u32[]{:S(2)}) collective-permute-start(bf16[1,128,768]{2,1,0:T(8,128)(2,1)S(1)} %fold.18.refs_3_), channel_id=1, source_target_pairs={{0,2},{1,3},{2,0},{3,1},{4,6},{5,7},{6,4},{7,5},{8,10},{9,11},{10,... | collective-permute-start | bytes 589832 | tf_op jit(solution)/shard_map/ppermute | solution.py:525
  86.6 5.6 %collective-permute-start.33 = (bf16[1,128,512]{2,1,0:T(8,128)(2,1)S(1)}, bf16[1,128,512]{2,1,0:T(8,128)(2,1)S(1)}, u32[]{:S(2)}, u32[]{:S(2)}) collective-permute-start(bf16[1,128,512]{2,1,0:T(8,128)(2,1)S(1)} %tie.21), channel_id=1, source_target_pairs={{0,1},{1,0},{2,3},{3,2},{4,5},{5,4},{6,7},{7,6},{8,9},{9,8},{10,11... | collective-permute-start | bytes 393224 | tf_op jit(solution)/shard_map/ppermute | solution.py:525
  88.1 6.2 %collective-permute-start.35 = (bf16[1,128,512]{2,1,0:T(8,128)(2,1)S(1)}, bf16[1,128,512]{2,1,0:T(8,128)(2,1)S(1)}, u32[]{:S(2)}, u32[]{:S(2)}) collective-permute-start(bf16[1,128,512]{2,1,0:T(8,128)(2,1)S(1)} %get-tuple-element.97), channel_id=1, source_target_pairs={{0,1},{1,0},{2,3},{3,2},{4,5},{5,4},{6,7},{7,6},{8,9},{9,8},{10,11... | collective-permute-start | bytes 393224 | tf_op jit(solution)/shard_map/ppermute | solution.py:525
  88.5 7.6 %collective-permute-start.36 = (bf16[1,128,512]{2,1,0:T(8,128)(2,1)S(1)}, bf16[1,128,512]{2,1,0:T(8,128)(2,1)S(1)}, u32[]{:S(2)}, u32[]{:S(2)}) collective-permute-start(bf16[1,128,512]{2,1,0:T(8,128)(2,1)S(1)} %fold.19.refs_10_), channel_id=1, source_target_pairs={{0,2},{1,3},{2,0},{3,1},{4,6},{5,7},{6,4},{7,5},{8,10},{9,11},{10,... | collective-permute-start | bytes 393224 | tf_op jit(solution)/shard_map/ppermute | solution.py:525
  92.4 4.1 %collective-permute-start.37 = (bf16[1,128,512]{2,1,0:T(8,128)(2,1)S(1)}, bf16[1,128,512]{2,1,0:T(8,128)(2,1)S(1)}, u32[]{:S(2)}, u32[]{:S(2)}) collective-permute-start(bf16[1,128,512]{2,1,0:T(8,128)(2,1)S(1)} %tie.22), channel_id=1, source_target_pairs={{0,1},{1,0},{2,3},{3,2},{4,5},{5,4},{6,7},{7,6},{8,9},{9,8},{10,11... | collective-permute-start | bytes 393224 | tf_op jit(solution)/shard_map/ppermute | solution.py:525
  93.0 6.2 %collective-permute-start.38 = (bf16[1,128,512]{2,1,0:T(8,128)(2,1)S(1)}, bf16[1,128,512]{2,1,0:T(8,128)(2,1)S(1)}, u32[]{:S(2)}, u32[]{:S(2)}) collective-permute-start(bf16[1,128,512]{2,1,0:T(8,128)(2,1)S(1)} %fold.20.refs_3_), channel_id=1, source_target_pairs={{0,2},{1,3},{2,0},{3,1},{4,6},{5,7},{6,4},{7,5},{8,10},{9,11},{10,... | collective-permute-start | bytes 393224 | tf_op jit(solution)/shard_map/ppermute | solution.py:525
  93.9 5.7 %collective-permute-start.29 = (bf16[1,128,256]{2,1,0:T(8,128)(2,1)S(1)}, bf16[1,128,256]{2,1,0:T(8,128)(2,1)S(1)}, u32[]{:S(2)}, u32[]{:S(2)}) collective-permute-start(bf16[1,128,256]{2,1,0:T(8,128)(2,1)S(1)} %get-tuple-element.89), channel_id=1, source_target_pairs={{0,1},{1,0},{2,3},{3,2},{4,5},{5,4},{6,7},{7,6},{8,9},{9,8},{10,11... | collective-permute-start | bytes 196616 | tf_op jit(solution)/shard_map/ppermute | solution.py:525
  94.4 5.5 %collective-permute-start.34 = (bf16[1,128,256]{2,1,0:T(8,128)(2,1)S(1)}, bf16[1,128,256]{2,1,0:T(8,128)(2,1)S(1)}, u32[]{:S(2)}, u32[]{:S(2)}) collective-permute-start(bf16[1,128,256]{2,1,0:T(8,128)(2,1)S(1)} %fold.21.refs_3_), channel_id=1, source_target_pairs={{0,2},{1,3},{2,0},{3,1},{4,6},{5,7},{6,4},{7,5},{8,10},{9,11},{10,... | collective-permute-start | bytes 196616 | tf_op jit(solution)/shard_map/ppermute | solution.py:525
  100.4 3.6 %collective-permute-start.39 = (f32[8,128]{1,0:T(8,128)S(1)}, f32[8,128]{1,0:T(8,128)S(1)}, u32[]{:S(2)}, u32[]{:S(2)}) collective-permute-start(f32[8,128]{1,0:T(8,128)S(1)} %get-tuple-element.104.refs_0_), channel_id=1, source_target_pairs={{0,4},{4,0},{8,12},{12,8},{1,5},{5,1},{9,13},{13,9},{2,6},{6,2},{1... | collective-permute-start | bytes 12296 | tf_op jit(solution)/shard_map/ppermute | solution.py:525
  104.0 4.5 %collective-permute-start.40 = (f32[8,128]{1,0:T(8,128)S(1)}, f32[8,128]{1,0:T(8,128)S(1)}, u32[]{:S(2)}, u32[]{:S(2)}) collective-permute-start(f32[8,128]{1,0:T(8,128)S(1)} %merge.1.refs_0_), channel_id=1, source_target_pairs={{0,8},{4,12},{8,0},{12,4},{1,9},{5,13},{9,1},{13,5},{2,10},{6,14},... | collective-permute-start | bytes 12296 | tf_op jit(solution)/shard_map/ppermute | solution.py:525
  108.9 8.2 %collective-permute-start.42 = (bf16[64,2048]{1,0:T(8,128)(2,1)S(1)}, bf16[64,2048]{1,0:T(8,128)(2,1)S(1)}, u32[]{:S(2)}, u32[]{:S(2)}) collective-permute-start(bf16[64,2048]{1,0:T(8,128)(2,1)S(1)} %get-tuple-element.107), channel_id=1, source_target_pairs={{0,2},{1,3},{2,0},{3,1},{4,6},{5,7},{6,4},{7,5},{8,10},{9,11},{10,... | collective-permute-start | bytes 786440 | tf_op jit(solution)/shard_map/ppermute | solution.py:525
  109.7 12.5 %collective-permute-start.41 = (bf16[64,2176]{1,0:T(8,128)(2,1)S(1)}, bf16[64,2176]{1,0:T(8,128)(2,1)S(1)}, u32[]{:S(2)}, u32[]{:S(2)}) collective-permute-start(bf16[64,2176]{1,0:T(8,128)(2,1)S(1)} %get-tuple-element.106), channel_id=1, source_target_pairs={{0,2},{1,3},{2,0},{3,1},{4,6},{5,7},{6,4},{7,5},{8,10},{9,11},{10,... | collective-permute-start | bytes 835592 | tf_op jit(solution)/shard_map/ppermute | solution.py:525
  111.0 6.7 %collective-permute-start.43 = (bf16[64,2048]{1,0:T(8,128)(2,1)S(1)}, bf16[64,2048]{1,0:T(8,128)(2,1)S(1)}, u32[]{:S(2)}, u32[]{:S(2)}) collective-permute-start(bf16[64,2048]{1,0:T(8,128)(2,1)S(1)} %get-tuple-element.107), channel_id=1, source_target_pairs={{0,1},{1,0},{2,3},{3,2},{4,5},{5,4},{6,7},{7,6},{8,9},{9,8},{10,11... | collective-permute-start | bytes 786440 | tf_op jit(solution)/shard_map/ppermute | solution.py:525
  117.2 10.7 %collective-permute-start.45 = (bf16[64,2176]{1,0:T(8,128)(2,1)S(1)}, bf16[64,2176]{1,0:T(8,128)(2,1)S(1)}, u32[]{:S(2)}, u32[]{:S(2)}) collective-permute-start(bf16[64,2176]{1,0:T(8,128)(2,1)S(1)} %get-tuple-element.106), channel_id=1, source_target_pairs={{0,1},{1,0},{2,3},{3,2},{4,5},{5,4},{6,7},{7,6},{8,9},{9,8},{10,11... | collective-permute-start | bytes 835592 | tf_op jit(solution)/shard_map/ppermute | solution.py:525
  122.2 5.8 %collective-permute-start.46 = (bf16[64,2176]{1,0:T(8,128)(2,1)S(1)}, bf16[64,2176]{1,0:T(8,128)(2,1)S(1)}, u32[]{:S(2)}, u32[]{:S(2)}) collective-permute-start(bf16[64,2176]{1,0:T(8,128)(2,1)S(1)} %tie.23), channel_id=1, source_target_pairs={{0,1},{1,0},{2,3},{3,2},{4,5},{5,4},{6,7},{7,6},{8,9},{9,8},{10,11... | collective-permute-start | bytes 835592 | tf_op jit(solution)/shard_map/ppermute | solution.py:525
  122.4 9.1 %collective-permute-start.47 = (bf16[2,4,16,1024]{3,2,1,0:T(8,128)(2,1)S(1)}, bf16[2,4,16,1024]{3,2,1,0:T(8,128)(2,1)S(1)}, u32[]{:S(2)}, u32[]{:S(2)}) collective-permute-start(bf16[2,4,16,1024]{3,2,1,0:T(8,128)(2,1)S(1)} %get-tuple-element.112), channel_id=1, source_target_pairs={{0,4},{4,0},{8,12},{12,8},{1,5},{5,1},{9,13},{13,9},{2,6},{6,2},{1... | collective-permute-start | bytes 786440 | tf_op jit(solution)/shard_map/ppermute | solution.py:525
  127.4 12.5 %collective-permute-start.49 = (bf16[2,4,16,1024]{3,2,1,0:T(8,128)(2,1)S(1)}, bf16[2,4,16,1024]{3,2,1,0:T(8,128)(2,1)S(1)}, u32[]{:S(2)}, u32[]{:S(2)}) collective-permute-start(bf16[2,4,16,1024]{3,2,1,0:T(8,128)(2,1)S(1)} %get-tuple-element.113), channel_id=1, source_target_pairs={{0,4},{4,0},{8,12},{12,8},{1,5},{5,1},{9,13},{13,9},{2,6},{6,2},{1... | collective-permute-start | bytes 786440 | tf_op jit(solution)/shard_map/ppermute | solution.py:525
  131.6 8.3 %collective-permute-start.51 = (bf16[1,4,16,1024]{3,2,1,0:T(8,128)(2,1)S(1)}, bf16[1,4,16,1024]{3,2,1,0:T(8,128)(2,1)S(1)}, u32[]{:S(2)}, u32[]{:S(2)}) collective-permute-start(bf16[1,4,16,1024]{3,2,1,0:T(8,128)(2,1)S(1)} %fold.22.refs_5_), channel_id=1, source_target_pairs={{0,8},{4,12},{8,0},{12,4},{1,9},{5,13},{9,1},{13,5},{2,10},{6,14},... | collective-permute-start | bytes 393224 | tf_op jit(solution)/shard_map/ppermute | solution.py:525
  134.4 12.6 %collective-permute-start.48 = (bf16[2,4,16,1024]{3,2,1,0:T(8,128)(2,1)S(1)}, bf16[2,4,16,1024]{3,2,1,0:T(8,128)(2,1)S(1)}, u32[]{:S(2)}, u32[]{:S(2)}) collective-permute-start(bf16[2,4,16,1024]{3,2,1,0:T(8,128)(2,1)S(1)} %tie.24), channel_id=1, source_target_pairs={{0,4},{4,0},{8,12},{12,8},{1,5},{5,1},{9,13},{13,9},{2,6},{6,2},{1... | collective-permute-start | bytes 786440 | tf_op jit(solution)/shard_map/ppermute | solution.py:525
  139.9 15.9 %collective-permute-start.52 = (bf16[2,4,16,1024]{3,2,1,0:T(8,128)(2,1)S(1)}, bf16[2,4,16,1024]{3,2,1,0:T(8,128)(2,1)S(1)}, u32[]{:S(2)}, u32[]{:S(2)}) collective-permute-start(bf16[2,4,16,1024]{3,2,1,0:T(8,128)(2,1)S(1)} %tie.25), channel_id=1, source_target_pairs={{0,4},{4,0},{8,12},{12,8},{1,5},{5,1},{9,13},{13,9},{2,6},{6,2},{1... | collective-permute-start | bytes 786440 | tf_op jit(solution)/shard_map/ppermute | solution.py:525
  142.8 13.3 %collective-permute-start.54 = (bf16[1,4,16,1024]{3,2,1,0:T(8,128)(2,1)S(1)}, bf16[1,4,16,1024]{3,2,1,0:T(8,128)(2,1)S(1)}, u32[]{:S(2)}, u32[]{:S(2)}) collective-permute-start(bf16[1,4,16,1024]{3,2,1,0:T(8,128)(2,1)S(1)} %fold.23.refs_2_), channel_id=1, source_target_pairs={{0,8},{4,12},{8,0},{12,4},{1,9},{5,13},{9,1},{13,5},{2,10},{6,14},... | collective-permute-start | bytes 393224 | tf_op jit(solution)/shard_map/ppermute | solution.py:525
  147.1 14.9 %collective-permute-start.50 = (bf16[1,4,16,1024]{3,2,1,0:T(8,128)(2,1)S(1)}, bf16[1,4,16,1024]{3,2,1,0:T(8,128)(2,1)S(1)}, u32[]{:S(2)}, u32[]{:S(2)}) collective-permute-start(bf16[1,4,16,1024]{3,2,1,0:T(8,128)(2,1)S(1)} %fold.24.refs_3_), channel_id=1, source_target_pairs={{0,8},{4,12},{8,0},{12,4},{1,9},{5,13},{9,1},{13,5},{2,10},{6,14},... | collective-permute-start | bytes 393224 | tf_op jit(solution)/shard_map/ppermute | solution.py:525
  155.9 8.5 %collective-permute-start.53 = (bf16[1,4,16,1024]{3,2,1,0:T(8,128)(2,1)S(1)}, bf16[1,4,16,1024]{3,2,1,0:T(8,128)(2,1)S(1)}, u32[]{:S(2)}, u32[]{:S(2)}) collective-permute-start(bf16[1,4,16,1024]{3,2,1,0:T(8,128)(2,1)S(1)} %fold.25.refs_4_), channel_id=1, source_target_pairs={{0,8},{4,12},{8,0},{12,4},{1,9},{5,13},{9,1},{13,5},{2,10},{6,14},... | collective-permute-start | bytes 393224 | tf_op jit(solution)/shard_map/ppermute | solution.py:525
  (17 other events, 80.3 us)

commit v19 on v18

--- a/solution.py
+++ b/solution.py
@@ -561,7 +561,9 @@
     if heads % 8:
         return [1] * heads
     unit = heads // 8
-    return [unit, 2 * unit, 2 * unit, 2 * unit, unit]
+    if unit % 2:
+        return [unit, 2 * unit, 2 * unit, 2 * unit, unit]
+    return [3 * unit // 2, 2 * unit, 2 * unit, 3 * unit // 2, unit]
 
 
 GROUPS = [[0, 1], [2], [3], [4]]

time: 167 us -> 176 us (1.054)
  waiting for transfers between devices: 37.3 us -> 43.9 us
  Pallas kernels: 81.5 us -> 85.5 us
  local copies, waits for them, and re-layouts: 2.4 us -> 0.03 us
    ppermute x55, waiting for transfers between devices: 37.3 us -> 43.9 us  [swap(): lax.ppermute(x, axis, [(i, i ^ 1 << bit) for i in range(lax.axis_size(axi...]
    pallas_call x4, Pallas kernels: 12.5 us -> 17.1 us  [attend(): pl.pallas_call(functools.partial(attend_kernel, owners, len(counts)), gri...]
    unnamed x20 -> x16, local copies, waits for them, and re-layouts: 2.4 us -> 0.03 us
  transfers between devices with their start and end apart: 55 -> 55, of which waited for: 16 -> 19; matrix products, arithmetic and copies ran while one was open for 0% -> 0% of each run, Pallas kernels for 44% -> 43%
where the time goes in v19:
time: 176 us; the launch traced here: 175 us
  Pallas kernels  85.5 us (49%)
  starting transfers between devices  44.9 us (26%)
  waiting for transfers between devices  43.9 us (25%)
    ppermute x55, starting transfers between devices, swap(): lax.ppermute(x, axis, [(i, i ^ 1 << bit) for i in range(lax.axis_size(axi...  44.9 us
    ppermute x55, waiting for transfers between devices, swap(): lax.ppermute(x, axis, [(i, i ^ 1 << bit) for i in range(lax.axis_size(axi...  43.9 us
    pallas_call x5, Pallas kernels, project(): pl.pallas_call(functools.partial(project_kernel, parts, owners, len(after...  37.9 us
    pallas_call x4, Pallas kernels, attend(): pl.pallas_call(functools.partial(attend_kernel, owners, len(counts)), gri...  17.1 us
    pallas_call x4, Pallas kernels, output(): pl.pallas_call(functools.partial(output_kernel, owners, slots, len(after)...  13.9 us
    pallas_call x3, Pallas kernels, close(): pl.pallas_call(functools.partial(close_kernel, [len(terms) for terms in g...  6.66 us
    pallas_call x13, Pallas kernels, fold(): pl.pallas_call(functools.partial(fold_kernel, len(terms)), grid=(steps,),...  4.1 us
  transfers between devices with their start and end apart: 55, of which 19 were waited for; matrix products, arithmetic and copies ran while one was open for 0% of the time, Pallas kernels for 43%

profile of v19, /device:TPU:0, one launch (start us, length us, event | category | flops | bytes accessed | tf_op | source)
XLA Modules:
  0.0 175.0 jit_solution(1385950919683724549)
XLA Ops:
  0.0 7.1 %project.5 = (bf16[2,4,128,384]{3,2,1,0:T(8,128)(2,1)S(1)}, bf16[1,4,128,384]{3,2,1,0:T(8,128)(2,1)S(1)}, bf16[1,4,128,384]{3,2,1,0:T(8,128)(2,1)S(1)}) custom-call(s32[1]{0:T(128)} %bitcast.at_ref, bf16[4,2,4,16,2048]{4,3,2,1,0:T(8,128)(2,1)} %bitcast.57, bf16[4,2,4,16,2048]{4,3,2,1,0:T(8,128)(2,1)} %bitcast.58, bf16[4,2,4,16,2048]{4,3,2,1,0:T(8,128)(2,1)} %bitcast.59, ...), custom_call_target="tpu_custom_call" | custom-call | flops 1000 | bytes 1000 | tf_op jit(solution)/shard_map/project/pallas_call | solution.py:80
  7.7 8.7 %project.6 = (bf16[2,4,128,512]{3,2,1,0:T(8,128)(2,1)S(1)}, bf16[1,4,128,512]{3,2,1,0:T(8,128)(2,1)S(1)}, bf16[1,4,128,512]{3,2,1,0:T(8,128)(2,1)S(1)}) custom-call(s32[1]{0:T(128)} %bitcast.at_ref, bf16[4,2,4,16,2048]{4,3,2,1,0:T(8,128)(2,1)} %bitcast.61, bf16[4,2,4,16,2048]{4,3,2,1,0:T(8,128)(2,1)} %bitcast.62, bf16[4,2,4,16,2048]{4,3,2,1,0:T(8,128)(2,1)} %bitcast.63, ...), custom_call_target="tpu_custom_call" | custom-call | flops 1000 | bytes 1000 | tf_op jit(solution)/shard_map/project/pallas_call | solution.py:80
  17.2 3.0 %collective-permute-start.4 = (bf16[1,4,128,384]{3,2,1,0:T(8,128)(2,1)S(1)}, bf16[1,4,128,384]{3,2,1,0:T(8,128)(2,1)S(1)}, u32[]{:S(2)}, u32[]{:S(2)}) collective-permute-start(bf16[1,4,128,384]{3,2,1,0:T(8,128)(2,1)S(1)} %fold.13.refs_8_), channel_id=1, source_target_pairs={{0,2},{1,3},{2,0},{3,1},{4,6},{5,7},{6,4},{7,5},{8,10},{9,11},{10,... | collective-permute-start | bytes 1179656 | tf_op jit(solution)/shard_map/ppermute | solution.py:525
  20.2 8.7 %project.7 = (bf16[2,4,128,512]{3,2,1,0:T(8,128)(2,1)S(1)}, bf16[1,4,128,512]{3,2,1,0:T(8,128)(2,1)S(1)}, bf16[1,4,128,512]{3,2,1,0:T(8,128)(2,1)S(1)}) custom-call(s32[1]{0:T(128)} %bitcast.at_ref, bf16[4,2,4,16,2048]{4,3,2,1,0:T(8,128)(2,1)} %bitcast.68, bf16[4,2,4,16,2048]{4,3,2,1,0:T(8,128)(2,1)} %bitcast.66, bf16[4,2,4,16,2048]{4,3,2,1,0:T(8,128)(2,1)} %bitcast.67, ...), custom_call_target="tpu_custom_call" | custom-call | flops 1000 | bytes 1000 | tf_op jit(solution)/shard_map/project/pallas_call | solution.py:80
  30.4 1.8 %collective-permute-start.8 = (bf16[1,4,128,512]{3,2,1,0:T(8,128)(2,1)S(1)}, bf16[1,4,128,512]{3,2,1,0:T(8,128)(2,1)S(1)}, u32[]{:S(2)}, u32[]{:S(2)}) collective-permute-start(bf16[1,4,128,512]{3,2,1,0:T(8,128)(2,1)S(1)} %fold.14.refs_8_), channel_id=1, source_target_pairs={{0,2},{1,3},{2,0},{3,1},{4,6},{5,7},{6,4},{7,5},{8,10},{9,11},{10,... | collective-permute-start | bytes 1572872 | tf_op jit(solution)/shard_map/ppermute | solution.py:525
  32.2 7.1 %project.8 = (bf16[2,4,128,384]{3,2,1,0:T(8,128)(2,1)S(1)}, bf16[1,4,128,384]{3,2,1,0:T(8,128)(2,1)S(1)}, bf16[1,4,128,384]{3,2,1,0:T(8,128)(2,1)S(1)}) custom-call(s32[1]{0:T(128)} %bitcast.at_ref, bf16[4,2,4,16,2048]{4,3,2,1,0:T(8,128)(2,1)} %bitcast.69, bf16[4,2,4,16,2048]{4,3,2,1,0:T(8,128)(2,1)} %bitcast.70, bf16[4,2,4,16,2048]{4,3,2,1,0:T(8,128)(2,1)} %bitcast.71, ...), custom_call_target="tpu_custom_call" | custom-call | flops 1000 | bytes 1000 | tf_op jit(solution)/shard_map/project/pallas_call | solution.py:80
  41.2 3.7 %collective-permute-done.8.refs_5_ = bf16[1,4,128,512]{3,2,1,0:T(8,128)(2,1)S(1)} collective-permute-done((bf16[1,4,128,512]{3,2,1,0:T(8,128)(2,1)S(1)}, bf16[1,4,128,512]{3,2,1,0:T(8,128)(2,1)S(1)}, u32[]{:S(2)}, u32[]{:S(2)}) %collective-permute-start.8) | collective-permute-done | bytes 524320 | tf_op jit(solution)/shard_map/ppermute | solution.py:525
  45.5 2.1 %collective-permute-start.18 = (bf16[128,896]{1,0:T(8,128)(2,1)S(1)}, bf16[128,896]{1,0:T(8,128)(2,1)}, u32[]{:S(2)}, u32[]{:S(2)}) collective-permute-start(bf16[128,896]{1,0:T(8,128)(2,1)S(1)} %get-tuple-element.74.refs_2_.refs_0_.q_ref), channel_id=1, source_target_pairs={{0,2},{1,3},{2,0},{3,1},{4,6},{5,7},{6,4},{7,5},{8,10},{9,11},{10,... | collective-permute-start | bytes 688136 | tf_op jit(solution)/shard_map/ppermute | solution.py:525
  48.6 6.2 %project.9 = (bf16[2,4,128,256]{3,2,1,0:T(8,128)(2,1)S(1)}, bf16[1,4,128,256]{3,2,1,0:T(8,128)(2,1)S(1)}, bf16[1,4,128,256]{3,2,1,0:T(8,128)(2,1)}) custom-call(s32[1]{0:T(128)} %bitcast.at_ref, bf16[4,2,4,16,2048]{4,3,2,1,0:T(8,128)(2,1)} %bitcast.73, bf16[4,2,4,16,2048]{4,3,2,1,0:T(8,128)(2,1)} %bitcast.74, bf16[4,2,4,16,2048]{4,3,2,1,0:T(8,128)(2,1)} %bitcast.75, ...), custom_call_target="tpu_custom_call" | custom-call | flops 1000 | bytes 1000 | tf_op jit(solution)/shard_map/project/pallas_call | solution.py:80
  55.3 5.3 %collective-permute-done.18.refs_1_ = bf16[128,896]{1,0:T(8,128)(2,1)} collective-permute-done((bf16[128,896]{1,0:T(8,128)(2,1)S(1)}, bf16[128,896]{1,0:T(8,128)(2,1)}, u32[]{:S(2)}, u32[]{:S(2)}) %collective-permute-start.18) | collective-permute-done | bytes 229408 | tf_op jit(solution)/shard_map/ppermute | solution.py:525
  60.7 1.7 collective-permute-start.17
  62.6 1.4 activate.5
  63.9 1.1 fold.17.refs_10_
  65.1 7.2 %attend.4 = (bf16[2,128,896]{2,1,0:T(8,128)(2,1)S(1)}, bf16[1,128,896]{2,1,0:T(8,128)(2,1)S(1)}, bf16[1,128,896]{2,1,0:T(8,128)(2,1)S(1)}) custom-call(s32[1]{0:T(128)} %bitcast.at_ref, bf16[128,896]{1,0:T(8,128)(2,1)S(1)} %get-tuple-element.74.refs_2_.refs_0_.q_ref, bf16[128,896]{1,0:T(8,128)(2,1)} %collective-permute-done.18.refs_1_, ...), custom_call_target="tpu_custom_call" | custom-call | flops 1000 | bytes 1000 | tf_op jit(solution)/shard_map/attend/pallas_call | solution.py:262
  72.9 1.7 collective-permute-start.13
  74.7 4.2 %collective-permute-done.14.refs_1_ = bf16[128,512]{1,0:T(8,128)(2,1)S(1)} collective-permute-done((bf16[128,512]{1,0:T(8,128)(2,1)S(1)}, bf16[128,512]{1,0:T(8,128)(2,1)S(1)}, u32[]{:S(2)}, u32[]{:S(2)}) %collective-permute-start.14) | collective-permute-done | bytes 131104 | tf_op jit(solution)/shard_map/ppermute | solution.py:525
  79.5 1.3 activate.6
  81.1 4.3 %attend.5 = (bf16[2,128,512]{2,1,0:T(8,128)(2,1)S(1)}, bf16[1,128,512]{2,1,0:T(8,128)(2,1)S(1)}, bf16[1,128,512]{2,1,0:T(8,128)(2,1)S(1)}) custom-call(s32[1]{0:T(128)} %bitcast.at_ref, bf16[128,512]{1,0:T(8,128)(2,1)S(1)} %get-tuple-element.79.refs_2_.refs_0_.q_ref, bf16[128,512]{1,0:T(8,128)(2,1)S(1)} %collective-permute-done.14.refs_1_, ...), custom_call_target="tpu_custom_call" | custom-call | flops 1000 | bytes 1000 | tf_op jit(solution)/shard_map/attend/pallas_call | solution.py:262
  86.5 1.7 collective-permute-start.32
  88.9 3.6 %attend.6 = (bf16[2,128,384]{2,1,0:T(8,128)(2,1)S(1)}, bf16[1,128,384]{2,1,0:T(8,128)(2,1)S(1)}, bf16[1,128,384]{2,1,0:T(8,128)(2,1)S(1)}) custom-call(s32[1]{0:T(128)} %bitcast.at_ref, bf16[128,384]{1,0:T(8,128)(2,1)S(1)} %get-tuple-element.82.refs_10_.refs_0_.q_ref, bf16[128,384]{1,0:T(8,128)(2,1)S(1)} %collective-permute-done.25.refs_1_, ...), custom_call_target="tpu_custom_call" | custom-call | flops 1000 | bytes 1000 | tf_op jit(solution)/shard_map/attend/pallas_call | solution.py:262
  92.5 3.0 %collective-permute-done.22.refs_1_ = bf16[128,256]{1,0:T(8,128)(2,1)S(1)} collective-permute-done((bf16[128,256]{1,0:T(8,128)(2,1)S(1)}, bf16[128,256]{1,0:T(8,128)(2,1)S(1)}, u32[]{:S(2)}, u32[]{:S(2)}) %collective-permute-start.22) | collective-permute-done | bytes 65568 | tf_op jit(solution)/shard_map/ppermute | solution.py:525
  96.9 1.7 collective-permute-start.36
  98.6 2.1 %attend.7 = (bf16[2,128,256]{2,1,0:T(8,128)(2,1)S(1)}, bf16[1,128,256]{2,1,0:T(8,128)(2,1)S(1)}, bf16[1,128,256]{2,1,0:T(8,128)(2,1)S(1)}) custom-call(s32[1]{0:T(128)} %bitcast.at_ref, bf16[128,256]{1,0:T(8,128)(2,1)S(1)} %get-tuple-element.84.refs_2_.refs_0_.q_ref, bf16[128,256]{1,0:T(8,128)(2,1)S(1)} %collective-permute-done.22.refs_1_, ...), custom_call_target="tpu_custom_call" | custom-call | flops 1000 | bytes 1000 | tf_op jit(solution)/shard_map/attend/pallas_call | solution.py:262
  102.6 1.7 collective-permute-start.34
  104.8 1.8 %collective-permute-done.38.refs_2_ = bf16[1,128,384]{2,1,0:T(8,128)(2,1)S(1)} collective-permute-done((bf16[1,128,384]{2,1,0:T(8,128)(2,1)S(1)}, bf16[1,128,384]{2,1,0:T(8,128)(2,1)S(1)}, u32[]{:S(2)}, u32[]{:S(2)}) %collective-permute-start.38) | collective-permute-done | bytes 98336 | tf_op jit(solution)/shard_map/ppermute | solution.py:525
  108.0 1.6 collective-permute-start.39
  109.7 2.0 %collective-permute-done.39.refs_1_ = f32[8,128]{1,0:T(8,128)S(1)} collective-permute-done((f32[8,128]{1,0:T(8,128)S(1)}, f32[8,128]{1,0:T(8,128)S(1)}, u32[]{:S(2)}, u32[]{:S(2)}) %collective-permute-start.39) | collective-permute-done | bytes 4128 | tf_op jit(solution)/shard_map/ppermute | solution.py:525
  111.7 2.6 %collective-permute-start.40 = (f32[8,128]{1,0:T(8,128)S(1)}, f32[8,128]{1,0:T(8,128)S(1)}, u32[]{:S(2)}, u32[]{:S(2)}) collective-permute-start(f32[8,128]{1,0:T(8,128)S(1)} %merge.1.refs_0_), channel_id=1, source_target_pairs={{0,8},{4,12},{8,0},{12,4},{1,9},{5,13},{9,1},{13,5},{2,10},{6,14},... | collective-permute-start | bytes 12296 | tf_op jit(solution)/shard_map/ppermute | solution.py:525
  114.3 1.9 %collective-permute-done.40.refs_1_ = f32[8,128]{1,0:T(8,128)S(1)} collective-permute-done((f32[8,128]{1,0:T(8,128)S(1)}, f32[8,128]{1,0:T(8,128)S(1)}, u32[]{:S(2)}, u32[]{:S(2)}) %collective-permute-start.40) | collective-permute-done | bytes 4128 | tf_op jit(solution)/shard_map/ppermute | solution.py:525
  116.6 1.3 collective-permute-start.42
  118.7 6.7 %collective-permute-done.42 = bf16[64,2048]{1,0:T(8,128)(2,1)S(1)} collective-permute-done((bf16[64,2048]{1,0:T(8,128)(2,1)S(1)}, bf16[64,2048]{1,0:T(8,128)(2,1)S(1)}, u32[]{:S(2)}, u32[]{:S(2)}) %collective-permute-start.42) | collective-permute-done | bytes 262176 | tf_op jit(solution)/shard_map/ppermute | solution.py:525
  126.9 3.4 %output.4 = (bf16[2,4,16,1024]{3,2,1,0:T(8,128)(2,1)S(1)}, bf16[2,4,16,1024]{3,2,1,0:T(8,128)(2,1)S(1)}) custom-call(s32[1]{0:T(128)} %bitcast.3.index_ref, bf16[4,16,2048]{2,1,0:T(8,128)(2,1)S(1)} %bitcast.47, bf16[4,16,2048]{2,1,0:T(8,128)(2,1)S(1)} %bitcast.49, bf16[4,16,2048]{2,1,0:T(8,128)(2,1)S(1)} %bitcast.51, bf16[4,16,2048]{2,1,0:T(8,128)(2,1)S(1)} %bitcast.53, ...), custom_call_target="tpu_custom_call" | custom-call | flops 1000 | bytes 1000 | tf_op jit(solution)/shard_map/output/pallas_call | solution.py:444
  130.6 1.6 collective-permute-start.47
  132.2 3.4 %output.5 = (bf16[2,4,16,1024]{3,2,1,0:T(8,128)(2,1)S(1)}, bf16[2,4,16,1024]{3,2,1,0:T(8,128)(2,1)S(1)}) custom-call(s32[1]{0:T(128)} %bitcast.3.index_ref, bf16[4,16,2048]{2,1,0:T(8,128)(2,1)S(1)} %bitcast.48, bf16[4,16,2048]{2,1,0:T(8,128)(2,1)S(1)} %bitcast.50, bf16[4,16,2048]{2,1,0:T(8,128)(2,1)S(1)} %bitcast.52, bf16[4,16,2048]{2,1,0:T(8,128)(2,1)S(1)} %bitcast.54, ...), custom_call_target="tpu_custom_call" | custom-call | flops 1000 | bytes 1000 | tf_op jit(solution)/shard_map/output/pallas_call | solution.py:444
  136.1 3.5 %output.6 = (bf16[2,4,16,1024]{3,2,1,0:T(8,128)(2,1)S(1)}, bf16[2,4,16,1024]{3,2,1,0:T(8,128)(2,1)S(1)}) custom-call(s32[1]{0:T(128)} %bitcast.3.index_ref, bf16[4,16,2176]{2,1,0:T(8,128)(2,1)S(1)} %bitcast.41, bf16[4,16,2176]{2,1,0:T(8,128)(2,1)S(1)} %bitcast.39, bf16[4,16,2176]{2,1,0:T(8,128)(2,1)S(1)} %bitcast.43, bf16[4,16,2176]{2,1,0:T(8,128)(2,1)S(1)} %bitcast.45, ...), custom_call_target="tpu_custom_call" | custom-call | flops 1000 | bytes 1000 | tf_op jit(solution)/shard_map/output/pallas_call | solution.py:444
  139.8 2.7 %collective-permute-start.51 = (bf16[1,4,16,1024]{3,2,1,0:T(8,128)(2,1)S(1)}, bf16[1,4,16,1024]{3,2,1,0:T(8,128)(2,1)S(1)}, u32[]{:S(2)}, u32[]{:S(2)}) collective-permute-start(bf16[1,4,16,1024]{3,2,1,0:T(8,128)(2,1)S(1)} %fold.22.refs_5_), channel_id=1, source_target_pairs={{0,8},{4,12},{8,0},{12,4},{1,9},{5,13},{9,1},{13,5},{2,10},{6,14},... | collective-permute-start | bytes 393224 | tf_op jit(solution)/shard_map/ppermute | solution.py:525
  142.5 1.6 collective-permute-start.48
  144.1 3.5 %output.7 = (bf16[2,4,16,1024]{3,2,1,0:T(8,128)(2,1)S(1)}, bf16[2,4,16,1024]{3,2,1,0:T(8,128)(2,1)S(1)}) custom-call(s32[1]{0:T(128)} %bitcast.3.index_ref, bf16[4,16,2176]{2,1,0:T(8,128)(2,1)S(1)} %bitcast.42, bf16[4,16,2176]{2,1,0:T(8,128)(2,1)S(1)} %bitcast.40, bf16[4,16,2176]{2,1,0:T(8,128)(2,1)S(1)} %bitcast.44, bf16[4,16,2176]{2,1,0:T(8,128)(2,1)S(1)} %bitcast.46, ...), custom_call_target="tpu_custom_call" | custom-call | flops 1000 | bytes 1000 | tf_op jit(solution)/shard_map/output/pallas_call | solution.py:444
  148.1 2.6 %collective-permute-start.52 = (bf16[2,4,16,1024]{3,2,1,0:T(8,128)(2,1)S(1)}, bf16[2,4,16,1024]{3,2,1,0:T(8,128)(2,1)S(1)}, u32[]{:S(2)}, u32[]{:S(2)}) collective-permute-start(bf16[2,4,16,1024]{3,2,1,0:T(8,128)(2,1)S(1)} %tie.25), channel_id=1, source_target_pairs={{0,4},{4,0},{8,12},{12,8},{1,5},{5,1},{9,13},{13,9},{2,6},{6,2},{1... | collective-permute-start | bytes 786440 | tf_op jit(solution)/shard_map/ppermute | solution.py:525
  151.0 2.4 %collective-permute-start.54 = (bf16[1,4,16,1024]{3,2,1,0:T(8,128)(2,1)S(1)}, bf16[1,4,16,1024]{3,2,1,0:T(8,128)(2,1)S(1)}, u32[]{:S(2)}, u32[]{:S(2)}) collective-permute-start(bf16[1,4,16,1024]{3,2,1,0:T(8,128)(2,1)S(1)} %fold.23.refs_2_), channel_id=1, source_target_pairs={{0,8},{4,12},{8,0},{12,4},{1,9},{5,13},{9,1},{13,5},{2,10},{6,14},... | collective-permute-start | bytes 393224 | tf_op jit(solution)/shard_map/ppermute | solution.py:525
  153.3 1.8 %collective-permute-done.48.refs_1_ = bf16[2,4,16,1024]{3,2,1,0:T(8,128)(2,1)S(1)} collective-permute-done((bf16[2,4,16,1024]{3,2,1,0:T(8,128)(2,1)S(1)}, bf16[2,4,16,1024]{3,2,1,0:T(8,128)(2,1)S(1)}, u32[]{:S(2)}, u32[]{:S(2)}) %collective-permute-start.48) | collective-permute-done | bytes 262176 | tf_op jit(solution)/shard_map/ppermute | solution.py:525
  155.3 3.2 %collective-permute-start.50 = (bf16[1,4,16,1024]{3,2,1,0:T(8,128)(2,1)S(1)}, bf16[1,4,16,1024]{3,2,1,0:T(8,128)(2,1)S(1)}, u32[]{:S(2)}, u32[]{:S(2)}) collective-permute-start(bf16[1,4,16,1024]{3,2,1,0:T(8,128)(2,1)S(1)} %fold.24.refs_3_), channel_id=1, source_target_pairs={{0,8},{4,12},{8,0},{12,4},{1,9},{5,13},{9,1},{13,5},{2,10},{6,14},... | collective-permute-start | bytes 393224 | tf_op jit(solution)/shard_map/ppermute | solution.py:525
  158.5 2.2 %close.3 = (bf16[8,16,2048]{2,1,0:T(8,128)(2,1)}, f32[8,128]{1,0:T(8,128)S(1)}) custom-call(s32[2]{0:T(128)S(1)} %pad_add_fusion.1.at_ref, bf16[32,16,2048]{2,1,0:T(8,128)(2,1)} %bitcast.77, bf16[2,4,16,1024]{3,2,1,0:T(8,128)(2,1)S(1)} %get-tuple-element.108.refs_1_.refs_5_.refs_0_, bf16[2,4,16,1024]{3,2,1,0:T(8,128)(2,1)S(1)} %collective-permute-done.47.refs_1_, ...), custom_call_target="tpu_custom_call" | custom-call | flops 1000 | bytes 1000 | tf_op jit(solution)/shard_map/close/pallas_call | solution.py:490
  160.6 3.4 %collective-permute-done.52.refs_1_.refs_4_ = bf16[2,4,16,1024]{3,2,1,0:T(8,128)(2,1)S(1)} collective-permute-done((bf16[2,4,16,1024]{3,2,1,0:T(8,128)(2,1)S(1)}, bf16[2,4,16,1024]{3,2,1,0:T(8,128)(2,1)S(1)}, u32[]{:S(2)}, u32[]{:S(2)}) %collective-permute-start.52) | collective-permute-done | bytes 262176 | tf_op jit(solution)/shard_map/ppermute | solution.py:525
  164.3 2.2 %close.4 = (bf16[8,16,2048]{2,1,0:T(8,128)(2,1)}, f32[8,128]{1,0:T(8,128)S(1)}) custom-call(s32[2]{0:T(128)S(1)} %pad_add_fusion.1.at_ref, bf16[32,16,2048]{2,1,0:T(8,128)(2,1)} %bitcast.78, bf16[2,4,16,1024]{3,2,1,0:T(8,128)(2,1)S(1)} %get-tuple-element.109.refs_5_.refs_0_, ...), custom_call_target="tpu_custom_call", output_to_operand_aliasing={{0}: (5, {})} | custom-call | flops 1000 | bytes 1000 | tf_op jit(solution)/shard_map/close/pallas_call | solution.py:490
  166.5 3.8 %collective-permute-done.50.refs_2_ = bf16[1,4,16,1024]{3,2,1,0:T(8,128)(2,1)S(1)} collective-permute-done((bf16[1,4,16,1024]{3,2,1,0:T(8,128)(2,1)S(1)}, bf16[1,4,16,1024]{3,2,1,0:T(8,128)(2,1)S(1)}, u32[]{:S(2)}, u32[]{:S(2)}) %collective-permute-start.50) | collective-permute-done | bytes 131104 | tf_op jit(solution)/shard_map/ppermute | solution.py:525
  170.2 2.4 %collective-permute-done.53.refs_5_ = bf16[1,4,16,1024]{3,2,1,0:T(8,128)(2,1)S(1)} collective-permute-done((bf16[1,4,16,1024]{3,2,1,0:T(8,128)(2,1)S(1)}, bf16[1,4,16,1024]{3,2,1,0:T(8,128)(2,1)S(1)}, u32[]{:S(2)}, u32[]{:S(2)}) %collective-permute-start.53) | collective-permute-done | bytes 131104 | tf_op jit(solution)/shard_map/ppermute | solution.py:525
  172.7 2.3 %close.5 = (bf16[8,16,2048]{2,1,0:T(8,128)(2,1)}, f32[8,128]{1,0:T(8,128)}) custom-call(s32[2]{0:T(128)S(1)} %pad_add_fusion.at_ref, bf16[32,16,2048]{2,1,0:T(8,128)(2,1)} %bitcast.79, bf16[2,4,16,1024]{3,2,1,0:T(8,128)(2,1)S(1)} %get-tuple-element.110.refs_2_.refs_0_, ...), custom_call_target="tpu_custom_call", output_to_operand_aliasing={{0}: (8, {})} | custom-call | flops 1000 | bytes 1000 | tf_op jit(solution)/shard_map/close/pallas_call | solution.py:490
  (133 shorter events, 20.1 us)
Async XLA Ops:
  7.1 9.4 %collective-permute-start = (bf16[1,4,128,384]{3,2,1,0:T(8,128)(2,1)S(1)}, bf16[1,4,128,384]{3,2,1,0:T(8,128)(2,1)S(1)}, u32[]{:S(2)}, u32[]{:S(2)}) collective-permute-start(bf16[1,4,128,384]{3,2,1,0:T(8,128)(2,1)S(1)} %get-tuple-element.66), channel_id=1, source_target_pairs={{0,1},{1,0},{2,3},{3,2},{4,5},{5,4},{6,7},{7,6},{8,9},{9,8},{10,11... | collective-permute-start | bytes 1179656 | tf_op jit(solution)/shard_map/ppermute | solution.py:525
  7.7 8.8 %collective-permute-start.1 = (bf16[1,4,128,384]{3,2,1,0:T(8,128)(2,1)S(1)}, bf16[1,4,128,384]{3,2,1,0:T(8,128)(2,1)S(1)}, u32[]{:S(2)}, u32[]{:S(2)}) collective-permute-start(bf16[1,4,128,384]{3,2,1,0:T(8,128)(2,1)S(1)} %get-tuple-element.67), channel_id=1, source_target_pairs={{0,1},{1,0},{2,3},{3,2},{4,5},{5,4},{6,7},{7,6},{8,9},{9,8},{10,11... | collective-permute-start | bytes 1179656 | tf_op jit(solution)/shard_map/ppermute | solution.py:525
  16.5 13.0 %collective-permute-start.3 = (bf16[1,4,128,512]{3,2,1,0:T(8,128)(2,1)S(1)}, bf16[1,4,128,512]{3,2,1,0:T(8,128)(2,1)S(1)}, u32[]{:S(2)}, u32[]{:S(2)}) collective-permute-start(bf16[1,4,128,512]{3,2,1,0:T(8,128)(2,1)S(1)} %tie.14), channel_id=1, source_target_pairs={{0,1},{1,0},{2,3},{3,2},{4,5},{5,4},{6,7},{7,6},{8,9},{9,8},{10,11... | collective-permute-start | bytes 1572872 | tf_op jit(solution)/shard_map/ppermute | solution.py:525
  17.0 12.5 %collective-permute-start.2 = (bf16[1,4,128,512]{3,2,1,0:T(8,128)(2,1)S(1)}, bf16[1,4,128,512]{3,2,1,0:T(8,128)(2,1)S(1)}, u32[]{:S(2)}, u32[]{:S(2)}) collective-permute-start(bf16[1,4,128,512]{3,2,1,0:T(8,128)(2,1)S(1)} %tie.13), channel_id=1, source_target_pairs={{0,1},{1,0},{2,3},{3,2},{4,5},{5,4},{6,7},{7,6},{8,9},{9,8},{10,11... | collective-permute-start | bytes 1572872 | tf_op jit(solution)/shard_map/ppermute | solution.py:525
  17.2 12.3 %collective-permute-start.4 = (bf16[1,4,128,384]{3,2,1,0:T(8,128)(2,1)S(1)}, bf16[1,4,128,384]{3,2,1,0:T(8,128)(2,1)S(1)}, u32[]{:S(2)}, u32[]{:S(2)}) collective-permute-start(bf16[1,4,128,384]{3,2,1,0:T(8,128)(2,1)S(1)} %fold.13.refs_8_), channel_id=1, source_target_pairs={{0,2},{1,3},{2,0},{3,1},{4,6},{5,7},{6,4},{7,5},{8,10},{9,11},{10,... | collective-permute-start | bytes 1179656 | tf_op jit(solution)/shard_map/ppermute | solution.py:525
  29.6 9.8 %collective-permute-start.6 = (bf16[1,4,128,512]{3,2,1,0:T(8,128)(2,1)S(1)}, bf16[1,4,128,512]{3,2,1,0:T(8,128)(2,1)S(1)}, u32[]{:S(2)}, u32[]{:S(2)}) collective-permute-start(bf16[1,4,128,512]{3,2,1,0:T(8,128)(2,1)S(1)} %tie.16), channel_id=1, source_target_pairs={{0,1},{1,0},{2,3},{3,2},{4,5},{5,4},{6,7},{7,6},{8,9},{9,8},{10,11... | collective-permute-start | bytes 1572872 | tf_op jit(solution)/shard_map/ppermute | solution.py:525
  29.6 9.7 %collective-permute-start.5 = (bf16[1,4,128,512]{3,2,1,0:T(8,128)(2,1)S(1)}, bf16[1,4,128,512]{3,2,1,0:T(8,128)(2,1)S(1)}, u32[]{:S(2)}, u32[]{:S(2)}) collective-permute-start(bf16[1,4,128,512]{3,2,1,0:T(8,128)(2,1)S(1)} %tie.15), channel_id=1, source_target_pairs={{0,1},{1,0},{2,3},{3,2},{4,5},{5,4},{6,7},{7,6},{8,9},{9,8},{10,11... | collective-permute-start | bytes 1572872 | tf_op jit(solution)/shard_map/ppermute | solution.py:525
  30.4 14.5 %collective-permute-start.8 = (bf16[1,4,128,512]{3,2,1,0:T(8,128)(2,1)S(1)}, bf16[1,4,128,512]{3,2,1,0:T(8,128)(2,1)S(1)}, u32[]{:S(2)}, u32[]{:S(2)}) collective-permute-start(bf16[1,4,128,512]{3,2,1,0:T(8,128)(2,1)S(1)} %fold.14.refs_8_), channel_id=1, source_target_pairs={{0,2},{1,3},{2,0},{3,1},{4,6},{5,7},{6,4},{7,5},{8,10},{9,11},{10,... | collective-permute-start | bytes 1572872 | tf_op jit(solution)/shard_map/ppermute | solution.py:525
  39.4 8.3 %collective-permute-start.7 = (bf16[1,4,128,384]{3,2,1,0:T(8,128)(2,1)S(1)}, bf16[1,4,128,384]{3,2,1,0:T(8,128)(2,1)S(1)}, u32[]{:S(2)}, u32[]{:S(2)}) collective-permute-start(bf16[1,4,128,384]{3,2,1,0:T(8,128)(2,1)S(1)} %tie.17), channel_id=1, source_target_pairs={{0,1},{1,0},{2,3},{3,2},{4,5},{5,4},{6,7},{7,6},{8,9},{9,8},{10,11... | collective-permute-start | bytes 1179656 | tf_op jit(solution)/shard_map/ppermute | solution.py:525
  39.5 15.2 %collective-permute-start.9 = (bf16[1,4,128,384]{3,2,1,0:T(8,128)(2,1)S(1)}, bf16[1,4,128,384]{3,2,1,0:T(8,128)(2,1)S(1)}, u32[]{:S(2)}, u32[]{:S(2)}) collective-permute-start(bf16[1,4,128,384]{3,2,1,0:T(8,128)(2,1)S(1)} %tie.18), channel_id=1, source_target_pairs={{0,1},{1,0},{2,3},{3,2},{4,5},{5,4},{6,7},{7,6},{8,9},{9,8},{10,11... | collective-permute-start | bytes 1179656 | tf_op jit(solution)/shard_map/ppermute | solution.py:525
  40.9 21.6 %collective-permute-start.12 = (bf16[1,4,128,512]{3,2,1,0:T(8,128)(2,1)}, bf16[1,4,128,512]{3,2,1,0:T(8,128)(2,1)}, u32[]{:S(2)}, u32[]{:S(2)}) collective-permute-start(bf16[1,4,128,512]{3,2,1,0:T(8,128)(2,1)} %fold.15.refs_6_), channel_id=1, source_target_pairs={{0,2},{1,3},{2,0},{3,1},{4,6},{5,7},{6,4},{7,5},{8,10},{9,11},{10,... | collective-permute-start | bytes 1572872 | tf_op jit(solution)/shard_map/ppermute | solution.py:525
  45.5 15.1 %collective-permute-start.18 = (bf16[128,896]{1,0:T(8,128)(2,1)S(1)}, bf16[128,896]{1,0:T(8,128)(2,1)}, u32[]{:S(2)}, u32[]{:S(2)}) collective-permute-start(bf16[128,896]{1,0:T(8,128)(2,1)S(1)} %get-tuple-element.74.refs_2_.refs_0_.q_ref), channel_id=1, source_target_pairs={{0,2},{1,3},{2,0},{3,1},{4,6},{5,7},{6,4},{7,5},{8,10},{9,11},{10,... | collective-permute-start | bytes 688136 | tf_op jit(solution)/shard_map/ppermute | solution.py:525
  54.7 9.2 %collective-permute-start.11 = (bf16[1,4,128,256]{3,2,1,0:T(8,128)(2,1)}, bf16[1,4,128,256]{3,2,1,0:T(8,128)(2,1)}, u32[]{:S(2)}, u32[]{:S(2)}) collective-permute-start(bf16[1,4,128,256]{3,2,1,0:T(8,128)(2,1)} %tie.20), channel_id=1, source_target_pairs={{0,1},{1,0},{2,3},{3,2},{4,5},{5,4},{6,7},{7,6},{8,9},{9,8},{10,11... | collective-permute-start | bytes 786440 | tf_op jit(solution)/shard_map/ppermute | solution.py:525
  54.8 10.2 %collective-permute-start.19 = (bf16[128,896]{1,0:T(8,128)(2,1)S(1)}, bf16[128,896]{1,0:T(8,128)(2,1)}, u32[]{:S(2)}, u32[]{:S(2)}) collective-permute-start(bf16[128,896]{1,0:T(8,128)(2,1)S(1)} %get-tuple-element.74.refs_2_.refs_0_.q_ref), channel_id=1, source_target_pairs={{0,1},{1,0},{2,3},{3,2},{4,5},{5,4},{6,7},{7,6},{8,9},{9,8},{10,11... | collective-permute-start | bytes 688136 | tf_op jit(solution)/shard_map/ppermute | solution.py:525
  60.7 4.4 %collective-permute-start.20 = (bf16[128,896]{1,0:T(8,128)(2,1)}, bf16[128,896]{1,0:T(8,128)(2,1)}, u32[]{:S(2)}, u32[]{:S(2)}) collective-permute-start(bf16[128,896]{1,0:T(8,128)(2,1)} %collective-permute-done.18.refs_1_), channel_id=1, source_target_pairs={{0,1},{1,0},{2,3},{3,2},{4,5},{5,4},{6,7},{7,6},{8,9},{9,8},{10,11... | collective-permute-start | bytes 688136 | tf_op jit(solution)/shard_map/ppermute | solution.py:525
  60.7 18.8 %collective-permute-start.17 = (bf16[1,4,128,384]{3,2,1,0:T(8,128)(2,1)}, bf16[1,4,128,384]{3,2,1,0:T(8,128)(2,1)}, u32[]{:S(2)}, u32[]{:S(2)}) collective-permute-start(bf16[1,4,128,384]{3,2,1,0:T(8,128)(2,1)} %fold.16.refs_8_), channel_id=1, source_target_pairs={{0,2},{1,3},{2,0},{3,1},{4,6},{5,7},{6,4},{7,5},{8,10},{9,11},{10,... | collective-permute-start | bytes 1179656 | tf_op jit(solution)/shard_map/ppermute | solution.py:525
  72.3 6.6 %collective-permute-start.21 = (bf16[1,128,896]{2,1,0:T(8,128)(2,1)S(1)}, bf16[1,128,896]{2,1,0:T(8,128)(2,1)S(1)}, u32[]{:S(2)}, u32[]{:S(2)}) collective-permute-start(bf16[1,128,896]{2,1,0:T(8,128)(2,1)S(1)} %get-tuple-element.81), channel_id=1, source_target_pairs={{0,1},{1,0},{2,3},{3,2},{4,5},{5,4},{6,7},{7,6},{8,9},{9,8},{10,11... | collective-permute-start | bytes 688136 | tf_op jit(solution)/shard_map/ppermute | solution.py:525
  72.6 6.3 %collective-permute-start.14 = (bf16[128,512]{1,0:T(8,128)(2,1)S(1)}, bf16[128,512]{1,0:T(8,128)(2,1)S(1)}, u32[]{:S(2)}, u32[]{:S(2)}) collective-permute-start(bf16[128,512]{1,0:T(8,128)(2,1)S(1)} %get-tuple-element.79.refs_2_.refs_0_.q_ref), channel_id=1, source_target_pairs={{0,2},{1,3},{2,0},{3,1},{4,6},{5,7},{6,4},{7,5},{8,10},{9,11},{10,... | collective-permute-start | bytes 393224 | tf_op jit(solution)/shard_map/ppermute | solution.py:525
  72.9 13.1 %collective-permute-start.10 = (bf16[1,4,128,256]{3,2,1,0:T(8,128)(2,1)S(1)}, bf16[1,4,128,256]{3,2,1,0:T(8,128)(2,1)S(1)}, u32[]{:S(2)}, u32[]{:S(2)}) collective-permute-start(bf16[1,4,128,256]{3,2,1,0:T(8,128)(2,1)S(1)} %tie.19), channel_id=1, source_target_pairs={{0,1},{1,0},{2,3},{3,2},{4,5},{5,4},{6,7},{7,6},{8,9},{9,8},{10,11... | collective-permute-start | bytes 786440 | tf_op jit(solution)/shard_map/ppermute | solution.py:525
  72.9 13.6 %collective-permute-start.13 = (bf16[1,4,128,256]{3,2,1,0:T(8,128)(2,1)S(1)}, bf16[1,4,128,256]{3,2,1,0:T(8,128)(2,1)S(1)}, u32[]{:S(2)}, u32[]{:S(2)}) collective-permute-start(bf16[1,4,128,256]{3,2,1,0:T(8,128)(2,1)S(1)} %fold.17.refs_10_), channel_id=1, source_target_pairs={{0,2},{1,3},{2,0},{3,1},{4,6},{5,7},{6,4},{7,5},{8,10},{9,11},{10,... | collective-permute-start | bytes 786440 | tf_op jit(solution)/shard_map/ppermute | solution.py:525
  80.7 5.2 %collective-permute-start.25 = (bf16[128,384]{1,0:T(8,128)(2,1)S(1)}, bf16[128,384]{1,0:T(8,128)(2,1)S(1)}, u32[]{:S(2)}, u32[]{:S(2)}) collective-permute-start(bf16[128,384]{1,0:T(8,128)(2,1)S(1)} %get-tuple-element.82.refs_10_.refs_0_.q_ref), channel_id=1, source_target_pairs={{0,2},{1,3},{2,0},{3,1},{4,6},{5,7},{6,4},{7,5},{8,10},{9,11},{10,... | collective-permute-start | bytes 294920 | tf_op jit(solution)/shard_map/ppermute | solution.py:525
  81.1 7.2 %collective-permute-start.26 = (bf16[128,384]{1,0:T(8,128)(2,1)S(1)}, bf16[128,384]{1,0:T(8,128)(2,1)S(1)}, u32[]{:S(2)}, u32[]{:S(2)}) collective-permute-start(bf16[128,384]{1,0:T(8,128)(2,1)S(1)} %get-tuple-element.82.refs_10_.refs_0_.q_ref), channel_id=1, source_target_pairs={{0,1},{1,0},{2,3},{3,2},{4,5},{5,4},{6,7},{7,6},{8,9},{9,8},{10,11... | collective-permute-start | bytes 294920 | tf_op jit(solution)/shard_map/ppermute | solution.py:525
  86.0 14.9 %collective-permute-start.31 = (bf16[1,128,896]{2,1,0:T(8,128)(2,1)S(1)}, bf16[1,128,896]{2,1,0:T(8,128)(2,1)S(1)}, u32[]{:S(2)}, u32[]{:S(2)}) collective-permute-start(bf16[1,128,896]{2,1,0:T(8,128)(2,1)S(1)} %get-tuple-element.92), channel_id=1, source_target_pairs={{0,1},{1,0},{2,3},{3,2},{4,5},{5,4},{6,7},{7,6},{8,9},{9,8},{10,11... | collective-permute-start | bytes 688136 | tf_op jit(solution)/shard_map/ppermute | solution.py:525
  86.5 14.9 %collective-permute-start.32 = (bf16[1,128,896]{2,1,0:T(8,128)(2,1)S(1)}, bf16[1,128,896]{2,1,0:T(8,128)(2,1)S(1)}, u32[]{:S(2)}, u32[]{:S(2)}) collective-permute-start(bf16[1,128,896]{2,1,0:T(8,128)(2,1)S(1)} %fold.18.refs_3_), channel_id=1, source_target_pairs={{0,2},{1,3},{2,0},{3,1},{4,6},{5,7},{6,4},{7,5},{8,10},{9,11},{10,... | collective-permute-start | bytes 688136 | tf_op jit(solution)/shard_map/ppermute | solution.py:525
  88.3 7.1 %collective-permute-start.22 = (bf16[128,256]{1,0:T(8,128)(2,1)S(1)}, bf16[128,256]{1,0:T(8,128)(2,1)S(1)}, u32[]{:S(2)}, u32[]{:S(2)}) collective-permute-start(bf16[128,256]{1,0:T(8,128)(2,1)S(1)} %get-tuple-element.84.refs_2_.refs_0_.q_ref), channel_id=1, source_target_pairs={{0,2},{1,3},{2,0},{3,1},{4,6},{5,7},{6,4},{7,5},{8,10},{9,11},{10,... | collective-permute-start | bytes 196616 | tf_op jit(solution)/shard_map/ppermute | solution.py:525
  88.8 7.2 %collective-permute-start.23 = (bf16[128,256]{1,0:T(8,128)(2,1)S(1)}, bf16[128,256]{1,0:T(8,128)(2,1)S(1)}, u32[]{:S(2)}, u32[]{:S(2)}) collective-permute-start(bf16[128,256]{1,0:T(8,128)(2,1)S(1)} %get-tuple-element.84.refs_2_.refs_0_.q_ref), channel_id=1, source_target_pairs={{0,1},{1,0},{2,3},{3,2},{4,5},{5,4},{6,7},{7,6},{8,9},{9,8},{10,11... | collective-permute-start | bytes 196616 | tf_op jit(solution)/shard_map/ppermute | solution.py:525
  95.5 5.2 %collective-permute-start.33 = (bf16[1,128,384]{2,1,0:T(8,128)(2,1)S(1)}, bf16[1,128,384]{2,1,0:T(8,128)(2,1)S(1)}, u32[]{:S(2)}, u32[]{:S(2)}) collective-permute-start(bf16[1,128,384]{2,1,0:T(8,128)(2,1)S(1)} %tie.21), channel_id=1, source_target_pairs={{0,1},{1,0},{2,3},{3,2},{4,5},{5,4},{6,7},{7,6},{8,9},{9,8},{10,11... | collective-permute-start | bytes 294920 | tf_op jit(solution)/shard_map/ppermute | solution.py:525
  96.0 6.6 %collective-permute-start.35 = (bf16[1,128,512]{2,1,0:T(8,128)(2,1)S(1)}, bf16[1,128,512]{2,1,0:T(8,128)(2,1)S(1)}, u32[]{:S(2)}, u32[]{:S(2)}) collective-permute-start(bf16[1,128,512]{2,1,0:T(8,128)(2,1)S(1)} %get-tuple-element.97), channel_id=1, source_target_pairs={{0,1},{1,0},{2,3},{3,2},{4,5},{5,4},{6,7},{7,6},{8,9},{9,8},{10,11... | collective-permute-start | bytes 393224 | tf_op jit(solution)/shard_map/ppermute | solution.py:525
  96.9 7.5 %collective-permute-start.36 = (bf16[1,128,512]{2,1,0:T(8,128)(2,1)S(1)}, bf16[1,128,512]{2,1,0:T(8,128)(2,1)S(1)}, u32[]{:S(2)}, u32[]{:S(2)}) collective-permute-start(bf16[1,128,512]{2,1,0:T(8,128)(2,1)S(1)} %fold.19.refs_10_), channel_id=1, source_target_pairs={{0,2},{1,3},{2,0},{3,1},{4,6},{5,7},{6,4},{7,5},{8,10},{9,11},{10,... | collective-permute-start | bytes 393224 | tf_op jit(solution)/shard_map/ppermute | solution.py:525
  100.9 3.9 %collective-permute-start.37 = (bf16[1,128,384]{2,1,0:T(8,128)(2,1)S(1)}, bf16[1,128,384]{2,1,0:T(8,128)(2,1)S(1)}, u32[]{:S(2)}, u32[]{:S(2)}) collective-permute-start(bf16[1,128,384]{2,1,0:T(8,128)(2,1)S(1)} %tie.22), channel_id=1, source_target_pairs={{0,1},{1,0},{2,3},{3,2},{4,5},{5,4},{6,7},{7,6},{8,9},{9,8},{10,11... | collective-permute-start | bytes 294920 | tf_op jit(solution)/shard_map/ppermute | solution.py:525
  101.4 5.2 %collective-permute-start.38 = (bf16[1,128,384]{2,1,0:T(8,128)(2,1)S(1)}, bf16[1,128,384]{2,1,0:T(8,128)(2,1)S(1)}, u32[]{:S(2)}, u32[]{:S(2)}) collective-permute-start(bf16[1,128,384]{2,1,0:T(8,128)(2,1)S(1)} %fold.20.refs_3_), channel_id=1, source_target_pairs={{0,2},{1,3},{2,0},{3,1},{4,6},{5,7},{6,4},{7,5},{8,10},{9,11},{10,... | collective-permute-start | bytes 294920 | tf_op jit(solution)/shard_map/ppermute | solution.py:525
  102.4 4.6 %collective-permute-start.29 = (bf16[1,128,256]{2,1,0:T(8,128)(2,1)S(1)}, bf16[1,128,256]{2,1,0:T(8,128)(2,1)S(1)}, u32[]{:S(2)}, u32[]{:S(2)}) collective-permute-start(bf16[1,128,256]{2,1,0:T(8,128)(2,1)S(1)} %get-tuple-element.89), channel_id=1, source_target_pairs={{0,1},{1,0},{2,3},{3,2},{4,5},{5,4},{6,7},{7,6},{8,9},{9,8},{10,11... | collective-permute-start | bytes 196616 | tf_op jit(solution)/shard_map/ppermute | solution.py:525
  102.6 4.9 %collective-permute-start.34 = (bf16[1,128,256]{2,1,0:T(8,128)(2,1)S(1)}, bf16[1,128,256]{2,1,0:T(8,128)(2,1)S(1)}, u32[]{:S(2)}, u32[]{:S(2)}) collective-permute-start(bf16[1,128,256]{2,1,0:T(8,128)(2,1)S(1)} %fold.21.refs_3_), channel_id=1, source_target_pairs={{0,2},{1,3},{2,0},{3,1},{4,6},{5,7},{6,4},{7,5},{8,10},{9,11},{10,... | collective-permute-start | bytes 196616 | tf_op jit(solution)/shard_map/ppermute | solution.py:525
  108.0 3.6 %collective-permute-start.39 = (f32[8,128]{1,0:T(8,128)S(1)}, f32[8,128]{1,0:T(8,128)S(1)}, u32[]{:S(2)}, u32[]{:S(2)}) collective-permute-start(f32[8,128]{1,0:T(8,128)S(1)} %get-tuple-element.104.refs_0_), channel_id=1, source_target_pairs={{0,4},{4,0},{8,12},{12,8},{1,5},{5,1},{9,13},{13,9},{2,6},{6,2},{1... | collective-permute-start | bytes 12296 | tf_op jit(solution)/shard_map/ppermute | solution.py:525
  111.7 4.5 %collective-permute-start.40 = (f32[8,128]{1,0:T(8,128)S(1)}, f32[8,128]{1,0:T(8,128)S(1)}, u32[]{:S(2)}, u32[]{:S(2)}) collective-permute-start(f32[8,128]{1,0:T(8,128)S(1)} %merge.1.refs_0_), channel_id=1, source_target_pairs={{0,8},{4,12},{8,0},{12,4},{1,9},{5,13},{9,1},{13,5},{2,10},{6,14},... | collective-permute-start | bytes 12296 | tf_op jit(solution)/shard_map/ppermute | solution.py:525
  116.6 8.8 %collective-permute-start.42 = (bf16[64,2048]{1,0:T(8,128)(2,1)S(1)}, bf16[64,2048]{1,0:T(8,128)(2,1)S(1)}, u32[]{:S(2)}, u32[]{:S(2)}) collective-permute-start(bf16[64,2048]{1,0:T(8,128)(2,1)S(1)} %get-tuple-element.107), channel_id=1, source_target_pairs={{0,2},{1,3},{2,0},{3,1},{4,6},{5,7},{6,4},{7,5},{8,10},{9,11},{10,... | collective-permute-start | bytes 786440 | tf_op jit(solution)/shard_map/ppermute | solution.py:525
  118.0 12.4 %collective-permute-start.41 = (bf16[64,2176]{1,0:T(8,128)(2,1)S(1)}, bf16[64,2176]{1,0:T(8,128)(2,1)S(1)}, u32[]{:S(2)}, u32[]{:S(2)}) collective-permute-start(bf16[64,2176]{1,0:T(8,128)(2,1)S(1)} %get-tuple-element.106), channel_id=1, source_target_pairs={{0,2},{1,3},{2,0},{3,1},{4,6},{5,7},{6,4},{7,5},{8,10},{9,11},{10,... | collective-permute-start | bytes 835592 | tf_op jit(solution)/shard_map/ppermute | solution.py:525
  118.7 7.2 %collective-permute-start.43 = (bf16[64,2048]{1,0:T(8,128)(2,1)S(1)}, bf16[64,2048]{1,0:T(8,128)(2,1)S(1)}, u32[]{:S(2)}, u32[]{:S(2)}) collective-permute-start(bf16[64,2048]{1,0:T(8,128)(2,1)S(1)} %get-tuple-element.107), channel_id=1, source_target_pairs={{0,1},{1,0},{2,3},{3,2},{4,5},{5,4},{6,7},{7,6},{8,9},{9,8},{10,11... | collective-permute-start | bytes 786440 | tf_op jit(solution)/shard_map/ppermute | solution.py:525
  125.4 10.7 %collective-permute-start.45 = (bf16[64,2176]{1,0:T(8,128)(2,1)S(1)}, bf16[64,2176]{1,0:T(8,128)(2,1)S(1)}, u32[]{:S(2)}, u32[]{:S(2)}) collective-permute-start(bf16[64,2176]{1,0:T(8,128)(2,1)S(1)} %get-tuple-element.106), channel_id=1, source_target_pairs={{0,1},{1,0},{2,3},{3,2},{4,5},{5,4},{6,7},{7,6},{8,9},{9,8},{10,11... | collective-permute-start | bytes 835592 | tf_op jit(solution)/shard_map/ppermute | solution.py:525
  130.4 5.8 %collective-permute-start.46 = (bf16[64,2176]{1,0:T(8,128)(2,1)S(1)}, bf16[64,2176]{1,0:T(8,128)(2,1)S(1)}, u32[]{:S(2)}, u32[]{:S(2)}) collective-permute-start(bf16[64,2176]{1,0:T(8,128)(2,1)S(1)} %tie.23), channel_id=1, source_target_pairs={{0,1},{1,0},{2,3},{3,2},{4,5},{5,4},{6,7},{7,6},{8,9},{9,8},{10,11... | collective-permute-start | bytes 835592 | tf_op jit(solution)/shard_map/ppermute | solution.py:525
  130.6 9.1 %collective-permute-start.47 = (bf16[2,4,16,1024]{3,2,1,0:T(8,128)(2,1)S(1)}, bf16[2,4,16,1024]{3,2,1,0:T(8,128)(2,1)S(1)}, u32[]{:S(2)}, u32[]{:S(2)}) collective-permute-start(bf16[2,4,16,1024]{3,2,1,0:T(8,128)(2,1)S(1)} %get-tuple-element.112), channel_id=1, source_target_pairs={{0,4},{4,0},{8,12},{12,8},{1,5},{5,1},{9,13},{13,9},{2,6},{6,2},{1... | collective-permute-start | bytes 786440 | tf_op jit(solution)/shard_map/ppermute | solution.py:525
  135.6 12.5 %collective-permute-start.49 = (bf16[2,4,16,1024]{3,2,1,0:T(8,128)(2,1)S(1)}, bf16[2,4,16,1024]{3,2,1,0:T(8,128)(2,1)S(1)}, u32[]{:S(2)}, u32[]{:S(2)}) collective-permute-start(bf16[2,4,16,1024]{3,2,1,0:T(8,128)(2,1)S(1)} %get-tuple-element.113), channel_id=1, source_target_pairs={{0,4},{4,0},{8,12},{12,8},{1,5},{5,1},{9,13},{13,9},{2,6},{6,2},{1... | collective-permute-start | bytes 786440 | tf_op jit(solution)/shard_map/ppermute | solution.py:525
  139.8 8.3 %collective-permute-start.51 = (bf16[1,4,16,1024]{3,2,1,0:T(8,128)(2,1)S(1)}, bf16[1,4,16,1024]{3,2,1,0:T(8,128)(2,1)S(1)}, u32[]{:S(2)}, u32[]{:S(2)}) collective-permute-start(bf16[1,4,16,1024]{3,2,1,0:T(8,128)(2,1)S(1)} %fold.22.refs_5_), channel_id=1, source_target_pairs={{0,8},{4,12},{8,0},{12,4},{1,9},{5,13},{9,1},{13,5},{2,10},{6,14},... | collective-permute-start | bytes 393224 | tf_op jit(solution)/shard_map/ppermute | solution.py:525
  142.5 12.6 %collective-permute-start.48 = (bf16[2,4,16,1024]{3,2,1,0:T(8,128)(2,1)S(1)}, bf16[2,4,16,1024]{3,2,1,0:T(8,128)(2,1)S(1)}, u32[]{:S(2)}, u32[]{:S(2)}) collective-permute-start(bf16[2,4,16,1024]{3,2,1,0:T(8,128)(2,1)S(1)} %tie.24), channel_id=1, source_target_pairs={{0,4},{4,0},{8,12},{12,8},{1,5},{5,1},{9,13},{13,9},{2,6},{6,2},{1... | collective-permute-start | bytes 786440 | tf_op jit(solution)/shard_map/ppermute | solution.py:525
  148.1 15.9 %collective-permute-start.52 = (bf16[2,4,16,1024]{3,2,1,0:T(8,128)(2,1)S(1)}, bf16[2,4,16,1024]{3,2,1,0:T(8,128)(2,1)S(1)}, u32[]{:S(2)}, u32[]{:S(2)}) collective-permute-start(bf16[2,4,16,1024]{3,2,1,0:T(8,128)(2,1)S(1)} %tie.25), channel_id=1, source_target_pairs={{0,4},{4,0},{8,12},{12,8},{1,5},{5,1},{9,13},{13,9},{2,6},{6,2},{1... | collective-permute-start | bytes 786440 | tf_op jit(solution)/shard_map/ppermute | solution.py:525
  151.0 13.3 %collective-permute-start.54 = (bf16[1,4,16,1024]{3,2,1,0:T(8,128)(2,1)S(1)}, bf16[1,4,16,1024]{3,2,1,0:T(8,128)(2,1)S(1)}, u32[]{:S(2)}, u32[]{:S(2)}) collective-permute-start(bf16[1,4,16,1024]{3,2,1,0:T(8,128)(2,1)S(1)} %fold.23.refs_2_), channel_id=1, source_target_pairs={{0,8},{4,12},{8,0},{12,4},{1,9},{5,13},{9,1},{13,5},{2,10},{6,14},... | collective-permute-start | bytes 393224 | tf_op jit(solution)/shard_map/ppermute | solution.py:525
  155.3 14.9 %collective-permute-start.50 = (bf16[1,4,16,1024]{3,2,1,0:T(8,128)(2,1)S(1)}, bf16[1,4,16,1024]{3,2,1,0:T(8,128)(2,1)S(1)}, u32[]{:S(2)}, u32[]{:S(2)}) collective-permute-start(bf16[1,4,16,1024]{3,2,1,0:T(8,128)(2,1)S(1)} %fold.24.refs_3_), channel_id=1, source_target_pairs={{0,8},{4,12},{8,0},{12,4},{1,9},{5,13},{9,1},{13,5},{2,10},{6,14},... | collective-permute-start | bytes 393224 | tf_op jit(solution)/shard_map/ppermute | solution.py:525
  164.1 8.5 %collective-permute-start.53 = (bf16[1,4,16,1024]{3,2,1,0:T(8,128)(2,1)S(1)}, bf16[1,4,16,1024]{3,2,1,0:T(8,128)(2,1)S(1)}, u32[]{:S(2)}, u32[]{:S(2)}) collective-permute-start(bf16[1,4,16,1024]{3,2,1,0:T(8,128)(2,1)S(1)} %fold.25.refs_4_), channel_id=1, source_target_pairs={{0,8},{4,12},{8,0},{12,4},{1,9},{5,13},{9,1},{13,5},{2,10},{6,14},... | collective-permute-start | bytes 393224 | tf_op jit(solution)/shard_map/ppermute | solution.py:525
  (15 other events, 84.0 us)

commit v20 on v18

--- a/solution.py
+++ b/solution.py
@@ -567,7 +567,7 @@
 GROUPS = [[0, 1], [2], [3], [4]]
 ORDER = [
     "P0", "P1", "F0", "P2", "F1", "P3", "F2", "A0", "F3", "P4", "A1", "F4", "T0", "G0", "A2",
-    "T1", "A3", "G1", "T2", "T3", "G2", "E0", "G3", "E1", "E2", "E3",
+    "T1", "A3", "G1", "T2", "T3", "G2", "G3", "E0", "E1", "E2", "E3",
 ]
 
 

time: 167 us -> 169 us (1.012)
  waiting for transfers between devices: 37.3 us -> 39.7 us
    ppermute x55, waiting for transfers between devices: 37.3 us -> 39.7 us  [swap(): lax.ppermute(x, axis, [(i, i ^ 1 << bit) for i in range(lax.axis_size(axi...]
  transfers between devices with their start and end apart: 55 -> 55, of which waited for: 16 -> 19; matrix products, arithmetic and copies ran while one was open for 0% -> 0% of each run, Pallas kernels for 44% -> 43%
where the time goes in v20:
time: 169 us; the launch traced here: 168 us
  Pallas kernels  81.5 us (48%)
  starting transfers between devices  44.1 us (26%)
  waiting for transfers between devices  39.7 us (23%)
  local copies, waits for them, and re-layouts  2.4 us (1%)
    ppermute x55, starting transfers between devices, swap(): lax.ppermute(x, axis, [(i, i ^ 1 << bit) for i in range(lax.axis_size(axi...  44.1 us
    ppermute x55, waiting for transfers between devices, swap(): lax.ppermute(x, axis, [(i, i ^ 1 << bit) for i in range(lax.axis_size(axi...  39.7 us
    pallas_call x5, Pallas kernels, project(): pl.pallas_call(functools.partial(project_kernel, parts, owners, len(after...  37.9 us
    pallas_call x4, Pallas kernels, output(): pl.pallas_call(functools.partial(output_kernel, owners, slots, len(after)...  13.9 us
    pallas_call x4, Pallas kernels, attend(): pl.pallas_call(functools.partial(attend_kernel, owners, len(counts)), gri...  12.4 us
    pallas_call x3, Pallas kernels, close(): pl.pallas_call(functools.partial(close_kernel, [len(terms) for terms in g...  6.66 us
    pallas_call x13, Pallas kernels, fold(): pl.pallas_call(functools.partial(fold_kernel, len(terms)), grid=(steps,),...  4.73 us
    pallas_call x4, Pallas kernels, activate(): pl.pallas_call(functools.partial(activate_kernel, [len(terms) for terms i...  3.41 us
  transfers between devices with their start and end apart: 55, of which 19 were waited for; matrix products, arithmetic and copies ran while one was open for 0% of the time, Pallas kernels for 43%

profile of v20, /device:TPU:0, one launch (start us, length us, event | category | flops | bytes accessed | tf_op | source)
XLA Modules:
  0.0 168.4 jit_solution(18277562254568271733)
XLA Ops:
  0.0 5.5 %project.5 = (bf16[2,4,128,256]{3,2,1,0:T(8,128)(2,1)S(1)}, bf16[1,4,128,256]{3,2,1,0:T(8,128)(2,1)S(1)}, bf16[1,4,128,256]{3,2,1,0:T(8,128)(2,1)S(1)}) custom-call(s32[1]{0:T(128)} %bitcast.at_ref, bf16[4,2,4,16,2048]{4,3,2,1,0:T(8,128)(2,1)} %bitcast.57, bf16[4,2,4,16,2048]{4,3,2,1,0:T(8,128)(2,1)} %bitcast.58, bf16[4,2,4,16,2048]{4,3,2,1,0:T(8,128)(2,1)} %bitcast.59, ...), custom_call_target="tpu_custom_call" | custom-call | flops 1000 | bytes 1000 | tf_op jit(solution)/shard_map/project/pallas_call | solution.py:80
  6.1 8.7 %project.6 = (bf16[2,4,128,512]{3,2,1,0:T(8,128)(2,1)S(1)}, bf16[1,4,128,512]{3,2,1,0:T(8,128)(2,1)S(1)}, bf16[1,4,128,512]{3,2,1,0:T(8,128)(2,1)S(1)}) custom-call(s32[1]{0:T(128)} %bitcast.at_ref, bf16[4,2,4,16,2048]{4,3,2,1,0:T(8,128)(2,1)} %bitcast.61, bf16[4,2,4,16,2048]{4,3,2,1,0:T(8,128)(2,1)} %bitcast.62, bf16[4,2,4,16,2048]{4,3,2,1,0:T(8,128)(2,1)} %bitcast.63, ...), custom_call_target="tpu_custom_call" | custom-call | flops 1000 | bytes 1000 | tf_op jit(solution)/shard_map/project/pallas_call | solution.py:80
  15.8 3.0 %collective-permute-start.4 = (bf16[1,4,128,256]{3,2,1,0:T(8,128)(2,1)S(1)}, bf16[1,4,128,256]{3,2,1,0:T(8,128)(2,1)S(1)}, u32[]{:S(2)}, u32[]{:S(2)}) collective-permute-start(bf16[1,4,128,256]{3,2,1,0:T(8,128)(2,1)S(1)} %fold.13.refs_8_), channel_id=1, source_target_pairs={{0,2},{1,3},{2,0},{3,1},{4,6},{5,7},{6,4},{7,5},{8,10},{9,11},{10,... | collective-permute-start | bytes 786440 | tf_op jit(solution)/shard_map/ppermute | solution.py:525
  18.7 8.7 %project.7 = (bf16[2,4,128,512]{3,2,1,0:T(8,128)(2,1)S(1)}, bf16[1,4,128,512]{3,2,1,0:T(8,128)(2,1)S(1)}, bf16[1,4,128,512]{3,2,1,0:T(8,128)(2,1)S(1)}) custom-call(s32[1]{0:T(128)} %bitcast.at_ref, bf16[4,2,4,16,2048]{4,3,2,1,0:T(8,128)(2,1)} %bitcast.68, bf16[4,2,4,16,2048]{4,3,2,1,0:T(8,128)(2,1)} %bitcast.66, bf16[4,2,4,16,2048]{4,3,2,1,0:T(8,128)(2,1)} %bitcast.67, ...), custom_call_target="tpu_custom_call" | custom-call | flops 1000 | bytes 1000 | tf_op jit(solution)/shard_map/project/pallas_call | solution.py:80
  28.5 8.8 %project.8 = (bf16[2,4,128,512]{3,2,1,0:T(8,128)(2,1)S(1)}, bf16[1,4,128,512]{3,2,1,0:T(8,128)(2,1)S(1)}, bf16[1,4,128,512]{3,2,1,0:T(8,128)(2,1)S(1)}) custom-call(s32[1]{0:T(128)} %bitcast.at_ref, bf16[4,2,4,16,2048]{4,3,2,1,0:T(8,128)(2,1)} %bitcast.69, bf16[4,2,4,16,2048]{4,3,2,1,0:T(8,128)(2,1)} %bitcast.70, bf16[4,2,4,16,2048]{4,3,2,1,0:T(8,128)(2,1)} %bitcast.71, ...), custom_call_target="tpu_custom_call" | custom-call | flops 1000 | bytes 1000 | tf_op jit(solution)/shard_map/project/pallas_call | solution.py:80
  39.1 1.9 %collective-permute-start.12 = (bf16[1,4,128,512]{3,2,1,0:T(8,128)(2,1)}, bf16[1,4,128,512]{3,2,1,0:T(8,128)(2,1)}, u32[]{:S(2)}, u32[]{:S(2)}) collective-permute-start(bf16[1,4,128,512]{3,2,1,0:T(8,128)(2,1)} %fold.15.refs_6_), channel_id=1, source_target_pairs={{0,2},{1,3},{2,0},{3,1},{4,6},{5,7},{6,4},{7,5},{8,10},{9,11},{10,... | collective-permute-start | bytes 1572872 | tf_op jit(solution)/shard_map/ppermute | solution.py:525
  41.0 1.4 collective-permute-done.8.refs_5_
  44.2 1.7 %collective-permute-start.17 = (bf16[1,4,128,512]{3,2,1,0:T(8,128)(2,1)}, bf16[1,4,128,512]{3,2,1,0:T(8,128)(2,1)}, u32[]{:S(2)}, u32[]{:S(2)}) collective-permute-start(bf16[1,4,128,512]{3,2,1,0:T(8,128)(2,1)} %fold.16.refs_8_), channel_id=1, source_target_pairs={{0,2},{1,3},{2,0},{3,1},{4,6},{5,7},{6,4},{7,5},{8,10},{9,11},{10,... | collective-permute-start | bytes 1572872 | tf_op jit(solution)/shard_map/ppermute | solution.py:525
  45.9 6.1 %project.9 = (bf16[2,4,128,256]{3,2,1,0:T(8,128)(2,1)S(1)}, bf16[1,4,128,256]{3,2,1,0:T(8,128)(2,1)S(1)}, bf16[1,4,128,256]{3,2,1,0:T(8,128)(2,1)}) custom-call(s32[1]{0:T(128)} %bitcast.at_ref, bf16[4,2,4,16,2048]{4,3,2,1,0:T(8,128)(2,1)} %bitcast.73, bf16[4,2,4,16,2048]{4,3,2,1,0:T(8,128)(2,1)} %bitcast.74, bf16[4,2,4,16,2048]{4,3,2,1,0:T(8,128)(2,1)} %bitcast.75, ...), custom_call_target="tpu_custom_call" | custom-call | flops 1000 | bytes 1000 | tf_op jit(solution)/shard_map/project/pallas_call | solution.py:80
  53.3 5.0 %collective-permute-done.18.refs_1_ = bf16[128,768]{1,0:T(8,128)(2,1)S(1)} collective-permute-done((bf16[128,768]{1,0:T(8,128)(2,1)S(1)}, bf16[128,768]{1,0:T(8,128)(2,1)S(1)}, u32[]{:S(2)}, u32[]{:S(2)}) %collective-permute-start.18) | collective-permute-done | bytes 196640 | tf_op jit(solution)/shard_map/ppermute | solution.py:525
  58.5 1.0 copy-done.3
  59.6 1.4 activate.5
  60.9 1.1 fold.17.refs_10_
  62.1 4.1 %attend.4 = (bf16[2,128,768]{2,1,0:T(8,128)(2,1)S(1)}, bf16[1,128,768]{2,1,0:T(8,128)(2,1)S(1)}, bf16[1,128,768]{2,1,0:T(8,128)(2,1)S(1)}) custom-call(s32[1]{0:T(128)} %bitcast.at_ref, bf16[128,768]{1,0:T(8,128)(2,1)S(1)} %get-tuple-element.74.refs_2_.refs_0_.q_ref, bf16[128,768]{1,0:T(8,128)(2,1)S(1)} %collective-permute-done.18.refs_1_, ...), custom_call_target="tpu_custom_call" | custom-call | flops 1000 | bytes 1000 | tf_op jit(solution)/shard_map/attend/pallas_call | solution.py:262
  66.7 1.8 %collective-permute-start.14 = (bf16[128,512]{1,0:T(8,128)(2,1)S(1)}, bf16[128,512]{1,0:T(8,128)(2,1)S(1)}, u32[]{:S(2)}, u32[]{:S(2)}) collective-permute-start(bf16[128,512]{1,0:T(8,128)(2,1)S(1)} %get-tuple-element.79.refs_2_.refs_0_.q_ref), channel_id=1, source_target_pairs={{0,2},{1,3},{2,0},{3,1},{4,6},{5,7},{6,4},{7,5},{8,10},{9,11},{10,... | collective-permute-start | bytes 393224 | tf_op jit(solution)/shard_map/ppermute | solution.py:525
  68.8 4.0 %collective-permute-done.14.refs_1_ = bf16[128,512]{1,0:T(8,128)(2,1)S(1)} collective-permute-done((bf16[128,512]{1,0:T(8,128)(2,1)S(1)}, bf16[128,512]{1,0:T(8,128)(2,1)S(1)}, u32[]{:S(2)}, u32[]{:S(2)}) %collective-permute-start.14) | collective-permute-done | bytes 131104 | tf_op jit(solution)/shard_map/ppermute | solution.py:525
  73.5 1.4 activate.6
  74.9 2.1 %collective-permute-start.25 = (bf16[128,512]{1,0:T(8,128)(2,1)S(1)}, bf16[128,512]{1,0:T(8,128)(2,1)S(1)}, u32[]{:S(2)}, u32[]{:S(2)}) collective-permute-start(bf16[128,512]{1,0:T(8,128)(2,1)S(1)} %get-tuple-element.82.refs_10_.refs_0_.q_ref), channel_id=1, source_target_pairs={{0,2},{1,3},{2,0},{3,1},{4,6},{5,7},{6,4},{7,5},{8,10},{9,11},{10,... | collective-permute-start | bytes 393224 | tf_op jit(solution)/shard_map/ppermute | solution.py:525
  77.0 3.1 %attend.5 = (bf16[2,128,512]{2,1,0:T(8,128)(2,1)S(1)}, bf16[1,128,512]{2,1,0:T(8,128)(2,1)S(1)}, bf16[1,128,512]{2,1,0:T(8,128)(2,1)S(1)}) custom-call(s32[1]{0:T(128)} %bitcast.at_ref, bf16[128,512]{1,0:T(8,128)(2,1)S(1)} %get-tuple-element.79.refs_2_.refs_0_.q_ref, bf16[128,512]{1,0:T(8,128)(2,1)S(1)} %collective-permute-done.14.refs_1_, ...), custom_call_target="tpu_custom_call" | custom-call | flops 1000 | bytes 1000 | tf_op jit(solution)/shard_map/attend/pallas_call | solution.py:262
  81.0 1.7 collective-permute-start.22
  83.1 3.2 %attend.6 = (bf16[2,128,512]{2,1,0:T(8,128)(2,1)S(1)}, bf16[1,128,512]{2,1,0:T(8,128)(2,1)S(1)}, bf16[1,128,512]{2,1,0:T(8,128)(2,1)S(1)}) custom-call(s32[1]{0:T(128)} %bitcast.at_ref, bf16[128,512]{1,0:T(8,128)(2,1)S(1)} %get-tuple-element.82.refs_10_.refs_0_.q_ref, bf16[128,512]{1,0:T(8,128)(2,1)S(1)} %collective-permute-done.25.refs_1_, ...), custom_call_target="tpu_custom_call" | custom-call | flops 1000 | bytes 1000 | tf_op jit(solution)/shard_map/attend/pallas_call | solution.py:262
  88.1 2.1 %attend.7 = (bf16[2,128,256]{2,1,0:T(8,128)(2,1)S(1)}, bf16[1,128,256]{2,1,0:T(8,128)(2,1)S(1)}, bf16[1,128,256]{2,1,0:T(8,128)(2,1)S(1)}) custom-call(s32[1]{0:T(128)} %bitcast.at_ref, bf16[128,256]{1,0:T(8,128)(2,1)S(1)} %get-tuple-element.84.refs_2_.refs_0_.q_ref, bf16[128,256]{1,0:T(8,128)(2,1)S(1)} %collective-permute-done.22.refs_1_, ...), custom_call_target="tpu_custom_call" | custom-call | flops 1000 | bytes 1000 | tf_op jit(solution)/shard_map/attend/pallas_call | solution.py:262
  90.8 1.1 collective-permute-start.36
  96.0 1.5 collective-permute-done.36.refs_2_
  97.9 2.4 %collective-permute-done.38.refs_2_ = bf16[1,128,512]{2,1,0:T(8,128)(2,1)S(1)} collective-permute-done((bf16[1,128,512]{2,1,0:T(8,128)(2,1)S(1)}, bf16[1,128,512]{2,1,0:T(8,128)(2,1)S(1)}, u32[]{:S(2)}, u32[]{:S(2)}) %collective-permute-start.38) | collective-permute-done | bytes 131104 | tf_op jit(solution)/shard_map/ppermute | solution.py:525
  101.7 1.6 collective-permute-start.39
  103.3 2.0 %collective-permute-done.39.refs_1_ = f32[8,128]{1,0:T(8,128)S(1)} collective-permute-done((f32[8,128]{1,0:T(8,128)S(1)}, f32[8,128]{1,0:T(8,128)S(1)}, u32[]{:S(2)}, u32[]{:S(2)}) %collective-permute-start.39) | collective-permute-done | bytes 4128 | tf_op jit(solution)/shard_map/ppermute | solution.py:525
  105.3 2.6 %collective-permute-start.40 = (f32[8,128]{1,0:T(8,128)S(1)}, f32[8,128]{1,0:T(8,128)S(1)}, u32[]{:S(2)}, u32[]{:S(2)}) collective-permute-start(f32[8,128]{1,0:T(8,128)S(1)} %merge.1.refs_0_), channel_id=1, source_target_pairs={{0,8},{4,12},{8,0},{12,4},{1,9},{5,13},{9,1},{13,5},{2,10},{6,14},... | collective-permute-start | bytes 12296 | tf_op jit(solution)/shard_map/ppermute | solution.py:525
  107.9 1.9 %collective-permute-done.40.refs_1_ = f32[8,128]{1,0:T(8,128)S(1)} collective-permute-done((f32[8,128]{1,0:T(8,128)S(1)}, f32[8,128]{1,0:T(8,128)S(1)}, u32[]{:S(2)}, u32[]{:S(2)}) %collective-permute-start.40) | collective-permute-done | bytes 4128 | tf_op jit(solution)/shard_map/ppermute | solution.py:525
  111.2 1.2 collective-permute-start.41
  112.3 6.5 %collective-permute-done.42 = bf16[64,2048]{1,0:T(8,128)(2,1)S(1)} collective-permute-done((bf16[64,2048]{1,0:T(8,128)(2,1)S(1)}, bf16[64,2048]{1,0:T(8,128)(2,1)S(1)}, u32[]{:S(2)}, u32[]{:S(2)}) %collective-permute-start.42) | collective-permute-done | bytes 262176 | tf_op jit(solution)/shard_map/ppermute | solution.py:525
  120.4 3.4 %output.4 = (bf16[2,4,16,1024]{3,2,1,0:T(8,128)(2,1)S(1)}, bf16[2,4,16,1024]{3,2,1,0:T(8,128)(2,1)S(1)}) custom-call(s32[1]{0:T(128)} %bitcast.3.index_ref, bf16[4,16,2048]{2,1,0:T(8,128)(2,1)S(1)} %bitcast.47, bf16[4,16,2048]{2,1,0:T(8,128)(2,1)S(1)} %bitcast.49, bf16[4,16,2048]{2,1,0:T(8,128)(2,1)S(1)} %bitcast.51, bf16[4,16,2048]{2,1,0:T(8,128)(2,1)S(1)} %bitcast.53, ...), custom_call_target="tpu_custom_call" | custom-call | flops 1000 | bytes 1000 | tf_op jit(solution)/shard_map/output/pallas_call | solution.py:444
  124.0 1.6 collective-permute-start.47
  125.6 3.4 %output.5 = (bf16[2,4,16,1024]{3,2,1,0:T(8,128)(2,1)S(1)}, bf16[2,4,16,1024]{3,2,1,0:T(8,128)(2,1)S(1)}) custom-call(s32[1]{0:T(128)} %bitcast.3.index_ref, bf16[4,16,2048]{2,1,0:T(8,128)(2,1)S(1)} %bitcast.48, bf16[4,16,2048]{2,1,0:T(8,128)(2,1)S(1)} %bitcast.50, bf16[4,16,2048]{2,1,0:T(8,128)(2,1)S(1)} %bitcast.52, bf16[4,16,2048]{2,1,0:T(8,128)(2,1)S(1)} %bitcast.54, ...), custom_call_target="tpu_custom_call" | custom-call | flops 1000 | bytes 1000 | tf_op jit(solution)/shard_map/output/pallas_call | solution.py:444
  129.6 3.5 %output.6 = (bf16[2,4,16,1024]{3,2,1,0:T(8,128)(2,1)S(1)}, bf16[2,4,16,1024]{3,2,1,0:T(8,128)(2,1)S(1)}) custom-call(s32[1]{0:T(128)} %bitcast.3.index_ref, bf16[4,16,2176]{2,1,0:T(8,128)(2,1)S(1)} %bitcast.41, bf16[4,16,2176]{2,1,0:T(8,128)(2,1)S(1)} %bitcast.39, bf16[4,16,2176]{2,1,0:T(8,128)(2,1)S(1)} %bitcast.43, bf16[4,16,2176]{2,1,0:T(8,128)(2,1)S(1)} %bitcast.45, ...), custom_call_target="tpu_custom_call" | custom-call | flops 1000 | bytes 1000 | tf_op jit(solution)/shard_map/output/pallas_call | solution.py:444
  133.3 2.7 %collective-permute-start.51 = (bf16[1,4,16,1024]{3,2,1,0:T(8,128)(2,1)S(1)}, bf16[1,4,16,1024]{3,2,1,0:T(8,128)(2,1)S(1)}, u32[]{:S(2)}, u32[]{:S(2)}) collective-permute-start(bf16[1,4,16,1024]{3,2,1,0:T(8,128)(2,1)S(1)} %fold.22.refs_5_), channel_id=1, source_target_pairs={{0,8},{4,12},{8,0},{12,4},{1,9},{5,13},{9,1},{13,5},{2,10},{6,14},... | collective-permute-start | bytes 393224 | tf_op jit(solution)/shard_map/ppermute | solution.py:525
  136.0 1.6 collective-permute-start.48
  137.5 3.5 %output.7 = (bf16[2,4,16,1024]{3,2,1,0:T(8,128)(2,1)S(1)}, bf16[2,4,16,1024]{3,2,1,0:T(8,128)(2,1)S(1)}) custom-call(s32[1]{0:T(128)} %bitcast.3.index_ref, bf16[4,16,2176]{2,1,0:T(8,128)(2,1)S(1)} %bitcast.42, bf16[4,16,2176]{2,1,0:T(8,128)(2,1)S(1)} %bitcast.40, bf16[4,16,2176]{2,1,0:T(8,128)(2,1)S(1)} %bitcast.44, bf16[4,16,2176]{2,1,0:T(8,128)(2,1)S(1)} %bitcast.46, ...), custom_call_target="tpu_custom_call" | custom-call | flops 1000 | bytes 1000 | tf_op jit(solution)/shard_map/output/pallas_call | solution.py:444
  141.6 2.6 %collective-permute-start.52 = (bf16[2,4,16,1024]{3,2,1,0:T(8,128)(2,1)S(1)}, bf16[2,4,16,1024]{3,2,1,0:T(8,128)(2,1)S(1)}, u32[]{:S(2)}, u32[]{:S(2)}) collective-permute-start(bf16[2,4,16,1024]{3,2,1,0:T(8,128)(2,1)S(1)} %tie.25), channel_id=1, source_target_pairs={{0,4},{4,0},{8,12},{12,8},{1,5},{5,1},{9,13},{13,9},{2,6},{6,2},{1... | collective-permute-start | bytes 786440 | tf_op jit(solution)/shard_map/ppermute | solution.py:525
  144.4 2.4 %collective-permute-start.54 = (bf16[1,4,16,1024]{3,2,1,0:T(8,128)(2,1)S(1)}, bf16[1,4,16,1024]{3,2,1,0:T(8,128)(2,1)S(1)}, u32[]{:S(2)}, u32[]{:S(2)}) collective-permute-start(bf16[1,4,16,1024]{3,2,1,0:T(8,128)(2,1)S(1)} %fold.23.refs_2_), channel_id=1, source_target_pairs={{0,8},{4,12},{8,0},{12,4},{1,9},{5,13},{9,1},{13,5},{2,10},{6,14},... | collective-permute-start | bytes 393224 | tf_op jit(solution)/shard_map/ppermute | solution.py:525
  146.8 1.9 %collective-permute-done.48.refs_1_ = bf16[2,4,16,1024]{3,2,1,0:T(8,128)(2,1)S(1)} collective-permute-done((bf16[2,4,16,1024]{3,2,1,0:T(8,128)(2,1)S(1)}, bf16[2,4,16,1024]{3,2,1,0:T(8,128)(2,1)S(1)}, u32[]{:S(2)}, u32[]{:S(2)}) %collective-permute-start.48) | collective-permute-done | bytes 262176 | tf_op jit(solution)/shard_map/ppermute | solution.py:525
  148.8 3.1 %collective-permute-start.50 = (bf16[1,4,16,1024]{3,2,1,0:T(8,128)(2,1)S(1)}, bf16[1,4,16,1024]{3,2,1,0:T(8,128)(2,1)S(1)}, u32[]{:S(2)}, u32[]{:S(2)}) collective-permute-start(bf16[1,4,16,1024]{3,2,1,0:T(8,128)(2,1)S(1)} %fold.24.refs_3_), channel_id=1, source_target_pairs={{0,8},{4,12},{8,0},{12,4},{1,9},{5,13},{9,1},{13,5},{2,10},{6,14},... | collective-permute-start | bytes 393224 | tf_op jit(solution)/shard_map/ppermute | solution.py:525
  151.9 2.2 %close.3 = (bf16[8,16,2048]{2,1,0:T(8,128)(2,1)}, f32[8,128]{1,0:T(8,128)S(1)}) custom-call(s32[2]{0:T(128)S(1)} %pad_add_fusion.1.at_ref, bf16[32,16,2048]{2,1,0:T(8,128)(2,1)} %bitcast.77, bf16[2,4,16,1024]{3,2,1,0:T(8,128)(2,1)S(1)} %get-tuple-element.108.refs_1_.refs_5_.refs_0_, bf16[2,4,16,1024]{3,2,1,0:T(8,128)(2,1)S(1)} %collective-permute-done.47.refs_1_, ...), custom_call_target="tpu_custom_call" | custom-call | flops 1000 | bytes 1000 | tf_op jit(solution)/shard_map/close/pallas_call | solution.py:490
  154.1 3.4 %collective-permute-done.52.refs_1_.refs_4_ = bf16[2,4,16,1024]{3,2,1,0:T(8,128)(2,1)S(1)} collective-permute-done((bf16[2,4,16,1024]{3,2,1,0:T(8,128)(2,1)S(1)}, bf16[2,4,16,1024]{3,2,1,0:T(8,128)(2,1)S(1)}, u32[]{:S(2)}, u32[]{:S(2)}) %collective-permute-start.52) | collective-permute-done | bytes 262176 | tf_op jit(solution)/shard_map/ppermute | solution.py:525
  157.8 2.2 %close.4 = (bf16[8,16,2048]{2,1,0:T(8,128)(2,1)}, f32[8,128]{1,0:T(8,128)S(1)}) custom-call(s32[2]{0:T(128)S(1)} %pad_add_fusion.1.at_ref, bf16[32,16,2048]{2,1,0:T(8,128)(2,1)} %bitcast.78, bf16[2,4,16,1024]{3,2,1,0:T(8,128)(2,1)S(1)} %get-tuple-element.109.refs_5_.refs_0_, ...), custom_call_target="tpu_custom_call", output_to_operand_aliasing={{0}: (5, {})} | custom-call | flops 1000 | bytes 1000 | tf_op jit(solution)/shard_map/close/pallas_call | solution.py:490
  159.9 3.7 %collective-permute-done.50.refs_2_ = bf16[1,4,16,1024]{3,2,1,0:T(8,128)(2,1)S(1)} collective-permute-done((bf16[1,4,16,1024]{3,2,1,0:T(8,128)(2,1)S(1)}, bf16[1,4,16,1024]{3,2,1,0:T(8,128)(2,1)S(1)}, u32[]{:S(2)}, u32[]{:S(2)}) %collective-permute-start.50) | collective-permute-done | bytes 131104 | tf_op jit(solution)/shard_map/ppermute | solution.py:525
  163.7 2.4 %collective-permute-done.53.refs_5_ = bf16[1,4,16,1024]{3,2,1,0:T(8,128)(2,1)S(1)} collective-permute-done((bf16[1,4,16,1024]{3,2,1,0:T(8,128)(2,1)S(1)}, bf16[1,4,16,1024]{3,2,1,0:T(8,128)(2,1)S(1)}, u32[]{:S(2)}, u32[]{:S(2)}) %collective-permute-start.53) | collective-permute-done | bytes 131104 | tf_op jit(solution)/shard_map/ppermute | solution.py:525
  166.1 2.3 %close.5 = (bf16[8,16,2048]{2,1,0:T(8,128)(2,1)}, f32[8,128]{1,0:T(8,128)}) custom-call(s32[2]{0:T(128)S(1)} %pad_add_fusion.at_ref, bf16[32,16,2048]{2,1,0:T(8,128)(2,1)} %bitcast.79, bf16[2,4,16,1024]{3,2,1,0:T(8,128)(2,1)S(1)} %get-tuple-element.110.refs_2_.refs_0_, ...), custom_call_target="tpu_custom_call", output_to_operand_aliasing={{0}: (8, {})} | custom-call | flops 1000 | bytes 1000 | tf_op jit(solution)/shard_map/close/pallas_call | solution.py:490
  (137 shorter events, 23.4 us)
Async XLA Ops:
  5.5 9.4 %collective-permute-start = (bf16[1,4,128,256]{3,2,1,0:T(8,128)(2,1)S(1)}, bf16[1,4,128,256]{3,2,1,0:T(8,128)(2,1)S(1)}, u32[]{:S(2)}, u32[]{:S(2)}) collective-permute-start(bf16[1,4,128,256]{3,2,1,0:T(8,128)(2,1)S(1)} %get-tuple-element.66), channel_id=1, source_target_pairs={{0,1},{1,0},{2,3},{3,2},{4,5},{5,4},{6,7},{7,6},{8,9},{9,8},{10,11... | collective-permute-start | bytes 786440 | tf_op jit(solution)/shard_map/ppermute | solution.py:525
  6.1 8.8 %collective-permute-start.1 = (bf16[1,4,128,256]{3,2,1,0:T(8,128)(2,1)S(1)}, bf16[1,4,128,256]{3,2,1,0:T(8,128)(2,1)S(1)}, u32[]{:S(2)}, u32[]{:S(2)}) collective-permute-start(bf16[1,4,128,256]{3,2,1,0:T(8,128)(2,1)S(1)} %get-tuple-element.67), channel_id=1, source_target_pairs={{0,1},{1,0},{2,3},{3,2},{4,5},{5,4},{6,7},{7,6},{8,9},{9,8},{10,11... | collective-permute-start | bytes 786440 | tf_op jit(solution)/shard_map/ppermute | solution.py:525
  14.9 12.6 %collective-permute-start.3 = (bf16[1,4,128,512]{3,2,1,0:T(8,128)(2,1)S(1)}, bf16[1,4,128,512]{3,2,1,0:T(8,128)(2,1)S(1)}, u32[]{:S(2)}, u32[]{:S(2)}) collective-permute-start(bf16[1,4,128,512]{3,2,1,0:T(8,128)(2,1)S(1)} %tie.14), channel_id=1, source_target_pairs={{0,1},{1,0},{2,3},{3,2},{4,5},{5,4},{6,7},{7,6},{8,9},{9,8},{10,11... | collective-permute-start | bytes 1572872 | tf_op jit(solution)/shard_map/ppermute | solution.py:525
  15.4 12.1 %collective-permute-start.2 = (bf16[1,4,128,512]{3,2,1,0:T(8,128)(2,1)S(1)}, bf16[1,4,128,512]{3,2,1,0:T(8,128)(2,1)S(1)}, u32[]{:S(2)}, u32[]{:S(2)}) collective-permute-start(bf16[1,4,128,512]{3,2,1,0:T(8,128)(2,1)S(1)} %tie.13), channel_id=1, source_target_pairs={{0,1},{1,0},{2,3},{3,2},{4,5},{5,4},{6,7},{7,6},{8,9},{9,8},{10,11... | collective-permute-start | bytes 1572872 | tf_op jit(solution)/shard_map/ppermute | solution.py:525
  15.8 11.7 %collective-permute-start.4 = (bf16[1,4,128,256]{3,2,1,0:T(8,128)(2,1)S(1)}, bf16[1,4,128,256]{3,2,1,0:T(8,128)(2,1)S(1)}, u32[]{:S(2)}, u32[]{:S(2)}) collective-permute-start(bf16[1,4,128,256]{3,2,1,0:T(8,128)(2,1)S(1)} %fold.13.refs_8_), channel_id=1, source_target_pairs={{0,2},{1,3},{2,0},{3,1},{4,6},{5,7},{6,4},{7,5},{8,10},{9,11},{10,... | collective-permute-start | bytes 786440 | tf_op jit(solution)/shard_map/ppermute | solution.py:525
  27.5 9.8 %collective-permute-start.6 = (bf16[1,4,128,512]{3,2,1,0:T(8,128)(2,1)S(1)}, bf16[1,4,128,512]{3,2,1,0:T(8,128)(2,1)S(1)}, u32[]{:S(2)}, u32[]{:S(2)}) collective-permute-start(bf16[1,4,128,512]{3,2,1,0:T(8,128)(2,1)S(1)} %tie.16), channel_id=1, source_target_pairs={{0,1},{1,0},{2,3},{3,2},{4,5},{5,4},{6,7},{7,6},{8,9},{9,8},{10,11... | collective-permute-start | bytes 1572872 | tf_op jit(solution)/shard_map/ppermute | solution.py:525
  27.6 9.7 %collective-permute-start.5 = (bf16[1,4,128,512]{3,2,1,0:T(8,128)(2,1)S(1)}, bf16[1,4,128,512]{3,2,1,0:T(8,128)(2,1)S(1)}, u32[]{:S(2)}, u32[]{:S(2)}) collective-permute-start(bf16[1,4,128,512]{3,2,1,0:T(8,128)(2,1)S(1)} %tie.15), channel_id=1, source_target_pairs={{0,1},{1,0},{2,3},{3,2},{4,5},{5,4},{6,7},{7,6},{8,9},{9,8},{10,11... | collective-permute-start | bytes 1572872 | tf_op jit(solution)/shard_map/ppermute | solution.py:525
  28.4 14.0 %collective-permute-start.8 = (bf16[1,4,128,512]{3,2,1,0:T(8,128)(2,1)S(1)}, bf16[1,4,128,512]{3,2,1,0:T(8,128)(2,1)S(1)}, u32[]{:S(2)}, u32[]{:S(2)}) collective-permute-start(bf16[1,4,128,512]{3,2,1,0:T(8,128)(2,1)S(1)} %fold.14.refs_8_), channel_id=1, source_target_pairs={{0,2},{1,3},{2,0},{3,1},{4,6},{5,7},{6,4},{7,5},{8,10},{9,11},{10,... | collective-permute-start | bytes 1572872 | tf_op jit(solution)/shard_map/ppermute | solution.py:525
  37.3 5.9 %collective-permute-start.7 = (bf16[1,4,128,512]{3,2,1,0:T(8,128)(2,1)S(1)}, bf16[1,4,128,512]{3,2,1,0:T(8,128)(2,1)S(1)}, u32[]{:S(2)}, u32[]{:S(2)}) collective-permute-start(bf16[1,4,128,512]{3,2,1,0:T(8,128)(2,1)S(1)} %tie.17), channel_id=1, source_target_pairs={{0,1},{1,0},{2,3},{3,2},{4,5},{5,4},{6,7},{7,6},{8,9},{9,8},{10,11... | collective-permute-start | bytes 1572872 | tf_op jit(solution)/shard_map/ppermute | solution.py:525
  38.1 14.7 %collective-permute-start.9 = (bf16[1,4,128,512]{3,2,1,0:T(8,128)(2,1)S(1)}, bf16[1,4,128,512]{3,2,1,0:T(8,128)(2,1)S(1)}, u32[]{:S(2)}, u32[]{:S(2)}) collective-permute-start(bf16[1,4,128,512]{3,2,1,0:T(8,128)(2,1)S(1)} %tie.18), channel_id=1, source_target_pairs={{0,1},{1,0},{2,3},{3,2},{4,5},{5,4},{6,7},{7,6},{8,9},{9,8},{10,11... | collective-permute-start | bytes 1572872 | tf_op jit(solution)/shard_map/ppermute | solution.py:525
  39.1 19.4 %collective-permute-start.12 = (bf16[1,4,128,512]{3,2,1,0:T(8,128)(2,1)}, bf16[1,4,128,512]{3,2,1,0:T(8,128)(2,1)}, u32[]{:S(2)}, u32[]{:S(2)}) collective-permute-start(bf16[1,4,128,512]{3,2,1,0:T(8,128)(2,1)} %fold.15.refs_6_), channel_id=1, source_target_pairs={{0,2},{1,3},{2,0},{3,1},{4,6},{5,7},{6,4},{7,5},{8,10},{9,11},{10,... | collective-permute-start | bytes 1572872 | tf_op jit(solution)/shard_map/ppermute | solution.py:525
  42.9 15.5 %collective-permute-start.18 = (bf16[128,768]{1,0:T(8,128)(2,1)S(1)}, bf16[128,768]{1,0:T(8,128)(2,1)S(1)}, u32[]{:S(2)}, u32[]{:S(2)}) collective-permute-start(bf16[128,768]{1,0:T(8,128)(2,1)S(1)} %get-tuple-element.74.refs_2_.refs_0_.q_ref), channel_id=1, source_target_pairs={{0,2},{1,3},{2,0},{3,1},{4,6},{5,7},{6,4},{7,5},{8,10},{9,11},{10,... | collective-permute-start | bytes 589832 | tf_op jit(solution)/shard_map/ppermute | solution.py:525
  44.2 29.3 %collective-permute-start.17 = (bf16[1,4,128,512]{3,2,1,0:T(8,128)(2,1)}, bf16[1,4,128,512]{3,2,1,0:T(8,128)(2,1)}, u32[]{:S(2)}, u32[]{:S(2)}) collective-permute-start(bf16[1,4,128,512]{3,2,1,0:T(8,128)(2,1)} %fold.16.refs_8_), channel_id=1, source_target_pairs={{0,2},{1,3},{2,0},{3,1},{4,6},{5,7},{6,4},{7,5},{8,10},{9,11},{10,... | collective-permute-start | bytes 1572872 | tf_op jit(solution)/shard_map/ppermute | solution.py:525
  52.8 8.1 %collective-permute-start.11 = (bf16[1,4,128,256]{3,2,1,0:T(8,128)(2,1)}, bf16[1,4,128,256]{3,2,1,0:T(8,128)(2,1)}, u32[]{:S(2)}, u32[]{:S(2)}) collective-permute-start(bf16[1,4,128,256]{3,2,1,0:T(8,128)(2,1)} %tie.20), channel_id=1, source_target_pairs={{0,1},{1,0},{2,3},{3,2},{4,5},{5,4},{6,7},{7,6},{8,9},{9,8},{10,11... | collective-permute-start | bytes 786440 | tf_op jit(solution)/shard_map/ppermute | solution.py:525
  52.8 9.2 %collective-permute-start.19 = (bf16[128,768]{1,0:T(8,128)(2,1)S(1)}, bf16[128,768]{1,0:T(8,128)(2,1)}, u32[]{:S(2)}, u32[]{:S(2)}) collective-permute-start(bf16[128,768]{1,0:T(8,128)(2,1)S(1)} %get-tuple-element.74.refs_2_.refs_0_.q_ref), channel_id=1, source_target_pairs={{0,1},{1,0},{2,3},{3,2},{4,5},{5,4},{6,7},{7,6},{8,9},{9,8},{10,11... | collective-permute-start | bytes 589832 | tf_op jit(solution)/shard_map/ppermute | solution.py:525
  58.4 3.7 %collective-permute-start.20 = (bf16[128,768]{1,0:T(8,128)(2,1)S(1)}, bf16[128,768]{1,0:T(8,128)(2,1)}, u32[]{:S(2)}, u32[]{:S(2)}) collective-permute-start(bf16[128,768]{1,0:T(8,128)(2,1)S(1)} %collective-permute-done.18.refs_1_), channel_id=1, source_target_pairs={{0,1},{1,0},{2,3},{3,2},{4,5},{5,4},{6,7},{7,6},{8,9},{9,8},{10,11... | collective-permute-start | bytes 589832 | tf_op jit(solution)/shard_map/ppermute | solution.py:525
  66.2 6.7 %collective-permute-start.21 = (bf16[1,128,768]{2,1,0:T(8,128)(2,1)S(1)}, bf16[1,128,768]{2,1,0:T(8,128)(2,1)S(1)}, u32[]{:S(2)}, u32[]{:S(2)}) collective-permute-start(bf16[1,128,768]{2,1,0:T(8,128)(2,1)S(1)} %get-tuple-element.81), channel_id=1, source_target_pairs={{0,1},{1,0},{2,3},{3,2},{4,5},{5,4},{6,7},{7,6},{8,9},{9,8},{10,11... | collective-permute-start | bytes 589832 | tf_op jit(solution)/shard_map/ppermute | solution.py:525
  66.7 6.1 %collective-permute-start.14 = (bf16[128,512]{1,0:T(8,128)(2,1)S(1)}, bf16[128,512]{1,0:T(8,128)(2,1)S(1)}, u32[]{:S(2)}, u32[]{:S(2)}) collective-permute-start(bf16[128,512]{1,0:T(8,128)(2,1)S(1)} %get-tuple-element.79.refs_2_.refs_0_.q_ref), channel_id=1, source_target_pairs={{0,2},{1,3},{2,0},{3,1},{4,6},{5,7},{6,4},{7,5},{8,10},{9,11},{10,... | collective-permute-start | bytes 393224 | tf_op jit(solution)/shard_map/ppermute | solution.py:525
  68.5 12.3 %collective-permute-start.10 = (bf16[1,4,128,256]{3,2,1,0:T(8,128)(2,1)S(1)}, bf16[1,4,128,256]{3,2,1,0:T(8,128)(2,1)S(1)}, u32[]{:S(2)}, u32[]{:S(2)}) collective-permute-start(bf16[1,4,128,256]{3,2,1,0:T(8,128)(2,1)S(1)} %tie.19), channel_id=1, source_target_pairs={{0,1},{1,0},{2,3},{3,2},{4,5},{5,4},{6,7},{7,6},{8,9},{9,8},{10,11... | collective-permute-start | bytes 786440 | tf_op jit(solution)/shard_map/ppermute | solution.py:525
  68.5 12.3 %collective-permute-start.13 = (bf16[1,4,128,256]{3,2,1,0:T(8,128)(2,1)S(1)}, bf16[1,4,128,256]{3,2,1,0:T(8,128)(2,1)S(1)}, u32[]{:S(2)}, u32[]{:S(2)}) collective-permute-start(bf16[1,4,128,256]{3,2,1,0:T(8,128)(2,1)S(1)} %fold.17.refs_10_), channel_id=1, source_target_pairs={{0,2},{1,3},{2,0},{3,1},{4,6},{5,7},{6,4},{7,5},{8,10},{9,11},{10,... | collective-permute-start | bytes 786440 | tf_op jit(solution)/shard_map/ppermute | solution.py:525
  72.8 4.2 %collective-permute-start.15 = (bf16[128,512]{1,0:T(8,128)(2,1)S(1)}, bf16[128,512]{1,0:T(8,128)(2,1)S(1)}, u32[]{:S(2)}, u32[]{:S(2)}) collective-permute-start(bf16[128,512]{1,0:T(8,128)(2,1)S(1)} %get-tuple-element.79.refs_2_.refs_0_.q_ref), channel_id=1, source_target_pairs={{0,1},{1,0},{2,3},{3,2},{4,5},{5,4},{6,7},{7,6},{8,9},{9,8},{10,11... | collective-permute-start | bytes 393224 | tf_op jit(solution)/shard_map/ppermute | solution.py:525
  72.9 4.2 %collective-permute-start.16 = (bf16[128,512]{1,0:T(8,128)(2,1)S(1)}, bf16[128,512]{1,0:T(8,128)(2,1)S(1)}, u32[]{:S(2)}, u32[]{:S(2)}) collective-permute-start(bf16[128,512]{1,0:T(8,128)(2,1)S(1)} %collective-permute-done.14.refs_1_), channel_id=1, source_target_pairs={{0,1},{1,0},{2,3},{3,2},{4,5},{5,4},{6,7},{7,6},{8,9},{9,8},{10,11... | collective-permute-start | bytes 393224 | tf_op jit(solution)/shard_map/ppermute | solution.py:525
  74.9 5.8 %collective-permute-start.25 = (bf16[128,512]{1,0:T(8,128)(2,1)S(1)}, bf16[128,512]{1,0:T(8,128)(2,1)S(1)}, u32[]{:S(2)}, u32[]{:S(2)}) collective-permute-start(bf16[128,512]{1,0:T(8,128)(2,1)S(1)} %get-tuple-element.82.refs_10_.refs_0_.q_ref), channel_id=1, source_target_pairs={{0,2},{1,3},{2,0},{3,1},{4,6},{5,7},{6,4},{7,5},{8,10},{9,11},{10,... | collective-permute-start | bytes 393224 | tf_op jit(solution)/shard_map/ppermute | solution.py:525
  81.0 5.2 %collective-permute-start.22 = (bf16[128,256]{1,0:T(8,128)(2,1)S(1)}, bf16[128,256]{1,0:T(8,128)(2,1)S(1)}, u32[]{:S(2)}, u32[]{:S(2)}) collective-permute-start(bf16[128,256]{1,0:T(8,128)(2,1)S(1)} %get-tuple-element.84.refs_2_.refs_0_.q_ref), channel_id=1, source_target_pairs={{0,2},{1,3},{2,0},{3,1},{4,6},{5,7},{6,4},{7,5},{8,10},{9,11},{10,... | collective-permute-start | bytes 196616 | tf_op jit(solution)/shard_map/ppermute | solution.py:525
  82.7 9.3 %collective-permute-start.33 = (bf16[1,128,768]{2,1,0:T(8,128)(2,1)S(1)}, bf16[1,128,768]{2,1,0:T(8,128)(2,1)S(1)}, u32[]{:S(2)}, u32[]{:S(2)}) collective-permute-start(bf16[1,128,768]{2,1,0:T(8,128)(2,1)S(1)} %get-tuple-element.93), channel_id=1, source_target_pairs={{0,1},{1,0},{2,3},{3,2},{4,5},{5,4},{6,7},{7,6},{8,9},{9,8},{10,11... | collective-permute-start | bytes 589832 | tf_op jit(solution)/shard_map/ppermute | solution.py:525
  86.3 4.5 %collective-permute-start.31 = (bf16[1,128,512]{2,1,0:T(8,128)(2,1)S(1)}, bf16[1,128,512]{2,1,0:T(8,128)(2,1)S(1)}, u32[]{:S(2)}, u32[]{:S(2)}) collective-permute-start(bf16[1,128,512]{2,1,0:T(8,128)(2,1)S(1)} %tie.21), channel_id=1, source_target_pairs={{0,1},{1,0},{2,3},{3,2},{4,5},{5,4},{6,7},{7,6},{8,9},{9,8},{10,11... | collective-permute-start | bytes 393224 | tf_op jit(solution)/shard_map/ppermute | solution.py:525
  87.1 7.5 %collective-permute-start.34 = (bf16[1,128,768]{2,1,0:T(8,128)(2,1)S(1)}, bf16[1,128,768]{2,1,0:T(8,128)(2,1)S(1)}, u32[]{:S(2)}, u32[]{:S(2)}) collective-permute-start(bf16[1,128,768]{2,1,0:T(8,128)(2,1)S(1)} %fold.18.refs_3_), channel_id=1, source_target_pairs={{0,2},{1,3},{2,0},{3,1},{4,6},{5,7},{6,4},{7,5},{8,10},{9,11},{10,... | collective-permute-start | bytes 589832 | tf_op jit(solution)/shard_map/ppermute | solution.py:525
  90.5 2.9 %collective-permute-start.35 = (bf16[1,128,512]{2,1,0:T(8,128)(2,1)S(1)}, bf16[1,128,512]{2,1,0:T(8,128)(2,1)S(1)}, u32[]{:S(2)}, u32[]{:S(2)}) collective-permute-start(bf16[1,128,512]{2,1,0:T(8,128)(2,1)S(1)} %get-tuple-element.96), channel_id=1, source_target_pairs={{0,1},{1,0},{2,3},{3,2},{4,5},{5,4},{6,7},{7,6},{8,9},{9,8},{10,11... | collective-permute-start | bytes 393224 | tf_op jit(solution)/shard_map/ppermute | solution.py:525
  90.8 6.7 %collective-permute-start.36 = (bf16[1,128,512]{2,1,0:T(8,128)(2,1)S(1)}, bf16[1,128,512]{2,1,0:T(8,128)(2,1)S(1)}, u32[]{:S(2)}, u32[]{:S(2)}) collective-permute-start(bf16[1,128,512]{2,1,0:T(8,128)(2,1)S(1)} %fold.19.refs_10_), channel_id=1, source_target_pairs={{0,2},{1,3},{2,0},{3,1},{4,6},{5,7},{6,4},{7,5},{8,10},{9,11},{10,... | collective-permute-start | bytes 393224 | tf_op jit(solution)/shard_map/ppermute | solution.py:525
  92.0 5.9 %collective-permute-start.37 = (bf16[1,128,512]{2,1,0:T(8,128)(2,1)S(1)}, bf16[1,128,512]{2,1,0:T(8,128)(2,1)S(1)}, u32[]{:S(2)}, u32[]{:S(2)}) collective-permute-start(bf16[1,128,512]{2,1,0:T(8,128)(2,1)S(1)} %tie.22), channel_id=1, source_target_pairs={{0,1},{1,0},{2,3},{3,2},{4,5},{5,4},{6,7},{7,6},{8,9},{9,8},{10,11... | collective-permute-start | bytes 393224 | tf_op jit(solution)/shard_map/ppermute | solution.py:525
  92.1 8.2 %collective-permute-start.38 = (bf16[1,128,512]{2,1,0:T(8,128)(2,1)S(1)}, bf16[1,128,512]{2,1,0:T(8,128)(2,1)S(1)}, u32[]{:S(2)}, u32[]{:S(2)}) collective-permute-start(bf16[1,128,512]{2,1,0:T(8,128)(2,1)S(1)} %fold.20.refs_2_), channel_id=1, source_target_pairs={{0,2},{1,3},{2,0},{3,1},{4,6},{5,7},{6,4},{7,5},{8,10},{9,11},{10,... | collective-permute-start | bytes 393224 | tf_op jit(solution)/shard_map/ppermute | solution.py:525
  93.4 7.2 %collective-permute-start.29 = (bf16[1,128,256]{2,1,0:T(8,128)(2,1)S(1)}, bf16[1,128,256]{2,1,0:T(8,128)(2,1)S(1)}, u32[]{:S(2)}, u32[]{:S(2)}) collective-permute-start(bf16[1,128,256]{2,1,0:T(8,128)(2,1)S(1)} %get-tuple-element.89), channel_id=1, source_target_pairs={{0,1},{1,0},{2,3},{3,2},{4,5},{5,4},{6,7},{7,6},{8,9},{9,8},{10,11... | collective-permute-start | bytes 196616 | tf_op jit(solution)/shard_map/ppermute | solution.py:525
  94.6 6.6 %collective-permute-start.32 = (bf16[1,128,256]{2,1,0:T(8,128)(2,1)S(1)}, bf16[1,128,256]{2,1,0:T(8,128)(2,1)S(1)}, u32[]{:S(2)}, u32[]{:S(2)}) collective-permute-start(bf16[1,128,256]{2,1,0:T(8,128)(2,1)S(1)} %fold.21.refs_3_), channel_id=1, source_target_pairs={{0,2},{1,3},{2,0},{3,1},{4,6},{5,7},{6,4},{7,5},{8,10},{9,11},{10,... | collective-permute-start | bytes 196616 | tf_op jit(solution)/shard_map/ppermute | solution.py:525
  101.7 3.6 %collective-permute-start.39 = (f32[8,128]{1,0:T(8,128)S(1)}, f32[8,128]{1,0:T(8,128)S(1)}, u32[]{:S(2)}, u32[]{:S(2)}) collective-permute-start(f32[8,128]{1,0:T(8,128)S(1)} %get-tuple-element.104.refs_0_), channel_id=1, source_target_pairs={{0,4},{4,0},{8,12},{12,8},{1,5},{5,1},{9,13},{13,9},{2,6},{6,2},{1... | collective-permute-start | bytes 12296 | tf_op jit(solution)/shard_map/ppermute | solution.py:525
  105.3 4.5 %collective-permute-start.40 = (f32[8,128]{1,0:T(8,128)S(1)}, f32[8,128]{1,0:T(8,128)S(1)}, u32[]{:S(2)}, u32[]{:S(2)}) collective-permute-start(f32[8,128]{1,0:T(8,128)S(1)} %merge.1.refs_0_), channel_id=1, source_target_pairs={{0,8},{4,12},{8,0},{12,4},{1,9},{5,13},{9,1},{13,5},{2,10},{6,14},... | collective-permute-start | bytes 12296 | tf_op jit(solution)/shard_map/ppermute | solution.py:525
  110.2 8.6 %collective-permute-start.42 = (bf16[64,2048]{1,0:T(8,128)(2,1)S(1)}, bf16[64,2048]{1,0:T(8,128)(2,1)S(1)}, u32[]{:S(2)}, u32[]{:S(2)}) collective-permute-start(bf16[64,2048]{1,0:T(8,128)(2,1)S(1)} %get-tuple-element.107), channel_id=1, source_target_pairs={{0,2},{1,3},{2,0},{3,1},{4,6},{5,7},{6,4},{7,5},{8,10},{9,11},{10,... | collective-permute-start | bytes 786440 | tf_op jit(solution)/shard_map/ppermute | solution.py:525
  111.2 12.7 %collective-permute-start.41 = (bf16[64,2176]{1,0:T(8,128)(2,1)S(1)}, bf16[64,2176]{1,0:T(8,128)(2,1)S(1)}, u32[]{:S(2)}, u32[]{:S(2)}) collective-permute-start(bf16[64,2176]{1,0:T(8,128)(2,1)S(1)} %get-tuple-element.106), channel_id=1, source_target_pairs={{0,2},{1,3},{2,0},{3,1},{4,6},{5,7},{6,4},{7,5},{8,10},{9,11},{10,... | collective-permute-start | bytes 835592 | tf_op jit(solution)/shard_map/ppermute | solution.py:525
  112.3 7.0 %collective-permute-start.43 = (bf16[64,2048]{1,0:T(8,128)(2,1)S(1)}, bf16[64,2048]{1,0:T(8,128)(2,1)S(1)}, u32[]{:S(2)}, u32[]{:S(2)}) collective-permute-start(bf16[64,2048]{1,0:T(8,128)(2,1)S(1)} %get-tuple-element.107), channel_id=1, source_target_pairs={{0,1},{1,0},{2,3},{3,2},{4,5},{5,4},{6,7},{7,6},{8,9},{9,8},{10,11... | collective-permute-start | bytes 786440 | tf_op jit(solution)/shard_map/ppermute | solution.py:525
  118.9 10.7 %collective-permute-start.45 = (bf16[64,2176]{1,0:T(8,128)(2,1)S(1)}, bf16[64,2176]{1,0:T(8,128)(2,1)S(1)}, u32[]{:S(2)}, u32[]{:S(2)}) collective-permute-start(bf16[64,2176]{1,0:T(8,128)(2,1)S(1)} %get-tuple-element.106), channel_id=1, source_target_pairs={{0,1},{1,0},{2,3},{3,2},{4,5},{5,4},{6,7},{7,6},{8,9},{9,8},{10,11... | collective-permute-start | bytes 835592 | tf_op jit(solution)/shard_map/ppermute | solution.py:525
  123.8 5.8 %collective-permute-start.46 = (bf16[64,2176]{1,0:T(8,128)(2,1)S(1)}, bf16[64,2176]{1,0:T(8,128)(2,1)S(1)}, u32[]{:S(2)}, u32[]{:S(2)}) collective-permute-start(bf16[64,2176]{1,0:T(8,128)(2,1)S(1)} %tie.23), channel_id=1, source_target_pairs={{0,1},{1,0},{2,3},{3,2},{4,5},{5,4},{6,7},{7,6},{8,9},{9,8},{10,11... | collective-permute-start | bytes 835592 | tf_op jit(solution)/shard_map/ppermute | solution.py:525
  124.0 9.1 %collective-permute-start.47 = (bf16[2,4,16,1024]{3,2,1,0:T(8,128)(2,1)S(1)}, bf16[2,4,16,1024]{3,2,1,0:T(8,128)(2,1)S(1)}, u32[]{:S(2)}, u32[]{:S(2)}) collective-permute-start(bf16[2,4,16,1024]{3,2,1,0:T(8,128)(2,1)S(1)} %get-tuple-element.112), channel_id=1, source_target_pairs={{0,4},{4,0},{8,12},{12,8},{1,5},{5,1},{9,13},{13,9},{2,6},{6,2},{1... | collective-permute-start | bytes 786440 | tf_op jit(solution)/shard_map/ppermute | solution.py:525
  129.1 12.5 %collective-permute-start.49 = (bf16[2,4,16,1024]{3,2,1,0:T(8,128)(2,1)S(1)}, bf16[2,4,16,1024]{3,2,1,0:T(8,128)(2,1)S(1)}, u32[]{:S(2)}, u32[]{:S(2)}) collective-permute-start(bf16[2,4,16,1024]{3,2,1,0:T(8,128)(2,1)S(1)} %get-tuple-element.113), channel_id=1, source_target_pairs={{0,4},{4,0},{8,12},{12,8},{1,5},{5,1},{9,13},{13,9},{2,6},{6,2},{1... | collective-permute-start | bytes 786440 | tf_op jit(solution)/shard_map/ppermute | solution.py:525
  133.3 8.3 %collective-permute-start.51 = (bf16[1,4,16,1024]{3,2,1,0:T(8,128)(2,1)S(1)}, bf16[1,4,16,1024]{3,2,1,0:T(8,128)(2,1)S(1)}, u32[]{:S(2)}, u32[]{:S(2)}) collective-permute-start(bf16[1,4,16,1024]{3,2,1,0:T(8,128)(2,1)S(1)} %fold.22.refs_5_), channel_id=1, source_target_pairs={{0,8},{4,12},{8,0},{12,4},{1,9},{5,13},{9,1},{13,5},{2,10},{6,14},... | collective-permute-start | bytes 393224 | tf_op jit(solution)/shard_map/ppermute | solution.py:525
  136.0 12.7 %collective-permute-start.48 = (bf16[2,4,16,1024]{3,2,1,0:T(8,128)(2,1)S(1)}, bf16[2,4,16,1024]{3,2,1,0:T(8,128)(2,1)S(1)}, u32[]{:S(2)}, u32[]{:S(2)}) collective-permute-start(bf16[2,4,16,1024]{3,2,1,0:T(8,128)(2,1)S(1)} %tie.24), channel_id=1, source_target_pairs={{0,4},{4,0},{8,12},{12,8},{1,5},{5,1},{9,13},{13,9},{2,6},{6,2},{1... | collective-permute-start | bytes 786440 | tf_op jit(solution)/shard_map/ppermute | solution.py:525
  141.6 15.9 %collective-permute-start.52 = (bf16[2,4,16,1024]{3,2,1,0:T(8,128)(2,1)S(1)}, bf16[2,4,16,1024]{3,2,1,0:T(8,128)(2,1)S(1)}, u32[]{:S(2)}, u32[]{:S(2)}) collective-permute-start(bf16[2,4,16,1024]{3,2,1,0:T(8,128)(2,1)S(1)} %tie.25), channel_id=1, source_target_pairs={{0,4},{4,0},{8,12},{12,8},{1,5},{5,1},{9,13},{13,9},{2,6},{6,2},{1... | collective-permute-start | bytes 786440 | tf_op jit(solution)/shard_map/ppermute | solution.py:525
  144.4 13.4 %collective-permute-start.54 = (bf16[1,4,16,1024]{3,2,1,0:T(8,128)(2,1)S(1)}, bf16[1,4,16,1024]{3,2,1,0:T(8,128)(2,1)S(1)}, u32[]{:S(2)}, u32[]{:S(2)}) collective-permute-start(bf16[1,4,16,1024]{3,2,1,0:T(8,128)(2,1)S(1)} %fold.23.refs_2_), channel_id=1, source_target_pairs={{0,8},{4,12},{8,0},{12,4},{1,9},{5,13},{9,1},{13,5},{2,10},{6,14},... | collective-permute-start | bytes 393224 | tf_op jit(solution)/shard_map/ppermute | solution.py:525
  148.8 14.9 %collective-permute-start.50 = (bf16[1,4,16,1024]{3,2,1,0:T(8,128)(2,1)S(1)}, bf16[1,4,16,1024]{3,2,1,0:T(8,128)(2,1)S(1)}, u32[]{:S(2)}, u32[]{:S(2)}) collective-permute-start(bf16[1,4,16,1024]{3,2,1,0:T(8,128)(2,1)S(1)} %fold.24.refs_3_), channel_id=1, source_target_pairs={{0,8},{4,12},{8,0},{12,4},{1,9},{5,13},{9,1},{13,5},{2,10},{6,14},... | collective-permute-start | bytes 393224 | tf_op jit(solution)/shard_map/ppermute | solution.py:525
  157.6 8.5 %collective-permute-start.53 = (bf16[1,4,16,1024]{3,2,1,0:T(8,128)(2,1)S(1)}, bf16[1,4,16,1024]{3,2,1,0:T(8,128)(2,1)S(1)}, u32[]{:S(2)}, u32[]{:S(2)}) collective-permute-start(bf16[1,4,16,1024]{3,2,1,0:T(8,128)(2,1)S(1)} %fold.25.refs_4_), channel_id=1, source_target_pairs={{0,8},{4,12},{8,0},{12,4},{1,9},{5,13},{9,1},{13,5},{2,10},{6,14},... | collective-permute-start | bytes 393224 | tf_op jit(solution)/shard_map/ppermute | solution.py:525
  (17 other events, 83.7 us)
